TPU v7x, 32 devices: a whole 2x2x4 slice. The times are simulated.
32 devices in a mesh: groups: 2 (over x), inner: 16 (over z, y, core).
Axes of the slice: x: 2, y: 2, z: 4, core: 2. Of those that a mesh axis runs over, the one named last changes fastest.
Arguments:
- hidden_rows: bfloat16 [2048, 2048], P(('groups', 'inner')), parts along dimension 0, may hold values from -6 to 6
- token_embed: bfloat16 [2048, 2048], P(('groups', 'inner')), parts along dimension 0, may hold values from -6 to 6
- first_routes: int32 [2048, 8], P(('groups', 'inner')), parts along dimension 0, may hold values from 0 to 15, all different within a row; in each aligned block of 64 rows (0 to 63, 64 to 127, ...) at most 48 rows name the same one
- first_gates: float32 [2048, 8], P(('groups', 'inner')), parts along dimension 0, may hold values from 0.2 to 0.6
- first_gate_up: bfloat16 [16, 2048, 1024], P('inner'), may hold values from -0.125 to 0.125
- first_down: bfloat16 [16, 512, 2048], P('inner'), may hold values from -0.25 to 0.25
- second_routes: int32 [2048, 8], P(('groups', 'inner')), parts along dimension 0, may hold values from 0 to 15, all different within a row; in each aligned block of 64 rows (0 to 63, 64 to 127, ...) at most 48 rows name the same one
- second_gates: float32 [2048, 8], P(('groups', 'inner')), parts along dimension 0, may hold values from 0.2 to 0.6
- second_gate_up: bfloat16 [16, 2048, 1024], P('inner'), may hold values from -0.125 to 0.125
- second_down: bfloat16 [16, 512, 2048], P('inner'), may hold values from -0.25 to 0.25
- hidden_gain: float32 [2048], replicated, may hold values from 0.25 to 1.75
- embed_gain: float32 [2048], replicated, may hold values from 0.25 to 1.75
- merge_weight: bfloat16 [4096, 2048], P('inner'), may hold values from -0.09375 to 0.09375
Outputs:
- final_rows: bfloat16 [2048, 2048], P(('groups', 'inner')), parts along dimension 0
There are 2 independent parts, one for each index of `groups`. A program takes and returns all parts, laid end to end along the dimension named above; an argument that names none is the same for every part. Nothing has to cross between parts.
Inputs may be any that keep to these rules, and one draw needn't show every extreme that they name: `first_routes`: among the 64 tokens of one block, no expert is named more than 48 times, and in every draw some expert is named exactly 48 times in some block. `second_routes`: among the 64 tokens of one block, no expert is named more than 48 times, and in every draw some expert is named exactly 48 times in some block.
All inputs are finite; a program needn't handle non-finite values.
Results may differ from a plain program's by a relative error of at most 0.01.
Values may be sent and summed in bfloat16 or wider, within the bound.
No kernel may reach another device: no remote copies, remote signals or barrier semaphores. Data moves between devices by JAX's collectives and lax.ppermute only.
A program may use at most 128 MiB of HBM per device.

v0:
```python
import jax
import jax.numpy as jnp
from jax import lax
from jax.sharding import PartitionSpec as P

EPSILON = 1e-06


def expert_apply(slot_rows, expert_gu, expert_down):
    inner_width = expert_down.shape[0]
    projected = jnp.dot(slot_rows, expert_gu, preferred_element_type=jnp.float32)
    inner = (jax.nn.silu(projected[:, :inner_width]) * projected[:, inner_width:]).astype(
        jnp.bfloat16
    )
    return jnp.dot(inner, expert_down, preferred_element_type=jnp.float32).astype(jnp.bfloat16)


def rms_scale(values, gain_vec):
    widened = values.astype(jnp.float32)
    inverse_rms = lax.rsqrt(jnp.mean(widened * widened, axis=-1, keepdims=True) + EPSILON)
    return (widened * inverse_rms * gain_vec).astype(jnp.bfloat16)


def routed_layer(inputs, routes, weights_in, gate_up, down_proj):
    tok_rows, feature_dim = inputs.shape
    top_count = routes.shape[1]
    experts = lax.axis_size("inner")
    capacity = max(2, 3 * tok_rows * top_count // (2 * experts))
    flat_ids = routes.reshape(-1)
    onehot = (flat_ids[:, None] == jnp.arange(experts, dtype=jnp.int32)[None, :]).astype(jnp.int32)
    ranking = jnp.sum(onehot * (jnp.cumsum(onehot, axis=0) - 1), axis=1)
    position = flat_ids * capacity + ranking
    target = jnp.arange(experts * capacity, dtype=jnp.int32)
    chosen = (
        (target[:, None] == position[None, :])
        .astype(jnp.int32)
        .reshape(experts * capacity, tok_rows, top_count)
    )
    dispatch = jnp.sum(chosen, axis=2).astype(jnp.bfloat16)
    packed = jnp.dot(dispatch, inputs, preferred_element_type=jnp.float32).astype(jnp.bfloat16)
    packed = packed.reshape(experts, capacity, feature_dim)
    received = lax.all_to_all(packed, "inner", split_axis=0, concat_axis=0, tiled=True)
    sources = received.shape[0]
    slot_count = received.shape[1]
    slot_rows = received.reshape(sources * slot_count, feature_dim)
    answer = expert_apply(slot_rows, gate_up[0], down_proj[0]).reshape(
        sources, slot_count, feature_dim
    )
    returned = lax.all_to_all(answer, "inner", split_axis=0, concat_axis=0, tiled=True)
    gathered = returned.reshape(experts * capacity, feature_dim)[position].reshape(
        tok_rows, top_count, feature_dim
    )
    return jnp.sum(gathered.astype(jnp.float32) * weights_in[:, :, None], axis=1)


def local(
    hidden_rows,
    token_embed,
    first_routes,
    first_gates,
    first_gate_up,
    first_down,
    second_routes,
    second_gates,
    second_gate_up,
    second_down,
    hidden_gain,
    embed_gain,
    merge_weight,
):
    first_moe = routed_layer(hidden_rows, first_routes, first_gates, first_gate_up, first_down)
    after_first = (hidden_rows.astype(jnp.float32) + first_moe).astype(jnp.bfloat16)
    merged_in = jnp.concatenate(
        [rms_scale(after_first, hidden_gain), rms_scale(token_embed, embed_gain)], axis=1
    )
    merged = jnp.dot(
        merged_in,
        lax.all_gather(merge_weight, "inner", axis=0, tiled=True),
        preferred_element_type=jnp.float32,
    )
    after_merge = (after_first.astype(jnp.float32) + jax.nn.silu(merged)).astype(jnp.bfloat16)
    second_moe = routed_layer(after_merge, second_routes, second_gates, second_gate_up, second_down)
    return (after_merge.astype(jnp.float32) + second_moe).astype(jnp.bfloat16)


def solution(mesh):
    return jax.shard_map(
        local,
        mesh=mesh,
        in_specs=(
            P(("groups", "inner"), None),
            P(("groups", "inner"), None),
            P(("groups", "inner"), None),
            P(("groups", "inner"), None),
            P("inner", None, None),
            P("inner", None, None),
            P(("groups", "inner"), None),
            P(("groups", "inner"), None),
            P("inner", None, None),
            P("inner", None, None),
            P(),
            P(),
            P("inner", None),
        ),
        out_specs=P(("groups", "inner"), None),
        check_vma=False,
    )
```

profile of v0, /device:TPU:13, one launch (start us, length us, event | category | flops | bytes accessed | tf_op | source)
XLA Modules:
  0.0 451.6 jit_solution(7088949590016978472)
XLA Ops:
  6.5 0.0 all-gather.2.cloned.1.call-start
  6.5 0.7 all-gather.2.cloned.1.call-update
  7.3 0.8 copy.28
  8.0 0.1 eq.83
  8.1 0.1 eq.79
  8.2 1.2 reduce-window.14
  9.4 0.2 slice_reduce_fusion.1
  9.6 0.1 fusion.32
  9.7 0.1 reduce_sum.81
  9.9 0.5 convert_reduce_fusion.1
  10.4 2.0 convolution_convert_fusion.3
  12.3 0.0 copy-start.10
  12.4 136.1 %all_to_all.20 = bf16[16,48,2048]{2,1,0:T(8,128)(2,1)S(1)} all-to-all(bf16[16,48,2048]{2,1,0:T(8,128)(2,1)S(1)} %bitcast.66), channel_id=1, replica_groups=mesh['groups'=2,'inner'=16] {'inner'}, dimensions={0} | all-to-all | bytes 6291456 | tf_op jit(solution)/shard_map/all_to_all | solution.py:42
  148.4 3.4 fusion.4
  151.8 0.0 copy-done
  151.8 3.5 convolution_convert_fusion.1
  155.3 7.6 %all-to-all-start.1 = ((bf16[16,48,2048]{2,1,0:T(8,128)(2,1)}), bf16[16,48,2048]{2,1,0:T(8,128)(2,1)S(1)}, u32[]{:S(2)}, u32[]{:S(2)}) async-start(bf16[16,48,2048]{2,1,0:T(8,128)(2,1)} %bitcast.68), calls=%async_computation.1 | async-start | bytes 6291456 | tf_op jit(solution)/shard_map/all_to_all | solution.py:49
  163.0 0.1 copy.33
  163.1 0.1 eq.94
  163.2 0.1 eq.90
  163.2 0.1 mul.115
  163.3 0.1 copy.32
  163.4 1.2 reduce-window.16
  164.6 0.2 slice_reduce_fusion
  164.8 0.1 fusion.30
  164.9 0.1 reduce_sum.88
  165.1 0.2 fusion.14
  165.2 1.2 convert_reduce_fusion
  166.5 91.1 %all-to-all-done.1 = bf16[16,48,2048]{2,1,0:T(8,128)(2,1)S(1)} async-done(((bf16[16,48,2048]{2,1,0:T(8,128)(2,1)}), bf16[16,48,2048]{2,1,0:T(8,128)(2,1)S(1)}, u32[]{:S(2)}, u32[]{:S(2)}) %all-to-all-start.1) | async-done | bytes 3145760 | tf_op jit(solution)/shard_map/all_to_all | solution.py:49
  257.6 3.3 gather_fusion
  260.9 3.4 fusion.1
  264.4 1.2 fusion.17
  265.6 0.1 fusion.19
  265.8 0.0 all-gather.2.cloned.1.call-done
  265.8 0.0 copy-start.4
  265.8 8.9 %fusion.20 = bf16[64,2048]{1,0:T(8,128)(2,1)S(1)} fusion(bf16[64,2048]{1,0:T(8,128)(2,1)S(1)} %get-tuple-element.6, bf16[4096,2048]{1,0:T(8,128)(2,1)} %all-gather.2.cloned.1.call-done, bf16[64,2048]{1,0:T(8,128)(2,1)S(1)} %get-tuple-element.11, bf16[64,2048]{1,0:T(8,128)(2,1)S(1)} %fusion.19), kind=kOutput, calls=%fused_computation.37 | convolution fusion | flops 1075707904 | bytes 17825792 | tf_op jit(solution)/shard_map/dot_general | solution.py:76
  274.7 1.0 convolution_convert_fusion.2
  275.7 0.0 copy-start.11
  275.7 74.8 %all_to_all.21 = bf16[16,48,2048]{2,1,0:T(8,128)(2,1)S(1)} all-to-all(bf16[16,48,2048]{2,1,0:T(8,128)(2,1)S(1)} %bitcast.67), channel_id=1, replica_groups=mesh['groups'=2,'inner'=16] {'inner'}, dimensions={0} | all-to-all | bytes 6291456 | tf_op jit(solution)/shard_map/all_to_all | solution.py:42
  350.5 3.4 fusion.2
  354.0 3.5 convolution_convert_fusion
  357.5 5.3 %all-to-all-start.3 = ((bf16[16,48,2048]{2,1,0:T(8,128)(2,1)}), bf16[16,48,2048]{2,1,0:T(8,128)(2,1)}, u32[]{:S(2)}, u32[]{:S(2)}) async-start(bf16[16,48,2048]{2,1,0:T(8,128)(2,1)} %bitcast.15), calls=%async_computation.3 | async-start | bytes 6291456 | tf_op jit(solution)/shard_map/all_to_all | solution.py:49
  362.9 0.1 mul.133
  363.0 0.1 copy.37
  363.1 69.8 %all-to-all-done.3 = bf16[16,48,2048]{2,1,0:T(8,128)(2,1)} async-done(((bf16[16,48,2048]{2,1,0:T(8,128)(2,1)}), bf16[16,48,2048]{2,1,0:T(8,128)(2,1)}, u32[]{:S(2)}, u32[]{:S(2)}) %all-to-all-start.3) | async-done | bytes 3145760 | tf_op jit(solution)/shard_map/all_to_all | solution.py:49
  432.9 7.7 %gather_fusion.1 = bf16[512,2048]{1,0:T(8,128)(2,1)} fusion(bf16[768,2048]{1,0:T(8,128)(2,1)} %bitcast.16, s32[1024]{0:T(1024)S(1)} %pad_clamp_fusion), kind=kCustom, calls=%fused_computation.1 | custom fusion | bytes 4196352 | tf_op jit(solution)/shard_map/gather | solution.py:50
  440.5 3.4 fusion
  444.0 0.8 add_convert_fusion
  (36 shorter events, 0.2 us)
Async XLA Ops:
  6.5 145.3 %copy-start = (bf16[1,512,2048]{2,1,0:T(8,128)(2,1)S(1)}, bf16[1,512,2048]{2,1,0:T(8,128)(2,1)}, u32[]{:S(2)}) copy-start(bf16[1,512,2048]{2,1,0:T(8,128)(2,1)} %param.18) | copy-start | bytes 6291460
  6.5 259.3 %all-gather.2.cloned.1.call-start = ((), (), s32[]{:S(2)}) async-start(), calls=%async_computation.4 | async-start | bytes 17825792 | tf_op jit(solution)/shard_map/all_gather | solution.py:78
  12.3 136.1 %copy-start.10 = (bf16[1,2048,1024]{2,1,0:T(8,128)(2,1)S(1)}, bf16[1,2048,1024]{2,1,0:T(8,128)(2,1)}, u32[]{:S(2)}) copy-start(bf16[1,2048,1024]{2,1,0:T(8,128)(2,1)} %param.17) | copy-start | bytes 12582916
  155.3 7.6 %copy-start.7 = (s32[64,8]{0,1:T(8,128)S(1)}, s32[64,8]{0,1:T(8,128)}, u32[]{:S(2)}) copy-start(s32[64,8]{0,1:T(8,128)} %param.19) | copy-start | bytes 6148
  155.3 8.0 %copy-start.8 = (f32[64,8]{0,1:T(8,128)S(1)}, f32[64,8]{0,1:T(8,128)}, u32[]{:S(2)}) copy-start(f32[64,8]{0,1:T(8,128)} %param.16) | copy-start | bytes 6148
  155.3 9.7 %copy-start.3 = (bf16[64,2048]{1,0:T(8,128)(2,1)S(1)}, bf16[64,2048]{1,0:T(8,128)(2,1)}, u32[]{:S(2)}) copy-start(bf16[64,2048]{1,0:T(8,128)(2,1)} %param.14) | copy-start | bytes 786436
  155.3 102.3 %all-to-all-start.1 = ((bf16[16,48,2048]{2,1,0:T(8,128)(2,1)}), bf16[16,48,2048]{2,1,0:T(8,128)(2,1)S(1)}, u32[]{:S(2)}, u32[]{:S(2)}) async-start(bf16[16,48,2048]{2,1,0:T(8,128)(2,1)} %bitcast.68), calls=%async_computation.1 | async-start | bytes 6291456 | tf_op jit(solution)/shard_map/all_to_all | solution.py:49
  257.6 6.8 %copy-start.2 = (bf16[64,2048]{1,0:T(8,128)(2,1)S(1)}, bf16[64,2048]{1,0:T(8,128)(2,1)}, u32[]{:S(2)}) copy-start(bf16[64,2048]{1,0:T(8,128)(2,1)} %param.13) | copy-start | bytes 786436
  257.6 6.8 %copy-start.5 = (f32[2048]{0:T(1024)S(1)}, f32[2048]{0:T(1024)}, u32[]{:S(2)}) copy-start(f32[2048]{0:T(1024)} %param.24) | copy-start | bytes 24580
  260.9 4.7 %copy-start.6 = (f32[2048]{0:T(1024)S(1)}, f32[2048]{0:T(1024)}, u32[]{:S(2)}) copy-start(f32[2048]{0:T(1024)} %param.23) | copy-start | bytes 24580
  265.8 8.9 %copy-start.4 = (s32[768,64]{0,1:T(8,128)S(1)}, s32[768,64]{0,1:T(8,128)}, u32[]{:S(2)}) copy-start(s32[768,64]{0,1:T(8,128)} %convert_reduce_fusion) | copy-start | bytes 589828
  275.7 74.8 %copy-start.11 = (bf16[1,2048,1024]{2,1,0:T(8,128)(2,1)S(1)}, bf16[1,2048,1024]{2,1,0:T(8,128)(2,1)}, u32[]{:S(2)}) copy-start(bf16[1,2048,1024]{2,1,0:T(8,128)(2,1)} %param.21) | copy-start | bytes 12582916
  350.5 3.4 copy-start.12
  357.5 5.4 %copy-start.9 = (f32[64,8]{0,1:T(8,128)S(1)}, f32[64,8]{0,1:T(8,128)}, u32[]{:S(2)}) copy-start(f32[64,8]{0,1:T(8,128)} %param.20) | copy-start | bytes 6148
  357.5 75.3 %all-to-all-start.3 = ((bf16[16,48,2048]{2,1,0:T(8,128)(2,1)}), bf16[16,48,2048]{2,1,0:T(8,128)(2,1)}, u32[]{:S(2)}, u32[]{:S(2)}) async-start(bf16[16,48,2048]{2,1,0:T(8,128)(2,1)} %bitcast.15), calls=%async_computation.3 | async-start | bytes 6291456 | tf_op jit(solution)/shard_map/all_to_all | solution.py:49
  432.8 11.9 %copy-start.1 = (bf16[1,512,2048]{2,1,0:T(8,128)(2,1)S(1)}, bf16[1,512,2048]{2,1,0:T(8,128)(2,1)}, u32[]{:S(2)}) copy-start(bf16[1,512,2048]{2,1,0:T(8,128)(2,1)} %param.18) | copy-start | bytes 6291460
Sparse Core Ops, SparseCore 0:
  9.5 227.8 all-gather.1
where the time goes:
time: 452 us
  blocking collectives  211 us (47%)
  waiting for transfers between devices  162 us (36%)
  matrix products  25.7 us (6%)
  between operations  13.7 us (3%)
  other arithmetic  13.5 us (3%)
  local copies, waits for them, and re-layouts  13.3 us (3%)
  starting transfers between devices  13 us (3%)
    all_to_all x2, blocking collectives, routed_layer(): lax.all_to_all(packed, 'inner', split_axis=0, concat_axis=0, tiled=True)  211 us
    all_to_all x2, waiting for transfers between devices, routed_layer(): lax.all_to_all(answer, 'inner', split_axis=0, concat_axis=0, tiled=True)  161 us
    all_to_all x2, starting transfers between devices, routed_layer(): lax.all_to_all(answer, 'inner', split_axis=0, concat_axis=0, tiled=True)  13 us
    gather x2, local copies, waits for them, and re-layouts, routed_layer(): returned.reshape(experts * capacity, feature_dim)[position]  11 us
  transfers between devices with their start and end apart: 3, of which 2 were waited for; matrix products, arithmetic and copies ran while one was open for 5% of the time, Pallas kernels for 0%

commit v1 on v0

v1 whole, which is shorter than its diff:
```python
import jax
import jax.numpy as jnp
from jax import lax
from jax.sharding import PartitionSpec as P

EPSILON = 1e-06


def gate_table(routes, gates, experts):
    named = routes[:, :, None] == jnp.arange(experts, dtype=jnp.int32)[None, None, :]
    return jnp.sum(jnp.where(named, gates[:, :, None], 0.0), axis=1)


def normed(values, gain):
    widened = values.astype(jnp.float32)
    inverse = lax.rsqrt(jnp.mean(widened * widened, axis=-1, keepdims=True) + EPSILON)
    return (widened * inverse * gain).astype(jnp.bfloat16)


def expert(rows, gate_column, gate_up, down):
    width = down.shape[0]
    projected = jnp.dot(rows, gate_up, preferred_element_type=jnp.float32)
    hidden = (jax.nn.silu(projected[:, :width]) * projected[:, width:]).astype(jnp.bfloat16)
    out = jnp.dot(hidden, down, preferred_element_type=jnp.float32)
    return (out * gate_column).astype(jnp.bfloat16)


def routed(rows, gate_column, gate_up, down):
    every = lax.all_gather(rows, "inner", axis=0, tiled=True)
    part = expert(every, gate_column, gate_up, down)
    return lax.psum_scatter(part, "inner", scatter_dimension=0, tiled=True)


def local(
    hidden_rows,
    token_embed,
    first_routes,
    first_gates,
    first_gate_up,
    first_down,
    second_routes,
    second_gates,
    second_gate_up,
    second_down,
    hidden_gain,
    embed_gain,
    merge_weight,
):
    experts = lax.axis_size("inner")
    tables = jnp.stack(
        [gate_table(first_routes, first_gates, experts), gate_table(second_routes, second_gates, experts)], axis=1
    )
    columns = lax.all_to_all(tables, "inner", split_axis=2, concat_axis=0, tiled=True)
    first = routed(hidden_rows, columns[:, 0], first_gate_up[0], first_down[0])
    after_first = (hidden_rows.astype(jnp.float32) + first.astype(jnp.float32)).astype(jnp.bfloat16)
    merged_in = jnp.concatenate([normed(after_first, hidden_gain), normed(token_embed, embed_gain)], axis=1)
    slices = lax.all_to_all(merged_in, "inner", split_axis=1, concat_axis=0, tiled=True)
    partial = jnp.dot(slices, merge_weight, preferred_element_type=jnp.float32).astype(jnp.bfloat16)
    merged = lax.psum_scatter(partial, "inner", scatter_dimension=0, tiled=True).astype(jnp.float32)
    after_merge = (after_first.astype(jnp.float32) + jax.nn.silu(merged)).astype(jnp.bfloat16)
    second = routed(after_merge, columns[:, 1], second_gate_up[0], second_down[0])
    return (after_merge.astype(jnp.float32) + second.astype(jnp.float32)).astype(jnp.bfloat16)


def solution(mesh):
    rows = P(("groups", "inner"), None)
    weight = P("inner", None, None)
    return jax.shard_map(
        local,
        mesh=mesh,
        in_specs=(rows, rows, rows, rows, weight, weight, rows, rows, weight, weight, P(), P(), P("inner", None)),
        out_specs=rows,
        check_vma=False,
    )
```

time: 452 us -> 385 us (0.85)
  the two profiles are of different devices: /device:TPU:13 before, /device:TPU:0 now
where the time goes in v1:
time: 385 us
  waiting for transfers between devices  303 us (79%)
  blocking collectives  31.6 us (8%)
  matrix products  27.1 us (7%)
  between operations  13.3 us (3%)
  other arithmetic  8.33 us (2%)
    reduce_scatter x2, waiting for transfers between devices, routed(): return lax.psum_scatter(part, 'inner', scatter_dimension=0, tiled=True)  141 us
    all_gather x2, waiting for transfers between devices, routed(): every = lax.all_gather(rows, 'inner', axis=0, tiled=True)  88.9 us
    reduce_scatter x1, waiting for transfers between devices, local(): lax.psum_scatter(partial, 'inner', scatter_dimension=0, tiled=True)  72.1 us
    all_to_all x1, blocking collectives, local(): lax.all_to_all(merged_in, 'inner', split_axis=1, concat_axis=0, tiled=True)  18 us
    dot_general x2, matrix products, expert(): projected = jnp.dot(rows, gate_up, preferred_element_type=jnp.float32)  15.1 us
    all_to_all x1, blocking collectives, local(): lax.all_to_all(tables, 'inner', split_axis=2, concat_axis=0, tiled=True)  13.6 us
    dot_general x2, matrix products, expert(): out = jnp.dot(hidden, down, preferred_element_type=jnp.float32)  8.72 us
  transfers between devices with their start and end apart: 5, of which 5 were waited for; matrix products, arithmetic and copies ran while one was open for 1% of the time, Pallas kernels for 0%

profile of v1, /device:TPU:0, one launch (start us, length us, event | category | flops | bytes accessed | tf_op | source)
XLA Modules:
  0.0 384.8 jit_solution(10534576378294099241)
XLA Ops:
  6.5 0.0 copy-start
  6.5 0.0 all-gather.3.cloned.1.call-start
  6.5 0.7 all-gather.3.cloned.1.call-update
  7.3 0.0 reduce-scatter.4.cloned.1.call-start
  7.3 0.7 select_reduce_fusion.1
  8.0 0.7 select_reduce_fusion
  8.8 0.1 reshape.27
  8.9 13.6 %all_to_all.37 = f32[16,1,128]{2,1,0:T(1,128)S(1)} all-to-all(f32[16,1,128]{2,1,0:T(1,128)S(1)} %reshape.27), channel_id=1, replica_groups=mesh['groups'=2,'inner'=16] {'inner'}, dimensions={0} | all-to-all | bytes 16384 | tf_op jit(solution)/shard_map/all_to_all | solution.py:53
  22.5 0.5 broadcast.45
  23.0 0.7 reduce
  23.6 0.1 reshape.28
  23.7 0.1 all_to_all.30
  23.8 39.1 %all-gather.3.cloned.1.call-done = bf16[1024,2048]{1,0:T(8,128)(2,1)} async-done(((bf16[64,2048]{1,0:T(8,128)(2,1)}), bf16[1024,2048]{1,0:T(8,128)(2,1)}) %all-gather.3.cloned.1.call-update) | async-done | bytes 4194320 | tf_op jit(solution)/shard_map/all_gather | solution.py:29
  63.0 7.5 %fusion.2 = f32[1024,1024]{1,0:T(8,128)S(1)} fusion(bf16[1024,2048]{1,0:T(8,128)(2,1)} %all-gather.3.cloned.1.call-done, bf16[1,2048,1024]{2,1,0:T(8,128)(2,1)} %param.17), kind=kOutput, calls=%fused_computation.4 | convolution fusion | flops 4294967296 | bytes 12582912 | tf_op jit(solution)/shard_map/dot_general | solution.py:22
  70.5 0.0 copy-done
  70.5 4.4 %multiply_convert_fusion.1 = bf16[1024,2048]{1,0:T(8,128)(2,1)} fusion(f32[1024]{0:T(1024)S(1)} %bitcast.47, bf16[1,512,2048]{2,1,0:T(8,128)(2,1)S(1)} %copy-done, f32[1024,1024]{1,0:T(8,128)S(1)} %fusion.2), kind=kOutput, calls=%fused_computation.1 | convolution fusion | flops 2154823680 | bytes 10489856 | tf_op jit(solution)/shard_map/dot_general | solution.py:24
  74.8 0.0 copy-start.4
  74.8 0.0 copy-start.6
  74.8 0.0 copy-start.1
  74.9 0.0 reduce-scatter.4.cloned.1.call-update
  74.9 0.0 reduce-scatter.6.cloned.1.call-start
  74.9 0.9 copy-done.4
  75.8 0.2 fusion.12
  76.0 0.0 copy-done.6
  76.0 0.1 fusion.14
  76.1 69.9 %reduce-scatter.4.cloned.1.call-done = bf16[64,2048]{1,0:T(8,128)(2,1)} async-done(((bf16[1024,2048]{1,0:T(8,128)(2,1)}), bf16[64,2048]{1,0:T(8,128)(2,1)}) %reduce-scatter.4.cloned.1.call-update) | async-done | bytes 262160 | tf_op jit(solution)/shard_map/reduce_scatter | solution.py:31
  146.0 0.0 copy-done.1
  146.0 1.2 fusion.18
  147.2 0.0 copy-done.7
  147.3 1.1 fusion.20
  148.4 18.0 %all_to_all.38 = bf16[64,16,256]{2,0,1:T(8,128)(2,1)S(1)} all-to-all(bf16[64,16,256]{2,0,1:T(8,128)(2,1)S(1)} %bitcast.42), channel_id=1, replica_groups=mesh['groups'=2,'inner'=16] {'inner'}, dimensions={1} | all-to-all | bytes 1048576 | tf_op jit(solution)/shard_map/all_to_all | solution.py:57
  166.4 0.0 copy-done.5
  166.4 3.2 convolution_convert_fusion
  169.6 0.0 reduce-scatter.6.cloned.1.call-update
  169.7 0.0 all-gather.5.cloned.1.call-start
  169.7 72.1 %reduce-scatter.6.cloned.1.call-done = bf16[64,2048]{1,0:T(8,128)(2,1)} async-done(((bf16[1024,2048]{1,0:T(8,128)(2,1)}), bf16[64,2048]{1,0:T(8,128)(2,1)}) %reduce-scatter.6.cloned.1.call-update) | async-done | bytes 262160 | tf_op jit(solution)/shard_map/reduce_scatter | solution.py:59
  241.8 0.0 copy-done.3
  241.8 1.8 fusion.21
  243.7 0.0 all-gather.5.cloned.1.call-update
  243.7 0.0 reduce-scatter.8.cloned.1.call-start
  243.7 49.8 %all-gather.5.cloned.1.call-done = bf16[1024,2048]{1,0:T(8,128)(2,1)} async-done(((bf16[64,2048]{1,0:T(8,128)(2,1)}), bf16[1024,2048]{1,0:T(8,128)(2,1)}) %all-gather.5.cloned.1.call-update) | async-done | bytes 4194320 | tf_op jit(solution)/shard_map/all_gather | solution.py:29
  293.5 7.6 %fusion = f32[1024,1024]{1,0:T(8,128)S(1)} fusion(bf16[1024,2048]{1,0:T(8,128)(2,1)} %all-gather.5.cloned.1.call-done, bf16[1,2048,1024]{2,1,0:T(8,128)(2,1)} %param.21), kind=kOutput, calls=%fused_computation.2 | convolution fusion | flops 4294967296 | bytes 12582912 | tf_op jit(solution)/shard_map/dot_general | solution.py:22
  301.2 0.0 copy-done.8
  301.2 4.4 %multiply_convert_fusion = bf16[1024,2048]{1,0:T(8,128)(2,1)} fusion(f32[1024]{0:T(1024)S(1)} %bitcast.46, bf16[1,512,2048]{2,1,0:T(8,128)(2,1)S(1)} %copy-done.8, f32[1024,1024]{1,0:T(8,128)S(1)} %fusion), kind=kOutput, calls=%fused_computation | convolution fusion | flops 2154823680 | bytes 10489856 | tf_op jit(solution)/shard_map/dot_general | solution.py:24
  305.5 0.0 reduce-scatter.8.cloned.1.call-update
  305.6 71.0 %reduce-scatter.8.cloned.1.call-done = bf16[64,2048]{1,0:T(8,128)(2,1)} async-done(((bf16[1024,2048]{1,0:T(8,128)(2,1)}), bf16[64,2048]{1,0:T(8,128)(2,1)}) %reduce-scatter.8.cloned.1.call-update) | async-done | bytes 262160 | tf_op jit(solution)/shard_map/reduce_scatter | solution.py:31
  376.5 0.0 copy-done.2
  376.5 1.7 add_convert_fusion
  (14 shorter events, 0.1 us)
Async XLA Ops:
  6.5 63.9 %copy-start = (bf16[1,512,2048]{2,1,0:T(8,128)(2,1)S(1)}, bf16[1,512,2048]{2,1,0:T(8,128)(2,1)}, u32[]{:S(2)}) copy-start(bf16[1,512,2048]{2,1,0:T(8,128)(2,1)} %param.18) | copy-start | bytes 6291460
  6.5 56.4 %all-gather.3.cloned.1.call-start = ((), (), s32[]{:S(2)}) async-start(), calls=%async_computation.5 | async-start | bytes 4456448 | tf_op jit(solution)/shard_map/all_gather | solution.py:29
  7.3 138.7 %reduce-scatter.4.cloned.1.call-start = ((), (), s32[]{:S(2)}) async-start(), calls=%async_computation.6 | async-start | bytes 4456448 | tf_op jit(solution)/shard_map/reduce_scatter | solution.py:31
  74.8 0.9 copy-start.4
  74.8 1.1 copy-start.6
  74.8 71.2 %copy-start.1 = (bf16[64,2048]{1,0:T(8,128)(2,1)S(1)}, bf16[64,2048]{1,0:T(8,128)(2,1)}, u32[]{:S(2)}) copy-start(bf16[64,2048]{1,0:T(8,128)(2,1)} %param.13) | copy-start | bytes 786436
  74.8 72.4 %copy-start.7 = (f32[2048]{0:T(1024)S(1)}, f32[2048]{0:T(1024)}, u32[]{:S(2)}) copy-start(f32[2048]{0:T(1024)} %param.23) | copy-start | bytes 24580
  74.9 166.9 %reduce-scatter.6.cloned.1.call-start = ((), (), s32[]{:S(2)}) async-start(), calls=%async_computation.7 | async-start | bytes 4456448 | tf_op jit(solution)/shard_map/reduce_scatter | solution.py:59
  146.0 20.4 %copy-start.5 = (bf16[256,2048]{1,0:T(8,128)(2,1)S(1)}, bf16[256,2048]{1,0:T(8,128)(2,1)}, u32[]{:S(2)}) copy-start(bf16[256,2048]{1,0:T(8,128)(2,1)} %param.25) | copy-start | bytes 3145732
  166.4 75.4 %copy-start.3 = (bf16[64,2048]{1,0:T(8,128)(2,1)S(1)}, bf16[64,2048]{1,0:T(8,128)(2,1)}, u32[]{:S(2)}) copy-start(bf16[64,2048]{1,0:T(8,128)(2,1)} %reduce-scatter.4.cloned.1.call-done) | copy-start | bytes 786436
  169.7 123.9 %all-gather.5.cloned.1.call-start = ((), (), s32[]{:S(2)}) async-start(), calls=%async_computation.8 | async-start | bytes 4456448 | tf_op jit(solution)/shard_map/all_gather | solution.py:29
  243.7 132.8 %reduce-scatter.8.cloned.1.call-start = ((), (), s32[]{:S(2)}) async-start(), calls=%async_computation.9 | async-start | bytes 4456448 | tf_op jit(solution)/shard_map/reduce_scatter | solution.py:31
  293.5 7.7 %copy-start.8 = (bf16[1,512,2048]{2,1,0:T(8,128)(2,1)S(1)}, bf16[1,512,2048]{2,1,0:T(8,128)(2,1)}, u32[]{:S(2)}) copy-start(bf16[1,512,2048]{2,1,0:T(8,128)(2,1)} %param.22) | copy-start | bytes 6291460
  305.5 71.0 %copy-start.2 = (bf16[64,2048]{1,0:T(8,128)(2,1)S(1)}, bf16[64,2048]{1,0:T(8,128)(2,1)}, u32[]{:S(2)}) copy-start(bf16[64,2048]{1,0:T(8,128)(2,1)} %fusion.21) | copy-start | bytes 786436
Sparse Core Ops, SparseCore 0:
  9.5 53.4 all-gather.2
  75.0 70.9 reduce-scatter.3
  169.8 71.9 reduce-scatter.5
  243.8 49.6 all-gather.4
  305.7 70.7 reduce-scatter.7

commit v2 on v1

v2 whole, which is shorter than its diff:
```python
import jax
import jax.numpy as jnp
from jax import lax
from jax.sharding import PartitionSpec as P

EPSILON = 1e-06
PLANE = 4


class Ring:
    def __init__(self):
        self.size = lax.axis_size("inner")
        self.planes = self.size // PLANE
        self.me = lax.axis_index("inner")
        self.z = self.me // PLANE
        self.y = (self.me // 2) % 2
        self.core = self.me % 2

    def along_z(self, values, step):
        perm = [(d, (d + step * PLANE) % self.size) for d in range(self.size)]
        return lax.ppermute(values, "inner", perm)

    def across_y(self, values):
        return lax.ppermute(values, "inner", [(d, d ^ 2) for d in range(self.size)])

    def across_core(self, values):
        return lax.ppermute(values, "inner", [(d, d ^ 1) for d in range(self.size)])


def add(left, right):
    return (left.astype(jnp.float32) + right.astype(jnp.float32)).astype(jnp.bfloat16)


def gather_rows(ring, rows):
    columns = [rows if k == 0 else ring.along_z(rows, k) for k in range(ring.planes)]
    halves = [jnp.concatenate([c, ring.across_y(c)], axis=0) for c in columns]
    return [jnp.concatenate([h, ring.across_core(h)], axis=0) for h in halves]


def scatter_sum(ring, chunks):
    rows = chunks[0].shape[0] // PLANE
    total = None
    for k in range(ring.planes - 1, -1, -1):
        chunk = chunks[k]
        half = add(chunk[: 2 * rows], ring.across_core(chunk[2 * rows :]))
        part = add(half[:rows], ring.across_y(half[rows:]))
        if k:
            part = ring.along_z(part, -k)
        part = part.astype(jnp.float32)
        total = part if total is None else total + part
    return total


def gate_table(routes, gates, experts):
    named = routes[:, :, None] == jnp.arange(experts, dtype=jnp.int32)[None, None, :]
    return jnp.sum(jnp.where(named, gates[:, :, None], 0.0), axis=1)


def gate_columns(ring, tables):
    layers, rows, experts = tables.shape
    every = lax.all_gather(tables, "inner", axis=0)
    mine = lax.dynamic_index_in_dim(every, ring.me, axis=3, keepdims=False)
    step = jnp.arange(ring.planes, dtype=jnp.int32)[:, None, None]
    core = jnp.arange(2, dtype=jnp.int32)[None, :, None]
    y = jnp.arange(2, dtype=jnp.int32)[None, None, :]
    source = ((ring.z - step) % ring.planes) * PLANE + (ring.y ^ y) * 2 + (ring.core ^ core)
    return jnp.take(mine, source.reshape(-1), axis=0).transpose(1, 0, 2).reshape(layers, ring.planes, PLANE * rows, 1)


def normed(values, gain):
    widened = values.astype(jnp.float32)
    inverse = lax.rsqrt(jnp.mean(widened * widened, axis=-1, keepdims=True) + EPSILON)
    return (widened * inverse * gain).astype(jnp.bfloat16)


def expert(rows, gate_column, gate_up, down):
    width = down.shape[0]
    projected = jnp.dot(rows, gate_up, preferred_element_type=jnp.float32)
    hidden = (jax.nn.silu(projected[:, :width]) * projected[:, width:]).astype(jnp.bfloat16)
    out = jnp.dot(hidden, down, preferred_element_type=jnp.float32)
    return (out * gate_column).astype(jnp.bfloat16)


def routed(ring, rows, columns, gate_up, down):
    chunks = gather_rows(ring, rows)
    return scatter_sum(ring, [expert(c, columns[k], gate_up, down) for k, c in enumerate(chunks)])


def plane_weight(ring, weight):
    pair = jnp.concatenate([weight, ring.across_y(weight)], axis=0)
    return jnp.concatenate([pair, ring.across_core(pair)], axis=0)


def merge(ring, merged_in, weight):
    rows, features = merged_in.shape
    blocks = merged_in.reshape(rows, ring.planes, 2, 2, features // ring.size)
    blocks = jnp.where(ring.y == 1, blocks[:, :, ::-1], blocks)
    blocks = jnp.where(ring.core == 1, blocks[:, :, :, ::-1], blocks)
    by_plane = blocks.transpose(1, 0, 3, 2, 4).reshape(ring.planes, rows, features // ring.planes)
    slices = []
    for k in range(ring.planes):
        piece = lax.dynamic_index_in_dim(by_plane, (ring.z + k) % ring.planes, axis=0, keepdims=False)
        slices.append(ring.along_z(piece, k) if k else piece)
    partial = jnp.dot(jnp.concatenate(slices, axis=0), weight, preferred_element_type=jnp.float32)
    total = partial[:rows]
    for k in range(1, ring.planes):
        part = partial[k * rows : (k + 1) * rows].astype(jnp.bfloat16)
        total = total + ring.along_z(part, -k).astype(jnp.float32)
    return total


def local(
    hidden_rows,
    token_embed,
    first_routes,
    first_gates,
    first_gate_up,
    first_down,
    second_routes,
    second_gates,
    second_gate_up,
    second_down,
    hidden_gain,
    embed_gain,
    merge_weight,
):
    ring = Ring()
    tables = jnp.stack(
        [gate_table(first_routes, first_gates, ring.size), gate_table(second_routes, second_gates, ring.size)]
    )
    columns = gate_columns(ring, tables)
    weight = plane_weight(ring, merge_weight)
    first = routed(ring, hidden_rows, columns[0], first_gate_up[0], first_down[0])
    after_first = (hidden_rows.astype(jnp.float32) + first).astype(jnp.bfloat16)
    merged_in = jnp.concatenate([normed(after_first, hidden_gain), normed(token_embed, embed_gain)], axis=1)
    merged = merge(ring, merged_in, weight)
    after_merge = (after_first.astype(jnp.float32) + jax.nn.silu(merged)).astype(jnp.bfloat16)
    second = routed(ring, after_merge, columns[1], second_gate_up[0], second_down[0])
    return (after_merge.astype(jnp.float32) + second).astype(jnp.bfloat16)


def solution(mesh):
    rows = P(("groups", "inner"), None)
    weight = P("inner", None, None)
    return jax.shard_map(
        local,
        mesh=mesh,
        in_specs=(rows, rows, rows, rows, weight, weight, rows, rows, weight, weight, P(), P(), P("inner", None)),
        out_specs=rows,
        check_vma=False,
    )
```

time: 385 us -> 260 us (0.68)
  waiting for transfers between devices: 303 us -> 133 us
  starting transfers between devices: 0.17 us -> 43.3 us
  between operations: 13.3 us -> 0.98 us
  local copies, waits for them, and re-layouts: 1.73 us -> 10.8 us
  blocking collectives: 31.6 us -> 37.5 us
    reduce_scatter x3 -> x0, waiting for transfers between devices: 213 us -> none  [the longest x2 141 us: routed(): return lax.psum_scatter(part, 'inner', scatter_dimension=0, tiled=True)]
    ppermute x0 -> x52, waiting for transfers between devices: none -> 133 us  [the longest x18 70.8 us: along_z(): return lax.ppermute(values, 'inner', perm)]
    all_gather x2 -> x0, waiting for transfers between devices: 88.9 us -> none  [routed(): every = lax.all_gather(rows, 'inner', axis=0, tiled=True)]
    ppermute x0 -> x52, starting transfers between devices: none -> 43.3 us  [the longest x18 22.3 us: along_z(): return lax.ppermute(values, 'inner', perm)]
    all_gather x0 -> x1, blocking collectives: none -> 37.5 us  [gate_columns(): every = lax.all_gather(tables, 'inner', axis=0)]
    all_to_all x2 -> x0, blocking collectives: 31.6 us -> none  [the longest x1 18 us: local(): lax.all_to_all(merged_in, 'inner', split_axis=1, concat_axis=0, tiled=True)]
    rev x0 -> x1, local copies, waits for them, and re-layouts: none -> 4.84 us  [merge(): blocks = jnp.where(ring.y == 1, blocks[:, :, ::-1], blocks)]
    dot_general x2 -> x8, matrix products: 8.72 us -> 6.07 us  [expert(): out = jnp.dot(hidden, down, preferred_element_type=jnp.float32)]
  transfers between devices with their start and end apart: 5 -> 52, of which waited for: 5 -> 20; matrix products, arithmetic and copies ran while one was open for 1% -> 15% of each run, Pallas kernels for 0% -> 0%
where the time goes in v2:
time: 260 us
  waiting for transfers between devices  133 us (51%)
  starting transfers between devices  43.3 us (17%)
  blocking collectives  37.5 us (14%)
  matrix products  23.8 us (9%)
  local copies, waits for them, and re-layouts  10.8 us (4%)
  other arithmetic  9.81 us (4%)
    ppermute x18, waiting for transfers between devices, along_z(): return lax.ppermute(values, 'inner', perm)  70.8 us
    ppermute x17, waiting for transfers between devices, across_y(): return lax.ppermute(values, 'inner', [(d, d ^ 2) for d in range(self.size)])  62.6 us
    all_gather x1, blocking collectives, gate_columns(): every = lax.all_gather(tables, 'inner', axis=0)  37.5 us
    ppermute x18, starting transfers between devices, along_z(): return lax.ppermute(values, 'inner', perm)  22.3 us
    ppermute x17, starting transfers between devices, across_y(): return lax.ppermute(values, 'inner', [(d, d ^ 2) for d in range(self.size)])  16.9 us
    dot_general x8, matrix products, expert(): projected = jnp.dot(rows, gate_up, preferred_element_type=jnp.float32)  14.7 us
    dot_general x8, matrix products, expert(): out = jnp.dot(hidden, down, preferred_element_type=jnp.float32)  6.07 us
  transfers between devices with their start and end apart: 52, of which 20 were waited for; matrix products, arithmetic and copies ran while one was open for 15% of the time, Pallas kernels for 0%

profile of v2, /device:TPU:0, one launch (start us, length us, event | category | flops | bytes accessed | tf_op | source)
XLA Modules:
  0.0 259.6 jit_solution(1861914210326593368)
XLA Ops:
  0.0 3.0 %collective-permute-start.18 = (bf16[64,2048]{1,0:T(8,128)(2,1)}, bf16[64,2048]{1,0:T(8,128)(2,1)S(1)}, u32[]{:S(2)}, u32[]{:S(2)}) collective-permute-start(bf16[64,2048]{1,0:T(8,128)(2,1)} %param.13), channel_id=1, source_target_pairs={{0,2},{1,3},{2,0},{3,1},{4,6},{5,7},{6,4},{7,5},{8,10},{9,11},{10,... | collective-permute-start | bytes 786440 | tf_op jit(solution)/shard_map/ppermute | solution.py:24
  3.0 1.6 collective-permute-start.12
  4.5 2.6 collective-permute-start.6
  7.1 1.3 collective-permute-start
  10.8 37.5 %all-gather = f32[32,64,16]{1,2,0:T(8,128)S(1)} all-gather(f32[2,64,16]{1,2,0:T(8,128)S(1)} %pad_maximum_fusion.10), channel_id=2, replica_groups=mesh['groups'=2,'inner'=16] {'inner'}, dimensions={0}, use_global_device_ids=true | all-gather | bytes 139264 | tf_op jit(solution)/shard_map/all_gather | solution.py:61
  50.7 2.0 collective-permute-start.7
  54.0 5.4 %collective-permute-done.13 = bf16[64,2048]{1,0:T(8,128)(2,1)S(1)} collective-permute-done((bf16[64,2048]{1,0:T(8,128)(2,1)S(1)}, bf16[64,2048]{1,0:T(8,128)(2,1)S(1)}, u32[]{:S(2)}, u32[]{:S(2)}) %collective-permute-start.13) | collective-permute-done | bytes 262176 | tf_op jit(solution)/shard_map/ppermute | solution.py:24
  59.5 5.5 %collective-permute-done.7 = bf16[64,2048]{1,0:T(8,128)(2,1)S(1)} collective-permute-done((bf16[64,2048]{1,0:T(8,128)(2,1)S(1)}, bf16[64,2048]{1,0:T(8,128)(2,1)S(1)}, u32[]{:S(2)}, u32[]{:S(2)}) %collective-permute-start.7) | collective-permute-done | bytes 262176 | tf_op jit(solution)/shard_map/ppermute | solution.py:24
  65.1 4.9 %collective-permute-done.1 = bf16[64,2048]{1,0:T(8,128)(2,1)S(1)} collective-permute-done((bf16[64,2048]{1,0:T(8,128)(2,1)S(1)}, bf16[64,2048]{1,0:T(8,128)(2,1)S(1)}, u32[]{:S(2)}, u32[]{:S(2)}) %collective-permute-start.1) | collective-permute-done | bytes 262176 | tf_op jit(solution)/shard_map/ppermute | solution.py:24
  70.2 3.5 %fusion.14 = f32[256,1024]{1,0:T(8,128)S(1)} fusion(bf16[1,2048,1024]{2,1,0:T(8,128)(2,1)} %param.17, bf16[128,2048]{1,0:T(8,128)(2,1)S(1)} %collective-permute-done.19, bf16[64,2048]{1,0:T(8,128)(2,1)S(1)} %collective-permute-done.18, bf16[64,2048]{1,0:T(8,128)(2,1)S(1)} %copy-done.4), kind=kOutput, calls=%fused_computation.15 | convolution fusion | flops 1076887552 | bytes 6291456 | tf_op jit(solution)/shard_map/dot_general | solution.py:78
  75.8 1.3 fusion.16
  78.5 1.3 fusion.18
  80.7 1.3 fusion.20
  84.0 1.8 collective-permute-start.16
  86.5 1.8 collective-permute-start.4
  88.3 10.0 %collective-permute-done.16 = bf16[64,2048]{1,0:T(8,128)(2,1)S(1)} collective-permute-done((bf16[64,2048]{1,0:T(8,128)(2,1)S(1)}, bf16[64,2048]{1,0:T(8,128)(2,1)S(1)}, u32[]{:S(2)}, u32[]{:S(2)}) %collective-permute-start.16) | collective-permute-done | bytes 262176 | tf_op jit(solution)/shard_map/ppermute | solution.py:24
  98.5 5.5 %collective-permute-done.10 = bf16[64,2048]{1,0:T(8,128)(2,1)S(1)} collective-permute-done((bf16[64,2048]{1,0:T(8,128)(2,1)S(1)}, bf16[64,2048]{1,0:T(8,128)(2,1)S(1)}, u32[]{:S(2)}, u32[]{:S(2)}) %collective-permute-start.10) | collective-permute-done | bytes 262176 | tf_op jit(solution)/shard_map/ppermute | solution.py:24
  104.1 4.5 %collective-permute-done.4 = bf16[64,2048]{1,0:T(8,128)(2,1)S(1)} collective-permute-done((bf16[64,2048]{1,0:T(8,128)(2,1)S(1)}, bf16[64,2048]{1,0:T(8,128)(2,1)S(1)}, u32[]{:S(2)}, u32[]{:S(2)}) %collective-permute-start.4) | collective-permute-done | bytes 262176 | tf_op jit(solution)/shard_map/ppermute | solution.py:24
  109.0 1.4 pad_maximum_fusion
  110.5 10.4 %collective-permute-done.11 = bf16[64,2048]{1,0:T(8,128)(2,1)S(1)} collective-permute-done((bf16[64,2048]{1,0:T(8,128)(2,1)S(1)}, bf16[64,2048]{1,0:T(8,128)(2,1)S(1)}, u32[]{:S(2)}, u32[]{:S(2)}) %collective-permute-start.11) | collective-permute-done | bytes 262176 | tf_op jit(solution)/shard_map/ppermute | solution.py:21
  121.9 1.4 copy.42
  123.3 4.8 %rev.6 = bf16[64,4,2,2,256]{4,2,3,0,1:T(2,128)(2,1)S(1)} reverse(bf16[64,4,2,2,256]{4,2,3,0,1:T(2,128)(2,1)} %copy.42), dimensions={2} | reverse | bytes 1048576 | tf_op jit(solution)/shard_map/rev | solution.py:97
  129.8 2.2 collective-permute-start.23
  132.0 1.9 collective-permute-start.22
  133.9 1.5 collective-permute-done.24
  135.4 8.6 %collective-permute-done.23 = bf16[64,1024]{1,0:T(8,128)(2,1)S(1)} collective-permute-done((bf16[64,1024]{1,0:T(8,128)(2,1)S(1)}, bf16[64,1024]{1,0:T(8,128)(2,1)S(1)}, u32[]{:S(2)}, u32[]{:S(2)}) %collective-permute-start.23) | collective-permute-done | bytes 131104 | tf_op jit(solution)/shard_map/ppermute | solution.py:21
  144.0 3.0 %fusion.140 = (bf16[256,2048]{1,0:T(8,128)(2,1)S(1)}, f32[256,2048]{1,0:T(8,128)S(1)}) fusion(bf16[512,2048]{1,0:T(8,128)(2,1)} %collective-permute-done.26, bf16[256,2048]{1,0:T(8,128)(2,1)} %collective-permute-done.25, bf16[256,2048]{1,0:T(8,128)(2,1)} %param.25, bf16[64,1024]{1,0:T(8,128)(2,1)S(1)} %collective-permute-done.24, ...), kind=kOutput, calls=%fused_computation.217 | convolution fusion | flops 1088946176 | bytes 7864320 | tf_op jit(solution)/shard_map/dot_general | solution.py:104
  147.1 2.0 collective-permute-start.29
  149.9 11.3 %collective-permute-done.27 = bf16[64,2048]{1,0:T(8,128)(2,1)S(1)} collective-permute-done((bf16[64,2048]{1,0:T(8,128)(2,1)S(1)}, bf16[64,2048]{1,0:T(8,128)(2,1)S(1)}, u32[]{:S(2)}, u32[]{:S(2)}) %collective-permute-start.27) | collective-permute-done | bytes 262176 | tf_op jit(solution)/shard_map/ppermute | solution.py:21
  162.2 9.0 %collective-permute-done.28 = bf16[64,2048]{1,0:T(8,128)(2,1)S(1)} collective-permute-done((bf16[64,2048]{1,0:T(8,128)(2,1)S(1)}, bf16[64,2048]{1,0:T(8,128)(2,1)S(1)}, u32[]{:S(2)}, u32[]{:S(2)}) %collective-permute-start.28) | collective-permute-done | bytes 262176 | tf_op jit(solution)/shard_map/ppermute | solution.py:21
  171.6 3.1 %collective-permute-start.36 = (bf16[64,2048]{1,0:T(8,128)(2,1)S(1)}, bf16[64,2048]{1,0:T(8,128)(2,1)S(1)}, u32[]{:S(2)}, u32[]{:S(2)}) collective-permute-start(bf16[64,2048]{1,0:T(8,128)(2,1)S(1)} %fusion.84), channel_id=1, source_target_pairs={{0,8},{1,9},{2,10},{3,11},{4,12},{5,13},{6,14},{7,15},{8,0},{9,1},... | collective-permute-start | bytes 786440 | tf_op jit(solution)/shard_map/ppermute | solution.py:21
  175.7 7.0 %collective-permute-done.42 = bf16[64,2048]{1,0:T(8,128)(2,1)S(1)} collective-permute-done((bf16[64,2048]{1,0:T(8,128)(2,1)S(1)}, bf16[64,2048]{1,0:T(8,128)(2,1)S(1)}, u32[]{:S(2)}, u32[]{:S(2)}) %collective-permute-start.42) | collective-permute-done | bytes 262176 | tf_op jit(solution)/shard_map/ppermute | solution.py:21
  183.3 9.1 %collective-permute-done.36 = bf16[64,2048]{1,0:T(8,128)(2,1)S(1)} collective-permute-done((bf16[64,2048]{1,0:T(8,128)(2,1)S(1)}, bf16[64,2048]{1,0:T(8,128)(2,1)S(1)}, u32[]{:S(2)}, u32[]{:S(2)}) %collective-permute-start.36) | collective-permute-done | bytes 262176 | tf_op jit(solution)/shard_map/ppermute | solution.py:21
  192.8 1.8 collective-permute-start.31
  194.9 6.7 %collective-permute-done.37 = bf16[64,2048]{1,0:T(8,128)(2,1)S(1)} collective-permute-done((bf16[64,2048]{1,0:T(8,128)(2,1)S(1)}, bf16[64,2048]{1,0:T(8,128)(2,1)S(1)}, u32[]{:S(2)}, u32[]{:S(2)}) %collective-permute-start.37) | collective-permute-done | bytes 262176 | tf_op jit(solution)/shard_map/ppermute | solution.py:24
  201.8 3.9 %collective-permute-done.31 = bf16[64,2048]{1,0:T(8,128)(2,1)S(1)} collective-permute-done((bf16[64,2048]{1,0:T(8,128)(2,1)S(1)}, bf16[64,2048]{1,0:T(8,128)(2,1)S(1)}, u32[]{:S(2)}, u32[]{:S(2)}) %collective-permute-start.31) | collective-permute-done | bytes 262176 | tf_op jit(solution)/shard_map/ppermute | solution.py:24
  205.9 3.6 %fusion.6 = f32[256,1024]{1,0:T(8,128)S(1)} fusion(bf16[1,2048,1024]{2,1,0:T(8,128)(2,1)} %param.21, bf16[128,2048]{1,0:T(8,128)(2,1)S(1)} %collective-permute-done.49, bf16[64,2048]{1,0:T(8,128)(2,1)S(1)} %collective-permute-done.48, bf16[64,2048]{1,0:T(8,128)(2,1)S(1)} %fusion.84), kind=kOutput, calls=%fused_computation.7 | convolution fusion | flops 1076887552 | bytes 6291456 | tf_op jit(solution)/shard_map/dot_general | solution.py:78
  211.6 1.3 fusion.8
  214.2 1.3 fusion.10
  216.5 1.3 fusion.12
  219.7 1.8 collective-permute-start.46
  222.2 1.8 collective-permute-start.34
  224.0 10.0 %collective-permute-done.46 = bf16[64,2048]{1,0:T(8,128)(2,1)S(1)} collective-permute-done((bf16[64,2048]{1,0:T(8,128)(2,1)S(1)}, bf16[64,2048]{1,0:T(8,128)(2,1)S(1)}, u32[]{:S(2)}, u32[]{:S(2)}) %collective-permute-start.46) | collective-permute-done | bytes 262176 | tf_op jit(solution)/shard_map/ppermute | solution.py:24
  234.1 4.2 %collective-permute-start.47 = (bf16[64,2048]{1,0:T(8,128)(2,1)S(1)}, bf16[64,2048]{1,0:T(8,128)(2,1)S(1)}, u32[]{:S(2)}, u32[]{:S(2)}) collective-permute-start(bf16[64,2048]{1,0:T(8,128)(2,1)S(1)} %add_convert_fusion.10), channel_id=1, source_target_pairs={{0,12},{1,13},{2,14},{3,15},{4,0},{5,1},{6,2},{7,3},{8,4},{9,5},{1... | collective-permute-start | bytes 786440 | tf_op jit(solution)/shard_map/ppermute | solution.py:21
  238.3 1.4 collective-permute-done.40
  239.8 4.7 %collective-permute-done.34 = bf16[64,2048]{1,0:T(8,128)(2,1)S(1)} collective-permute-done((bf16[64,2048]{1,0:T(8,128)(2,1)S(1)}, bf16[64,2048]{1,0:T(8,128)(2,1)S(1)}, u32[]{:S(2)}, u32[]{:S(2)}) %collective-permute-start.34) | collective-permute-done | bytes 262176 | tf_op jit(solution)/shard_map/ppermute | solution.py:24
  244.6 1.3 collective-permute-start.35
  245.9 12.8 %collective-permute-done.41 = bf16[64,2048]{1,0:T(8,128)(2,1)S(1)} collective-permute-done((bf16[64,2048]{1,0:T(8,128)(2,1)S(1)}, bf16[64,2048]{1,0:T(8,128)(2,1)S(1)}, u32[]{:S(2)}, u32[]{:S(2)}) %collective-permute-start.41) | collective-permute-done | bytes 262176 | tf_op jit(solution)/shard_map/ppermute | solution.py:21
  (174 shorter events, 29.3 us)
Async XLA Ops:
  0.0 52.7 %collective-permute-start.18 = (bf16[64,2048]{1,0:T(8,128)(2,1)}, bf16[64,2048]{1,0:T(8,128)(2,1)S(1)}, u32[]{:S(2)}, u32[]{:S(2)}) collective-permute-start(bf16[64,2048]{1,0:T(8,128)(2,1)} %param.13), channel_id=1, source_target_pairs={{0,2},{1,3},{2,0},{3,1},{4,6},{5,7},{6,4},{7,5},{8,10},{9,11},{10,... | collective-permute-start | bytes 786440 | tf_op jit(solution)/shard_map/ppermute | solution.py:24
  3.0 47.2 %collective-permute-start.12 = (bf16[64,2048]{1,0:T(8,128)(2,1)}, bf16[64,2048]{1,0:T(8,128)(2,1)S(1)}, u32[]{:S(2)}, u32[]{:S(2)}) collective-permute-start(bf16[64,2048]{1,0:T(8,128)(2,1)} %param.13), channel_id=1, source_target_pairs={{0,4},{1,5},{2,6},{3,7},{4,8},{5,9},{6,10},{7,11},{8,12},{9,13},{1... | collective-permute-start | bytes 786440 | tf_op jit(solution)/shard_map/ppermute | solution.py:21
  4.5 46.2 %collective-permute-start.6 = (bf16[64,2048]{1,0:T(8,128)(2,1)}, bf16[64,2048]{1,0:T(8,128)(2,1)S(1)}, u32[]{:S(2)}, u32[]{:S(2)}) collective-permute-start(bf16[64,2048]{1,0:T(8,128)(2,1)} %param.13), channel_id=1, source_target_pairs={{0,8},{1,9},{2,10},{3,11},{4,12},{5,13},{6,14},{7,15},{8,0},{9,1},... | collective-permute-start | bytes 786440 | tf_op jit(solution)/shard_map/ppermute | solution.py:21
  7.1 46.7 %collective-permute-start = (bf16[64,2048]{1,0:T(8,128)(2,1)}, bf16[64,2048]{1,0:T(8,128)(2,1)S(1)}, u32[]{:S(2)}, u32[]{:S(2)}) collective-permute-start(bf16[64,2048]{1,0:T(8,128)(2,1)} %param.13), channel_id=1, source_target_pairs={{0,12},{1,13},{2,14},{3,15},{4,0},{5,1},{6,2},{7,3},{8,4},{9,5},{1... | collective-permute-start | bytes 786440 | tf_op jit(solution)/shard_map/ppermute | solution.py:21
  8.5 100.5 %collective-permute-start.25 = (bf16[256,2048]{1,0:T(8,128)(2,1)}, bf16[256,2048]{1,0:T(8,128)(2,1)}, u32[]{:S(2)}, u32[]{:S(2)}) collective-permute-start(bf16[256,2048]{1,0:T(8,128)(2,1)} %param.25), channel_id=1, source_target_pairs={{0,2},{1,3},{2,0},{3,1},{4,6},{5,7},{6,4},{7,5},{8,10},{9,11},{10,... | collective-permute-start | bytes 3145736 | tf_op jit(solution)/shard_map/ppermute | solution.py:24
  50.2 9.2 %collective-permute-start.13 = (bf16[64,2048]{1,0:T(8,128)(2,1)S(1)}, bf16[64,2048]{1,0:T(8,128)(2,1)S(1)}, u32[]{:S(2)}, u32[]{:S(2)}) collective-permute-start(bf16[64,2048]{1,0:T(8,128)(2,1)S(1)} %collective-permute-done.12), channel_id=1, source_target_pairs={{0,2},{1,3},{2,0},{3,1},{4,6},{5,7},{6,4},{7,5},{8,10},{9,11},{10,... | collective-permute-start | bytes 786440 | tf_op jit(solution)/shard_map/ppermute | solution.py:24
  50.7 14.2 %collective-permute-start.7 = (bf16[64,2048]{1,0:T(8,128)(2,1)S(1)}, bf16[64,2048]{1,0:T(8,128)(2,1)S(1)}, u32[]{:S(2)}, u32[]{:S(2)}) collective-permute-start(bf16[64,2048]{1,0:T(8,128)(2,1)S(1)} %collective-permute-done.6), channel_id=1, source_target_pairs={{0,2},{1,3},{2,0},{3,1},{4,6},{5,7},{6,4},{7,5},{8,10},{9,11},{10,... | collective-permute-start | bytes 786440 | tf_op jit(solution)/shard_map/ppermute | solution.py:24
  53.7 16.4 %collective-permute-start.19 = (bf16[128,2048]{1,0:T(8,128)(2,1)S(1)}, bf16[128,2048]{1,0:T(8,128)(2,1)S(1)}, u32[]{:S(2)}, u32[]{:S(2)}) collective-permute-start(bf16[128,2048]{1,0:T(8,128)(2,1)S(1)} %pad_maximum_fusion.4), channel_id=1, source_target_pairs={{0,1},{1,0},{2,3},{3,2},{4,5},{5,4},{6,7},{7,6},{8,9},{9,8},{10,11... | collective-permute-start | bytes 1572872 | tf_op jit(solution)/shard_map/ppermute | solution.py:27
  53.8 16.2 %collective-permute-start.1 = (bf16[64,2048]{1,0:T(8,128)(2,1)S(1)}, bf16[64,2048]{1,0:T(8,128)(2,1)S(1)}, u32[]{:S(2)}, u32[]{:S(2)}) collective-permute-start(bf16[64,2048]{1,0:T(8,128)(2,1)S(1)} %collective-permute-done), channel_id=1, source_target_pairs={{0,2},{1,3},{2,0},{3,1},{4,6},{5,7},{6,4},{7,5},{8,10},{9,11},{10,... | collective-permute-start | bytes 786440 | tf_op jit(solution)/shard_map/ppermute | solution.py:24
  59.4 15.6 %collective-permute-start.14 = (bf16[128,2048]{1,0:T(8,128)(2,1)S(1)}, bf16[128,2048]{1,0:T(8,128)(2,1)S(1)}, u32[]{:S(2)}, u32[]{:S(2)}) collective-permute-start(bf16[128,2048]{1,0:T(8,128)(2,1)S(1)} %pad_maximum_fusion.3), channel_id=1, source_target_pairs={{0,1},{1,0},{2,3},{3,2},{4,5},{5,4},{6,7},{7,6},{8,9},{9,8},{10,11... | collective-permute-start | bytes 1572872 | tf_op jit(solution)/shard_map/ppermute | solution.py:27
  65.0 13.5 %collective-permute-start.8 = (bf16[128,2048]{1,0:T(8,128)(2,1)S(1)}, bf16[128,2048]{1,0:T(8,128)(2,1)S(1)}, u32[]{:S(2)}, u32[]{:S(2)}) collective-permute-start(bf16[128,2048]{1,0:T(8,128)(2,1)S(1)} %pad_maximum_fusion.2), channel_id=1, source_target_pairs={{0,1},{1,0},{2,3},{3,2},{4,5},{5,4},{6,7},{7,6},{8,9},{9,8},{10,11... | collective-permute-start | bytes 1572872 | tf_op jit(solution)/shard_map/ppermute | solution.py:27
  70.1 10.6 %collective-permute-start.2 = (bf16[128,2048]{1,0:T(8,128)(2,1)S(1)}, bf16[128,2048]{1,0:T(8,128)(2,1)S(1)}, u32[]{:S(2)}, u32[]{:S(2)}) collective-permute-start(bf16[128,2048]{1,0:T(8,128)(2,1)S(1)} %pad_maximum_fusion.1), channel_id=1, source_target_pairs={{0,1},{1,0},{2,3},{3,2},{4,5},{5,4},{6,7},{7,6},{8,9},{9,8},{10,11... | collective-permute-start | bytes 1572872 | tf_op jit(solution)/shard_map/ppermute | solution.py:27
  74.5 8.8 %collective-permute-start.20 = (bf16[128,2048]{1,0:T(8,128)(2,1)S(1)}, bf16[128,2048]{1,0:T(8,128)(2,1)S(1)}, u32[]{:S(2)}, u32[]{:S(2)}) collective-permute-start(bf16[128,2048]{1,0:T(8,128)(2,1)S(1)} %slice.290), channel_id=1, source_target_pairs={{0,1},{1,0},{2,3},{3,2},{4,5},{5,4},{6,7},{7,6},{8,9},{9,8},{10,11... | collective-permute-start | bytes 1572872 | tf_op jit(solution)/shard_map/ppermute | solution.py:27
  77.9 5.9 %collective-permute-start.15 = (bf16[128,2048]{1,0:T(8,128)(2,1)S(1)}, bf16[128,2048]{1,0:T(8,128)(2,1)S(1)}, u32[]{:S(2)}, u32[]{:S(2)}) collective-permute-start(bf16[128,2048]{1,0:T(8,128)(2,1)S(1)} %slice.283), channel_id=1, source_target_pairs={{0,1},{1,0},{2,3},{3,2},{4,5},{5,4},{6,7},{7,6},{8,9},{9,8},{10,11... | collective-permute-start | bytes 1572872 | tf_op jit(solution)/shard_map/ppermute | solution.py:27
  83.5 27.0 %collective-permute-start.21 = (bf16[64,2048]{1,0:T(8,128)(2,1)S(1)}, bf16[64,2048]{1,0:T(8,128)(2,1)S(1)}, u32[]{:S(2)}, u32[]{:S(2)}) collective-permute-start(bf16[64,2048]{1,0:T(8,128)(2,1)S(1)} %slice.292), channel_id=1, source_target_pairs={{0,2},{1,3},{2,0},{3,1},{4,6},{5,7},{6,4},{7,5},{8,10},{9,11},{10,... | collective-permute-start | bytes 786440 | tf_op jit(solution)/shard_map/ppermute | solution.py:24
  84.0 14.3 %collective-permute-start.16 = (bf16[64,2048]{1,0:T(8,128)(2,1)S(1)}, bf16[64,2048]{1,0:T(8,128)(2,1)S(1)}, u32[]{:S(2)}, u32[]{:S(2)}) collective-permute-start(bf16[64,2048]{1,0:T(8,128)(2,1)S(1)} %slice.285), channel_id=1, source_target_pairs={{0,2},{1,3},{2,0},{3,1},{4,6},{5,7},{6,4},{7,5},{8,10},{9,11},{10,... | collective-permute-start | bytes 786440 | tf_op jit(solution)/shard_map/ppermute | solution.py:24
  86.0 18.0 %collective-permute-start.10 = (bf16[64,2048]{1,0:T(8,128)(2,1)S(1)}, bf16[64,2048]{1,0:T(8,128)(2,1)S(1)}, u32[]{:S(2)}, u32[]{:S(2)}) collective-permute-start(bf16[64,2048]{1,0:T(8,128)(2,1)S(1)} %slice.278), channel_id=1, source_target_pairs={{0,2},{1,3},{2,0},{3,1},{4,6},{5,7},{6,4},{7,5},{8,10},{9,11},{10,... | collective-permute-start | bytes 786440 | tf_op jit(solution)/shard_map/ppermute | solution.py:24
  86.5 22.1 %collective-permute-start.4 = (bf16[64,2048]{1,0:T(8,128)(2,1)S(1)}, bf16[64,2048]{1,0:T(8,128)(2,1)S(1)}, u32[]{:S(2)}, u32[]{:S(2)}) collective-permute-start(bf16[64,2048]{1,0:T(8,128)(2,1)S(1)} %slice.271), channel_id=1, source_target_pairs={{0,2},{1,3},{2,0},{3,1},{4,6},{5,7},{6,4},{7,5},{8,10},{9,11},{10,... | collective-permute-start | bytes 786440 | tf_op jit(solution)/shard_map/ppermute | solution.py:24
  98.4 12.1 %collective-permute-start.17 = (bf16[64,2048]{1,0:T(8,128)(2,1)S(1)}, bf16[64,2048]{1,0:T(8,128)(2,1)S(1)}, u32[]{:S(2)}, u32[]{:S(2)}) collective-permute-start(bf16[64,2048]{1,0:T(8,128)(2,1)S(1)} %add_convert_fusion.15), channel_id=1, source_target_pairs={{0,12},{1,13},{2,14},{3,15},{4,0},{5,1},{6,2},{7,3},{8,4},{9,5},{1... | collective-permute-start | bytes 786440 | tf_op jit(solution)/shard_map/ppermute | solution.py:21
  104.0 16.9 %collective-permute-start.11 = (bf16[64,2048]{1,0:T(8,128)(2,1)S(1)}, bf16[64,2048]{1,0:T(8,128)(2,1)S(1)}, u32[]{:S(2)}, u32[]{:S(2)}) collective-permute-start(bf16[64,2048]{1,0:T(8,128)(2,1)S(1)} %add_convert_fusion.16), channel_id=1, source_target_pairs={{0,8},{1,9},{2,10},{3,11},{4,12},{5,13},{6,14},{7,15},{8,0},{9,1},... | collective-permute-start | bytes 786440 | tf_op jit(solution)/shard_map/ppermute | solution.py:21
  108.8 12.1 %collective-permute-start.5 = (bf16[64,2048]{1,0:T(8,128)(2,1)S(1)}, bf16[64,2048]{1,0:T(8,128)(2,1)S(1)}, u32[]{:S(2)}, u32[]{:S(2)}) collective-permute-start(bf16[64,2048]{1,0:T(8,128)(2,1)S(1)} %add_convert_fusion.17), channel_id=1, source_target_pairs={{0,4},{1,5},{2,6},{3,7},{4,8},{5,9},{6,10},{7,11},{8,12},{9,13},{1... | collective-permute-start | bytes 786440 | tf_op jit(solution)/shard_map/ppermute | solution.py:21
  110.4 33.6 %collective-permute-start.26 = (bf16[512,2048]{1,0:T(8,128)(2,1)S(1)}, bf16[512,2048]{1,0:T(8,128)(2,1)}, u32[]{:S(2)}, u32[]{:S(2)}) collective-permute-start(bf16[512,2048]{1,0:T(8,128)(2,1)S(1)} %pad_maximum_fusion), channel_id=1, source_target_pairs={{0,1},{1,0},{2,3},{3,2},{4,5},{5,4},{6,7},{7,6},{8,9},{9,8},{10,11... | collective-permute-start | bytes 6291464 | tf_op jit(solution)/shard_map/ppermute | solution.py:27
  129.7 5.7 %collective-permute-start.24 = (bf16[64,1024]{1,0:T(8,128)(2,1)S(1)}, bf16[64,1024]{1,0:T(8,128)(2,1)S(1)}, u32[]{:S(2)}, u32[]{:S(2)}) collective-permute-start(bf16[64,1024]{1,0:T(8,128)(2,1)S(1)} %get-tuple-element.19), channel_id=1, source_target_pairs={{0,12},{1,13},{2,14},{3,15},{4,0},{5,1},{6,2},{7,3},{8,4},{9,5},{1... | collective-permute-start | bytes 393224 | tf_op jit(solution)/shard_map/ppermute | solution.py:21
  129.8 14.2 %collective-permute-start.23 = (bf16[64,1024]{1,0:T(8,128)(2,1)S(1)}, bf16[64,1024]{1,0:T(8,128)(2,1)S(1)}, u32[]{:S(2)}, u32[]{:S(2)}) collective-permute-start(bf16[64,1024]{1,0:T(8,128)(2,1)S(1)} %get-tuple-element.20), channel_id=1, source_target_pairs={{0,8},{1,9},{2,10},{3,11},{4,12},{5,13},{6,14},{7,15},{8,0},{9,1},... | collective-permute-start | bytes 393224 | tf_op jit(solution)/shard_map/ppermute | solution.py:21
  132.0 12.0 %collective-permute-start.22 = (bf16[64,1024]{1,0:T(8,128)(2,1)S(1)}, bf16[64,1024]{1,0:T(8,128)(2,1)S(1)}, u32[]{:S(2)}, u32[]{:S(2)}) collective-permute-start(bf16[64,1024]{1,0:T(8,128)(2,1)S(1)} %get-tuple-element.21), channel_id=1, source_target_pairs={{0,4},{1,5},{2,6},{3,7},{4,8},{5,9},{6,10},{7,11},{8,12},{9,13},{1... | collective-permute-start | bytes 393224 | tf_op jit(solution)/shard_map/ppermute | solution.py:21
  147.1 14.1 %collective-permute-start.27 = (bf16[64,2048]{1,0:T(8,128)(2,1)S(1)}, bf16[64,2048]{1,0:T(8,128)(2,1)S(1)}, u32[]{:S(2)}, u32[]{:S(2)}) collective-permute-start(bf16[64,2048]{1,0:T(8,128)(2,1)S(1)} %get-tuple-element.15), channel_id=1, source_target_pairs={{0,12},{1,13},{2,14},{3,15},{4,0},{5,1},{6,2},{7,3},{8,4},{9,5},{1... | collective-permute-start | bytes 786440 | tf_op jit(solution)/shard_map/ppermute | solution.py:21
  147.1 15.1 %collective-permute-start.29 = (bf16[64,2048]{1,0:T(8,128)(2,1)S(1)}, bf16[64,2048]{1,0:T(8,128)(2,1)S(1)}, u32[]{:S(2)}, u32[]{:S(2)}) collective-permute-start(bf16[64,2048]{1,0:T(8,128)(2,1)S(1)} %get-tuple-element.16), channel_id=1, source_target_pairs={{0,4},{1,5},{2,6},{3,7},{4,8},{5,9},{6,10},{7,11},{8,12},{9,13},{1... | collective-permute-start | bytes 786440 | tf_op jit(solution)/shard_map/ppermute | solution.py:21
  149.1 22.1 %collective-permute-start.28 = (bf16[64,2048]{1,0:T(8,128)(2,1)S(1)}, bf16[64,2048]{1,0:T(8,128)(2,1)S(1)}, u32[]{:S(2)}, u32[]{:S(2)}) collective-permute-start(bf16[64,2048]{1,0:T(8,128)(2,1)S(1)} %get-tuple-element.17), channel_id=1, source_target_pairs={{0,8},{1,9},{2,10},{3,11},{4,12},{5,13},{6,14},{7,15},{8,0},{9,1},... | collective-permute-start | bytes 786440 | tf_op jit(solution)/shard_map/ppermute | solution.py:21
  171.5 11.2 %collective-permute-start.42 = (bf16[64,2048]{1,0:T(8,128)(2,1)S(1)}, bf16[64,2048]{1,0:T(8,128)(2,1)S(1)}, u32[]{:S(2)}, u32[]{:S(2)}) collective-permute-start(bf16[64,2048]{1,0:T(8,128)(2,1)S(1)} %fusion.84), channel_id=1, source_target_pairs={{0,4},{1,5},{2,6},{3,7},{4,8},{5,9},{6,10},{7,11},{8,12},{9,13},{1... | collective-permute-start | bytes 786440 | tf_op jit(solution)/shard_map/ppermute | solution.py:21
  171.6 20.9 %collective-permute-start.36 = (bf16[64,2048]{1,0:T(8,128)(2,1)S(1)}, bf16[64,2048]{1,0:T(8,128)(2,1)S(1)}, u32[]{:S(2)}, u32[]{:S(2)}) collective-permute-start(bf16[64,2048]{1,0:T(8,128)(2,1)S(1)} %fusion.84), channel_id=1, source_target_pairs={{0,8},{1,9},{2,10},{3,11},{4,12},{5,13},{6,14},{7,15},{8,0},{9,1},... | collective-permute-start | bytes 786440 | tf_op jit(solution)/shard_map/ppermute | solution.py:21
  174.6 18.1 %collective-permute-start.48 = (bf16[64,2048]{1,0:T(8,128)(2,1)S(1)}, bf16[64,2048]{1,0:T(8,128)(2,1)S(1)}, u32[]{:S(2)}, u32[]{:S(2)}) collective-permute-start(bf16[64,2048]{1,0:T(8,128)(2,1)S(1)} %fusion.84), channel_id=1, source_target_pairs={{0,2},{1,3},{2,0},{3,1},{4,6},{5,7},{6,4},{7,5},{8,10},{9,11},{10,... | collective-permute-start | bytes 786440 | tf_op jit(solution)/shard_map/ppermute | solution.py:24
  174.9 17.9 %collective-permute-start.30 = (bf16[64,2048]{1,0:T(8,128)(2,1)S(1)}, bf16[64,2048]{1,0:T(8,128)(2,1)S(1)}, u32[]{:S(2)}, u32[]{:S(2)}) collective-permute-start(bf16[64,2048]{1,0:T(8,128)(2,1)S(1)} %fusion.84), channel_id=1, source_target_pairs={{0,12},{1,13},{2,14},{3,15},{4,0},{5,1},{6,2},{7,3},{8,4},{9,5},{1... | collective-permute-start | bytes 786440 | tf_op jit(solution)/shard_map/ppermute | solution.py:21
  182.7 12.0 %collective-permute-start.43 = (bf16[64,2048]{1,0:T(8,128)(2,1)S(1)}, bf16[64,2048]{1,0:T(8,128)(2,1)S(1)}, u32[]{:S(2)}, u32[]{:S(2)}) collective-permute-start(bf16[64,2048]{1,0:T(8,128)(2,1)S(1)} %collective-permute-done.42), channel_id=1, source_target_pairs={{0,2},{1,3},{2,0},{3,1},{4,6},{5,7},{6,4},{7,5},{8,10},{9,11},{10,... | collective-permute-start | bytes 786440 | tf_op jit(solution)/shard_map/ppermute | solution.py:24
  192.4 9.2 %collective-permute-start.37 = (bf16[64,2048]{1,0:T(8,128)(2,1)S(1)}, bf16[64,2048]{1,0:T(8,128)(2,1)S(1)}, u32[]{:S(2)}, u32[]{:S(2)}) collective-permute-start(bf16[64,2048]{1,0:T(8,128)(2,1)S(1)} %collective-permute-done.36), channel_id=1, source_target_pairs={{0,2},{1,3},{2,0},{3,1},{4,6},{5,7},{6,4},{7,5},{8,10},{9,11},{10,... | collective-permute-start | bytes 786440 | tf_op jit(solution)/shard_map/ppermute | solution.py:24
  192.7 13.1 %collective-permute-start.49 = (bf16[128,2048]{1,0:T(8,128)(2,1)S(1)}, bf16[128,2048]{1,0:T(8,128)(2,1)S(1)}, u32[]{:S(2)}, u32[]{:S(2)}) collective-permute-start(bf16[128,2048]{1,0:T(8,128)(2,1)S(1)} %pad_maximum_fusion.9), channel_id=1, source_target_pairs={{0,1},{1,0},{2,3},{3,2},{4,5},{5,4},{6,7},{7,6},{8,9},{9,8},{10,11... | collective-permute-start | bytes 1572872 | tf_op jit(solution)/shard_map/ppermute | solution.py:27
  192.8 12.9 %collective-permute-start.31 = (bf16[64,2048]{1,0:T(8,128)(2,1)S(1)}, bf16[64,2048]{1,0:T(8,128)(2,1)S(1)}, u32[]{:S(2)}, u32[]{:S(2)}) collective-permute-start(bf16[64,2048]{1,0:T(8,128)(2,1)S(1)} %collective-permute-done.30), channel_id=1, source_target_pairs={{0,2},{1,3},{2,0},{3,1},{4,6},{5,7},{6,4},{7,5},{8,10},{9,11},{10,... | collective-permute-start | bytes 786440 | tf_op jit(solution)/shard_map/ppermute | solution.py:24
  194.7 16.0 %collective-permute-start.44 = (bf16[128,2048]{1,0:T(8,128)(2,1)S(1)}, bf16[128,2048]{1,0:T(8,128)(2,1)S(1)}, u32[]{:S(2)}, u32[]{:S(2)}) collective-permute-start(bf16[128,2048]{1,0:T(8,128)(2,1)S(1)} %pad_maximum_fusion.8), channel_id=1, source_target_pairs={{0,1},{1,0},{2,3},{3,2},{4,5},{5,4},{6,7},{7,6},{8,9},{9,8},{10,11... | collective-permute-start | bytes 1572872 | tf_op jit(solution)/shard_map/ppermute | solution.py:27
  201.7 12.5 %collective-permute-start.38 = (bf16[128,2048]{1,0:T(8,128)(2,1)S(1)}, bf16[128,2048]{1,0:T(8,128)(2,1)S(1)}, u32[]{:S(2)}, u32[]{:S(2)}) collective-permute-start(bf16[128,2048]{1,0:T(8,128)(2,1)S(1)} %pad_maximum_fusion.7), channel_id=1, source_target_pairs={{0,1},{1,0},{2,3},{3,2},{4,5},{5,4},{6,7},{7,6},{8,9},{9,8},{10,11... | collective-permute-start | bytes 1572872 | tf_op jit(solution)/shard_map/ppermute | solution.py:27
  205.8 10.7 %collective-permute-start.32 = (bf16[128,2048]{1,0:T(8,128)(2,1)S(1)}, bf16[128,2048]{1,0:T(8,128)(2,1)S(1)}, u32[]{:S(2)}, u32[]{:S(2)}) collective-permute-start(bf16[128,2048]{1,0:T(8,128)(2,1)S(1)} %pad_maximum_fusion.6), channel_id=1, source_target_pairs={{0,1},{1,0},{2,3},{3,2},{4,5},{5,4},{6,7},{7,6},{8,9},{9,8},{10,11... | collective-permute-start | bytes 1572872 | tf_op jit(solution)/shard_map/ppermute | solution.py:27
  210.3 8.7 %collective-permute-start.50 = (bf16[128,2048]{1,0:T(8,128)(2,1)S(1)}, bf16[128,2048]{1,0:T(8,128)(2,1)S(1)}, u32[]{:S(2)}, u32[]{:S(2)}) collective-permute-start(bf16[128,2048]{1,0:T(8,128)(2,1)S(1)} %slice.322), channel_id=1, source_target_pairs={{0,1},{1,0},{2,3},{3,2},{4,5},{5,4},{6,7},{7,6},{8,9},{9,8},{10,11... | collective-permute-start | bytes 1572872 | tf_op jit(solution)/shard_map/ppermute | solution.py:27
  213.8 5.8 %collective-permute-start.45 = (bf16[128,2048]{1,0:T(8,128)(2,1)S(1)}, bf16[128,2048]{1,0:T(8,128)(2,1)S(1)}, u32[]{:S(2)}, u32[]{:S(2)}) collective-permute-start(bf16[128,2048]{1,0:T(8,128)(2,1)S(1)} %slice.315), channel_id=1, source_target_pairs={{0,1},{1,0},{2,3},{3,2},{4,5},{5,4},{6,7},{7,6},{8,9},{9,8},{10,11... | collective-permute-start | bytes 1572872 | tf_op jit(solution)/shard_map/ppermute | solution.py:27
  219.2 26.7 %collective-permute-start.51 = (bf16[64,2048]{1,0:T(8,128)(2,1)S(1)}, bf16[64,2048]{1,0:T(8,128)(2,1)S(1)}, u32[]{:S(2)}, u32[]{:S(2)}) collective-permute-start(bf16[64,2048]{1,0:T(8,128)(2,1)S(1)} %slice.324), channel_id=1, source_target_pairs={{0,2},{1,3},{2,0},{3,1},{4,6},{5,7},{6,4},{7,5},{8,10},{9,11},{10,... | collective-permute-start | bytes 786440 | tf_op jit(solution)/shard_map/ppermute | solution.py:24
  219.7 14.3 %collective-permute-start.46 = (bf16[64,2048]{1,0:T(8,128)(2,1)S(1)}, bf16[64,2048]{1,0:T(8,128)(2,1)S(1)}, u32[]{:S(2)}, u32[]{:S(2)}) collective-permute-start(bf16[64,2048]{1,0:T(8,128)(2,1)S(1)} %slice.317), channel_id=1, source_target_pairs={{0,2},{1,3},{2,0},{3,1},{4,6},{5,7},{6,4},{7,5},{8,10},{9,11},{10,... | collective-permute-start | bytes 786440 | tf_op jit(solution)/shard_map/ppermute | solution.py:24
  221.7 18.0 %collective-permute-start.40 = (bf16[64,2048]{1,0:T(8,128)(2,1)S(1)}, bf16[64,2048]{1,0:T(8,128)(2,1)S(1)}, u32[]{:S(2)}, u32[]{:S(2)}) collective-permute-start(bf16[64,2048]{1,0:T(8,128)(2,1)S(1)} %slice.310), channel_id=1, source_target_pairs={{0,2},{1,3},{2,0},{3,1},{4,6},{5,7},{6,4},{7,5},{8,10},{9,11},{10,... | collective-permute-start | bytes 786440 | tf_op jit(solution)/shard_map/ppermute | solution.py:24
  222.2 22.2 %collective-permute-start.34 = (bf16[64,2048]{1,0:T(8,128)(2,1)S(1)}, bf16[64,2048]{1,0:T(8,128)(2,1)S(1)}, u32[]{:S(2)}, u32[]{:S(2)}) collective-permute-start(bf16[64,2048]{1,0:T(8,128)(2,1)S(1)} %slice.303), channel_id=1, source_target_pairs={{0,2},{1,3},{2,0},{3,1},{4,6},{5,7},{6,4},{7,5},{8,10},{9,11},{10,... | collective-permute-start | bytes 786440 | tf_op jit(solution)/shard_map/ppermute | solution.py:24
  234.1 11.8 %collective-permute-start.47 = (bf16[64,2048]{1,0:T(8,128)(2,1)S(1)}, bf16[64,2048]{1,0:T(8,128)(2,1)S(1)}, u32[]{:S(2)}, u32[]{:S(2)}) collective-permute-start(bf16[64,2048]{1,0:T(8,128)(2,1)S(1)} %add_convert_fusion.10), channel_id=1, source_target_pairs={{0,12},{1,13},{2,14},{3,15},{4,0},{5,1},{6,2},{7,3},{8,4},{9,5},{1... | collective-permute-start | bytes 786440 | tf_op jit(solution)/shard_map/ppermute | solution.py:21
  239.7 19.0 %collective-permute-start.41 = (bf16[64,2048]{1,0:T(8,128)(2,1)S(1)}, bf16[64,2048]{1,0:T(8,128)(2,1)S(1)}, u32[]{:S(2)}, u32[]{:S(2)}) collective-permute-start(bf16[64,2048]{1,0:T(8,128)(2,1)S(1)} %add_convert_fusion.11), channel_id=1, source_target_pairs={{0,8},{1,9},{2,10},{3,11},{4,12},{5,13},{6,14},{7,15},{8,0},{9,1},... | collective-permute-start | bytes 786440 | tf_op jit(solution)/shard_map/ppermute | solution.py:21
  244.6 14.1 %collective-permute-start.35 = (bf16[64,2048]{1,0:T(8,128)(2,1)S(1)}, bf16[64,2048]{1,0:T(8,128)(2,1)S(1)}, u32[]{:S(2)}, u32[]{:S(2)}) collective-permute-start(bf16[64,2048]{1,0:T(8,128)(2,1)S(1)} %add_convert_fusion.12), channel_id=1, source_target_pairs={{0,4},{1,5},{2,6},{3,7},{4,8},{5,9},{6,10},{7,11},{8,12},{9,13},{1... | collective-permute-start | bytes 786440 | tf_op jit(solution)/shard_map/ppermute | solution.py:21
  (14 other events, 216.6 us)

commit v3 on v2

v3 whole, which is shorter than its diff:
```python
import jax
import jax.numpy as jnp
from jax import lax
from jax.sharding import PartitionSpec as P

EPSILON = 1e-06
PLANE = 4


class Ring:
    def __init__(self):
        self.size = lax.axis_size("inner")
        self.planes = self.size // PLANE
        self.me = lax.axis_index("inner")
        self.z = self.me // PLANE
        self.y = (self.me // 2) % 2
        self.core = self.me % 2

    def along_z(self, values, step):
        perm = [(d, (d + step * PLANE) % self.size) for d in range(self.size)]
        return lax.ppermute(values, "inner", perm)

    def across_y(self, values):
        return lax.ppermute(values, "inner", [(d, d ^ 2) for d in range(self.size)])

    def across_core(self, values):
        return lax.ppermute(values, "inner", [(d, d ^ 1) for d in range(self.size)])


def add(left, right):
    return (left.astype(jnp.float32) + right.astype(jnp.float32)).astype(jnp.bfloat16)


def after(values, *others):
    return lax.optimization_barrier((values, *others))[0]


def nearest_first(planes):
    return sorted(range(planes), key=lambda k: (min(k, planes - k), k))


def gather_rows(ring, rows):
    chunks = {}
    reached = {}
    for k in nearest_first(ring.planes):
        far = min(k, ring.planes - k)
        if far > 1:
            rows = after(rows, *[reached[j] for j in reached if min(j, ring.planes - j) == far - 1])
        column = ring.along_z(rows, k) if k else rows
        if k:
            reached[k] = column
        crossed = ring.across_y(column)
        if k == 0:
            first = crossed
        half = jnp.concatenate([column, crossed], axis=0)
        chunks[k] = jnp.concatenate([half, ring.across_core(half)], axis=0)
    return chunks, first


def scatter_sum(ring, chunks):
    rows = chunks[0].shape[0] // PLANE
    order = nearest_first(ring.planes)
    total = None
    halves = []
    crossed = []
    for k in order[1:] + order[:1]:
        chunk = chunks[k]
        half = add(chunk[: 2 * rows], ring.across_core(chunk[2 * rows :]))
        away = half[rows:]
        if len(crossed) > 1:
            away = after(away, crossed[-2])
        if k == 0 and halves:
            away = after(away, halves[-1])
        other = ring.across_y(away)
        halves.append(half)
        crossed.append(other)
        part = add(half[:rows], other)
        if k:
            part = ring.along_z(part, -k)
        part = part.astype(jnp.float32)
        total = part if total is None else total + part
    return total


def gate_halves(routes, gates, experts):
    named = routes[:, :, None] == jnp.arange(experts, dtype=jnp.int32)[None, None, :]
    table = jnp.sum(jnp.where(named, gates[:, :, None], 0.0), axis=1)
    high = table.astype(jnp.bfloat16)
    low = (table - high.astype(jnp.float32)).astype(jnp.bfloat16)
    spare = -2 * experts % 128
    return jnp.concatenate([high, low, jnp.zeros((routes.shape[0], spare), jnp.bfloat16)], axis=1)


def gate_column(ring, halves):
    lane = jnp.arange(halves.shape[1], dtype=jnp.int32)[None, :]
    mine = (lane == ring.me) | (lane == ring.me + ring.size)
    return jnp.sum(jnp.where(mine, halves.astype(jnp.float32), 0.0), axis=1, keepdims=True)


def normed(values, gain):
    widened = values.astype(jnp.float32)
    inverse = lax.rsqrt(jnp.mean(widened * widened, axis=-1, keepdims=True) + EPSILON)
    return (widened * inverse * gain).astype(jnp.bfloat16)


def expert(rows, gate_column, gate_up, down):
    width = down.shape[0]
    projected = jnp.dot(rows, gate_up, preferred_element_type=jnp.float32)
    hidden = (jax.nn.silu(projected[:, :width]) * projected[:, width:]).astype(jnp.bfloat16)
    out = jnp.dot(hidden, down, preferred_element_type=jnp.float32)
    return (out * gate_column).astype(jnp.bfloat16)


def experts_on(ring, chunks, width, gate_up, down):
    results = {}
    last = None
    for k in nearest_first(ring.planes):
        chunk = chunks[k] if last is None else after(chunks[k], last)
        last = expert(chunk[:, :width], gate_column(ring, chunk[:, width:]), gate_up, down)
        results[k] = last
    return results


def plane_weight(ring, weight, groups):
    rows = weight.shape[0]
    if groups % 2:
        other = ring.across_y(weight)
    else:
        odd = lax.axis_index("groups") % 2
        sent = lax.dynamic_slice_in_dim(weight, odd * (rows // 2), rows // 2, axis=0)
        here = ring.across_y(sent)
        there = lax.ppermute(here, "groups", [(g, g ^ 1) for g in range(groups)])
        other = jnp.where(odd == 0, jnp.concatenate([here, there]), jnp.concatenate([there, here]))
    pair = jnp.where(ring.y == 0, jnp.concatenate([weight, other]), jnp.concatenate([other, weight]))
    sibling = ring.across_core(pair)
    mine = [pair[:rows], sibling[:rows], pair[rows:], sibling[rows:]]
    theirs = [sibling[:rows], pair[:rows], sibling[rows:], pair[rows:]]
    return jnp.where(ring.core == 0, jnp.concatenate(mine), jnp.concatenate(theirs))


def merge(ring, merged_in, weight):
    rows, features = merged_in.shape
    share = features // ring.planes
    total = None
    for k in reversed(nearest_first(ring.planes)):
        piece = lax.dynamic_slice_in_dim(merged_in, (ring.z + k) % ring.planes * share, share, axis=1)
        if k:
            piece = ring.along_z(piece, k)
        product = jnp.dot(piece, weight, preferred_element_type=jnp.float32)
        if k:
            product = ring.along_z(product.astype(jnp.bfloat16), -k).astype(jnp.float32)
        total = product if total is None else total + product
    return total


def local(
    hidden_rows,
    token_embed,
    first_routes,
    first_gates,
    first_gate_up,
    first_down,
    second_routes,
    second_gates,
    second_gate_up,
    second_down,
    hidden_gain,
    embed_gain,
    merge_weight,
):
    ring = Ring()
    width = hidden_rows.shape[1]
    halves = gate_halves(first_routes, first_gates, ring.size)
    second_halves = gate_halves(second_routes, second_gates, ring.size)
    rows = after(jnp.concatenate([hidden_rows, halves], axis=1), second_halves)
    chunks, crossed = gather_rows(ring, rows)
    weight = plane_weight(ring, after(merge_weight, crossed), lax.axis_size("groups"))
    first = scatter_sum(ring, experts_on(ring, chunks, width, first_gate_up[0], first_down[0]))
    after_first = (hidden_rows.astype(jnp.float32) + first).astype(jnp.bfloat16)
    merged_in = jnp.concatenate([normed(after_first, hidden_gain), normed(token_embed, embed_gain)], axis=1)
    merged = merge(ring, merged_in, weight)
    after_merge = (after_first.astype(jnp.float32) + jax.nn.silu(merged)).astype(jnp.bfloat16)
    chunks, _ = gather_rows(ring, jnp.concatenate([after_merge, second_halves], axis=1))
    second = scatter_sum(ring, experts_on(ring, chunks, width, second_gate_up[0], second_down[0]))
    return (after_merge.astype(jnp.float32) + second).astype(jnp.bfloat16)


def solution(mesh):
    rows = P(("groups", "inner"), None)
    weight = P("inner", None, None)
    return jax.shard_map(
        local,
        mesh=mesh,
        in_specs=(rows, rows, rows, rows, weight, weight, rows, rows, weight, weight, P(), P(), P("inner", None)),
        out_specs=rows,
        check_vma=False,
    )
```

time: 260 us -> 224 us (0.86)
  blocking collectives: 37.5 us -> 0 us
  starting transfers between devices: 43.3 us -> 56.1 us
  local copies, waits for them, and re-layouts: 10.8 us -> 3.99 us
  waiting for transfers between devices: 133 us -> 128 us
    all_gather x1 -> x0, blocking collectives: 37.5 us -> none  [gate_columns(): every = lax.all_gather(tables, 'inner', axis=0)]
    ppermute x18, waiting for transfers between devices: 70.8 us -> 59.2 us  [along_z(): return lax.ppermute(values, 'inner', perm)]
    ppermute x18, starting transfers between devices: 22.3 us -> 28.9 us  [along_z(): return lax.ppermute(values, 'inner', perm)]
    ppermute x17, waiting for transfers between devices: 62.6 us -> 69 us  [across_y(): return lax.ppermute(values, 'inner', [(d, d ^ 2) for d in range(self.size)])]
    ppermute x17, starting transfers between devices: 16.9 us -> 22.4 us  [across_y(): return lax.ppermute(values, 'inner', [(d, d ^ 2) for d in range(self.size)])]
    rev x1 -> x0, local copies, waits for them, and re-layouts: 4.84 us -> none  [merge(): blocks = jnp.where(ring.y == 1, blocks[:, :, ::-1], blocks)]
    dot_general x8, matrix products: 14.7 us -> 10.2 us  [expert(): projected = jnp.dot(rows, gate_up, preferred_element_type=jnp.float32)]
    select_n x3, other arithmetic: 0.7 us -> 3.93 us  [the longest x1 2.69 us: plane_weight(): jnp.where(ring.core == 0, jnp.concatenate(mine), jnp.concatenate(theirs))]
  transfers between devices with their start and end apart: 52 -> 53, of which waited for: 20 -> 26; matrix products, arithmetic and copies ran while one was open for 15% -> 14% of each run, Pallas kernels for 0% -> 0%
where the time goes in v3:
time: 224 us
  waiting for transfers between devices  128 us (57%)
  starting transfers between devices  56.1 us (25%)
  matrix products  22 us (10%)
  other arithmetic  12.1 us (5%)
  local copies, waits for them, and re-layouts  3.99 us (2%)
    ppermute x17, waiting for transfers between devices, across_y(): return lax.ppermute(values, 'inner', [(d, d ^ 2) for d in range(self.size)])  69 us
    ppermute x18, waiting for transfers between devices, along_z(): return lax.ppermute(values, 'inner', perm)  59.2 us
    ppermute x18, starting transfers between devices, along_z(): return lax.ppermute(values, 'inner', perm)  28.9 us
    ppermute x17, starting transfers between devices, across_y(): return lax.ppermute(values, 'inner', [(d, d ^ 2) for d in range(self.size)])  22.4 us
    dot_general x8, matrix products, expert(): projected = jnp.dot(rows, gate_up, preferred_element_type=jnp.float32)  10.2 us
    dot_general x8, matrix products, expert(): out = jnp.dot(hidden, down, preferred_element_type=jnp.float32)  6.15 us
    dot_general x4, matrix products, merge(): product = jnp.dot(piece, weight, preferred_element_type=jnp.float32)  5.68 us
  transfers between devices with their start and end apart: 53, of which 26 were waited for; matrix products, arithmetic and copies ran while one was open for 14% of the time, Pallas kernels for 0%

profile of v3, /device:TPU:0, one launch (start us, length us, event | category | flops | bytes accessed | tf_op | source)
XLA Modules:
  0.0 223.6 jit_solution(14454913655991590389)
XLA Ops:
  2.1 3.0 %collective-permute-start.3 = (bf16[64,2176]{1,0:T(8,128)(2,1)S(1)}, bf16[64,2176]{1,0:T(8,128)(2,1)S(1)}, u32[]{:S(2)}, u32[]{:S(2)}) collective-permute-start(bf16[64,2176]{1,0:T(8,128)(2,1)S(1)} %concatenate.85), channel_id=1, source_target_pairs={{0,2},{1,3},{2,0},{3,1},{4,6},{5,7},{6,4},{7,5},{8,10},{9,11},{10,... | collective-permute-start | bytes 835592 | tf_op jit(solution)/shard_map/ppermute | solution.py:24
  5.2 3.6 %collective-permute-start.8 = (bf16[64,2176]{1,0:T(8,128)(2,1)S(1)}, bf16[64,2176]{1,0:T(8,128)(2,1)S(1)}, u32[]{:S(2)}, u32[]{:S(2)}) collective-permute-start(bf16[64,2176]{1,0:T(8,128)(2,1)S(1)} %concatenate.85), channel_id=1, source_target_pairs={{0,12},{1,13},{2,14},{3,15},{4,0},{5,1},{6,2},{7,3},{8,4},{9,5},{1... | collective-permute-start | bytes 835592 | tf_op jit(solution)/shard_map/ppermute | solution.py:21
  11.1 4.8 %collective-permute-done.8 = bf16[64,2176]{1,0:T(8,128)(2,1)S(1)} collective-permute-done((bf16[64,2176]{1,0:T(8,128)(2,1)S(1)}, bf16[64,2176]{1,0:T(8,128)(2,1)S(1)}, u32[]{:S(2)}, u32[]{:S(2)}) %collective-permute-start.8) | collective-permute-done | bytes 278560 | tf_op jit(solution)/shard_map/ppermute | solution.py:21
  16.5 4.8 %collective-permute-done = bf16[64,2176]{1,0:T(8,128)(2,1)S(1)} collective-permute-done((bf16[64,2176]{1,0:T(8,128)(2,1)S(1)}, bf16[64,2176]{1,0:T(8,128)(2,1)S(1)}, u32[]{:S(2)}, u32[]{:S(2)}) %collective-permute-start) | collective-permute-done | bytes 278560 | tf_op jit(solution)/shard_map/ppermute | solution.py:21
  23.7 1.5 collective-permute-start.1
  25.3 15.7 %collective-permute-done.1 = bf16[64,2176]{1,0:T(8,128)(2,1)S(1)} collective-permute-done((bf16[64,2176]{1,0:T(8,128)(2,1)S(1)}, bf16[64,2176]{1,0:T(8,128)(2,1)S(1)}, u32[]{:S(2)}, u32[]{:S(2)}) %collective-permute-start.1) | collective-permute-done | bytes 278560 | tf_op jit(solution)/shard_map/ppermute | solution.py:24
  41.8 1.5 collective-permute-start.24
  45.6 4.6 %collective-permute-done.15 = bf16[64,2176]{1,0:T(8,128)(2,1)S(1)} collective-permute-done((bf16[64,2176]{1,0:T(8,128)(2,1)S(1)}, bf16[64,2176]{1,0:T(8,128)(2,1)S(1)}, u32[]{:S(2)}, u32[]{:S(2)}) %collective-permute-start.15) | collective-permute-done | bytes 278560 | tf_op jit(solution)/shard_map/ppermute | solution.py:24
  60.4 1.5 collective-permute-start.12
  62.8 6.8 %collective-permute-done.12 = bf16[64,2048]{1,0:T(8,128)(2,1)S(1)} collective-permute-done((bf16[64,2048]{1,0:T(8,128)(2,1)S(1)}, bf16[64,2048]{1,0:T(8,128)(2,1)S(1)}, u32[]{:S(2)}, u32[]{:S(2)}) %collective-permute-start.12) | collective-permute-done | bytes 262176 | tf_op jit(solution)/shard_map/ppermute | solution.py:24
  69.7 2.5 %collective-permute-start.13 = (bf16[64,2048]{1,0:T(8,128)(2,1)S(1)}, bf16[64,2048]{1,0:T(8,128)(2,1)S(1)}, u32[]{:S(2)}, u32[]{:S(2)}) collective-permute-start(bf16[64,2048]{1,0:T(8,128)(2,1)S(1)} %add_convert_fusion.16), channel_id=1, source_target_pairs={{0,4},{1,5},{2,6},{3,7},{4,8},{5,9},{6,10},{7,11},{8,12},{9,13},{1... | collective-permute-start | bytes 786440 | tf_op jit(solution)/shard_map/ppermute | solution.py:21
  72.4 2.4 %collective-permute-done.6 = bf16[64,2048]{1,0:T(8,128)(2,1)S(1)} collective-permute-done((bf16[64,2048]{1,0:T(8,128)(2,1)S(1)}, bf16[64,2048]{1,0:T(8,128)(2,1)S(1)}, u32[]{:S(2)}, u32[]{:S(2)}) %collective-permute-start.6) | collective-permute-done | bytes 262176 | tf_op jit(solution)/shard_map/ppermute | solution.py:24
  75.8 3.8 %collective-permute-start.7 = (bf16[64,2048]{1,0:T(8,128)(2,1)S(1)}, bf16[64,2048]{1,0:T(8,128)(2,1)S(1)}, u32[]{:S(2)}, u32[]{:S(2)}) collective-permute-start(bf16[64,2048]{1,0:T(8,128)(2,1)S(1)} %add_convert_fusion.17), channel_id=1, source_target_pairs={{0,12},{1,13},{2,14},{3,15},{4,0},{5,1},{6,2},{7,3},{8,4},{9,5},{1... | collective-permute-start | bytes 786440 | tf_op jit(solution)/shard_map/ppermute | solution.py:21
  80.7 3.3 %collective-permute-done.18 = bf16[64,2048]{1,0:T(8,128)(2,1)S(1)} collective-permute-done((bf16[64,2048]{1,0:T(8,128)(2,1)S(1)}, bf16[64,2048]{1,0:T(8,128)(2,1)S(1)}, u32[]{:S(2)}, u32[]{:S(2)}) %collective-permute-start.18) | collective-permute-done | bytes 262176 | tf_op jit(solution)/shard_map/ppermute | solution.py:24
  84.1 2.5 %collective-permute-start.19 = (bf16[64,2048]{1,0:T(8,128)(2,1)S(1)}, bf16[64,2048]{1,0:T(8,128)(2,1)S(1)}, u32[]{:S(2)}, u32[]{:S(2)}) collective-permute-start(bf16[64,2048]{1,0:T(8,128)(2,1)S(1)} %add_convert_fusion.15), channel_id=1, source_target_pairs={{0,8},{1,9},{2,10},{3,11},{4,12},{5,13},{6,14},{7,15},{8,0},{9,1},... | collective-permute-start | bytes 786440 | tf_op jit(solution)/shard_map/ppermute | solution.py:21
  86.9 1.4 collective-permute-done.21
  88.3 8.1 %collective-permute-done.19 = bf16[64,2048]{1,0:T(8,128)(2,1)S(1)} collective-permute-done((bf16[64,2048]{1,0:T(8,128)(2,1)S(1)}, bf16[64,2048]{1,0:T(8,128)(2,1)S(1)}, u32[]{:S(2)}, u32[]{:S(2)}) %collective-permute-start.19) | collective-permute-done | bytes 262176 | tf_op jit(solution)/shard_map/ppermute | solution.py:21
  97.8 3.2 %collective-permute-start.27 = (bf16[64,1024]{1,0:T(8,128)(2,1)S(1)}, bf16[64,1024]{1,0:T(8,128)(2,1)S(1)}, u32[]{:S(2)}, u32[]{:S(2)}) collective-permute-start(bf16[64,1024]{1,0:T(8,128)(2,1)S(1)} %get-tuple-element.46), channel_id=1, source_target_pairs={{0,12},{1,13},{2,14},{3,15},{4,0},{5,1},{6,2},{7,3},{8,4},{9,5},{1... | collective-permute-start | bytes 393224 | tf_op jit(solution)/shard_map/ppermute | solution.py:21
  101.4 2.7 %maximum_select_fusion = bf16[1024,2048]{1,0:T(8,128)(2,1)S(1)} fusion(bf16[256,2048]{1,0:T(8,128)(2,1)S(1)} %get-tuple-element.44, bf16[256,2048]{1,0:T(8,128)(2,1)S(1)} %get-tuple-element.42, bf16[256,2048]{1,0:T(8,128)(2,1)S(1)} %get-tuple-element.43, bf16[256,2048]{1,0:T(8,128)(2,1)S(1)} %get-tuple-element.41, pred[]{:T(512)S(6)} %eq.100), kind=kLoop, calls=%fused_computation | loop fusion | flops 35651584 | bytes 8388609 | tf_op jit(solution)/shard_map/jit(_where)/select_n | solution.py:138
  104.1 1.3 collective-permute-done.29
  106.3 2.2 collective-permute-start.30
  109.3 1.4 collective-permute-start.28
  110.7 1.9 collective-permute-done.22
  113.8 2.6 %collective-permute-done.30 = bf16[64,2048]{1,0:T(8,128)(2,1)S(1)} collective-permute-done((bf16[64,2048]{1,0:T(8,128)(2,1)S(1)}, bf16[64,2048]{1,0:T(8,128)(2,1)S(1)}, u32[]{:S(2)}, u32[]{:S(2)}) %collective-permute-start.30) | collective-permute-done | bytes 262176 | tf_op jit(solution)/shard_map/ppermute | solution.py:21
  116.4 5.1 %collective-permute-done.28 = bf16[64,2048]{1,0:T(8,128)(2,1)S(1)} collective-permute-done((bf16[64,2048]{1,0:T(8,128)(2,1)S(1)}, bf16[64,2048]{1,0:T(8,128)(2,1)S(1)}, u32[]{:S(2)}, u32[]{:S(2)}) %collective-permute-start.28) | collective-permute-done | bytes 262176 | tf_op jit(solution)/shard_map/ppermute | solution.py:21
  121.5 13.0 %collective-permute-done.26 = bf16[64,2048]{1,0:T(8,128)(2,1)S(1)} collective-permute-done((bf16[64,2048]{1,0:T(8,128)(2,1)S(1)}, bf16[64,2048]{1,0:T(8,128)(2,1)S(1)}, u32[]{:S(2)}, u32[]{:S(2)}) %collective-permute-start.26) | collective-permute-done | bytes 262176 | tf_op jit(solution)/shard_map/ppermute | solution.py:21
  134.5 3.1 %fusion.46 = bf16[64,2048]{1,0:T(8,128)(2,1)S(1)} fusion(bf16[64,2048]{1,0:T(8,128)(2,1)S(1)} %get-tuple-element.38, bf16[64,2048]{1,0:T(8,128)(2,1)S(1)} %collective-permute-done.30, bf16[64,2048]{1,0:T(8,128)(2,1)S(1)} %collective-permute-done.28, bf16[64,2048]{1,0:T(8,128)(2,1)S(1)} %collective-permute-done.26, bf16[1024,2048]{1,0:T(8,128)(2,1)} %copy-done.2, ...), kind=kOutput, calls=%fused_computation.97 | convolution fusion | flops 270401536 | bytes 6029316 | tf_op jit(solution)/shard_map/dot_general | solution.py:149
  137.9 3.8 %collective-permute-start.39 = (bf16[64,2176]{1,0:T(8,128)(2,1)S(1)}, bf16[64,2176]{1,0:T(8,128)(2,1)S(1)}, u32[]{:S(2)}, u32[]{:S(2)}) collective-permute-start(bf16[64,2176]{1,0:T(8,128)(2,1)S(1)} %concatenate.101), channel_id=1, source_target_pairs={{0,12},{1,13},{2,14},{3,15},{4,0},{5,1},{6,2},{7,3},{8,4},{9,5},{1... | collective-permute-start | bytes 835592 | tf_op jit(solution)/shard_map/ppermute | solution.py:21
  141.7 2.3 %collective-permute-start.34 = (bf16[64,2176]{1,0:T(8,128)(2,1)S(1)}, bf16[64,2176]{1,0:T(8,128)(2,1)S(1)}, u32[]{:S(2)}, u32[]{:S(2)}) collective-permute-start(bf16[64,2176]{1,0:T(8,128)(2,1)S(1)} %concatenate.101), channel_id=1, source_target_pairs={{0,2},{1,3},{2,0},{3,1},{4,6},{5,7},{6,4},{7,5},{8,10},{9,11},{10,... | collective-permute-start | bytes 835592 | tf_op jit(solution)/shard_map/ppermute | solution.py:24
  143.9 5.3 %collective-permute-done.31 = bf16[64,2176]{1,0:T(8,128)(2,1)S(1)} collective-permute-done((bf16[64,2176]{1,0:T(8,128)(2,1)S(1)}, bf16[64,2176]{1,0:T(8,128)(2,1)S(1)}, u32[]{:S(2)}, u32[]{:S(2)}) %collective-permute-start.31) | collective-permute-done | bytes 278560 | tf_op jit(solution)/shard_map/ppermute | solution.py:21
  149.2 2.8 %collective-permute-done.39 = bf16[64,2176]{1,0:T(8,128)(2,1)S(1)} collective-permute-done((bf16[64,2176]{1,0:T(8,128)(2,1)S(1)}, bf16[64,2176]{1,0:T(8,128)(2,1)S(1)}, u32[]{:S(2)}, u32[]{:S(2)}) %collective-permute-start.39) | collective-permute-done | bytes 278560 | tf_op jit(solution)/shard_map/ppermute | solution.py:21
  152.0 2.3 %collective-permute-start.45 = (bf16[64,2176]{1,0:T(8,128)(2,1)S(1)}, bf16[64,2176]{1,0:T(8,128)(2,1)S(1)}, u32[]{:S(2)}, u32[]{:S(2)}) collective-permute-start(bf16[64,2176]{1,0:T(8,128)(2,1)S(1)} %concatenate.101), channel_id=1, source_target_pairs={{0,8},{1,9},{2,10},{3,11},{4,12},{5,13},{6,14},{7,15},{8,0},{9,1},... | collective-permute-start | bytes 835592 | tf_op jit(solution)/shard_map/ppermute | solution.py:21
  154.4 2.7 %collective-permute-start.40 = (bf16[64,2176]{1,0:T(8,128)(2,1)S(1)}, bf16[64,2176]{1,0:T(8,128)(2,1)S(1)}, u32[]{:S(2)}, u32[]{:S(2)}) collective-permute-start(bf16[64,2176]{1,0:T(8,128)(2,1)S(1)} %collective-permute-done.39), channel_id=1, source_target_pairs={{0,2},{1,3},{2,0},{3,1},{4,6},{5,7},{6,4},{7,5},{8,10},{9,11},{10,... | collective-permute-start | bytes 835592 | tf_op jit(solution)/shard_map/ppermute | solution.py:24
  157.3 7.4 %collective-permute-done.40 = bf16[64,2176]{1,0:T(8,128)(2,1)S(1)} collective-permute-done((bf16[64,2176]{1,0:T(8,128)(2,1)S(1)}, bf16[64,2176]{1,0:T(8,128)(2,1)S(1)}, u32[]{:S(2)}, u32[]{:S(2)}) %collective-permute-start.40) | collective-permute-done | bytes 278560 | tf_op jit(solution)/shard_map/ppermute | solution.py:24
  164.8 1.4 collective-permute-done.45
  166.2 2.9 %collective-permute-start.46 = (bf16[64,2176]{1,0:T(8,128)(2,1)S(1)}, bf16[64,2176]{1,0:T(8,128)(2,1)S(1)}, u32[]{:S(2)}, u32[]{:S(2)}) collective-permute-start(bf16[64,2176]{1,0:T(8,128)(2,1)S(1)} %collective-permute-done.45), channel_id=1, source_target_pairs={{0,2},{1,3},{2,0},{3,1},{4,6},{5,7},{6,4},{7,5},{8,10},{9,11},{10,... | collective-permute-start | bytes 835592 | tf_op jit(solution)/shard_map/ppermute | solution.py:24
  169.2 6.7 %collective-permute-done.46 = bf16[64,2176]{1,0:T(8,128)(2,1)S(1)} collective-permute-done((bf16[64,2176]{1,0:T(8,128)(2,1)S(1)}, bf16[64,2176]{1,0:T(8,128)(2,1)S(1)}, u32[]{:S(2)}, u32[]{:S(2)}) %collective-permute-start.46) | collective-permute-done | bytes 278560 | tf_op jit(solution)/shard_map/ppermute | solution.py:24
  179.2 1.3 fusion.4
  181.5 1.3 fusion.2
  184.7 1.3 fusion
  187.2 1.8 collective-permute-start.43
  189.5 6.8 %collective-permute-done.43 = bf16[64,2048]{1,0:T(8,128)(2,1)S(1)} collective-permute-done((bf16[64,2048]{1,0:T(8,128)(2,1)S(1)}, bf16[64,2048]{1,0:T(8,128)(2,1)S(1)}, u32[]{:S(2)}, u32[]{:S(2)}) %collective-permute-start.43) | collective-permute-done | bytes 262176 | tf_op jit(solution)/shard_map/ppermute | solution.py:24
  196.7 4.9 %collective-permute-done.37 = bf16[64,2048]{1,0:T(8,128)(2,1)S(1)} collective-permute-done((bf16[64,2048]{1,0:T(8,128)(2,1)S(1)}, bf16[64,2048]{1,0:T(8,128)(2,1)S(1)}, u32[]{:S(2)}, u32[]{:S(2)}) %collective-permute-start.37) | collective-permute-done | bytes 262176 | tf_op jit(solution)/shard_map/ppermute | solution.py:24
  201.6 1.7 collective-permute-start.49
  203.4 1.7 collective-permute-start.38
  205.4 5.4 %collective-permute-done.49 = bf16[64,2048]{1,0:T(8,128)(2,1)S(1)} collective-permute-done((bf16[64,2048]{1,0:T(8,128)(2,1)S(1)}, bf16[64,2048]{1,0:T(8,128)(2,1)S(1)}, u32[]{:S(2)}, u32[]{:S(2)}) %collective-permute-start.49) | collective-permute-done | bytes 262176 | tf_op jit(solution)/shard_map/ppermute | solution.py:24
  211.6 3.5 %collective-permute-done.52 = bf16[64,2048]{1,0:T(8,128)(2,1)S(1)} collective-permute-done((bf16[64,2048]{1,0:T(8,128)(2,1)S(1)}, bf16[64,2048]{1,0:T(8,128)(2,1)S(1)}, u32[]{:S(2)}, u32[]{:S(2)}) %collective-permute-start.52) | collective-permute-done | bytes 262176 | tf_op jit(solution)/shard_map/ppermute | solution.py:24
  215.1 7.5 %collective-permute-done.50 = bf16[64,2048]{1,0:T(8,128)(2,1)S(1)} collective-permute-done((bf16[64,2048]{1,0:T(8,128)(2,1)S(1)}, bf16[64,2048]{1,0:T(8,128)(2,1)S(1)}, u32[]{:S(2)}, u32[]{:S(2)}) %collective-permute-start.50) | collective-permute-done | bytes 262176 | tf_op jit(solution)/shard_map/ppermute | solution.py:21
  (180 shorter events, 39.2 us)
Async XLA Ops:
  2.1 14.2 %collective-permute-start.3 = (bf16[64,2176]{1,0:T(8,128)(2,1)S(1)}, bf16[64,2176]{1,0:T(8,128)(2,1)S(1)}, u32[]{:S(2)}, u32[]{:S(2)}) collective-permute-start(bf16[64,2176]{1,0:T(8,128)(2,1)S(1)} %concatenate.85), channel_id=1, source_target_pairs={{0,2},{1,3},{2,0},{3,1},{4,6},{5,7},{6,4},{7,5},{8,10},{9,11},{10,... | collective-permute-start | bytes 835592 | tf_op jit(solution)/shard_map/ppermute | solution.py:24
  5.2 10.7 %collective-permute-start.8 = (bf16[64,2176]{1,0:T(8,128)(2,1)S(1)}, bf16[64,2176]{1,0:T(8,128)(2,1)S(1)}, u32[]{:S(2)}, u32[]{:S(2)}) collective-permute-start(bf16[64,2176]{1,0:T(8,128)(2,1)S(1)} %concatenate.85), channel_id=1, source_target_pairs={{0,12},{1,13},{2,14},{3,15},{4,0},{5,1},{6,2},{7,3},{8,4},{9,5},{1... | collective-permute-start | bytes 835592 | tf_op jit(solution)/shard_map/ppermute | solution.py:21
  8.8 12.5 %collective-permute-start = (bf16[64,2176]{1,0:T(8,128)(2,1)S(1)}, bf16[64,2176]{1,0:T(8,128)(2,1)S(1)}, u32[]{:S(2)}, u32[]{:S(2)}) collective-permute-start(bf16[64,2176]{1,0:T(8,128)(2,1)S(1)} %concatenate.85), channel_id=1, source_target_pairs={{0,4},{1,5},{2,6},{3,7},{4,8},{5,9},{6,10},{7,11},{8,12},{9,13},{1... | collective-permute-start | bytes 835592 | tf_op jit(solution)/shard_map/ppermute | solution.py:21
  15.9 9.3 %collective-permute-start.9 = (bf16[64,2176]{1,0:T(8,128)(2,1)S(1)}, bf16[64,2176]{1,0:T(8,128)(2,1)S(1)}, u32[]{:S(2)}, u32[]{:S(2)}) collective-permute-start(bf16[64,2176]{1,0:T(8,128)(2,1)S(1)} %collective-permute-done.8), channel_id=1, source_target_pairs={{0,2},{1,3},{2,0},{3,1},{4,6},{5,7},{6,4},{7,5},{8,10},{9,11},{10,... | collective-permute-start | bytes 835592 | tf_op jit(solution)/shard_map/ppermute | solution.py:24
  16.4 26.8 %collective-permute-start.4 = (bf16[128,2176]{1,0:T(8,128)(2,1)S(1)}, bf16[128,2176]{1,0:T(8,128)(2,1)S(1)}, u32[]{:S(2)}, u32[]{:S(2)}) collective-permute-start(bf16[128,2176]{1,0:T(8,128)(2,1)S(1)} %pad_maximum_fusion.9), channel_id=1, source_target_pairs={{0,1},{1,0},{2,3},{3,2},{4,5},{5,4},{6,7},{7,6},{8,9},{9,8},{10,11... | collective-permute-start | bytes 1671176 | tf_op jit(solution)/shard_map/ppermute | solution.py:27
  21.3 19.9 %collective-permute-start.14 = (bf16[64,2176]{1,0:T(8,128)(2,1)S(1)}, bf16[64,2176]{1,0:T(8,128)(2,1)S(1)}, u32[]{:S(2)}, u32[]{:S(2)}) collective-permute-start(bf16[64,2176]{1,0:T(8,128)(2,1)S(1)} %concatenate.85), channel_id=1, source_target_pairs={{0,8},{1,9},{2,10},{3,11},{4,12},{5,13},{6,14},{7,15},{8,0},{9,1},... | collective-permute-start | bytes 835592 | tf_op jit(solution)/shard_map/ppermute | solution.py:21
  23.1 18.6 %collective-permute-start.23 = (bf16[128,2048]{1,0:T(8,128)(2,1)S(1)}, bf16[128,2048]{1,0:T(8,128)(2,1)S(1)}, u32[]{:S(2)}, u32[]{:S(2)}) collective-permute-start(bf16[128,2048]{1,0:T(8,128)(2,1)S(1)} %constant_dynamic-slice_fusion), channel_id=1, source_target_pairs={{0,2},{1,3},{2,0},{3,1},{4,6},{5,7},{6,4},{7,5},{8,10},{9,11},{10,... | collective-permute-start | bytes 1572872 | tf_op jit(solution)/shard_map/ppermute | solution.py:24
  23.7 17.4 %collective-permute-start.1 = (bf16[64,2176]{1,0:T(8,128)(2,1)S(1)}, bf16[64,2176]{1,0:T(8,128)(2,1)S(1)}, u32[]{:S(2)}, u32[]{:S(2)}) collective-permute-start(bf16[64,2176]{1,0:T(8,128)(2,1)S(1)} %collective-permute-done), channel_id=1, source_target_pairs={{0,2},{1,3},{2,0},{3,1},{4,6},{5,7},{6,4},{7,5},{8,10},{9,11},{10,... | collective-permute-start | bytes 835592 | tf_op jit(solution)/shard_map/ppermute | solution.py:24
  25.3 27.4 %collective-permute-start.10 = (bf16[128,2176]{1,0:T(8,128)(2,1)S(1)}, bf16[128,2176]{1,0:T(8,128)(2,1)S(1)}, u32[]{:S(2)}, u32[]{:S(2)}) collective-permute-start(bf16[128,2176]{1,0:T(8,128)(2,1)S(1)} %pad_maximum_fusion.10), channel_id=1, source_target_pairs={{0,1},{1,0},{2,3},{3,2},{4,5},{5,4},{6,7},{7,6},{8,9},{9,8},{10,11... | collective-permute-start | bytes 1671176 | tf_op jit(solution)/shard_map/ppermute | solution.py:27
  41.1 9.3 %collective-permute-start.2 = (bf16[128,2176]{1,0:T(8,128)(2,1)S(1)}, bf16[128,2176]{1,0:T(8,128)(2,1)S(1)}, u32[]{:S(2)}, u32[]{:S(2)}) collective-permute-start(bf16[128,2176]{1,0:T(8,128)(2,1)S(1)} %pad_maximum_fusion.8), channel_id=1, source_target_pairs={{0,1},{1,0},{2,3},{3,2},{4,5},{5,4},{6,7},{7,6},{8,9},{9,8},{10,11... | collective-permute-start | bytes 1671176 | tf_op jit(solution)/shard_map/ppermute | solution.py:27
  41.2 9.1 %collective-permute-start.15 = (bf16[64,2176]{1,0:T(8,128)(2,1)S(1)}, bf16[64,2176]{1,0:T(8,128)(2,1)S(1)}, u32[]{:S(2)}, u32[]{:S(2)}) collective-permute-start(bf16[64,2176]{1,0:T(8,128)(2,1)S(1)} %collective-permute-done.14), channel_id=1, source_target_pairs={{0,2},{1,3},{2,0},{3,1},{4,6},{5,7},{6,4},{7,5},{8,10},{9,11},{10,... | collective-permute-start | bytes 835592 | tf_op jit(solution)/shard_map/ppermute | solution.py:24
  41.8 14.0 %collective-permute-start.24 = (bf16[128,2048]{1,0:T(8,128)(2,1)S(1)}, bf16[128,2048]{1,0:T(8,128)(2,1)S(1)}, u32[]{:S(2)}, u32[]{:S(2)}) collective-permute-start(bf16[128,2048]{1,0:T(8,128)(2,1)S(1)} %collective-permute-done.23), channel_id=1, source_target_pairs={{0,16},{16,0},{1,17},{17,1},{2,18},{18,2},{3,19},{19,3},{4,20},{20... | collective-permute-start | bytes 1572872 | tf_op jit(solution)/shard_map/ppermute | solution.py:132
  45.5 12.1 %collective-permute-start.20 = (bf16[128,2048]{1,0:T(8,128)(2,1)S(1)}, bf16[128,2048]{1,0:T(8,128)(2,1)S(1)}, u32[]{:S(2)}, u32[]{:S(2)}) collective-permute-start(bf16[128,2048]{1,0:T(8,128)(2,1)S(1)} %slice.298), channel_id=1, source_target_pairs={{0,1},{1,0},{2,3},{3,2},{4,5},{5,4},{6,7},{7,6},{8,9},{9,8},{10,11... | collective-permute-start | bytes 1572872 | tf_op jit(solution)/shard_map/ppermute | solution.py:27
  50.3 7.5 %collective-permute-start.16 = (bf16[128,2176]{1,0:T(8,128)(2,1)S(1)}, bf16[128,2176]{1,0:T(8,128)(2,1)S(1)}, u32[]{:S(2)}, u32[]{:S(2)}) collective-permute-start(bf16[128,2176]{1,0:T(8,128)(2,1)S(1)} %pad_maximum_fusion.11), channel_id=1, source_target_pairs={{0,1},{1,0},{2,3},{3,2},{4,5},{5,4},{6,7},{7,6},{8,9},{9,8},{10,11... | collective-permute-start | bytes 1671176 | tf_op jit(solution)/shard_map/ppermute | solution.py:27
  57.1 44.1 %collective-permute-start.25 = (bf16[512,2048]{1,0:T(8,128)(2,1)S(1)}, bf16[512,2048]{1,0:T(8,128)(2,1)S(1)}, u32[]{:S(2)}, u32[]{:S(2)}) collective-permute-start(bf16[512,2048]{1,0:T(8,128)(2,1)S(1)} %maximum_select_fusion.1), channel_id=1, source_target_pairs={{0,1},{1,0},{2,3},{3,2},{4,5},{5,4},{6,7},{7,6},{8,9},{9,8},{10,11... | collective-permute-start | bytes 6291464 | tf_op jit(solution)/shard_map/ppermute | solution.py:27
  60.1 12.0 %collective-permute-start.17 = (bf16[128,2048]{1,0:T(8,128)(2,1)S(1)}, bf16[128,2048]{1,0:T(8,128)(2,1)S(1)}, u32[]{:S(2)}, u32[]{:S(2)}) collective-permute-start(bf16[128,2048]{1,0:T(8,128)(2,1)S(1)} %slice.294), channel_id=1, source_target_pairs={{0,1},{1,0},{2,3},{3,2},{4,5},{5,4},{6,7},{7,6},{8,9},{9,8},{10,11... | collective-permute-start | bytes 1572872 | tf_op jit(solution)/shard_map/ppermute | solution.py:27
  60.4 9.2 %collective-permute-start.12 = (bf16[64,2048]{1,0:T(8,128)(2,1)S(1)}, bf16[64,2048]{1,0:T(8,128)(2,1)S(1)}, u32[]{:S(2)}, u32[]{:S(2)}) collective-permute-start(bf16[64,2048]{1,0:T(8,128)(2,1)S(1)} %slice.290), channel_id=1, source_target_pairs={{0,2},{1,3},{2,0},{3,1},{4,6},{5,7},{6,4},{7,5},{8,10},{9,11},{10,... | collective-permute-start | bytes 786440 | tf_op jit(solution)/shard_map/ppermute | solution.py:24
  62.1 12.7 %collective-permute-start.6 = (bf16[64,2048]{1,0:T(8,128)(2,1)S(1)}, bf16[64,2048]{1,0:T(8,128)(2,1)S(1)}, u32[]{:S(2)}, u32[]{:S(2)}) collective-permute-start(bf16[64,2048]{1,0:T(8,128)(2,1)S(1)} %slice.284), channel_id=1, source_target_pairs={{0,2},{1,3},{2,0},{3,1},{4,6},{5,7},{6,4},{7,5},{8,10},{9,11},{10,... | collective-permute-start | bytes 786440 | tf_op jit(solution)/shard_map/ppermute | solution.py:24
  69.7 17.2 %collective-permute-start.13 = (bf16[64,2048]{1,0:T(8,128)(2,1)S(1)}, bf16[64,2048]{1,0:T(8,128)(2,1)S(1)}, u32[]{:S(2)}, u32[]{:S(2)}) collective-permute-start(bf16[64,2048]{1,0:T(8,128)(2,1)S(1)} %add_convert_fusion.16), channel_id=1, source_target_pairs={{0,4},{1,5},{2,6},{3,7},{4,8},{5,9},{6,10},{7,11},{8,12},{9,13},{1... | collective-permute-start | bytes 786440 | tf_op jit(solution)/shard_map/ppermute | solution.py:21
  74.8 9.2 %collective-permute-start.18 = (bf16[64,2048]{1,0:T(8,128)(2,1)S(1)}, bf16[64,2048]{1,0:T(8,128)(2,1)S(1)}, u32[]{:S(2)}, u32[]{:S(2)}) collective-permute-start(bf16[64,2048]{1,0:T(8,128)(2,1)S(1)} %slice.296), channel_id=1, source_target_pairs={{0,2},{1,3},{2,0},{3,1},{4,6},{5,7},{6,4},{7,5},{8,10},{9,11},{10,... | collective-permute-start | bytes 786440 | tf_op jit(solution)/shard_map/ppermute | solution.py:24
  75.8 11.1 %collective-permute-start.7 = (bf16[64,2048]{1,0:T(8,128)(2,1)S(1)}, bf16[64,2048]{1,0:T(8,128)(2,1)S(1)}, u32[]{:S(2)}, u32[]{:S(2)}) collective-permute-start(bf16[64,2048]{1,0:T(8,128)(2,1)S(1)} %add_convert_fusion.17), channel_id=1, source_target_pairs={{0,12},{1,13},{2,14},{3,15},{4,0},{5,1},{6,2},{7,3},{8,4},{9,5},{1... | collective-permute-start | bytes 786440 | tf_op jit(solution)/shard_map/ppermute | solution.py:21
  79.6 8.7 %collective-permute-start.21 = (bf16[64,2048]{1,0:T(8,128)(2,1)S(1)}, bf16[64,2048]{1,0:T(8,128)(2,1)S(1)}, u32[]{:S(2)}, u32[]{:S(2)}) collective-permute-start(bf16[64,2048]{1,0:T(8,128)(2,1)S(1)} %slice.300), channel_id=1, source_target_pairs={{0,2},{1,3},{2,0},{3,1},{4,6},{5,7},{6,4},{7,5},{8,10},{9,11},{10,... | collective-permute-start | bytes 786440 | tf_op jit(solution)/shard_map/ppermute | solution.py:24
  84.1 12.3 %collective-permute-start.19 = (bf16[64,2048]{1,0:T(8,128)(2,1)S(1)}, bf16[64,2048]{1,0:T(8,128)(2,1)S(1)}, u32[]{:S(2)}, u32[]{:S(2)}) collective-permute-start(bf16[64,2048]{1,0:T(8,128)(2,1)S(1)} %add_convert_fusion.15), channel_id=1, source_target_pairs={{0,8},{1,9},{2,10},{3,11},{4,12},{5,13},{6,14},{7,15},{8,0},{9,1},... | collective-permute-start | bytes 786440 | tf_op jit(solution)/shard_map/ppermute | solution.py:21
  97.2 8.3 %collective-permute-start.29 = (bf16[64,1024]{1,0:T(8,128)(2,1)S(1)}, bf16[64,1024]{1,0:T(8,128)(2,1)S(1)}, u32[]{:S(2)}, u32[]{:S(2)}) collective-permute-start(bf16[64,1024]{1,0:T(8,128)(2,1)S(1)} %get-tuple-element.47), channel_id=1, source_target_pairs={{0,4},{1,5},{2,6},{3,7},{4,8},{5,9},{6,10},{7,11},{8,12},{9,13},{1... | collective-permute-start | bytes 393224 | tf_op jit(solution)/shard_map/ppermute | solution.py:21
  97.8 10.7 %collective-permute-start.27 = (bf16[64,1024]{1,0:T(8,128)(2,1)S(1)}, bf16[64,1024]{1,0:T(8,128)(2,1)S(1)}, u32[]{:S(2)}, u32[]{:S(2)}) collective-permute-start(bf16[64,1024]{1,0:T(8,128)(2,1)S(1)} %get-tuple-element.46), channel_id=1, source_target_pairs={{0,12},{1,13},{2,14},{3,15},{4,0},{5,1},{6,2},{7,3},{8,4},{9,5},{1... | collective-permute-start | bytes 393224 | tf_op jit(solution)/shard_map/ppermute | solution.py:21
  101.0 11.6 %collective-permute-start.22 = (bf16[64,1024]{1,0:T(8,128)(2,1)S(1)}, bf16[64,1024]{1,0:T(8,128)(2,1)S(1)}, u32[]{:S(2)}, u32[]{:S(2)}) collective-permute-start(bf16[64,1024]{1,0:T(8,128)(2,1)S(1)} %get-tuple-element.45), channel_id=1, source_target_pairs={{0,8},{1,9},{2,10},{3,11},{4,12},{5,13},{6,14},{7,15},{8,0},{9,1},... | collective-permute-start | bytes 393224 | tf_op jit(solution)/shard_map/ppermute | solution.py:21
  106.3 10.1 %collective-permute-start.30 = (bf16[64,2048]{1,0:T(8,128)(2,1)S(1)}, bf16[64,2048]{1,0:T(8,128)(2,1)S(1)}, u32[]{:S(2)}, u32[]{:S(2)}) collective-permute-start(bf16[64,2048]{1,0:T(8,128)(2,1)S(1)} %convolution_convert_fusion), channel_id=1, source_target_pairs={{0,12},{1,13},{2,14},{3,15},{4,0},{5,1},{6,2},{7,3},{8,4},{9,5},{1... | collective-permute-start | bytes 786440 | tf_op jit(solution)/shard_map/ppermute | solution.py:21
  109.3 12.2 %collective-permute-start.28 = (bf16[64,2048]{1,0:T(8,128)(2,1)S(1)}, bf16[64,2048]{1,0:T(8,128)(2,1)S(1)}, u32[]{:S(2)}, u32[]{:S(2)}) collective-permute-start(bf16[64,2048]{1,0:T(8,128)(2,1)S(1)} %convolution_convert_fusion.1), channel_id=1, source_target_pairs={{0,4},{1,5},{2,6},{3,7},{4,8},{5,9},{6,10},{7,11},{8,12},{9,13},{1... | collective-permute-start | bytes 786440 | tf_op jit(solution)/shard_map/ppermute | solution.py:21
  113.4 21.1 %collective-permute-start.26 = (bf16[64,2048]{1,0:T(8,128)(2,1)S(1)}, bf16[64,2048]{1,0:T(8,128)(2,1)S(1)}, u32[]{:S(2)}, u32[]{:S(2)}) collective-permute-start(bf16[64,2048]{1,0:T(8,128)(2,1)S(1)} %convolution_convert_fusion.2), channel_id=1, source_target_pairs={{0,8},{1,9},{2,10},{3,11},{4,12},{5,13},{6,14},{7,15},{8,0},{9,1},... | collective-permute-start | bytes 786440 | tf_op jit(solution)/shard_map/ppermute | solution.py:21
  137.8 11.4 %collective-permute-start.31 = (bf16[64,2176]{1,0:T(8,128)(2,1)S(1)}, bf16[64,2176]{1,0:T(8,128)(2,1)S(1)}, u32[]{:S(2)}, u32[]{:S(2)}) collective-permute-start(bf16[64,2176]{1,0:T(8,128)(2,1)S(1)} %concatenate.101), channel_id=1, source_target_pairs={{0,4},{1,5},{2,6},{3,7},{4,8},{5,9},{6,10},{7,11},{8,12},{9,13},{1... | collective-permute-start | bytes 835592 | tf_op jit(solution)/shard_map/ppermute | solution.py:21
  137.9 14.2 %collective-permute-start.39 = (bf16[64,2176]{1,0:T(8,128)(2,1)S(1)}, bf16[64,2176]{1,0:T(8,128)(2,1)S(1)}, u32[]{:S(2)}, u32[]{:S(2)}) collective-permute-start(bf16[64,2176]{1,0:T(8,128)(2,1)S(1)} %concatenate.101), channel_id=1, source_target_pairs={{0,12},{1,13},{2,14},{3,15},{4,0},{5,1},{6,2},{7,3},{8,4},{9,5},{1... | collective-permute-start | bytes 835592 | tf_op jit(solution)/shard_map/ppermute | solution.py:21
  141.7 15.4 %collective-permute-start.34 = (bf16[64,2176]{1,0:T(8,128)(2,1)S(1)}, bf16[64,2176]{1,0:T(8,128)(2,1)S(1)}, u32[]{:S(2)}, u32[]{:S(2)}) collective-permute-start(bf16[64,2176]{1,0:T(8,128)(2,1)S(1)} %concatenate.101), channel_id=1, source_target_pairs={{0,2},{1,3},{2,0},{3,1},{4,6},{5,7},{6,4},{7,5},{8,10},{9,11},{10,... | collective-permute-start | bytes 835592 | tf_op jit(solution)/shard_map/ppermute | solution.py:24
  152.0 14.1 %collective-permute-start.45 = (bf16[64,2176]{1,0:T(8,128)(2,1)S(1)}, bf16[64,2176]{1,0:T(8,128)(2,1)S(1)}, u32[]{:S(2)}, u32[]{:S(2)}) collective-permute-start(bf16[64,2176]{1,0:T(8,128)(2,1)S(1)} %concatenate.101), channel_id=1, source_target_pairs={{0,8},{1,9},{2,10},{3,11},{4,12},{5,13},{6,14},{7,15},{8,0},{9,1},... | collective-permute-start | bytes 835592 | tf_op jit(solution)/shard_map/ppermute | solution.py:21
  154.4 10.2 %collective-permute-start.40 = (bf16[64,2176]{1,0:T(8,128)(2,1)S(1)}, bf16[64,2176]{1,0:T(8,128)(2,1)S(1)}, u32[]{:S(2)}, u32[]{:S(2)}) collective-permute-start(bf16[64,2176]{1,0:T(8,128)(2,1)S(1)} %collective-permute-done.39), channel_id=1, source_target_pairs={{0,2},{1,3},{2,0},{3,1},{4,6},{5,7},{6,4},{7,5},{8,10},{9,11},{10,... | collective-permute-start | bytes 835592 | tf_op jit(solution)/shard_map/ppermute | solution.py:24
  157.1 18.9 %collective-permute-start.35 = (bf16[128,2176]{1,0:T(8,128)(2,1)S(1)}, bf16[128,2176]{1,0:T(8,128)(2,1)S(1)}, u32[]{:S(2)}, u32[]{:S(2)}) collective-permute-start(bf16[128,2176]{1,0:T(8,128)(2,1)S(1)} %pad_maximum_fusion.13), channel_id=1, source_target_pairs={{0,1},{1,0},{2,3},{3,2},{4,5},{5,4},{6,7},{7,6},{8,9},{9,8},{10,11... | collective-permute-start | bytes 1671176 | tf_op jit(solution)/shard_map/ppermute | solution.py:27
  157.2 11.8 %collective-permute-start.32 = (bf16[64,2176]{1,0:T(8,128)(2,1)S(1)}, bf16[64,2176]{1,0:T(8,128)(2,1)S(1)}, u32[]{:S(2)}, u32[]{:S(2)}) collective-permute-start(bf16[64,2176]{1,0:T(8,128)(2,1)S(1)} %collective-permute-done.31), channel_id=1, source_target_pairs={{0,2},{1,3},{2,0},{3,1},{4,6},{5,7},{6,4},{7,5},{8,10},{9,11},{10,... | collective-permute-start | bytes 835592 | tf_op jit(solution)/shard_map/ppermute | solution.py:24
  164.7 16.7 %collective-permute-start.41 = (bf16[128,2176]{1,0:T(8,128)(2,1)S(1)}, bf16[128,2176]{1,0:T(8,128)(2,1)S(1)}, u32[]{:S(2)}, u32[]{:S(2)}) collective-permute-start(bf16[128,2176]{1,0:T(8,128)(2,1)S(1)} %pad_maximum_fusion.14), channel_id=1, source_target_pairs={{0,1},{1,0},{2,3},{3,2},{4,5},{5,4},{6,7},{7,6},{8,9},{9,8},{10,11... | collective-permute-start | bytes 1671176 | tf_op jit(solution)/shard_map/ppermute | solution.py:27
  166.2 9.7 %collective-permute-start.46 = (bf16[64,2176]{1,0:T(8,128)(2,1)S(1)}, bf16[64,2176]{1,0:T(8,128)(2,1)S(1)}, u32[]{:S(2)}, u32[]{:S(2)}) collective-permute-start(bf16[64,2176]{1,0:T(8,128)(2,1)S(1)} %collective-permute-done.45), channel_id=1, source_target_pairs={{0,2},{1,3},{2,0},{3,1},{4,6},{5,7},{6,4},{7,5},{8,10},{9,11},{10,... | collective-permute-start | bytes 835592 | tf_op jit(solution)/shard_map/ppermute | solution.py:24
  169.1 10.0 %collective-permute-start.33 = (bf16[128,2176]{1,0:T(8,128)(2,1)S(1)}, bf16[128,2176]{1,0:T(8,128)(2,1)S(1)}, u32[]{:S(2)}, u32[]{:S(2)}) collective-permute-start(bf16[128,2176]{1,0:T(8,128)(2,1)S(1)} %pad_maximum_fusion.12), channel_id=1, source_target_pairs={{0,1},{1,0},{2,3},{3,2},{4,5},{5,4},{6,7},{7,6},{8,9},{9,8},{10,11... | collective-permute-start | bytes 1671176 | tf_op jit(solution)/shard_map/ppermute | solution.py:27
  175.9 8.7 %collective-permute-start.47 = (bf16[128,2176]{1,0:T(8,128)(2,1)S(1)}, bf16[128,2176]{1,0:T(8,128)(2,1)S(1)}, u32[]{:S(2)}, u32[]{:S(2)}) collective-permute-start(bf16[128,2176]{1,0:T(8,128)(2,1)S(1)} %pad_maximum_fusion.15), channel_id=1, source_target_pairs={{0,1},{1,0},{2,3},{3,2},{4,5},{5,4},{6,7},{7,6},{8,9},{9,8},{10,11... | collective-permute-start | bytes 1671176 | tf_op jit(solution)/shard_map/ppermute | solution.py:27
  186.9 9.6 %collective-permute-start.48 = (bf16[128,2048]{1,0:T(8,128)(2,1)S(1)}, bf16[128,2048]{1,0:T(8,128)(2,1)S(1)}, u32[]{:S(2)}, u32[]{:S(2)}) collective-permute-start(bf16[128,2048]{1,0:T(8,128)(2,1)S(1)} %slice.323), channel_id=1, source_target_pairs={{0,1},{1,0},{2,3},{3,2},{4,5},{5,4},{6,7},{7,6},{8,9},{9,8},{10,11... | collective-permute-start | bytes 1572872 | tf_op jit(solution)/shard_map/ppermute | solution.py:27
  187.2 9.2 %collective-permute-start.43 = (bf16[64,2048]{1,0:T(8,128)(2,1)S(1)}, bf16[64,2048]{1,0:T(8,128)(2,1)S(1)}, u32[]{:S(2)}, u32[]{:S(2)}) collective-permute-start(bf16[64,2048]{1,0:T(8,128)(2,1)S(1)} %slice.319), channel_id=1, source_target_pairs={{0,2},{1,3},{2,0},{3,1},{4,6},{5,7},{6,4},{7,5},{8,10},{9,11},{10,... | collective-permute-start | bytes 786440 | tf_op jit(solution)/shard_map/ppermute | solution.py:24
  189.2 12.4 %collective-permute-start.37 = (bf16[64,2048]{1,0:T(8,128)(2,1)S(1)}, bf16[64,2048]{1,0:T(8,128)(2,1)S(1)}, u32[]{:S(2)}, u32[]{:S(2)}) collective-permute-start(bf16[64,2048]{1,0:T(8,128)(2,1)S(1)} %slice.313), channel_id=1, source_target_pairs={{0,2},{1,3},{2,0},{3,1},{4,6},{5,7},{6,4},{7,5},{8,10},{9,11},{10,... | collective-permute-start | bytes 786440 | tf_op jit(solution)/shard_map/ppermute | solution.py:24
  196.4 14.5 %collective-permute-start.44 = (bf16[64,2048]{1,0:T(8,128)(2,1)S(1)}, bf16[64,2048]{1,0:T(8,128)(2,1)S(1)}, u32[]{:S(2)}, u32[]{:S(2)}) collective-permute-start(bf16[64,2048]{1,0:T(8,128)(2,1)S(1)} %add_convert_fusion.11), channel_id=1, source_target_pairs={{0,4},{1,5},{2,6},{3,7},{4,8},{5,9},{6,10},{7,11},{8,12},{9,13},{1... | collective-permute-start | bytes 786440 | tf_op jit(solution)/shard_map/ppermute | solution.py:21
  201.6 9.2 %collective-permute-start.49 = (bf16[64,2048]{1,0:T(8,128)(2,1)S(1)}, bf16[64,2048]{1,0:T(8,128)(2,1)S(1)}, u32[]{:S(2)}, u32[]{:S(2)}) collective-permute-start(bf16[64,2048]{1,0:T(8,128)(2,1)S(1)} %slice.325), channel_id=1, source_target_pairs={{0,2},{1,3},{2,0},{3,1},{4,6},{5,7},{6,4},{7,5},{8,10},{9,11},{10,... | collective-permute-start | bytes 786440 | tf_op jit(solution)/shard_map/ppermute | solution.py:24
  203.4 8.2 %collective-permute-start.38 = (bf16[64,2048]{1,0:T(8,128)(2,1)S(1)}, bf16[64,2048]{1,0:T(8,128)(2,1)S(1)}, u32[]{:S(2)}, u32[]{:S(2)}) collective-permute-start(bf16[64,2048]{1,0:T(8,128)(2,1)S(1)} %add_convert_fusion.12), channel_id=1, source_target_pairs={{0,12},{1,13},{2,14},{3,15},{4,0},{5,1},{6,2},{7,3},{8,4},{9,5},{1... | collective-permute-start | bytes 786440 | tf_op jit(solution)/shard_map/ppermute | solution.py:21
  205.1 10.0 %collective-permute-start.52 = (bf16[64,2048]{1,0:T(8,128)(2,1)S(1)}, bf16[64,2048]{1,0:T(8,128)(2,1)S(1)}, u32[]{:S(2)}, u32[]{:S(2)}) collective-permute-start(bf16[64,2048]{1,0:T(8,128)(2,1)S(1)} %slice.329), channel_id=1, source_target_pairs={{0,2},{1,3},{2,0},{3,1},{4,6},{5,7},{6,4},{7,5},{8,10},{9,11},{10,... | collective-permute-start | bytes 786440 | tf_op jit(solution)/shard_map/ppermute | solution.py:24
  210.9 11.8 %collective-permute-start.50 = (bf16[64,2048]{1,0:T(8,128)(2,1)S(1)}, bf16[64,2048]{1,0:T(8,128)(2,1)S(1)}, u32[]{:S(2)}, u32[]{:S(2)}) collective-permute-start(bf16[64,2048]{1,0:T(8,128)(2,1)S(1)} %add_convert_fusion.10), channel_id=1, source_target_pairs={{0,8},{1,9},{2,10},{3,11},{4,12},{5,13},{6,14},{7,15},{8,0},{9,1},... | collective-permute-start | bytes 786440 | tf_op jit(solution)/shard_map/ppermute | solution.py:21
  (16 other events, 175.0 us)

commit v4 on v1

v4 whole, which is shorter than its diff:
```python
import jax
import jax.numpy as jnp
from jax import lax
from jax.sharding import PartitionSpec as P

EPSILON = 1e-06
PLANES = 4
ORDER = (0, 1, 2, 3)


class Ring:
    def __init__(self):
        self.size = lax.axis_size("inner")
        self.plane = self.size // PLANES
        self.me = lax.axis_index("inner")
        self.z = self.me // self.plane
        self.inside = (self.z == 1) | (self.z == 2)
        self.bits = []
        bit = self.plane // 2
        while bit:
            self.bits.append(bit)
            bit //= 2

    def send(self, values, pairs):
        perm = [(a * self.plane + i, b * self.plane + i) for a, b in pairs for i in range(self.plane)]
        return lax.ppermute(values, "inner", perm)

    def across(self, values, bit):
        return lax.ppermute(values, "inner", [(d, d ^ bit) for d in range(self.size)])

    def high(self, bit):
        return (self.me // bit) % 2 == 1


def after(values, *others):
    return lax.optimization_barrier((values, *others))[0]


def add(*terms):
    return sum(t.astype(jnp.float32) for t in terms).astype(jnp.bfloat16)


def gather_rows(ring, rows, work):
    def fill(column, ties):
        for i, bit in enumerate(ring.bits):
            if i == 1:
                column = after(column, *ties)
            column = jnp.concatenate([column, ring.across(column, bit)], axis=0)
        return column

    done = {}
    slots = {0: rows}
    chunk0 = fill(rows, [])
    slots[1] = ring.send(rows, [(0, 1), (1, 0), (2, 3), (3, 2)])
    middle = ring.send(rows, [(1, 2), (2, 1)])
    chunk1 = fill(slots[1], [])
    near = ring.send(middle, [(1, 0), (2, 3)])
    far = ring.send(slots[1], [(1, 2), (2, 1)])
    slots[2] = jnp.where(ring.inside, far, near)
    done[0] = work(0, chunk0)
    chunk2 = fill(after(slots[2], done[0]), [])
    outer = ring.send(slots[2], [(1, 0), (2, 3)])
    slots[3] = jnp.where(ring.inside, middle, outer)
    done[1] = work(1, after(chunk1, done[0]))
    column3 = after(slots[3], done[1])
    done[2] = work(2, after(chunk2, done[1]))
    chunk3 = fill(column3, [done[2]])
    return done, chunk3


def within_plane(ring, chunk):
    for bit in reversed(ring.bits[1:]):
        rows = chunk.shape[0] // 2
        chunk = add(chunk[:rows], ring.across(chunk[rows:], bit))
    return chunk


def plane_sums(ring, part):
    two = part(2)
    inward = ring.send(two, [(0, 1), (3, 2)])
    swapped = ring.send(two, [(1, 2), (2, 1)])
    three = part(3)
    ends = ring.send(three, [(0, 3), (3, 0)])
    middle = ring.send(add(three, inward), [(1, 2), (2, 1)])
    one = ring.send(add(part(1), swapped), [(0, 1), (1, 0), (2, 3), (3, 2)])
    return sum(t.astype(jnp.float32) for t in (part(0), one, middle, ends))


def gate_halves(layers, experts):
    columns = []
    for routes, gates in layers:
        named = routes[:, :, None] == jnp.arange(experts, dtype=jnp.int32)[None, None, :]
        table = jnp.sum(jnp.where(named, gates[:, :, None], 0.0), axis=1)
        high = table.astype(jnp.bfloat16)
        columns += [high, (table - high.astype(jnp.float32)).astype(jnp.bfloat16)]
    spare = -2 * experts * len(layers) % 128
    return jnp.concatenate(columns + [jnp.zeros((columns[0].shape[0], spare), jnp.bfloat16)], axis=1)


def gate_column(ring, halves, layer):
    lane = jnp.arange(halves.shape[1], dtype=jnp.int32)[None, :]
    first = 2 * layer * ring.size + ring.me
    mine = (lane == first) | (lane == first + ring.size)
    return jnp.sum(jnp.where(mine, halves.astype(jnp.float32), 0.0), axis=1, keepdims=True)


def normed(values, gain):
    widened = values.astype(jnp.float32)
    inverse = lax.rsqrt(jnp.mean(widened * widened, axis=-1, keepdims=True) + EPSILON)
    return (widened * inverse * gain).astype(jnp.bfloat16)


def expert(rows, gates, gate_up, down):
    width = down.shape[0]
    projected = jnp.dot(rows, gate_up, preferred_element_type=jnp.float32)
    hidden = (jax.nn.silu(projected[:, :width]) * projected[:, width:]).astype(jnp.bfloat16)
    out = jnp.dot(hidden, down, preferred_element_type=jnp.float32)
    return (out * gates).astype(jnp.bfloat16)


def routed(ring, rows, work):
    done, chunk3 = gather_rows(ring, rows, work)
    halves = {2: within_plane(ring, done[2])}
    done[3] = work(3, after(chunk3, halves[2]))
    for slot in (3, 1, 0):
        halves[slot] = within_plane(ring, done[slot])
    own = rows.shape[0]
    crossed = {}
    for slot, earlier in ((2, []), (3, []), (1, [2]), (0, [3])):
        away = after(halves[slot][own:], *[crossed[e] for e in earlier], halves[3] if earlier else halves[2])
        crossed[slot] = ring.across(away, ring.bits[0])
    return plane_sums(ring, lambda slot: add(halves[slot][:own], crossed[slot]))


def plane_weight(ring, weight, groups):
    rows = weight.shape[0]
    first = ring.bits[0]
    if groups % 2:
        other = ring.across(weight, first)
    else:
        odd = lax.axis_index("groups") % 2
        sent = lax.dynamic_slice_in_dim(weight, odd * (rows // 2), rows // 2, axis=0)
        here = ring.across(sent, first)
        there = lax.ppermute(here, "groups", [(g, g ^ 1) for g in range(groups)])
        other = jnp.where(odd == 0, jnp.concatenate([here, there]), jnp.concatenate([there, here]))
    held = jnp.where(ring.high(first), jnp.stack([other, weight]), jnp.stack([weight, other]))
    for i, bit in enumerate(ring.bits[1:]):
        other = ring.across(held, bit)
        axis = i + 1
        held = jnp.where(ring.high(bit), jnp.stack([other, held], axis), jnp.stack([held, other], axis))
    return held.reshape(ring.plane * rows, weight.shape[1])


def merge(ring, merged_in, weight):
    share = merged_in.shape[1] // PLANES
    products = {}
    for slot in (2, 3, 1, 0):
        piece = lax.dynamic_slice_in_dim(merged_in, (ring.z ^ slot) * share, share, axis=1)
        if slot:
            piece = ring.send(piece, [(p, p ^ slot) for p in range(PLANES)])
        products[slot] = jnp.dot(piece, weight, preferred_element_type=jnp.float32)
        if slot:
            products[slot] = products[slot].astype(jnp.bfloat16)
    return plane_sums(ring, lambda slot: products[slot])


def local(
    hidden_rows,
    token_embed,
    first_routes,
    first_gates,
    first_gate_up,
    first_down,
    second_routes,
    second_gates,
    second_gate_up,
    second_down,
    hidden_gain,
    embed_gain,
    merge_weight,
):
    ring = Ring()
    width = hidden_rows.shape[1]
    halves = gate_halves([(first_routes, first_gates), (second_routes, second_gates)], ring.size)
    weight = plane_weight(ring, merge_weight, lax.axis_size("groups"))
    second_columns = {}

    def first_work(slot, chunk):
        second_columns[slot] = gate_column(ring, chunk[:, width:], 1)
        gates = gate_column(ring, chunk[:, width:], 0)
        return expert(chunk[:, :width], gates, first_gate_up[0], first_down[0])

    def second_work(slot, chunk):
        return expert(chunk, second_columns[slot], second_gate_up[0], second_down[0])

    first = routed(ring, jnp.concatenate([hidden_rows, halves], axis=1), first_work)
    after_first = (hidden_rows.astype(jnp.float32) + first).astype(jnp.bfloat16)
    merged_in = jnp.concatenate([normed(after_first, hidden_gain), normed(token_embed, embed_gain)], axis=1)
    merged = merge(ring, merged_in, weight)
    after_merge = (after_first.astype(jnp.float32) + jax.nn.silu(merged)).astype(jnp.bfloat16)
    second = routed(ring, after_merge, second_work)
    return (after_merge.astype(jnp.float32) + second).astype(jnp.bfloat16)


def solution(mesh):
    rows = P(("groups", "inner"), None)
    weight = P("inner", None, None)
    return jax.shard_map(
        local,
        mesh=mesh,
        in_specs=(rows, rows, rows, rows, weight, weight, rows, rows, weight, weight, P(), P(), P("inner", None)),
        out_specs=rows,
        check_vma=False,
    )
```

time: 385 us -> 220 us (0.57)
  waiting for transfers between devices: 303 us -> 96.3 us
  starting transfers between devices: 0.17 us -> 84.7 us
  blocking collectives: 31.6 us -> 0 us
  between operations: 13.3 us -> 1.21 us
  matrix products: 27.1 us -> 21.9 us
    reduce_scatter x3 -> x0, waiting for transfers between devices: 213 us -> none  [the longest x2 141 us: routed(): return lax.psum_scatter(part, 'inner', scatter_dimension=0, tiled=True)]
    ppermute x0 -> x63, waiting for transfers between devices: none -> 96.3 us  [the longest x34 55.6 us: across(): lax.ppermute(values, 'inner', [(d, d ^ bit) for d in range(self.size)])]
    all_gather x2 -> x0, waiting for transfers between devices: 88.9 us -> none  [routed(): every = lax.all_gather(rows, 'inner', axis=0, tiled=True)]
    ppermute x0 -> x63, starting transfers between devices: none -> 84.7 us  [the longest x28 55.2 us: send(): return lax.ppermute(values, 'inner', perm)]
    all_to_all x2 -> x0, blocking collectives: 31.6 us -> none  [the longest x1 18 us: local(): lax.all_to_all(merged_in, 'inner', split_axis=1, concat_axis=0, tiled=True)]
    dot_general x2 -> x8, matrix products: 15.1 us -> 12.4 us  [expert(): projected = jnp.dot(rows, gate_up, preferred_element_type=jnp.float32)]
    dot_general x2 -> x8, matrix products: 8.72 us -> 6.1 us  [expert(): out = jnp.dot(hidden, down, preferred_element_type=jnp.float32)]
  transfers between devices with their start and end apart: 5 -> 63, of which waited for: 5 -> 24; matrix products, arithmetic and copies ran while one was open for 1% -> 15% of each run, Pallas kernels for 0% -> 0%
where the time goes in v4:
time: 220 us; the launch traced here: 219 us
  waiting for transfers between devices  96.3 us (44%)
  starting transfers between devices  84.7 us (38%)
  matrix products  21.9 us (10%)
  other arithmetic  11.3 us (5%)
  local copies, waits for them, and re-layouts  3.87 us (2%)
    ppermute x34, waiting for transfers between devices, across(): lax.ppermute(values, 'inner', [(d, d ^ bit) for d in range(self.size)])  55.6 us
    ppermute x28, starting transfers between devices, send(): return lax.ppermute(values, 'inner', perm)  55.2 us
    ppermute x28, waiting for transfers between devices, send(): return lax.ppermute(values, 'inner', perm)  40.7 us
    ppermute x34, starting transfers between devices, across(): lax.ppermute(values, 'inner', [(d, d ^ bit) for d in range(self.size)])  28 us
    dot_general x8, matrix products, expert(): projected = jnp.dot(rows, gate_up, preferred_element_type=jnp.float32)  12.4 us
    dot_general x8, matrix products, expert(): out = jnp.dot(hidden, down, preferred_element_type=jnp.float32)  6.1 us
  transfers between devices with their start and end apart: 63, of which 24 were waited for; matrix products, arithmetic and copies ran while one was open for 15% of the time, Pallas kernels for 0%

profile of v4, /device:TPU:0, one launch (start us, length us, event | category | flops | bytes accessed | tf_op | source)
XLA Modules:
  0.0 219.2 jit_solution(17435528972171008703)
XLA Ops:
  3.1 3.1 %collective-permute-start.4 = (bf16[64,2176]{1,0:T(8,128)(2,1)S(1)}, bf16[64,2176]{1,0:T(8,128)(2,1)}, u32[]{:S(2)}, u32[]{:S(2)}) collective-permute-start(bf16[64,2176]{1,0:T(8,128)(2,1)S(1)} %concatenate.110), channel_id=1, source_target_pairs={{0,4},{1,5},{2,6},{3,7},{4,0},{5,1},{6,2},{7,3},{8,12},{9,13},{10,... | collective-permute-start | bytes 835592 | tf_op jit(solution)/shard_map/ppermute | solution.py:26
  7.6 1.5 collective-permute-start
  9.1 1.9 constant_dynamic-slice_fusion
  13.0 1.7 collective-permute-start.8
  14.6 2.6 %collective-permute-done = bf16[64,2176]{1,0:T(8,128)(2,1)} collective-permute-done((bf16[64,2176]{1,0:T(8,128)(2,1)S(1)}, bf16[64,2176]{1,0:T(8,128)(2,1)}, u32[]{:S(2)}, u32[]{:S(2)}) %collective-permute-start) | collective-permute-done | bytes 278560 | tf_op jit(solution)/shard_map/ppermute | solution.py:29
  20.3 8.1 %collective-permute-done.26 = bf16[128,2048]{1,0:T(8,128)(2,1)S(1)} collective-permute-done((bf16[128,2048]{1,0:T(8,128)(2,1)}, bf16[128,2048]{1,0:T(8,128)(2,1)S(1)}, u32[]{:S(2)}, u32[]{:S(2)}) %collective-permute-start.26) | collective-permute-done | bytes 524320 | tf_op jit(solution)/shard_map/ppermute | solution.py:29
  28.4 1.5 collective-permute-start.27
  29.9 3.0 %collective-permute-done.8 = bf16[64,2176]{1,0:T(8,128)(2,1)S(1)} collective-permute-done((bf16[64,2176]{1,0:T(8,128)(2,1)}, bf16[64,2176]{1,0:T(8,128)(2,1)S(1)}, u32[]{:S(2)}, u32[]{:S(2)}) %collective-permute-start.8) | collective-permute-done | bytes 278560 | tf_op jit(solution)/shard_map/ppermute | solution.py:29
  35.3 3.5 %fusion.14 = f32[256,1024]{1,0:T(8,128)S(1)} fusion(bf16[1,2048,1024]{2,1,0:T(8,128)(2,1)} %param.17, bf16[128,2176]{1,0:T(8,128)(2,1)S(1)} %pad_maximum_fusion.6, bf16[128,2176]{1,0:T(8,128)(2,1)S(1)} %collective-permute-done.1), kind=kOutput, calls=%fused_computation.15 | convolution fusion | flops 1075838976 | bytes 6356992 | tf_op jit(solution)/shard_map/dot_general | solution.py:115
  39.8 1.6 collective-permute-start.11
  41.6 2.3 %collective-permute-done.7 = bf16[64,2176]{1,0:T(8,128)(2,1)S(1)} collective-permute-done((bf16[64,2176]{1,0:T(8,128)(2,1)S(1)}, bf16[64,2176]{1,0:T(8,128)(2,1)S(1)}, u32[]{:S(2)}, u32[]{:S(2)}) %collective-permute-start.7) | collective-permute-done | bytes 278560 | tf_op jit(solution)/shard_map/ppermute | solution.py:26
  44.2 4.7 %collective-permute-done.11 = bf16[64,2176]{1,0:T(8,128)(2,1)S(1)} collective-permute-done((bf16[64,2176]{1,0:T(8,128)(2,1)S(1)}, bf16[64,2176]{1,0:T(8,128)(2,1)S(1)}, u32[]{:S(2)}, u32[]{:S(2)}) %collective-permute-start.11) | collective-permute-done | bytes 278560 | tf_op jit(solution)/shard_map/ppermute | solution.py:29
  51.3 1.6 collective-permute-start.10
  55.5 4.9 %collective-permute-done.10 = bf16[64,2176]{1,0:T(8,128)(2,1)S(1)} collective-permute-done((bf16[64,2176]{1,0:T(8,128)(2,1)S(1)}, bf16[64,2176]{1,0:T(8,128)(2,1)S(1)}, u32[]{:S(2)}, u32[]{:S(2)}) %collective-permute-start.10) | collective-permute-done | bytes 278560 | tf_op jit(solution)/shard_map/ppermute | solution.py:29
  61.7 1.6 collective-permute-start.19
  66.1 4.4 %collective-permute-done.19 = bf16[64,2048]{1,0:T(8,128)(2,1)S(1)} collective-permute-done((bf16[64,2048]{1,0:T(8,128)(2,1)S(1)}, bf16[64,2048]{1,0:T(8,128)(2,1)S(1)}, u32[]{:S(2)}, u32[]{:S(2)}) %collective-permute-start.19) | collective-permute-done | bytes 262176 | tf_op jit(solution)/shard_map/ppermute | solution.py:29
  70.5 5.4 %collective-permute-start.23 = (bf16[64,2048]{1,0:T(8,128)(2,1)S(1)}, bf16[64,2048]{1,0:T(8,128)(2,1)S(1)}, u32[]{:S(2)}, u32[]{:S(2)}) collective-permute-start(bf16[64,2048]{1,0:T(8,128)(2,1)S(1)} %add_convert_fusion.20), channel_id=1, source_target_pairs={{0,4},{1,5},{2,6},{3,7},{12,8},{13,9},{14,10},{15,11},{16,20},{17,... | collective-permute-start | bytes 786440 | tf_op jit(solution)/shard_map/ppermute | solution.py:26
  76.1 1.6 collective-permute-start.16
  79.1 6.3 %collective-permute-done.16 = bf16[64,2048]{1,0:T(8,128)(2,1)S(1)} collective-permute-done((bf16[64,2048]{1,0:T(8,128)(2,1)S(1)}, bf16[64,2048]{1,0:T(8,128)(2,1)S(1)}, u32[]{:S(2)}, u32[]{:S(2)}) %collective-permute-start.16) | collective-permute-done | bytes 262176 | tf_op jit(solution)/shard_map/ppermute | solution.py:29
  86.2 3.7 %collective-permute-start.25 = (bf16[64,2048]{1,0:T(8,128)(2,1)S(1)}, bf16[64,2048]{1,0:T(8,128)(2,1)S(1)}, u32[]{:S(2)}, u32[]{:S(2)}) collective-permute-start(bf16[64,2048]{1,0:T(8,128)(2,1)S(1)} %get-tuple-element.58), channel_id=1, source_target_pairs={{0,12},{1,13},{2,14},{3,15},{12,0},{13,1},{14,2},{15,3},{16,28},{1... | collective-permute-start | bytes 786440 | tf_op jit(solution)/shard_map/ppermute | solution.py:26
  90.0 1.6 collective-permute-start.17
  92.1 5.9 %collective-permute-done.25 = bf16[64,2048]{1,0:T(8,128)(2,1)S(1)} collective-permute-done((bf16[64,2048]{1,0:T(8,128)(2,1)S(1)}, bf16[64,2048]{1,0:T(8,128)(2,1)S(1)}, u32[]{:S(2)}, u32[]{:S(2)}) %collective-permute-start.25) | collective-permute-done | bytes 262176 | tf_op jit(solution)/shard_map/ppermute | solution.py:26
  98.0 2.8 %collective-permute-done.22 = bf16[64,2048]{1,0:T(8,128)(2,1)S(1)} collective-permute-done((bf16[64,2048]{1,0:T(8,128)(2,1)S(1)}, bf16[64,2048]{1,0:T(8,128)(2,1)S(1)}, u32[]{:S(2)}, u32[]{:S(2)}) %collective-permute-start.22) | collective-permute-done | bytes 262176 | tf_op jit(solution)/shard_map/ppermute | solution.py:26
  102.8 1.8 collective-permute-start.29
  104.5 2.2 collective-permute-start.33
  106.7 3.7 %collective-permute-done.30 = bf16[64,1024]{1,0:T(8,128)(2,1)S(1)} collective-permute-done((bf16[64,1024]{1,0:T(8,128)(2,1)S(1)}, bf16[64,1024]{1,0:T(8,128)(2,1)S(1)}, u32[]{:S(2)}, u32[]{:S(2)}) %collective-permute-start.30) | collective-permute-done | bytes 131104 | tf_op jit(solution)/shard_map/ppermute | solution.py:26
  111.3 2.1 collective-permute-start.34
  114.9 4.6 %collective-permute-start.36 = (bf16[64,2048]{1,0:T(8,128)(2,1)S(1)}, bf16[64,2048]{1,0:T(8,128)(2,1)S(1)}, u32[]{:S(2)}, u32[]{:S(2)}) collective-permute-start(bf16[64,2048]{1,0:T(8,128)(2,1)S(1)} %convolution_convert_fusion), channel_id=1, source_target_pairs={{0,12},{1,13},{2,14},{3,15},{12,0},{13,1},{14,2},{15,3},{16,28},{1... | collective-permute-start | bytes 786440 | tf_op jit(solution)/shard_map/ppermute | solution.py:26
  121.6 7.0 %collective-permute-start.32 = (bf16[64,2048]{1,0:T(8,128)(2,1)S(1)}, bf16[64,2048]{1,0:T(8,128)(2,1)S(1)}, u32[]{:S(2)}, u32[]{:S(2)}) collective-permute-start(bf16[64,2048]{1,0:T(8,128)(2,1)S(1)} %fusion.26), channel_id=1, source_target_pairs={{0,4},{1,5},{2,6},{3,7},{4,0},{5,1},{6,2},{7,3},{8,12},{9,13},{10,... | collective-permute-start | bytes 786440 | tf_op jit(solution)/shard_map/ppermute | solution.py:26
  129.5 6.0 %collective-permute-done.32 = bf16[64,2048]{1,0:T(8,128)(2,1)S(1)} collective-permute-done((bf16[64,2048]{1,0:T(8,128)(2,1)S(1)}, bf16[64,2048]{1,0:T(8,128)(2,1)S(1)}, u32[]{:S(2)}, u32[]{:S(2)}) %collective-permute-start.32) | collective-permute-done | bytes 262176 | tf_op jit(solution)/shard_map/ppermute | solution.py:26
  135.7 2.4 %collective-permute-start.41 = (bf16[64,2048]{1,0:T(8,128)(2,1)S(1)}, bf16[64,2048]{1,0:T(8,128)(2,1)S(1)}, u32[]{:S(2)}, u32[]{:S(2)}) collective-permute-start(bf16[64,2048]{1,0:T(8,128)(2,1)S(1)} %fusion.49), channel_id=1, source_target_pairs={{0,4},{1,5},{2,6},{3,7},{4,0},{5,1},{6,2},{7,3},{8,12},{9,13},{10,... | collective-permute-start | bytes 786440 | tf_op jit(solution)/shard_map/ppermute | solution.py:26
  138.7 2.5 %collective-permute-start.37 = (bf16[64,2048]{1,0:T(8,128)(2,1)S(1)}, bf16[64,2048]{1,0:T(8,128)(2,1)S(1)}, u32[]{:S(2)}, u32[]{:S(2)}) collective-permute-start(bf16[64,2048]{1,0:T(8,128)(2,1)S(1)} %fusion.49), channel_id=1, source_target_pairs={{0,2},{1,3},{2,0},{3,1},{4,6},{5,7},{6,4},{7,5},{8,10},{9,11},{10,... | collective-permute-start | bytes 786440 | tf_op jit(solution)/shard_map/ppermute | solution.py:29
  142.4 2.9 %collective-permute-start.45 = (bf16[64,2048]{1,0:T(8,128)(2,1)S(1)}, bf16[64,2048]{1,0:T(8,128)(2,1)S(1)}, u32[]{:S(2)}, u32[]{:S(2)}) collective-permute-start(bf16[64,2048]{1,0:T(8,128)(2,1)S(1)} %collective-permute-done.41), channel_id=1, source_target_pairs={{0,2},{1,3},{2,0},{3,1},{4,6},{5,7},{6,4},{7,5},{8,10},{9,11},{10,... | collective-permute-start | bytes 786440 | tf_op jit(solution)/shard_map/ppermute | solution.py:29
  147.5 2.2 %collective-permute-done.45 = bf16[64,2048]{1,0:T(8,128)(2,1)S(1)} collective-permute-done((bf16[64,2048]{1,0:T(8,128)(2,1)S(1)}, bf16[64,2048]{1,0:T(8,128)(2,1)S(1)}, u32[]{:S(2)}, u32[]{:S(2)}) %collective-permute-start.45) | collective-permute-done | bytes 262176 | tf_op jit(solution)/shard_map/ppermute | solution.py:29
  149.7 5.9 %collective-permute-done.43 = bf16[64,2048]{1,0:T(8,128)(2,1)S(1)} collective-permute-done((bf16[64,2048]{1,0:T(8,128)(2,1)S(1)}, bf16[64,2048]{1,0:T(8,128)(2,1)S(1)}, u32[]{:S(2)}, u32[]{:S(2)}) %collective-permute-start.43) | collective-permute-done | bytes 262176 | tf_op jit(solution)/shard_map/ppermute | solution.py:26
  159.2 1.6 collective-permute-start.48
  160.8 3.3 %collective-permute-done.44 = bf16[64,2048]{1,0:T(8,128)(2,1)S(1)} collective-permute-done((bf16[64,2048]{1,0:T(8,128)(2,1)S(1)}, bf16[64,2048]{1,0:T(8,128)(2,1)S(1)}, u32[]{:S(2)}, u32[]{:S(2)}) %collective-permute-start.44) | collective-permute-done | bytes 262176 | tf_op jit(solution)/shard_map/ppermute | solution.py:26
  164.1 3.9 %collective-permute-done.48 = bf16[64,2048]{1,0:T(8,128)(2,1)S(1)} collective-permute-done((bf16[64,2048]{1,0:T(8,128)(2,1)S(1)}, bf16[64,2048]{1,0:T(8,128)(2,1)S(1)}, u32[]{:S(2)}, u32[]{:S(2)}) %collective-permute-start.48) | collective-permute-done | bytes 262176 | tf_op jit(solution)/shard_map/ppermute | solution.py:29
  170.3 1.6 collective-permute-start.47
  174.3 4.7 %collective-permute-done.47 = bf16[64,2048]{1,0:T(8,128)(2,1)S(1)} collective-permute-done((bf16[64,2048]{1,0:T(8,128)(2,1)S(1)}, bf16[64,2048]{1,0:T(8,128)(2,1)S(1)}, u32[]{:S(2)}, u32[]{:S(2)}) %collective-permute-start.47) | collective-permute-done | bytes 262176 | tf_op jit(solution)/shard_map/ppermute | solution.py:29
  180.1 1.6 collective-permute-start.56
  184.3 4.6 %collective-permute-done.56 = bf16[64,2048]{1,0:T(8,128)(2,1)S(1)} collective-permute-done((bf16[64,2048]{1,0:T(8,128)(2,1)S(1)}, bf16[64,2048]{1,0:T(8,128)(2,1)S(1)}, u32[]{:S(2)}, u32[]{:S(2)}) %collective-permute-start.56) | collective-permute-done | bytes 262176 | tf_op jit(solution)/shard_map/ppermute | solution.py:29
  188.9 4.6 %collective-permute-start.60 = (bf16[64,2048]{1,0:T(8,128)(2,1)S(1)}, bf16[64,2048]{1,0:T(8,128)(2,1)S(1)}, u32[]{:S(2)}, u32[]{:S(2)}) collective-permute-start(bf16[64,2048]{1,0:T(8,128)(2,1)S(1)} %add_convert_fusion.12), channel_id=1, source_target_pairs={{0,4},{1,5},{2,6},{3,7},{12,8},{13,9},{14,10},{15,11},{16,20},{17,... | collective-permute-start | bytes 786440 | tf_op jit(solution)/shard_map/ppermute | solution.py:26
  193.6 1.6 collective-permute-start.53
  196.8 6.2 %collective-permute-done.53 = bf16[64,2048]{1,0:T(8,128)(2,1)S(1)} collective-permute-done((bf16[64,2048]{1,0:T(8,128)(2,1)S(1)}, bf16[64,2048]{1,0:T(8,128)(2,1)S(1)}, u32[]{:S(2)}, u32[]{:S(2)}) %collective-permute-start.53) | collective-permute-done | bytes 262176 | tf_op jit(solution)/shard_map/ppermute | solution.py:29
  203.8 4.8 %collective-permute-start.62 = (bf16[64,2048]{1,0:T(8,128)(2,1)S(1)}, bf16[64,2048]{1,0:T(8,128)(2,1)S(1)}, u32[]{:S(2)}, u32[]{:S(2)}) collective-permute-start(bf16[64,2048]{1,0:T(8,128)(2,1)S(1)} %get-tuple-element.54), channel_id=1, source_target_pairs={{0,12},{1,13},{2,14},{3,15},{12,0},{13,1},{14,2},{15,3},{16,28},{1... | collective-permute-start | bytes 786440 | tf_op jit(solution)/shard_map/ppermute | solution.py:26
  209.1 6.4 %collective-permute-done.62 = bf16[64,2048]{1,0:T(8,128)(2,1)S(1)} collective-permute-done((bf16[64,2048]{1,0:T(8,128)(2,1)S(1)}, bf16[64,2048]{1,0:T(8,128)(2,1)S(1)}, u32[]{:S(2)}, u32[]{:S(2)}) %collective-permute-start.62) | collective-permute-done | bytes 262176 | tf_op jit(solution)/shard_map/ppermute | solution.py:26
  215.6 2.7 %collective-permute-done.59 = bf16[64,2048]{1,0:T(8,128)(2,1)S(1)} collective-permute-done((bf16[64,2048]{1,0:T(8,128)(2,1)S(1)}, bf16[64,2048]{1,0:T(8,128)(2,1)S(1)}, u32[]{:S(2)}, u32[]{:S(2)}) %collective-permute-start.59) | collective-permute-done | bytes 262176 | tf_op jit(solution)/shard_map/ppermute | solution.py:26
  (196 shorter events, 52.3 us)
Async XLA Ops:
  3.1 9.9 %collective-permute-start.4 = (bf16[64,2176]{1,0:T(8,128)(2,1)S(1)}, bf16[64,2176]{1,0:T(8,128)(2,1)}, u32[]{:S(2)}, u32[]{:S(2)}) collective-permute-start(bf16[64,2176]{1,0:T(8,128)(2,1)S(1)} %concatenate.110), channel_id=1, source_target_pairs={{0,4},{1,5},{2,6},{3,7},{4,0},{5,1},{6,2},{7,3},{8,12},{9,13},{10,... | collective-permute-start | bytes 835592 | tf_op jit(solution)/shard_map/ppermute | solution.py:26
  6.2 12.8 %collective-permute-start.3 = (bf16[64,2176]{1,0:T(8,128)(2,1)S(1)}, bf16[64,2176]{1,0:T(8,128)(2,1)}, u32[]{:S(2)}, u32[]{:S(2)}) collective-permute-start(bf16[64,2176]{1,0:T(8,128)(2,1)S(1)} %concatenate.110), channel_id=1, source_target_pairs={{4,8},{5,9},{6,10},{7,11},{8,4},{9,5},{10,6},{11,7},{20,24},{21,25... | collective-permute-start | bytes 835592 | tf_op jit(solution)/shard_map/ppermute | solution.py:26
  7.6 9.7 %collective-permute-start = (bf16[64,2176]{1,0:T(8,128)(2,1)S(1)}, bf16[64,2176]{1,0:T(8,128)(2,1)}, u32[]{:S(2)}, u32[]{:S(2)}) collective-permute-start(bf16[64,2176]{1,0:T(8,128)(2,1)S(1)} %concatenate.110), channel_id=1, source_target_pairs={{0,2},{1,3},{2,0},{3,1},{4,6},{5,7},{6,4},{7,5},{8,10},{9,11},{10,... | collective-permute-start | bytes 835592 | tf_op jit(solution)/shard_map/ppermute | solution.py:29
  11.0 17.4 %collective-permute-start.26 = (bf16[128,2048]{1,0:T(8,128)(2,1)}, bf16[128,2048]{1,0:T(8,128)(2,1)S(1)}, u32[]{:S(2)}, u32[]{:S(2)}) collective-permute-start(bf16[128,2048]{1,0:T(8,128)(2,1)} %constant_dynamic-slice_fusion), channel_id=1, source_target_pairs={{0,2},{1,3},{2,0},{3,1},{4,6},{5,7},{6,4},{7,5},{8,10},{9,11},{10,... | collective-permute-start | bytes 1572872 | tf_op jit(solution)/shard_map/ppermute | solution.py:29
  13.0 19.9 %collective-permute-start.8 = (bf16[64,2176]{1,0:T(8,128)(2,1)}, bf16[64,2176]{1,0:T(8,128)(2,1)S(1)}, u32[]{:S(2)}, u32[]{:S(2)}) collective-permute-start(bf16[64,2176]{1,0:T(8,128)(2,1)} %collective-permute-done.4), channel_id=1, source_target_pairs={{0,2},{1,3},{2,0},{3,1},{4,6},{5,7},{6,4},{7,5},{8,10},{9,11},{10,... | collective-permute-start | bytes 835592 | tf_op jit(solution)/shard_map/ppermute | solution.py:29
  18.2 17.1 %collective-permute-start.1 = (bf16[128,2176]{1,0:T(8,128)(2,1)S(1)}, bf16[128,2176]{1,0:T(8,128)(2,1)S(1)}, u32[]{:S(2)}, u32[]{:S(2)}) collective-permute-start(bf16[128,2176]{1,0:T(8,128)(2,1)S(1)} %pad_maximum_fusion.6), channel_id=1, source_target_pairs={{0,1},{1,0},{2,3},{3,2},{4,5},{5,4},{6,7},{7,6},{8,9},{9,8},{10,11... | collective-permute-start | bytes 1671176 | tf_op jit(solution)/shard_map/ppermute | solution.py:29
  18.3 15.6 %collective-permute-start.5 = (bf16[64,2176]{1,0:T(8,128)(2,1)}, bf16[64,2176]{1,0:T(8,128)(2,1)S(1)}, u32[]{:S(2)}, u32[]{:S(2)}) collective-permute-start(bf16[64,2176]{1,0:T(8,128)(2,1)} %collective-permute-done.4), channel_id=1, source_target_pairs={{4,8},{5,9},{6,10},{7,11},{8,4},{9,5},{10,6},{11,7},{20,24},{21,25... | collective-permute-start | bytes 835592 | tf_op jit(solution)/shard_map/ppermute | solution.py:26
  19.0 14.9 %collective-permute-start.6 = (bf16[64,2176]{1,0:T(8,128)(2,1)}, bf16[64,2176]{1,0:T(8,128)(2,1)S(1)}, u32[]{:S(2)}, u32[]{:S(2)}) collective-permute-start(bf16[64,2176]{1,0:T(8,128)(2,1)} %collective-permute-done.3), channel_id=1, source_target_pairs={{4,0},{5,1},{6,2},{7,3},{8,12},{9,13},{10,14},{11,15},{20,16},{21,... | collective-permute-start | bytes 835592 | tf_op jit(solution)/shard_map/ppermute | solution.py:26
  28.4 15.6 %collective-permute-start.27 = (bf16[128,2048]{1,0:T(8,128)(2,1)S(1)}, bf16[128,2048]{1,0:T(8,128)(2,1)S(1)}, u32[]{:S(2)}, u32[]{:S(2)}) collective-permute-start(bf16[128,2048]{1,0:T(8,128)(2,1)S(1)} %collective-permute-done.26), channel_id=1, source_target_pairs={{0,16},{16,0},{1,17},{17,1},{2,18},{18,2},{3,19},{19,3},{4,20},{20... | collective-permute-start | bytes 1572872 | tf_op jit(solution)/shard_map/ppermute | solution.py:144
  33.9 9.9 %collective-permute-start.7 = (bf16[64,2176]{1,0:T(8,128)(2,1)S(1)}, bf16[64,2176]{1,0:T(8,128)(2,1)S(1)}, u32[]{:S(2)}, u32[]{:S(2)}) collective-permute-start(bf16[64,2176]{1,0:T(8,128)(2,1)S(1)} %broadcast_select_fusion.1), channel_id=1, source_target_pairs={{4,0},{5,1},{6,2},{7,3},{8,12},{9,13},{10,14},{11,15},{20,16},{21,... | collective-permute-start | bytes 835592 | tf_op jit(solution)/shard_map/ppermute | solution.py:26
  35.2 13.8 %collective-permute-start.9 = (bf16[128,2176]{1,0:T(8,128)(2,1)S(1)}, bf16[128,2176]{1,0:T(8,128)(2,1)S(1)}, u32[]{:S(2)}, u32[]{:S(2)}) collective-permute-start(bf16[128,2176]{1,0:T(8,128)(2,1)S(1)} %pad_maximum_fusion.7), channel_id=1, source_target_pairs={{0,1},{1,0},{2,3},{3,2},{4,5},{5,4},{6,7},{7,6},{8,9},{9,8},{10,11... | collective-permute-start | bytes 1671176 | tf_op jit(solution)/shard_map/ppermute | solution.py:29
  39.8 9.1 %collective-permute-start.11 = (bf16[64,2176]{1,0:T(8,128)(2,1)S(1)}, bf16[64,2176]{1,0:T(8,128)(2,1)S(1)}, u32[]{:S(2)}, u32[]{:S(2)}) collective-permute-start(bf16[64,2176]{1,0:T(8,128)(2,1)S(1)} %broadcast_select_fusion.1), channel_id=1, source_target_pairs={{0,2},{1,3},{2,0},{3,1},{4,6},{5,7},{6,4},{7,5},{8,10},{9,11},{10,... | collective-permute-start | bytes 835592 | tf_op jit(solution)/shard_map/ppermute | solution.py:29
  41.3 24.6 %collective-permute-start.2 = (bf16[128,2048]{1,0:T(8,128)(2,1)S(1)}, bf16[128,2048]{1,0:T(8,128)(2,1)S(1)}, u32[]{:S(2)}, u32[]{:S(2)}) collective-permute-start(bf16[128,2048]{1,0:T(8,128)(2,1)S(1)} %slice.233), channel_id=1, source_target_pairs={{0,1},{1,0},{2,3},{3,2},{4,5},{5,4},{6,7},{7,6},{8,9},{9,8},{10,11... | collective-permute-start | bytes 1572872 | tf_op jit(solution)/shard_map/ppermute | solution.py:29
  51.3 9.1 %collective-permute-start.10 = (bf16[64,2176]{1,0:T(8,128)(2,1)S(1)}, bf16[64,2176]{1,0:T(8,128)(2,1)S(1)}, u32[]{:S(2)}, u32[]{:S(2)}) collective-permute-start(bf16[64,2176]{1,0:T(8,128)(2,1)S(1)} %broadcast_select_fusion), channel_id=1, source_target_pairs={{0,2},{1,3},{2,0},{3,1},{4,6},{5,7},{6,4},{7,5},{8,10},{9,11},{10,... | collective-permute-start | bytes 835592 | tf_op jit(solution)/shard_map/ppermute | solution.py:29
  60.9 41.2 %collective-permute-start.28 = (bf16[2,256,2048]{2,1,0:T(8,128)(2,1)S(1)}, bf16[2,256,2048]{2,1,0:T(8,128)(2,1)S(1)}, u32[]{:S(2)}, u32[]{:S(2)}) collective-permute-start(bf16[2,256,2048]{2,1,0:T(8,128)(2,1)S(1)} %maximum_select_fusion.1), channel_id=1, source_target_pairs={{0,1},{1,0},{2,3},{3,2},{4,5},{5,4},{6,7},{7,6},{8,9},{9,8},{10,11... | collective-permute-start | bytes 6291464 | tf_op jit(solution)/shard_map/ppermute | solution.py:29
  61.4 16.3 %collective-permute-start.18 = (bf16[128,2048]{1,0:T(8,128)(2,1)S(1)}, bf16[128,2048]{1,0:T(8,128)(2,1)S(1)}, u32[]{:S(2)}, u32[]{:S(2)}) collective-permute-start(bf16[128,2048]{1,0:T(8,128)(2,1)S(1)} %slice.248), channel_id=1, source_target_pairs={{0,1},{1,0},{2,3},{3,2},{4,5},{5,4},{6,7},{7,6},{8,9},{9,8},{10,11... | collective-permute-start | bytes 1572872 | tf_op jit(solution)/shard_map/ppermute | solution.py:29
  61.7 8.8 %collective-permute-start.19 = (bf16[64,2048]{1,0:T(8,128)(2,1)S(1)}, bf16[64,2048]{1,0:T(8,128)(2,1)S(1)}, u32[]{:S(2)}, u32[]{:S(2)}) collective-permute-start(bf16[64,2048]{1,0:T(8,128)(2,1)S(1)} %slice.251), channel_id=1, source_target_pairs={{0,2},{1,3},{2,0},{3,1},{4,6},{5,7},{6,4},{7,5},{8,10},{9,11},{10,... | collective-permute-start | bytes 786440 | tf_op jit(solution)/shard_map/ppermute | solution.py:29
  65.6 10.3 %collective-permute-start.15 = (bf16[128,2048]{1,0:T(8,128)(2,1)S(1)}, bf16[128,2048]{1,0:T(8,128)(2,1)S(1)}, u32[]{:S(2)}, u32[]{:S(2)}) collective-permute-start(bf16[128,2048]{1,0:T(8,128)(2,1)S(1)} %slice.245), channel_id=1, source_target_pairs={{0,1},{1,0},{2,3},{3,2},{4,5},{5,4},{6,7},{7,6},{8,9},{9,8},{10,11... | collective-permute-start | bytes 1572872 | tf_op jit(solution)/shard_map/ppermute | solution.py:29
  70.5 14.9 %collective-permute-start.23 = (bf16[64,2048]{1,0:T(8,128)(2,1)S(1)}, bf16[64,2048]{1,0:T(8,128)(2,1)S(1)}, u32[]{:S(2)}, u32[]{:S(2)}) collective-permute-start(bf16[64,2048]{1,0:T(8,128)(2,1)S(1)} %add_convert_fusion.20), channel_id=1, source_target_pairs={{0,4},{1,5},{2,6},{3,7},{12,8},{13,9},{14,10},{15,11},{16,20},{17,... | collective-permute-start | bytes 786440 | tf_op jit(solution)/shard_map/ppermute | solution.py:26
  76.1 9.3 %collective-permute-start.16 = (bf16[64,2048]{1,0:T(8,128)(2,1)S(1)}, bf16[64,2048]{1,0:T(8,128)(2,1)S(1)}, u32[]{:S(2)}, u32[]{:S(2)}) collective-permute-start(bf16[64,2048]{1,0:T(8,128)(2,1)S(1)} %slice.246), channel_id=1, source_target_pairs={{0,2},{1,3},{2,0},{3,1},{4,6},{5,7},{6,4},{7,5},{8,10},{9,11},{10,... | collective-permute-start | bytes 786440 | tf_op jit(solution)/shard_map/ppermute | solution.py:29
  77.9 12.1 %collective-permute-start.21 = (bf16[64,2048]{1,0:T(8,128)(2,1)S(1)}, bf16[64,2048]{1,0:T(8,128)(2,1)S(1)}, u32[]{:S(2)}, u32[]{:S(2)}) collective-permute-start(bf16[64,2048]{1,0:T(8,128)(2,1)S(1)} %add_convert_fusion.20), channel_id=1, source_target_pairs={{4,8},{5,9},{6,10},{7,11},{8,4},{9,5},{10,6},{11,7},{20,24},{21,25... | collective-permute-start | bytes 786440 | tf_op jit(solution)/shard_map/ppermute | solution.py:26
  78.6 13.0 %collective-permute-start.20 = (bf16[64,2048]{1,0:T(8,128)(2,1)S(1)}, bf16[64,2048]{1,0:T(8,128)(2,1)S(1)}, u32[]{:S(2)}, u32[]{:S(2)}) collective-permute-start(bf16[64,2048]{1,0:T(8,128)(2,1)S(1)} %slice.250), channel_id=1, source_target_pairs={{0,2},{1,3},{2,0},{3,1},{4,6},{5,7},{6,4},{7,5},{8,10},{9,11},{10,... | collective-permute-start | bytes 786440 | tf_op jit(solution)/shard_map/ppermute | solution.py:29
  86.2 11.8 %collective-permute-start.25 = (bf16[64,2048]{1,0:T(8,128)(2,1)S(1)}, bf16[64,2048]{1,0:T(8,128)(2,1)S(1)}, u32[]{:S(2)}, u32[]{:S(2)}) collective-permute-start(bf16[64,2048]{1,0:T(8,128)(2,1)S(1)} %get-tuple-element.58), channel_id=1, source_target_pairs={{0,12},{1,13},{2,14},{3,15},{12,0},{13,1},{14,2},{15,3},{16,28},{1... | collective-permute-start | bytes 786440 | tf_op jit(solution)/shard_map/ppermute | solution.py:26
  90.0 8.0 %collective-permute-start.17 = (bf16[64,2048]{1,0:T(8,128)(2,1)S(1)}, bf16[64,2048]{1,0:T(8,128)(2,1)S(1)}, u32[]{:S(2)}, u32[]{:S(2)}) collective-permute-start(bf16[64,2048]{1,0:T(8,128)(2,1)S(1)} %slice.235), channel_id=1, source_target_pairs={{0,2},{1,3},{2,0},{3,1},{4,6},{5,7},{6,4},{7,5},{8,10},{9,11},{10,... | collective-permute-start | bytes 786440 | tf_op jit(solution)/shard_map/ppermute | solution.py:29
  91.7 9.1 %collective-permute-start.22 = (bf16[64,2048]{1,0:T(8,128)(2,1)S(1)}, bf16[64,2048]{1,0:T(8,128)(2,1)S(1)}, u32[]{:S(2)}, u32[]{:S(2)}) collective-permute-start(bf16[64,2048]{1,0:T(8,128)(2,1)S(1)} %add_convert_fusion.19), channel_id=1, source_target_pairs={{0,4},{1,5},{2,6},{3,7},{4,0},{5,1},{6,2},{7,3},{8,12},{9,13},{10,... | collective-permute-start | bytes 786440 | tf_op jit(solution)/shard_map/ppermute | solution.py:26
  101.5 8.9 %collective-permute-start.30 = (bf16[64,1024]{1,0:T(8,128)(2,1)S(1)}, bf16[64,1024]{1,0:T(8,128)(2,1)S(1)}, u32[]{:S(2)}, u32[]{:S(2)}) collective-permute-start(bf16[64,1024]{1,0:T(8,128)(2,1)S(1)} %get-tuple-element.64), channel_id=1, source_target_pairs={{0,8},{1,9},{2,10},{3,11},{4,12},{5,13},{6,14},{7,15},{8,0},{9,1},... | collective-permute-start | bytes 393224 | tf_op jit(solution)/shard_map/ppermute | solution.py:26
  102.8 17.9 %collective-permute-start.29 = (bf16[64,1024]{1,0:T(8,128)(2,1)S(1)}, bf16[64,1024]{1,0:T(8,128)(2,1)S(1)}, u32[]{:S(2)}, u32[]{:S(2)}) collective-permute-start(bf16[64,1024]{1,0:T(8,128)(2,1)S(1)} %get-tuple-element.63), channel_id=1, source_target_pairs={{0,4},{1,5},{2,6},{3,7},{4,0},{5,1},{6,2},{7,3},{8,12},{9,13},{10,... | collective-permute-start | bytes 393224 | tf_op jit(solution)/shard_map/ppermute | solution.py:26
  104.5 9.5 %collective-permute-start.33 = (bf16[64,1024]{1,0:T(8,128)(2,1)S(1)}, bf16[64,1024]{1,0:T(8,128)(2,1)S(1)}, u32[]{:S(2)}, u32[]{:S(2)}) collective-permute-start(bf16[64,1024]{1,0:T(8,128)(2,1)S(1)} %get-tuple-element.65), channel_id=1, source_target_pairs={{0,12},{1,13},{2,14},{3,15},{4,8},{5,9},{6,10},{7,11},{8,4},{9,5},... | collective-permute-start | bytes 393224 | tf_op jit(solution)/shard_map/ppermute | solution.py:26
  111.3 8.7 %collective-permute-start.34 = (bf16[64,2048]{1,0:T(8,128)(2,1)S(1)}, bf16[64,2048]{1,0:T(8,128)(2,1)S(1)}, u32[]{:S(2)}, u32[]{:S(2)}) collective-permute-start(bf16[64,2048]{1,0:T(8,128)(2,1)S(1)} %convolution_convert_fusion.1), channel_id=1, source_target_pairs={{0,4},{1,5},{2,6},{3,7},{12,8},{13,9},{14,10},{15,11},{16,20},{17,... | collective-permute-start | bytes 786440 | tf_op jit(solution)/shard_map/ppermute | solution.py:26
  114.9 14.5 %collective-permute-start.36 = (bf16[64,2048]{1,0:T(8,128)(2,1)S(1)}, bf16[64,2048]{1,0:T(8,128)(2,1)S(1)}, u32[]{:S(2)}, u32[]{:S(2)}) collective-permute-start(bf16[64,2048]{1,0:T(8,128)(2,1)S(1)} %convolution_convert_fusion), channel_id=1, source_target_pairs={{0,12},{1,13},{2,14},{3,15},{12,0},{13,1},{14,2},{15,3},{16,28},{1... | collective-permute-start | bytes 786440 | tf_op jit(solution)/shard_map/ppermute | solution.py:26
  120.0 9.4 %collective-permute-start.35 = (bf16[64,2048]{1,0:T(8,128)(2,1)S(1)}, bf16[64,2048]{1,0:T(8,128)(2,1)S(1)}, u32[]{:S(2)}, u32[]{:S(2)}) collective-permute-start(bf16[64,2048]{1,0:T(8,128)(2,1)S(1)} %add_convert_fusion.15), channel_id=1, source_target_pairs={{4,8},{5,9},{6,10},{7,11},{8,4},{9,5},{10,6},{11,7},{20,24},{21,25... | collective-permute-start | bytes 786440 | tf_op jit(solution)/shard_map/ppermute | solution.py:26
  121.6 13.9 %collective-permute-start.32 = (bf16[64,2048]{1,0:T(8,128)(2,1)S(1)}, bf16[64,2048]{1,0:T(8,128)(2,1)S(1)}, u32[]{:S(2)}, u32[]{:S(2)}) collective-permute-start(bf16[64,2048]{1,0:T(8,128)(2,1)S(1)} %fusion.26), channel_id=1, source_target_pairs={{0,4},{1,5},{2,6},{3,7},{4,0},{5,1},{6,2},{7,3},{8,12},{9,13},{10,... | collective-permute-start | bytes 786440 | tf_op jit(solution)/shard_map/ppermute | solution.py:26
  138.7 8.6 %collective-permute-start.37 = (bf16[64,2048]{1,0:T(8,128)(2,1)S(1)}, bf16[64,2048]{1,0:T(8,128)(2,1)S(1)}, u32[]{:S(2)}, u32[]{:S(2)}) collective-permute-start(bf16[64,2048]{1,0:T(8,128)(2,1)S(1)} %fusion.49), channel_id=1, source_target_pairs={{0,2},{1,3},{2,0},{3,1},{4,6},{5,7},{6,4},{7,5},{8,10},{9,11},{10,... | collective-permute-start | bytes 786440 | tf_op jit(solution)/shard_map/ppermute | solution.py:29
  146.0 9.6 %collective-permute-start.43 = (bf16[64,2048]{1,0:T(8,128)(2,1)S(1)}, bf16[64,2048]{1,0:T(8,128)(2,1)S(1)}, u32[]{:S(2)}, u32[]{:S(2)}) collective-permute-start(bf16[64,2048]{1,0:T(8,128)(2,1)S(1)} %collective-permute-done.40), channel_id=1, source_target_pairs={{4,0},{5,1},{6,2},{7,3},{8,12},{9,13},{10,14},{11,15},{20,16},{21,... | collective-permute-start | bytes 786440 | tf_op jit(solution)/shard_map/ppermute | solution.py:26
  147.4 9.8 %collective-permute-start.38 = (bf16[128,2048]{1,0:T(8,128)(2,1)S(1)}, bf16[128,2048]{1,0:T(8,128)(2,1)S(1)}, u32[]{:S(2)}, u32[]{:S(2)}) collective-permute-start(bf16[128,2048]{1,0:T(8,128)(2,1)S(1)} %pad_maximum_fusion.10), channel_id=1, source_target_pairs={{0,1},{1,0},{2,3},{3,2},{4,5},{5,4},{6,7},{7,6},{8,9},{9,8},{10,11... | collective-permute-start | bytes 1572872 | tf_op jit(solution)/shard_map/ppermute | solution.py:29
  155.7 8.4 %collective-permute-start.44 = (bf16[64,2048]{1,0:T(8,128)(2,1)S(1)}, bf16[64,2048]{1,0:T(8,128)(2,1)S(1)}, u32[]{:S(2)}, u32[]{:S(2)}) collective-permute-start(bf16[64,2048]{1,0:T(8,128)(2,1)S(1)} %broadcast_select_fusion.3), channel_id=1, source_target_pairs={{4,0},{5,1},{6,2},{7,3},{8,12},{9,13},{10,14},{11,15},{20,16},{21,... | collective-permute-start | bytes 786440 | tf_op jit(solution)/shard_map/ppermute | solution.py:26
  157.1 11.0 %collective-permute-start.46 = (bf16[128,2048]{1,0:T(8,128)(2,1)S(1)}, bf16[128,2048]{1,0:T(8,128)(2,1)S(1)}, u32[]{:S(2)}, u32[]{:S(2)}) collective-permute-start(bf16[128,2048]{1,0:T(8,128)(2,1)S(1)} %pad_maximum_fusion.11), channel_id=1, source_target_pairs={{0,1},{1,0},{2,3},{3,2},{4,5},{5,4},{6,7},{7,6},{8,9},{9,8},{10,11... | collective-permute-start | bytes 1572872 | tf_op jit(solution)/shard_map/ppermute | solution.py:29
  159.2 8.8 %collective-permute-start.48 = (bf16[64,2048]{1,0:T(8,128)(2,1)S(1)}, bf16[64,2048]{1,0:T(8,128)(2,1)S(1)}, u32[]{:S(2)}, u32[]{:S(2)}) collective-permute-start(bf16[64,2048]{1,0:T(8,128)(2,1)S(1)} %broadcast_select_fusion.3), channel_id=1, source_target_pairs={{0,2},{1,3},{2,0},{3,1},{4,6},{5,7},{6,4},{7,5},{8,10},{9,11},{10,... | collective-permute-start | bytes 786440 | tf_op jit(solution)/shard_map/ppermute | solution.py:29
  170.3 8.8 %collective-permute-start.47 = (bf16[64,2048]{1,0:T(8,128)(2,1)S(1)}, bf16[64,2048]{1,0:T(8,128)(2,1)S(1)}, u32[]{:S(2)}, u32[]{:S(2)}) collective-permute-start(bf16[64,2048]{1,0:T(8,128)(2,1)S(1)} %broadcast_select_fusion.2), channel_id=1, source_target_pairs={{0,2},{1,3},{2,0},{3,1},{4,6},{5,7},{6,4},{7,5},{8,10},{9,11},{10,... | collective-permute-start | bytes 786440 | tf_op jit(solution)/shard_map/ppermute | solution.py:29
  179.8 15.4 %collective-permute-start.55 = (bf16[128,2048]{1,0:T(8,128)(2,1)S(1)}, bf16[128,2048]{1,0:T(8,128)(2,1)S(1)}, u32[]{:S(2)}, u32[]{:S(2)}) collective-permute-start(bf16[128,2048]{1,0:T(8,128)(2,1)S(1)} %slice.272), channel_id=1, source_target_pairs={{0,1},{1,0},{2,3},{3,2},{4,5},{5,4},{6,7},{7,6},{8,9},{9,8},{10,11... | collective-permute-start | bytes 1572872 | tf_op jit(solution)/shard_map/ppermute | solution.py:29
  180.1 8.8 %collective-permute-start.56 = (bf16[64,2048]{1,0:T(8,128)(2,1)S(1)}, bf16[64,2048]{1,0:T(8,128)(2,1)S(1)}, u32[]{:S(2)}, u32[]{:S(2)}) collective-permute-start(bf16[64,2048]{1,0:T(8,128)(2,1)S(1)} %slice.275), channel_id=1, source_target_pairs={{0,2},{1,3},{2,0},{3,1},{4,6},{5,7},{6,4},{7,5},{8,10},{9,11},{10,... | collective-permute-start | bytes 786440 | tf_op jit(solution)/shard_map/ppermute | solution.py:29
  183.8 9.7 %collective-permute-start.52 = (bf16[128,2048]{1,0:T(8,128)(2,1)S(1)}, bf16[128,2048]{1,0:T(8,128)(2,1)S(1)}, u32[]{:S(2)}, u32[]{:S(2)}) collective-permute-start(bf16[128,2048]{1,0:T(8,128)(2,1)S(1)} %slice.269), channel_id=1, source_target_pairs={{0,1},{1,0},{2,3},{3,2},{4,5},{5,4},{6,7},{7,6},{8,9},{9,8},{10,11... | collective-permute-start | bytes 1572872 | tf_op jit(solution)/shard_map/ppermute | solution.py:29
  188.9 14.1 %collective-permute-start.60 = (bf16[64,2048]{1,0:T(8,128)(2,1)S(1)}, bf16[64,2048]{1,0:T(8,128)(2,1)S(1)}, u32[]{:S(2)}, u32[]{:S(2)}) collective-permute-start(bf16[64,2048]{1,0:T(8,128)(2,1)S(1)} %add_convert_fusion.12), channel_id=1, source_target_pairs={{0,4},{1,5},{2,6},{3,7},{12,8},{13,9},{14,10},{15,11},{16,20},{17,... | collective-permute-start | bytes 786440 | tf_op jit(solution)/shard_map/ppermute | solution.py:26
  193.6 9.3 %collective-permute-start.53 = (bf16[64,2048]{1,0:T(8,128)(2,1)S(1)}, bf16[64,2048]{1,0:T(8,128)(2,1)S(1)}, u32[]{:S(2)}, u32[]{:S(2)}) collective-permute-start(bf16[64,2048]{1,0:T(8,128)(2,1)S(1)} %slice.270), channel_id=1, source_target_pairs={{0,2},{1,3},{2,0},{3,1},{4,6},{5,7},{6,4},{7,5},{8,10},{9,11},{10,... | collective-permute-start | bytes 786440 | tf_op jit(solution)/shard_map/ppermute | solution.py:29
  195.4 13.6 %collective-permute-start.58 = (bf16[64,2048]{1,0:T(8,128)(2,1)S(1)}, bf16[64,2048]{1,0:T(8,128)(2,1)S(1)}, u32[]{:S(2)}, u32[]{:S(2)}) collective-permute-start(bf16[64,2048]{1,0:T(8,128)(2,1)S(1)} %add_convert_fusion.12), channel_id=1, source_target_pairs={{4,8},{5,9},{6,10},{7,11},{8,4},{9,5},{10,6},{11,7},{20,24},{21,25... | collective-permute-start | bytes 786440 | tf_op jit(solution)/shard_map/ppermute | solution.py:26
  196.2 12.7 %collective-permute-start.57 = (bf16[64,2048]{1,0:T(8,128)(2,1)S(1)}, bf16[64,2048]{1,0:T(8,128)(2,1)S(1)}, u32[]{:S(2)}, u32[]{:S(2)}) collective-permute-start(bf16[64,2048]{1,0:T(8,128)(2,1)S(1)} %slice.274), channel_id=1, source_target_pairs={{0,2},{1,3},{2,0},{3,1},{4,6},{5,7},{6,4},{7,5},{8,10},{9,11},{10,... | collective-permute-start | bytes 786440 | tf_op jit(solution)/shard_map/ppermute | solution.py:29
  203.8 11.8 %collective-permute-start.62 = (bf16[64,2048]{1,0:T(8,128)(2,1)S(1)}, bf16[64,2048]{1,0:T(8,128)(2,1)S(1)}, u32[]{:S(2)}, u32[]{:S(2)}) collective-permute-start(bf16[64,2048]{1,0:T(8,128)(2,1)S(1)} %get-tuple-element.54), channel_id=1, source_target_pairs={{0,12},{1,13},{2,14},{3,15},{12,0},{13,1},{14,2},{15,3},{16,28},{1... | collective-permute-start | bytes 786440 | tf_op jit(solution)/shard_map/ppermute | solution.py:26
  209.1 9.2 %collective-permute-start.59 = (bf16[64,2048]{1,0:T(8,128)(2,1)S(1)}, bf16[64,2048]{1,0:T(8,128)(2,1)S(1)}, u32[]{:S(2)}, u32[]{:S(2)}) collective-permute-start(bf16[64,2048]{1,0:T(8,128)(2,1)S(1)} %add_convert_fusion.11), channel_id=1, source_target_pairs={{0,4},{1,5},{2,6},{3,7},{4,0},{5,1},{6,2},{7,3},{8,12},{9,13},{10,... | collective-permute-start | bytes 786440 | tf_op jit(solution)/shard_map/ppermute | solution.py:26
  (25 other events, 231.1 us)

commit v5 on v4

--- a/solution.py
+++ b/solution.py
@@ -5,7 +5,7 @@
 
 EPSILON = 1e-06
 PLANES = 4
-ORDER = (0, 1, 2, 3)
+PARTS = 2
 
 
 class Ring:
@@ -28,6 +28,9 @@
     def across(self, values, bit):
         return lax.ppermute(values, "inner", [(d, d ^ bit) for d in range(self.size)])
 
+    def same_core(self):
+        return [list(range(c, self.size, 2)) for c in range(2)]
+
     def high(self, bit):
         return (self.me // bit) % 2 == 1
 
@@ -38,41 +41,6 @@
 
 def add(*terms):
     return sum(t.astype(jnp.float32) for t in terms).astype(jnp.bfloat16)
-
-
-def gather_rows(ring, rows, work):
-    def fill(column, ties):
-        for i, bit in enumerate(ring.bits):
-            if i == 1:
-                column = after(column, *ties)
-            column = jnp.concatenate([column, ring.across(column, bit)], axis=0)
-        return column
-
-    done = {}
-    slots = {0: rows}
-    chunk0 = fill(rows, [])
-    slots[1] = ring.send(rows, [(0, 1), (1, 0), (2, 3), (3, 2)])
-    middle = ring.send(rows, [(1, 2), (2, 1)])
-    chunk1 = fill(slots[1], [])
-    near = ring.send(middle, [(1, 0), (2, 3)])
-    far = ring.send(slots[1], [(1, 2), (2, 1)])
-    slots[2] = jnp.where(ring.inside, far, near)
-    done[0] = work(0, chunk0)
-    chunk2 = fill(after(slots[2], done[0]), [])
-    outer = ring.send(slots[2], [(1, 0), (2, 3)])
-    slots[3] = jnp.where(ring.inside, middle, outer)
-    done[1] = work(1, after(chunk1, done[0]))
-    column3 = after(slots[3], done[1])
-    done[2] = work(2, after(chunk2, done[1]))
-    chunk3 = fill(column3, [done[2]])
-    return done, chunk3
-
-
-def within_plane(ring, chunk):
-    for bit in reversed(ring.bits[1:]):
-        rows = chunk.shape[0] // 2
-        chunk = add(chunk[:rows], ring.across(chunk[rows:], bit))
-    return chunk
 
 
 def plane_sums(ring, part):
@@ -119,17 +87,20 @@
 
 
 def routed(ring, rows, work):
-    done, chunk3 = gather_rows(ring, rows, work)
-    halves = {2: within_plane(ring, done[2])}
-    done[3] = work(3, after(chunk3, halves[2]))
-    for slot in (3, 1, 0):
-        halves[slot] = within_plane(ring, done[slot])
-    own = rows.shape[0]
-    crossed = {}
-    for slot, earlier in ((2, []), (3, []), (1, [2]), (0, [3])):
-        away = after(halves[slot][own:], *[crossed[e] for e in earlier], halves[3] if earlier else halves[2])
-        crossed[slot] = ring.across(away, ring.bits[0])
-    return plane_sums(ring, lambda slot: add(halves[slot][:own], crossed[slot]))
+    count = rows.shape[0] // PARTS
+    sums = []
+    for part in range(PARTS):
+        mine = lax.all_gather(
+            rows[part * count : (part + 1) * count], "inner", axis_index_groups=ring.same_core(), axis=0, tiled=True
+        )
+        every = jnp.concatenate([mine, ring.across(mine, 1)], axis=0)
+        out = work(part, every)
+        half = out.shape[0] // 2
+        pair = add(out[:half], ring.across(out[half:], 1))
+        sums.append(
+            lax.psum_scatter(pair, "inner", axis_index_groups=ring.same_core(), scatter_dimension=0, tiled=True)
+        )
+    return jnp.concatenate(sums, axis=0).astype(jnp.float32)
 
 
 def plane_weight(ring, weight, groups):
@@ -185,13 +156,13 @@
     weight = plane_weight(ring, merge_weight, lax.axis_size("groups"))
     second_columns = {}
 
-    def first_work(slot, chunk):
-        second_columns[slot] = gate_column(ring, chunk[:, width:], 1)
+    def first_work(part, chunk):
+        second_columns[part] = gate_column(ring, chunk[:, width:], 1)
         gates = gate_column(ring, chunk[:, width:], 0)
         return expert(chunk[:, :width], gates, first_gate_up[0], first_down[0])
 
-    def second_work(slot, chunk):
-        return expert(chunk, second_columns[slot], second_gate_up[0], second_down[0])
+    def second_work(part, chunk):
+        return expert(chunk, second_columns[part], second_gate_up[0], second_down[0])
 
     first = routed(ring, jnp.concatenate([hidden_rows, halves], axis=1), first_work)
     after_first = (hidden_rows.astype(jnp.float32) + first).astype(jnp.bfloat16)

time: 220 us -> 493 us (2.24)
  waiting for transfers between devices: 96.3 us -> 397 us
  starting transfers between devices: 84.7 us -> 20.4 us
  between operations: 1.21 us -> 14 us
  other arithmetic: 11.3 us -> 23.4 us
  local copies, waits for them, and re-layouts: 3.87 us -> 9.49 us
  matrix products: 21.9 us -> 27.4 us
    reduce_scatter x0 -> x4, waiting for transfers between devices: none -> 201 us  [routed(): lax.psum_scatter(pair, 'inner', axis_index_groups=ring.same_core(), scatt...]
    all_gather x0 -> x4, waiting for transfers between devices: none -> 156 us  [routed(): lax.all_gather(rows[part * count:(part + 1) * count], 'inner', axis_index...]
    ppermute x28 -> x8, starting transfers between devices: 55.2 us -> 17 us  [send(): return lax.ppermute(values, 'inner', perm)]
    ppermute x28 -> x8, waiting for transfers between devices: 40.7 us -> 6.06 us  [send(): return lax.ppermute(values, 'inner', perm)]
    ppermute x34 -> x10, waiting for transfers between devices: 55.6 us -> 24.3 us  [across(): lax.ppermute(values, 'inner', [(d, d ^ bit) for d in range(self.size)])]
    ppermute x34 -> x10, starting transfers between devices: 28 us -> 1.64 us  [across(): lax.ppermute(values, 'inner', [(d, d ^ bit) for d in range(self.size)])]
    ppermute x1, waiting for transfers between devices: 0.01 us -> 9.37 us  [plane_weight(): there = lax.ppermute(here, 'groups', [(g, g ^ 1) for g in range(groups)])]
    convert_element_type x15 -> x5, other arithmetic: 1.62 us -> 6.8 us  [add(): return sum((t.astype(jnp.float32) for t in terms)).astype(jnp.bfloat16)]
  transfers between devices with their start and end apart: 63 -> 27, of which waited for: 24 -> 17; matrix products, arithmetic and copies ran while one was open for 15% -> 10% of each run, Pallas kernels for 0% -> 0%
where the time goes in v5:
time: 493 us; the launch traced here: 492 us
  waiting for transfers between devices  397 us (81%)
  matrix products  27.4 us (6%)
  other arithmetic  23.4 us (5%)
  starting transfers between devices  20.4 us (4%)
  between operations  14 us (3%)
  local copies, waits for them, and re-layouts  9.49 us (2%)
    reduce_scatter x4, waiting for transfers between devices, routed(): lax.psum_scatter(pair, 'inner', axis_index_groups=ring.same_core(), scatt...  201 us
    all_gather x4, waiting for transfers between devices, routed(): lax.all_gather(rows[part * count:(part + 1) * count], 'inner', axis_index...  156 us
    ppermute x10, waiting for transfers between devices, across(): lax.ppermute(values, 'inner', [(d, d ^ bit) for d in range(self.size)])  24.3 us
    dot_general x4, matrix products, expert(): projected = jnp.dot(rows, gate_up, preferred_element_type=jnp.float32)  17.5 us
    ppermute x8, starting transfers between devices, send(): return lax.ppermute(values, 'inner', perm)  17 us
  transfers between devices with their start and end apart: 27, of which 17 were waited for; matrix products, arithmetic and copies ran while one was open for 10% of the time, Pallas kernels for 0%

profile of v5, /device:TPU:0, one launch (start us, length us, event | category | flops | bytes accessed | tf_op | source)
XLA Modules:
  0.0 492.1 jit_solution(12977864590930702758)
XLA Ops:
  8.6 1.1 concatenate.80
  11.2 42.7 %all-gather.5.cloned.1.call-done = bf16[256,2176]{1,0:T(8,128)(2,1)} async-done(((bf16[32,2176]{1,0:T(8,128)(2,1)}), bf16[256,2176]{1,0:T(8,128)(2,1)}) %all-gather.5.cloned.1.call-update) | async-done | bytes 1114128 | tf_op jit(solution)/shard_map/all_gather | solution.py:93
  53.9 41.7 %all-gather.7.cloned.1.call-done = bf16[256,2176]{1,0:T(8,128)(2,1)} async-done(((bf16[32,2176]{1,0:T(8,128)(2,1)}), bf16[256,2176]{1,0:T(8,128)(2,1)}) %all-gather.7.cloned.1.call-update) | async-done | bytes 1114128 | tf_op jit(solution)/shard_map/all_gather | solution.py:93
  95.5 1.4 constant_dynamic-update-slice_fusion.1
  97.4 1.9 copy-done.12
  99.3 2.3 fusion.6
  102.1 1.3 multiply_convert_fusion.3
  103.8 2.4 collective-permute-done.1
  106.2 1.4 add_convert_fusion.3
  107.7 5.2 %fusion.4 = f32[512,1024]{1,0:T(8,128)S(1)} fusion(bf16[1,2048,1024]{2,1,0:T(8,128)(2,1)} %param.17, bf16[512,2176]{1,0:T(8,128)(2,1)} %copy-done.9), kind=kOutput, calls=%fused_computation.5 | convolution fusion | flops 2147483648 | bytes 8388608 | tf_op jit(solution)/shard_map/dot_general | solution.py:83
  112.8 2.6 multiply_convert_fusion.2
  115.5 1.4 slice.111
  117.8 15.0 %collective-permute-done.4 = bf16[128,2048]{1,0:T(8,128)(2,1)} collective-permute-done((bf16[128,2048]{1,0:T(8,128)(2,1)S(1)}, bf16[128,2048]{1,0:T(8,128)(2,1)}, u32[]{:S(2)}, u32[]{:S(2)}) %collective-permute-start.4) | collective-permute-done | bytes 524320 | tf_op jit(solution)/shard_map/ppermute | solution.py:29
  132.9 1.5 collective-permute-start.5
  134.4 2.6 add_convert_fusion.2
  137.1 9.4 %collective-permute-done.5 = bf16[128,2048]{1,0:T(8,128)(2,1)} collective-permute-done((bf16[128,2048]{1,0:T(8,128)(2,1)}, bf16[128,2048]{1,0:T(8,128)(2,1)}, u32[]{:S(2)}, u32[]{:S(2)}) %collective-permute-start.5) | collective-permute-done | bytes 524320 | tf_op jit(solution)/shard_map/ppermute | solution.py:115
  146.4 1.9 maximum_select_fusion.3
  148.4 1.7 maximum_select_fusion.1
  151.1 2.0 maximum_select_fusion.2
  153.0 17.0 %reduce-scatter.5.cloned.1.call-done = bf16[32,2048]{1,0:T(8,128)(2,1)} async-done(((bf16[256,2048]{1,0:T(8,128)(2,1)}), bf16[32,2048]{1,0:T(8,128)(2,1)}) %reduce-scatter.5.cloned.1.call-update) | async-done | bytes 131088 | tf_op jit(solution)/shard_map/reduce_scatter | solution.py:101
  170.0 66.1 %reduce-scatter.7.cloned.1.call-done = bf16[32,2048]{1,0:T(8,128)(2,1)} async-done(((bf16[256,2048]{1,0:T(8,128)(2,1)}), bf16[32,2048]{1,0:T(8,128)(2,1)}) %reduce-scatter.7.cloned.1.call-update) | async-done | bytes 131088 | tf_op jit(solution)/shard_map/reduce_scatter | solution.py:101
  236.1 1.2 fusion.30
  237.3 1.1 fusion.32
  238.4 1.2 fusion.50
  239.5 1.4 collective-permute-start.8
  241.0 2.8 maximum_select_fusion
  243.8 1.3 collective-permute-start.7
  245.1 1.8 collective-permute-start.11
  249.1 4.2 collective-permute-start.12
  254.2 5.0 %collective-permute-start.14 = (bf16[64,2048]{1,0:T(8,128)(2,1)S(1)}, bf16[64,2048]{1,0:T(8,128)(2,1)S(1)}, u32[]{:S(2)}, u32[]{:S(2)}) collective-permute-start(bf16[64,2048]{1,0:T(8,128)(2,1)S(1)} %convolution_convert_fusion), channel_id=1, source_target_pairs={{0,12},{1,13},{2,14},{3,15},{12,0},{13,1},{14,2},{15,3},{16,28},{1... | collective-permute-start | bytes 786440 | tf_op jit(solution)/shard_map/ppermute | solution.py:26
  260.1 1.9 collective-permute-start.10
  263.7 4.4 collective-permute-done.14
  268.2 0.9 collective-permute-done.10
  270.1 40.8 %all-gather.9.cloned.1.call-done = bf16[256,2048]{1,0:T(8,128)(2,1)} async-done(((bf16[32,2048]{1,0:T(8,128)(2,1)}), bf16[256,2048]{1,0:T(8,128)(2,1)}) %all-gather.9.cloned.1.call-update) | async-done | bytes 1048592 | tf_op jit(solution)/shard_map/all_gather | solution.py:93
  311.0 2.8 collective-permute-done.15
  313.8 4.8 fusion.2
  318.7 1.3 multiply_convert_fusion.1
  320.0 1.0 slice.116
  321.1 30.7 %all-gather.11.cloned.1.call-done = bf16[256,2048]{1,0:T(8,128)(2,1)} async-done(((bf16[32,2048]{1,0:T(8,128)(2,1)}), bf16[256,2048]{1,0:T(8,128)(2,1)}) %all-gather.11.cloned.1.call-update) | async-done | bytes 1048592 | tf_op jit(solution)/shard_map/all_gather | solution.py:93
  351.9 1.3 add_convert_fusion.1
  353.3 1.6 collective-permute-done.17
  354.8 5.2 %fusion = f32[512,1024]{1,0:T(8,128)S(1)} fusion(bf16[1,2048,1024]{2,1,0:T(8,128)(2,1)} %param.21, bf16[256,2048]{1,0:T(8,128)(2,1)} %collective-permute-done.17, bf16[256,2048]{1,0:T(8,128)(2,1)} %all-gather.11.cloned.1.call-done), kind=kOutput, calls=%fused_computation.1 | convolution fusion | flops 2151677952 | bytes 8388608 | tf_op jit(solution)/shard_map/dot_general | solution.py:83
  360.0 1.3 multiply_convert_fusion
  361.7 2.5 collective-permute-done.18
  364.2 1.4 add_convert_fusion
  365.6 51.8 %reduce-scatter.9.cloned.1.call-done = bf16[32,2048]{1,0:T(8,128)(2,1)} async-done(((bf16[256,2048]{1,0:T(8,128)(2,1)}), bf16[32,2048]{1,0:T(8,128)(2,1)}) %reduce-scatter.9.cloned.1.call-update) | async-done | bytes 131088 | tf_op jit(solution)/shard_map/reduce_scatter | solution.py:101
  417.4 66.2 %reduce-scatter.11.cloned.1.call-done = bf16[32,2048]{1,0:T(8,128)(2,1)} async-done(((bf16[256,2048]{1,0:T(8,128)(2,1)}), bf16[32,2048]{1,0:T(8,128)(2,1)}) %reduce-scatter.11.cloned.1.call-update) | async-done | bytes 131088 | tf_op jit(solution)/shard_map/reduce_scatter | solution.py:101
  483.5 1.7 add_convert_fusion.4
  (97 shorter events, 14.3 us)
Async XLA Ops:
  6.5 95.5 %copy-start = (bf16[1,512,2048]{2,1,0:T(8,128)(2,1)S(1)}, bf16[1,512,2048]{2,1,0:T(8,128)(2,1)}, u32[]{:S(2)}) copy-start(bf16[1,512,2048]{2,1,0:T(8,128)(2,1)} %param.18) | copy-start | bytes 6291460
  6.5 47.3 %all-gather.5.cloned.1.call-start = ((), (), s32[]{:S(2)}) async-start(), calls=%async_computation.4 | async-start | bytes 1253376 | tf_op jit(solution)/shard_map/all_gather | solution.py:93
  10.4 85.1 %all-gather.7.cloned.1.call-start = ((), (), s32[]{:S(2)}) async-start(), calls=%async_computation.6 | async-start | bytes 1253376 | tf_op jit(solution)/shard_map/all_gather | solution.py:93
  11.1 158.8 %reduce-scatter.5.cloned.1.call-start = ((), (), s32[]{:S(2)}) async-start(), calls=%async_computation.5 | async-start | bytes 1179648 | tf_op jit(solution)/shard_map/reduce_scatter | solution.py:101
  53.8 43.4 %collective-permute-start = (bf16[256,2176]{1,0:T(8,128)(2,1)}, bf16[256,2176]{1,0:T(8,128)(2,1)S(1)}, u32[]{:S(2)}, u32[]{:S(2)}) collective-permute-start(bf16[256,2176]{1,0:T(8,128)(2,1)} %all-gather.5.cloned.1.call-done), channel_id=1, source_target_pairs={{0,1},{1,0},{2,3},{3,2},{4,5},{5,4},{6,7},{7,6},{8,9},{9,8},{10,11... | collective-permute-start | bytes 3342344 | tf_op jit(solution)/shard_map/ppermute | solution.py:29
  95.5 1.6 copy-start.7
  95.5 6.1 %collective-permute-start.2 = (bf16[256,2176]{1,0:T(8,128)(2,1)}, bf16[256,2176]{1,0:T(8,128)(2,1)S(1)}, u32[]{:S(2)}, u32[]{:S(2)}) collective-permute-start(bf16[256,2176]{1,0:T(8,128)(2,1)} %all-gather.7.cloned.1.call-done), channel_id=1, source_target_pairs={{0,1},{1,0},{2,3},{3,2},{4,5},{5,4},{6,7},{7,6},{8,9},{9,8},{10,11... | collective-permute-start | bytes 3342344 | tf_op jit(solution)/shard_map/ppermute | solution.py:29
  97.1 2.2 copy-start.12
  101.8 1.6 copy-start.9
  103.5 2.7 collective-permute-start.1
  107.6 128.5 %reduce-scatter.7.cloned.1.call-start = ((), (), s32[]{:S(2)}) async-start(), calls=%async_computation.7 | async-start | bytes 1179648 | tf_op jit(solution)/shard_map/reduce_scatter | solution.py:101
  115.5 1.7 copy-start.2
  116.8 17.5 %collective-permute-start.3 = (bf16[256,2048]{1,0:T(8,128)(2,1)S(1)}, bf16[256,2048]{1,0:T(8,128)(2,1)S(1)}, u32[]{:S(2)}, u32[]{:S(2)}) collective-permute-start(bf16[256,2048]{1,0:T(8,128)(2,1)S(1)} %slice.111), channel_id=1, source_target_pairs={{0,1},{1,0},{2,3},{3,2},{4,5},{5,4},{6,7},{7,6},{8,9},{9,8},{10,11... | collective-permute-start | bytes 3145736 | tf_op jit(solution)/shard_map/ppermute | solution.py:29
  117.2 15.6 %collective-permute-start.4 = (bf16[128,2048]{1,0:T(8,128)(2,1)S(1)}, bf16[128,2048]{1,0:T(8,128)(2,1)}, u32[]{:S(2)}, u32[]{:S(2)}) collective-permute-start(bf16[128,2048]{1,0:T(8,128)(2,1)S(1)} %constant_dynamic-slice_fusion), channel_id=1, source_target_pairs={{0,2},{1,3},{2,0},{3,1},{4,6},{5,7},{6,4},{7,5},{8,10},{9,11},{10,... | collective-permute-start | bytes 1572872 | tf_op jit(solution)/shard_map/ppermute | solution.py:29
  132.9 13.6 %collective-permute-start.5 = (bf16[128,2048]{1,0:T(8,128)(2,1)}, bf16[128,2048]{1,0:T(8,128)(2,1)}, u32[]{:S(2)}, u32[]{:S(2)}) collective-permute-start(bf16[128,2048]{1,0:T(8,128)(2,1)} %collective-permute-done.4), channel_id=1, source_target_pairs={{0,16},{16,0},{1,17},{17,1},{2,18},{18,2},{3,19},{19,3},{4,20},{20... | collective-permute-start | bytes 1572872 | tf_op jit(solution)/shard_map/ppermute | solution.py:115
  137.0 173.9 %all-gather.9.cloned.1.call-start = ((), (), s32[]{:S(2)}) async-start(), calls=%async_computation.8 | async-start | bytes 1179648 | tf_op jit(solution)/shard_map/all_gather | solution.py:93
  148.4 1.7 copy-start.8
  148.4 1.8 copy-start.10
  150.1 90.9 %collective-permute-start.6 = (bf16[2,256,2048]{2,1,0:T(8,128)(2,1)}, bf16[2,256,2048]{2,1,0:T(8,128)(2,1)}, u32[]{:S(2)}, u32[]{:S(2)}) collective-permute-start(bf16[2,256,2048]{2,1,0:T(8,128)(2,1)} %maximum_select_fusion.1), channel_id=1, source_target_pairs={{0,1},{1,0},{2,3},{3,2},{4,5},{5,4},{6,7},{7,6},{8,9},{9,8},{10,11... | collective-permute-start | bytes 6291464 | tf_op jit(solution)/shard_map/ppermute | solution.py:29
  151.1 85.0 %copy-start.3 = (bf16[64,2048]{1,0:T(8,128)(2,1)S(1)}, bf16[64,2048]{1,0:T(8,128)(2,1)}, u32[]{:S(2)}) copy-start(bf16[64,2048]{1,0:T(8,128)(2,1)} %param.13) | copy-start | bytes 786436
  151.1 86.2 %copy-start.11 = (f32[2048]{0:T(1024)S(1)}, f32[2048]{0:T(1024)}, u32[]{:S(2)}) copy-start(f32[2048]{0:T(1024)} %param.23) | copy-start | bytes 24580
  239.5 8.1 %collective-permute-start.8 = (bf16[64,1024]{1,0:T(8,128)(2,1)S(1)}, bf16[64,1024]{1,0:T(8,128)(2,1)S(1)}, u32[]{:S(2)}, u32[]{:S(2)}) collective-permute-start(bf16[64,1024]{1,0:T(8,128)(2,1)S(1)} %get-tuple-element.16), channel_id=1, source_target_pairs={{0,8},{1,9},{2,10},{3,11},{4,12},{5,13},{6,14},{7,15},{8,0},{9,1},... | collective-permute-start | bytes 393224 | tf_op jit(solution)/shard_map/ppermute | solution.py:26
  243.8 15.4 %collective-permute-start.7 = (bf16[64,1024]{1,0:T(8,128)(2,1)S(1)}, bf16[64,1024]{1,0:T(8,128)(2,1)S(1)}, u32[]{:S(2)}, u32[]{:S(2)}) collective-permute-start(bf16[64,1024]{1,0:T(8,128)(2,1)S(1)} %get-tuple-element.15), channel_id=1, source_target_pairs={{0,4},{1,5},{2,6},{3,7},{4,0},{5,1},{6,2},{7,3},{8,12},{9,13},{10,... | collective-permute-start | bytes 393224 | tf_op jit(solution)/shard_map/ppermute | solution.py:26
  245.1 8.2 %collective-permute-start.11 = (bf16[64,1024]{1,0:T(8,128)(2,1)S(1)}, bf16[64,1024]{1,0:T(8,128)(2,1)S(1)}, u32[]{:S(2)}, u32[]{:S(2)}) collective-permute-start(bf16[64,1024]{1,0:T(8,128)(2,1)S(1)} %get-tuple-element.17), channel_id=1, source_target_pairs={{0,12},{1,13},{2,14},{3,15},{4,8},{5,9},{6,10},{7,11},{8,4},{9,5},... | collective-permute-start | bytes 393224 | tf_op jit(solution)/shard_map/ppermute | solution.py:26
  248.4 10.7 %collective-permute-start.9 = (bf16[64,2048]{1,0:T(8,128)(2,1)S(1)}, bf16[64,2048]{1,0:T(8,128)(2,1)S(1)}, u32[]{:S(2)}, u32[]{:S(2)}) collective-permute-start(bf16[64,2048]{1,0:T(8,128)(2,1)S(1)} %convolution_convert_fusion.1), channel_id=1, source_target_pairs={{4,8},{5,9},{6,10},{7,11},{8,4},{9,5},{10,6},{11,7},{20,24},{21,25... | collective-permute-start | bytes 786440 | tf_op jit(solution)/shard_map/ppermute | solution.py:26
  249.1 12.8 %collective-permute-start.12 = (bf16[64,2048]{1,0:T(8,128)(2,1)S(1)}, bf16[64,2048]{1,0:T(8,128)(2,1)S(1)}, u32[]{:S(2)}, u32[]{:S(2)}) collective-permute-start(bf16[64,2048]{1,0:T(8,128)(2,1)S(1)} %convolution_convert_fusion.1), channel_id=1, source_target_pairs={{0,4},{1,5},{2,6},{3,7},{12,8},{13,9},{14,10},{15,11},{16,20},{17,... | collective-permute-start | bytes 786440 | tf_op jit(solution)/shard_map/ppermute | solution.py:26
  254.2 8.7 %copy-start.4 = (bf16[64,2048]{1,0:T(8,128)(2,1)S(1)}, bf16[64,2048]{1,0:T(8,128)(2,1)}, u32[]{:S(2)}) copy-start(bf16[64,2048]{1,0:T(8,128)(2,1)} %fusion.29) | copy-start | bytes 786436
  254.2 14.0 %collective-permute-start.14 = (bf16[64,2048]{1,0:T(8,128)(2,1)S(1)}, bf16[64,2048]{1,0:T(8,128)(2,1)S(1)}, u32[]{:S(2)}, u32[]{:S(2)}) collective-permute-start(bf16[64,2048]{1,0:T(8,128)(2,1)S(1)} %convolution_convert_fusion), channel_id=1, source_target_pairs={{0,12},{1,13},{2,14},{3,15},{12,0},{13,1},{14,2},{15,3},{16,28},{1... | collective-permute-start | bytes 786440 | tf_op jit(solution)/shard_map/ppermute | solution.py:26
  260.1 9.0 %collective-permute-start.10 = (bf16[64,2048]{1,0:T(8,128)(2,1)S(1)}, bf16[64,2048]{1,0:T(8,128)(2,1)S(1)}, u32[]{:S(2)}, u32[]{:S(2)}) collective-permute-start(bf16[64,2048]{1,0:T(8,128)(2,1)S(1)} %fusion.10), channel_id=1, source_target_pairs={{0,4},{1,5},{2,6},{3,7},{4,0},{5,1},{6,2},{7,3},{8,12},{9,13},{10,... | collective-permute-start | bytes 786440 | tf_op jit(solution)/shard_map/ppermute | solution.py:26
  262.0 7.0 %copy-start.5 = (bf16[32,2048]{1,0:T(8,128)(2,1)S(1)}, bf16[32,2048]{1,0:T(8,128)(2,1)}, u32[]{:S(2)}) copy-start(bf16[32,2048]{1,0:T(8,128)(2,1)} %reduce-scatter.5.cloned.1.call-done) | copy-start | bytes 393220
  262.0 7.0 %copy-start.6 = (bf16[32,2048]{1,0:T(8,128)(2,1)S(1)}, bf16[32,2048]{1,0:T(8,128)(2,1)}, u32[]{:S(2)}) copy-start(bf16[32,2048]{1,0:T(8,128)(2,1)} %reduce-scatter.7.cloned.1.call-done) | copy-start | bytes 393220
  262.0 7.0 %collective-permute-start.13 = (bf16[64,2048]{1,0:T(8,128)(2,1)S(1)}, bf16[64,2048]{1,0:T(8,128)(2,1)S(1)}, u32[]{:S(2)}, u32[]{:S(2)}) collective-permute-start(bf16[64,2048]{1,0:T(8,128)(2,1)S(1)} %add_convert_fusion.5), channel_id=1, source_target_pairs={{4,8},{5,9},{6,10},{7,11},{8,4},{9,5},{10,6},{11,7},{20,24},{21,25... | collective-permute-start | bytes 786440 | tf_op jit(solution)/shard_map/ppermute | solution.py:26
  270.1 81.8 %all-gather.11.cloned.1.call-start = ((), (), s32[]{:S(2)}) async-start(), calls=%async_computation.10 | async-start | bytes 1179648 | tf_op jit(solution)/shard_map/all_gather | solution.py:93
  310.9 2.9 collective-permute-start.15
  311.0 106.4 %reduce-scatter.9.cloned.1.call-start = ((), (), s32[]{:S(2)}) async-start(), calls=%async_computation.9 | async-start | bytes 1179648 | tf_op jit(solution)/shard_map/reduce_scatter | solution.py:101
  311.0 7.6 %copy-start.13 = (bf16[1,512,2048]{2,1,0:T(8,128)(2,1)S(1)}, bf16[1,512,2048]{2,1,0:T(8,128)(2,1)}, u32[]{:S(2)}) copy-start(bf16[1,512,2048]{2,1,0:T(8,128)(2,1)} %param.22) | copy-start | bytes 6291460
  321.0 30.9 %collective-permute-start.16 = (bf16[256,2048]{1,0:T(8,128)(2,1)}, bf16[256,2048]{1,0:T(8,128)(2,1)S(1)}, u32[]{:S(2)}, u32[]{:S(2)}) collective-permute-start(bf16[256,2048]{1,0:T(8,128)(2,1)} %slice.116), channel_id=1, source_target_pairs={{0,1},{1,0},{2,3},{3,2},{4,5},{5,4},{6,7},{7,6},{8,9},{9,8},{10,11... | collective-permute-start | bytes 3145736 | tf_op jit(solution)/shard_map/ppermute | solution.py:29
  351.8 3.0 collective-permute-start.17
  353.2 6.8 %copy-start.14 = (bf16[1,512,2048]{2,1,0:T(8,128)(2,1)S(1)}, bf16[1,512,2048]{2,1,0:T(8,128)(2,1)}, u32[]{:S(2)}) copy-start(bf16[1,512,2048]{2,1,0:T(8,128)(2,1)} %param.22) | copy-start | bytes 6291460
  353.2 130.3 %reduce-scatter.11.cloned.1.call-start = ((), (), s32[]{:S(2)}) async-start(), calls=%async_computation.11 | async-start | bytes 1179648 | tf_op jit(solution)/shard_map/reduce_scatter | solution.py:101
  361.3 123.9 %copy-start.1 = (bf16[1,512,2048]{2,1,0:T(8,128)(2,1)S(1)}, bf16[1,512,2048]{2,1,0:T(8,128)(2,1)}, u32[]{:S(2)}) copy-start(bf16[1,512,2048]{2,1,0:T(8,128)(2,1)} %param.18) | copy-start | bytes 6291460
  361.5 2.7 collective-permute-start.18
Sparse Core Ops, SparseCore 0:
  10.5 43.2 all-gather.4
  56.0 39.4 all-gather.6
  107.7 62.1 reduce-scatter.4
  173.6 62.4 reduce-scatter.6
  270.2 40.6 all-gather.8
  312.9 38.8 all-gather.10
  355.2 62.0 reduce-scatter.8
  421.1 62.3 reduce-scatter.10

commit v6 on v1

v6 whole, which is shorter than its diff:
```python
import jax
import jax.numpy as jnp
from jax import lax
from jax.sharding import PartitionSpec as P

EPSILON = 1e-06
PLANES = 4
PARTS = 2


class Ring:
    def __init__(self):
        self.size = lax.axis_size("inner")
        self.plane = self.size // PLANES
        self.me = lax.axis_index("inner")
        self.z = self.me // self.plane
        self.bits = []
        bit = self.plane // 2
        while bit:
            self.bits.append(bit)
            bit //= 2

    def between(self, values, slot):
        step = slot * self.plane
        return lax.ppermute(values, "inner", [(d, d ^ step) for d in range(self.size)]) if slot else values

    def across(self, values, bit):
        return lax.ppermute(values, "inner", [(d, d ^ bit) for d in range(self.size)])

    def high(self, bit):
        return (self.me // bit) % 2 == 1


def add(*terms):
    return sum(t.astype(jnp.float32) for t in terms).astype(jnp.bfloat16)


def gather_rows(ring, rows):
    rows = jnp.concatenate([ring.between(rows, slot) for slot in range(PLANES)], axis=0)
    for bit in ring.bits:
        rows = jnp.concatenate([rows, ring.across(rows, bit)], axis=0)
    return rows


def plane_sums(ring, parts):
    return sum(ring.between(part, slot).astype(jnp.float32) for slot, part in enumerate(parts))


def scatter_sum(ring, rows):
    for bit in reversed(ring.bits):
        half = rows.shape[0] // 2
        rows = add(rows[:half], ring.across(rows[half:], bit))
    return plane_sums(ring, jnp.split(rows, PLANES))


def gate_lanes(layers):
    lanes = []
    for routes, gates in layers:
        high = gates.astype(jnp.bfloat16)
        lanes += [routes.astype(jnp.bfloat16), high, (gates - high.astype(jnp.float32)).astype(jnp.bfloat16)]
    lanes = jnp.concatenate(lanes, axis=1)
    return jnp.pad(lanes, ((0, 0), (0, -lanes.shape[1] % 128)))


def gate_column(ring, lanes, layer, top):
    named, high, low = (lanes[:, (3 * layer + i) * top :][:, :top].astype(jnp.float32) for i in range(3))
    return jnp.sum(jnp.where(named == ring.me.astype(jnp.float32), high + low, 0.0), axis=1, keepdims=True)


def normed(values, gain):
    widened = values.astype(jnp.float32)
    inverse = lax.rsqrt(jnp.mean(widened * widened, axis=-1, keepdims=True) + EPSILON)
    return (widened * inverse * gain).astype(jnp.bfloat16)


def expert(rows, gates, gate_up, down):
    width = down.shape[0]
    projected = jnp.dot(rows, gate_up, preferred_element_type=jnp.float32)
    hidden = (jax.nn.silu(projected[:, :width]) * projected[:, width:]).astype(jnp.bfloat16)
    out = jnp.dot(hidden, down, preferred_element_type=jnp.float32)
    return (out * gates).astype(jnp.bfloat16)


def plane_weight(ring, weight, groups):
    rows = weight.shape[0]
    first = ring.bits[0]
    if groups % 2:
        other = ring.across(weight, first)
    else:
        odd = lax.axis_index("groups") % 2
        sent = lax.dynamic_slice_in_dim(weight, odd * (rows // 2), rows // 2, axis=0)
        here = ring.across(sent, first)
        there = lax.ppermute(here, "groups", [(g, g ^ 1) for g in range(groups)])
        other = jnp.where(odd == 0, jnp.concatenate([here, there]), jnp.concatenate([there, here]))
    held = jnp.where(ring.high(first), jnp.stack([other, weight]), jnp.stack([weight, other]))
    for i, bit in enumerate(ring.bits[1:]):
        other = ring.across(held, bit)
        axis = i + 1
        held = jnp.where(ring.high(bit), jnp.stack([other, held], axis), jnp.stack([held, other], axis))
    return held.reshape(ring.plane * rows, weight.shape[1])


def merge(ring, merged_in, weight):
    share = merged_in.shape[1] // PLANES
    pieces = []
    for slot in range(PLANES):
        piece = lax.dynamic_slice_in_dim(merged_in, (ring.z ^ slot) * share, share, axis=1)
        pieces.append(ring.between(piece, slot))
    products = jnp.dot(jnp.concatenate(pieces, axis=0), weight, preferred_element_type=jnp.float32)
    return plane_sums(ring, jnp.split(products.astype(jnp.bfloat16), PLANES))


def local(
    hidden_rows,
    token_embed,
    first_routes,
    first_gates,
    first_gate_up,
    first_down,
    second_routes,
    second_gates,
    second_gate_up,
    second_down,
    hidden_gain,
    embed_gain,
    merge_weight,
):
    ring = Ring()
    width = hidden_rows.shape[1]
    top = first_routes.shape[1]
    lanes = gate_lanes([(first_routes, first_gates), (second_routes, second_gates)])
    weight = plane_weight(ring, merge_weight, lax.axis_size("groups"))

    def program(hidden, embed, lanes):
        chunk = gather_rows(ring, jnp.concatenate([hidden, lanes], axis=1))
        gates = [gate_column(ring, chunk[:, width:], layer, top) for layer in range(2)]
        first = scatter_sum(ring, expert(chunk[:, :width], gates[0], first_gate_up[0], first_down[0]))
        after_first = (hidden.astype(jnp.float32) + first).astype(jnp.bfloat16)
        merged_in = jnp.concatenate([normed(after_first, hidden_gain), normed(embed, embed_gain)], axis=1)
        merged = merge(ring, merged_in, weight)
        after_merge = (after_first.astype(jnp.float32) + jax.nn.silu(merged)).astype(jnp.bfloat16)
        chunk = gather_rows(ring, after_merge)
        second = scatter_sum(ring, expert(chunk, gates[1], second_gate_up[0], second_down[0]))
        return (after_merge.astype(jnp.float32) + second).astype(jnp.bfloat16)

    count = hidden_rows.shape[0] // PARTS
    parts = [slice(p * count, (p + 1) * count) for p in range(PARTS)]
    return jnp.concatenate([program(hidden_rows[p], token_embed[p], lanes[p]) for p in parts], axis=0)


def solution(mesh):
    rows = P(("groups", "inner"), None)
    weight = P("inner", None, None)
    return jax.shard_map(
        local,
        mesh=mesh,
        in_specs=(rows, rows, rows, rows, weight, weight, rows, rows, weight, weight, P(), P(), P("inner", None)),
        out_specs=rows,
        check_vma=False,
    )
```

time: 385 us -> 261 us (0.68)
  waiting for transfers between devices: 303 us -> 110 us
  starting transfers between devices: 0.17 us -> 99.6 us
  blocking collectives: 31.6 us -> 0 us
  between operations: 13.3 us -> 0.71 us
  local copies, waits for them, and re-layouts: 1.73 us -> 13.8 us
  other arithmetic: 8.33 us -> 19.8 us
  matrix products: 27.1 us -> 16.1 us
    reduce_scatter x3 -> x0, waiting for transfers between devices: 213 us -> none  [the longest x2 141 us: routed(): return lax.psum_scatter(part, 'inner', scatter_dimension=0, tiled=True)]
    ppermute x0 -> x55, waiting for transfers between devices: none -> 110 us  [the longest x18 68.6 us: across(): lax.ppermute(values, 'inner', [(d, d ^ bit) for d in range(self.size)])]
    ppermute x0 -> x55, starting transfers between devices: none -> 99.6 us  [the longest x36 83.5 us: between(): lax.ppermute(values, 'inner', [(d, d ^ step) for d in range(self.size)])]
    all_gather x2 -> x0, waiting for transfers between devices: 88.9 us -> none  [routed(): every = lax.all_gather(rows, 'inner', axis=0, tiled=True)]
    all_to_all x2 -> x0, blocking collectives: 31.6 us -> none  [the longest x1 18 us: local(): lax.all_to_all(merged_in, 'inner', split_axis=1, concat_axis=0, tiled=True)]
    unnamed x20 -> x38, local copies, waits for them, and re-layouts: 1.06 us -> 7.82 us
    unnamed x0 -> x9, other arithmetic: none -> 6.13 us
    dot_general x2 -> x4, matrix products: 15.1 us -> 9.42 us  [expert(): projected = jnp.dot(rows, gate_up, preferred_element_type=jnp.float32)]
  transfers between devices with their start and end apart: 5 -> 55, of which waited for: 5 -> 15; matrix products, arithmetic and copies ran while one was open for 1% -> 14% of each run, Pallas kernels for 0% -> 0%
where the time goes in v6:
time: 261 us; the launch traced here: 260 us
  waiting for transfers between devices  110 us (42%)
  starting transfers between devices  99.6 us (38%)
  other arithmetic  19.8 us (8%)
  matrix products  16.1 us (6%)
  local copies, waits for them, and re-layouts  13.8 us (5%)
    ppermute x36, starting transfers between devices, between(): lax.ppermute(values, 'inner', [(d, d ^ step) for d in range(self.size)])  83.5 us
    ppermute x18, waiting for transfers between devices, across(): lax.ppermute(values, 'inner', [(d, d ^ bit) for d in range(self.size)])  68.6 us
    ppermute x36, waiting for transfers between devices, between(): lax.ppermute(values, 'inner', [(d, d ^ step) for d in range(self.size)])  29.3 us
    ppermute x18, starting transfers between devices, across(): lax.ppermute(values, 'inner', [(d, d ^ bit) for d in range(self.size)])  14.5 us
    ppermute x1, waiting for transfers between devices, plane_weight(): there = lax.ppermute(here, 'groups', [(g, g ^ 1) for g in range(groups)])  12.4 us
    dot_general x4, matrix products, expert(): projected = jnp.dot(rows, gate_up, preferred_element_type=jnp.float32)  9.42 us
    unnamed x38, local copies, waits for them, and re-layouts  7.82 us
    unnamed x9, other arithmetic  6.13 us
  transfers between devices with their start and end apart: 55, of which 15 were waited for; matrix products, arithmetic and copies ran while one was open for 14% of the time, Pallas kernels for 0%

profile of v6, /device:TPU:0, one launch (start us, length us, event | category | flops | bytes accessed | tf_op | source)
XLA Modules:
  0.0 260.3 jit_solution(15876789459752859312)
XLA Ops:
  7.1 3.0 %collective-permute-start = (bf16[32,2176]{1,0:T(8,128)(2,1)}, bf16[32,2176]{1,0:T(8,128)(2,1)}, u32[]{:S(2)}, u32[]{:S(2)}) collective-permute-start(bf16[32,2176]{1,0:T(8,128)(2,1)} %get-tuple-element.67), channel_id=1, source_target_pairs={{0,4},{1,5},{2,6},{3,7},{4,0},{5,1},{6,2},{7,3},{8,12},{9,13},{10,... | collective-permute-start | bytes 417800 | tf_op jit(solution)/shard_map/ppermute | solution.py:25
  10.1 2.6 collective-permute-start.1
  16.5 3.5 %collective-permute-start.30 = (bf16[32,2176]{1,0:T(8,128)(2,1)}, bf16[32,2176]{1,0:T(8,128)(2,1)}, u32[]{:S(2)}, u32[]{:S(2)}) collective-permute-start(bf16[32,2176]{1,0:T(8,128)(2,1)} %get-tuple-element.76), channel_id=1, source_target_pairs={{0,8},{1,9},{2,10},{3,11},{4,12},{5,13},{6,14},{7,15},{8,0},{9,1},... | collective-permute-start | bytes 417800 | tf_op jit(solution)/shard_map/ppermute | solution.py:25
  20.0 1.7 fusion.26
  24.3 1.7 collective-permute-start.13
  27.5 8.3 %collective-permute-done.30 = bf16[32,2176]{1,0:T(8,128)(2,1)} collective-permute-done((bf16[32,2176]{1,0:T(8,128)(2,1)}, bf16[32,2176]{1,0:T(8,128)(2,1)}, u32[]{:S(2)}, u32[]{:S(2)}) %collective-permute-start.30) | collective-permute-done | bytes 139296 | tf_op jit(solution)/shard_map/ppermute | solution.py:25
  36.8 1.6 collective-permute-start.32
  39.4 1.6 constant_dynamic-update-slice_fusion.31
  41.0 1.6 constant_dynamic-update-slice_fusion.30
  43.4 17.2 %collective-permute-done.32 = bf16[128,2176]{1,0:T(8,128)(2,1)S(1)} collective-permute-done((bf16[128,2176]{1,0:T(8,128)(2,1)S(1)}, bf16[128,2176]{1,0:T(8,128)(2,1)S(1)}, u32[]{:S(2)}, u32[]{:S(2)}) %collective-permute-start.32) | collective-permute-done | bytes 557088 | tf_op jit(solution)/shard_map/ppermute | solution.py:28
  62.6 1.6 collective-permute-start.14
  64.6 12.4 %collective-permute-done.14 = bf16[128,2048]{1,0:T(8,128)(2,1)S(1)} collective-permute-done((bf16[128,2048]{1,0:T(8,128)(2,1)S(1)}, bf16[128,2048]{1,0:T(8,128)(2,1)S(1)}, u32[]{:S(2)}, u32[]{:S(2)}) %collective-permute-start.14) | collective-permute-done | bytes 524320 | tf_op jit(solution)/shard_map/ppermute | solution.py:93
  77.4 1.8 copy-done.9
  79.1 2.4 fusion.4
  84.1 2.3 fusion.6
  89.6 1.6 collective-permute-start.35
  92.7 11.7 %collective-permute-done.35 = bf16[128,2048]{1,0:T(8,128)(2,1)S(1)} collective-permute-done((bf16[128,2048]{1,0:T(8,128)(2,1)S(1)}, bf16[128,2048]{1,0:T(8,128)(2,1)S(1)}, u32[]{:S(2)}, u32[]{:S(2)}) %collective-permute-start.35) | collective-permute-done | bytes 524320 | tf_op jit(solution)/shard_map/ppermute | solution.py:28
  105.1 3.5 %collective-permute-start.37 = (bf16[32,2048]{1,0:T(8,128)(2,1)S(1)}, bf16[32,2048]{1,0:T(8,128)(2,1)S(1)}, u32[]{:S(2)}, u32[]{:S(2)}) collective-permute-start(bf16[32,2048]{1,0:T(8,128)(2,1)S(1)} %get-tuple-element.44), channel_id=1, source_target_pairs={{0,8},{1,9},{2,10},{3,11},{4,12},{5,13},{6,14},{7,15},{8,0},{9,1},... | collective-permute-start | bytes 393224 | tf_op jit(solution)/shard_map/ppermute | solution.py:25
  109.0 6.2 %collective-permute-done.6 = bf16[128,2048]{1,0:T(8,128)(2,1)S(1)} collective-permute-done((bf16[128,2048]{1,0:T(8,128)(2,1)S(1)}, bf16[128,2048]{1,0:T(8,128)(2,1)S(1)}, u32[]{:S(2)}, u32[]{:S(2)}) %collective-permute-start.6) | collective-permute-done | bytes 524320 | tf_op jit(solution)/shard_map/ppermute | solution.py:28
  116.0 3.5 %collective-permute-start.8 = (bf16[32,2048]{1,0:T(8,128)(2,1)S(1)}, bf16[32,2048]{1,0:T(8,128)(2,1)S(1)}, u32[]{:S(2)}, u32[]{:S(2)}) collective-permute-start(bf16[32,2048]{1,0:T(8,128)(2,1)S(1)} %get-tuple-element.33), channel_id=1, source_target_pairs={{0,8},{1,9},{2,10},{3,11},{4,12},{5,13},{6,14},{7,15},{8,0},{9,1},... | collective-permute-start | bytes 393224 | tf_op jit(solution)/shard_map/ppermute | solution.py:25
  120.7 2.0 collective-permute-done.7
  122.8 6.7 %collective-permute-done.8 = bf16[32,2048]{1,0:T(8,128)(2,1)S(1)} collective-permute-done((bf16[32,2048]{1,0:T(8,128)(2,1)S(1)}, bf16[32,2048]{1,0:T(8,128)(2,1)S(1)}, u32[]{:S(2)}, u32[]{:S(2)}) %collective-permute-start.8) | collective-permute-done | bytes 131104 | tf_op jit(solution)/shard_map/ppermute | solution.py:25
  130.3 2.2 collective-permute-start.10
  136.3 2.0 collective-permute-start.40
  141.3 3.6 %collective-permute-start.16 = (bf16[32,2048]{1,0:T(8,128)(2,1)S(1)}, bf16[32,2048]{1,0:T(8,128)(2,1)S(1)}, u32[]{:S(2)}, u32[]{:S(2)}) collective-permute-start(bf16[32,2048]{1,0:T(8,128)(2,1)S(1)} %get-tuple-element.28), channel_id=1, source_target_pairs={{0,4},{1,5},{2,6},{3,7},{4,0},{5,1},{6,2},{7,3},{8,12},{9,13},{10,... | collective-permute-start | bytes 393224 | tf_op jit(solution)/shard_map/ppermute | solution.py:25
  144.9 1.5 collective-permute-start.17
  148.6 2.7 %collective-permute-start.42 = (bf16[32,2048]{1,0:T(8,128)(2,1)S(1)}, bf16[32,2048]{1,0:T(8,128)(2,1)S(1)}, u32[]{:S(2)}, u32[]{:S(2)}) collective-permute-start(bf16[32,2048]{1,0:T(8,128)(2,1)S(1)} %get-tuple-element.39), channel_id=1, source_target_pairs={{0,4},{1,5},{2,6},{3,7},{4,0},{5,1},{6,2},{7,3},{8,12},{9,13},{10,... | collective-permute-start | bytes 393224 | tf_op jit(solution)/shard_map/ppermute | solution.py:25
  151.2 1.5 collective-permute-start.43
  154.1 2.5 collective-permute-done.17
  156.8 7.9 %collective-permute-start.19 = (bf16[32,2048]{1,0:T(8,128)(2,1)S(1)}, bf16[32,2048]{1,0:T(8,128)(2,1)S(1)}, u32[]{:S(2)}, u32[]{:S(2)}) collective-permute-start(bf16[32,2048]{1,0:T(8,128)(2,1)S(1)} %get-tuple-element.12), channel_id=1, source_target_pairs={{0,4},{1,5},{2,6},{3,7},{4,0},{5,1},{6,2},{7,3},{8,12},{9,13},{10,... | collective-permute-start | bytes 393224 | tf_op jit(solution)/shard_map/ppermute | solution.py:25
  165.5 1.7 collective-permute-start.21
  167.4 8.6 %collective-permute-start.45 = (bf16[32,2048]{1,0:T(8,128)(2,1)S(1)}, bf16[32,2048]{1,0:T(8,128)(2,1)S(1)}, u32[]{:S(2)}, u32[]{:S(2)}) collective-permute-start(bf16[32,2048]{1,0:T(8,128)(2,1)S(1)} %get-tuple-element.16), channel_id=1, source_target_pairs={{0,4},{1,5},{2,6},{3,7},{4,0},{5,1},{6,2},{7,3},{8,12},{9,13},{10,... | collective-permute-start | bytes 393224 | tf_op jit(solution)/shard_map/ppermute | solution.py:25
  176.7 1.7 collective-permute-start.47
  178.5 1.6 collective-permute-start.22
  180.2 9.7 %collective-permute-done.22 = bf16[128,2048]{1,0:T(8,128)(2,1)S(1)} collective-permute-done((bf16[128,2048]{1,0:T(8,128)(2,1)S(1)}, bf16[128,2048]{1,0:T(8,128)(2,1)S(1)}, u32[]{:S(2)}, u32[]{:S(2)}) %collective-permute-start.22) | collective-permute-done | bytes 524320 | tf_op jit(solution)/shard_map/ppermute | solution.py:28
  190.1 1.6 collective-permute-start.48
  191.8 12.7 %collective-permute-done.48 = bf16[128,2048]{1,0:T(8,128)(2,1)S(1)} collective-permute-done((bf16[128,2048]{1,0:T(8,128)(2,1)S(1)}, bf16[128,2048]{1,0:T(8,128)(2,1)S(1)}, u32[]{:S(2)}, u32[]{:S(2)}) %collective-permute-start.48) | collective-permute-done | bytes 524320 | tf_op jit(solution)/shard_map/ppermute | solution.py:28
  204.8 2.3 fusion.2
  209.2 2.4 fusion
  213.5 1.6 collective-permute-start.25
  216.2 1.6 collective-permute-start.51
  217.8 10.6 %collective-permute-done.25 = bf16[128,2048]{1,0:T(8,128)(2,1)S(1)} collective-permute-done((bf16[128,2048]{1,0:T(8,128)(2,1)S(1)}, bf16[128,2048]{1,0:T(8,128)(2,1)S(1)}, u32[]{:S(2)}, u32[]{:S(2)}) %collective-permute-start.25) | collective-permute-done | bytes 524320 | tf_op jit(solution)/shard_map/ppermute | solution.py:28
  228.5 6.5 %collective-permute-start.26 = (bf16[32,2048]{1,0:T(8,128)(2,1)S(1)}, bf16[32,2048]{1,0:T(8,128)(2,1)S(1)}, u32[]{:S(2)}, u32[]{:S(2)}) collective-permute-start(bf16[32,2048]{1,0:T(8,128)(2,1)S(1)} %get-tuple-element.23), channel_id=1, source_target_pairs={{0,4},{1,5},{2,6},{3,7},{4,0},{5,1},{6,2},{7,3},{8,12},{9,13},{10,... | collective-permute-start | bytes 393224 | tf_op jit(solution)/shard_map/ppermute | solution.py:25
  235.0 3.5 %collective-permute-start.27 = (bf16[32,2048]{1,0:T(8,128)(2,1)S(1)}, bf16[32,2048]{1,0:T(8,128)(2,1)S(1)}, u32[]{:S(2)}, u32[]{:S(2)}) collective-permute-start(bf16[32,2048]{1,0:T(8,128)(2,1)S(1)} %get-tuple-element.25), channel_id=1, source_target_pairs={{0,8},{1,9},{2,10},{3,11},{4,12},{5,13},{6,14},{7,15},{8,0},{9,1},... | collective-permute-start | bytes 393224 | tf_op jit(solution)/shard_map/ppermute | solution.py:25
  240.0 5.8 %collective-permute-start.52 = (bf16[32,2048]{1,0:T(8,128)(2,1)S(1)}, bf16[32,2048]{1,0:T(8,128)(2,1)S(1)}, u32[]{:S(2)}, u32[]{:S(2)}) collective-permute-start(bf16[32,2048]{1,0:T(8,128)(2,1)S(1)} %get-tuple-element.34), channel_id=1, source_target_pairs={{0,4},{1,5},{2,6},{3,7},{4,0},{5,1},{6,2},{7,3},{8,12},{9,13},{10,... | collective-permute-start | bytes 393224 | tf_op jit(solution)/shard_map/ppermute | solution.py:25
  245.8 3.5 %collective-permute-start.53 = (bf16[32,2048]{1,0:T(8,128)(2,1)S(1)}, bf16[32,2048]{1,0:T(8,128)(2,1)S(1)}, u32[]{:S(2)}, u32[]{:S(2)}) collective-permute-start(bf16[32,2048]{1,0:T(8,128)(2,1)S(1)} %get-tuple-element.36), channel_id=1, source_target_pairs={{0,8},{1,9},{2,10},{3,11},{4,12},{5,13},{6,14},{7,15},{8,0},{9,1},... | collective-permute-start | bytes 393224 | tf_op jit(solution)/shard_map/ppermute | solution.py:25
  250.8 2.7 %collective-permute-done.52 = bf16[32,2048]{1,0:T(8,128)(2,1)S(1)} collective-permute-done((bf16[32,2048]{1,0:T(8,128)(2,1)S(1)}, bf16[32,2048]{1,0:T(8,128)(2,1)S(1)}, u32[]{:S(2)}, u32[]{:S(2)}) %collective-permute-start.52) | collective-permute-done | bytes 131104 | tf_op jit(solution)/shard_map/ppermute | solution.py:25
  253.4 6.0 %collective-permute-done.54 = bf16[32,2048]{1,0:T(8,128)(2,1)S(1)} collective-permute-done((bf16[32,2048]{1,0:T(8,128)(2,1)S(1)}, bf16[32,2048]{1,0:T(8,128)(2,1)S(1)}, u32[]{:S(2)}, u32[]{:S(2)}) %collective-permute-start.54) | collective-permute-done | bytes 131104 | tf_op jit(solution)/shard_map/ppermute | solution.py:25
  (176 shorter events, 53.3 us)
Async XLA Ops:
  7.1 17.2 %collective-permute-start = (bf16[32,2176]{1,0:T(8,128)(2,1)}, bf16[32,2176]{1,0:T(8,128)(2,1)}, u32[]{:S(2)}, u32[]{:S(2)}) collective-permute-start(bf16[32,2176]{1,0:T(8,128)(2,1)} %get-tuple-element.67), channel_id=1, source_target_pairs={{0,4},{1,5},{2,6},{3,7},{4,0},{5,1},{6,2},{7,3},{8,12},{9,13},{10,... | collective-permute-start | bytes 417800 | tf_op jit(solution)/shard_map/ppermute | solution.py:25
  10.1 14.2 %collective-permute-start.1 = (bf16[32,2176]{1,0:T(8,128)(2,1)}, bf16[32,2176]{1,0:T(8,128)(2,1)}, u32[]{:S(2)}, u32[]{:S(2)}) collective-permute-start(bf16[32,2176]{1,0:T(8,128)(2,1)} %get-tuple-element.67), channel_id=1, source_target_pairs={{0,8},{1,9},{2,10},{3,11},{4,12},{5,13},{6,14},{7,15},{8,0},{9,1},... | collective-permute-start | bytes 417800 | tf_op jit(solution)/shard_map/ppermute | solution.py:25
  12.7 13.4 %collective-permute-start.2 = (bf16[32,2176]{1,0:T(8,128)(2,1)}, bf16[32,2176]{1,0:T(8,128)(2,1)S(1)}, u32[]{:S(2)}, u32[]{:S(2)}) collective-permute-start(bf16[32,2176]{1,0:T(8,128)(2,1)} %get-tuple-element.67), channel_id=1, source_target_pairs={{0,12},{1,13},{2,14},{3,15},{4,8},{5,9},{6,10},{7,11},{8,4},{9,5},... | collective-permute-start | bytes 417800 | tf_op jit(solution)/shard_map/ppermute | solution.py:25
  15.6 11.9 %collective-permute-start.29 = (bf16[32,2176]{1,0:T(8,128)(2,1)}, bf16[32,2176]{1,0:T(8,128)(2,1)}, u32[]{:S(2)}, u32[]{:S(2)}) collective-permute-start(bf16[32,2176]{1,0:T(8,128)(2,1)} %get-tuple-element.76), channel_id=1, source_target_pairs={{0,4},{1,5},{2,6},{3,7},{4,0},{5,1},{6,2},{7,3},{8,12},{9,13},{10,... | collective-permute-start | bytes 417800 | tf_op jit(solution)/shard_map/ppermute | solution.py:25
  16.5 19.3 %collective-permute-start.30 = (bf16[32,2176]{1,0:T(8,128)(2,1)}, bf16[32,2176]{1,0:T(8,128)(2,1)}, u32[]{:S(2)}, u32[]{:S(2)}) collective-permute-start(bf16[32,2176]{1,0:T(8,128)(2,1)} %get-tuple-element.76), channel_id=1, source_target_pairs={{0,8},{1,9},{2,10},{3,11},{4,12},{5,13},{6,14},{7,15},{8,0},{9,1},... | collective-permute-start | bytes 417800 | tf_op jit(solution)/shard_map/ppermute | solution.py:25
  24.2 11.6 %collective-permute-start.31 = (bf16[32,2176]{1,0:T(8,128)(2,1)}, bf16[32,2176]{1,0:T(8,128)(2,1)S(1)}, u32[]{:S(2)}, u32[]{:S(2)}) collective-permute-start(bf16[32,2176]{1,0:T(8,128)(2,1)} %get-tuple-element.76), channel_id=1, source_target_pairs={{0,12},{1,13},{2,14},{3,15},{4,8},{5,9},{6,10},{7,11},{8,4},{9,5},... | collective-permute-start | bytes 417800 | tf_op jit(solution)/shard_map/ppermute | solution.py:25
  24.3 38.2 %collective-permute-start.13 = (bf16[128,2048]{1,0:T(8,128)(2,1)S(1)}, bf16[128,2048]{1,0:T(8,128)(2,1)S(1)}, u32[]{:S(2)}, u32[]{:S(2)}) collective-permute-start(bf16[128,2048]{1,0:T(8,128)(2,1)S(1)} %constant_dynamic-slice_fusion), channel_id=1, source_target_pairs={{0,2},{1,3},{2,0},{3,1},{4,6},{5,7},{6,4},{7,5},{8,10},{9,11},{10,... | collective-permute-start | bytes 1572872 | tf_op jit(solution)/shard_map/ppermute | solution.py:28
  27.1 37.1 %collective-permute-start.3 = (bf16[128,2176]{1,0:T(8,128)(2,1)S(1)}, bf16[128,2176]{1,0:T(8,128)(2,1)S(1)}, u32[]{:S(2)}, u32[]{:S(2)}) collective-permute-start(bf16[128,2176]{1,0:T(8,128)(2,1)S(1)} %pad_maximum_fusion), channel_id=1, source_target_pairs={{0,2},{1,3},{2,0},{3,1},{4,6},{5,7},{6,4},{7,5},{8,10},{9,11},{10,... | collective-permute-start | bytes 1671176 | tf_op jit(solution)/shard_map/ppermute | solution.py:28
  36.8 23.7 %collective-permute-start.32 = (bf16[128,2176]{1,0:T(8,128)(2,1)S(1)}, bf16[128,2176]{1,0:T(8,128)(2,1)S(1)}, u32[]{:S(2)}, u32[]{:S(2)}) collective-permute-start(bf16[128,2176]{1,0:T(8,128)(2,1)S(1)} %pad_maximum_fusion.1), channel_id=1, source_target_pairs={{0,2},{1,3},{2,0},{3,1},{4,6},{5,7},{6,4},{7,5},{8,10},{9,11},{10,... | collective-permute-start | bytes 1671176 | tf_op jit(solution)/shard_map/ppermute | solution.py:28
  61.6 15.6 %collective-permute-start.33 = (bf16[256,2176]{1,0:T(8,128)(2,1)}, bf16[256,2176]{1,0:T(8,128)(2,1)S(1)}, u32[]{:S(2)}, u32[]{:S(2)}) collective-permute-start(bf16[256,2176]{1,0:T(8,128)(2,1)} %get-tuple-element.21), channel_id=1, source_target_pairs={{0,1},{1,0},{2,3},{3,2},{4,5},{5,4},{6,7},{7,6},{8,9},{9,8},{10,11... | collective-permute-start | bytes 3342344 | tf_op jit(solution)/shard_map/ppermute | solution.py:28
  62.6 14.4 %collective-permute-start.14 = (bf16[128,2048]{1,0:T(8,128)(2,1)S(1)}, bf16[128,2048]{1,0:T(8,128)(2,1)S(1)}, u32[]{:S(2)}, u32[]{:S(2)}) collective-permute-start(bf16[128,2048]{1,0:T(8,128)(2,1)S(1)} %collective-permute-done.13), channel_id=1, source_target_pairs={{0,16},{16,0},{1,17},{17,1},{2,18},{18,2},{3,19},{19,3},{4,20},{20... | collective-permute-start | bytes 1572872 | tf_op jit(solution)/shard_map/ppermute | solution.py:93
  64.3 17.3 %collective-permute-start.4 = (bf16[256,2176]{1,0:T(8,128)(2,1)S(1)}, bf16[256,2176]{1,0:T(8,128)(2,1)S(1)}, u32[]{:S(2)}, u32[]{:S(2)}) collective-permute-start(bf16[256,2176]{1,0:T(8,128)(2,1)S(1)} %get-tuple-element.19), channel_id=1, source_target_pairs={{0,1},{1,0},{2,3},{3,2},{4,5},{5,4},{6,7},{7,6},{8,9},{9,8},{10,11... | collective-permute-start | bytes 3342344 | tf_op jit(solution)/shard_map/ppermute | solution.py:28
  88.7 27.2 %collective-permute-start.15 = (bf16[2,256,2048]{2,1,0:T(8,128)(2,1)S(1)}, bf16[2,256,2048]{2,1,0:T(8,128)(2,1)S(1)}, u32[]{:S(2)}, u32[]{:S(2)}) collective-permute-start(bf16[2,256,2048]{2,1,0:T(8,128)(2,1)S(1)} %maximum_select_fusion.1), channel_id=1, source_target_pairs={{0,1},{1,0},{2,3},{3,2},{4,5},{5,4},{6,7},{7,6},{8,9},{9,8},{10,11... | collective-permute-start | bytes 6291464 | tf_op jit(solution)/shard_map/ppermute | solution.py:28
  89.6 14.8 %collective-permute-start.35 = (bf16[128,2048]{1,0:T(8,128)(2,1)S(1)}, bf16[128,2048]{1,0:T(8,128)(2,1)S(1)}, u32[]{:S(2)}, u32[]{:S(2)}) collective-permute-start(bf16[128,2048]{1,0:T(8,128)(2,1)S(1)} %slice.240), channel_id=1, source_target_pairs={{0,2},{1,3},{2,0},{3,1},{4,6},{5,7},{6,4},{7,5},{8,10},{9,11},{10,... | collective-permute-start | bytes 1572872 | tf_op jit(solution)/shard_map/ppermute | solution.py:28
  91.6 23.6 %collective-permute-start.6 = (bf16[128,2048]{1,0:T(8,128)(2,1)S(1)}, bf16[128,2048]{1,0:T(8,128)(2,1)S(1)}, u32[]{:S(2)}, u32[]{:S(2)}) collective-permute-start(bf16[128,2048]{1,0:T(8,128)(2,1)S(1)} %slice.221), channel_id=1, source_target_pairs={{0,2},{1,3},{2,0},{3,1},{4,6},{5,7},{6,4},{7,5},{8,10},{9,11},{10,... | collective-permute-start | bytes 1572872 | tf_op jit(solution)/shard_map/ppermute | solution.py:28
  104.6 14.9 %collective-permute-start.36 = (bf16[32,2048]{1,0:T(8,128)(2,1)S(1)}, bf16[32,2048]{1,0:T(8,128)(2,1)S(1)}, u32[]{:S(2)}, u32[]{:S(2)}) collective-permute-start(bf16[32,2048]{1,0:T(8,128)(2,1)S(1)} %get-tuple-element.42), channel_id=1, source_target_pairs={{0,4},{1,5},{2,6},{3,7},{4,0},{5,1},{6,2},{7,3},{8,12},{9,13},{10,... | collective-permute-start | bytes 393224 | tf_op jit(solution)/shard_map/ppermute | solution.py:25
  105.1 15.6 %collective-permute-start.37 = (bf16[32,2048]{1,0:T(8,128)(2,1)S(1)}, bf16[32,2048]{1,0:T(8,128)(2,1)S(1)}, u32[]{:S(2)}, u32[]{:S(2)}) collective-permute-start(bf16[32,2048]{1,0:T(8,128)(2,1)S(1)} %get-tuple-element.44), channel_id=1, source_target_pairs={{0,8},{1,9},{2,10},{3,11},{4,12},{5,13},{6,14},{7,15},{8,0},{9,1},... | collective-permute-start | bytes 393224 | tf_op jit(solution)/shard_map/ppermute | solution.py:25
  108.7 12.1 %collective-permute-start.38 = (bf16[32,2048]{1,0:T(8,128)(2,1)S(1)}, bf16[32,2048]{1,0:T(8,128)(2,1)S(1)}, u32[]{:S(2)}, u32[]{:S(2)}) collective-permute-start(bf16[32,2048]{1,0:T(8,128)(2,1)S(1)} %get-tuple-element.43), channel_id=1, source_target_pairs={{0,12},{1,13},{2,14},{3,15},{4,8},{5,9},{6,10},{7,11},{8,4},{9,5},... | collective-permute-start | bytes 393224 | tf_op jit(solution)/shard_map/ppermute | solution.py:25
  116.0 13.5 %collective-permute-start.8 = (bf16[32,2048]{1,0:T(8,128)(2,1)S(1)}, bf16[32,2048]{1,0:T(8,128)(2,1)S(1)}, u32[]{:S(2)}, u32[]{:S(2)}) collective-permute-start(bf16[32,2048]{1,0:T(8,128)(2,1)S(1)} %get-tuple-element.33), channel_id=1, source_target_pairs={{0,8},{1,9},{2,10},{3,11},{4,12},{5,13},{6,14},{7,15},{8,0},{9,1},... | collective-permute-start | bytes 393224 | tf_op jit(solution)/shard_map/ppermute | solution.py:25
  119.5 10.0 %collective-permute-start.9 = (bf16[32,2048]{1,0:T(8,128)(2,1)S(1)}, bf16[32,2048]{1,0:T(8,128)(2,1)S(1)}, u32[]{:S(2)}, u32[]{:S(2)}) collective-permute-start(bf16[32,2048]{1,0:T(8,128)(2,1)S(1)} %get-tuple-element.32), channel_id=1, source_target_pairs={{0,12},{1,13},{2,14},{3,15},{4,8},{5,9},{6,10},{7,11},{8,4},{9,5},... | collective-permute-start | bytes 393224 | tf_op jit(solution)/shard_map/ppermute | solution.py:25
  130.3 8.0 %collective-permute-start.10 = (bf16[32,1024]{1,0:T(8,128)(2,1)S(1)}, bf16[32,1024]{1,0:T(8,128)(2,1)S(1)}, u32[]{:S(2)}, u32[]{:S(2)}) collective-permute-start(bf16[32,1024]{1,0:T(8,128)(2,1)S(1)} %get-tuple-element.48), channel_id=1, source_target_pairs={{0,4},{1,5},{2,6},{3,7},{4,0},{5,1},{6,2},{7,3},{8,12},{9,13},{10,... | collective-permute-start | bytes 196616 | tf_op jit(solution)/shard_map/ppermute | solution.py:25
  132.5 8.1 %collective-permute-start.11 = (bf16[32,1024]{1,0:T(8,128)(2,1)S(1)}, bf16[32,1024]{1,0:T(8,128)(2,1)S(1)}, u32[]{:S(2)}, u32[]{:S(2)}) collective-permute-start(bf16[32,1024]{1,0:T(8,128)(2,1)S(1)} %get-tuple-element.49), channel_id=1, source_target_pairs={{0,8},{1,9},{2,10},{3,11},{4,12},{5,13},{6,14},{7,15},{8,0},{9,1},... | collective-permute-start | bytes 196616 | tf_op jit(solution)/shard_map/ppermute | solution.py:25
  135.2 11.3 %collective-permute-start.39 = (bf16[32,1024]{1,0:T(8,128)(2,1)S(1)}, bf16[32,1024]{1,0:T(8,128)(2,1)S(1)}, u32[]{:S(2)}, u32[]{:S(2)}) collective-permute-start(bf16[32,1024]{1,0:T(8,128)(2,1)S(1)} %get-tuple-element.56), channel_id=1, source_target_pairs={{0,4},{1,5},{2,6},{3,7},{4,0},{5,1},{6,2},{7,3},{8,12},{9,13},{10,... | collective-permute-start | bytes 196616 | tf_op jit(solution)/shard_map/ppermute | solution.py:25
  136.3 11.5 %collective-permute-start.40 = (bf16[32,1024]{1,0:T(8,128)(2,1)S(1)}, bf16[32,1024]{1,0:T(8,128)(2,1)S(1)}, u32[]{:S(2)}, u32[]{:S(2)}) collective-permute-start(bf16[32,1024]{1,0:T(8,128)(2,1)S(1)} %get-tuple-element.57), channel_id=1, source_target_pairs={{0,8},{1,9},{2,10},{3,11},{4,12},{5,13},{6,14},{7,15},{8,0},{9,1},... | collective-permute-start | bytes 196616 | tf_op jit(solution)/shard_map/ppermute | solution.py:25
  138.2 9.6 %collective-permute-start.41 = (bf16[32,1024]{1,0:T(8,128)(2,1)S(1)}, bf16[32,1024]{1,0:T(8,128)(2,1)S(1)}, u32[]{:S(2)}, u32[]{:S(2)}) collective-permute-start(bf16[32,1024]{1,0:T(8,128)(2,1)S(1)} %get-tuple-element.58), channel_id=1, source_target_pairs={{0,12},{1,13},{2,14},{3,15},{4,8},{5,9},{6,10},{7,11},{8,4},{9,5},... | collective-permute-start | bytes 196616 | tf_op jit(solution)/shard_map/ppermute | solution.py:25
  141.3 11.4 %collective-permute-start.16 = (bf16[32,2048]{1,0:T(8,128)(2,1)S(1)}, bf16[32,2048]{1,0:T(8,128)(2,1)S(1)}, u32[]{:S(2)}, u32[]{:S(2)}) collective-permute-start(bf16[32,2048]{1,0:T(8,128)(2,1)S(1)} %get-tuple-element.28), channel_id=1, source_target_pairs={{0,4},{1,5},{2,6},{3,7},{4,0},{5,1},{6,2},{7,3},{8,12},{9,13},{10,... | collective-permute-start | bytes 393224 | tf_op jit(solution)/shard_map/ppermute | solution.py:25
  144.9 11.8 %collective-permute-start.17 = (bf16[32,2048]{1,0:T(8,128)(2,1)S(1)}, bf16[32,2048]{1,0:T(8,128)(2,1)S(1)}, u32[]{:S(2)}, u32[]{:S(2)}) collective-permute-start(bf16[32,2048]{1,0:T(8,128)(2,1)S(1)} %get-tuple-element.30), channel_id=1, source_target_pairs={{0,8},{1,9},{2,10},{3,11},{4,12},{5,13},{6,14},{7,15},{8,0},{9,1},... | collective-permute-start | bytes 393224 | tf_op jit(solution)/shard_map/ppermute | solution.py:25
  146.4 10.2 %collective-permute-start.18 = (bf16[32,2048]{1,0:T(8,128)(2,1)S(1)}, bf16[32,2048]{1,0:T(8,128)(2,1)S(1)}, u32[]{:S(2)}, u32[]{:S(2)}) collective-permute-start(bf16[32,2048]{1,0:T(8,128)(2,1)S(1)} %get-tuple-element.29), channel_id=1, source_target_pairs={{0,12},{1,13},{2,14},{3,15},{4,8},{5,9},{6,10},{7,11},{8,4},{9,5},... | collective-permute-start | bytes 393224 | tf_op jit(solution)/shard_map/ppermute | solution.py:25
  148.6 16.9 %collective-permute-start.42 = (bf16[32,2048]{1,0:T(8,128)(2,1)S(1)}, bf16[32,2048]{1,0:T(8,128)(2,1)S(1)}, u32[]{:S(2)}, u32[]{:S(2)}) collective-permute-start(bf16[32,2048]{1,0:T(8,128)(2,1)S(1)} %get-tuple-element.39), channel_id=1, source_target_pairs={{0,4},{1,5},{2,6},{3,7},{4,0},{5,1},{6,2},{7,3},{8,12},{9,13},{10,... | collective-permute-start | bytes 393224 | tf_op jit(solution)/shard_map/ppermute | solution.py:25
  151.2 16.0 %collective-permute-start.43 = (bf16[32,2048]{1,0:T(8,128)(2,1)S(1)}, bf16[32,2048]{1,0:T(8,128)(2,1)S(1)}, u32[]{:S(2)}, u32[]{:S(2)}) collective-permute-start(bf16[32,2048]{1,0:T(8,128)(2,1)S(1)} %get-tuple-element.41), channel_id=1, source_target_pairs={{0,8},{1,9},{2,10},{3,11},{4,12},{5,13},{6,14},{7,15},{8,0},{9,1},... | collective-permute-start | bytes 393224 | tf_op jit(solution)/shard_map/ppermute | solution.py:25
  152.7 14.5 %collective-permute-start.44 = (bf16[32,2048]{1,0:T(8,128)(2,1)S(1)}, bf16[32,2048]{1,0:T(8,128)(2,1)S(1)}, u32[]{:S(2)}, u32[]{:S(2)}) collective-permute-start(bf16[32,2048]{1,0:T(8,128)(2,1)S(1)} %get-tuple-element.40), channel_id=1, source_target_pairs={{0,12},{1,13},{2,14},{3,15},{4,8},{5,9},{6,10},{7,11},{8,4},{9,5},... | collective-permute-start | bytes 393224 | tf_op jit(solution)/shard_map/ppermute | solution.py:25
  156.8 19.9 %collective-permute-start.19 = (bf16[32,2048]{1,0:T(8,128)(2,1)S(1)}, bf16[32,2048]{1,0:T(8,128)(2,1)S(1)}, u32[]{:S(2)}, u32[]{:S(2)}) collective-permute-start(bf16[32,2048]{1,0:T(8,128)(2,1)S(1)} %get-tuple-element.12), channel_id=1, source_target_pairs={{0,4},{1,5},{2,6},{3,7},{4,0},{5,1},{6,2},{7,3},{8,12},{9,13},{10,... | collective-permute-start | bytes 393224 | tf_op jit(solution)/shard_map/ppermute | solution.py:25
  164.7 13.8 %collective-permute-start.20 = (bf16[32,2048]{1,0:T(8,128)(2,1)S(1)}, bf16[32,2048]{1,0:T(8,128)(2,1)S(1)}, u32[]{:S(2)}, u32[]{:S(2)}) collective-permute-start(bf16[32,2048]{1,0:T(8,128)(2,1)S(1)} %get-tuple-element.12), channel_id=1, source_target_pairs={{0,8},{1,9},{2,10},{3,11},{4,12},{5,13},{6,14},{7,15},{8,0},{9,1},... | collective-permute-start | bytes 393224 | tf_op jit(solution)/shard_map/ppermute | solution.py:25
  165.5 13.0 %collective-permute-start.21 = (bf16[32,2048]{1,0:T(8,128)(2,1)S(1)}, bf16[32,2048]{1,0:T(8,128)(2,1)S(1)}, u32[]{:S(2)}, u32[]{:S(2)}) collective-permute-start(bf16[32,2048]{1,0:T(8,128)(2,1)S(1)} %get-tuple-element.12), channel_id=1, source_target_pairs={{0,12},{1,13},{2,14},{3,15},{4,8},{5,9},{6,10},{7,11},{8,4},{9,5},... | collective-permute-start | bytes 393224 | tf_op jit(solution)/shard_map/ppermute | solution.py:25
  167.4 22.7 %collective-permute-start.45 = (bf16[32,2048]{1,0:T(8,128)(2,1)S(1)}, bf16[32,2048]{1,0:T(8,128)(2,1)S(1)}, u32[]{:S(2)}, u32[]{:S(2)}) collective-permute-start(bf16[32,2048]{1,0:T(8,128)(2,1)S(1)} %get-tuple-element.16), channel_id=1, source_target_pairs={{0,4},{1,5},{2,6},{3,7},{4,0},{5,1},{6,2},{7,3},{8,12},{9,13},{10,... | collective-permute-start | bytes 393224 | tf_op jit(solution)/shard_map/ppermute | solution.py:25
  175.9 14.1 %collective-permute-start.46 = (bf16[32,2048]{1,0:T(8,128)(2,1)S(1)}, bf16[32,2048]{1,0:T(8,128)(2,1)S(1)}, u32[]{:S(2)}, u32[]{:S(2)}) collective-permute-start(bf16[32,2048]{1,0:T(8,128)(2,1)S(1)} %get-tuple-element.16), channel_id=1, source_target_pairs={{0,8},{1,9},{2,10},{3,11},{4,12},{5,13},{6,14},{7,15},{8,0},{9,1},... | collective-permute-start | bytes 393224 | tf_op jit(solution)/shard_map/ppermute | solution.py:25
  176.7 13.3 %collective-permute-start.47 = (bf16[32,2048]{1,0:T(8,128)(2,1)S(1)}, bf16[32,2048]{1,0:T(8,128)(2,1)S(1)}, u32[]{:S(2)}, u32[]{:S(2)}) collective-permute-start(bf16[32,2048]{1,0:T(8,128)(2,1)S(1)} %get-tuple-element.16), channel_id=1, source_target_pairs={{0,12},{1,13},{2,14},{3,15},{4,8},{5,9},{6,10},{7,11},{8,4},{9,5},... | collective-permute-start | bytes 393224 | tf_op jit(solution)/shard_map/ppermute | solution.py:25
  178.5 11.3 %collective-permute-start.22 = (bf16[128,2048]{1,0:T(8,128)(2,1)S(1)}, bf16[128,2048]{1,0:T(8,128)(2,1)S(1)}, u32[]{:S(2)}, u32[]{:S(2)}) collective-permute-start(bf16[128,2048]{1,0:T(8,128)(2,1)S(1)} %pad_maximum_fusion.2), channel_id=1, source_target_pairs={{0,2},{1,3},{2,0},{3,1},{4,6},{5,7},{6,4},{7,5},{8,10},{9,11},{10,... | collective-permute-start | bytes 1572872 | tf_op jit(solution)/shard_map/ppermute | solution.py:28
  189.9 14.7 %collective-permute-start.23 = (bf16[256,2048]{1,0:T(8,128)(2,1)S(1)}, bf16[256,2048]{1,0:T(8,128)(2,1)S(1)}, u32[]{:S(2)}, u32[]{:S(2)}) collective-permute-start(bf16[256,2048]{1,0:T(8,128)(2,1)S(1)} %get-tuple-element.26), channel_id=1, source_target_pairs={{0,1},{1,0},{2,3},{3,2},{4,5},{5,4},{6,7},{7,6},{8,9},{9,8},{10,11... | collective-permute-start | bytes 3145736 | tf_op jit(solution)/shard_map/ppermute | solution.py:28
  190.1 14.4 %collective-permute-start.48 = (bf16[128,2048]{1,0:T(8,128)(2,1)S(1)}, bf16[128,2048]{1,0:T(8,128)(2,1)S(1)}, u32[]{:S(2)}, u32[]{:S(2)}) collective-permute-start(bf16[128,2048]{1,0:T(8,128)(2,1)S(1)} %pad_maximum_fusion.3), channel_id=1, source_target_pairs={{0,2},{1,3},{2,0},{3,1},{4,6},{5,7},{6,4},{7,5},{8,10},{9,11},{10,... | collective-permute-start | bytes 1572872 | tf_op jit(solution)/shard_map/ppermute | solution.py:28
  213.5 14.8 %collective-permute-start.25 = (bf16[128,2048]{1,0:T(8,128)(2,1)S(1)}, bf16[128,2048]{1,0:T(8,128)(2,1)S(1)}, u32[]{:S(2)}, u32[]{:S(2)}) collective-permute-start(bf16[128,2048]{1,0:T(8,128)(2,1)S(1)} %slice.230), channel_id=1, source_target_pairs={{0,2},{1,3},{2,0},{3,1},{4,6},{5,7},{6,4},{7,5},{8,10},{9,11},{10,... | collective-permute-start | bytes 1572872 | tf_op jit(solution)/shard_map/ppermute | solution.py:28
  216.2 23.6 %collective-permute-start.51 = (bf16[128,2048]{1,0:T(8,128)(2,1)S(1)}, bf16[128,2048]{1,0:T(8,128)(2,1)S(1)}, u32[]{:S(2)}, u32[]{:S(2)}) collective-permute-start(bf16[128,2048]{1,0:T(8,128)(2,1)S(1)} %slice.249), channel_id=1, source_target_pairs={{0,2},{1,3},{2,0},{3,1},{4,6},{5,7},{6,4},{7,5},{8,10},{9,11},{10,... | collective-permute-start | bytes 1572872 | tf_op jit(solution)/shard_map/ppermute | solution.py:28
  228.5 20.8 %collective-permute-start.26 = (bf16[32,2048]{1,0:T(8,128)(2,1)S(1)}, bf16[32,2048]{1,0:T(8,128)(2,1)S(1)}, u32[]{:S(2)}, u32[]{:S(2)}) collective-permute-start(bf16[32,2048]{1,0:T(8,128)(2,1)S(1)} %get-tuple-element.23), channel_id=1, source_target_pairs={{0,4},{1,5},{2,6},{3,7},{4,0},{5,1},{6,2},{7,3},{8,12},{9,13},{10,... | collective-permute-start | bytes 393224 | tf_op jit(solution)/shard_map/ppermute | solution.py:25
  235.0 15.7 %collective-permute-start.27 = (bf16[32,2048]{1,0:T(8,128)(2,1)S(1)}, bf16[32,2048]{1,0:T(8,128)(2,1)S(1)}, u32[]{:S(2)}, u32[]{:S(2)}) collective-permute-start(bf16[32,2048]{1,0:T(8,128)(2,1)S(1)} %get-tuple-element.25), channel_id=1, source_target_pairs={{0,8},{1,9},{2,10},{3,11},{4,12},{5,13},{6,14},{7,15},{8,0},{9,1},... | collective-permute-start | bytes 393224 | tf_op jit(solution)/shard_map/ppermute | solution.py:25
  238.4 12.2 %collective-permute-start.28 = (bf16[32,2048]{1,0:T(8,128)(2,1)S(1)}, bf16[32,2048]{1,0:T(8,128)(2,1)S(1)}, u32[]{:S(2)}, u32[]{:S(2)}) collective-permute-start(bf16[32,2048]{1,0:T(8,128)(2,1)S(1)} %get-tuple-element.24), channel_id=1, source_target_pairs={{0,12},{1,13},{2,14},{3,15},{4,8},{5,9},{6,10},{7,11},{8,4},{9,5},... | collective-permute-start | bytes 393224 | tf_op jit(solution)/shard_map/ppermute | solution.py:25
  240.0 13.4 %collective-permute-start.52 = (bf16[32,2048]{1,0:T(8,128)(2,1)S(1)}, bf16[32,2048]{1,0:T(8,128)(2,1)S(1)}, u32[]{:S(2)}, u32[]{:S(2)}) collective-permute-start(bf16[32,2048]{1,0:T(8,128)(2,1)S(1)} %get-tuple-element.34), channel_id=1, source_target_pairs={{0,4},{1,5},{2,6},{3,7},{4,0},{5,1},{6,2},{7,3},{8,12},{9,13},{10,... | collective-permute-start | bytes 393224 | tf_op jit(solution)/shard_map/ppermute | solution.py:25
  245.8 7.6 %collective-permute-start.53 = (bf16[32,2048]{1,0:T(8,128)(2,1)S(1)}, bf16[32,2048]{1,0:T(8,128)(2,1)S(1)}, u32[]{:S(2)}, u32[]{:S(2)}) collective-permute-start(bf16[32,2048]{1,0:T(8,128)(2,1)S(1)} %get-tuple-element.36), channel_id=1, source_target_pairs={{0,8},{1,9},{2,10},{3,11},{4,12},{5,13},{6,14},{7,15},{8,0},{9,1},... | collective-permute-start | bytes 393224 | tf_op jit(solution)/shard_map/ppermute | solution.py:25
  249.3 10.2 %collective-permute-start.54 = (bf16[32,2048]{1,0:T(8,128)(2,1)S(1)}, bf16[32,2048]{1,0:T(8,128)(2,1)S(1)}, u32[]{:S(2)}, u32[]{:S(2)}) collective-permute-start(bf16[32,2048]{1,0:T(8,128)(2,1)S(1)} %get-tuple-element.35), channel_id=1, source_target_pairs={{0,12},{1,13},{2,14},{3,15},{4,8},{5,9},{6,10},{7,11},{8,4},{9,5},... | collective-permute-start | bytes 393224 | tf_op jit(solution)/shard_map/ppermute | solution.py:25
  (19 other events, 257.7 us)

commit v7 on v6

v7 whole, which is shorter than its diff:
```python
import jax
import jax.numpy as jnp
from jax import lax
from jax.sharding import PartitionSpec as P

EPSILON = 1e-06
PLANES = 4


class Ring:
    def __init__(self):
        self.size = lax.axis_size("inner")
        self.plane = self.size // PLANES
        self.me = lax.axis_index("inner")
        self.z = self.me // self.plane
        self.inside = (self.z == 1) | (self.z == 2)
        self.bits = []
        bit = self.plane // 2
        while bit:
            self.bits.append(bit)
            bit //= 2

    def send(self, values, pairs):
        perm = [(a * self.plane + i, b * self.plane + i) for a, b in pairs for i in range(self.plane)]
        return lax.ppermute(values, "inner", perm)

    def between(self, values, slot):
        return self.send(values, [(p, p ^ slot) for p in range(PLANES)]) if slot else values

    def across(self, values, bit):
        return lax.ppermute(values, "inner", [(d, d ^ bit) for d in range(self.size)])

    def high(self, bit):
        return (self.me // bit) % 2 == 1


def after(values, *others):
    return lax.optimization_barrier((values, *others))[0]


def add(*terms):
    return sum(t.astype(jnp.float32) for t in terms).astype(jnp.bfloat16)


def within_plane(ring, chunk):
    for bit in reversed(ring.bits[1:]):
        rows = chunk.shape[0] // 2
        chunk = add(chunk[:rows], ring.across(chunk[rows:], bit))
    return chunk


def plane_sums(ring, part):
    return sum(ring.between(part(slot), slot).astype(jnp.float32) for slot in (0, 3, 2, 1))


def gate_lanes(layers):
    lanes = []
    for routes, gates in layers:
        high = gates.astype(jnp.bfloat16)
        lanes += [routes.astype(jnp.bfloat16), high, (gates - high.astype(jnp.float32)).astype(jnp.bfloat16)]
    lanes = jnp.concatenate(lanes, axis=1)
    return jnp.pad(lanes, ((0, 0), (0, -lanes.shape[1] % 128)))


def gate_column(ring, lanes, layer, top):
    named, high, low = (lanes[:, (3 * layer + i) * top :][:, :top].astype(jnp.float32) for i in range(3))
    return jnp.sum(jnp.where(named == ring.me.astype(jnp.float32), high + low, 0.0), axis=1, keepdims=True)


def normed(values, gain):
    widened = values.astype(jnp.float32)
    inverse = lax.rsqrt(jnp.mean(widened * widened, axis=-1, keepdims=True) + EPSILON)
    return (widened * inverse * gain).astype(jnp.bfloat16)


def expert(rows, gates, gate_up, down):
    width = down.shape[0]
    projected = jnp.dot(rows, gate_up, preferred_element_type=jnp.float32)
    hidden = (jax.nn.silu(projected[:, :width]) * projected[:, width:]).astype(jnp.bfloat16)
    out = jnp.dot(hidden, down, preferred_element_type=jnp.float32)
    return (out * gates).astype(jnp.bfloat16)


def routed(ring, rows, work):
    top = ring.bits[0]
    columns = {0: rows, 1: ring.between(rows, 1)}
    crossed = {0: ring.across(rows, top)}
    middle = ring.send(rows, [(1, 2), (2, 1)])
    ends = ring.send(rows, [(0, 3), (3, 0)])
    near = ring.send(middle, [(1, 0), (2, 3)])
    far = ring.send(columns[1], [(1, 2), (2, 1)])
    columns[3] = jnp.where(ring.inside, middle, ends)
    columns[2] = jnp.where(ring.inside, far, near)
    crossed[1] = ring.across(after(columns[1], middle), top)
    crossed[3] = ring.across(columns[3], top)
    crossed[2] = ring.across(columns[2], top)

    done = {}
    halves = {}
    last = [columns[2], crossed[1], crossed[3]]
    for slot in (0, 1, 3, 2):
        chunk = jnp.concatenate([columns[slot], crossed[slot]], axis=0)
        if slot == 2:
            chunk = after(chunk, *last)
            halves[3] = within_plane(ring, done[3])
            last = [halves[3]]
        for bit in ring.bits[1:]:
            chunk = jnp.concatenate([chunk, ring.across(chunk, bit)], axis=0)
        done[slot] = work(slot, after(chunk, *last))
        last = [done[slot]]
    for slot in (2, 1, 0):
        halves[slot] = within_plane(ring, done[slot])

    own = rows.shape[0]
    back = {}
    for slot, ties in ((3, []), (2, []), (1, [3]), (0, [2])):
        away = after(halves[slot][own:], *[back[t] for t in ties], *([halves[2]] if ties else []))
        back[slot] = ring.across(away, top)
    sums = plane_sums(ring, lambda slot: add(halves[slot][:own], back[slot]))
    return sums, [crossed[1], crossed[2], back[2]]


def other_half(ring, weight, groups, ties):
    top = ring.bits[0]
    rows = weight.shape[0] // 2
    odd = lax.axis_index("groups") % 2
    pieces = []
    for piece, (begin, swap) in enumerate(ties):
        if groups % 2:
            pieces.append(ring.across(after(weight[piece * rows : (piece + 1) * rows], *begin), top))
            continue
        sent = lax.dynamic_slice_in_dim(weight, piece * rows + odd * (rows // 2), rows // 2, axis=0)
        here = after(ring.across(after(sent, *begin), top), *swap)
        there = lax.ppermute(here, "groups", [(g, g ^ 1) for g in range(groups)])
        pieces += [jnp.where(odd == 0, here, there), jnp.where(odd == 0, there, here)]
    return jnp.concatenate(pieces, axis=0)


def plane_weight(ring, weight, other):
    held = jnp.where(ring.high(ring.bits[0]), jnp.stack([other, weight]), jnp.stack([weight, other]))
    for i, bit in enumerate(ring.bits[1:]):
        other = ring.across(held, bit)
        axis = i + 1
        held = jnp.where(ring.high(bit), jnp.stack([other, held], axis), jnp.stack([held, other], axis))
    return held.reshape(ring.plane * weight.shape[0], weight.shape[1])


def merge(ring, merged_in, weight):
    share = merged_in.shape[1] // PLANES
    products = {}
    for slot in (2, 3, 1, 0):
        piece = lax.dynamic_slice_in_dim(merged_in, (ring.z ^ slot) * share, share, axis=1)
        products[slot] = jnp.dot(ring.between(piece, slot), weight, preferred_element_type=jnp.float32)
        if slot:
            products[slot] = products[slot].astype(jnp.bfloat16)
    return plane_sums(ring, lambda slot: products[slot])


def local(
    hidden_rows,
    token_embed,
    first_routes,
    first_gates,
    first_gate_up,
    first_down,
    second_routes,
    second_gates,
    second_gate_up,
    second_down,
    hidden_gain,
    embed_gain,
    merge_weight,
):
    ring = Ring()
    width = hidden_rows.shape[1]
    lanes = gate_lanes([(first_routes, first_gates), (second_routes, second_gates)])
    top = first_routes.shape[1]
    second_columns = {}

    def first_work(slot, chunk):
        second_columns[slot] = gate_column(ring, chunk[:, width:], 1, top)
        gates = gate_column(ring, chunk[:, width:], 0, top)
        return expert(chunk[:, :width], gates, first_gate_up[0], first_down[0])

    def second_work(slot, chunk):
        return expert(chunk, second_columns[slot], second_gate_up[0], second_down[0])

    first, steps = routed(ring, jnp.concatenate([hidden_rows, lanes], axis=1), first_work)
    ties = [([], [steps[0]]), ([steps[1]], [steps[2]])]
    weight = plane_weight(ring, merge_weight, other_half(ring, merge_weight, lax.axis_size("groups"), ties))
    after_first = (hidden_rows.astype(jnp.float32) + first).astype(jnp.bfloat16)
    merged_in = jnp.concatenate([normed(after_first, hidden_gain), normed(token_embed, embed_gain)], axis=1)
    merged = merge(ring, merged_in, weight)
    after_merge = (after_first.astype(jnp.float32) + jax.nn.silu(merged)).astype(jnp.bfloat16)
    second, _ = routed(ring, after_merge, second_work)
    return (after_merge.astype(jnp.float32) + second).astype(jnp.bfloat16)


def solution(mesh):
    rows = P(("groups", "inner"), None)
    weight = P("inner", None, None)
    return jax.shard_map(
        local,
        mesh=mesh,
        in_specs=(rows, rows, rows, rows, weight, weight, rows, rows, weight, weight, P(), P(), P("inner", None)),
        out_specs=rows,
        check_vma=False,
    )
```

time: 261 us -> 210 us (0.80)
  starting transfers between devices: 99.6 us -> 59.4 us
  local copies, waits for them, and re-layouts: 13.8 us -> 3.48 us
  waiting for transfers between devices: 110 us -> 105 us
  matrix products: 16.1 us -> 19.5 us
    ppermute x37 -> x24, starting transfers between devices: 85.1 us -> 34.3 us  [the longest x22 31.3 us: send(): return lax.ppermute(values, 'inner', perm)]
    ppermute x18 -> x35, waiting for transfers between devices: 68.6 us -> 32.9 us  [across(): lax.ppermute(values, 'inner', [(d, d ^ bit) for d in range(self.size)])]
    ppermute x37 -> x24, waiting for transfers between devices: 41.6 us -> 71.6 us  [the longest x22 67.2 us: send(): return lax.ppermute(values, 'inner', perm)]
    ppermute x18 -> x35, starting transfers between devices: 14.5 us -> 25.2 us  [across(): lax.ppermute(values, 'inner', [(d, d ^ bit) for d in range(self.size)])]
    unnamed x38 -> x23, local copies, waits for them, and re-layouts: 7.82 us -> 0.45 us
    select_n x3 -> x8, other arithmetic: 0.94 us -> 4.29 us  [the longest x2 2.18 us: plane_weight(): jnp.where(ring.high(ring.bits[0]), jnp.stack([other, weight]), jnp.stack(...]
    slice x12 -> x16, local copies, waits for them, and re-layouts: 3.85 us -> 1.16 us  [the longest x8 0.84 us: routed(): halves[slot][own:]]
    unnamed x9 -> x5, other arithmetic: 6.13 us -> 3.7 us
  transfers between devices with their start and end apart: 55 -> 59, of which waited for: 15 -> 23; matrix products, arithmetic and copies ran while one was open for 14% -> 18% of each run, Pallas kernels for 0% -> 0%
where the time goes in v7:
time: 210 us; the launch traced here: 209 us
  waiting for transfers between devices  105 us (50%)
  starting transfers between devices  59.4 us (28%)
  other arithmetic  21.2 us (10%)
  matrix products  19.5 us (9%)
  local copies, waits for them, and re-layouts  3.48 us (2%)
    ppermute x22, waiting for transfers between devices, send(): return lax.ppermute(values, 'inner', perm)  67.2 us
    ppermute x35, waiting for transfers between devices, across(): lax.ppermute(values, 'inner', [(d, d ^ bit) for d in range(self.size)])  32.9 us
    ppermute x22, starting transfers between devices, send(): return lax.ppermute(values, 'inner', perm)  31.3 us
    ppermute x35, starting transfers between devices, across(): lax.ppermute(values, 'inner', [(d, d ^ bit) for d in range(self.size)])  25.2 us
    dot_general x8, matrix products, expert(): projected = jnp.dot(rows, gate_up, preferred_element_type=jnp.float32)  10.1 us
    dot_general x8, matrix products, expert(): out = jnp.dot(hidden, down, preferred_element_type=jnp.float32)  6.08 us
    ppermute x2, waiting for transfers between devices, other_half(): there = lax.ppermute(here, 'groups', [(g, g ^ 1) for g in range(groups)])  4.42 us
  transfers between devices with their start and end apart: 59, of which 23 were waited for; matrix products, arithmetic and copies ran while one was open for 18% of the time, Pallas kernels for 0%

profile of v7, /device:TPU:0, one launch (start us, length us, event | category | flops | bytes accessed | tf_op | source)
XLA Modules:
  0.0 209.2 jit_solution(6566793303519065074)
XLA Ops:
  5.6 3.1 %collective-permute-start.2 = (bf16[64,2176]{1,0:T(8,128)(2,1)S(1)}, bf16[64,2176]{1,0:T(8,128)(2,1)S(1)}, u32[]{:S(2)}, u32[]{:S(2)}) collective-permute-start(bf16[64,2176]{1,0:T(8,128)(2,1)S(1)} %pad_maximum_fusion.17), channel_id=1, source_target_pairs={{0,4},{1,5},{2,6},{3,7},{4,0},{5,1},{6,2},{7,3},{8,12},{9,13},{10,... | collective-permute-start | bytes 835592 | tf_op jit(solution)/shard_map/ppermute | solution.py:25
  9.3 4.4 %collective-permute-start.7 = (bf16[64,2176]{1,0:T(8,128)(2,1)S(1)}, bf16[64,2176]{1,0:T(8,128)(2,1)}, u32[]{:S(2)}, u32[]{:S(2)}) collective-permute-start(bf16[64,2176]{1,0:T(8,128)(2,1)S(1)} %pad_maximum_fusion.17), channel_id=1, source_target_pairs={{0,12},{1,13},{2,14},{3,15},{12,0},{13,1},{14,2},{15,3},{16,28},{1... | collective-permute-start | bytes 835592 | tf_op jit(solution)/shard_map/ppermute | solution.py:25
  13.7 1.6 collective-permute-start
  15.3 1.9 constant_dynamic-slice_fusion.1
  17.7 1.5 collective-permute-start.6
  19.2 4.5 %collective-permute-done.7 = bf16[64,2176]{1,0:T(8,128)(2,1)} collective-permute-done((bf16[64,2176]{1,0:T(8,128)(2,1)S(1)}, bf16[64,2176]{1,0:T(8,128)(2,1)}, u32[]{:S(2)}, u32[]{:S(2)}) %collective-permute-start.7) | collective-permute-done | bytes 278560 | tf_op jit(solution)/shard_map/ppermute | solution.py:25
  24.7 1.6 collective-permute-start.8
  26.9 1.3 collective-permute-start.5
  28.4 9.4 %collective-permute-done.5 = bf16[64,2176]{1,0:T(8,128)(2,1)S(1)} collective-permute-done((bf16[64,2176]{1,0:T(8,128)(2,1)S(1)}, bf16[64,2176]{1,0:T(8,128)(2,1)S(1)}, u32[]{:S(2)}, u32[]{:S(2)}) %collective-permute-start.5) | collective-permute-done | bytes 278560 | tf_op jit(solution)/shard_map/ppermute | solution.py:25
  37.9 1.6 collective-permute-start.10
  39.5 1.5 collective-permute-start.25
  46.9 1.2 fusion.10
  55.8 1.5 collective-permute-start.18
  58.2 6.8 %collective-permute-done.18 = bf16[64,2048]{1,0:T(8,128)(2,1)S(1)} collective-permute-done((bf16[64,2048]{1,0:T(8,128)(2,1)S(1)}, bf16[64,2048]{1,0:T(8,128)(2,1)S(1)}, u32[]{:S(2)}, u32[]{:S(2)}) %collective-permute-start.18) | collective-permute-done | bytes 262176 | tf_op jit(solution)/shard_map/ppermute | solution.py:31
  65.1 1.5 collective-permute-start.19
  66.5 1.5 collective-permute-start.22
  68.0 2.6 %collective-permute-done.16 = bf16[64,2048]{1,0:T(8,128)(2,1)S(1)} collective-permute-done((bf16[64,2048]{1,0:T(8,128)(2,1)S(1)}, bf16[64,2048]{1,0:T(8,128)(2,1)S(1)}, u32[]{:S(2)}, u32[]{:S(2)}) %collective-permute-start.16) | collective-permute-done | bytes 262176 | tf_op jit(solution)/shard_map/ppermute | solution.py:31
  70.6 1.5 collective-permute-start.27
  73.8 4.4 %collective-permute-done.27 = bf16[64,2048]{1,0:T(8,128)(2,1)S(1)} collective-permute-done((bf16[64,2048]{1,0:T(8,128)(2,1)S(1)}, bf16[64,2048]{1,0:T(8,128)(2,1)S(1)}, u32[]{:S(2)}, u32[]{:S(2)}) %collective-permute-start.27) | collective-permute-done | bytes 262176 | tf_op jit(solution)/shard_map/ppermute | solution.py:134
  78.6 1.7 maximum_select_fusion.1
  81.3 7.5 %collective-permute-done.20 = bf16[64,2048]{1,0:T(8,128)(2,1)} collective-permute-done((bf16[64,2048]{1,0:T(8,128)(2,1)}, bf16[64,2048]{1,0:T(8,128)(2,1)}, u32[]{:S(2)}, u32[]{:S(2)}) %collective-permute-start.20) | collective-permute-done | bytes 262176 | tf_op jit(solution)/shard_map/ppermute | solution.py:25
  88.7 5.2 %collective-permute-done.23 = bf16[64,2048]{1,0:T(8,128)(2,1)} collective-permute-done((bf16[64,2048]{1,0:T(8,128)(2,1)}, bf16[64,2048]{1,0:T(8,128)(2,1)}, u32[]{:S(2)}, u32[]{:S(2)}) %collective-permute-start.23) | collective-permute-done | bytes 262176 | tf_op jit(solution)/shard_map/ppermute | solution.py:25
  93.9 1.5 fusion.39
  95.9 2.3 %collective-permute-start.29 = (bf16[64,1024]{1,0:T(8,128)(2,1)S(1)}, bf16[64,1024]{1,0:T(8,128)(2,1)S(1)}, u32[]{:S(2)}, u32[]{:S(2)}) collective-permute-start(bf16[64,1024]{1,0:T(8,128)(2,1)S(1)} %get-tuple-element.57), channel_id=1, source_target_pairs={{0,12},{1,13},{2,14},{3,15},{4,8},{5,9},{6,10},{7,11},{8,4},{9,5},... | collective-permute-start | bytes 393224 | tf_op jit(solution)/shard_map/ppermute | solution.py:25
  98.2 2.1 %collective-permute-start.33 = (bf16[64,1024]{1,0:T(8,128)(2,1)S(1)}, bf16[64,1024]{1,0:T(8,128)(2,1)S(1)}, u32[]{:S(2)}, u32[]{:S(2)}) collective-permute-start(bf16[64,1024]{1,0:T(8,128)(2,1)S(1)} %get-tuple-element.59), channel_id=1, source_target_pairs={{0,4},{1,5},{2,6},{3,7},{4,0},{5,1},{6,2},{7,3},{8,12},{9,13},{10,... | collective-permute-start | bytes 393224 | tf_op jit(solution)/shard_map/ppermute | solution.py:25
  100.9 2.8 %maximum_select_fusion = bf16[2,2,256,2048]{3,2,1,0:T(8,128)(2,1)S(1)} fusion(bf16[2,1,256,2048]{3,2,1,0:T(8,128)(2,1)S(1)} %maximum_select_fusion.2, bf16[2,1,256,2048]{3,2,1,0:T(8,128)(2,1)} %bitcast.4, pred[]{:T(512)S(6)} %eq.63), kind=kLoop, calls=%fused_computation | loop fusion | flops 6291456 | bytes 8388609 | tf_op jit(solution)/shard_map/jit(_where)/select_n | solution.py:144
  105.1 2.3 %collective-permute-start.30 = (bf16[64,2048]{1,0:T(8,128)(2,1)S(1)}, bf16[64,2048]{1,0:T(8,128)(2,1)S(1)}, u32[]{:S(2)}, u32[]{:S(2)}) collective-permute-start(bf16[64,2048]{1,0:T(8,128)(2,1)S(1)} %convolution_convert_fusion.2), channel_id=1, source_target_pairs={{0,12},{1,13},{2,14},{3,15},{4,8},{5,9},{6,10},{7,11},{8,4},{9,5},... | collective-permute-start | bytes 786440 | tf_op jit(solution)/shard_map/ppermute | solution.py:25
  107.4 1.9 collective-permute-done.31
  111.2 2.9 %collective-permute-start.34 = (bf16[64,2048]{1,0:T(8,128)(2,1)S(1)}, bf16[64,2048]{1,0:T(8,128)(2,1)S(1)}, u32[]{:S(2)}, u32[]{:S(2)}) collective-permute-start(bf16[64,2048]{1,0:T(8,128)(2,1)S(1)} %convolution_convert_fusion), channel_id=1, source_target_pairs={{0,4},{1,5},{2,6},{3,7},{4,0},{5,1},{6,2},{7,3},{8,12},{9,13},{10,... | collective-permute-start | bytes 786440 | tf_op jit(solution)/shard_map/ppermute | solution.py:25
  115.5 15.6 %collective-permute-done.32 = bf16[64,2048]{1,0:T(8,128)(2,1)S(1)} collective-permute-done((bf16[64,2048]{1,0:T(8,128)(2,1)S(1)}, bf16[64,2048]{1,0:T(8,128)(2,1)S(1)}, u32[]{:S(2)}, u32[]{:S(2)}) %collective-permute-start.32) | collective-permute-done | bytes 262176 | tf_op jit(solution)/shard_map/ppermute | solution.py:25
  132.1 1.4 collective-permute-start.37
  133.5 4.2 %collective-permute-start.42 = (bf16[64,2048]{1,0:T(8,128)(2,1)S(1)}, bf16[64,2048]{1,0:T(8,128)(2,1)S(1)}, u32[]{:S(2)}, u32[]{:S(2)}) collective-permute-start(bf16[64,2048]{1,0:T(8,128)(2,1)S(1)} %fusion.42), channel_id=1, source_target_pairs={{0,12},{1,13},{2,14},{3,15},{12,0},{13,1},{14,2},{15,3},{16,28},{1... | collective-permute-start | bytes 786440 | tf_op jit(solution)/shard_map/ppermute | solution.py:25
  138.7 1.3 collective-permute-start.40
  141.0 6.5 %collective-permute-done.42 = bf16[64,2048]{1,0:T(8,128)(2,1)S(1)} collective-permute-done((bf16[64,2048]{1,0:T(8,128)(2,1)S(1)}, bf16[64,2048]{1,0:T(8,128)(2,1)S(1)}, u32[]{:S(2)}, u32[]{:S(2)}) %collective-permute-start.42) | collective-permute-done | bytes 262176 | tf_op jit(solution)/shard_map/ppermute | solution.py:25
  149.8 2.8 %collective-permute-done.40 = bf16[64,2048]{1,0:T(8,128)(2,1)S(1)} collective-permute-done((bf16[64,2048]{1,0:T(8,128)(2,1)S(1)}, bf16[64,2048]{1,0:T(8,128)(2,1)S(1)}, u32[]{:S(2)}, u32[]{:S(2)}) %collective-permute-start.40) | collective-permute-done | bytes 262176 | tf_op jit(solution)/shard_map/ppermute | solution.py:25
  153.7 3.2 %collective-permute-done.43 = bf16[64,2048]{1,0:T(8,128)(2,1)S(1)} collective-permute-done((bf16[64,2048]{1,0:T(8,128)(2,1)S(1)}, bf16[64,2048]{1,0:T(8,128)(2,1)S(1)}, u32[]{:S(2)}, u32[]{:S(2)}) %collective-permute-start.43) | collective-permute-done | bytes 262176 | tf_op jit(solution)/shard_map/ppermute | solution.py:31
  157.0 5.5 %collective-permute-done.41 = bf16[64,2048]{1,0:T(8,128)(2,1)S(1)} collective-permute-done((bf16[64,2048]{1,0:T(8,128)(2,1)S(1)}, bf16[64,2048]{1,0:T(8,128)(2,1)S(1)}, u32[]{:S(2)}, u32[]{:S(2)}) %collective-permute-start.41) | collective-permute-done | bytes 262176 | tf_op jit(solution)/shard_map/ppermute | solution.py:31
  162.7 1.3 fusion.6
  165.2 1.3 fusion.4
  167.4 1.3 fusion.2
  172.4 1.3 fusion
  177.8 6.8 %collective-permute-done.53 = bf16[64,2048]{1,0:T(8,128)(2,1)S(1)} collective-permute-done((bf16[64,2048]{1,0:T(8,128)(2,1)S(1)}, bf16[64,2048]{1,0:T(8,128)(2,1)S(1)}, u32[]{:S(2)}, u32[]{:S(2)}) %collective-permute-start.53) | collective-permute-done | bytes 262176 | tf_op jit(solution)/shard_map/ppermute | solution.py:31
  184.6 1.6 collective-permute-start.54
  186.2 1.6 collective-permute-start.57
  187.9 2.3 %collective-permute-done.51 = bf16[64,2048]{1,0:T(8,128)(2,1)S(1)} collective-permute-done((bf16[64,2048]{1,0:T(8,128)(2,1)S(1)}, bf16[64,2048]{1,0:T(8,128)(2,1)S(1)}, u32[]{:S(2)}, u32[]{:S(2)}) %collective-permute-start.51) | collective-permute-done | bytes 262176 | tf_op jit(solution)/shard_map/ppermute | solution.py:31
  191.4 4.4 %collective-permute-done.57 = bf16[64,2048]{1,0:T(8,128)(2,1)S(1)} collective-permute-done((bf16[64,2048]{1,0:T(8,128)(2,1)S(1)}, bf16[64,2048]{1,0:T(8,128)(2,1)S(1)}, u32[]{:S(2)}, u32[]{:S(2)}) %collective-permute-start.57) | collective-permute-done | bytes 262176 | tf_op jit(solution)/shard_map/ppermute | solution.py:31
  196.0 9.7 %collective-permute-done.55 = bf16[64,2048]{1,0:T(8,128)(2,1)S(1)} collective-permute-done((bf16[64,2048]{1,0:T(8,128)(2,1)S(1)}, bf16[64,2048]{1,0:T(8,128)(2,1)S(1)}, u32[]{:S(2)}, u32[]{:S(2)}) %collective-permute-start.55) | collective-permute-done | bytes 262176 | tf_op jit(solution)/shard_map/ppermute | solution.py:25
  205.6 2.6 %collective-permute-done.58 = bf16[64,2048]{1,0:T(8,128)(2,1)S(1)} collective-permute-done((bf16[64,2048]{1,0:T(8,128)(2,1)S(1)}, bf16[64,2048]{1,0:T(8,128)(2,1)S(1)}, u32[]{:S(2)}, u32[]{:S(2)}) %collective-permute-start.58) | collective-permute-done | bytes 262176 | tf_op jit(solution)/shard_map/ppermute | solution.py:25
  (190 shorter events, 50.3 us)
Async XLA Ops:
  5.6 12.1 %collective-permute-start.2 = (bf16[64,2176]{1,0:T(8,128)(2,1)S(1)}, bf16[64,2176]{1,0:T(8,128)(2,1)S(1)}, u32[]{:S(2)}, u32[]{:S(2)}) collective-permute-start(bf16[64,2176]{1,0:T(8,128)(2,1)S(1)} %pad_maximum_fusion.17), channel_id=1, source_target_pairs={{0,4},{1,5},{2,6},{3,7},{4,0},{5,1},{6,2},{7,3},{8,12},{9,13},{10,... | collective-permute-start | bytes 835592 | tf_op jit(solution)/shard_map/ppermute | solution.py:25
  8.7 9.0 %collective-permute-start.4 = (bf16[64,2176]{1,0:T(8,128)(2,1)S(1)}, bf16[64,2176]{1,0:T(8,128)(2,1)S(1)}, u32[]{:S(2)}, u32[]{:S(2)}) collective-permute-start(bf16[64,2176]{1,0:T(8,128)(2,1)S(1)} %pad_maximum_fusion.17), channel_id=1, source_target_pairs={{4,8},{5,9},{6,10},{7,11},{8,4},{9,5},{10,6},{11,7},{20,24},{21,25... | collective-permute-start | bytes 835592 | tf_op jit(solution)/shard_map/ppermute | solution.py:25
  9.3 14.3 %collective-permute-start.7 = (bf16[64,2176]{1,0:T(8,128)(2,1)S(1)}, bf16[64,2176]{1,0:T(8,128)(2,1)}, u32[]{:S(2)}, u32[]{:S(2)}) collective-permute-start(bf16[64,2176]{1,0:T(8,128)(2,1)S(1)} %pad_maximum_fusion.17), channel_id=1, source_target_pairs={{0,12},{1,13},{2,14},{3,15},{12,0},{13,1},{14,2},{15,3},{16,28},{1... | collective-permute-start | bytes 835592 | tf_op jit(solution)/shard_map/ppermute | solution.py:25
  13.7 13.2 %collective-permute-start = (bf16[64,2176]{1,0:T(8,128)(2,1)S(1)}, bf16[64,2176]{1,0:T(8,128)(2,1)S(1)}, u32[]{:S(2)}, u32[]{:S(2)}) collective-permute-start(bf16[64,2176]{1,0:T(8,128)(2,1)S(1)} %pad_maximum_fusion.17), channel_id=1, source_target_pairs={{0,2},{1,3},{2,0},{3,1},{4,6},{5,7},{6,4},{7,5},{8,10},{9,11},{10,... | collective-permute-start | bytes 835592 | tf_op jit(solution)/shard_map/ppermute | solution.py:31
  17.2 22.3 %collective-permute-start.24 = (bf16[64,2048]{1,0:T(8,128)(2,1)}, bf16[64,2048]{1,0:T(8,128)(2,1)}, u32[]{:S(2)}, u32[]{:S(2)}) collective-permute-start(bf16[64,2048]{1,0:T(8,128)(2,1)} %get-tuple-element.55), channel_id=1, source_target_pairs={{0,2},{1,3},{2,0},{3,1},{4,6},{5,7},{6,4},{7,5},{8,10},{9,11},{10,... | collective-permute-start | bytes 786440 | tf_op jit(solution)/shard_map/ppermute | solution.py:31
  17.7 21.8 %collective-permute-start.6 = (bf16[64,2176]{1,0:T(8,128)(2,1)S(1)}, bf16[64,2176]{1,0:T(8,128)(2,1)S(1)}, u32[]{:S(2)}, u32[]{:S(2)}) collective-permute-start(bf16[64,2176]{1,0:T(8,128)(2,1)S(1)} %collective-permute-done.2), channel_id=1, source_target_pairs={{0,2},{1,3},{2,0},{3,1},{4,6},{5,7},{6,4},{7,5},{8,10},{9,11},{10,... | collective-permute-start | bytes 835592 | tf_op jit(solution)/shard_map/ppermute | solution.py:31
  24.7 16.4 %collective-permute-start.8 = (bf16[64,2176]{1,0:T(8,128)(2,1)S(1)}, bf16[64,2176]{1,0:T(8,128)(2,1)S(1)}, u32[]{:S(2)}, u32[]{:S(2)}) collective-permute-start(bf16[64,2176]{1,0:T(8,128)(2,1)S(1)} %broadcast_select_fusion), channel_id=1, source_target_pairs={{0,2},{1,3},{2,0},{3,1},{4,6},{5,7},{6,4},{7,5},{8,10},{9,11},{10,... | collective-permute-start | bytes 835592 | tf_op jit(solution)/shard_map/ppermute | solution.py:31
  26.9 10.9 %collective-permute-start.5 = (bf16[64,2176]{1,0:T(8,128)(2,1)S(1)}, bf16[64,2176]{1,0:T(8,128)(2,1)S(1)}, u32[]{:S(2)}, u32[]{:S(2)}) collective-permute-start(bf16[64,2176]{1,0:T(8,128)(2,1)S(1)} %collective-permute-done.4), channel_id=1, source_target_pairs={{4,0},{5,1},{6,2},{7,3},{8,12},{9,13},{10,14},{11,15},{20,16},{21,... | collective-permute-start | bytes 835592 | tf_op jit(solution)/shard_map/ppermute | solution.py:25
  28.3 13.4 %collective-permute-start.1 = (bf16[128,2176]{1,0:T(8,128)(2,1)S(1)}, bf16[128,2176]{1,0:T(8,128)(2,1)S(1)}, u32[]{:S(2)}, u32[]{:S(2)}) collective-permute-start(bf16[128,2176]{1,0:T(8,128)(2,1)S(1)} %pad_maximum_fusion.9), channel_id=1, source_target_pairs={{0,1},{1,0},{2,3},{3,2},{4,5},{5,4},{6,7},{7,6},{8,9},{9,8},{10,11... | collective-permute-start | bytes 1671176 | tf_op jit(solution)/shard_map/ppermute | solution.py:31
  37.9 11.2 %collective-permute-start.10 = (bf16[64,2176]{1,0:T(8,128)(2,1)S(1)}, bf16[64,2176]{1,0:T(8,128)(2,1)S(1)}, u32[]{:S(2)}, u32[]{:S(2)}) collective-permute-start(bf16[64,2176]{1,0:T(8,128)(2,1)S(1)} %broadcast_select_fusion.1), channel_id=1, source_target_pairs={{0,2},{1,3},{2,0},{3,1},{4,6},{5,7},{6,4},{7,5},{8,10},{9,11},{10,... | collective-permute-start | bytes 835592 | tf_op jit(solution)/shard_map/ppermute | solution.py:31
  39.5 10.2 %collective-permute-start.25 = (bf16[64,2048]{1,0:T(8,128)(2,1)}, bf16[64,2048]{1,0:T(8,128)(2,1)S(1)}, u32[]{:S(2)}, u32[]{:S(2)}) collective-permute-start(bf16[64,2048]{1,0:T(8,128)(2,1)} %collective-permute-done.24), channel_id=1, source_target_pairs={{0,16},{16,0},{1,17},{17,1},{2,18},{18,2},{3,19},{19,3},{4,20},{20... | collective-permute-start | bytes 786440 | tf_op jit(solution)/shard_map/ppermute | solution.py:134
  41.2 5.4 %collective-permute-start.11 = (bf16[128,2176]{1,0:T(8,128)(2,1)S(1)}, bf16[128,2176]{1,0:T(8,128)(2,1)S(1)}, u32[]{:S(2)}, u32[]{:S(2)}) collective-permute-start(bf16[128,2176]{1,0:T(8,128)(2,1)S(1)} %pad_maximum_fusion.11), channel_id=1, source_target_pairs={{0,1},{1,0},{2,3},{3,2},{4,5},{5,4},{6,7},{7,6},{8,9},{9,8},{10,11... | collective-permute-start | bytes 1671176 | tf_op jit(solution)/shard_map/ppermute | solution.py:31
  50.7 17.3 %collective-permute-start.26 = (bf16[64,2048]{1,0:T(8,128)(2,1)S(1)}, bf16[64,2048]{1,0:T(8,128)(2,1)S(1)}, u32[]{:S(2)}, u32[]{:S(2)}) collective-permute-start(bf16[64,2048]{1,0:T(8,128)(2,1)S(1)} %copy-done.5), channel_id=1, source_target_pairs={{0,2},{1,3},{2,0},{3,1},{4,6},{5,7},{6,4},{7,5},{8,10},{9,11},{10,... | collective-permute-start | bytes 786440 | tf_op jit(solution)/shard_map/ppermute | solution.py:31
  55.8 9.2 %collective-permute-start.18 = (bf16[64,2048]{1,0:T(8,128)(2,1)S(1)}, bf16[64,2048]{1,0:T(8,128)(2,1)S(1)}, u32[]{:S(2)}, u32[]{:S(2)}) collective-permute-start(bf16[64,2048]{1,0:T(8,128)(2,1)S(1)} %slice.394), channel_id=1, source_target_pairs={{0,2},{1,3},{2,0},{3,1},{4,6},{5,7},{6,4},{7,5},{8,10},{9,11},{10,... | collective-permute-start | bytes 786440 | tf_op jit(solution)/shard_map/ppermute | solution.py:31
  57.4 13.2 %collective-permute-start.16 = (bf16[64,2048]{1,0:T(8,128)(2,1)S(1)}, bf16[64,2048]{1,0:T(8,128)(2,1)S(1)}, u32[]{:S(2)}, u32[]{:S(2)}) collective-permute-start(bf16[64,2048]{1,0:T(8,128)(2,1)S(1)} %slice.392), channel_id=1, source_target_pairs={{0,2},{1,3},{2,0},{3,1},{4,6},{5,7},{6,4},{7,5},{8,10},{9,11},{10,... | collective-permute-start | bytes 786440 | tf_op jit(solution)/shard_map/ppermute | solution.py:31
  65.1 16.2 %collective-permute-start.19 = (bf16[64,2048]{1,0:T(8,128)(2,1)S(1)}, bf16[64,2048]{1,0:T(8,128)(2,1)}, u32[]{:S(2)}, u32[]{:S(2)}) collective-permute-start(bf16[64,2048]{1,0:T(8,128)(2,1)S(1)} %add_convert_fusion.16), channel_id=1, source_target_pairs={{0,12},{1,13},{2,14},{3,15},{4,8},{5,9},{6,10},{7,11},{8,4},{9,5},... | collective-permute-start | bytes 786440 | tf_op jit(solution)/shard_map/ppermute | solution.py:25
  66.5 13.7 %collective-permute-start.22 = (bf16[64,2048]{1,0:T(8,128)(2,1)S(1)}, bf16[64,2048]{1,0:T(8,128)(2,1)S(1)}, u32[]{:S(2)}, u32[]{:S(2)}) collective-permute-start(bf16[64,2048]{1,0:T(8,128)(2,1)S(1)} %slice.399), channel_id=1, source_target_pairs={{0,2},{1,3},{2,0},{3,1},{4,6},{5,7},{6,4},{7,5},{8,10},{9,11},{10,... | collective-permute-start | bytes 786440 | tf_op jit(solution)/shard_map/ppermute | solution.py:31
  70.6 7.6 %collective-permute-start.27 = (bf16[64,2048]{1,0:T(8,128)(2,1)S(1)}, bf16[64,2048]{1,0:T(8,128)(2,1)S(1)}, u32[]{:S(2)}, u32[]{:S(2)}) collective-permute-start(bf16[64,2048]{1,0:T(8,128)(2,1)S(1)} %collective-permute-done.26), channel_id=1, source_target_pairs={{0,16},{16,0},{1,17},{17,1},{2,18},{18,2},{3,19},{19,3},{4,20},{20... | collective-permute-start | bytes 786440 | tf_op jit(solution)/shard_map/ppermute | solution.py:134
  72.8 15.9 %collective-permute-start.20 = (bf16[64,2048]{1,0:T(8,128)(2,1)}, bf16[64,2048]{1,0:T(8,128)(2,1)}, u32[]{:S(2)}, u32[]{:S(2)}) collective-permute-start(bf16[64,2048]{1,0:T(8,128)(2,1)} %add_convert_fusion.15), channel_id=1, source_target_pairs={{0,8},{1,9},{2,10},{3,11},{4,12},{5,13},{6,14},{7,15},{8,0},{9,1},... | collective-permute-start | bytes 786440 | tf_op jit(solution)/shard_map/ppermute | solution.py:25
  72.9 15.9 %collective-permute-start.17 = (bf16[64,2048]{1,0:T(8,128)(2,1)}, bf16[64,2048]{1,0:T(8,128)(2,1)}, u32[]{:S(2)}, u32[]{:S(2)}) collective-permute-start(bf16[64,2048]{1,0:T(8,128)(2,1)} %slice.381), channel_id=1, source_target_pairs={{0,2},{1,3},{2,0},{3,1},{4,6},{5,7},{6,4},{7,5},{8,10},{9,11},{10,... | collective-permute-start | bytes 786440 | tf_op jit(solution)/shard_map/ppermute | solution.py:31
  80.3 20.6 %collective-permute-start.28 = (bf16[2,256,2048]{2,1,0:T(8,128)(2,1)}, bf16[2,256,2048]{2,1,0:T(8,128)(2,1)}, u32[]{:S(2)}, u32[]{:S(2)}) collective-permute-start(bf16[2,256,2048]{2,1,0:T(8,128)(2,1)} %maximum_select_fusion.1), channel_id=1, source_target_pairs={{0,1},{1,0},{2,3},{3,2},{4,5},{5,4},{6,7},{7,6},{8,9},{9,8},{10,11... | collective-permute-start | bytes 6291464 | tf_op jit(solution)/shard_map/ppermute | solution.py:31
  81.0 12.9 %collective-permute-start.23 = (bf16[64,2048]{1,0:T(8,128)(2,1)}, bf16[64,2048]{1,0:T(8,128)(2,1)}, u32[]{:S(2)}, u32[]{:S(2)}) collective-permute-start(bf16[64,2048]{1,0:T(8,128)(2,1)} %add_convert_fusion.14), channel_id=1, source_target_pairs={{0,4},{1,5},{2,6},{3,7},{4,0},{5,1},{6,2},{7,3},{8,12},{9,13},{10,... | collective-permute-start | bytes 786440 | tf_op jit(solution)/shard_map/ppermute | solution.py:25
  95.9 8.3 %collective-permute-start.29 = (bf16[64,1024]{1,0:T(8,128)(2,1)S(1)}, bf16[64,1024]{1,0:T(8,128)(2,1)S(1)}, u32[]{:S(2)}, u32[]{:S(2)}) collective-permute-start(bf16[64,1024]{1,0:T(8,128)(2,1)S(1)} %get-tuple-element.57), channel_id=1, source_target_pairs={{0,12},{1,13},{2,14},{3,15},{4,8},{5,9},{6,10},{7,11},{8,4},{9,5},... | collective-permute-start | bytes 393224 | tf_op jit(solution)/shard_map/ppermute | solution.py:25
  98.2 11.1 %collective-permute-start.31 = (bf16[64,1024]{1,0:T(8,128)(2,1)S(1)}, bf16[64,1024]{1,0:T(8,128)(2,1)S(1)}, u32[]{:S(2)}, u32[]{:S(2)}) collective-permute-start(bf16[64,1024]{1,0:T(8,128)(2,1)S(1)} %get-tuple-element.58), channel_id=1, source_target_pairs={{0,8},{1,9},{2,10},{3,11},{4,12},{5,13},{6,14},{7,15},{8,0},{9,1},... | collective-permute-start | bytes 393224 | tf_op jit(solution)/shard_map/ppermute | solution.py:25
  98.2 12.1 %collective-permute-start.33 = (bf16[64,1024]{1,0:T(8,128)(2,1)S(1)}, bf16[64,1024]{1,0:T(8,128)(2,1)S(1)}, u32[]{:S(2)}, u32[]{:S(2)}) collective-permute-start(bf16[64,1024]{1,0:T(8,128)(2,1)S(1)} %get-tuple-element.59), channel_id=1, source_target_pairs={{0,4},{1,5},{2,6},{3,7},{4,0},{5,1},{6,2},{7,3},{8,12},{9,13},{10,... | collective-permute-start | bytes 393224 | tf_op jit(solution)/shard_map/ppermute | solution.py:25
  105.1 10.4 %collective-permute-start.30 = (bf16[64,2048]{1,0:T(8,128)(2,1)S(1)}, bf16[64,2048]{1,0:T(8,128)(2,1)S(1)}, u32[]{:S(2)}, u32[]{:S(2)}) collective-permute-start(bf16[64,2048]{1,0:T(8,128)(2,1)S(1)} %convolution_convert_fusion.2), channel_id=1, source_target_pairs={{0,12},{1,13},{2,14},{3,15},{4,8},{5,9},{6,10},{7,11},{8,4},{9,5},... | collective-permute-start | bytes 786440 | tf_op jit(solution)/shard_map/ppermute | solution.py:25
  110.2 20.9 %collective-permute-start.32 = (bf16[64,2048]{1,0:T(8,128)(2,1)S(1)}, bf16[64,2048]{1,0:T(8,128)(2,1)S(1)}, u32[]{:S(2)}, u32[]{:S(2)}) collective-permute-start(bf16[64,2048]{1,0:T(8,128)(2,1)S(1)} %convolution_convert_fusion.1), channel_id=1, source_target_pairs={{0,8},{1,9},{2,10},{3,11},{4,12},{5,13},{6,14},{7,15},{8,0},{9,1},... | collective-permute-start | bytes 786440 | tf_op jit(solution)/shard_map/ppermute | solution.py:25
  111.2 20.0 %collective-permute-start.34 = (bf16[64,2048]{1,0:T(8,128)(2,1)S(1)}, bf16[64,2048]{1,0:T(8,128)(2,1)S(1)}, u32[]{:S(2)}, u32[]{:S(2)}) collective-permute-start(bf16[64,2048]{1,0:T(8,128)(2,1)S(1)} %convolution_convert_fusion), channel_id=1, source_target_pairs={{0,4},{1,5},{2,6},{3,7},{4,0},{5,1},{6,2},{7,3},{8,12},{9,13},{10,... | collective-permute-start | bytes 786440 | tf_op jit(solution)/shard_map/ppermute | solution.py:25
  131.4 7.3 %collective-permute-start.39 = (bf16[64,2048]{1,0:T(8,128)(2,1)S(1)}, bf16[64,2048]{1,0:T(8,128)(2,1)S(1)}, u32[]{:S(2)}, u32[]{:S(2)}) collective-permute-start(bf16[64,2048]{1,0:T(8,128)(2,1)S(1)} %fusion.42), channel_id=1, source_target_pairs={{4,8},{5,9},{6,10},{7,11},{8,4},{9,5},{10,6},{11,7},{20,24},{21,25... | collective-permute-start | bytes 786440 | tf_op jit(solution)/shard_map/ppermute | solution.py:25
  132.1 8.3 %collective-permute-start.37 = (bf16[64,2048]{1,0:T(8,128)(2,1)S(1)}, bf16[64,2048]{1,0:T(8,128)(2,1)S(1)}, u32[]{:S(2)}, u32[]{:S(2)}) collective-permute-start(bf16[64,2048]{1,0:T(8,128)(2,1)S(1)} %fusion.42), channel_id=1, source_target_pairs={{0,4},{1,5},{2,6},{3,7},{4,0},{5,1},{6,2},{7,3},{8,12},{9,13},{10,... | collective-permute-start | bytes 786440 | tf_op jit(solution)/shard_map/ppermute | solution.py:25
  133.5 14.0 %collective-permute-start.42 = (bf16[64,2048]{1,0:T(8,128)(2,1)S(1)}, bf16[64,2048]{1,0:T(8,128)(2,1)S(1)}, u32[]{:S(2)}, u32[]{:S(2)}) collective-permute-start(bf16[64,2048]{1,0:T(8,128)(2,1)S(1)} %fusion.42), channel_id=1, source_target_pairs={{0,12},{1,13},{2,14},{3,15},{12,0},{13,1},{14,2},{15,3},{16,28},{1... | collective-permute-start | bytes 786440 | tf_op jit(solution)/shard_map/ppermute | solution.py:25
  137.7 12.0 %collective-permute-start.35 = (bf16[64,2048]{1,0:T(8,128)(2,1)S(1)}, bf16[64,2048]{1,0:T(8,128)(2,1)S(1)}, u32[]{:S(2)}, u32[]{:S(2)}) collective-permute-start(bf16[64,2048]{1,0:T(8,128)(2,1)S(1)} %fusion.42), channel_id=1, source_target_pairs={{0,2},{1,3},{2,0},{3,1},{4,6},{5,7},{6,4},{7,5},{8,10},{9,11},{10,... | collective-permute-start | bytes 786440 | tf_op jit(solution)/shard_map/ppermute | solution.py:31
  138.7 13.8 %collective-permute-start.40 = (bf16[64,2048]{1,0:T(8,128)(2,1)S(1)}, bf16[64,2048]{1,0:T(8,128)(2,1)S(1)}, u32[]{:S(2)}, u32[]{:S(2)}) collective-permute-start(bf16[64,2048]{1,0:T(8,128)(2,1)S(1)} %collective-permute-done.39), channel_id=1, source_target_pairs={{4,0},{5,1},{6,2},{7,3},{8,12},{9,13},{10,14},{11,15},{20,16},{21,... | collective-permute-start | bytes 786440 | tf_op jit(solution)/shard_map/ppermute | solution.py:25
  140.4 12.2 %collective-permute-start.38 = (bf16[64,2048]{1,0:T(8,128)(2,1)S(1)}, bf16[64,2048]{1,0:T(8,128)(2,1)S(1)}, u32[]{:S(2)}, u32[]{:S(2)}) collective-permute-start(bf16[64,2048]{1,0:T(8,128)(2,1)S(1)} %collective-permute-done.37), channel_id=1, source_target_pairs={{4,8},{5,9},{6,10},{7,11},{8,4},{9,5},{10,6},{11,7},{20,24},{21,25... | collective-permute-start | bytes 786440 | tf_op jit(solution)/shard_map/ppermute | solution.py:25
  147.5 9.3 %collective-permute-start.43 = (bf16[64,2048]{1,0:T(8,128)(2,1)S(1)}, bf16[64,2048]{1,0:T(8,128)(2,1)S(1)}, u32[]{:S(2)}, u32[]{:S(2)}) collective-permute-start(bf16[64,2048]{1,0:T(8,128)(2,1)S(1)} %broadcast_select_fusion.2), channel_id=1, source_target_pairs={{0,2},{1,3},{2,0},{3,1},{4,6},{5,7},{6,4},{7,5},{8,10},{9,11},{10,... | collective-permute-start | bytes 786440 | tf_op jit(solution)/shard_map/ppermute | solution.py:31
  148.6 13.9 %collective-permute-start.41 = (bf16[64,2048]{1,0:T(8,128)(2,1)S(1)}, bf16[64,2048]{1,0:T(8,128)(2,1)S(1)}, u32[]{:S(2)}, u32[]{:S(2)}) collective-permute-start(bf16[64,2048]{1,0:T(8,128)(2,1)S(1)} %collective-permute-done.37), channel_id=1, source_target_pairs={{0,2},{1,3},{2,0},{3,1},{4,6},{5,7},{6,4},{7,5},{8,10},{9,11},{10,... | collective-permute-start | bytes 786440 | tf_op jit(solution)/shard_map/ppermute | solution.py:31
  149.7 12.9 %collective-permute-start.36 = (bf16[128,2048]{1,0:T(8,128)(2,1)S(1)}, bf16[128,2048]{1,0:T(8,128)(2,1)S(1)}, u32[]{:S(2)}, u32[]{:S(2)}) collective-permute-start(bf16[128,2048]{1,0:T(8,128)(2,1)S(1)} %pad_maximum_fusion.13), channel_id=1, source_target_pairs={{0,1},{1,0},{2,3},{3,2},{4,5},{5,4},{6,7},{7,6},{8,9},{9,8},{10,11... | collective-permute-start | bytes 1572872 | tf_op jit(solution)/shard_map/ppermute | solution.py:31
  152.6 17.4 %collective-permute-start.45 = (bf16[64,2048]{1,0:T(8,128)(2,1)S(1)}, bf16[64,2048]{1,0:T(8,128)(2,1)S(1)}, u32[]{:S(2)}, u32[]{:S(2)}) collective-permute-start(bf16[64,2048]{1,0:T(8,128)(2,1)S(1)} %broadcast_select_fusion.3), channel_id=1, source_target_pairs={{0,2},{1,3},{2,0},{3,1},{4,6},{5,7},{6,4},{7,5},{8,10},{9,11},{10,... | collective-permute-start | bytes 786440 | tf_op jit(solution)/shard_map/ppermute | solution.py:31
  156.9 10.3 %collective-permute-start.46 = (bf16[128,2048]{1,0:T(8,128)(2,1)S(1)}, bf16[128,2048]{1,0:T(8,128)(2,1)S(1)}, u32[]{:S(2)}, u32[]{:S(2)}) collective-permute-start(bf16[128,2048]{1,0:T(8,128)(2,1)S(1)} %pad_maximum_fusion.15), channel_id=1, source_target_pairs={{0,1},{1,0},{2,3},{3,2},{4,5},{5,4},{6,7},{7,6},{8,9},{9,8},{10,11... | collective-permute-start | bytes 1572872 | tf_op jit(solution)/shard_map/ppermute | solution.py:31
  170.2 4.7 %collective-permute-start.44 = (bf16[128,2048]{1,0:T(8,128)(2,1)S(1)}, bf16[128,2048]{1,0:T(8,128)(2,1)S(1)}, u32[]{:S(2)}, u32[]{:S(2)}) collective-permute-start(bf16[128,2048]{1,0:T(8,128)(2,1)S(1)} %slice.403), channel_id=1, source_target_pairs={{0,1},{1,0},{2,3},{3,2},{4,5},{5,4},{6,7},{7,6},{8,9},{9,8},{10,11... | collective-permute-start | bytes 1572872 | tf_op jit(solution)/shard_map/ppermute | solution.py:31
  170.8 4.4 %collective-permute-start.56 = (bf16[128,2048]{1,0:T(8,128)(2,1)S(1)}, bf16[128,2048]{1,0:T(8,128)(2,1)S(1)}, u32[]{:S(2)}, u32[]{:S(2)}) collective-permute-start(bf16[128,2048]{1,0:T(8,128)(2,1)S(1)} %slice.421), channel_id=1, source_target_pairs={{0,1},{1,0},{2,3},{3,2},{4,5},{5,4},{6,7},{7,6},{8,9},{9,8},{10,11... | collective-permute-start | bytes 1572872 | tf_op jit(solution)/shard_map/ppermute | solution.py:31
  175.4 9.2 %collective-permute-start.53 = (bf16[64,2048]{1,0:T(8,128)(2,1)S(1)}, bf16[64,2048]{1,0:T(8,128)(2,1)S(1)}, u32[]{:S(2)}, u32[]{:S(2)}) collective-permute-start(bf16[64,2048]{1,0:T(8,128)(2,1)S(1)} %slice.418), channel_id=1, source_target_pairs={{0,2},{1,3},{2,0},{3,1},{4,6},{5,7},{6,4},{7,5},{8,10},{9,11},{10,... | collective-permute-start | bytes 786440 | tf_op jit(solution)/shard_map/ppermute | solution.py:31
  176.7 13.5 %collective-permute-start.51 = (bf16[64,2048]{1,0:T(8,128)(2,1)S(1)}, bf16[64,2048]{1,0:T(8,128)(2,1)S(1)}, u32[]{:S(2)}, u32[]{:S(2)}) collective-permute-start(bf16[64,2048]{1,0:T(8,128)(2,1)S(1)} %slice.416), channel_id=1, source_target_pairs={{0,2},{1,3},{2,0},{3,1},{4,6},{5,7},{6,4},{7,5},{8,10},{9,11},{10,... | collective-permute-start | bytes 786440 | tf_op jit(solution)/shard_map/ppermute | solution.py:31
  184.6 11.3 %collective-permute-start.54 = (bf16[64,2048]{1,0:T(8,128)(2,1)S(1)}, bf16[64,2048]{1,0:T(8,128)(2,1)S(1)}, u32[]{:S(2)}, u32[]{:S(2)}) collective-permute-start(bf16[64,2048]{1,0:T(8,128)(2,1)S(1)} %add_convert_fusion.11), channel_id=1, source_target_pairs={{0,12},{1,13},{2,14},{3,15},{4,8},{5,9},{6,10},{7,11},{8,4},{9,5},... | collective-permute-start | bytes 786440 | tf_op jit(solution)/shard_map/ppermute | solution.py:25
  186.2 9.6 %collective-permute-start.57 = (bf16[64,2048]{1,0:T(8,128)(2,1)S(1)}, bf16[64,2048]{1,0:T(8,128)(2,1)S(1)}, u32[]{:S(2)}, u32[]{:S(2)}) collective-permute-start(bf16[64,2048]{1,0:T(8,128)(2,1)S(1)} %slice.423), channel_id=1, source_target_pairs={{0,2},{1,3},{2,0},{3,1},{4,6},{5,7},{6,4},{7,5},{8,10},{9,11},{10,... | collective-permute-start | bytes 786440 | tf_op jit(solution)/shard_map/ppermute | solution.py:31
  190.3 15.4 %collective-permute-start.55 = (bf16[64,2048]{1,0:T(8,128)(2,1)S(1)}, bf16[64,2048]{1,0:T(8,128)(2,1)S(1)}, u32[]{:S(2)}, u32[]{:S(2)}) collective-permute-start(bf16[64,2048]{1,0:T(8,128)(2,1)S(1)} %add_convert_fusion.10), channel_id=1, source_target_pairs={{0,8},{1,9},{2,10},{3,11},{4,12},{5,13},{6,14},{7,15},{8,0},{9,1},... | collective-permute-start | bytes 786440 | tf_op jit(solution)/shard_map/ppermute | solution.py:25
  190.3 15.3 %collective-permute-start.52 = (bf16[64,2048]{1,0:T(8,128)(2,1)S(1)}, bf16[64,2048]{1,0:T(8,128)(2,1)S(1)}, u32[]{:S(2)}, u32[]{:S(2)}) collective-permute-start(bf16[64,2048]{1,0:T(8,128)(2,1)S(1)} %slice.405), channel_id=1, source_target_pairs={{0,2},{1,3},{2,0},{3,1},{4,6},{5,7},{6,4},{7,5},{8,10},{9,11},{10,... | collective-permute-start | bytes 786440 | tf_op jit(solution)/shard_map/ppermute | solution.py:31
  195.9 12.4 %collective-permute-start.58 = (bf16[64,2048]{1,0:T(8,128)(2,1)S(1)}, bf16[64,2048]{1,0:T(8,128)(2,1)S(1)}, u32[]{:S(2)}, u32[]{:S(2)}) collective-permute-start(bf16[64,2048]{1,0:T(8,128)(2,1)S(1)} %add_convert_fusion.9), channel_id=1, source_target_pairs={{0,4},{1,5},{2,6},{3,7},{4,0},{5,1},{6,2},{7,3},{8,12},{9,13},{10,... | collective-permute-start | bytes 786440 | tf_op jit(solution)/shard_map/ppermute | solution.py:25
  (22 other events, 190.3 us)

commit v8 on v7

--- a/solution.py
+++ b/solution.py
@@ -54,12 +54,14 @@
 
 
 def gate_lanes(layers):
-    lanes = []
+    pieces = []
     for routes, gates in layers:
-        high = gates.astype(jnp.bfloat16)
-        lanes += [routes.astype(jnp.bfloat16), high, (gates - high.astype(jnp.float32)).astype(jnp.bfloat16)]
-    lanes = jnp.concatenate(lanes, axis=1)
-    return jnp.pad(lanes, ((0, 0), (0, -lanes.shape[1] % 128)))
+        high = gates.astype(jnp.bfloat16).astype(jnp.float32)
+        pieces += [routes.astype(jnp.float32), high, gates - high]
+    top = pieces[0].shape[1]
+    width = -(-top * len(pieces) // 128) * 128
+    placed = [jnp.pad(p, ((0, 0), (i * top, width - (i + 1) * top))) for i, p in enumerate(pieces)]
+    return sum(placed).astype(jnp.bfloat16)
 
 
 def gate_column(ring, lanes, layer, top):
@@ -91,53 +93,39 @@
     far = ring.send(columns[1], [(1, 2), (2, 1)])
     columns[3] = jnp.where(ring.inside, middle, ends)
     columns[2] = jnp.where(ring.inside, far, near)
-    crossed[1] = ring.across(after(columns[1], middle), top)
-    crossed[3] = ring.across(columns[3], top)
-    crossed[2] = ring.across(columns[2], top)
-
-    done = {}
+    crossed[1] = ring.across(after(columns[1], crossed[0]), top)
+    crossed[3] = ring.across(after(columns[3], crossed[0]), top)
+    crossed[2] = ring.across(after(columns[2], crossed[1]), top)
+
+    chunks = {}
+    for slot in (3, 0, 1, 2):
+        chunks[slot] = jnp.concatenate([columns[slot], crossed[slot]], axis=0)
+        for bit in ring.bits[1:]:
+            chunks[slot] = jnp.concatenate([chunks[slot], ring.across(chunks[slot], bit)], axis=0)
+
+    own = rows.shape[0]
     halves = {}
-    last = [columns[2], crossed[1], crossed[3]]
-    for slot in (0, 1, 3, 2):
-        chunk = jnp.concatenate([columns[slot], crossed[slot]], axis=0)
-        if slot == 2:
-            chunk = after(chunk, *last)
-            halves[3] = within_plane(ring, done[3])
-            last = [halves[3]]
-        for bit in ring.bits[1:]:
-            chunk = jnp.concatenate([chunk, ring.across(chunk, bit)], axis=0)
-        done[slot] = work(slot, after(chunk, *last))
-        last = [done[slot]]
-    for slot in (2, 1, 0):
-        halves[slot] = within_plane(ring, done[slot])
-
-    own = rows.shape[0]
     back = {}
-    for slot, ties in ((3, []), (2, []), (1, [3]), (0, [2])):
-        away = after(halves[slot][own:], *[back[t] for t in ties], *([halves[2]] if ties else []))
-        back[slot] = ring.across(away, top)
+
+    def turn(slot, *ties):
+        done = work(slot, after(chunks[slot], *ties))
+        halves[slot] = within_plane(ring, done)
+        return done
+
+    turn(3, columns[2], crossed[1], crossed[3])
+    back[3] = ring.across(halves[3][own:], top)
+    second = turn(1, turn(0, halves[3]))
+    turn(2, second, back[3])
+    back[2] = ring.across(halves[2][own:], top)
+    back[1] = ring.across(after(halves[1][own:], halves[2]), top)
+    back[0] = ring.across(after(halves[0][own:], halves[2], back[2]), top)
     sums = plane_sums(ring, lambda slot: add(halves[slot][:own], back[slot]))
-    return sums, [crossed[1], crossed[2], back[2]]
-
-
-def other_half(ring, weight, groups, ties):
-    top = ring.bits[0]
-    rows = weight.shape[0] // 2
-    odd = lax.axis_index("groups") % 2
-    pieces = []
-    for piece, (begin, swap) in enumerate(ties):
-        if groups % 2:
-            pieces.append(ring.across(after(weight[piece * rows : (piece + 1) * rows], *begin), top))
-            continue
-        sent = lax.dynamic_slice_in_dim(weight, piece * rows + odd * (rows // 2), rows // 2, axis=0)
-        here = after(ring.across(after(sent, *begin), top), *swap)
-        there = lax.ppermute(here, "groups", [(g, g ^ 1) for g in range(groups)])
-        pieces += [jnp.where(odd == 0, here, there), jnp.where(odd == 0, there, here)]
-    return jnp.concatenate(pieces, axis=0)
-
-
-def plane_weight(ring, weight, other):
-    held = jnp.where(ring.high(ring.bits[0]), jnp.stack([other, weight]), jnp.stack([weight, other]))
+    return sums, columns[2]
+
+
+def shared_weight(ring, weight):
+    other = ring.between(weight, 1)
+    held = jnp.where(ring.z % 2 == 1, jnp.stack([other, weight]), jnp.stack([weight, other]))
     for i, bit in enumerate(ring.bits[1:]):
         other = ring.across(held, bit)
         axis = i + 1
@@ -146,14 +134,22 @@
 
 
 def merge(ring, merged_in, weight):
-    share = merged_in.shape[1] // PLANES
-    products = {}
-    for slot in (2, 3, 1, 0):
-        piece = lax.dynamic_slice_in_dim(merged_in, (ring.z ^ slot) * share, share, axis=1)
-        products[slot] = jnp.dot(ring.between(piece, slot), weight, preferred_element_type=jnp.float32)
-        if slot:
-            products[slot] = products[slot].astype(jnp.bfloat16)
-    return plane_sums(ring, lambda slot: products[slot])
+    top = ring.bits[0]
+    share = merged_in.shape[1] // (2 * PLANES)
+    steps = ((1, 1), (1, 0), (0, 1), (0, 0))
+    pieces = []
+    for far, side in steps:
+        start = (2 * (ring.z // 2 ^ far) * 2 + (ring.high(top).astype(jnp.int32) ^ side)) * share
+        halves = [lax.dynamic_slice_in_dim(merged_in, start + low * 2 * share, share, axis=1) for low in range(2)]
+        piece = jnp.concatenate(halves, axis=1)
+        crossing = far * 2 * ring.plane + side * top
+        pieces.append(ring.across(piece, crossing) if crossing else piece)
+    pieces[0] = after(pieces[0], *pieces[1:3])
+    products = {s: jnp.dot(p, weight, preferred_element_type=jnp.float32) for s, p in zip(steps, pieces)}
+    beyond = ring.across(products[1, 1].astype(jnp.bfloat16), top)
+    beside = ring.across(products[0, 1].astype(jnp.bfloat16), top)
+    away = ring.between(add(products[1, 0], beyond), 2)
+    return products[0, 0] + beside.astype(jnp.float32) + away.astype(jnp.float32)
 
 
 def local(
@@ -185,9 +181,8 @@
     def second_work(slot, chunk):
         return expert(chunk, second_columns[slot], second_gate_up[0], second_down[0])
 
-    first, steps = routed(ring, jnp.concatenate([hidden_rows, lanes], axis=1), first_work)
-    ties = [([], [steps[0]]), ([steps[1]], [steps[2]])]
-    weight = plane_weight(ring, merge_weight, other_half(ring, merge_weight, lax.axis_size("groups"), ties))
+    first, gathered = routed(ring, jnp.concatenate([hidden_rows, lanes], axis=1), first_work)
+    weight = shared_weight(ring, after(merge_weight, gathered))
     after_first = (hidden_rows.astype(jnp.float32) + first).astype(jnp.bfloat16)
     merged_in = jnp.concatenate([normed(after_first, hidden_gain), normed(token_embed, embed_gain)], axis=1)
     merged = merge(ring, merged_in, weight)

time: 210 us -> 226 us (1.076)
  waiting for transfers between devices: 105 us -> 127 us
  other arithmetic: 21.2 us -> 12.6 us
    ppermute x35 -> x38, waiting for transfers between devices: 32.9 us -> 62.1 us  [across(): lax.ppermute(values, 'inner', [(d, d ^ bit) for d in range(self.size)])]
    select_n x5 -> x3, other arithmetic: 5.99 us -> 1.35 us  [the longest x2 0.68 us: shared_weight(): jnp.where(ring.z % 2 == 1, jnp.stack([other, weight]), jnp.stack([weight,...]
    ppermute x2 -> x0, waiting for transfers between devices: 4.42 us -> none  [other_half(): there = lax.ppermute(here, 'groups', [(g, g ^ 1) for g in range(groups)])]
    unnamed x5 -> x0, other arithmetic: 3.7 us -> none
    ppermute x22 -> x18, starting transfers between devices: 31.3 us -> 34.3 us  [send(): return lax.ppermute(values, 'inner', perm)]
    ppermute x2 -> x0, starting transfers between devices: 2.96 us -> none  [other_half(): there = lax.ppermute(here, 'groups', [(g, g ^ 1) for g in range(groups)])]
    convert_element_type x0 -> x4, other arithmetic: none -> 2.31 us  [the longest x2 1.53 us: gate_lanes(): pieces += [routes.astype(jnp.float32), high, gates - high]]
    ppermute x35 -> x38, starting transfers between devices: 25.2 us -> 27.2 us  [across(): lax.ppermute(values, 'inner', [(d, d ^ bit) for d in range(self.size)])]
  transfers between devices with their start and end apart: 59 -> 56, of which waited for: 23 -> 27; matrix products, arithmetic and copies ran while one was open for 18% -> 11% of each run, Pallas kernels for 0% -> 0%
where the time goes in v8:
time: 226 us; the launch traced here: 225 us
  waiting for transfers between devices  127 us (56%)
  starting transfers between devices  61.5 us (27%)
  matrix products  19.7 us (9%)
  other arithmetic  12.6 us (6%)
  local copies, waits for them, and re-layouts  2.82 us (1%)
    ppermute x18, waiting for transfers between devices, send(): return lax.ppermute(values, 'inner', perm)  65.4 us
    ppermute x38, waiting for transfers between devices, across(): lax.ppermute(values, 'inner', [(d, d ^ bit) for d in range(self.size)])  62.1 us
    ppermute x18, starting transfers between devices, send(): return lax.ppermute(values, 'inner', perm)  34.3 us
    ppermute x38, starting transfers between devices, across(): lax.ppermute(values, 'inner', [(d, d ^ bit) for d in range(self.size)])  27.2 us
    dot_general x8, matrix products, expert(): projected = jnp.dot(rows, gate_up, preferred_element_type=jnp.float32)  10.3 us
    dot_general x8, matrix products, expert(): out = jnp.dot(hidden, down, preferred_element_type=jnp.float32)  6.1 us
  transfers between devices with their start and end apart: 56, of which 27 were waited for; matrix products, arithmetic and copies ran while one was open for 11% of the time, Pallas kernels for 0%

profile of v8, /device:TPU:0, one launch (start us, length us, event | category | flops | bytes accessed | tf_op | source)
XLA Modules:
  0.0 225.2 jit_solution(5889746588580195024)
XLA Ops:
  4.1 5.9 %collective-permute-start.6 = (bf16[64,2176]{1,0:T(8,128)(2,1)S(1)}, bf16[64,2176]{1,0:T(8,128)(2,1)S(1)}, u32[]{:S(2)}, u32[]{:S(2)}) collective-permute-start(bf16[64,2176]{1,0:T(8,128)(2,1)S(1)} %pad_maximum_fusion.16), channel_id=1, source_target_pairs={{0,4},{1,5},{2,6},{3,7},{4,0},{5,1},{6,2},{7,3},{8,12},{9,13},{10,... | collective-permute-start | bytes 835592 | tf_op jit(solution)/shard_map/ppermute | solution.py:25
  10.0 3.2 %collective-permute-start.3 = (bf16[64,2176]{1,0:T(8,128)(2,1)S(1)}, bf16[64,2176]{1,0:T(8,128)(2,1)}, u32[]{:S(2)}, u32[]{:S(2)}) collective-permute-start(bf16[64,2176]{1,0:T(8,128)(2,1)S(1)} %pad_maximum_fusion.16), channel_id=1, source_target_pairs={{0,12},{1,13},{2,14},{3,15},{12,0},{13,1},{14,2},{15,3},{16,28},{1... | collective-permute-start | bytes 835592 | tf_op jit(solution)/shard_map/ppermute | solution.py:25
  13.2 1.6 collective-permute-start
  17.1 3.8 %collective-permute-done = bf16[64,2176]{1,0:T(8,128)(2,1)S(1)} collective-permute-done((bf16[64,2176]{1,0:T(8,128)(2,1)S(1)}, bf16[64,2176]{1,0:T(8,128)(2,1)S(1)}, u32[]{:S(2)}, u32[]{:S(2)}) %collective-permute-start) | collective-permute-done | bytes 278560 | tf_op jit(solution)/shard_map/ppermute | solution.py:31
  20.9 2.6 %collective-permute-done.3 = bf16[64,2176]{1,0:T(8,128)(2,1)} collective-permute-done((bf16[64,2176]{1,0:T(8,128)(2,1)S(1)}, bf16[64,2176]{1,0:T(8,128)(2,1)}, u32[]{:S(2)}, u32[]{:S(2)}) %collective-permute-start.3) | collective-permute-done | bytes 278560 | tf_op jit(solution)/shard_map/ppermute | solution.py:25
  24.5 1.6 collective-permute-start.4
  28.7 6.4 %collective-permute-done.8 = bf16[64,2176]{1,0:T(8,128)(2,1)S(1)} collective-permute-done((bf16[64,2176]{1,0:T(8,128)(2,1)S(1)}, bf16[64,2176]{1,0:T(8,128)(2,1)S(1)}, u32[]{:S(2)}, u32[]{:S(2)}) %collective-permute-start.8) | collective-permute-done | bytes 278560 | tf_op jit(solution)/shard_map/ppermute | solution.py:25
  35.2 2.6 %collective-permute-done.9 = bf16[64,2176]{1,0:T(8,128)(2,1)S(1)} collective-permute-done((bf16[64,2176]{1,0:T(8,128)(2,1)S(1)}, bf16[64,2176]{1,0:T(8,128)(2,1)S(1)}, u32[]{:S(2)}, u32[]{:S(2)}) %collective-permute-start.9) | collective-permute-done | bytes 278560 | tf_op jit(solution)/shard_map/ppermute | solution.py:31
  37.7 1.5 collective-permute-start.12
  40.0 1.3 collective-permute-start.24
  41.3 2.9 %collective-permute-done.12 = bf16[64,2176]{1,0:T(8,128)(2,1)S(1)} collective-permute-done((bf16[64,2176]{1,0:T(8,128)(2,1)S(1)}, bf16[64,2176]{1,0:T(8,128)(2,1)S(1)}, u32[]{:S(2)}, u32[]{:S(2)}) %collective-permute-start.12) | collective-permute-done | bytes 278560 | tf_op jit(solution)/shard_map/ppermute | solution.py:31
  44.6 1.9 copy-done.7
  46.5 1.3 fusion.14
  49.2 15.9 %collective-permute-done.24 = bf16[256,2048]{1,0:T(8,128)(2,1)S(1)} collective-permute-done((bf16[256,2048]{1,0:T(8,128)(2,1)S(1)}, bf16[256,2048]{1,0:T(8,128)(2,1)S(1)}, u32[]{:S(2)}, u32[]{:S(2)}) %collective-permute-start.24) | collective-permute-done | bytes 1048608 | tf_op jit(solution)/shard_map/ppermute | solution.py:25
  66.0 1.3 fusion.12
  68.4 1.3 fusion.10
  71.7 6.8 %collective-permute-done.15 = bf16[64,2048]{1,0:T(8,128)(2,1)S(1)} collective-permute-done((bf16[64,2048]{1,0:T(8,128)(2,1)S(1)}, bf16[64,2048]{1,0:T(8,128)(2,1)S(1)}, u32[]{:S(2)}, u32[]{:S(2)}) %collective-permute-start.15) | collective-permute-done | bytes 262176 | tf_op jit(solution)/shard_map/ppermute | solution.py:31
  78.8 1.3 fusion.8
  81.1 2.5 %collective-permute-start.19 = (bf16[64,2048]{1,0:T(8,128)(2,1)S(1)}, bf16[64,2048]{1,0:T(8,128)(2,1)S(1)}, u32[]{:S(2)}, u32[]{:S(2)}) collective-permute-start(bf16[64,2048]{1,0:T(8,128)(2,1)S(1)} %add_convert_fusion.16), channel_id=1, source_target_pairs={{0,12},{1,13},{2,14},{3,15},{4,8},{5,9},{6,10},{7,11},{8,4},{9,5},... | collective-permute-start | bytes 786440 | tf_op jit(solution)/shard_map/ppermute | solution.py:25
  84.7 1.6 collective-permute-start.22
  86.3 6.9 %collective-permute-done.17 = bf16[64,2048]{1,0:T(8,128)(2,1)S(1)} collective-permute-done((bf16[64,2048]{1,0:T(8,128)(2,1)S(1)}, bf16[64,2048]{1,0:T(8,128)(2,1)S(1)}, u32[]{:S(2)}, u32[]{:S(2)}) %collective-permute-start.17) | collective-permute-done | bytes 262176 | tf_op jit(solution)/shard_map/ppermute | solution.py:31
  93.2 1.5 collective-permute-start.20
  95.3 3.5 %collective-permute-done.22 = bf16[64,2048]{1,0:T(8,128)(2,1)S(1)} collective-permute-done((bf16[64,2048]{1,0:T(8,128)(2,1)S(1)}, bf16[64,2048]{1,0:T(8,128)(2,1)S(1)}, u32[]{:S(2)}, u32[]{:S(2)}) %collective-permute-start.22) | collective-permute-done | bytes 262176 | tf_op jit(solution)/shard_map/ppermute | solution.py:31
  99.5 8.0 %collective-permute-done.20 = bf16[64,2048]{1,0:T(8,128)(2,1)S(1)} collective-permute-done((bf16[64,2048]{1,0:T(8,128)(2,1)S(1)}, bf16[64,2048]{1,0:T(8,128)(2,1)S(1)}, u32[]{:S(2)}, u32[]{:S(2)}) %collective-permute-start.20) | collective-permute-done | bytes 262176 | tf_op jit(solution)/shard_map/ppermute | solution.py:25
  107.6 3.9 %collective-permute-done.23 = bf16[64,2048]{1,0:T(8,128)(2,1)S(1)} collective-permute-done((bf16[64,2048]{1,0:T(8,128)(2,1)S(1)}, bf16[64,2048]{1,0:T(8,128)(2,1)S(1)}, u32[]{:S(2)}, u32[]{:S(2)}) %collective-permute-start.23) | collective-permute-done | bytes 262176 | tf_op jit(solution)/shard_map/ppermute | solution.py:25
  113.0 3.9 %collective-permute-start.29 = (bf16[64,1024]{1,0:T(8,128)(2,1)S(1)}, bf16[64,1024]{1,0:T(8,128)(2,1)S(1)}, u32[]{:S(2)}, u32[]{:S(2)}) collective-permute-start(bf16[64,1024]{1,0:T(8,128)(2,1)S(1)} %pad_maximum_fusion.19), channel_id=1, source_target_pairs={{0,10},{1,11},{2,8},{3,9},{4,14},{5,15},{6,12},{7,13},{8,2},{9,3},... | collective-permute-start | bytes 393224 | tf_op jit(solution)/shard_map/ppermute | solution.py:31
  117.3 5.6 %collective-permute-done.28 = bf16[64,1024]{1,0:T(8,128)(2,1)S(1)} collective-permute-done((bf16[64,1024]{1,0:T(8,128)(2,1)S(1)}, bf16[64,1024]{1,0:T(8,128)(2,1)S(1)}, u32[]{:S(2)}, u32[]{:S(2)}) %collective-permute-start.28) | collective-permute-done | bytes 131104 | tf_op jit(solution)/shard_map/ppermute | solution.py:31
  122.9 1.3 collective-permute-done.29
  125.8 1.6 collective-permute-start.30
  128.8 6.3 %collective-permute-done.30 = bf16[64,2048]{1,0:T(8,128)(2,1)S(1)} collective-permute-done((bf16[64,2048]{1,0:T(8,128)(2,1)S(1)}, bf16[64,2048]{1,0:T(8,128)(2,1)S(1)}, u32[]{:S(2)}, u32[]{:S(2)}) %collective-permute-start.30) | collective-permute-done | bytes 262176 | tf_op jit(solution)/shard_map/ppermute | solution.py:31
  138.1 7.1 %collective-permute-done.31 = bf16[64,2048]{1,0:T(8,128)(2,1)S(1)} collective-permute-done((bf16[64,2048]{1,0:T(8,128)(2,1)S(1)}, bf16[64,2048]{1,0:T(8,128)(2,1)S(1)}, u32[]{:S(2)}, u32[]{:S(2)}) %collective-permute-start.31) | collective-permute-done | bytes 262176 | tf_op jit(solution)/shard_map/ppermute | solution.py:25
  145.4 1.6 collective-permute-start.32
  147.7 3.9 %collective-permute-start.35 = (bf16[64,2048]{1,0:T(8,128)(2,1)S(1)}, bf16[64,2048]{1,0:T(8,128)(2,1)S(1)}, u32[]{:S(2)}, u32[]{:S(2)}) collective-permute-start(bf16[64,2048]{1,0:T(8,128)(2,1)S(1)} %fusion.43), channel_id=1, source_target_pairs={{0,12},{1,13},{2,14},{3,15},{12,0},{13,1},{14,2},{15,3},{16,28},{1... | collective-permute-start | bytes 786440 | tf_op jit(solution)/shard_map/ppermute | solution.py:25
  151.6 1.5 collective-permute-done.38
  155.0 2.9 %collective-permute-done.35 = bf16[64,2048]{1,0:T(8,128)(2,1)S(1)} collective-permute-done((bf16[64,2048]{1,0:T(8,128)(2,1)S(1)}, bf16[64,2048]{1,0:T(8,128)(2,1)S(1)}, u32[]{:S(2)}, u32[]{:S(2)}) %collective-permute-start.35) | collective-permute-done | bytes 262176 | tf_op jit(solution)/shard_map/ppermute | solution.py:25
  158.5 1.5 collective-permute-start.41
  160.0 6.1 %collective-permute-done.40 = bf16[64,2048]{1,0:T(8,128)(2,1)S(1)} collective-permute-done((bf16[64,2048]{1,0:T(8,128)(2,1)S(1)}, bf16[64,2048]{1,0:T(8,128)(2,1)S(1)}, u32[]{:S(2)}, u32[]{:S(2)}) %collective-permute-start.40) | collective-permute-done | bytes 262176 | tf_op jit(solution)/shard_map/ppermute | solution.py:25
  166.2 3.8 %collective-permute-done.41 = bf16[64,2048]{1,0:T(8,128)(2,1)S(1)} collective-permute-done((bf16[64,2048]{1,0:T(8,128)(2,1)S(1)}, bf16[64,2048]{1,0:T(8,128)(2,1)S(1)}, u32[]{:S(2)}, u32[]{:S(2)}) %collective-permute-start.41) | collective-permute-done | bytes 262176 | tf_op jit(solution)/shard_map/ppermute | solution.py:31
  171.5 4.9 %collective-permute-done.44 = bf16[64,2048]{1,0:T(8,128)(2,1)S(1)} collective-permute-done((bf16[64,2048]{1,0:T(8,128)(2,1)S(1)}, bf16[64,2048]{1,0:T(8,128)(2,1)S(1)}, u32[]{:S(2)}, u32[]{:S(2)}) %collective-permute-start.44) | collective-permute-done | bytes 262176 | tf_op jit(solution)/shard_map/ppermute | solution.py:31
  186.8 4.4 %collective-permute-done.47 = bf16[64,2048]{1,0:T(8,128)(2,1)S(1)} collective-permute-done((bf16[64,2048]{1,0:T(8,128)(2,1)S(1)}, bf16[64,2048]{1,0:T(8,128)(2,1)S(1)}, u32[]{:S(2)}, u32[]{:S(2)}) %collective-permute-start.47) | collective-permute-done | bytes 262176 | tf_op jit(solution)/shard_map/ppermute | solution.py:31
  193.4 2.0 collective-permute-start.51
  196.7 1.4 collective-permute-start.54
  198.2 6.9 %collective-permute-done.49 = bf16[64,2048]{1,0:T(8,128)(2,1)S(1)} collective-permute-done((bf16[64,2048]{1,0:T(8,128)(2,1)S(1)}, bf16[64,2048]{1,0:T(8,128)(2,1)S(1)}, u32[]{:S(2)}, u32[]{:S(2)}) %collective-permute-start.49) | collective-permute-done | bytes 262176 | tf_op jit(solution)/shard_map/ppermute | solution.py:31
  205.1 4.4 %collective-permute-start.52 = (bf16[64,2048]{1,0:T(8,128)(2,1)S(1)}, bf16[64,2048]{1,0:T(8,128)(2,1)S(1)}, u32[]{:S(2)}, u32[]{:S(2)}) collective-permute-start(bf16[64,2048]{1,0:T(8,128)(2,1)S(1)} %add_convert_fusion.10), channel_id=1, source_target_pairs={{0,8},{1,9},{2,10},{3,11},{4,12},{5,13},{6,14},{7,15},{8,0},{9,1},... | collective-permute-start | bytes 786440 | tf_op jit(solution)/shard_map/ppermute | solution.py:25
  209.5 1.3 collective-permute-start.50
  210.8 3.5 %collective-permute-start.55 = (bf16[64,2048]{1,0:T(8,128)(2,1)S(1)}, bf16[64,2048]{1,0:T(8,128)(2,1)S(1)}, u32[]{:S(2)}, u32[]{:S(2)}) collective-permute-start(bf16[64,2048]{1,0:T(8,128)(2,1)S(1)} %add_convert_fusion.9), channel_id=1, source_target_pairs={{0,4},{1,5},{2,6},{3,7},{4,0},{5,1},{6,2},{7,3},{8,12},{9,13},{10,... | collective-permute-start | bytes 786440 | tf_op jit(solution)/shard_map/ppermute | solution.py:25
  214.4 6.6 %collective-permute-done.52 = bf16[64,2048]{1,0:T(8,128)(2,1)S(1)} collective-permute-done((bf16[64,2048]{1,0:T(8,128)(2,1)S(1)}, bf16[64,2048]{1,0:T(8,128)(2,1)S(1)}, u32[]{:S(2)}, u32[]{:S(2)}) %collective-permute-start.52) | collective-permute-done | bytes 262176 | tf_op jit(solution)/shard_map/ppermute | solution.py:25
  221.0 3.3 %collective-permute-done.55 = bf16[64,2048]{1,0:T(8,128)(2,1)S(1)} collective-permute-done((bf16[64,2048]{1,0:T(8,128)(2,1)S(1)}, bf16[64,2048]{1,0:T(8,128)(2,1)S(1)}, u32[]{:S(2)}, u32[]{:S(2)}) %collective-permute-start.55) | collective-permute-done | bytes 262176 | tf_op jit(solution)/shard_map/ppermute | solution.py:25
  (180 shorter events, 47.1 us)
Async XLA Ops:
  3.4 17.5 %collective-permute-start.2 = (bf16[64,2176]{1,0:T(8,128)(2,1)S(1)}, bf16[64,2176]{1,0:T(8,128)(2,1)S(1)}, u32[]{:S(2)}, u32[]{:S(2)}) collective-permute-start(bf16[64,2176]{1,0:T(8,128)(2,1)S(1)} %pad_maximum_fusion.16), channel_id=1, source_target_pairs={{4,8},{5,9},{6,10},{7,11},{8,4},{9,5},{10,6},{11,7},{20,24},{21,25... | collective-permute-start | bytes 835592 | tf_op jit(solution)/shard_map/ppermute | solution.py:25
  4.1 13.0 %collective-permute-start.6 = (bf16[64,2176]{1,0:T(8,128)(2,1)S(1)}, bf16[64,2176]{1,0:T(8,128)(2,1)S(1)}, u32[]{:S(2)}, u32[]{:S(2)}) collective-permute-start(bf16[64,2176]{1,0:T(8,128)(2,1)S(1)} %pad_maximum_fusion.16), channel_id=1, source_target_pairs={{0,4},{1,5},{2,6},{3,7},{4,0},{5,1},{6,2},{7,3},{8,12},{9,13},{10,... | collective-permute-start | bytes 835592 | tf_op jit(solution)/shard_map/ppermute | solution.py:25
  10.0 13.5 %collective-permute-start.3 = (bf16[64,2176]{1,0:T(8,128)(2,1)S(1)}, bf16[64,2176]{1,0:T(8,128)(2,1)}, u32[]{:S(2)}, u32[]{:S(2)}) collective-permute-start(bf16[64,2176]{1,0:T(8,128)(2,1)S(1)} %pad_maximum_fusion.16), channel_id=1, source_target_pairs={{0,12},{1,13},{2,14},{3,15},{12,0},{13,1},{14,2},{15,3},{16,28},{1... | collective-permute-start | bytes 835592 | tf_op jit(solution)/shard_map/ppermute | solution.py:25
  13.2 7.6 %collective-permute-start = (bf16[64,2176]{1,0:T(8,128)(2,1)S(1)}, bf16[64,2176]{1,0:T(8,128)(2,1)S(1)}, u32[]{:S(2)}, u32[]{:S(2)}) collective-permute-start(bf16[64,2176]{1,0:T(8,128)(2,1)S(1)} %pad_maximum_fusion.16), channel_id=1, source_target_pairs={{0,2},{1,3},{2,0},{3,1},{4,6},{5,7},{6,4},{7,5},{8,10},{9,11},{10,... | collective-permute-start | bytes 835592 | tf_op jit(solution)/shard_map/ppermute | solution.py:31
  24.5 14.8 %collective-permute-start.4 = (bf16[64,2176]{1,0:T(8,128)(2,1)S(1)}, bf16[64,2176]{1,0:T(8,128)(2,1)S(1)}, u32[]{:S(2)}, u32[]{:S(2)}) collective-permute-start(bf16[64,2176]{1,0:T(8,128)(2,1)S(1)} %broadcast_select_fusion.1), channel_id=1, source_target_pairs={{0,2},{1,3},{2,0},{3,1},{4,6},{5,7},{6,4},{7,5},{8,10},{9,11},{10,... | collective-permute-start | bytes 835592 | tf_op jit(solution)/shard_map/ppermute | solution.py:31
  26.1 11.7 %collective-permute-start.9 = (bf16[64,2176]{1,0:T(8,128)(2,1)S(1)}, bf16[64,2176]{1,0:T(8,128)(2,1)S(1)}, u32[]{:S(2)}, u32[]{:S(2)}) collective-permute-start(bf16[64,2176]{1,0:T(8,128)(2,1)S(1)} %collective-permute-done.6), channel_id=1, source_target_pairs={{0,2},{1,3},{2,0},{3,1},{4,6},{5,7},{6,4},{7,5},{8,10},{9,11},{10,... | collective-permute-start | bytes 835592 | tf_op jit(solution)/shard_map/ppermute | solution.py:31
  26.6 8.5 %collective-permute-start.8 = (bf16[64,2176]{1,0:T(8,128)(2,1)S(1)}, bf16[64,2176]{1,0:T(8,128)(2,1)S(1)}, u32[]{:S(2)}, u32[]{:S(2)}) collective-permute-start(bf16[64,2176]{1,0:T(8,128)(2,1)S(1)} %collective-permute-done.2), channel_id=1, source_target_pairs={{4,0},{5,1},{6,2},{7,3},{8,12},{9,13},{10,14},{11,15},{20,16},{21,... | collective-permute-start | bytes 835592 | tf_op jit(solution)/shard_map/ppermute | solution.py:25
  27.9 7.2 %collective-permute-start.7 = (bf16[64,2176]{1,0:T(8,128)(2,1)S(1)}, bf16[64,2176]{1,0:T(8,128)(2,1)S(1)}, u32[]{:S(2)}, u32[]{:S(2)}) collective-permute-start(bf16[64,2176]{1,0:T(8,128)(2,1)S(1)} %collective-permute-done.6), channel_id=1, source_target_pairs={{4,8},{5,9},{6,10},{7,11},{8,4},{9,5},{10,6},{11,7},{20,24},{21,25... | collective-permute-start | bytes 835592 | tf_op jit(solution)/shard_map/ppermute | solution.py:25
  28.6 15.8 %collective-permute-start.1 = (bf16[128,2176]{1,0:T(8,128)(2,1)S(1)}, bf16[128,2176]{1,0:T(8,128)(2,1)S(1)}, u32[]{:S(2)}, u32[]{:S(2)}) collective-permute-start(bf16[128,2176]{1,0:T(8,128)(2,1)S(1)} %pad_maximum_fusion.8), channel_id=1, source_target_pairs={{0,1},{1,0},{2,3},{3,2},{4,5},{5,4},{6,7},{7,6},{8,9},{9,8},{10,11... | collective-permute-start | bytes 1671176 | tf_op jit(solution)/shard_map/ppermute | solution.py:31
  37.7 6.5 %collective-permute-start.12 = (bf16[64,2176]{1,0:T(8,128)(2,1)S(1)}, bf16[64,2176]{1,0:T(8,128)(2,1)S(1)}, u32[]{:S(2)}, u32[]{:S(2)}) collective-permute-start(bf16[64,2176]{1,0:T(8,128)(2,1)S(1)} %broadcast_select_fusion), channel_id=1, source_target_pairs={{0,2},{1,3},{2,0},{3,1},{4,6},{5,7},{6,4},{7,5},{8,10},{9,11},{10,... | collective-permute-start | bytes 835592 | tf_op jit(solution)/shard_map/ppermute | solution.py:31
  39.4 9.6 %collective-permute-start.14 = (bf16[128,2176]{1,0:T(8,128)(2,1)S(1)}, bf16[128,2176]{1,0:T(8,128)(2,1)S(1)}, u32[]{:S(2)}, u32[]{:S(2)}) collective-permute-start(bf16[128,2176]{1,0:T(8,128)(2,1)S(1)} %pad_maximum_fusion.11), channel_id=1, source_target_pairs={{0,1},{1,0},{2,3},{3,2},{4,5},{5,4},{6,7},{7,6},{8,9},{9,8},{10,11... | collective-permute-start | bytes 1671176 | tf_op jit(solution)/shard_map/ppermute | solution.py:31
  40.0 25.1 %collective-permute-start.24 = (bf16[256,2048]{1,0:T(8,128)(2,1)S(1)}, bf16[256,2048]{1,0:T(8,128)(2,1)S(1)}, u32[]{:S(2)}, u32[]{:S(2)}) collective-permute-start(bf16[256,2048]{1,0:T(8,128)(2,1)S(1)} %copy-done.2), channel_id=1, source_target_pairs={{0,4},{1,5},{2,6},{3,7},{4,0},{5,1},{6,2},{7,3},{8,12},{9,13},{10,... | collective-permute-start | bytes 3145736 | tf_op jit(solution)/shard_map/ppermute | solution.py:25
  48.9 16.6 %collective-permute-start.10 = (bf16[128,2048]{1,0:T(8,128)(2,1)S(1)}, bf16[128,2048]{1,0:T(8,128)(2,1)S(1)}, u32[]{:S(2)}, u32[]{:S(2)}) collective-permute-start(bf16[128,2048]{1,0:T(8,128)(2,1)S(1)} %slice.379), channel_id=1, source_target_pairs={{0,1},{1,0},{2,3},{3,2},{4,5},{5,4},{6,7},{7,6},{8,9},{9,8},{10,11... | collective-permute-start | bytes 1572872 | tf_op jit(solution)/shard_map/ppermute | solution.py:31
  65.5 58.8 %collective-permute-start.25 = (bf16[2,256,2048]{2,1,0:T(8,128)(2,1)S(1)}, bf16[2,256,2048]{2,1,0:T(8,128)(2,1)S(1)}, u32[]{:S(2)}, u32[]{:S(2)}) collective-permute-start(bf16[2,256,2048]{2,1,0:T(8,128)(2,1)S(1)} %maximum_select_fusion.1), channel_id=1, source_target_pairs={{0,1},{1,0},{2,3},{3,2},{4,5},{5,4},{6,7},{7,6},{8,9},{9,8},{10,11... | collective-permute-start | bytes 6291464 | tf_op jit(solution)/shard_map/ppermute | solution.py:31
  69.7 8.8 %collective-permute-start.15 = (bf16[64,2048]{1,0:T(8,128)(2,1)S(1)}, bf16[64,2048]{1,0:T(8,128)(2,1)S(1)}, u32[]{:S(2)}, u32[]{:S(2)}) collective-permute-start(bf16[64,2048]{1,0:T(8,128)(2,1)S(1)} %slice.388), channel_id=1, source_target_pairs={{0,2},{1,3},{2,0},{3,1},{4,6},{5,7},{6,4},{7,5},{8,10},{9,11},{10,... | collective-permute-start | bytes 786440 | tf_op jit(solution)/shard_map/ppermute | solution.py:31
  70.3 13.3 %collective-permute-start.11 = (bf16[128,2048]{1,0:T(8,128)(2,1)S(1)}, bf16[128,2048]{1,0:T(8,128)(2,1)S(1)}, u32[]{:S(2)}, u32[]{:S(2)}) collective-permute-start(bf16[128,2048]{1,0:T(8,128)(2,1)S(1)} %slice.383), channel_id=1, source_target_pairs={{0,1},{1,0},{2,3},{3,2},{4,5},{5,4},{6,7},{7,6},{8,9},{9,8},{10,11... | collective-permute-start | bytes 1572872 | tf_op jit(solution)/shard_map/ppermute | solution.py:31
  71.3 13.2 %collective-permute-start.21 = (bf16[128,2048]{1,0:T(8,128)(2,1)S(1)}, bf16[128,2048]{1,0:T(8,128)(2,1)S(1)}, u32[]{:S(2)}, u32[]{:S(2)}) collective-permute-start(bf16[128,2048]{1,0:T(8,128)(2,1)S(1)} %slice.397), channel_id=1, source_target_pairs={{0,1},{1,0},{2,3},{3,2},{4,5},{5,4},{6,7},{7,6},{8,9},{9,8},{10,11... | collective-permute-start | bytes 1572872 | tf_op jit(solution)/shard_map/ppermute | solution.py:31
  81.1 18.5 %collective-permute-start.19 = (bf16[64,2048]{1,0:T(8,128)(2,1)S(1)}, bf16[64,2048]{1,0:T(8,128)(2,1)S(1)}, u32[]{:S(2)}, u32[]{:S(2)}) collective-permute-start(bf16[64,2048]{1,0:T(8,128)(2,1)S(1)} %add_convert_fusion.16), channel_id=1, source_target_pairs={{0,12},{1,13},{2,14},{3,15},{4,8},{5,9},{6,10},{7,11},{8,4},{9,5},... | collective-permute-start | bytes 786440 | tf_op jit(solution)/shard_map/ppermute | solution.py:25
  84.0 9.2 %collective-permute-start.17 = (bf16[64,2048]{1,0:T(8,128)(2,1)S(1)}, bf16[64,2048]{1,0:T(8,128)(2,1)S(1)}, u32[]{:S(2)}, u32[]{:S(2)}) collective-permute-start(bf16[64,2048]{1,0:T(8,128)(2,1)S(1)} %slice.393), channel_id=1, source_target_pairs={{0,2},{1,3},{2,0},{3,1},{4,6},{5,7},{6,4},{7,5},{8,10},{9,11},{10,... | collective-permute-start | bytes 786440 | tf_op jit(solution)/shard_map/ppermute | solution.py:31
  84.7 14.1 %collective-permute-start.22 = (bf16[64,2048]{1,0:T(8,128)(2,1)S(1)}, bf16[64,2048]{1,0:T(8,128)(2,1)S(1)}, u32[]{:S(2)}, u32[]{:S(2)}) collective-permute-start(bf16[64,2048]{1,0:T(8,128)(2,1)S(1)} %slice.399), channel_id=1, source_target_pairs={{0,2},{1,3},{2,0},{3,1},{4,6},{5,7},{6,4},{7,5},{8,10},{9,11},{10,... | collective-permute-start | bytes 786440 | tf_op jit(solution)/shard_map/ppermute | solution.py:31
  93.2 14.3 %collective-permute-start.20 = (bf16[64,2048]{1,0:T(8,128)(2,1)S(1)}, bf16[64,2048]{1,0:T(8,128)(2,1)S(1)}, u32[]{:S(2)}, u32[]{:S(2)}) collective-permute-start(bf16[64,2048]{1,0:T(8,128)(2,1)S(1)} %add_convert_fusion.15), channel_id=1, source_target_pairs={{0,8},{1,9},{2,10},{3,11},{4,12},{5,13},{6,14},{7,15},{8,0},{9,1},... | collective-permute-start | bytes 786440 | tf_op jit(solution)/shard_map/ppermute | solution.py:25
  94.8 12.8 %collective-permute-start.18 = (bf16[64,2048]{1,0:T(8,128)(2,1)S(1)}, bf16[64,2048]{1,0:T(8,128)(2,1)S(1)}, u32[]{:S(2)}, u32[]{:S(2)}) collective-permute-start(bf16[64,2048]{1,0:T(8,128)(2,1)S(1)} %slice.385), channel_id=1, source_target_pairs={{0,2},{1,3},{2,0},{3,1},{4,6},{5,7},{6,4},{7,5},{8,10},{9,11},{10,... | collective-permute-start | bytes 786440 | tf_op jit(solution)/shard_map/ppermute | solution.py:31
  98.9 12.6 %collective-permute-start.23 = (bf16[64,2048]{1,0:T(8,128)(2,1)S(1)}, bf16[64,2048]{1,0:T(8,128)(2,1)S(1)}, u32[]{:S(2)}, u32[]{:S(2)}) collective-permute-start(bf16[64,2048]{1,0:T(8,128)(2,1)S(1)} %add_convert_fusion.14), channel_id=1, source_target_pairs={{0,4},{1,5},{2,6},{3,7},{4,0},{5,1},{6,2},{7,3},{8,12},{9,13},{10,... | collective-permute-start | bytes 786440 | tf_op jit(solution)/shard_map/ppermute | solution.py:25
  112.2 10.7 %collective-permute-start.28 = (bf16[64,1024]{1,0:T(8,128)(2,1)S(1)}, bf16[64,1024]{1,0:T(8,128)(2,1)S(1)}, u32[]{:S(2)}, u32[]{:S(2)}) collective-permute-start(bf16[64,1024]{1,0:T(8,128)(2,1)S(1)} %pad_maximum_fusion.18), channel_id=1, source_target_pairs={{0,8},{1,9},{2,10},{3,11},{4,12},{5,13},{6,14},{7,15},{8,0},{9,1},... | collective-permute-start | bytes 393224 | tf_op jit(solution)/shard_map/ppermute | solution.py:31
  112.3 10.6 %collective-permute-start.26 = (bf16[64,1024]{1,0:T(8,128)(2,1)S(1)}, bf16[64,1024]{1,0:T(8,128)(2,1)S(1)}, u32[]{:S(2)}, u32[]{:S(2)}) collective-permute-start(bf16[64,1024]{1,0:T(8,128)(2,1)S(1)} %pad_maximum_fusion.17), channel_id=1, source_target_pairs={{0,2},{1,3},{2,0},{3,1},{4,6},{5,7},{6,4},{7,5},{8,10},{9,11},{10,... | collective-permute-start | bytes 393224 | tf_op jit(solution)/shard_map/ppermute | solution.py:31
  113.0 11.2 %collective-permute-start.29 = (bf16[64,1024]{1,0:T(8,128)(2,1)S(1)}, bf16[64,1024]{1,0:T(8,128)(2,1)S(1)}, u32[]{:S(2)}, u32[]{:S(2)}) collective-permute-start(bf16[64,1024]{1,0:T(8,128)(2,1)S(1)} %pad_maximum_fusion.19), channel_id=1, source_target_pairs={{0,10},{1,11},{2,8},{3,9},{4,14},{5,15},{6,12},{7,13},{8,2},{9,3},... | collective-permute-start | bytes 393224 | tf_op jit(solution)/shard_map/ppermute | solution.py:31
  125.8 9.3 %collective-permute-start.30 = (bf16[64,2048]{1,0:T(8,128)(2,1)S(1)}, bf16[64,2048]{1,0:T(8,128)(2,1)S(1)}, u32[]{:S(2)}, u32[]{:S(2)}) collective-permute-start(bf16[64,2048]{1,0:T(8,128)(2,1)S(1)} %convolution_convert_fusion), channel_id=1, source_target_pairs={{0,2},{1,3},{2,0},{3,1},{4,6},{5,7},{6,4},{7,5},{8,10},{9,11},{10,... | collective-permute-start | bytes 786440 | tf_op jit(solution)/shard_map/ppermute | solution.py:31
  128.2 9.8 %collective-permute-start.27 = (bf16[64,2048]{1,0:T(8,128)(2,1)S(1)}, bf16[64,2048]{1,0:T(8,128)(2,1)S(1)}, u32[]{:S(2)}, u32[]{:S(2)}) collective-permute-start(bf16[64,2048]{1,0:T(8,128)(2,1)S(1)} %convolution_convert_fusion.1), channel_id=1, source_target_pairs={{0,2},{1,3},{2,0},{3,1},{4,6},{5,7},{6,4},{7,5},{8,10},{9,11},{10,... | collective-permute-start | bytes 786440 | tf_op jit(solution)/shard_map/ppermute | solution.py:31
  135.9 9.2 %collective-permute-start.31 = (bf16[64,2048]{1,0:T(8,128)(2,1)S(1)}, bf16[64,2048]{1,0:T(8,128)(2,1)S(1)}, u32[]{:S(2)}, u32[]{:S(2)}) collective-permute-start(bf16[64,2048]{1,0:T(8,128)(2,1)S(1)} %fusion.24), channel_id=1, source_target_pairs={{0,8},{1,9},{2,10},{3,11},{4,12},{5,13},{6,14},{7,15},{8,0},{9,1},... | collective-permute-start | bytes 786440 | tf_op jit(solution)/shard_map/ppermute | solution.py:25
  145.3 7.7 %collective-permute-start.38 = (bf16[64,2048]{1,0:T(8,128)(2,1)S(1)}, bf16[64,2048]{1,0:T(8,128)(2,1)S(1)}, u32[]{:S(2)}, u32[]{:S(2)}) collective-permute-start(bf16[64,2048]{1,0:T(8,128)(2,1)S(1)} %fusion.43), channel_id=1, source_target_pairs={{0,4},{1,5},{2,6},{3,7},{4,0},{5,1},{6,2},{7,3},{8,12},{9,13},{10,... | collective-permute-start | bytes 786440 | tf_op jit(solution)/shard_map/ppermute | solution.py:25
  145.4 7.7 %collective-permute-start.32 = (bf16[64,2048]{1,0:T(8,128)(2,1)S(1)}, bf16[64,2048]{1,0:T(8,128)(2,1)S(1)}, u32[]{:S(2)}, u32[]{:S(2)}) collective-permute-start(bf16[64,2048]{1,0:T(8,128)(2,1)S(1)} %fusion.43), channel_id=1, source_target_pairs={{0,2},{1,3},{2,0},{3,1},{4,6},{5,7},{6,4},{7,5},{8,10},{9,11},{10,... | collective-permute-start | bytes 786440 | tf_op jit(solution)/shard_map/ppermute | solution.py:31
  147.0 6.7 %collective-permute-start.34 = (bf16[64,2048]{1,0:T(8,128)(2,1)S(1)}, bf16[64,2048]{1,0:T(8,128)(2,1)S(1)}, u32[]{:S(2)}, u32[]{:S(2)}) collective-permute-start(bf16[64,2048]{1,0:T(8,128)(2,1)S(1)} %fusion.43), channel_id=1, source_target_pairs={{4,8},{5,9},{6,10},{7,11},{8,4},{9,5},{10,6},{11,7},{20,24},{21,25... | collective-permute-start | bytes 786440 | tf_op jit(solution)/shard_map/ppermute | solution.py:25
  147.7 10.2 %collective-permute-start.35 = (bf16[64,2048]{1,0:T(8,128)(2,1)S(1)}, bf16[64,2048]{1,0:T(8,128)(2,1)S(1)}, u32[]{:S(2)}, u32[]{:S(2)}) collective-permute-start(bf16[64,2048]{1,0:T(8,128)(2,1)S(1)} %fusion.43), channel_id=1, source_target_pairs={{0,12},{1,13},{2,14},{3,15},{12,0},{13,1},{14,2},{15,3},{16,28},{1... | collective-permute-start | bytes 786440 | tf_op jit(solution)/shard_map/ppermute | solution.py:25
  153.1 7.0 %collective-permute-start.39 = (bf16[64,2048]{1,0:T(8,128)(2,1)S(1)}, bf16[64,2048]{1,0:T(8,128)(2,1)S(1)}, u32[]{:S(2)}, u32[]{:S(2)}) collective-permute-start(bf16[64,2048]{1,0:T(8,128)(2,1)S(1)} %collective-permute-done.38), channel_id=1, source_target_pairs={{4,8},{5,9},{6,10},{7,11},{8,4},{9,5},{10,6},{11,7},{20,24},{21,25... | collective-permute-start | bytes 786440 | tf_op jit(solution)/shard_map/ppermute | solution.py:25
  153.7 12.4 %collective-permute-start.40 = (bf16[64,2048]{1,0:T(8,128)(2,1)S(1)}, bf16[64,2048]{1,0:T(8,128)(2,1)S(1)}, u32[]{:S(2)}, u32[]{:S(2)}) collective-permute-start(bf16[64,2048]{1,0:T(8,128)(2,1)S(1)} %collective-permute-done.34), channel_id=1, source_target_pairs={{4,0},{5,1},{6,2},{7,3},{8,12},{9,13},{10,14},{11,15},{20,16},{21,... | collective-permute-start | bytes 786440 | tf_op jit(solution)/shard_map/ppermute | solution.py:25
  157.9 12.7 %collective-permute-start.36 = (bf16[64,2048]{1,0:T(8,128)(2,1)S(1)}, bf16[64,2048]{1,0:T(8,128)(2,1)S(1)}, u32[]{:S(2)}, u32[]{:S(2)}) collective-permute-start(bf16[64,2048]{1,0:T(8,128)(2,1)S(1)} %broadcast_select_fusion.3), channel_id=1, source_target_pairs={{0,2},{1,3},{2,0},{3,1},{4,6},{5,7},{6,4},{7,5},{8,10},{9,11},{10,... | collective-permute-start | bytes 786440 | tf_op jit(solution)/shard_map/ppermute | solution.py:31
  158.5 11.5 %collective-permute-start.41 = (bf16[64,2048]{1,0:T(8,128)(2,1)S(1)}, bf16[64,2048]{1,0:T(8,128)(2,1)S(1)}, u32[]{:S(2)}, u32[]{:S(2)}) collective-permute-start(bf16[64,2048]{1,0:T(8,128)(2,1)S(1)} %collective-permute-done.38), channel_id=1, source_target_pairs={{0,2},{1,3},{2,0},{3,1},{4,6},{5,7},{6,4},{7,5},{8,10},{9,11},{10,... | collective-permute-start | bytes 786440 | tf_op jit(solution)/shard_map/ppermute | solution.py:31
  170.8 8.8 %collective-permute-start.33 = (bf16[128,2048]{1,0:T(8,128)(2,1)S(1)}, bf16[128,2048]{1,0:T(8,128)(2,1)S(1)}, u32[]{:S(2)}, u32[]{:S(2)}) collective-permute-start(bf16[128,2048]{1,0:T(8,128)(2,1)S(1)} %pad_maximum_fusion.12), channel_id=1, source_target_pairs={{0,1},{1,0},{2,3},{3,2},{4,5},{5,4},{6,7},{7,6},{8,9},{9,8},{10,11... | collective-permute-start | bytes 1572872 | tf_op jit(solution)/shard_map/ppermute | solution.py:31
  171.4 8.3 %collective-permute-start.46 = (bf16[128,2048]{1,0:T(8,128)(2,1)S(1)}, bf16[128,2048]{1,0:T(8,128)(2,1)S(1)}, u32[]{:S(2)}, u32[]{:S(2)}) collective-permute-start(bf16[128,2048]{1,0:T(8,128)(2,1)S(1)} %pad_maximum_fusion.15), channel_id=1, source_target_pairs={{0,1},{1,0},{2,3},{3,2},{4,5},{5,4},{6,7},{7,6},{8,9},{9,8},{10,11... | collective-permute-start | bytes 1572872 | tf_op jit(solution)/shard_map/ppermute | solution.py:31
  182.5 8.7 %collective-permute-start.47 = (bf16[64,2048]{1,0:T(8,128)(2,1)S(1)}, bf16[64,2048]{1,0:T(8,128)(2,1)S(1)}, u32[]{:S(2)}, u32[]{:S(2)}) collective-permute-start(bf16[64,2048]{1,0:T(8,128)(2,1)S(1)} %slice.412), channel_id=1, source_target_pairs={{0,2},{1,3},{2,0},{3,1},{4,6},{5,7},{6,4},{7,5},{8,10},{9,11},{10,... | collective-permute-start | bytes 786440 | tf_op jit(solution)/shard_map/ppermute | solution.py:31
  184.1 11.4 %collective-permute-start.43 = (bf16[128,2048]{1,0:T(8,128)(2,1)S(1)}, bf16[128,2048]{1,0:T(8,128)(2,1)S(1)}, u32[]{:S(2)}, u32[]{:S(2)}) collective-permute-start(bf16[128,2048]{1,0:T(8,128)(2,1)S(1)} %slice.407), channel_id=1, source_target_pairs={{0,1},{1,0},{2,3},{3,2},{4,5},{5,4},{6,7},{7,6},{8,9},{9,8},{10,11... | collective-permute-start | bytes 1572872 | tf_op jit(solution)/shard_map/ppermute | solution.py:31
  186.3 10.2 %collective-permute-start.53 = (bf16[128,2048]{1,0:T(8,128)(2,1)S(1)}, bf16[128,2048]{1,0:T(8,128)(2,1)S(1)}, u32[]{:S(2)}, u32[]{:S(2)}) collective-permute-start(bf16[128,2048]{1,0:T(8,128)(2,1)S(1)} %slice.421), channel_id=1, source_target_pairs={{0,1},{1,0},{2,3},{3,2},{4,5},{5,4},{6,7},{7,6},{8,9},{9,8},{10,11... | collective-permute-start | bytes 1572872 | tf_op jit(solution)/shard_map/ppermute | solution.py:31
  193.4 20.9 %collective-permute-start.51 = (bf16[64,2048]{1,0:T(8,128)(2,1)S(1)}, bf16[64,2048]{1,0:T(8,128)(2,1)S(1)}, u32[]{:S(2)}, u32[]{:S(2)}) collective-permute-start(bf16[64,2048]{1,0:T(8,128)(2,1)S(1)} %add_convert_fusion.11), channel_id=1, source_target_pairs={{0,12},{1,13},{2,14},{3,15},{4,8},{5,9},{6,10},{7,11},{8,4},{9,5},... | collective-permute-start | bytes 786440 | tf_op jit(solution)/shard_map/ppermute | solution.py:25
  195.8 9.2 %collective-permute-start.49 = (bf16[64,2048]{1,0:T(8,128)(2,1)S(1)}, bf16[64,2048]{1,0:T(8,128)(2,1)S(1)}, u32[]{:S(2)}, u32[]{:S(2)}) collective-permute-start(bf16[64,2048]{1,0:T(8,128)(2,1)S(1)} %slice.417), channel_id=1, source_target_pairs={{0,2},{1,3},{2,0},{3,1},{4,6},{5,7},{6,4},{7,5},{8,10},{9,11},{10,... | collective-permute-start | bytes 786440 | tf_op jit(solution)/shard_map/ppermute | solution.py:31
  196.7 14.0 %collective-permute-start.54 = (bf16[64,2048]{1,0:T(8,128)(2,1)S(1)}, bf16[64,2048]{1,0:T(8,128)(2,1)S(1)}, u32[]{:S(2)}, u32[]{:S(2)}) collective-permute-start(bf16[64,2048]{1,0:T(8,128)(2,1)S(1)} %slice.423), channel_id=1, source_target_pairs={{0,2},{1,3},{2,0},{3,1},{4,6},{5,7},{6,4},{7,5},{8,10},{9,11},{10,... | collective-permute-start | bytes 786440 | tf_op jit(solution)/shard_map/ppermute | solution.py:31
  205.1 15.9 %collective-permute-start.52 = (bf16[64,2048]{1,0:T(8,128)(2,1)S(1)}, bf16[64,2048]{1,0:T(8,128)(2,1)S(1)}, u32[]{:S(2)}, u32[]{:S(2)}) collective-permute-start(bf16[64,2048]{1,0:T(8,128)(2,1)S(1)} %add_convert_fusion.10), channel_id=1, source_target_pairs={{0,8},{1,9},{2,10},{3,11},{4,12},{5,13},{6,14},{7,15},{8,0},{9,1},... | collective-permute-start | bytes 786440 | tf_op jit(solution)/shard_map/ppermute | solution.py:25
  209.5 11.5 %collective-permute-start.50 = (bf16[64,2048]{1,0:T(8,128)(2,1)S(1)}, bf16[64,2048]{1,0:T(8,128)(2,1)S(1)}, u32[]{:S(2)}, u32[]{:S(2)}) collective-permute-start(bf16[64,2048]{1,0:T(8,128)(2,1)S(1)} %slice.409), channel_id=1, source_target_pairs={{0,2},{1,3},{2,0},{3,1},{4,6},{5,7},{6,4},{7,5},{8,10},{9,11},{10,... | collective-permute-start | bytes 786440 | tf_op jit(solution)/shard_map/ppermute | solution.py:31
  210.8 13.4 %collective-permute-start.55 = (bf16[64,2048]{1,0:T(8,128)(2,1)S(1)}, bf16[64,2048]{1,0:T(8,128)(2,1)S(1)}, u32[]{:S(2)}, u32[]{:S(2)}) collective-permute-start(bf16[64,2048]{1,0:T(8,128)(2,1)S(1)} %add_convert_fusion.9), channel_id=1, source_target_pairs={{0,4},{1,5},{2,6},{3,7},{4,0},{5,1},{6,2},{7,3},{8,12},{9,13},{10,... | collective-permute-start | bytes 786440 | tf_op jit(solution)/shard_map/ppermute | solution.py:25
  (18 other events, 221.4 us)

commit v9 on v8

--- a/solution.py
+++ b/solution.py
@@ -93,38 +93,44 @@
     far = ring.send(columns[1], [(1, 2), (2, 1)])
     columns[3] = jnp.where(ring.inside, middle, ends)
     columns[2] = jnp.where(ring.inside, far, near)
-    crossed[1] = ring.across(after(columns[1], crossed[0]), top)
-    crossed[3] = ring.across(after(columns[3], crossed[0]), top)
-    crossed[2] = ring.across(after(columns[2], crossed[1]), top)
-
-    chunks = {}
-    for slot in (3, 0, 1, 2):
-        chunks[slot] = jnp.concatenate([columns[slot], crossed[slot]], axis=0)
+    crossed[1] = ring.across(after(columns[1], middle), top)
+    crossed[3] = ring.across(columns[3], top)
+    crossed[2] = ring.across(columns[2], top)
+
+    def chunk(slot, *ties):
+        values = after(jnp.concatenate([columns[slot], crossed[slot]], axis=0), *ties)
         for bit in ring.bits[1:]:
-            chunks[slot] = jnp.concatenate([chunks[slot], ring.across(chunks[slot], bit)], axis=0)
+            values = jnp.concatenate([values, ring.across(values, bit)], axis=0)
+        return values
 
     own = rows.shape[0]
     halves = {}
     back = {}
 
-    def turn(slot, *ties):
-        done = work(slot, after(chunks[slot], *ties))
+    def turn(slot, rows, *ties):
+        done = work(slot, after(rows, *ties))
         halves[slot] = within_plane(ring, done)
         return done
 
-    turn(3, columns[2], crossed[1], crossed[3])
-    back[3] = ring.across(halves[3][own:], top)
-    second = turn(1, turn(0, halves[3]))
-    turn(2, second, back[3])
-    back[2] = ring.across(halves[2][own:], top)
-    back[1] = ring.across(after(halves[1][own:], halves[2]), top)
-    back[0] = ring.across(after(halves[0][own:], halves[2], back[2]), top)
-    sums = plane_sums(ring, lambda slot: add(halves[slot][:own], back[slot]))
-    return sums, columns[2]
-
-
-def shared_weight(ring, weight):
-    other = ring.between(weight, 1)
+    def swap(slot, *ties):
+        back[slot] = ring.across(after(halves[slot][own:], *ties), top)
+        parts[slot] = add(halves[slot][:own], back[slot])
+
+    parts = {}
+    last = [columns[2], crossed[1], crossed[3]]
+    for slot in (3, 0, 1):
+        last = [turn(slot, chunk(slot), *last)]
+    turn(2, chunk(2, *last), halves[3])
+    swap(3)
+    swap(2)
+    swap(1, halves[2], back[3])
+    swap(0, halves[2], back[2])
+    sums = plane_sums(ring, lambda slot: parts[slot])
+    return sums, columns[2], back[0]
+
+
+def shared_weight(ring, weight, *ties):
+    other = after(ring.between(weight, 1), *ties)
     held = jnp.where(ring.z % 2 == 1, jnp.stack([other, weight]), jnp.stack([weight, other]))
     for i, bit in enumerate(ring.bits[1:]):
         other = ring.across(held, bit)
@@ -181,13 +187,13 @@
     def second_work(slot, chunk):
         return expert(chunk, second_columns[slot], second_gate_up[0], second_down[0])
 
-    first, gathered = routed(ring, jnp.concatenate([hidden_rows, lanes], axis=1), first_work)
-    weight = shared_weight(ring, after(merge_weight, gathered))
+    first, gathered, summed = routed(ring, jnp.concatenate([hidden_rows, lanes], axis=1), first_work)
+    weight = shared_weight(ring, after(merge_weight, gathered), summed)
     after_first = (hidden_rows.astype(jnp.float32) + first).astype(jnp.bfloat16)
     merged_in = jnp.concatenate([normed(after_first, hidden_gain), normed(token_embed, embed_gain)], axis=1)
     merged = merge(ring, merged_in, weight)
     after_merge = (after_first.astype(jnp.float32) + jax.nn.silu(merged)).astype(jnp.bfloat16)
-    second, _ = routed(ring, after_merge, second_work)
+    second, _, _ = routed(ring, after_merge, second_work)
     return (after_merge.astype(jnp.float32) + second).astype(jnp.bfloat16)
 
 

time: 226 us -> 214 us (0.947)
  waiting for transfers between devices: 127 us -> 114 us
  starting transfers between devices: 61.5 us -> 53.1 us
  local copies, waits for them, and re-layouts: 2.82 us -> 7 us
  other arithmetic: 12.6 us -> 15.9 us
    ppermute x38, waiting for transfers between devices: 62.1 us -> 49.2 us  [across(): lax.ppermute(values, 'inner', [(d, d ^ bit) for d in range(self.size)])]
    ppermute x18, starting transfers between devices: 34.3 us -> 23.1 us  [send(): return lax.ppermute(values, 'inner', perm)]
    concatenate x16, other arithmetic: 1.06 us -> 4.04 us  [the longest x8 2.09 us: chunk(): jnp.concatenate([columns[slot], crossed[slot]], axis=0)]
    slice x8, local copies, waits for them, and re-layouts: 0.33 us -> 3.19 us  [within_plane(): chunk = add(chunk[:rows], ring.across(chunk[rows:], bit))]
    ppermute x38, starting transfers between devices: 27.2 us -> 30 us  [across(): lax.ppermute(values, 'inner', [(d, d ^ bit) for d in range(self.size)])]
  transfers between devices with their start and end apart: 56 -> 56, of which waited for: 27 -> 27; matrix products, arithmetic and copies ran while one was open for 11% -> 15% of each run, Pallas kernels for 0% -> 0%
where the time goes in v9:
time: 214 us; the launch traced here: 213 us
  waiting for transfers between devices  114 us (53%)
  starting transfers between devices  53.1 us (25%)
  matrix products  21.7 us (10%)
  other arithmetic  15.9 us (7%)
  local copies, waits for them, and re-layouts  7 us (3%)
    ppermute x18, waiting for transfers between devices, send(): return lax.ppermute(values, 'inner', perm)  65 us
    ppermute x38, waiting for transfers between devices, across(): lax.ppermute(values, 'inner', [(d, d ^ bit) for d in range(self.size)])  49.2 us
    ppermute x38, starting transfers between devices, across(): lax.ppermute(values, 'inner', [(d, d ^ bit) for d in range(self.size)])  30 us
    ppermute x18, starting transfers between devices, send(): return lax.ppermute(values, 'inner', perm)  23.1 us
    dot_general x8, matrix products, expert(): projected = jnp.dot(rows, gate_up, preferred_element_type=jnp.float32)  10.3 us
    dot_general x8, matrix products, expert(): out = jnp.dot(hidden, down, preferred_element_type=jnp.float32)  8.06 us
  transfers between devices with their start and end apart: 56, of which 27 were waited for; matrix products, arithmetic and copies ran while one was open for 15% of the time, Pallas kernels for 0%

profile of v9, /device:TPU:0, one launch (start us, length us, event | category | flops | bytes accessed | tf_op | source)
XLA Modules:
  0.0 212.9 jit_solution(14152092294416633037)
XLA Ops:
  3.4 7.0 %collective-permute-start.3 = (bf16[64,2176]{1,0:T(8,128)(2,1)S(1)}, bf16[64,2176]{1,0:T(8,128)(2,1)S(1)}, u32[]{:S(2)}, u32[]{:S(2)}) collective-permute-start(bf16[64,2176]{1,0:T(8,128)(2,1)S(1)} %pad_maximum_fusion.16), channel_id=1, source_target_pairs={{0,12},{1,13},{2,14},{3,15},{12,0},{13,1},{14,2},{15,3},{16,28},{1... | collective-permute-start | bytes 835592 | tf_op jit(solution)/shard_map/ppermute | solution.py:25
  11.1 1.6 collective-permute-start
  13.8 4.1 %collective-permute-done.3 = bf16[64,2176]{1,0:T(8,128)(2,1)S(1)} collective-permute-done((bf16[64,2176]{1,0:T(8,128)(2,1)S(1)}, bf16[64,2176]{1,0:T(8,128)(2,1)S(1)}, u32[]{:S(2)}, u32[]{:S(2)}) %collective-permute-start.3) | collective-permute-done | bytes 278560 | tf_op jit(solution)/shard_map/ppermute | solution.py:25
  18.0 1.8 collective-permute-start.4
  19.7 3.3 %collective-permute-done.6 = bf16[64,2176]{1,0:T(8,128)(2,1)S(1)} collective-permute-done((bf16[64,2176]{1,0:T(8,128)(2,1)S(1)}, bf16[64,2176]{1,0:T(8,128)(2,1)S(1)}, u32[]{:S(2)}, u32[]{:S(2)}) %collective-permute-start.6) | collective-permute-done | bytes 278560 | tf_op jit(solution)/shard_map/ppermute | solution.py:25
  23.1 1.5 collective-permute-start.9
  24.6 1.3 collective-permute-start.8
  27.6 7.1 %collective-permute-done.8 = bf16[64,2176]{1,0:T(8,128)(2,1)S(1)} collective-permute-done((bf16[64,2176]{1,0:T(8,128)(2,1)S(1)}, bf16[64,2176]{1,0:T(8,128)(2,1)S(1)}, u32[]{:S(2)}, u32[]{:S(2)}) %collective-permute-start.8) | collective-permute-done | bytes 278560 | tf_op jit(solution)/shard_map/ppermute | solution.py:25
  36.1 6.3 %collective-permute-done.11 = bf16[64,2176]{1,0:T(8,128)(2,1)S(1)} collective-permute-done((bf16[64,2176]{1,0:T(8,128)(2,1)S(1)}, bf16[64,2176]{1,0:T(8,128)(2,1)S(1)}, u32[]{:S(2)}, u32[]{:S(2)}) %collective-permute-start.11) | collective-permute-done | bytes 278560 | tf_op jit(solution)/shard_map/ppermute | solution.py:31
  43.6 1.7 copy-done.11
  45.4 1.3 fusion.14
  47.4 1.3 fusion.12
  49.0 1.7 fusion.17
  51.1 1.3 fusion.10
  53.3 1.8 fusion.18
  55.6 3.4 %collective-permute-start.24 = (bf16[256,2048]{1,0:T(8,128)(2,1)S(1)}, bf16[256,2048]{1,0:T(8,128)(2,1)S(1)}, u32[]{:S(2)}, u32[]{:S(2)}) collective-permute-start(bf16[256,2048]{1,0:T(8,128)(2,1)S(1)} %copy-done.2), channel_id=1, source_target_pairs={{0,4},{1,5},{2,6},{3,7},{4,0},{5,1},{6,2},{7,3},{8,12},{9,13},{10,... | collective-permute-start | bytes 3145736 | tf_op jit(solution)/shard_map/ppermute | solution.py:25
  61.8 1.5 add_convert_fusion.6
  63.8 1.3 pad_maximum_fusion.3
  65.2 1.3 fusion.8
  69.7 1.6 collective-permute-start.16
  73.1 5.8 %collective-permute-done.16 = bf16[64,2048]{1,0:T(8,128)(2,1)S(1)} collective-permute-done((bf16[64,2048]{1,0:T(8,128)(2,1)S(1)}, bf16[64,2048]{1,0:T(8,128)(2,1)S(1)}, u32[]{:S(2)}, u32[]{:S(2)}) %collective-permute-start.16) | collective-permute-done | bytes 262176 | tf_op jit(solution)/shard_map/ppermute | solution.py:31
  79.1 1.6 collective-permute-start.17
  80.7 3.9 %collective-permute-done.22 = bf16[64,2048]{1,0:T(8,128)(2,1)S(1)} collective-permute-done((bf16[64,2048]{1,0:T(8,128)(2,1)S(1)}, bf16[64,2048]{1,0:T(8,128)(2,1)S(1)}, u32[]{:S(2)}, u32[]{:S(2)}) %collective-permute-start.22) | collective-permute-done | bytes 262176 | tf_op jit(solution)/shard_map/ppermute | solution.py:31
  84.8 5.6 %collective-permute-done.24 = bf16[256,2048]{1,0:T(8,128)(2,1)S(1)} collective-permute-done((bf16[256,2048]{1,0:T(8,128)(2,1)S(1)}, bf16[256,2048]{1,0:T(8,128)(2,1)S(1)}, u32[]{:S(2)}, u32[]{:S(2)}) %collective-permute-start.24) | collective-permute-done | bytes 1048608 | tf_op jit(solution)/shard_map/ppermute | solution.py:25
  91.5 6.6 %collective-permute-done.20 = bf16[64,2048]{1,0:T(8,128)(2,1)S(1)} collective-permute-done((bf16[64,2048]{1,0:T(8,128)(2,1)S(1)}, bf16[64,2048]{1,0:T(8,128)(2,1)S(1)}, u32[]{:S(2)}, u32[]{:S(2)}) %collective-permute-start.20) | collective-permute-done | bytes 262176 | tf_op jit(solution)/shard_map/ppermute | solution.py:25
  101.9 2.8 %collective-permute-start.29 = (bf16[64,1024]{1,0:T(8,128)(2,1)S(1)}, bf16[64,1024]{1,0:T(8,128)(2,1)S(1)}, u32[]{:S(2)}, u32[]{:S(2)}) collective-permute-start(bf16[64,1024]{1,0:T(8,128)(2,1)S(1)} %pad_maximum_fusion.19), channel_id=1, source_target_pairs={{0,10},{1,11},{2,8},{3,9},{4,14},{5,15},{6,12},{7,13},{8,2},{9,3},... | collective-permute-start | bytes 393224 | tf_op jit(solution)/shard_map/ppermute | solution.py:31
  105.1 7.5 %collective-permute-done.28 = bf16[64,1024]{1,0:T(8,128)(2,1)S(1)} collective-permute-done((bf16[64,1024]{1,0:T(8,128)(2,1)S(1)}, bf16[64,1024]{1,0:T(8,128)(2,1)S(1)}, u32[]{:S(2)}, u32[]{:S(2)}) %collective-permute-start.28) | collective-permute-done | bytes 131104 | tf_op jit(solution)/shard_map/ppermute | solution.py:31
  115.3 2.1 collective-permute-start.30
  118.3 6.3 %collective-permute-done.30 = bf16[64,2048]{1,0:T(8,128)(2,1)S(1)} collective-permute-done((bf16[64,2048]{1,0:T(8,128)(2,1)S(1)}, bf16[64,2048]{1,0:T(8,128)(2,1)S(1)}, u32[]{:S(2)}, u32[]{:S(2)}) %collective-permute-start.30) | collective-permute-done | bytes 262176 | tf_op jit(solution)/shard_map/ppermute | solution.py:31
  126.4 2.1 collective-permute-done.27
  128.5 8.1 %collective-permute-done.31 = bf16[64,2048]{1,0:T(8,128)(2,1)S(1)} collective-permute-done((bf16[64,2048]{1,0:T(8,128)(2,1)S(1)}, bf16[64,2048]{1,0:T(8,128)(2,1)S(1)}, u32[]{:S(2)}, u32[]{:S(2)}) %collective-permute-start.31) | collective-permute-done | bytes 262176 | tf_op jit(solution)/shard_map/ppermute | solution.py:25
  136.8 3.4 %collective-permute-start.35 = (bf16[64,2048]{1,0:T(8,128)(2,1)S(1)}, bf16[64,2048]{1,0:T(8,128)(2,1)S(1)}, u32[]{:S(2)}, u32[]{:S(2)}) collective-permute-start(bf16[64,2048]{1,0:T(8,128)(2,1)S(1)} %fusion.43), channel_id=1, source_target_pairs={{0,12},{1,13},{2,14},{3,15},{12,0},{13,1},{14,2},{15,3},{16,28},{1... | collective-permute-start | bytes 786440 | tf_op jit(solution)/shard_map/ppermute | solution.py:25
  141.0 1.5 collective-permute-start.32
  142.5 7.2 %collective-permute-done.35 = bf16[64,2048]{1,0:T(8,128)(2,1)S(1)} collective-permute-done((bf16[64,2048]{1,0:T(8,128)(2,1)S(1)}, bf16[64,2048]{1,0:T(8,128)(2,1)S(1)}, u32[]{:S(2)}, u32[]{:S(2)}) %collective-permute-start.35) | collective-permute-done | bytes 262176 | tf_op jit(solution)/shard_map/ppermute | solution.py:25
  149.8 1.3 collective-permute-start.36
  151.0 2.2 %collective-permute-done.38 = bf16[64,2048]{1,0:T(8,128)(2,1)S(1)} collective-permute-done((bf16[64,2048]{1,0:T(8,128)(2,1)S(1)}, bf16[64,2048]{1,0:T(8,128)(2,1)S(1)}, u32[]{:S(2)}, u32[]{:S(2)}) %collective-permute-start.38) | collective-permute-done | bytes 262176 | tf_op jit(solution)/shard_map/ppermute | solution.py:25
  154.9 1.3 collective-permute-start.40
  157.1 7.2 %collective-permute-done.40 = bf16[64,2048]{1,0:T(8,128)(2,1)S(1)} collective-permute-done((bf16[64,2048]{1,0:T(8,128)(2,1)S(1)}, bf16[64,2048]{1,0:T(8,128)(2,1)S(1)}, u32[]{:S(2)}, u32[]{:S(2)}) %collective-permute-start.40) | collective-permute-done | bytes 262176 | tf_op jit(solution)/shard_map/ppermute | solution.py:25
  166.1 4.6 %collective-permute-done.43 = bf16[64,2048]{1,0:T(8,128)(2,1)S(1)} collective-permute-done((bf16[64,2048]{1,0:T(8,128)(2,1)S(1)}, bf16[64,2048]{1,0:T(8,128)(2,1)S(1)}, u32[]{:S(2)}, u32[]{:S(2)}) %collective-permute-start.43) | collective-permute-done | bytes 262176 | tf_op jit(solution)/shard_map/ppermute | solution.py:31
  175.6 1.3 fusion.2
  180.2 1.3 fusion
  182.8 1.5 collective-permute-done.47
  185.5 1.9 collective-permute-done.50
  187.5 1.9 collective-permute-start.51
  189.3 1.9 collective-permute-start.54
  191.3 2.4 %collective-permute-done.48 = bf16[64,2048]{1,0:T(8,128)(2,1)S(1)} collective-permute-done((bf16[64,2048]{1,0:T(8,128)(2,1)S(1)}, bf16[64,2048]{1,0:T(8,128)(2,1)S(1)}, u32[]{:S(2)}, u32[]{:S(2)}) %collective-permute-start.48) | collective-permute-done | bytes 262176 | tf_op jit(solution)/shard_map/ppermute | solution.py:31
  195.1 4.2 %collective-permute-done.54 = bf16[64,2048]{1,0:T(8,128)(2,1)S(1)} collective-permute-done((bf16[64,2048]{1,0:T(8,128)(2,1)S(1)}, bf16[64,2048]{1,0:T(8,128)(2,1)S(1)}, u32[]{:S(2)}, u32[]{:S(2)}) %collective-permute-start.54) | collective-permute-done | bytes 262176 | tf_op jit(solution)/shard_map/ppermute | solution.py:31
  199.5 11.4 %collective-permute-done.52 = bf16[64,2048]{1,0:T(8,128)(2,1)S(1)} collective-permute-done((bf16[64,2048]{1,0:T(8,128)(2,1)S(1)}, bf16[64,2048]{1,0:T(8,128)(2,1)S(1)}, u32[]{:S(2)}, u32[]{:S(2)}) %collective-permute-start.52) | collective-permute-done | bytes 262176 | tf_op jit(solution)/shard_map/ppermute | solution.py:25
  (190 shorter events, 51.1 us)
Async XLA Ops:
  3.4 14.5 %collective-permute-start.3 = (bf16[64,2176]{1,0:T(8,128)(2,1)S(1)}, bf16[64,2176]{1,0:T(8,128)(2,1)S(1)}, u32[]{:S(2)}, u32[]{:S(2)}) collective-permute-start(bf16[64,2176]{1,0:T(8,128)(2,1)S(1)} %pad_maximum_fusion.16), channel_id=1, source_target_pairs={{0,12},{1,13},{2,14},{3,15},{12,0},{13,1},{14,2},{15,3},{16,28},{1... | collective-permute-start | bytes 835592 | tf_op jit(solution)/shard_map/ppermute | solution.py:25
  10.4 7.6 %collective-permute-start.2 = (bf16[64,2176]{1,0:T(8,128)(2,1)S(1)}, bf16[64,2176]{1,0:T(8,128)(2,1)S(1)}, u32[]{:S(2)}, u32[]{:S(2)}) collective-permute-start(bf16[64,2176]{1,0:T(8,128)(2,1)S(1)} %pad_maximum_fusion.16), channel_id=1, source_target_pairs={{4,8},{5,9},{6,10},{7,11},{8,4},{9,5},{10,6},{11,7},{20,24},{21,25... | collective-permute-start | bytes 835592 | tf_op jit(solution)/shard_map/ppermute | solution.py:25
  11.0 12.0 %collective-permute-start.6 = (bf16[64,2176]{1,0:T(8,128)(2,1)S(1)}, bf16[64,2176]{1,0:T(8,128)(2,1)S(1)}, u32[]{:S(2)}, u32[]{:S(2)}) collective-permute-start(bf16[64,2176]{1,0:T(8,128)(2,1)S(1)} %pad_maximum_fusion.16), channel_id=1, source_target_pairs={{0,4},{1,5},{2,6},{3,7},{4,0},{5,1},{6,2},{7,3},{8,12},{9,13},{10,... | collective-permute-start | bytes 835592 | tf_op jit(solution)/shard_map/ppermute | solution.py:25
  11.1 15.4 %collective-permute-start = (bf16[64,2176]{1,0:T(8,128)(2,1)S(1)}, bf16[64,2176]{1,0:T(8,128)(2,1)S(1)}, u32[]{:S(2)}, u32[]{:S(2)}) collective-permute-start(bf16[64,2176]{1,0:T(8,128)(2,1)S(1)} %pad_maximum_fusion.16), channel_id=1, source_target_pairs={{0,2},{1,3},{2,0},{3,1},{4,6},{5,7},{6,4},{7,5},{8,10},{9,11},{10,... | collective-permute-start | bytes 835592 | tf_op jit(solution)/shard_map/ppermute | solution.py:31
  18.0 16.9 %collective-permute-start.4 = (bf16[64,2176]{1,0:T(8,128)(2,1)S(1)}, bf16[64,2176]{1,0:T(8,128)(2,1)S(1)}, u32[]{:S(2)}, u32[]{:S(2)}) collective-permute-start(bf16[64,2176]{1,0:T(8,128)(2,1)S(1)} %broadcast_select_fusion.1), channel_id=1, source_target_pairs={{0,2},{1,3},{2,0},{3,1},{4,6},{5,7},{6,4},{7,5},{8,10},{9,11},{10,... | collective-permute-start | bytes 835592 | tf_op jit(solution)/shard_map/ppermute | solution.py:31
  23.1 12.4 %collective-permute-start.9 = (bf16[64,2176]{1,0:T(8,128)(2,1)S(1)}, bf16[64,2176]{1,0:T(8,128)(2,1)S(1)}, u32[]{:S(2)}, u32[]{:S(2)}) collective-permute-start(bf16[64,2176]{1,0:T(8,128)(2,1)S(1)} %collective-permute-done.6), channel_id=1, source_target_pairs={{0,2},{1,3},{2,0},{3,1},{4,6},{5,7},{6,4},{7,5},{8,10},{9,11},{10,... | collective-permute-start | bytes 835592 | tf_op jit(solution)/shard_map/ppermute | solution.py:31
  24.6 10.2 %collective-permute-start.8 = (bf16[64,2176]{1,0:T(8,128)(2,1)S(1)}, bf16[64,2176]{1,0:T(8,128)(2,1)S(1)}, u32[]{:S(2)}, u32[]{:S(2)}) collective-permute-start(bf16[64,2176]{1,0:T(8,128)(2,1)S(1)} %collective-permute-done.2), channel_id=1, source_target_pairs={{4,0},{5,1},{6,2},{7,3},{8,12},{9,13},{10,14},{11,15},{20,16},{21,... | collective-permute-start | bytes 835592 | tf_op jit(solution)/shard_map/ppermute | solution.py:25
  25.9 8.9 %collective-permute-start.7 = (bf16[64,2176]{1,0:T(8,128)(2,1)S(1)}, bf16[64,2176]{1,0:T(8,128)(2,1)S(1)}, u32[]{:S(2)}, u32[]{:S(2)}) collective-permute-start(bf16[64,2176]{1,0:T(8,128)(2,1)S(1)} %collective-permute-done.6), channel_id=1, source_target_pairs={{4,8},{5,9},{6,10},{7,11},{8,4},{9,5},{10,6},{11,7},{20,24},{21,25... | collective-permute-start | bytes 835592 | tf_op jit(solution)/shard_map/ppermute | solution.py:25
  27.6 15.6 %collective-permute-start.1 = (bf16[128,2176]{1,0:T(8,128)(2,1)S(1)}, bf16[128,2176]{1,0:T(8,128)(2,1)S(1)}, u32[]{:S(2)}, u32[]{:S(2)}) collective-permute-start(bf16[128,2176]{1,0:T(8,128)(2,1)S(1)} %pad_maximum_fusion.8), channel_id=1, source_target_pairs={{0,1},{1,0},{2,3},{3,2},{4,5},{5,4},{6,7},{7,6},{8,9},{9,8},{10,11... | collective-permute-start | bytes 1671176 | tf_op jit(solution)/shard_map/ppermute | solution.py:31
  34.9 7.5 %collective-permute-start.11 = (bf16[64,2176]{1,0:T(8,128)(2,1)S(1)}, bf16[64,2176]{1,0:T(8,128)(2,1)S(1)}, u32[]{:S(2)}, u32[]{:S(2)}) collective-permute-start(bf16[64,2176]{1,0:T(8,128)(2,1)S(1)} %broadcast_select_fusion), channel_id=1, source_target_pairs={{0,2},{1,3},{2,0},{3,1},{4,6},{5,7},{6,4},{7,5},{8,10},{9,11},{10,... | collective-permute-start | bytes 835592 | tf_op jit(solution)/shard_map/ppermute | solution.py:31
  35.5 15.3 %collective-permute-start.12 = (bf16[128,2176]{1,0:T(8,128)(2,1)S(1)}, bf16[128,2176]{1,0:T(8,128)(2,1)S(1)}, u32[]{:S(2)}, u32[]{:S(2)}) collective-permute-start(bf16[128,2176]{1,0:T(8,128)(2,1)S(1)} %pad_maximum_fusion.11), channel_id=1, source_target_pairs={{0,1},{1,0},{2,3},{3,2},{4,5},{5,4},{6,7},{7,6},{8,9},{9,8},{10,11... | collective-permute-start | bytes 1671176 | tf_op jit(solution)/shard_map/ppermute | solution.py:31
  35.6 7.7 %collective-permute-start.5 = (bf16[128,2176]{1,0:T(8,128)(2,1)S(1)}, bf16[128,2176]{1,0:T(8,128)(2,1)S(1)}, u32[]{:S(2)}, u32[]{:S(2)}) collective-permute-start(bf16[128,2176]{1,0:T(8,128)(2,1)S(1)} %pad_maximum_fusion.9), channel_id=1, source_target_pairs={{0,1},{1,0},{2,3},{3,2},{4,5},{5,4},{6,7},{7,6},{8,9},{9,8},{10,11... | collective-permute-start | bytes 1671176 | tf_op jit(solution)/shard_map/ppermute | solution.py:31
  53.3 8.5 %collective-permute-start.14 = (bf16[128,2048]{1,0:T(8,128)(2,1)}, bf16[128,2048]{1,0:T(8,128)(2,1)}, u32[]{:S(2)}, u32[]{:S(2)}) collective-permute-start(bf16[128,2048]{1,0:T(8,128)(2,1)} %slice.387), channel_id=1, source_target_pairs={{0,1},{1,0},{2,3},{3,2},{4,5},{5,4},{6,7},{7,6},{8,9},{9,8},{10,11... | collective-permute-start | bytes 1572872 | tf_op jit(solution)/shard_map/ppermute | solution.py:31
  55.1 8.8 %collective-permute-start.13 = (bf16[128,2176]{1,0:T(8,128)(2,1)}, bf16[128,2176]{1,0:T(8,128)(2,1)}, u32[]{:S(2)}, u32[]{:S(2)}) collective-permute-start(bf16[128,2176]{1,0:T(8,128)(2,1)} %pad_maximum_fusion.10), channel_id=1, source_target_pairs={{0,1},{1,0},{2,3},{3,2},{4,5},{5,4},{6,7},{7,6},{8,9},{9,8},{10,11... | collective-permute-start | bytes 1671176 | tf_op jit(solution)/shard_map/ppermute | solution.py:31
  55.6 34.8 %collective-permute-start.24 = (bf16[256,2048]{1,0:T(8,128)(2,1)S(1)}, bf16[256,2048]{1,0:T(8,128)(2,1)S(1)}, u32[]{:S(2)}, u32[]{:S(2)}) collective-permute-start(bf16[256,2048]{1,0:T(8,128)(2,1)S(1)} %copy-done.2), channel_id=1, source_target_pairs={{0,4},{1,5},{2,6},{3,7},{4,0},{5,1},{6,2},{7,3},{8,12},{9,13},{10,... | collective-permute-start | bytes 3145736 | tf_op jit(solution)/shard_map/ppermute | solution.py:25
  61.2 6.5 %collective-permute-start.10 = (bf16[128,2048]{1,0:T(8,128)(2,1)S(1)}, bf16[128,2048]{1,0:T(8,128)(2,1)S(1)}, u32[]{:S(2)}, u32[]{:S(2)}) collective-permute-start(bf16[128,2048]{1,0:T(8,128)(2,1)S(1)} %slice.381), channel_id=1, source_target_pairs={{0,1},{1,0},{2,3},{3,2},{4,5},{5,4},{6,7},{7,6},{8,9},{9,8},{10,11... | collective-permute-start | bytes 1572872 | tf_op jit(solution)/shard_map/ppermute | solution.py:31
  61.3 6.9 %collective-permute-start.21 = (bf16[128,2048]{1,0:T(8,128)(2,1)S(1)}, bf16[128,2048]{1,0:T(8,128)(2,1)S(1)}, u32[]{:S(2)}, u32[]{:S(2)}) collective-permute-start(bf16[128,2048]{1,0:T(8,128)(2,1)S(1)} %slice.397), channel_id=1, source_target_pairs={{0,1},{1,0},{2,3},{3,2},{4,5},{5,4},{6,7},{7,6},{8,9},{9,8},{10,11... | collective-permute-start | bytes 1572872 | tf_op jit(solution)/shard_map/ppermute | solution.py:31
  63.3 8.4 %collective-permute-start.18 = (bf16[64,2048]{1,0:T(8,128)(2,1)S(1)}, bf16[64,2048]{1,0:T(8,128)(2,1)S(1)}, u32[]{:S(2)}, u32[]{:S(2)}) collective-permute-start(bf16[64,2048]{1,0:T(8,128)(2,1)S(1)} %slice.394), channel_id=1, source_target_pairs={{0,2},{1,3},{2,0},{3,1},{4,6},{5,7},{6,4},{7,5},{8,10},{9,11},{10,... | collective-permute-start | bytes 786440 | tf_op jit(solution)/shard_map/ppermute | solution.py:31
  69.7 9.2 %collective-permute-start.16 = (bf16[64,2048]{1,0:T(8,128)(2,1)S(1)}, bf16[64,2048]{1,0:T(8,128)(2,1)S(1)}, u32[]{:S(2)}, u32[]{:S(2)}) collective-permute-start(bf16[64,2048]{1,0:T(8,128)(2,1)S(1)} %slice.392), channel_id=1, source_target_pairs={{0,2},{1,3},{2,0},{3,1},{4,6},{5,7},{6,4},{7,5},{8,10},{9,11},{10,... | collective-permute-start | bytes 786440 | tf_op jit(solution)/shard_map/ppermute | solution.py:31
  71.7 19.7 %collective-permute-start.19 = (bf16[64,2048]{1,0:T(8,128)(2,1)S(1)}, bf16[64,2048]{1,0:T(8,128)(2,1)S(1)}, u32[]{:S(2)}, u32[]{:S(2)}) collective-permute-start(bf16[64,2048]{1,0:T(8,128)(2,1)S(1)} %add_convert_fusion.16), channel_id=1, source_target_pairs={{0,12},{1,13},{2,14},{3,15},{4,8},{5,9},{6,10},{7,11},{8,4},{9,5},... | collective-permute-start | bytes 786440 | tf_op jit(solution)/shard_map/ppermute | solution.py:25
  72.6 12.0 %collective-permute-start.22 = (bf16[64,2048]{1,0:T(8,128)(2,1)S(1)}, bf16[64,2048]{1,0:T(8,128)(2,1)S(1)}, u32[]{:S(2)}, u32[]{:S(2)}) collective-permute-start(bf16[64,2048]{1,0:T(8,128)(2,1)S(1)} %slice.399), channel_id=1, source_target_pairs={{0,2},{1,3},{2,0},{3,1},{4,6},{5,7},{6,4},{7,5},{8,10},{9,11},{10,... | collective-permute-start | bytes 786440 | tf_op jit(solution)/shard_map/ppermute | solution.py:31
  79.0 19.1 %collective-permute-start.20 = (bf16[64,2048]{1,0:T(8,128)(2,1)S(1)}, bf16[64,2048]{1,0:T(8,128)(2,1)S(1)}, u32[]{:S(2)}, u32[]{:S(2)}) collective-permute-start(bf16[64,2048]{1,0:T(8,128)(2,1)S(1)} %add_convert_fusion.15), channel_id=1, source_target_pairs={{0,8},{1,9},{2,10},{3,11},{4,12},{5,13},{6,14},{7,15},{8,0},{9,1},... | collective-permute-start | bytes 786440 | tf_op jit(solution)/shard_map/ppermute | solution.py:25
  79.1 11.3 %collective-permute-start.17 = (bf16[64,2048]{1,0:T(8,128)(2,1)S(1)}, bf16[64,2048]{1,0:T(8,128)(2,1)S(1)}, u32[]{:S(2)}, u32[]{:S(2)}) collective-permute-start(bf16[64,2048]{1,0:T(8,128)(2,1)S(1)} %slice.383), channel_id=1, source_target_pairs={{0,2},{1,3},{2,0},{3,1},{4,6},{5,7},{6,4},{7,5},{8,10},{9,11},{10,... | collective-permute-start | bytes 786440 | tf_op jit(solution)/shard_map/ppermute | solution.py:31
  84.6 14.6 %collective-permute-start.23 = (bf16[64,2048]{1,0:T(8,128)(2,1)S(1)}, bf16[64,2048]{1,0:T(8,128)(2,1)S(1)}, u32[]{:S(2)}, u32[]{:S(2)}) collective-permute-start(bf16[64,2048]{1,0:T(8,128)(2,1)S(1)} %add_convert_fusion.14), channel_id=1, source_target_pairs={{0,4},{1,5},{2,6},{3,7},{4,0},{5,1},{6,2},{7,3},{8,12},{9,13},{10,... | collective-permute-start | bytes 786440 | tf_op jit(solution)/shard_map/ppermute | solution.py:25
  90.7 23.0 %collective-permute-start.25 = (bf16[2,256,2048]{2,1,0:T(8,128)(2,1)S(1)}, bf16[2,256,2048]{2,1,0:T(8,128)(2,1)S(1)}, u32[]{:S(2)}, u32[]{:S(2)}) collective-permute-start(bf16[2,256,2048]{2,1,0:T(8,128)(2,1)S(1)} %maximum_select_fusion.1), channel_id=1, source_target_pairs={{0,1},{1,0},{2,3},{3,2},{4,5},{5,4},{6,7},{7,6},{8,9},{9,8},{10,11... | collective-permute-start | bytes 6291464 | tf_op jit(solution)/shard_map/ppermute | solution.py:31
  100.0 12.5 %collective-permute-start.28 = (bf16[64,1024]{1,0:T(8,128)(2,1)S(1)}, bf16[64,1024]{1,0:T(8,128)(2,1)S(1)}, u32[]{:S(2)}, u32[]{:S(2)}) collective-permute-start(bf16[64,1024]{1,0:T(8,128)(2,1)S(1)} %pad_maximum_fusion.18), channel_id=1, source_target_pairs={{0,8},{1,9},{2,10},{3,11},{4,12},{5,13},{6,14},{7,15},{8,0},{9,1},... | collective-permute-start | bytes 393224 | tf_op jit(solution)/shard_map/ppermute | solution.py:31
  101.2 11.4 %collective-permute-start.26 = (bf16[64,1024]{1,0:T(8,128)(2,1)S(1)}, bf16[64,1024]{1,0:T(8,128)(2,1)S(1)}, u32[]{:S(2)}, u32[]{:S(2)}) collective-permute-start(bf16[64,1024]{1,0:T(8,128)(2,1)S(1)} %pad_maximum_fusion.17), channel_id=1, source_target_pairs={{0,2},{1,3},{2,0},{3,1},{4,6},{5,7},{6,4},{7,5},{8,10},{9,11},{10,... | collective-permute-start | bytes 393224 | tf_op jit(solution)/shard_map/ppermute | solution.py:31
  101.9 11.8 %collective-permute-start.29 = (bf16[64,1024]{1,0:T(8,128)(2,1)S(1)}, bf16[64,1024]{1,0:T(8,128)(2,1)S(1)}, u32[]{:S(2)}, u32[]{:S(2)}) collective-permute-start(bf16[64,1024]{1,0:T(8,128)(2,1)S(1)} %pad_maximum_fusion.19), channel_id=1, source_target_pairs={{0,10},{1,11},{2,8},{3,9},{4,14},{5,15},{6,12},{7,13},{8,2},{9,3},... | collective-permute-start | bytes 393224 | tf_op jit(solution)/shard_map/ppermute | solution.py:31
  115.3 9.3 %collective-permute-start.30 = (bf16[64,2048]{1,0:T(8,128)(2,1)S(1)}, bf16[64,2048]{1,0:T(8,128)(2,1)S(1)}, u32[]{:S(2)}, u32[]{:S(2)}) collective-permute-start(bf16[64,2048]{1,0:T(8,128)(2,1)S(1)} %convolution_convert_fusion), channel_id=1, source_target_pairs={{0,2},{1,3},{2,0},{3,1},{4,6},{5,7},{6,4},{7,5},{8,10},{9,11},{10,... | collective-permute-start | bytes 786440 | tf_op jit(solution)/shard_map/ppermute | solution.py:31
  118.2 10.3 %collective-permute-start.27 = (bf16[64,2048]{1,0:T(8,128)(2,1)S(1)}, bf16[64,2048]{1,0:T(8,128)(2,1)S(1)}, u32[]{:S(2)}, u32[]{:S(2)}) collective-permute-start(bf16[64,2048]{1,0:T(8,128)(2,1)S(1)} %convolution_convert_fusion.1), channel_id=1, source_target_pairs={{0,2},{1,3},{2,0},{3,1},{4,6},{5,7},{6,4},{7,5},{8,10},{9,11},{10,... | collective-permute-start | bytes 786440 | tf_op jit(solution)/shard_map/ppermute | solution.py:31
  125.4 11.1 %collective-permute-start.31 = (bf16[64,2048]{1,0:T(8,128)(2,1)S(1)}, bf16[64,2048]{1,0:T(8,128)(2,1)S(1)}, u32[]{:S(2)}, u32[]{:S(2)}) collective-permute-start(bf16[64,2048]{1,0:T(8,128)(2,1)S(1)} %fusion.24), channel_id=1, source_target_pairs={{0,8},{1,9},{2,10},{3,11},{4,12},{5,13},{6,14},{7,15},{8,0},{9,1},... | collective-permute-start | bytes 786440 | tf_op jit(solution)/shard_map/ppermute | solution.py:25
  136.8 12.9 %collective-permute-start.35 = (bf16[64,2048]{1,0:T(8,128)(2,1)S(1)}, bf16[64,2048]{1,0:T(8,128)(2,1)S(1)}, u32[]{:S(2)}, u32[]{:S(2)}) collective-permute-start(bf16[64,2048]{1,0:T(8,128)(2,1)S(1)} %fusion.43), channel_id=1, source_target_pairs={{0,12},{1,13},{2,14},{3,15},{12,0},{13,1},{14,2},{15,3},{16,28},{1... | collective-permute-start | bytes 786440 | tf_op jit(solution)/shard_map/ppermute | solution.py:25
  140.2 9.5 %collective-permute-start.34 = (bf16[64,2048]{1,0:T(8,128)(2,1)S(1)}, bf16[64,2048]{1,0:T(8,128)(2,1)S(1)}, u32[]{:S(2)}, u32[]{:S(2)}) collective-permute-start(bf16[64,2048]{1,0:T(8,128)(2,1)S(1)} %fusion.43), channel_id=1, source_target_pairs={{4,8},{5,9},{6,10},{7,11},{8,4},{9,5},{10,6},{11,7},{20,24},{21,25... | collective-permute-start | bytes 786440 | tf_op jit(solution)/shard_map/ppermute | solution.py:25
  140.9 12.3 %collective-permute-start.38 = (bf16[64,2048]{1,0:T(8,128)(2,1)S(1)}, bf16[64,2048]{1,0:T(8,128)(2,1)S(1)}, u32[]{:S(2)}, u32[]{:S(2)}) collective-permute-start(bf16[64,2048]{1,0:T(8,128)(2,1)S(1)} %fusion.43), channel_id=1, source_target_pairs={{0,4},{1,5},{2,6},{3,7},{4,0},{5,1},{6,2},{7,3},{8,12},{9,13},{10,... | collective-permute-start | bytes 786440 | tf_op jit(solution)/shard_map/ppermute | solution.py:25
  141.0 15.2 %collective-permute-start.32 = (bf16[64,2048]{1,0:T(8,128)(2,1)S(1)}, bf16[64,2048]{1,0:T(8,128)(2,1)S(1)}, u32[]{:S(2)}, u32[]{:S(2)}) collective-permute-start(bf16[64,2048]{1,0:T(8,128)(2,1)S(1)} %fusion.43), channel_id=1, source_target_pairs={{0,2},{1,3},{2,0},{3,1},{4,6},{5,7},{6,4},{7,5},{8,10},{9,11},{10,... | collective-permute-start | bytes 786440 | tf_op jit(solution)/shard_map/ppermute | solution.py:31
  149.8 7.2 %collective-permute-start.36 = (bf16[64,2048]{1,0:T(8,128)(2,1)S(1)}, bf16[64,2048]{1,0:T(8,128)(2,1)S(1)}, u32[]{:S(2)}, u32[]{:S(2)}) collective-permute-start(bf16[64,2048]{1,0:T(8,128)(2,1)S(1)} %broadcast_select_fusion.3), channel_id=1, source_target_pairs={{0,2},{1,3},{2,0},{3,1},{4,6},{5,7},{6,4},{7,5},{8,10},{9,11},{10,... | collective-permute-start | bytes 786440 | tf_op jit(solution)/shard_map/ppermute | solution.py:31
  153.2 12.2 %collective-permute-start.41 = (bf16[64,2048]{1,0:T(8,128)(2,1)S(1)}, bf16[64,2048]{1,0:T(8,128)(2,1)S(1)}, u32[]{:S(2)}, u32[]{:S(2)}) collective-permute-start(bf16[64,2048]{1,0:T(8,128)(2,1)S(1)} %collective-permute-done.38), channel_id=1, source_target_pairs={{0,2},{1,3},{2,0},{3,1},{4,6},{5,7},{6,4},{7,5},{8,10},{9,11},{10,... | collective-permute-start | bytes 786440 | tf_op jit(solution)/shard_map/ppermute | solution.py:31
  154.9 9.3 %collective-permute-start.40 = (bf16[64,2048]{1,0:T(8,128)(2,1)S(1)}, bf16[64,2048]{1,0:T(8,128)(2,1)S(1)}, u32[]{:S(2)}, u32[]{:S(2)}) collective-permute-start(bf16[64,2048]{1,0:T(8,128)(2,1)S(1)} %collective-permute-done.34), channel_id=1, source_target_pairs={{4,0},{5,1},{6,2},{7,3},{8,12},{9,13},{10,14},{11,15},{20,16},{21,... | collective-permute-start | bytes 786440 | tf_op jit(solution)/shard_map/ppermute | solution.py:25
  156.3 9.7 %collective-permute-start.33 = (bf16[128,2048]{1,0:T(8,128)(2,1)S(1)}, bf16[128,2048]{1,0:T(8,128)(2,1)S(1)}, u32[]{:S(2)}, u32[]{:S(2)}) collective-permute-start(bf16[128,2048]{1,0:T(8,128)(2,1)S(1)} %pad_maximum_fusion.12), channel_id=1, source_target_pairs={{0,1},{1,0},{2,3},{3,2},{4,5},{5,4},{6,7},{7,6},{8,9},{9,8},{10,11... | collective-permute-start | bytes 1572872 | tf_op jit(solution)/shard_map/ppermute | solution.py:31
  164.3 6.5 %collective-permute-start.43 = (bf16[64,2048]{1,0:T(8,128)(2,1)S(1)}, bf16[64,2048]{1,0:T(8,128)(2,1)S(1)}, u32[]{:S(2)}, u32[]{:S(2)}) collective-permute-start(bf16[64,2048]{1,0:T(8,128)(2,1)S(1)} %broadcast_select_fusion.2), channel_id=1, source_target_pairs={{0,2},{1,3},{2,0},{3,1},{4,6},{5,7},{6,4},{7,5},{8,10},{9,11},{10,... | collective-permute-start | bytes 786440 | tf_op jit(solution)/shard_map/ppermute | solution.py:31
  165.4 10.0 %collective-permute-start.44 = (bf16[128,2048]{1,0:T(8,128)(2,1)S(1)}, bf16[128,2048]{1,0:T(8,128)(2,1)S(1)}, u32[]{:S(2)}, u32[]{:S(2)}) collective-permute-start(bf16[128,2048]{1,0:T(8,128)(2,1)S(1)} %pad_maximum_fusion.15), channel_id=1, source_target_pairs={{0,1},{1,0},{2,3},{3,2},{4,5},{5,4},{6,7},{7,6},{8,9},{9,8},{10,11... | collective-permute-start | bytes 1572872 | tf_op jit(solution)/shard_map/ppermute | solution.py:31
  179.0 8.4 %collective-permute-start.50 = (bf16[64,2048]{1,0:T(8,128)(2,1)S(1)}, bf16[64,2048]{1,0:T(8,128)(2,1)S(1)}, u32[]{:S(2)}, u32[]{:S(2)}) collective-permute-start(bf16[64,2048]{1,0:T(8,128)(2,1)S(1)} %slice.418), channel_id=1, source_target_pairs={{0,2},{1,3},{2,0},{3,1},{4,6},{5,7},{6,4},{7,5},{8,10},{9,11},{10,... | collective-permute-start | bytes 786440 | tf_op jit(solution)/shard_map/ppermute | solution.py:31
  184.5 9.2 %collective-permute-start.48 = (bf16[64,2048]{1,0:T(8,128)(2,1)S(1)}, bf16[64,2048]{1,0:T(8,128)(2,1)S(1)}, u32[]{:S(2)}, u32[]{:S(2)}) collective-permute-start(bf16[64,2048]{1,0:T(8,128)(2,1)S(1)} %slice.416), channel_id=1, source_target_pairs={{0,2},{1,3},{2,0},{3,1},{4,6},{5,7},{6,4},{7,5},{8,10},{9,11},{10,... | collective-permute-start | bytes 786440 | tf_op jit(solution)/shard_map/ppermute | solution.py:31
  187.5 12.0 %collective-permute-start.51 = (bf16[64,2048]{1,0:T(8,128)(2,1)S(1)}, bf16[64,2048]{1,0:T(8,128)(2,1)S(1)}, u32[]{:S(2)}, u32[]{:S(2)}) collective-permute-start(bf16[64,2048]{1,0:T(8,128)(2,1)S(1)} %add_convert_fusion.11), channel_id=1, source_target_pairs={{0,12},{1,13},{2,14},{3,15},{4,8},{5,9},{6,10},{7,11},{8,4},{9,5},... | collective-permute-start | bytes 786440 | tf_op jit(solution)/shard_map/ppermute | solution.py:25
  189.3 10.0 %collective-permute-start.54 = (bf16[64,2048]{1,0:T(8,128)(2,1)S(1)}, bf16[64,2048]{1,0:T(8,128)(2,1)S(1)}, u32[]{:S(2)}, u32[]{:S(2)}) collective-permute-start(bf16[64,2048]{1,0:T(8,128)(2,1)S(1)} %slice.423), channel_id=1, source_target_pairs={{0,2},{1,3},{2,0},{3,1},{4,6},{5,7},{6,4},{7,5},{8,10},{9,11},{10,... | collective-permute-start | bytes 786440 | tf_op jit(solution)/shard_map/ppermute | solution.py:31
  193.7 17.1 %collective-permute-start.52 = (bf16[64,2048]{1,0:T(8,128)(2,1)S(1)}, bf16[64,2048]{1,0:T(8,128)(2,1)S(1)}, u32[]{:S(2)}, u32[]{:S(2)}) collective-permute-start(bf16[64,2048]{1,0:T(8,128)(2,1)S(1)} %add_convert_fusion.10), channel_id=1, source_target_pairs={{0,8},{1,9},{2,10},{3,11},{4,12},{5,13},{6,14},{7,15},{8,0},{9,1},... | collective-permute-start | bytes 786440 | tf_op jit(solution)/shard_map/ppermute | solution.py:25
  194.4 16.4 %collective-permute-start.49 = (bf16[64,2048]{1,0:T(8,128)(2,1)S(1)}, bf16[64,2048]{1,0:T(8,128)(2,1)S(1)}, u32[]{:S(2)}, u32[]{:S(2)}) collective-permute-start(bf16[64,2048]{1,0:T(8,128)(2,1)S(1)} %slice.407), channel_id=1, source_target_pairs={{0,2},{1,3},{2,0},{3,1},{4,6},{5,7},{6,4},{7,5},{8,10},{9,11},{10,... | collective-permute-start | bytes 786440 | tf_op jit(solution)/shard_map/ppermute | solution.py:31
  199.4 12.6 %collective-permute-start.55 = (bf16[64,2048]{1,0:T(8,128)(2,1)S(1)}, bf16[64,2048]{1,0:T(8,128)(2,1)S(1)}, u32[]{:S(2)}, u32[]{:S(2)}) collective-permute-start(bf16[64,2048]{1,0:T(8,128)(2,1)S(1)} %add_convert_fusion.9), channel_id=1, source_target_pairs={{0,4},{1,5},{2,6},{3,7},{4,0},{5,1},{6,2},{7,3},{8,12},{9,13},{10,... | collective-permute-start | bytes 786440 | tf_op jit(solution)/shard_map/ppermute | solution.py:25
  (23 other events, 150.7 us)

commit v10 on v9

--- a/solution.py
+++ b/solution.py
@@ -88,14 +88,13 @@
     columns = {0: rows, 1: ring.between(rows, 1)}
     crossed = {0: ring.across(rows, top)}
     middle = ring.send(rows, [(1, 2), (2, 1)])
-    ends = ring.send(rows, [(0, 3), (3, 0)])
     near = ring.send(middle, [(1, 0), (2, 3)])
     far = ring.send(columns[1], [(1, 2), (2, 1)])
+    ends = ring.send(after(rows, columns[1], middle), [(0, 3), (3, 0)])
+    columns[2] = jnp.where(ring.inside, far, near)
     columns[3] = jnp.where(ring.inside, middle, ends)
-    columns[2] = jnp.where(ring.inside, far, near)
-    crossed[1] = ring.across(after(columns[1], middle), top)
-    crossed[3] = ring.across(columns[3], top)
-    crossed[2] = ring.across(columns[2], top)
+    for slot in (1, 2, 3):
+        crossed[slot] = ring.across(columns[slot], top)
 
     def chunk(slot, *ties):
         values = after(jnp.concatenate([columns[slot], crossed[slot]], axis=0), *ties)
@@ -117,20 +116,28 @@
         parts[slot] = add(halves[slot][:own], back[slot])
 
     parts = {}
-    last = [columns[2], crossed[1], crossed[3]]
-    for slot in (3, 0, 1):
+    last = [columns[3]]
+    for slot in (0, 1, 2):
         last = [turn(slot, chunk(slot), *last)]
-    turn(2, chunk(2, *last), halves[3])
+    turn(3, chunk(3, *last), halves[2])
+    swap(2)
     swap(3)
-    swap(2)
-    swap(1, halves[2], back[3])
-    swap(0, halves[2], back[2])
+    swap(1, halves[3], back[2])
+    swap(0, halves[3], back[3])
     sums = plane_sums(ring, lambda slot: parts[slot])
-    return sums, columns[2], back[0]
-
-
-def shared_weight(ring, weight, *ties):
-    other = after(ring.between(weight, 1), *ties)
+    return sums, columns[3], back[3]
+
+
+def shared_weight(ring, weight, groups, begin, swap):
+    if groups % 2:
+        other = after(ring.between(after(weight, begin), 1), swap)
+    else:
+        rows = weight.shape[0] // 2
+        odd = lax.axis_index("groups") % 2
+        sent = lax.dynamic_slice_in_dim(weight, odd * rows, rows, axis=0)
+        here = after(ring.between(after(sent, begin), 1), swap)
+        there = lax.ppermute(here, "groups", [(g, g ^ 1) for g in range(groups)])
+        other = jnp.where(odd == 0, jnp.concatenate([here, there]), jnp.concatenate([there, here]))
     held = jnp.where(ring.z % 2 == 1, jnp.stack([other, weight]), jnp.stack([weight, other]))
     for i, bit in enumerate(ring.bits[1:]):
         other = ring.across(held, bit)
@@ -188,7 +195,7 @@
         return expert(chunk, second_columns[slot], second_gate_up[0], second_down[0])
 
     first, gathered, summed = routed(ring, jnp.concatenate([hidden_rows, lanes], axis=1), first_work)
-    weight = shared_weight(ring, after(merge_weight, gathered), summed)
+    weight = shared_weight(ring, merge_weight, lax.axis_size("groups"), gathered, summed)
     after_first = (hidden_rows.astype(jnp.float32) + first).astype(jnp.bfloat16)
     merged_in = jnp.concatenate([normed(after_first, hidden_gain), normed(token_embed, embed_gain)], axis=1)
     merged = merge(ring, merged_in, weight)

time: 214 us -> 219 us (1.023)
  starting transfers between devices: 53.1 us -> 64.8 us
  waiting for transfers between devices: 114 us -> 105 us
  other arithmetic: 15.9 us -> 19.7 us
    ppermute x18, waiting for transfers between devices: 65 us -> 49.6 us  [send(): return lax.ppermute(values, 'inner', perm)]
    ppermute x18, starting transfers between devices: 23.1 us -> 33.6 us  [send(): return lax.ppermute(values, 'inner', perm)]
    ppermute x0 -> x1, waiting for transfers between devices: none -> 3.88 us  [shared_weight(): there = lax.ppermute(here, 'groups', [(g, g ^ 1) for g in range(groups)])]
    unnamed x30 -> x34, local copies, waits for them, and re-layouts: 3.57 us -> 0.45 us
    ppermute x38, waiting for transfers between devices: 49.2 us -> 51.5 us  [across(): lax.ppermute(values, 'inner', [(d, d ^ bit) for d in range(self.size)])]
  transfers between devices with their start and end apart: 56 -> 57, of which waited for: 27 -> 22; matrix products, arithmetic and copies ran while one was open for 15% -> 18% of each run, Pallas kernels for 0% -> 0%
where the time goes in v10:
time: 219 us
  waiting for transfers between devices  105 us (48%)
  starting transfers between devices  64.8 us (30%)
  matrix products  21.5 us (10%)
  other arithmetic  19.7 us (9%)
  local copies, waits for them, and re-layouts  6.71 us (3%)
    ppermute x38, waiting for transfers between devices, across(): lax.ppermute(values, 'inner', [(d, d ^ bit) for d in range(self.size)])  51.5 us
    ppermute x18, waiting for transfers between devices, send(): return lax.ppermute(values, 'inner', perm)  49.6 us
    ppermute x18, starting transfers between devices, send(): return lax.ppermute(values, 'inner', perm)  33.6 us
    ppermute x38, starting transfers between devices, across(): lax.ppermute(values, 'inner', [(d, d ^ bit) for d in range(self.size)])  29.7 us
    dot_general x8, matrix products, expert(): projected = jnp.dot(rows, gate_up, preferred_element_type=jnp.float32)  10.1 us
    dot_general x8, matrix products, expert(): out = jnp.dot(hidden, down, preferred_element_type=jnp.float32)  8.09 us
  transfers between devices with their start and end apart: 57, of which 22 were waited for; matrix products, arithmetic and copies ran while one was open for 18% of the time, Pallas kernels for 0%

profile of v10, /device:TPU:0, one launch (start us, length us, event | category | flops | bytes accessed | tf_op | source)
XLA Modules:
  0.0 218.7 jit_solution(7271334105358700403)
XLA Ops:
  3.4 3.1 %collective-permute-start.3 = (bf16[64,2176]{1,0:T(8,128)(2,1)S(1)}, bf16[64,2176]{1,0:T(8,128)(2,1)S(1)}, u32[]{:S(2)}, u32[]{:S(2)}) collective-permute-start(bf16[64,2176]{1,0:T(8,128)(2,1)S(1)} %pad_maximum_fusion.16), channel_id=1, source_target_pairs={{0,4},{1,5},{2,6},{3,7},{4,0},{5,1},{6,2},{7,3},{8,12},{9,13},{10,... | collective-permute-start | bytes 835592 | tf_op jit(solution)/shard_map/ppermute | solution.py:25
  7.2 1.6 collective-permute-start
  9.9 1.9 constant_dynamic-slice_fusion
  11.8 1.4 collective-permute-done.3
  13.1 5.7 %collective-permute-start.4 = (bf16[64,2176]{1,0:T(8,128)(2,1)S(1)}, bf16[64,2176]{1,0:T(8,128)(2,1)S(1)}, u32[]{:S(2)}, u32[]{:S(2)}) collective-permute-start(bf16[64,2176]{1,0:T(8,128)(2,1)S(1)} %pad_maximum_fusion.16), channel_id=1, source_target_pairs={{0,12},{1,13},{2,14},{3,15},{12,0},{13,1},{14,2},{15,3},{16,28},{1... | collective-permute-start | bytes 835592 | tf_op jit(solution)/shard_map/ppermute | solution.py:25
  19.5 1.3 collective-permute-start.8
  21.0 1.6 collective-permute-start.11
  22.5 8.2 %collective-permute-done.8 = bf16[64,2176]{1,0:T(8,128)(2,1)S(1)} collective-permute-done((bf16[64,2176]{1,0:T(8,128)(2,1)S(1)}, bf16[64,2176]{1,0:T(8,128)(2,1)S(1)}, u32[]{:S(2)}, u32[]{:S(2)}) %collective-permute-start.8) | collective-permute-done | bytes 278560 | tf_op jit(solution)/shard_map/ppermute | solution.py:25
  30.8 1.5 collective-permute-start.9
  33.0 7.3 %collective-permute-done.9 = bf16[64,2176]{1,0:T(8,128)(2,1)S(1)} collective-permute-done((bf16[64,2176]{1,0:T(8,128)(2,1)S(1)}, bf16[64,2176]{1,0:T(8,128)(2,1)S(1)}, u32[]{:S(2)}, u32[]{:S(2)}) %collective-permute-start.9) | collective-permute-done | bytes 278560 | tf_op jit(solution)/shard_map/ppermute | solution.py:31
  42.2 1.8 fusion.16
  45.5 1.8 fusion.17
  60.0 1.6 collective-permute-start.19
  62.3 6.8 %collective-permute-done.19 = bf16[64,2048]{1,0:T(8,128)(2,1)S(1)} collective-permute-done((bf16[64,2048]{1,0:T(8,128)(2,1)S(1)}, bf16[64,2048]{1,0:T(8,128)(2,1)S(1)}, u32[]{:S(2)}, u32[]{:S(2)}) %collective-permute-start.19) | collective-permute-done | bytes 262176 | tf_op jit(solution)/shard_map/ppermute | solution.py:31
  69.2 3.5 %collective-permute-start.20 = (bf16[64,2048]{1,0:T(8,128)(2,1)S(1)}, bf16[64,2048]{1,0:T(8,128)(2,1)}, u32[]{:S(2)}, u32[]{:S(2)}) collective-permute-start(bf16[64,2048]{1,0:T(8,128)(2,1)S(1)} %add_convert_fusion.15), channel_id=1, source_target_pairs={{0,8},{1,9},{2,10},{3,11},{4,12},{5,13},{6,14},{7,15},{8,0},{9,1},... | collective-permute-start | bytes 786440 | tf_op jit(solution)/shard_map/ppermute | solution.py:25
  72.7 1.5 collective-permute-start.22
  74.4 1.5 collective-permute-start.25
  76.6 3.8 %collective-permute-start.18 = (bf16[64,2048]{1,0:T(8,128)(2,1)}, bf16[64,2048]{1,0:T(8,128)(2,1)}, u32[]{:S(2)}, u32[]{:S(2)}) collective-permute-start(bf16[64,2048]{1,0:T(8,128)(2,1)} %add_convert_fusion.16), channel_id=1, source_target_pairs={{0,12},{1,13},{2,14},{3,15},{4,8},{5,9},{6,10},{7,11},{8,4},{9,5},... | collective-permute-start | bytes 786440 | tf_op jit(solution)/shard_map/ppermute | solution.py:25
  80.4 1.5 collective-permute-start.17
  83.3 3.9 %collective-permute-done.25 = bf16[128,2048]{1,0:T(8,128)(2,1)S(1)} collective-permute-done((bf16[128,2048]{1,0:T(8,128)(2,1)S(1)}, bf16[128,2048]{1,0:T(8,128)(2,1)S(1)}, u32[]{:S(2)}, u32[]{:S(2)}) %collective-permute-start.25) | collective-permute-done | bytes 524320 | tf_op jit(solution)/shard_map/ppermute | solution.py:139
  87.5 1.7 maximum_select_fusion.1
  89.4 5.3 %collective-permute-done.23 = bf16[64,2048]{1,0:T(8,128)(2,1)} collective-permute-done((bf16[64,2048]{1,0:T(8,128)(2,1)}, bf16[64,2048]{1,0:T(8,128)(2,1)}, u32[]{:S(2)}, u32[]{:S(2)}) %collective-permute-start.23) | collective-permute-done | bytes 262176 | tf_op jit(solution)/shard_map/ppermute | solution.py:25
  94.8 1.5 fusion.40
  96.7 1.8 collective-permute-start.29
  99.2 1.5 collective-permute-start.27
  102.2 6.6 %collective-permute-done.29 = bf16[64,1024]{1,0:T(8,128)(2,1)S(1)} collective-permute-done((bf16[64,1024]{1,0:T(8,128)(2,1)S(1)}, bf16[64,1024]{1,0:T(8,128)(2,1)S(1)}, u32[]{:S(2)}, u32[]{:S(2)}) %collective-permute-start.29) | collective-permute-done | bytes 131104 | tf_op jit(solution)/shard_map/ppermute | solution.py:31
  108.8 3.7 %collective-permute-done.30 = bf16[64,1024]{1,0:T(8,128)(2,1)S(1)} collective-permute-done((bf16[64,1024]{1,0:T(8,128)(2,1)S(1)}, bf16[64,1024]{1,0:T(8,128)(2,1)S(1)}, u32[]{:S(2)}, u32[]{:S(2)}) %collective-permute-start.30) | collective-permute-done | bytes 131104 | tf_op jit(solution)/shard_map/ppermute | solution.py:31
  112.8 2.8 %maximum_select_fusion = bf16[2,2,256,2048]{3,2,1,0:T(8,128)(2,1)S(1)} fusion(bf16[2,1,256,2048]{3,2,1,0:T(8,128)(2,1)S(1)} %maximum_select_fusion.2, bf16[2,1,256,2048]{3,2,1,0:T(8,128)(2,1)} %bitcast.5, pred[]{:T(512)S(6)} %eq.71), kind=kLoop, calls=%fused_computation | loop fusion | flops 6291456 | bytes 8388609 | tf_op jit(solution)/shard_map/jit(_where)/select_n | solution.py:145
  117.9 1.6 collective-permute-start.28
  119.5 6.2 %collective-permute-done.31 = bf16[64,2048]{1,0:T(8,128)(2,1)S(1)} collective-permute-done((bf16[64,2048]{1,0:T(8,128)(2,1)S(1)}, bf16[64,2048]{1,0:T(8,128)(2,1)S(1)}, u32[]{:S(2)}, u32[]{:S(2)}) %collective-permute-start.31) | collective-permute-done | bytes 262176 | tf_op jit(solution)/shard_map/ppermute | solution.py:31
  127.5 2.9 %collective-permute-done.28 = bf16[64,2048]{1,0:T(8,128)(2,1)S(1)} collective-permute-done((bf16[64,2048]{1,0:T(8,128)(2,1)S(1)}, bf16[64,2048]{1,0:T(8,128)(2,1)S(1)}, u32[]{:S(2)}, u32[]{:S(2)}) %collective-permute-start.28) | collective-permute-done | bytes 262176 | tf_op jit(solution)/shard_map/ppermute | solution.py:31
  130.4 7.4 %collective-permute-done.32 = bf16[64,2048]{1,0:T(8,128)(2,1)S(1)} collective-permute-done((bf16[64,2048]{1,0:T(8,128)(2,1)S(1)}, bf16[64,2048]{1,0:T(8,128)(2,1)S(1)}, u32[]{:S(2)}, u32[]{:S(2)}) %collective-permute-start.32) | collective-permute-done | bytes 262176 | tf_op jit(solution)/shard_map/ppermute | solution.py:25
  139.3 6.3 %collective-permute-done.36 = bf16[64,2048]{1,0:T(8,128)(2,1)S(1)} collective-permute-done((bf16[64,2048]{1,0:T(8,128)(2,1)S(1)}, bf16[64,2048]{1,0:T(8,128)(2,1)S(1)}, u32[]{:S(2)}, u32[]{:S(2)}) %collective-permute-start.36) | collective-permute-done | bytes 262176 | tf_op jit(solution)/shard_map/ppermute | solution.py:25
  146.1 4.7 %collective-permute-start.37 = (bf16[64,2048]{1,0:T(8,128)(2,1)S(1)}, bf16[64,2048]{1,0:T(8,128)(2,1)S(1)}, u32[]{:S(2)}, u32[]{:S(2)}) collective-permute-start(bf16[64,2048]{1,0:T(8,128)(2,1)S(1)} %fusion.43), channel_id=1, source_target_pairs={{0,12},{1,13},{2,14},{3,15},{12,0},{13,1},{14,2},{15,3},{16,28},{1... | collective-permute-start | bytes 786440 | tf_op jit(solution)/shard_map/ppermute | solution.py:25
  151.6 1.3 collective-permute-start.41
  153.1 8.9 %collective-permute-done.41 = bf16[64,2048]{1,0:T(8,128)(2,1)S(1)} collective-permute-done((bf16[64,2048]{1,0:T(8,128)(2,1)S(1)}, bf16[64,2048]{1,0:T(8,128)(2,1)S(1)}, u32[]{:S(2)}, u32[]{:S(2)}) %collective-permute-start.41) | collective-permute-done | bytes 262176 | tf_op jit(solution)/shard_map/ppermute | solution.py:25
  162.0 1.5 collective-permute-start.42
  164.2 7.1 %collective-permute-done.42 = bf16[64,2048]{1,0:T(8,128)(2,1)S(1)} collective-permute-done((bf16[64,2048]{1,0:T(8,128)(2,1)S(1)}, bf16[64,2048]{1,0:T(8,128)(2,1)S(1)}, u32[]{:S(2)}, u32[]{:S(2)}) %collective-permute-start.42) | collective-permute-done | bytes 262176 | tf_op jit(solution)/shard_map/ppermute | solution.py:31
  171.5 1.3 fusion.6
  183.8 1.5 collective-permute-start.52
  186.8 6.2 %collective-permute-done.52 = bf16[64,2048]{1,0:T(8,128)(2,1)S(1)} collective-permute-done((bf16[64,2048]{1,0:T(8,128)(2,1)S(1)}, bf16[64,2048]{1,0:T(8,128)(2,1)S(1)}, u32[]{:S(2)}, u32[]{:S(2)}) %collective-permute-start.52) | collective-permute-done | bytes 262176 | tf_op jit(solution)/shard_map/ppermute | solution.py:31
  193.1 2.0 collective-permute-start.53
  195.1 1.5 collective-permute-start.55
  196.6 2.0 collective-permute-done.49
  198.7 2.9 %collective-permute-start.51 = (bf16[64,2048]{1,0:T(8,128)(2,1)S(1)}, bf16[64,2048]{1,0:T(8,128)(2,1)S(1)}, u32[]{:S(2)}, u32[]{:S(2)}) collective-permute-start(bf16[64,2048]{1,0:T(8,128)(2,1)S(1)} %add_convert_fusion.11), channel_id=1, source_target_pairs={{0,12},{1,13},{2,14},{3,15},{4,8},{5,9},{6,10},{7,11},{8,4},{9,5},... | collective-permute-start | bytes 786440 | tf_op jit(solution)/shard_map/ppermute | solution.py:25
  201.7 1.5 collective-permute-start.50
  205.7 6.9 %collective-permute-done.53 = bf16[64,2048]{1,0:T(8,128)(2,1)S(1)} collective-permute-done((bf16[64,2048]{1,0:T(8,128)(2,1)S(1)}, bf16[64,2048]{1,0:T(8,128)(2,1)S(1)}, u32[]{:S(2)}, u32[]{:S(2)}) %collective-permute-start.53) | collective-permute-done | bytes 262176 | tf_op jit(solution)/shard_map/ppermute | solution.py:25
  212.6 5.2 %collective-permute-done.56 = bf16[64,2048]{1,0:T(8,128)(2,1)S(1)} collective-permute-done((bf16[64,2048]{1,0:T(8,128)(2,1)S(1)}, bf16[64,2048]{1,0:T(8,128)(2,1)S(1)}, u32[]{:S(2)}, u32[]{:S(2)}) %collective-permute-start.56) | collective-permute-done | bytes 262176 | tf_op jit(solution)/shard_map/ppermute | solution.py:25
  (198 shorter events, 52.5 us)
Async XLA Ops:
  3.4 9.7 %collective-permute-start.3 = (bf16[64,2176]{1,0:T(8,128)(2,1)S(1)}, bf16[64,2176]{1,0:T(8,128)(2,1)S(1)}, u32[]{:S(2)}, u32[]{:S(2)}) collective-permute-start(bf16[64,2176]{1,0:T(8,128)(2,1)S(1)} %pad_maximum_fusion.16), channel_id=1, source_target_pairs={{0,4},{1,5},{2,6},{3,7},{4,0},{5,1},{6,2},{7,3},{8,12},{9,13},{10,... | collective-permute-start | bytes 835592 | tf_op jit(solution)/shard_map/ppermute | solution.py:25
  6.5 6.7 %collective-permute-start.2 = (bf16[64,2176]{1,0:T(8,128)(2,1)S(1)}, bf16[64,2176]{1,0:T(8,128)(2,1)S(1)}, u32[]{:S(2)}, u32[]{:S(2)}) collective-permute-start(bf16[64,2176]{1,0:T(8,128)(2,1)S(1)} %pad_maximum_fusion.16), channel_id=1, source_target_pairs={{4,8},{5,9},{6,10},{7,11},{8,4},{9,5},{10,6},{11,7},{20,24},{21,25... | collective-permute-start | bytes 835592 | tf_op jit(solution)/shard_map/ppermute | solution.py:25
  7.2 13.6 %collective-permute-start = (bf16[64,2176]{1,0:T(8,128)(2,1)S(1)}, bf16[64,2176]{1,0:T(8,128)(2,1)S(1)}, u32[]{:S(2)}, u32[]{:S(2)}) collective-permute-start(bf16[64,2176]{1,0:T(8,128)(2,1)S(1)} %pad_maximum_fusion.16), channel_id=1, source_target_pairs={{0,2},{1,3},{2,0},{3,1},{4,6},{5,7},{6,4},{7,5},{8,10},{9,11},{10,... | collective-permute-start | bytes 835592 | tf_op jit(solution)/shard_map/ppermute | solution.py:31
  13.1 19.1 %collective-permute-start.4 = (bf16[64,2176]{1,0:T(8,128)(2,1)S(1)}, bf16[64,2176]{1,0:T(8,128)(2,1)S(1)}, u32[]{:S(2)}, u32[]{:S(2)}) collective-permute-start(bf16[64,2176]{1,0:T(8,128)(2,1)S(1)} %pad_maximum_fusion.16), channel_id=1, source_target_pairs={{0,12},{1,13},{2,14},{3,15},{12,0},{13,1},{14,2},{15,3},{16,28},{1... | collective-permute-start | bytes 835592 | tf_op jit(solution)/shard_map/ppermute | solution.py:25
  19.5 11.2 %collective-permute-start.8 = (bf16[64,2176]{1,0:T(8,128)(2,1)S(1)}, bf16[64,2176]{1,0:T(8,128)(2,1)S(1)}, u32[]{:S(2)}, u32[]{:S(2)}) collective-permute-start(bf16[64,2176]{1,0:T(8,128)(2,1)S(1)} %collective-permute-done.2), channel_id=1, source_target_pairs={{4,0},{5,1},{6,2},{7,3},{8,12},{9,13},{10,14},{11,15},{20,16},{21,... | collective-permute-start | bytes 835592 | tf_op jit(solution)/shard_map/ppermute | solution.py:25
  20.9 19.6 %collective-permute-start.1 = (bf16[128,2176]{1,0:T(8,128)(2,1)S(1)}, bf16[128,2176]{1,0:T(8,128)(2,1)S(1)}, u32[]{:S(2)}, u32[]{:S(2)}) collective-permute-start(bf16[128,2176]{1,0:T(8,128)(2,1)S(1)} %pad_maximum_fusion.8), channel_id=1, source_target_pairs={{0,1},{1,0},{2,3},{3,2},{4,5},{5,4},{6,7},{7,6},{8,9},{9,8},{10,11... | collective-permute-start | bytes 1671176 | tf_op jit(solution)/shard_map/ppermute | solution.py:31
  21.0 11.4 %collective-permute-start.11 = (bf16[64,2176]{1,0:T(8,128)(2,1)S(1)}, bf16[64,2176]{1,0:T(8,128)(2,1)S(1)}, u32[]{:S(2)}, u32[]{:S(2)}) collective-permute-start(bf16[64,2176]{1,0:T(8,128)(2,1)S(1)} %collective-permute-done.3), channel_id=1, source_target_pairs={{0,2},{1,3},{2,0},{3,1},{4,6},{5,7},{6,4},{7,5},{8,10},{9,11},{10,... | collective-permute-start | bytes 835592 | tf_op jit(solution)/shard_map/ppermute | solution.py:31
  30.8 9.6 %collective-permute-start.9 = (bf16[64,2176]{1,0:T(8,128)(2,1)S(1)}, bf16[64,2176]{1,0:T(8,128)(2,1)S(1)}, u32[]{:S(2)}, u32[]{:S(2)}) collective-permute-start(bf16[64,2176]{1,0:T(8,128)(2,1)S(1)} %broadcast_select_fusion), channel_id=1, source_target_pairs={{0,2},{1,3},{2,0},{3,1},{4,6},{5,7},{6,4},{7,5},{8,10},{9,11},{10,... | collective-permute-start | bytes 835592 | tf_op jit(solution)/shard_map/ppermute | solution.py:31
  32.4 18.7 %collective-permute-start.6 = (bf16[64,2176]{1,0:T(8,128)(2,1)S(1)}, bf16[64,2176]{1,0:T(8,128)(2,1)S(1)}, u32[]{:S(2)}, u32[]{:S(2)}) collective-permute-start(bf16[64,2176]{1,0:T(8,128)(2,1)S(1)} %broadcast_select_fusion.1), channel_id=1, source_target_pairs={{0,2},{1,3},{2,0},{3,1},{4,6},{5,7},{6,4},{7,5},{8,10},{9,11},{10,... | collective-permute-start | bytes 835592 | tf_op jit(solution)/shard_map/ppermute | solution.py:31
  33.0 10.9 %collective-permute-start.12 = (bf16[128,2176]{1,0:T(8,128)(2,1)S(1)}, bf16[128,2176]{1,0:T(8,128)(2,1)S(1)}, u32[]{:S(2)}, u32[]{:S(2)}) collective-permute-start(bf16[128,2176]{1,0:T(8,128)(2,1)S(1)} %pad_maximum_fusion.11), channel_id=1, source_target_pairs={{0,1},{1,0},{2,3},{3,2},{4,5},{5,4},{6,7},{7,6},{8,9},{9,8},{10,11... | collective-permute-start | bytes 1671176 | tf_op jit(solution)/shard_map/ppermute | solution.py:31
  40.5 6.8 %collective-permute-start.10 = (bf16[128,2176]{1,0:T(8,128)(2,1)S(1)}, bf16[128,2176]{1,0:T(8,128)(2,1)S(1)}, u32[]{:S(2)}, u32[]{:S(2)}) collective-permute-start(bf16[128,2176]{1,0:T(8,128)(2,1)S(1)} %pad_maximum_fusion.10), channel_id=1, source_target_pairs={{0,1},{1,0},{2,3},{3,2},{4,5},{5,4},{6,7},{7,6},{8,9},{9,8},{10,11... | collective-permute-start | bytes 1671176 | tf_op jit(solution)/shard_map/ppermute | solution.py:31
  51.2 4.9 %collective-permute-start.13 = (bf16[128,2176]{1,0:T(8,128)(2,1)S(1)}, bf16[128,2176]{1,0:T(8,128)(2,1)S(1)}, u32[]{:S(2)}, u32[]{:S(2)}) collective-permute-start(bf16[128,2176]{1,0:T(8,128)(2,1)S(1)} %pad_maximum_fusion.9), channel_id=1, source_target_pairs={{0,1},{1,0},{2,3},{3,2},{4,5},{5,4},{6,7},{7,6},{8,9},{9,8},{10,11... | collective-permute-start | bytes 1671176 | tf_op jit(solution)/shard_map/ppermute | solution.py:31
  51.3 22.9 %collective-permute-start.24 = (bf16[128,2048]{1,0:T(8,128)(2,1)}, bf16[128,2048]{1,0:T(8,128)(2,1)S(1)}, u32[]{:S(2)}, u32[]{:S(2)}) collective-permute-start(bf16[128,2048]{1,0:T(8,128)(2,1)} %constant_dynamic-slice_fusion), channel_id=1, source_target_pairs={{0,4},{1,5},{2,6},{3,7},{4,0},{5,1},{6,2},{7,3},{8,12},{9,13},{10,... | collective-permute-start | bytes 1572872 | tf_op jit(solution)/shard_map/ppermute | solution.py:25
  53.0 5.8 %collective-permute-start.5 = (bf16[128,2048]{1,0:T(8,128)(2,1)S(1)}, bf16[128,2048]{1,0:T(8,128)(2,1)S(1)}, u32[]{:S(2)}, u32[]{:S(2)}) collective-permute-start(bf16[128,2048]{1,0:T(8,128)(2,1)S(1)} %slice.379), channel_id=1, source_target_pairs={{0,1},{1,0},{2,3},{3,2},{4,5},{5,4},{6,7},{7,6},{8,9},{9,8},{10,11... | collective-permute-start | bytes 1572872 | tf_op jit(solution)/shard_map/ppermute | solution.py:31
  54.4 5.3 %collective-permute-start.21 = (bf16[128,2048]{1,0:T(8,128)(2,1)S(1)}, bf16[128,2048]{1,0:T(8,128)(2,1)S(1)}, u32[]{:S(2)}, u32[]{:S(2)}) collective-permute-start(bf16[128,2048]{1,0:T(8,128)(2,1)S(1)} %slice.397), channel_id=1, source_target_pairs={{0,1},{1,0},{2,3},{3,2},{4,5},{5,4},{6,7},{7,6},{8,9},{9,8},{10,11... | collective-permute-start | bytes 1572872 | tf_op jit(solution)/shard_map/ppermute | solution.py:31
  60.0 9.2 %collective-permute-start.19 = (bf16[64,2048]{1,0:T(8,128)(2,1)S(1)}, bf16[64,2048]{1,0:T(8,128)(2,1)S(1)}, u32[]{:S(2)}, u32[]{:S(2)}) collective-permute-start(bf16[64,2048]{1,0:T(8,128)(2,1)S(1)} %slice.395), channel_id=1, source_target_pairs={{0,2},{1,3},{2,0},{3,1},{4,6},{5,7},{6,4},{7,5},{8,10},{9,11},{10,... | collective-permute-start | bytes 786440 | tf_op jit(solution)/shard_map/ppermute | solution.py:31
  61.8 12.6 %collective-permute-start.16 = (bf16[64,2048]{1,0:T(8,128)(2,1)S(1)}, bf16[64,2048]{1,0:T(8,128)(2,1)S(1)}, u32[]{:S(2)}, u32[]{:S(2)}) collective-permute-start(bf16[64,2048]{1,0:T(8,128)(2,1)S(1)} %slice.392), channel_id=1, source_target_pairs={{0,2},{1,3},{2,0},{3,1},{4,6},{5,7},{6,4},{7,5},{8,10},{9,11},{10,... | collective-permute-start | bytes 786440 | tf_op jit(solution)/shard_map/ppermute | solution.py:31
  69.2 20.2 %collective-permute-start.20 = (bf16[64,2048]{1,0:T(8,128)(2,1)S(1)}, bf16[64,2048]{1,0:T(8,128)(2,1)}, u32[]{:S(2)}, u32[]{:S(2)}) collective-permute-start(bf16[64,2048]{1,0:T(8,128)(2,1)S(1)} %add_convert_fusion.15), channel_id=1, source_target_pairs={{0,8},{1,9},{2,10},{3,11},{4,12},{5,13},{6,14},{7,15},{8,0},{9,1},... | collective-permute-start | bytes 786440 | tf_op jit(solution)/shard_map/ppermute | solution.py:25
  72.7 9.2 %collective-permute-start.22 = (bf16[64,2048]{1,0:T(8,128)(2,1)S(1)}, bf16[64,2048]{1,0:T(8,128)(2,1)S(1)}, u32[]{:S(2)}, u32[]{:S(2)}) collective-permute-start(bf16[64,2048]{1,0:T(8,128)(2,1)S(1)} %slice.399), channel_id=1, source_target_pairs={{0,2},{1,3},{2,0},{3,1},{4,6},{5,7},{6,4},{7,5},{8,10},{9,11},{10,... | collective-permute-start | bytes 786440 | tf_op jit(solution)/shard_map/ppermute | solution.py:31
  74.4 12.9 %collective-permute-start.25 = (bf16[128,2048]{1,0:T(8,128)(2,1)S(1)}, bf16[128,2048]{1,0:T(8,128)(2,1)S(1)}, u32[]{:S(2)}, u32[]{:S(2)}) collective-permute-start(bf16[128,2048]{1,0:T(8,128)(2,1)S(1)} %collective-permute-done.24), channel_id=1, source_target_pairs={{0,16},{16,0},{1,17},{17,1},{2,18},{18,2},{3,19},{19,3},{4,20},{20... | collective-permute-start | bytes 1572872 | tf_op jit(solution)/shard_map/ppermute | solution.py:139
  76.6 12.8 %collective-permute-start.18 = (bf16[64,2048]{1,0:T(8,128)(2,1)}, bf16[64,2048]{1,0:T(8,128)(2,1)}, u32[]{:S(2)}, u32[]{:S(2)}) collective-permute-start(bf16[64,2048]{1,0:T(8,128)(2,1)} %add_convert_fusion.16), channel_id=1, source_target_pairs={{0,12},{1,13},{2,14},{3,15},{4,8},{5,9},{6,10},{7,11},{8,4},{9,5},... | collective-permute-start | bytes 786440 | tf_op jit(solution)/shard_map/ppermute | solution.py:25
  80.4 9.0 %collective-permute-start.17 = (bf16[64,2048]{1,0:T(8,128)(2,1)}, bf16[64,2048]{1,0:T(8,128)(2,1)}, u32[]{:S(2)}, u32[]{:S(2)}) collective-permute-start(bf16[64,2048]{1,0:T(8,128)(2,1)} %slice.381), channel_id=1, source_target_pairs={{0,2},{1,3},{2,0},{3,1},{4,6},{5,7},{6,4},{7,5},{8,10},{9,11},{10,... | collective-permute-start | bytes 786440 | tf_op jit(solution)/shard_map/ppermute | solution.py:31
  82.7 12.0 %collective-permute-start.23 = (bf16[64,2048]{1,0:T(8,128)(2,1)}, bf16[64,2048]{1,0:T(8,128)(2,1)}, u32[]{:S(2)}, u32[]{:S(2)}) collective-permute-start(bf16[64,2048]{1,0:T(8,128)(2,1)} %add_convert_fusion.14), channel_id=1, source_target_pairs={{0,4},{1,5},{2,6},{3,7},{4,0},{5,1},{6,2},{7,3},{8,12},{9,13},{10,... | collective-permute-start | bytes 786440 | tf_op jit(solution)/shard_map/ppermute | solution.py:25
  89.2 23.6 %collective-permute-start.26 = (bf16[2,256,2048]{2,1,0:T(8,128)(2,1)}, bf16[2,256,2048]{2,1,0:T(8,128)(2,1)}, u32[]{:S(2)}, u32[]{:S(2)}) collective-permute-start(bf16[2,256,2048]{2,1,0:T(8,128)(2,1)} %maximum_select_fusion.1), channel_id=1, source_target_pairs={{0,1},{1,0},{2,3},{3,2},{4,5},{5,4},{6,7},{7,6},{8,9},{9,8},{10,11... | collective-permute-start | bytes 6291464 | tf_op jit(solution)/shard_map/ppermute | solution.py:31
  96.7 12.0 %collective-permute-start.29 = (bf16[64,1024]{1,0:T(8,128)(2,1)S(1)}, bf16[64,1024]{1,0:T(8,128)(2,1)S(1)}, u32[]{:S(2)}, u32[]{:S(2)}) collective-permute-start(bf16[64,1024]{1,0:T(8,128)(2,1)S(1)} %pad_maximum_fusion.18), channel_id=1, source_target_pairs={{0,8},{1,9},{2,10},{3,11},{4,12},{5,13},{6,14},{7,15},{8,0},{9,1},... | collective-permute-start | bytes 393224 | tf_op jit(solution)/shard_map/ppermute | solution.py:31
  99.2 9.6 %collective-permute-start.27 = (bf16[64,1024]{1,0:T(8,128)(2,1)}, bf16[64,1024]{1,0:T(8,128)(2,1)S(1)}, u32[]{:S(2)}, u32[]{:S(2)}) collective-permute-start(bf16[64,1024]{1,0:T(8,128)(2,1)} %pad_maximum_fusion.17), channel_id=1, source_target_pairs={{0,2},{1,3},{2,0},{3,1},{4,6},{5,7},{6,4},{7,5},{8,10},{9,11},{10,... | collective-permute-start | bytes 393224 | tf_op jit(solution)/shard_map/ppermute | solution.py:31
  101.0 11.4 %collective-permute-start.30 = (bf16[64,1024]{1,0:T(8,128)(2,1)S(1)}, bf16[64,1024]{1,0:T(8,128)(2,1)S(1)}, u32[]{:S(2)}, u32[]{:S(2)}) collective-permute-start(bf16[64,1024]{1,0:T(8,128)(2,1)S(1)} %pad_maximum_fusion.19), channel_id=1, source_target_pairs={{0,10},{1,11},{2,8},{3,9},{4,14},{5,15},{6,12},{7,13},{8,2},{9,3},... | collective-permute-start | bytes 393224 | tf_op jit(solution)/shard_map/ppermute | solution.py:31
  116.5 9.2 %collective-permute-start.31 = (bf16[64,2048]{1,0:T(8,128)(2,1)S(1)}, bf16[64,2048]{1,0:T(8,128)(2,1)S(1)}, u32[]{:S(2)}, u32[]{:S(2)}) collective-permute-start(bf16[64,2048]{1,0:T(8,128)(2,1)S(1)} %convolution_convert_fusion), channel_id=1, source_target_pairs={{0,2},{1,3},{2,0},{3,1},{4,6},{5,7},{6,4},{7,5},{8,10},{9,11},{10,... | collective-permute-start | bytes 786440 | tf_op jit(solution)/shard_map/ppermute | solution.py:31
  117.9 12.5 %collective-permute-start.28 = (bf16[64,2048]{1,0:T(8,128)(2,1)S(1)}, bf16[64,2048]{1,0:T(8,128)(2,1)S(1)}, u32[]{:S(2)}, u32[]{:S(2)}) collective-permute-start(bf16[64,2048]{1,0:T(8,128)(2,1)S(1)} %convolution_convert_fusion.1), channel_id=1, source_target_pairs={{0,2},{1,3},{2,0},{3,1},{4,6},{5,7},{6,4},{7,5},{8,10},{9,11},{10,... | collective-permute-start | bytes 786440 | tf_op jit(solution)/shard_map/ppermute | solution.py:31
  126.5 11.2 %collective-permute-start.32 = (bf16[64,2048]{1,0:T(8,128)(2,1)S(1)}, bf16[64,2048]{1,0:T(8,128)(2,1)S(1)}, u32[]{:S(2)}, u32[]{:S(2)}) collective-permute-start(bf16[64,2048]{1,0:T(8,128)(2,1)S(1)} %fusion.24), channel_id=1, source_target_pairs={{0,8},{1,9},{2,10},{3,11},{4,12},{5,13},{6,14},{7,15},{8,0},{9,1},... | collective-permute-start | bytes 786440 | tf_op jit(solution)/shard_map/ppermute | solution.py:25
  138.0 7.6 %collective-permute-start.36 = (bf16[64,2048]{1,0:T(8,128)(2,1)S(1)}, bf16[64,2048]{1,0:T(8,128)(2,1)S(1)}, u32[]{:S(2)}, u32[]{:S(2)}) collective-permute-start(bf16[64,2048]{1,0:T(8,128)(2,1)S(1)} %fusion.43), channel_id=1, source_target_pairs={{0,4},{1,5},{2,6},{3,7},{4,0},{5,1},{6,2},{7,3},{8,12},{9,13},{10,... | collective-permute-start | bytes 786440 | tf_op jit(solution)/shard_map/ppermute | solution.py:25
  138.0 8.1 %collective-permute-start.35 = (bf16[64,2048]{1,0:T(8,128)(2,1)S(1)}, bf16[64,2048]{1,0:T(8,128)(2,1)S(1)}, u32[]{:S(2)}, u32[]{:S(2)}) collective-permute-start(bf16[64,2048]{1,0:T(8,128)(2,1)S(1)} %fusion.43), channel_id=1, source_target_pairs={{4,8},{5,9},{6,10},{7,11},{8,4},{9,5},{10,6},{11,7},{20,24},{21,25... | collective-permute-start | bytes 786440 | tf_op jit(solution)/shard_map/ppermute | solution.py:25
  138.7 14.1 %collective-permute-start.33 = (bf16[64,2048]{1,0:T(8,128)(2,1)S(1)}, bf16[64,2048]{1,0:T(8,128)(2,1)S(1)}, u32[]{:S(2)}, u32[]{:S(2)}) collective-permute-start(bf16[64,2048]{1,0:T(8,128)(2,1)S(1)} %fusion.43), channel_id=1, source_target_pairs={{0,2},{1,3},{2,0},{3,1},{4,6},{5,7},{6,4},{7,5},{8,10},{9,11},{10,... | collective-permute-start | bytes 786440 | tf_op jit(solution)/shard_map/ppermute | solution.py:31
  145.6 7.4 %collective-permute-start.44 = (bf16[64,2048]{1,0:T(8,128)(2,1)S(1)}, bf16[64,2048]{1,0:T(8,128)(2,1)S(1)}, u32[]{:S(2)}, u32[]{:S(2)}) collective-permute-start(bf16[64,2048]{1,0:T(8,128)(2,1)S(1)} %collective-permute-done.36), channel_id=1, source_target_pairs={{0,2},{1,3},{2,0},{3,1},{4,6},{5,7},{6,4},{7,5},{8,10},{9,11},{10,... | collective-permute-start | bytes 786440 | tf_op jit(solution)/shard_map/ppermute | solution.py:31
  146.1 17.4 %collective-permute-start.37 = (bf16[64,2048]{1,0:T(8,128)(2,1)S(1)}, bf16[64,2048]{1,0:T(8,128)(2,1)S(1)}, u32[]{:S(2)}, u32[]{:S(2)}) collective-permute-start(bf16[64,2048]{1,0:T(8,128)(2,1)S(1)} %fusion.43), channel_id=1, source_target_pairs={{0,12},{1,13},{2,14},{3,15},{12,0},{13,1},{14,2},{15,3},{16,28},{1... | collective-permute-start | bytes 786440 | tf_op jit(solution)/shard_map/ppermute | solution.py:25
  151.6 10.4 %collective-permute-start.41 = (bf16[64,2048]{1,0:T(8,128)(2,1)S(1)}, bf16[64,2048]{1,0:T(8,128)(2,1)S(1)}, u32[]{:S(2)}, u32[]{:S(2)}) collective-permute-start(bf16[64,2048]{1,0:T(8,128)(2,1)S(1)} %collective-permute-done.35), channel_id=1, source_target_pairs={{4,0},{5,1},{6,2},{7,3},{8,12},{9,13},{10,14},{11,15},{20,16},{21,... | collective-permute-start | bytes 786440 | tf_op jit(solution)/shard_map/ppermute | solution.py:25
  152.9 18.4 %collective-permute-start.34 = (bf16[128,2048]{1,0:T(8,128)(2,1)S(1)}, bf16[128,2048]{1,0:T(8,128)(2,1)S(1)}, u32[]{:S(2)}, u32[]{:S(2)}) collective-permute-start(bf16[128,2048]{1,0:T(8,128)(2,1)S(1)} %pad_maximum_fusion.12), channel_id=1, source_target_pairs={{0,1},{1,0},{2,3},{3,2},{4,5},{5,4},{6,7},{7,6},{8,9},{9,8},{10,11... | collective-permute-start | bytes 1572872 | tf_op jit(solution)/shard_map/ppermute | solution.py:31
  162.0 9.3 %collective-permute-start.42 = (bf16[64,2048]{1,0:T(8,128)(2,1)S(1)}, bf16[64,2048]{1,0:T(8,128)(2,1)S(1)}, u32[]{:S(2)}, u32[]{:S(2)}) collective-permute-start(bf16[64,2048]{1,0:T(8,128)(2,1)S(1)} %broadcast_select_fusion.2), channel_id=1, source_target_pairs={{0,2},{1,3},{2,0},{3,1},{4,6},{5,7},{6,4},{7,5},{8,10},{9,11},{10,... | collective-permute-start | bytes 786440 | tf_op jit(solution)/shard_map/ppermute | solution.py:31
  163.6 15.0 %collective-permute-start.39 = (bf16[64,2048]{1,0:T(8,128)(2,1)S(1)}, bf16[64,2048]{1,0:T(8,128)(2,1)S(1)}, u32[]{:S(2)}, u32[]{:S(2)}) collective-permute-start(bf16[64,2048]{1,0:T(8,128)(2,1)S(1)} %broadcast_select_fusion.3), channel_id=1, source_target_pairs={{0,2},{1,3},{2,0},{3,1},{4,6},{5,7},{6,4},{7,5},{8,10},{9,11},{10,... | collective-permute-start | bytes 786440 | tf_op jit(solution)/shard_map/ppermute | solution.py:31
  164.2 9.6 %collective-permute-start.45 = (bf16[128,2048]{1,0:T(8,128)(2,1)S(1)}, bf16[128,2048]{1,0:T(8,128)(2,1)S(1)}, u32[]{:S(2)}, u32[]{:S(2)}) collective-permute-start(bf16[128,2048]{1,0:T(8,128)(2,1)S(1)} %pad_maximum_fusion.15), channel_id=1, source_target_pairs={{0,1},{1,0},{2,3},{3,2},{4,5},{5,4},{6,7},{7,6},{8,9},{9,8},{10,11... | collective-permute-start | bytes 1572872 | tf_op jit(solution)/shard_map/ppermute | solution.py:31
  178.9 4.6 %collective-permute-start.38 = (bf16[128,2048]{1,0:T(8,128)(2,1)S(1)}, bf16[128,2048]{1,0:T(8,128)(2,1)S(1)}, u32[]{:S(2)}, u32[]{:S(2)}) collective-permute-start(bf16[128,2048]{1,0:T(8,128)(2,1)S(1)} %slice.403), channel_id=1, source_target_pairs={{0,1},{1,0},{2,3},{3,2},{4,5},{5,4},{6,7},{7,6},{8,9},{9,8},{10,11... | collective-permute-start | bytes 1572872 | tf_op jit(solution)/shard_map/ppermute | solution.py:31
  183.8 9.2 %collective-permute-start.52 = (bf16[64,2048]{1,0:T(8,128)(2,1)S(1)}, bf16[64,2048]{1,0:T(8,128)(2,1)S(1)}, u32[]{:S(2)}, u32[]{:S(2)}) collective-permute-start(bf16[64,2048]{1,0:T(8,128)(2,1)S(1)} %slice.419), channel_id=1, source_target_pairs={{0,2},{1,3},{2,0},{3,1},{4,6},{5,7},{6,4},{7,5},{8,10},{9,11},{10,... | collective-permute-start | bytes 786440 | tf_op jit(solution)/shard_map/ppermute | solution.py:31
  185.6 13.1 %collective-permute-start.49 = (bf16[64,2048]{1,0:T(8,128)(2,1)S(1)}, bf16[64,2048]{1,0:T(8,128)(2,1)S(1)}, u32[]{:S(2)}, u32[]{:S(2)}) collective-permute-start(bf16[64,2048]{1,0:T(8,128)(2,1)S(1)} %slice.416), channel_id=1, source_target_pairs={{0,2},{1,3},{2,0},{3,1},{4,6},{5,7},{6,4},{7,5},{8,10},{9,11},{10,... | collective-permute-start | bytes 786440 | tf_op jit(solution)/shard_map/ppermute | solution.py:31
  193.1 19.5 %collective-permute-start.53 = (bf16[64,2048]{1,0:T(8,128)(2,1)S(1)}, bf16[64,2048]{1,0:T(8,128)(2,1)S(1)}, u32[]{:S(2)}, u32[]{:S(2)}) collective-permute-start(bf16[64,2048]{1,0:T(8,128)(2,1)S(1)} %add_convert_fusion.10), channel_id=1, source_target_pairs={{0,8},{1,9},{2,10},{3,11},{4,12},{5,13},{6,14},{7,15},{8,0},{9,1},... | collective-permute-start | bytes 786440 | tf_op jit(solution)/shard_map/ppermute | solution.py:25
  195.1 9.2 %collective-permute-start.55 = (bf16[64,2048]{1,0:T(8,128)(2,1)S(1)}, bf16[64,2048]{1,0:T(8,128)(2,1)S(1)}, u32[]{:S(2)}, u32[]{:S(2)}) collective-permute-start(bf16[64,2048]{1,0:T(8,128)(2,1)S(1)} %slice.423), channel_id=1, source_target_pairs={{0,2},{1,3},{2,0},{3,1},{4,6},{5,7},{6,4},{7,5},{8,10},{9,11},{10,... | collective-permute-start | bytes 786440 | tf_op jit(solution)/shard_map/ppermute | solution.py:31
  198.7 13.9 %collective-permute-start.51 = (bf16[64,2048]{1,0:T(8,128)(2,1)S(1)}, bf16[64,2048]{1,0:T(8,128)(2,1)S(1)}, u32[]{:S(2)}, u32[]{:S(2)}) collective-permute-start(bf16[64,2048]{1,0:T(8,128)(2,1)S(1)} %add_convert_fusion.11), channel_id=1, source_target_pairs={{0,12},{1,13},{2,14},{3,15},{4,8},{5,9},{6,10},{7,11},{8,4},{9,5},... | collective-permute-start | bytes 786440 | tf_op jit(solution)/shard_map/ppermute | solution.py:25
  201.7 10.9 %collective-permute-start.50 = (bf16[64,2048]{1,0:T(8,128)(2,1)S(1)}, bf16[64,2048]{1,0:T(8,128)(2,1)S(1)}, u32[]{:S(2)}, u32[]{:S(2)}) collective-permute-start(bf16[64,2048]{1,0:T(8,128)(2,1)S(1)} %slice.405), channel_id=1, source_target_pairs={{0,2},{1,3},{2,0},{3,1},{4,6},{5,7},{6,4},{7,5},{8,10},{9,11},{10,... | collective-permute-start | bytes 786440 | tf_op jit(solution)/shard_map/ppermute | solution.py:31
  204.5 13.3 %collective-permute-start.56 = (bf16[64,2048]{1,0:T(8,128)(2,1)S(1)}, bf16[64,2048]{1,0:T(8,128)(2,1)S(1)}, u32[]{:S(2)}, u32[]{:S(2)}) collective-permute-start(bf16[64,2048]{1,0:T(8,128)(2,1)S(1)} %add_convert_fusion.9), channel_id=1, source_target_pairs={{0,4},{1,5},{2,6},{3,7},{4,0},{5,1},{6,2},{7,3},{8,12},{9,13},{10,... | collective-permute-start | bytes 786440 | tf_op jit(solution)/shard_map/ppermute | solution.py:25
  (26 other events, 196.5 us)

commit v11 on v7

--- a/solution.py
+++ b/solution.py
@@ -43,7 +43,7 @@
 
 
 def within_plane(ring, chunk):
-    for bit in reversed(ring.bits[1:]):
+    for bit in reversed(ring.bits[1:-1]):
         rows = chunk.shape[0] // 2
         chunk = add(chunk[:rows], ring.across(chunk[rows:], bit))
     return chunk
@@ -54,17 +54,19 @@
 
 
 def gate_lanes(layers):
-    lanes = []
+    pieces = []
     for routes, gates in layers:
-        high = gates.astype(jnp.bfloat16)
-        lanes += [routes.astype(jnp.bfloat16), high, (gates - high.astype(jnp.float32)).astype(jnp.bfloat16)]
-    lanes = jnp.concatenate(lanes, axis=1)
-    return jnp.pad(lanes, ((0, 0), (0, -lanes.shape[1] % 128)))
-
-
-def gate_column(ring, lanes, layer, top):
+        high = gates.astype(jnp.bfloat16).astype(jnp.float32)
+        pieces += [routes.astype(jnp.float32), high, gates - high]
+    top = pieces[0].shape[1]
+    width = -(-top * len(pieces) // 128) * 128
+    placed = [jnp.pad(p, ((0, 0), (i * top, width - (i + 1) * top))) for i, p in enumerate(pieces)]
+    return sum(placed).astype(jnp.bfloat16)
+
+
+def gate_column(lanes, who, layer, top):
     named, high, low = (lanes[:, (3 * layer + i) * top :][:, :top].astype(jnp.float32) for i in range(3))
-    return jnp.sum(jnp.where(named == ring.me.astype(jnp.float32), high + low, 0.0), axis=1, keepdims=True)
+    return jnp.sum(jnp.where(named == who.astype(jnp.float32), high + low, 0.0), axis=1, keepdims=True)
 
 
 def normed(values, gain):
@@ -73,12 +75,14 @@
     return (widened * inverse * gain).astype(jnp.bfloat16)
 
 
-def expert(rows, gates, gate_up, down):
-    width = down.shape[0]
-    projected = jnp.dot(rows, gate_up, preferred_element_type=jnp.float32)
-    hidden = (jax.nn.silu(projected[:, :width]) * projected[:, width:]).astype(jnp.bfloat16)
-    out = jnp.dot(hidden, down, preferred_element_type=jnp.float32)
-    return (out * gates).astype(jnp.bfloat16)
+def two_experts(rows, gates, weights):
+    total = 0.0
+    for gate, (gate_up, down) in zip(gates, weights):
+        width = down.shape[0]
+        projected = jnp.dot(rows, gate_up, preferred_element_type=jnp.float32)
+        hidden = jax.nn.silu(projected[:, :width]) * projected[:, width:] * gate
+        total = total + jnp.dot(hidden.astype(jnp.bfloat16), down, preferred_element_type=jnp.float32)
+    return total.astype(jnp.bfloat16)
 
 
 def routed(ring, rows, work):
@@ -91,25 +95,26 @@
     far = ring.send(columns[1], [(1, 2), (2, 1)])
     columns[3] = jnp.where(ring.inside, middle, ends)
     columns[2] = jnp.where(ring.inside, far, near)
-    crossed[1] = ring.across(after(columns[1], middle), top)
+    crossed[1] = ring.across(after(columns[1], middle, crossed[0]), top)
     crossed[3] = ring.across(columns[3], top)
     crossed[2] = ring.across(columns[2], top)
 
-    done = {}
-    halves = {}
-    last = [columns[2], crossed[1], crossed[3]]
-    for slot in (0, 1, 3, 2):
-        chunk = jnp.concatenate([columns[slot], crossed[slot]], axis=0)
-        if slot == 2:
-            chunk = after(chunk, *last)
-            halves[3] = within_plane(ring, done[3])
-            last = [halves[3]]
-        for bit in ring.bits[1:]:
-            chunk = jnp.concatenate([chunk, ring.across(chunk, bit)], axis=0)
-        done[slot] = work(slot, after(chunk, *last))
-        last = [done[slot]]
-    for slot in (2, 1, 0):
-        halves[slot] = within_plane(ring, done[slot])
+    def chunk(*slots):
+        parts = []
+        for slot in slots:
+            part = jnp.concatenate([columns[slot], crossed[slot]], axis=0)
+            for bit in ring.bits[1:-1]:
+                part = jnp.concatenate([part, ring.across(part, bit)], axis=0)
+            parts.append(part)
+        return jnp.concatenate(parts, axis=0)
+
+    both = work((0, 1), after(chunk(0, 1), columns[2]))
+    third = work((3,), after(chunk(3), both))
+    halves = {3: within_plane(ring, third)}
+    last = work((2,), after(chunk(2), halves[3]))
+    count = both.shape[0] // 2
+    for slot, done in ((2, last), (1, both[count:]), (0, both[:count])):
+        halves[slot] = within_plane(ring, done)
 
     own = rows.shape[0]
     back = {}
@@ -175,17 +180,25 @@
     width = hidden_rows.shape[1]
     lanes = gate_lanes([(first_routes, first_gates), (second_routes, second_gates)])
     top = first_routes.shape[1]
+    people = (ring.me, ring.me ^ 1)
     second_columns = {}
 
-    def first_work(slot, chunk):
-        second_columns[slot] = gate_column(ring, chunk[:, width:], 1, top)
-        gates = gate_column(ring, chunk[:, width:], 0, top)
-        return expert(chunk[:, :width], gates, first_gate_up[0], first_down[0])
-
-    def second_work(slot, chunk):
-        return expert(chunk, second_columns[slot], second_gate_up[0], second_down[0])
+    def pair(gate_up, down, *ties):
+        mine = (gate_up[0], down[0])
+        return mine, tuple(ring.across(after(w, *ties), ring.bits[-1]) for w in mine)
+
+    first_pair = pair(first_gate_up, first_down)
+
+    def first_work(slots, chunk):
+        lanes = chunk[:, width:]
+        second_columns[slots] = [gate_column(lanes, who, 1, top) for who in people]
+        return two_experts(chunk[:, :width], [gate_column(lanes, who, 0, top) for who in people], first_pair)
+
+    def second_work(slots, chunk):
+        return two_experts(chunk, second_columns[slots], second_pair)
 
     first, steps = routed(ring, jnp.concatenate([hidden_rows, lanes], axis=1), first_work)
+    second_pair = pair(second_gate_up, second_down, steps[1])
     ties = [([], [steps[0]]), ([steps[1]], [steps[2]])]
     weight = plane_weight(ring, merge_weight, other_half(ring, merge_weight, lax.axis_size("groups"), ties))
     after_first = (hidden_rows.astype(jnp.float32) + first).astype(jnp.bfloat16)

time: 210 us -> 210 us (level)
  starting transfers between devices: 59.4 us -> 72.6 us
  waiting for transfers between devices: 105 us -> 93.3 us
  other arithmetic: 21.2 us -> 11.8 us
  matrix products: 19.5 us -> 28.5 us
    ppermute x22, starting transfers between devices: 31.3 us -> 51.5 us  [send(): return lax.ppermute(values, 'inner', perm)]
    dot_general x16 -> x24, matrix products: 16.1 us -> 25.2 us  [the longest x12 17.7 us: two_experts(): projected = jnp.dot(rows, gate_up, preferred_element_type=jnp.float32)]
    ppermute x35 -> x23, starting transfers between devices: 25.2 us -> 18 us  [across(): lax.ppermute(values, 'inner', [(d, d ^ bit) for d in range(self.size)])]
    ppermute x35 -> x23, waiting for transfers between devices: 32.9 us -> 27 us  [across(): lax.ppermute(values, 'inner', [(d, d ^ bit) for d in range(self.size)])]
    ppermute x2, waiting for transfers between devices: 4.42 us -> 0.32 us  [other_half(): there = lax.ppermute(here, 'groups', [(g, g ^ 1) for g in range(groups)])]
    unnamed x5 -> x0, other arithmetic: 3.7 us -> none
    convert_element_type x14 -> x6, other arithmetic: 2.97 us -> 0.38 us  [add(): return sum((t.astype(jnp.float32) for t in terms)).astype(jnp.bfloat16)]
    convert_element_type x0 -> x4, other arithmetic: none -> 2.31 us  [the longest x2 1.54 us: gate_lanes(): pieces += [routes.astype(jnp.float32), high, gates - high]]
  transfers between devices with their start and end apart: 59 -> 47, of which waited for: 23 -> 21; matrix products, arithmetic and copies ran while one was open for 18% -> 18% of each run, Pallas kernels for 0% -> 0%
where the time goes in v11:
time: 210 us; the launch traced here: 209 us
  waiting for transfers between devices  93.3 us (44%)
  starting transfers between devices  72.6 us (35%)
  matrix products  28.5 us (14%)
  other arithmetic  11.8 us (6%)
  local copies, waits for them, and re-layouts  2.16 us (1%)
    ppermute x22, waiting for transfers between devices, send(): return lax.ppermute(values, 'inner', perm)  66 us
    ppermute x22, starting transfers between devices, send(): return lax.ppermute(values, 'inner', perm)  51.5 us
    ppermute x23, waiting for transfers between devices, across(): lax.ppermute(values, 'inner', [(d, d ^ bit) for d in range(self.size)])  27 us
    ppermute x23, starting transfers between devices, across(): lax.ppermute(values, 'inner', [(d, d ^ bit) for d in range(self.size)])  18 us
    dot_general x12, matrix products, two_experts(): projected = jnp.dot(rows, gate_up, preferred_element_type=jnp.float32)  17.7 us
    dot_general x12, matrix products, two_experts(): jnp.dot(hidden.astype(jnp.bfloat16), down, preferred_element_type=jnp.flo...  7.48 us
  transfers between devices with their start and end apart: 47, of which 21 were waited for; matrix products, arithmetic and copies ran while one was open for 18% of the time, Pallas kernels for 0%

profile of v11, /device:TPU:0, one launch (start us, length us, event | category | flops | bytes accessed | tf_op | source)
XLA Modules:
  0.0 209.2 jit_solution(6087495968873474758)
XLA Ops:
  3.5 3.1 %collective-permute-start.1 = (bf16[64,2176]{1,0:T(8,128)(2,1)S(1)}, bf16[64,2176]{1,0:T(8,128)(2,1)S(1)}, u32[]{:S(2)}, u32[]{:S(2)}) collective-permute-start(bf16[64,2176]{1,0:T(8,128)(2,1)S(1)} %pad_maximum_fusion.7), channel_id=1, source_target_pairs={{0,4},{1,5},{2,6},{3,7},{4,0},{5,1},{6,2},{7,3},{8,12},{9,13},{10,... | collective-permute-start | bytes 835592 | tf_op jit(solution)/shard_map/ppermute | solution.py:25
  7.2 1.6 collective-permute-start
  8.8 4.4 %collective-permute-start.9 = (bf16[64,2176]{1,0:T(8,128)(2,1)S(1)}, bf16[64,2176]{1,0:T(8,128)(2,1)}, u32[]{:S(2)}, u32[]{:S(2)}) collective-permute-start(bf16[64,2176]{1,0:T(8,128)(2,1)S(1)} %pad_maximum_fusion.7), channel_id=1, source_target_pairs={{0,12},{1,13},{2,14},{3,15},{12,0},{13,1},{14,2},{15,3},{16,28},{1... | collective-permute-start | bytes 835592 | tf_op jit(solution)/shard_map/ppermute | solution.py:25
  14.5 1.9 constant_dynamic-slice_fusion.1
  18.6 3.0 %collective-permute-done.9 = bf16[64,2176]{1,0:T(8,128)(2,1)} collective-permute-done((bf16[64,2176]{1,0:T(8,128)(2,1)S(1)}, bf16[64,2176]{1,0:T(8,128)(2,1)}, u32[]{:S(2)}, u32[]{:S(2)}) %collective-permute-start.9) | collective-permute-done | bytes 278560 | tf_op jit(solution)/shard_map/ppermute | solution.py:25
  21.6 1.3 collective-permute-start.5
  23.9 1.6 collective-permute-start.18
  26.0 8.1 %collective-permute-done.5 = bf16[64,2176]{1,0:T(8,128)(2,1)S(1)} collective-permute-done((bf16[64,2176]{1,0:T(8,128)(2,1)S(1)}, bf16[64,2176]{1,0:T(8,128)(2,1)S(1)}, u32[]{:S(2)}, u32[]{:S(2)}) %collective-permute-start.5) | collective-permute-done | bytes 278560 | tf_op jit(solution)/shard_map/ppermute | solution.py:25
  34.1 1.5 collective-permute-start.10
  35.6 3.8 %collective-permute-done.3 = bf16[64,2176]{1,0:T(8,128)(2,1)S(1)} collective-permute-done((bf16[64,2176]{1,0:T(8,128)(2,1)S(1)}, bf16[64,2176]{1,0:T(8,128)(2,1)S(1)}, u32[]{:S(2)}, u32[]{:S(2)}) %collective-permute-start.3) | collective-permute-done | bytes 278560 | tf_op jit(solution)/shard_map/ppermute | solution.py:31
  39.4 1.5 collective-permute-start.8
  41.0 1.6 collective-permute-start.19
  42.6 2.8 %collective-permute-done.10 = bf16[64,2176]{1,0:T(8,128)(2,1)S(1)} collective-permute-done((bf16[64,2176]{1,0:T(8,128)(2,1)S(1)}, bf16[64,2176]{1,0:T(8,128)(2,1)S(1)}, u32[]{:S(2)}, u32[]{:S(2)}) %collective-permute-start.10) | collective-permute-done | bytes 278560 | tf_op jit(solution)/shard_map/ppermute | solution.py:31
  45.8 1.3 fusion.8
  48.0 1.4 collective-permute-done.8
  49.4 1.3 collective-permute-start.20
  50.8 3.5 %fusion.6 = f32[256,1024]{1,0:T(8,128)S(1)} fusion(bf16[2048,1024]{1,0:T(8,128)(2,1)} %collective-permute-done.6, bf16[256,2176]{1,0:T(8,128)(2,1)S(1)} %pad_maximum_fusion), kind=kOutput, calls=%fused_computation.21 | convolution fusion | flops 1073741824 | bytes 6291456 | tf_op jit(solution)/shard_map/dot_general | solution.py:82
  56.7 2.9 %fusion.29 = f32[128,1024]{1,0:T(8,128)S(1)} fusion(bf16[2048,1024]{1,0:T(8,128)(2,1)} %collective-permute-done.6, bf16[128,2176]{1,0:T(8,128)(2,1)S(1)} %pad_maximum_fusion.4), kind=kOutput, calls=%fused_computation.75 | convolution fusion | flops 536870912 | bytes 5242880 | tf_op jit(solution)/shard_map/dot_general | solution.py:82
  62.5 2.9 %fusion.25 = f32[128,1024]{1,0:T(8,128)S(1)} fusion(bf16[2048,1024]{1,0:T(8,128)(2,1)} %collective-permute-done.6, bf16[128,2176]{1,0:T(8,128)(2,1)S(1)} %pad_maximum_fusion.3), kind=kOutput, calls=%fused_computation.71 | convolution fusion | flops 536870912 | bytes 5242880 | tf_op jit(solution)/shard_map/dot_general | solution.py:82
  66.0 1.4 collective-permute-start.11
  67.5 1.5 collective-permute-done.13
  69.2 6.2 %collective-permute-done.11 = bf16[64,2048]{1,0:T(8,128)(2,1)S(1)} collective-permute-done((bf16[64,2048]{1,0:T(8,128)(2,1)S(1)}, bf16[64,2048]{1,0:T(8,128)(2,1)S(1)}, u32[]{:S(2)}, u32[]{:S(2)}) %collective-permute-start.11) | collective-permute-done | bytes 262176 | tf_op jit(solution)/shard_map/ppermute | solution.py:31
  75.3 1.5 collective-permute-start.21
  76.9 4.5 %collective-permute-start.15 = (bf16[64,2048]{1,0:T(8,128)(2,1)S(1)}, bf16[64,2048]{1,0:T(8,128)(2,1)S(1)}, u32[]{:S(2)}, u32[]{:S(2)}) collective-permute-start(bf16[64,2048]{1,0:T(8,128)(2,1)S(1)} %add_convert_fusion.7), channel_id=1, source_target_pairs={{0,8},{1,9},{2,10},{3,11},{4,12},{5,13},{6,14},{7,15},{8,0},{9,1},... | collective-permute-start | bytes 786440 | tf_op jit(solution)/shard_map/ppermute | solution.py:25
  82.6 4.3 %collective-permute-start.14 = (bf16[64,2048]{1,0:T(8,128)(2,1)S(1)}, bf16[64,2048]{1,0:T(8,128)(2,1)S(1)}, u32[]{:S(2)}, u32[]{:S(2)}) collective-permute-start(bf16[64,2048]{1,0:T(8,128)(2,1)S(1)} %add_convert_fusion.8), channel_id=1, source_target_pairs={{0,12},{1,13},{2,14},{3,15},{4,8},{5,9},{6,10},{7,11},{8,4},{9,5},... | collective-permute-start | bytes 786440 | tf_op jit(solution)/shard_map/ppermute | solution.py:25
  87.7 1.4 collective-permute-start.17
  89.5 7.0 %collective-permute-done.15 = bf16[64,2048]{1,0:T(8,128)(2,1)S(1)} collective-permute-done((bf16[64,2048]{1,0:T(8,128)(2,1)S(1)}, bf16[64,2048]{1,0:T(8,128)(2,1)S(1)}, u32[]{:S(2)}, u32[]{:S(2)}) %collective-permute-start.15) | collective-permute-done | bytes 262176 | tf_op jit(solution)/shard_map/ppermute | solution.py:25
  96.6 4.2 %collective-permute-done.17 = bf16[64,2048]{1,0:T(8,128)(2,1)S(1)} collective-permute-done((bf16[64,2048]{1,0:T(8,128)(2,1)S(1)}, bf16[64,2048]{1,0:T(8,128)(2,1)S(1)}, u32[]{:S(2)}, u32[]{:S(2)}) %collective-permute-start.17) | collective-permute-done | bytes 262176 | tf_op jit(solution)/shard_map/ppermute | solution.py:25
  102.4 3.3 %collective-permute-start.25 = (bf16[64,1024]{1,0:T(8,128)(2,1)S(1)}, bf16[64,1024]{1,0:T(8,128)(2,1)S(1)}, u32[]{:S(2)}, u32[]{:S(2)}) collective-permute-start(bf16[64,1024]{1,0:T(8,128)(2,1)S(1)} %get-tuple-element.62), channel_id=1, source_target_pairs={{0,8},{1,9},{2,10},{3,11},{4,12},{5,13},{6,14},{7,15},{8,0},{9,1},... | collective-permute-start | bytes 393224 | tf_op jit(solution)/shard_map/ppermute | solution.py:25
  106.7 2.2 %collective-permute-done.27 = bf16[64,1024]{1,0:T(8,128)(2,1)S(1)} collective-permute-done((bf16[64,1024]{1,0:T(8,128)(2,1)S(1)}, bf16[64,1024]{1,0:T(8,128)(2,1)S(1)}, u32[]{:S(2)}, u32[]{:S(2)}) %collective-permute-start.27) | collective-permute-done | bytes 131104 | tf_op jit(solution)/shard_map/ppermute | solution.py:25
  109.8 5.8 %collective-permute-done.25 = bf16[64,1024]{1,0:T(8,128)(2,1)S(1)} collective-permute-done((bf16[64,1024]{1,0:T(8,128)(2,1)S(1)}, bf16[64,1024]{1,0:T(8,128)(2,1)S(1)}, u32[]{:S(2)}, u32[]{:S(2)}) %collective-permute-start.25) | collective-permute-done | bytes 131104 | tf_op jit(solution)/shard_map/ppermute | solution.py:25
  117.4 2.9 %collective-permute-start.24 = (bf16[64,2048]{1,0:T(8,128)(2,1)S(1)}, bf16[64,2048]{1,0:T(8,128)(2,1)S(1)}, u32[]{:S(2)}, u32[]{:S(2)}) collective-permute-start(bf16[64,2048]{1,0:T(8,128)(2,1)S(1)} %convolution_convert_fusion.2), channel_id=1, source_target_pairs={{0,12},{1,13},{2,14},{3,15},{4,8},{5,9},{6,10},{7,11},{8,4},{9,5},... | collective-permute-start | bytes 786440 | tf_op jit(solution)/shard_map/ppermute | solution.py:25
  121.4 15.5 %collective-permute-done.26 = bf16[64,2048]{1,0:T(8,128)(2,1)S(1)} collective-permute-done((bf16[64,2048]{1,0:T(8,128)(2,1)S(1)}, bf16[64,2048]{1,0:T(8,128)(2,1)S(1)}, u32[]{:S(2)}, u32[]{:S(2)}) %collective-permute-start.26) | collective-permute-done | bytes 262176 | tf_op jit(solution)/shard_map/ppermute | solution.py:25
  137.1 3.9 %collective-permute-start.30 = (bf16[64,2048]{1,0:T(8,128)(2,1)S(1)}, bf16[64,2048]{1,0:T(8,128)(2,1)S(1)}, u32[]{:S(2)}, u32[]{:S(2)}) collective-permute-start(bf16[64,2048]{1,0:T(8,128)(2,1)S(1)} %fusion.16), channel_id=1, source_target_pairs={{0,4},{1,5},{2,6},{3,7},{4,0},{5,1},{6,2},{7,3},{8,12},{9,13},{10,... | collective-permute-start | bytes 786440 | tf_op jit(solution)/shard_map/ppermute | solution.py:25
  141.7 4.3 %collective-permute-start.38 = (bf16[64,2048]{1,0:T(8,128)(2,1)S(1)}, bf16[64,2048]{1,0:T(8,128)(2,1)S(1)}, u32[]{:S(2)}, u32[]{:S(2)}) collective-permute-start(bf16[64,2048]{1,0:T(8,128)(2,1)S(1)} %fusion.16), channel_id=1, source_target_pairs={{0,12},{1,13},{2,14},{3,15},{12,0},{13,1},{14,2},{15,3},{16,28},{1... | collective-permute-start | bytes 786440 | tf_op jit(solution)/shard_map/ppermute | solution.py:25
  146.2 1.9 collective-permute-done.29
  148.9 5.2 %collective-permute-done.38 = bf16[64,2048]{1,0:T(8,128)(2,1)S(1)} collective-permute-done((bf16[64,2048]{1,0:T(8,128)(2,1)S(1)}, bf16[64,2048]{1,0:T(8,128)(2,1)S(1)}, u32[]{:S(2)}, u32[]{:S(2)}) %collective-permute-start.38) | collective-permute-done | bytes 262176 | tf_op jit(solution)/shard_map/ppermute | solution.py:25
  154.1 1.3 collective-permute-start.34
  155.6 9.1 %collective-permute-done.34 = bf16[64,2048]{1,0:T(8,128)(2,1)S(1)} collective-permute-done((bf16[64,2048]{1,0:T(8,128)(2,1)S(1)}, bf16[64,2048]{1,0:T(8,128)(2,1)S(1)}, u32[]{:S(2)}, u32[]{:S(2)}) %collective-permute-start.34) | collective-permute-done | bytes 262176 | tf_op jit(solution)/shard_map/ppermute | solution.py:25
  164.7 2.1 collective-permute-start.37
  166.9 1.3 fusion.110
  176.4 6.1 %collective-permute-done.42 = bf16[64,2048]{1,0:T(8,128)(2,1)S(1)} collective-permute-done((bf16[64,2048]{1,0:T(8,128)(2,1)S(1)}, bf16[64,2048]{1,0:T(8,128)(2,1)S(1)}, u32[]{:S(2)}, u32[]{:S(2)}) %collective-permute-start.42) | collective-permute-done | bytes 262176 | tf_op jit(solution)/shard_map/ppermute | solution.py:31
  182.6 2.0 collective-permute-start.40
  185.6 3.4 %collective-permute-done.45 = bf16[64,2048]{1,0:T(8,128)(2,1)S(1)} collective-permute-done((bf16[64,2048]{1,0:T(8,128)(2,1)S(1)}, bf16[64,2048]{1,0:T(8,128)(2,1)S(1)}, u32[]{:S(2)}, u32[]{:S(2)}) %collective-permute-start.45) | collective-permute-done | bytes 262176 | tf_op jit(solution)/shard_map/ppermute | solution.py:31
  189.0 7.9 %collective-permute-start.46 = (bf16[64,2048]{1,0:T(8,128)(2,1)S(1)}, bf16[64,2048]{1,0:T(8,128)(2,1)S(1)}, u32[]{:S(2)}, u32[]{:S(2)}) collective-permute-start(bf16[64,2048]{1,0:T(8,128)(2,1)S(1)} %add_convert_fusion.1), channel_id=1, source_target_pairs={{0,4},{1,5},{2,6},{3,7},{4,0},{5,1},{6,2},{7,3},{8,12},{9,13},{10,... | collective-permute-start | bytes 786440 | tf_op jit(solution)/shard_map/ppermute | solution.py:25
  197.0 4.2 %collective-permute-start.44 = (bf16[64,2048]{1,0:T(8,128)(2,1)S(1)}, bf16[64,2048]{1,0:T(8,128)(2,1)S(1)}, u32[]{:S(2)}, u32[]{:S(2)}) collective-permute-start(bf16[64,2048]{1,0:T(8,128)(2,1)S(1)} %add_convert_fusion.2), channel_id=1, source_target_pairs={{0,8},{1,9},{2,10},{3,11},{4,12},{5,13},{6,14},{7,15},{8,0},{9,1},... | collective-permute-start | bytes 786440 | tf_op jit(solution)/shard_map/ppermute | solution.py:25
  201.1 1.5 collective-permute-start.41
  202.7 5.6 %collective-permute-done.44 = bf16[64,2048]{1,0:T(8,128)(2,1)S(1)} collective-permute-done((bf16[64,2048]{1,0:T(8,128)(2,1)S(1)}, bf16[64,2048]{1,0:T(8,128)(2,1)S(1)}, u32[]{:S(2)}, u32[]{:S(2)}) %collective-permute-start.44) | collective-permute-done | bytes 262176 | tf_op jit(solution)/shard_map/ppermute | solution.py:25
  (139 shorter events, 37.7 us)
Async XLA Ops:
  2.4 38.5 %copy-start.5 = (bf16[64,2048]{1,0:T(8,128)(2,1)S(1)}, bf16[64,2048]{1,0:T(8,128)(2,1)}, u32[]{:S(2)}) copy-start(bf16[64,2048]{1,0:T(8,128)(2,1)} %param.13) | copy-start | bytes 786436
  3.5 14.0 %collective-permute-start.1 = (bf16[64,2176]{1,0:T(8,128)(2,1)S(1)}, bf16[64,2176]{1,0:T(8,128)(2,1)S(1)}, u32[]{:S(2)}, u32[]{:S(2)}) collective-permute-start(bf16[64,2176]{1,0:T(8,128)(2,1)S(1)} %pad_maximum_fusion.7), channel_id=1, source_target_pairs={{0,4},{1,5},{2,6},{3,7},{4,0},{5,1},{6,2},{7,3},{8,12},{9,13},{10,... | collective-permute-start | bytes 835592 | tf_op jit(solution)/shard_map/ppermute | solution.py:25
  6.6 11.4 %collective-permute-start.2 = (bf16[64,2176]{1,0:T(8,128)(2,1)S(1)}, bf16[64,2176]{1,0:T(8,128)(2,1)S(1)}, u32[]{:S(2)}, u32[]{:S(2)}) collective-permute-start(bf16[64,2176]{1,0:T(8,128)(2,1)S(1)} %pad_maximum_fusion.7), channel_id=1, source_target_pairs={{4,8},{5,9},{6,10},{7,11},{8,4},{9,5},{10,6},{11,7},{20,24},{21,25... | collective-permute-start | bytes 835592 | tf_op jit(solution)/shard_map/ppermute | solution.py:25
  7.2 16.7 %collective-permute-start = (bf16[64,2176]{1,0:T(8,128)(2,1)S(1)}, bf16[64,2176]{1,0:T(8,128)(2,1)S(1)}, u32[]{:S(2)}, u32[]{:S(2)}) collective-permute-start(bf16[64,2176]{1,0:T(8,128)(2,1)S(1)} %pad_maximum_fusion.7), channel_id=1, source_target_pairs={{0,2},{1,3},{2,0},{3,1},{4,6},{5,7},{6,4},{7,5},{8,10},{9,11},{10,... | collective-permute-start | bytes 835592 | tf_op jit(solution)/shard_map/ppermute | solution.py:31
  8.8 12.8 %collective-permute-start.9 = (bf16[64,2176]{1,0:T(8,128)(2,1)S(1)}, bf16[64,2176]{1,0:T(8,128)(2,1)}, u32[]{:S(2)}, u32[]{:S(2)}) collective-permute-start(bf16[64,2176]{1,0:T(8,128)(2,1)S(1)} %pad_maximum_fusion.7), channel_id=1, source_target_pairs={{0,12},{1,13},{2,14},{3,15},{12,0},{13,1},{14,2},{15,3},{16,28},{1... | collective-permute-start | bytes 835592 | tf_op jit(solution)/shard_map/ppermute | solution.py:25
  13.2 37.6 %collective-permute-start.6 = (bf16[2048,1024]{1,0:T(8,128)(2,1)}, bf16[2048,1024]{1,0:T(8,128)(2,1)}, u32[]{:S(2)}, u32[]{:S(2)}) collective-permute-start(bf16[2048,1024]{1,0:T(8,128)(2,1)} %bitcast.65), channel_id=1, source_target_pairs={{0,1},{1,0},{2,3},{3,2},{4,5},{5,4},{6,7},{7,6},{8,9},{9,8},{10,11... | collective-permute-start | bytes 12582920 | tf_op jit(solution)/shard_map/ppermute | solution.py:31
  17.5 36.8 %collective-permute-start.7 = (bf16[512,2048]{1,0:T(8,128)(2,1)S(1)}, bf16[512,2048]{1,0:T(8,128)(2,1)S(1)}, u32[]{:S(2)}, u32[]{:S(2)}) collective-permute-start(bf16[512,2048]{1,0:T(8,128)(2,1)S(1)} %bitcast.67), channel_id=1, source_target_pairs={{0,1},{1,0},{2,3},{3,2},{4,5},{5,4},{6,7},{7,6},{8,9},{9,8},{10,11... | collective-permute-start | bytes 6291464 | tf_op jit(solution)/shard_map/ppermute | solution.py:31
  18.0 7.5 %collective-permute-start.4 = (bf16[64,2176]{1,0:T(8,128)(2,1)S(1)}, bf16[64,2176]{1,0:T(8,128)(2,1)S(1)}, u32[]{:S(2)}, u32[]{:S(2)}) collective-permute-start(bf16[64,2176]{1,0:T(8,128)(2,1)S(1)} %collective-permute-done.1), channel_id=1, source_target_pairs={{4,8},{5,9},{6,10},{7,11},{8,4},{9,5},{10,6},{11,7},{20,24},{21,25... | collective-permute-start | bytes 835592 | tf_op jit(solution)/shard_map/ppermute | solution.py:25
  21.6 12.5 %collective-permute-start.5 = (bf16[64,2176]{1,0:T(8,128)(2,1)S(1)}, bf16[64,2176]{1,0:T(8,128)(2,1)S(1)}, u32[]{:S(2)}, u32[]{:S(2)}) collective-permute-start(bf16[64,2176]{1,0:T(8,128)(2,1)S(1)} %collective-permute-done.2), channel_id=1, source_target_pairs={{4,0},{5,1},{6,2},{7,3},{8,12},{9,13},{10,14},{11,15},{20,16},{21,... | collective-permute-start | bytes 835592 | tf_op jit(solution)/shard_map/ppermute | solution.py:25
  23.9 17.1 %collective-permute-start.18 = (bf16[64,2048]{1,0:T(8,128)(2,1)}, bf16[64,2048]{1,0:T(8,128)(2,1)S(1)}, u32[]{:S(2)}, u32[]{:S(2)}) collective-permute-start(bf16[64,2048]{1,0:T(8,128)(2,1)} %get-tuple-element.57), channel_id=1, source_target_pairs={{0,2},{1,3},{2,0},{3,1},{4,6},{5,7},{6,4},{7,5},{8,10},{9,11},{10,... | collective-permute-start | bytes 786440 | tf_op jit(solution)/shard_map/ppermute | solution.py:31
  25.5 13.9 %collective-permute-start.3 = (bf16[64,2176]{1,0:T(8,128)(2,1)S(1)}, bf16[64,2176]{1,0:T(8,128)(2,1)S(1)}, u32[]{:S(2)}, u32[]{:S(2)}) collective-permute-start(bf16[64,2176]{1,0:T(8,128)(2,1)S(1)} %collective-permute-done.1), channel_id=1, source_target_pairs={{0,2},{1,3},{2,0},{3,1},{4,6},{5,7},{6,4},{7,5},{8,10},{9,11},{10,... | collective-permute-start | bytes 835592 | tf_op jit(solution)/shard_map/ppermute | solution.py:31
  34.1 11.3 %collective-permute-start.10 = (bf16[64,2176]{1,0:T(8,128)(2,1)S(1)}, bf16[64,2176]{1,0:T(8,128)(2,1)S(1)}, u32[]{:S(2)}, u32[]{:S(2)}) collective-permute-start(bf16[64,2176]{1,0:T(8,128)(2,1)S(1)} %broadcast_select_fusion), channel_id=1, source_target_pairs={{0,2},{1,3},{2,0},{3,1},{4,6},{5,7},{6,4},{7,5},{8,10},{9,11},{10,... | collective-permute-start | bytes 835592 | tf_op jit(solution)/shard_map/ppermute | solution.py:31
  39.4 10.0 %collective-permute-start.8 = (bf16[64,2176]{1,0:T(8,128)(2,1)S(1)}, bf16[64,2176]{1,0:T(8,128)(2,1)S(1)}, u32[]{:S(2)}, u32[]{:S(2)}) collective-permute-start(bf16[64,2176]{1,0:T(8,128)(2,1)S(1)} %broadcast_select_fusion.1), channel_id=1, source_target_pairs={{0,2},{1,3},{2,0},{3,1},{4,6},{5,7},{6,4},{7,5},{8,10},{9,11},{10,... | collective-permute-start | bytes 835592 | tf_op jit(solution)/shard_map/ppermute | solution.py:31
  41.0 6.9 %collective-permute-start.19 = (bf16[64,2048]{1,0:T(8,128)(2,1)S(1)}, bf16[64,2048]{1,0:T(8,128)(2,1)S(1)}, u32[]{:S(2)}, u32[]{:S(2)}) collective-permute-start(bf16[64,2048]{1,0:T(8,128)(2,1)S(1)} %collective-permute-done.18), channel_id=1, source_target_pairs={{0,16},{16,0},{1,17},{17,1},{2,18},{18,2},{3,19},{19,3},{4,20},{20... | collective-permute-start | bytes 786440 | tf_op jit(solution)/shard_map/ppermute | solution.py:139
  49.4 19.8 %collective-permute-start.20 = (bf16[64,2048]{1,0:T(8,128)(2,1)S(1)}, bf16[64,2048]{1,0:T(8,128)(2,1)S(1)}, u32[]{:S(2)}, u32[]{:S(2)}) collective-permute-start(bf16[64,2048]{1,0:T(8,128)(2,1)S(1)} %copy-done.6), channel_id=1, source_target_pairs={{0,2},{1,3},{2,0},{3,1},{4,6},{5,7},{6,4},{7,5},{8,10},{9,11},{10,... | collective-permute-start | bytes 786440 | tf_op jit(solution)/shard_map/ppermute | solution.py:31
  61.2 7.7 %collective-permute-start.13 = (bf16[64,2048]{1,0:T(8,128)(2,1)S(1)}, bf16[64,2048]{1,0:T(8,128)(2,1)S(1)}, u32[]{:S(2)}, u32[]{:S(2)}) collective-permute-start(bf16[64,2048]{1,0:T(8,128)(2,1)S(1)} %slice.356), channel_id=1, source_target_pairs={{0,2},{1,3},{2,0},{3,1},{4,6},{5,7},{6,4},{7,5},{8,10},{9,11},{10,... | collective-permute-start | bytes 786440 | tf_op jit(solution)/shard_map/ppermute | solution.py:31
  66.0 9.3 %collective-permute-start.11 = (bf16[64,2048]{1,0:T(8,128)(2,1)S(1)}, bf16[64,2048]{1,0:T(8,128)(2,1)S(1)}, u32[]{:S(2)}, u32[]{:S(2)}) collective-permute-start(bf16[64,2048]{1,0:T(8,128)(2,1)S(1)} %slice.354), channel_id=1, source_target_pairs={{0,2},{1,3},{2,0},{3,1},{4,6},{5,7},{6,4},{7,5},{8,10},{9,11},{10,... | collective-permute-start | bytes 786440 | tf_op jit(solution)/shard_map/ppermute | solution.py:31
  68.9 18.7 %collective-permute-start.16 = (bf16[64,2048]{1,0:T(8,128)(2,1)S(1)}, bf16[64,2048]{1,0:T(8,128)(2,1)S(1)}, u32[]{:S(2)}, u32[]{:S(2)}) collective-permute-start(bf16[64,2048]{1,0:T(8,128)(2,1)S(1)} %get-tuple-element.27), channel_id=1, source_target_pairs={{0,2},{1,3},{2,0},{3,1},{4,6},{5,7},{6,4},{7,5},{8,10},{9,11},{10,... | collective-permute-start | bytes 786440 | tf_op jit(solution)/shard_map/ppermute | solution.py:31
  75.3 6.4 %collective-permute-start.21 = (bf16[64,2048]{1,0:T(8,128)(2,1)S(1)}, bf16[64,2048]{1,0:T(8,128)(2,1)S(1)}, u32[]{:S(2)}, u32[]{:S(2)}) collective-permute-start(bf16[64,2048]{1,0:T(8,128)(2,1)S(1)} %collective-permute-done.20), channel_id=1, source_target_pairs={{0,16},{16,0},{1,17},{17,1},{2,18},{18,2},{3,19},{19,3},{4,20},{20... | collective-permute-start | bytes 786440 | tf_op jit(solution)/shard_map/ppermute | solution.py:139
  76.9 19.6 %collective-permute-start.15 = (bf16[64,2048]{1,0:T(8,128)(2,1)S(1)}, bf16[64,2048]{1,0:T(8,128)(2,1)S(1)}, u32[]{:S(2)}, u32[]{:S(2)}) collective-permute-start(bf16[64,2048]{1,0:T(8,128)(2,1)S(1)} %add_convert_fusion.7), channel_id=1, source_target_pairs={{0,8},{1,9},{2,10},{3,11},{4,12},{5,13},{6,14},{7,15},{8,0},{9,1},... | collective-permute-start | bytes 786440 | tf_op jit(solution)/shard_map/ppermute | solution.py:25
  82.4 23.6 %collective-permute-start.22 = (bf16[2,256,2048]{2,1,0:T(8,128)(2,1)S(1)}, bf16[2,256,2048]{2,1,0:T(8,128)(2,1)S(1)}, u32[]{:S(2)}, u32[]{:S(2)}) collective-permute-start(bf16[2,256,2048]{2,1,0:T(8,128)(2,1)S(1)} %maximum_select_fusion.1), channel_id=1, source_target_pairs={{0,1},{1,0},{2,3},{3,2},{4,5},{5,4},{6,7},{7,6},{8,9},{9,8},{10,11... | collective-permute-start | bytes 6291464 | tf_op jit(solution)/shard_map/ppermute | solution.py:31
  82.6 14.0 %collective-permute-start.14 = (bf16[64,2048]{1,0:T(8,128)(2,1)S(1)}, bf16[64,2048]{1,0:T(8,128)(2,1)S(1)}, u32[]{:S(2)}, u32[]{:S(2)}) collective-permute-start(bf16[64,2048]{1,0:T(8,128)(2,1)S(1)} %add_convert_fusion.8), channel_id=1, source_target_pairs={{0,12},{1,13},{2,14},{3,15},{4,8},{5,9},{6,10},{7,11},{8,4},{9,5},... | collective-permute-start | bytes 786440 | tf_op jit(solution)/shard_map/ppermute | solution.py:25
  86.8 9.7 %collective-permute-start.12 = (bf16[64,2048]{1,0:T(8,128)(2,1)S(1)}, bf16[64,2048]{1,0:T(8,128)(2,1)S(1)}, u32[]{:S(2)}, u32[]{:S(2)}) collective-permute-start(bf16[64,2048]{1,0:T(8,128)(2,1)S(1)} %get-tuple-element.26), channel_id=1, source_target_pairs={{0,2},{1,3},{2,0},{3,1},{4,6},{5,7},{6,4},{7,5},{8,10},{9,11},{10,... | collective-permute-start | bytes 786440 | tf_op jit(solution)/shard_map/ppermute | solution.py:31
  87.7 13.1 %collective-permute-start.17 = (bf16[64,2048]{1,0:T(8,128)(2,1)S(1)}, bf16[64,2048]{1,0:T(8,128)(2,1)S(1)}, u32[]{:S(2)}, u32[]{:S(2)}) collective-permute-start(bf16[64,2048]{1,0:T(8,128)(2,1)S(1)} %add_convert_fusion.6), channel_id=1, source_target_pairs={{0,4},{1,5},{2,6},{3,7},{4,0},{5,1},{6,2},{7,3},{8,12},{9,13},{10,... | collective-permute-start | bytes 786440 | tf_op jit(solution)/shard_map/ppermute | solution.py:25
  96.5 72.5 %collective-permute-start.35 = (bf16[2048,1024]{1,0:T(8,128)(2,1)S(1)}, bf16[2048,1024]{1,0:T(8,128)(2,1)S(1)}, u32[]{:S(2)}, u32[]{:S(2)}) collective-permute-start(bf16[2048,1024]{1,0:T(8,128)(2,1)S(1)} %bitcast.66), channel_id=1, source_target_pairs={{0,1},{1,0},{2,3},{3,2},{4,5},{5,4},{6,7},{7,6},{8,9},{9,8},{10,11... | collective-permute-start | bytes 12582920 | tf_op jit(solution)/shard_map/ppermute | solution.py:31
  101.5 7.3 %collective-permute-start.27 = (bf16[64,1024]{1,0:T(8,128)(2,1)S(1)}, bf16[64,1024]{1,0:T(8,128)(2,1)S(1)}, u32[]{:S(2)}, u32[]{:S(2)}) collective-permute-start(bf16[64,1024]{1,0:T(8,128)(2,1)S(1)} %get-tuple-element.63), channel_id=1, source_target_pairs={{0,4},{1,5},{2,6},{3,7},{4,0},{5,1},{6,2},{7,3},{8,12},{9,13},{10,... | collective-permute-start | bytes 393224 | tf_op jit(solution)/shard_map/ppermute | solution.py:25
  102.4 13.2 %collective-permute-start.25 = (bf16[64,1024]{1,0:T(8,128)(2,1)S(1)}, bf16[64,1024]{1,0:T(8,128)(2,1)S(1)}, u32[]{:S(2)}, u32[]{:S(2)}) collective-permute-start(bf16[64,1024]{1,0:T(8,128)(2,1)S(1)} %get-tuple-element.62), channel_id=1, source_target_pairs={{0,8},{1,9},{2,10},{3,11},{4,12},{5,13},{6,14},{7,15},{8,0},{9,1},... | collective-permute-start | bytes 393224 | tf_op jit(solution)/shard_map/ppermute | solution.py:25
  105.7 10.8 %collective-permute-start.23 = (bf16[64,1024]{1,0:T(8,128)(2,1)S(1)}, bf16[64,1024]{1,0:T(8,128)(2,1)S(1)}, u32[]{:S(2)}, u32[]{:S(2)}) collective-permute-start(bf16[64,1024]{1,0:T(8,128)(2,1)S(1)} %get-tuple-element.61), channel_id=1, source_target_pairs={{0,12},{1,13},{2,14},{3,15},{4,8},{5,9},{6,10},{7,11},{8,4},{9,5},... | collective-permute-start | bytes 393224 | tf_op jit(solution)/shard_map/ppermute | solution.py:25
  109.7 11.6 %collective-permute-start.28 = (bf16[64,2048]{1,0:T(8,128)(2,1)S(1)}, bf16[64,2048]{1,0:T(8,128)(2,1)S(1)}, u32[]{:S(2)}, u32[]{:S(2)}) collective-permute-start(bf16[64,2048]{1,0:T(8,128)(2,1)S(1)} %convolution_convert_fusion), channel_id=1, source_target_pairs={{0,4},{1,5},{2,6},{3,7},{4,0},{5,1},{6,2},{7,3},{8,12},{9,13},{10,... | collective-permute-start | bytes 786440 | tf_op jit(solution)/shard_map/ppermute | solution.py:25
  116.5 20.4 %collective-permute-start.26 = (bf16[64,2048]{1,0:T(8,128)(2,1)S(1)}, bf16[64,2048]{1,0:T(8,128)(2,1)S(1)}, u32[]{:S(2)}, u32[]{:S(2)}) collective-permute-start(bf16[64,2048]{1,0:T(8,128)(2,1)S(1)} %convolution_convert_fusion.1), channel_id=1, source_target_pairs={{0,8},{1,9},{2,10},{3,11},{4,12},{5,13},{6,14},{7,15},{8,0},{9,1},... | collective-permute-start | bytes 786440 | tf_op jit(solution)/shard_map/ppermute | solution.py:25
  117.4 19.4 %collective-permute-start.24 = (bf16[64,2048]{1,0:T(8,128)(2,1)S(1)}, bf16[64,2048]{1,0:T(8,128)(2,1)S(1)}, u32[]{:S(2)}, u32[]{:S(2)}) collective-permute-start(bf16[64,2048]{1,0:T(8,128)(2,1)S(1)} %convolution_convert_fusion.2), channel_id=1, source_target_pairs={{0,12},{1,13},{2,14},{3,15},{4,8},{5,9},{6,10},{7,11},{8,4},{9,5},... | collective-permute-start | bytes 786440 | tf_op jit(solution)/shard_map/ppermute | solution.py:25
  137.1 9.0 %collective-permute-start.30 = (bf16[64,2048]{1,0:T(8,128)(2,1)S(1)}, bf16[64,2048]{1,0:T(8,128)(2,1)S(1)}, u32[]{:S(2)}, u32[]{:S(2)}) collective-permute-start(bf16[64,2048]{1,0:T(8,128)(2,1)S(1)} %fusion.16), channel_id=1, source_target_pairs={{0,4},{1,5},{2,6},{3,7},{4,0},{5,1},{6,2},{7,3},{8,12},{9,13},{10,... | collective-permute-start | bytes 786440 | tf_op jit(solution)/shard_map/ppermute | solution.py:25
  140.9 5.2 %collective-permute-start.31 = (bf16[64,2048]{1,0:T(8,128)(2,1)S(1)}, bf16[64,2048]{1,0:T(8,128)(2,1)S(1)}, u32[]{:S(2)}, u32[]{:S(2)}) collective-permute-start(bf16[64,2048]{1,0:T(8,128)(2,1)S(1)} %fusion.16), channel_id=1, source_target_pairs={{4,8},{5,9},{6,10},{7,11},{8,4},{9,5},{10,6},{11,7},{20,24},{21,25... | collective-permute-start | bytes 786440 | tf_op jit(solution)/shard_map/ppermute | solution.py:25
  141.6 6.4 %collective-permute-start.29 = (bf16[64,2048]{1,0:T(8,128)(2,1)S(1)}, bf16[64,2048]{1,0:T(8,128)(2,1)S(1)}, u32[]{:S(2)}, u32[]{:S(2)}) collective-permute-start(bf16[64,2048]{1,0:T(8,128)(2,1)S(1)} %fusion.16), channel_id=1, source_target_pairs={{0,2},{1,3},{2,0},{3,1},{4,6},{5,7},{6,4},{7,5},{8,10},{9,11},{10,... | collective-permute-start | bytes 786440 | tf_op jit(solution)/shard_map/ppermute | solution.py:31
  141.7 12.4 %collective-permute-start.38 = (bf16[64,2048]{1,0:T(8,128)(2,1)S(1)}, bf16[64,2048]{1,0:T(8,128)(2,1)S(1)}, u32[]{:S(2)}, u32[]{:S(2)}) collective-permute-start(bf16[64,2048]{1,0:T(8,128)(2,1)S(1)} %fusion.16), channel_id=1, source_target_pairs={{0,12},{1,13},{2,14},{3,15},{12,0},{13,1},{14,2},{15,3},{16,28},{1... | collective-permute-start | bytes 786440 | tf_op jit(solution)/shard_map/ppermute | solution.py:25
  146.1 24.2 %collective-permute-start.36 = (bf16[512,2048]{1,0:T(8,128)(2,1)S(1)}, bf16[512,2048]{1,0:T(8,128)(2,1)S(1)}, u32[]{:S(2)}, u32[]{:S(2)}) collective-permute-start(bf16[512,2048]{1,0:T(8,128)(2,1)S(1)} %bitcast.68), channel_id=1, source_target_pairs={{0,1},{1,0},{2,3},{3,2},{4,5},{5,4},{6,7},{7,6},{8,9},{9,8},{10,11... | collective-permute-start | bytes 6291464 | tf_op jit(solution)/shard_map/ppermute | solution.py:31
  148.1 18.7 %collective-permute-start.32 = (bf16[64,2048]{1,0:T(8,128)(2,1)S(1)}, bf16[64,2048]{1,0:T(8,128)(2,1)S(1)}, u32[]{:S(2)}, u32[]{:S(2)}) collective-permute-start(bf16[64,2048]{1,0:T(8,128)(2,1)S(1)} %collective-permute-done.30), channel_id=1, source_target_pairs={{0,2},{1,3},{2,0},{3,1},{4,6},{5,7},{6,4},{7,5},{8,10},{9,11},{10,... | collective-permute-start | bytes 786440 | tf_op jit(solution)/shard_map/ppermute | solution.py:31
  148.2 7.2 %collective-permute-start.33 = (bf16[64,2048]{1,0:T(8,128)(2,1)S(1)}, bf16[64,2048]{1,0:T(8,128)(2,1)S(1)}, u32[]{:S(2)}, u32[]{:S(2)}) collective-permute-start(bf16[64,2048]{1,0:T(8,128)(2,1)S(1)} %collective-permute-done.30), channel_id=1, source_target_pairs={{4,8},{5,9},{6,10},{7,11},{8,4},{9,5},{10,6},{11,7},{20,24},{21,25... | collective-permute-start | bytes 786440 | tf_op jit(solution)/shard_map/ppermute | solution.py:25
  154.1 10.5 %collective-permute-start.34 = (bf16[64,2048]{1,0:T(8,128)(2,1)S(1)}, bf16[64,2048]{1,0:T(8,128)(2,1)S(1)}, u32[]{:S(2)}, u32[]{:S(2)}) collective-permute-start(bf16[64,2048]{1,0:T(8,128)(2,1)S(1)} %collective-permute-done.31), channel_id=1, source_target_pairs={{4,0},{5,1},{6,2},{7,3},{8,12},{9,13},{10,14},{11,15},{20,16},{21,... | collective-permute-start | bytes 786440 | tf_op jit(solution)/shard_map/ppermute | solution.py:25
  155.5 11.4 %collective-permute-start.39 = (bf16[64,2048]{1,0:T(8,128)(2,1)S(1)}, bf16[64,2048]{1,0:T(8,128)(2,1)S(1)}, u32[]{:S(2)}, u32[]{:S(2)}) collective-permute-start(bf16[64,2048]{1,0:T(8,128)(2,1)S(1)} %broadcast_select_fusion.2), channel_id=1, source_target_pairs={{0,2},{1,3},{2,0},{3,1},{4,6},{5,7},{6,4},{7,5},{8,10},{9,11},{10,... | collective-permute-start | bytes 786440 | tf_op jit(solution)/shard_map/ppermute | solution.py:31
  164.7 9.2 %collective-permute-start.37 = (bf16[64,2048]{1,0:T(8,128)(2,1)S(1)}, bf16[64,2048]{1,0:T(8,128)(2,1)S(1)}, u32[]{:S(2)}, u32[]{:S(2)}) collective-permute-start(bf16[64,2048]{1,0:T(8,128)(2,1)S(1)} %broadcast_select_fusion.3), channel_id=1, source_target_pairs={{0,2},{1,3},{2,0},{3,1},{4,6},{5,7},{6,4},{7,5},{8,10},{9,11},{10,... | collective-permute-start | bytes 786440 | tf_op jit(solution)/shard_map/ppermute | solution.py:31
  173.7 8.9 %collective-permute-start.42 = (bf16[64,2048]{1,0:T(8,128)(2,1)S(1)}, bf16[64,2048]{1,0:T(8,128)(2,1)S(1)}, u32[]{:S(2)}, u32[]{:S(2)}) collective-permute-start(bf16[64,2048]{1,0:T(8,128)(2,1)S(1)} %slice.376), channel_id=1, source_target_pairs={{0,2},{1,3},{2,0},{3,1},{4,6},{5,7},{6,4},{7,5},{8,10},{9,11},{10,... | collective-permute-start | bytes 786440 | tf_op jit(solution)/shard_map/ppermute | solution.py:31
  182.6 6.4 %collective-permute-start.45 = (bf16[64,2048]{1,0:T(8,128)(2,1)S(1)}, bf16[64,2048]{1,0:T(8,128)(2,1)S(1)}, u32[]{:S(2)}, u32[]{:S(2)}) collective-permute-start(bf16[64,2048]{1,0:T(8,128)(2,1)S(1)} %get-tuple-element.38), channel_id=1, source_target_pairs={{0,2},{1,3},{2,0},{3,1},{4,6},{5,7},{6,4},{7,5},{8,10},{9,11},{10,... | collective-permute-start | bytes 786440 | tf_op jit(solution)/shard_map/ppermute | solution.py:31
  182.6 14.3 %collective-permute-start.40 = (bf16[64,2048]{1,0:T(8,128)(2,1)S(1)}, bf16[64,2048]{1,0:T(8,128)(2,1)S(1)}, u32[]{:S(2)}, u32[]{:S(2)}) collective-permute-start(bf16[64,2048]{1,0:T(8,128)(2,1)S(1)} %slice.374), channel_id=1, source_target_pairs={{0,2},{1,3},{2,0},{3,1},{4,6},{5,7},{6,4},{7,5},{8,10},{9,11},{10,... | collective-permute-start | bytes 786440 | tf_op jit(solution)/shard_map/ppermute | solution.py:31
  184.6 17.9 %collective-permute-start.43 = (bf16[64,2048]{1,0:T(8,128)(2,1)S(1)}, bf16[64,2048]{1,0:T(8,128)(2,1)S(1)}, u32[]{:S(2)}, u32[]{:S(2)}) collective-permute-start(bf16[64,2048]{1,0:T(8,128)(2,1)S(1)} %add_convert_fusion.3), channel_id=1, source_target_pairs={{0,12},{1,13},{2,14},{3,15},{4,8},{5,9},{6,10},{7,11},{8,4},{9,5},... | collective-permute-start | bytes 786440 | tf_op jit(solution)/shard_map/ppermute | solution.py:25
  189.0 13.7 %collective-permute-start.46 = (bf16[64,2048]{1,0:T(8,128)(2,1)S(1)}, bf16[64,2048]{1,0:T(8,128)(2,1)S(1)}, u32[]{:S(2)}, u32[]{:S(2)}) collective-permute-start(bf16[64,2048]{1,0:T(8,128)(2,1)S(1)} %add_convert_fusion.1), channel_id=1, source_target_pairs={{0,4},{1,5},{2,6},{3,7},{4,0},{5,1},{6,2},{7,3},{8,12},{9,13},{10,... | collective-permute-start | bytes 786440 | tf_op jit(solution)/shard_map/ppermute | solution.py:25
  197.0 11.3 %collective-permute-start.44 = (bf16[64,2048]{1,0:T(8,128)(2,1)S(1)}, bf16[64,2048]{1,0:T(8,128)(2,1)S(1)}, u32[]{:S(2)}, u32[]{:S(2)}) collective-permute-start(bf16[64,2048]{1,0:T(8,128)(2,1)S(1)} %add_convert_fusion.2), channel_id=1, source_target_pairs={{0,8},{1,9},{2,10},{3,11},{4,12},{5,13},{6,14},{7,15},{8,0},{9,1},... | collective-permute-start | bytes 786440 | tf_op jit(solution)/shard_map/ppermute | solution.py:25
  201.1 7.2 %collective-permute-start.41 = (bf16[64,2048]{1,0:T(8,128)(2,1)S(1)}, bf16[64,2048]{1,0:T(8,128)(2,1)S(1)}, u32[]{:S(2)}, u32[]{:S(2)}) collective-permute-start(bf16[64,2048]{1,0:T(8,128)(2,1)S(1)} %get-tuple-element.37), channel_id=1, source_target_pairs={{0,2},{1,3},{2,0},{3,1},{4,6},{5,7},{6,4},{7,5},{8,10},{9,11},{10,... | collective-permute-start | bytes 786440 | tf_op jit(solution)/shard_map/ppermute | solution.py:31
  (8 other events, 111.2 us)

commit v12 on v11

--- a/solution.py
+++ b/solution.py
@@ -42,8 +42,8 @@
     return sum(t.astype(jnp.float32) for t in terms).astype(jnp.bfloat16)
 
 
-def within_plane(ring, chunk):
-    for bit in reversed(ring.bits[1:-1]):
+def within_plane(ring, chunk, bits):
+    for bit in reversed(bits):
         rows = chunk.shape[0] // 2
         chunk = add(chunk[:rows], ring.across(chunk[rows:], bit))
     return chunk
@@ -75,7 +75,7 @@
     return (widened * inverse * gain).astype(jnp.bfloat16)
 
 
-def two_experts(rows, gates, weights):
+def experts(rows, gates, weights):
     total = 0.0
     for gate, (gate_up, down) in zip(gates, weights):
         width = down.shape[0]
@@ -85,36 +85,44 @@
     return total.astype(jnp.bfloat16)
 
 
-def routed(ring, rows, work):
+def routed(ring, rows, work, paired):
     top = ring.bits[0]
-    columns = {0: rows, 1: ring.between(rows, 1)}
-    crossed = {0: ring.across(rows, top)}
-    middle = ring.send(rows, [(1, 2), (2, 1)])
-    ends = ring.send(rows, [(0, 3), (3, 0)])
-    near = ring.send(middle, [(1, 0), (2, 3)])
-    far = ring.send(columns[1], [(1, 2), (2, 1)])
-    columns[3] = jnp.where(ring.inside, middle, ends)
-    columns[2] = jnp.where(ring.inside, far, near)
-    crossed[1] = ring.across(after(columns[1], middle, crossed[0]), top)
-    crossed[3] = ring.across(columns[3], top)
-    crossed[2] = ring.across(columns[2], top)
-
-    def chunk(*slots):
-        parts = []
-        for slot in slots:
-            part = jnp.concatenate([columns[slot], crossed[slot]], axis=0)
-            for bit in ring.bits[1:-1]:
-                part = jnp.concatenate([part, ring.across(part, bit)], axis=0)
-            parts.append(part)
-        return jnp.concatenate(parts, axis=0)
-
-    both = work((0, 1), after(chunk(0, 1), columns[2]))
-    third = work((3,), after(chunk(3), both))
-    halves = {3: within_plane(ring, third)}
-    last = work((2,), after(chunk(2), halves[3]))
-    count = both.shape[0] // 2
-    for slot, done in ((2, last), (1, both[count:]), (0, both[:count])):
-        halves[slot] = within_plane(ring, done)
+    below = ring.bits[1:-1] if paired else ring.bits[1:]
+    columns = {0: rows}
+    for slot in (1, 3, 2):
+        columns[slot] = ring.between(rows, slot)
+    crossed = {slot: ring.across(columns[slot], top) for slot in (0, 1)}
+    crossed[3] = ring.across(after(columns[3], crossed[1]), top)
+    crossed[2] = ring.across(after(columns[2], crossed[3]), top)
+
+    def chunk(slot, *ties):
+        part = after(jnp.concatenate([columns[slot], crossed[slot]], axis=0), *ties)
+        for bit in below:
+            part = jnp.concatenate([part, ring.across(part, bit)], axis=0)
+        return part
+
+    def halve(done):
+        return within_plane(ring, done, below)
+
+    halves = {}
+    if paired:
+        both = work((0, 1), after(jnp.concatenate([chunk(0), chunk(1)], axis=0), crossed[3]))
+        third = work((3,), after(chunk(3), both))
+        halves[3] = halve(third)
+        last = work((2,), after(chunk(2), halves[3]))
+        count = both.shape[0] // 2
+        done = {0: both[:count], 1: both[count:]}
+    else:
+        done = {}
+        ties = [crossed[3]]
+        for slot in (0, 1, 3):
+            done[slot] = work((slot,), after(chunk(slot), *ties))
+            ties = [done[slot]]
+        halves[3] = halve(done[3])
+        last = work((2,), after(chunk(2, *ties), halves[3]))
+    halves[2] = halve(last)
+    for slot in (1, 0):
+        halves[slot] = halve(done[slot])
 
     own = rows.shape[0]
     back = {}
@@ -181,31 +189,29 @@
     lanes = gate_lanes([(first_routes, first_gates), (second_routes, second_gates)])
     top = first_routes.shape[1]
     people = (ring.me, ring.me ^ 1)
-    second_columns = {}
-
-    def pair(gate_up, down, *ties):
-        mine = (gate_up[0], down[0])
-        return mine, tuple(ring.across(after(w, *ties), ring.bits[-1]) for w in mine)
-
-    first_pair = pair(first_gate_up, first_down)
+    second_lanes = {}
 
     def first_work(slots, chunk):
         lanes = chunk[:, width:]
-        second_columns[slots] = [gate_column(lanes, who, 1, top) for who in people]
-        return two_experts(chunk[:, :width], [gate_column(lanes, who, 0, top) for who in people], first_pair)
+        second_lanes[slots[0]] = lanes[: chunk.shape[0] // 2]
+        return experts(
+            chunk[:, :width], [gate_column(lanes, ring.me, 0, top)], [(first_gate_up[0], first_down[0])]
+        )
 
     def second_work(slots, chunk):
-        return two_experts(chunk, second_columns[slots], second_pair)
-
-    first, steps = routed(ring, jnp.concatenate([hidden_rows, lanes], axis=1), first_work)
-    second_pair = pair(second_gate_up, second_down, steps[1])
+        lanes = jnp.concatenate([second_lanes[slot] for slot in slots], axis=0)
+        return experts(chunk, [gate_column(lanes, who, 1, top) for who in people], second_pair)
+
+    first, steps = routed(ring, jnp.concatenate([hidden_rows, lanes], axis=1), first_work, False)
+    mine = (second_gate_up[0], second_down[0])
+    second_pair = (mine, tuple(ring.across(after(w, steps[1]), ring.bits[-1]) for w in mine))
     ties = [([], [steps[0]]), ([steps[1]], [steps[2]])]
     weight = plane_weight(ring, merge_weight, other_half(ring, merge_weight, lax.axis_size("groups"), ties))
     after_first = (hidden_rows.astype(jnp.float32) + first).astype(jnp.bfloat16)
     merged_in = jnp.concatenate([normed(after_first, hidden_gain), normed(token_embed, embed_gain)], axis=1)
     merged = merge(ring, merged_in, weight)
     after_merge = (after_first.astype(jnp.float32) + jax.nn.silu(merged)).astype(jnp.bfloat16)
-    second, _ = routed(ring, after_merge, second_work)
+    second, _ = routed(ring, after(after_merge, *second_pair[1]), second_work, True)
     return (after_merge.astype(jnp.float32) + second).astype(jnp.bfloat16)
 
 

time: 210 us -> 202 us (0.962)
  waiting for transfers between devices: 93.3 us -> 82.6 us
  matrix products: 28.5 us -> 20.9 us
  local copies, waits for them, and re-layouts: 2.16 us -> 8.16 us
  other arithmetic: 11.8 us -> 16.5 us
    ppermute x22 -> x18, waiting for transfers between devices: 66 us -> 50.8 us  [send(): return lax.ppermute(values, 'inner', perm)]
    dot_general x24 -> x20, matrix products: 25.2 us -> 17.6 us  [the longest x10 10.6 us: experts(): projected = jnp.dot(rows, gate_up, preferred_element_type=jnp.float32)]
    unnamed x18 -> x38, local copies, waits for them, and re-layouts: 0.04 us -> 4.37 us
    ppermute x23 -> x29, starting transfers between devices: 18 us -> 22 us  [across(): lax.ppermute(values, 'inner', [(d, d ^ bit) for d in range(self.size)])]
    ppermute x22 -> x18, starting transfers between devices: 51.5 us -> 47.7 us  [send(): return lax.ppermute(values, 'inner', perm)]
    concatenate x6 -> x13, other arithmetic: 0.34 us -> 4.02 us  [the longest x8 3.63 us: chunk(): part = after(jnp.concatenate([columns[slot], crossed[slot]], axis=0), *ties)]
    ppermute x2, waiting for transfers between devices: 0.32 us -> 2.58 us  [other_half(): there = lax.ppermute(here, 'groups', [(g, g ^ 1) for g in range(groups)])]
    ppermute x23 -> x29, waiting for transfers between devices: 27 us -> 29.2 us  [across(): lax.ppermute(values, 'inner', [(d, d ^ bit) for d in range(self.size)])]
  transfers between devices with their start and end apart: 47 -> 49, of which waited for: 21 -> 20; matrix products, arithmetic and copies ran while one was open for 18% -> 18% of each run, Pallas kernels for 0% -> 0%
where the time goes in v12:
time: 202 us
  waiting for transfers between devices  82.6 us (41%)
  starting transfers between devices  72.7 us (36%)
  matrix products  20.9 us (10%)
  other arithmetic  16.5 us (8%)
  local copies, waits for them, and re-layouts  8.16 us (4%)
    ppermute x18, waiting for transfers between devices, send(): return lax.ppermute(values, 'inner', perm)  50.8 us
    ppermute x18, starting transfers between devices, send(): return lax.ppermute(values, 'inner', perm)  47.7 us
    ppermute x29, waiting for transfers between devices, across(): lax.ppermute(values, 'inner', [(d, d ^ bit) for d in range(self.size)])  29.2 us
    ppermute x29, starting transfers between devices, across(): lax.ppermute(values, 'inner', [(d, d ^ bit) for d in range(self.size)])  22 us
    dot_general x10, matrix products, experts(): projected = jnp.dot(rows, gate_up, preferred_element_type=jnp.float32)  10.6 us
    dot_general x10, matrix products, experts(): jnp.dot(hidden.astype(jnp.bfloat16), down, preferred_element_type=jnp.flo...  6.98 us
    unnamed x38, local copies, waits for them, and re-layouts  4.37 us
  transfers between devices with their start and end apart: 49, of which 20 were waited for; matrix products, arithmetic and copies ran while one was open for 18% of the time, Pallas kernels for 0%

profile of v12, /device:TPU:0, one launch (start us, length us, event | category | flops | bytes accessed | tf_op | source)
XLA Modules:
  0.0 201.9 jit_solution(792671093452689216)
XLA Ops:
  3.4 3.1 %collective-permute-start.3 = (bf16[64,2176]{1,0:T(8,128)(2,1)S(1)}, bf16[64,2176]{1,0:T(8,128)(2,1)S(1)}, u32[]{:S(2)}, u32[]{:S(2)}) collective-permute-start(bf16[64,2176]{1,0:T(8,128)(2,1)S(1)} %pad_maximum_fusion.14), channel_id=1, source_target_pairs={{0,4},{1,5},{2,6},{3,7},{4,0},{5,1},{6,2},{7,3},{8,12},{9,13},{10,... | collective-permute-start | bytes 835592 | tf_op jit(solution)/shard_map/ppermute | solution.py:25
  6.5 2.5 %collective-permute-start.2 = (bf16[64,2176]{1,0:T(8,128)(2,1)S(1)}, bf16[64,2176]{1,0:T(8,128)(2,1)S(1)}, u32[]{:S(2)}, u32[]{:S(2)}) collective-permute-start(bf16[64,2176]{1,0:T(8,128)(2,1)S(1)} %pad_maximum_fusion.14), channel_id=1, source_target_pairs={{0,12},{1,13},{2,14},{3,15},{4,8},{5,9},{6,10},{7,11},{8,4},{9,5},... | collective-permute-start | bytes 835592 | tf_op jit(solution)/shard_map/ppermute | solution.py:25
  9.1 1.5 collective-permute-start
  10.6 1.9 constant_dynamic-slice_fusion.1
  14.2 1.6 collective-permute-start.4
  15.8 2.9 %collective-permute-done = bf16[64,2176]{1,0:T(8,128)(2,1)S(1)} collective-permute-done((bf16[64,2176]{1,0:T(8,128)(2,1)S(1)}, bf16[64,2176]{1,0:T(8,128)(2,1)S(1)}, u32[]{:S(2)}, u32[]{:S(2)}) %collective-permute-start) | collective-permute-done | bytes 278560 | tf_op jit(solution)/shard_map/ppermute | solution.py:31
  18.8 3.7 %collective-permute-done.2 = bf16[64,2176]{1,0:T(8,128)(2,1)S(1)} collective-permute-done((bf16[64,2176]{1,0:T(8,128)(2,1)S(1)}, bf16[64,2176]{1,0:T(8,128)(2,1)S(1)}, u32[]{:S(2)}, u32[]{:S(2)}) %collective-permute-start.2) | collective-permute-done | bytes 278560 | tf_op jit(solution)/shard_map/ppermute | solution.py:25
  22.5 6.0 %collective-permute-done.4 = bf16[64,2176]{1,0:T(8,128)(2,1)S(1)} collective-permute-done((bf16[64,2176]{1,0:T(8,128)(2,1)S(1)}, bf16[64,2176]{1,0:T(8,128)(2,1)S(1)}, u32[]{:S(2)}, u32[]{:S(2)}) %collective-permute-start.4) | collective-permute-done | bytes 278560 | tf_op jit(solution)/shard_map/ppermute | solution.py:31
  28.5 1.5 collective-permute-start.5
  30.1 1.6 collective-permute-start.23
  31.6 3.8 %collective-permute-done.5 = bf16[64,2176]{1,0:T(8,128)(2,1)S(1)} collective-permute-done((bf16[64,2176]{1,0:T(8,128)(2,1)S(1)}, bf16[64,2176]{1,0:T(8,128)(2,1)S(1)}, u32[]{:S(2)}, u32[]{:S(2)}) %collective-permute-start.5) | collective-permute-done | bytes 278560 | tf_op jit(solution)/shard_map/ppermute | solution.py:31
  35.5 1.6 collective-permute-start.8
  37.2 1.3 fusion.6
  39.7 1.3 fusion.4
  45.0 1.3 pad_maximum_fusion.7
  49.4 1.3 fusion
  52.3 1.6 collective-permute-start.16
  53.8 3.4 %collective-permute-done.13 = bf16[128,2048]{1,0:T(8,128)(2,1)S(1)} collective-permute-done((bf16[128,2048]{1,0:T(8,128)(2,1)S(1)}, bf16[128,2048]{1,0:T(8,128)(2,1)S(1)}, u32[]{:S(2)}, u32[]{:S(2)}) %collective-permute-start.13) | collective-permute-done | bytes 524320 | tf_op jit(solution)/shard_map/ppermute | solution.py:31
  57.4 1.6 collective-permute-start.14
  59.0 3.9 %collective-permute-done.16 = bf16[64,2048]{1,0:T(8,128)(2,1)S(1)} collective-permute-done((bf16[64,2048]{1,0:T(8,128)(2,1)S(1)}, bf16[64,2048]{1,0:T(8,128)(2,1)S(1)}, u32[]{:S(2)}, u32[]{:S(2)}) %collective-permute-start.16) | collective-permute-done | bytes 262176 | tf_op jit(solution)/shard_map/ppermute | solution.py:31
  63.0 2.4 %collective-permute-start.17 = (bf16[64,2048]{1,0:T(8,128)(2,1)S(1)}, bf16[64,2048]{1,0:T(8,128)(2,1)S(1)}, u32[]{:S(2)}, u32[]{:S(2)}) collective-permute-start(bf16[64,2048]{1,0:T(8,128)(2,1)S(1)} %add_convert_fusion.12), channel_id=1, source_target_pairs={{0,12},{1,13},{2,14},{3,15},{4,8},{5,9},{6,10},{7,11},{8,4},{9,5},... | collective-permute-start | bytes 786440 | tf_op jit(solution)/shard_map/ppermute | solution.py:25
  65.5 3.0 %collective-permute-done.14 = bf16[64,2048]{1,0:T(8,128)(2,1)S(1)} collective-permute-done((bf16[64,2048]{1,0:T(8,128)(2,1)S(1)}, bf16[64,2048]{1,0:T(8,128)(2,1)S(1)}, u32[]{:S(2)}, u32[]{:S(2)}) %collective-permute-start.14) | collective-permute-done | bytes 262176 | tf_op jit(solution)/shard_map/ppermute | solution.py:31
  68.5 1.5 collective-permute-start.25
  70.1 2.3 %collective-permute-start.18 = (bf16[64,2048]{1,0:T(8,128)(2,1)S(1)}, bf16[64,2048]{1,0:T(8,128)(2,1)S(1)}, u32[]{:S(2)}, u32[]{:S(2)}) collective-permute-start(bf16[64,2048]{1,0:T(8,128)(2,1)S(1)} %add_convert_fusion.11), channel_id=1, source_target_pairs={{0,8},{1,9},{2,10},{3,11},{4,12},{5,13},{6,14},{7,15},{8,0},{9,1},... | collective-permute-start | bytes 786440 | tf_op jit(solution)/shard_map/ppermute | solution.py:25
  72.4 2.6 %collective-permute-done.25 = bf16[64,2048]{1,0:T(8,128)(2,1)S(1)} collective-permute-done((bf16[64,2048]{1,0:T(8,128)(2,1)S(1)}, bf16[64,2048]{1,0:T(8,128)(2,1)S(1)}, u32[]{:S(2)}, u32[]{:S(2)}) %collective-permute-start.25) | collective-permute-done | bytes 262176 | tf_op jit(solution)/shard_map/ppermute | solution.py:147
  76.9 6.4 %collective-permute-start.21 = (bf16[64,2048]{1,0:T(8,128)(2,1)S(1)}, bf16[64,2048]{1,0:T(8,128)(2,1)S(1)}, u32[]{:S(2)}, u32[]{:S(2)}) collective-permute-start(bf16[64,2048]{1,0:T(8,128)(2,1)S(1)} %add_convert_fusion.10), channel_id=1, source_target_pairs={{0,4},{1,5},{2,6},{3,7},{4,0},{5,1},{6,2},{7,3},{8,12},{9,13},{10,... | collective-permute-start | bytes 786440 | tf_op jit(solution)/shard_map/ppermute | solution.py:25
  83.4 3.7 %collective-permute-done.18 = bf16[64,2048]{1,0:T(8,128)(2,1)S(1)} collective-permute-done((bf16[64,2048]{1,0:T(8,128)(2,1)S(1)}, bf16[64,2048]{1,0:T(8,128)(2,1)S(1)}, u32[]{:S(2)}, u32[]{:S(2)}) %collective-permute-start.18) | collective-permute-done | bytes 262176 | tf_op jit(solution)/shard_map/ppermute | solution.py:25
  87.1 5.0 %collective-permute-done.21 = bf16[64,2048]{1,0:T(8,128)(2,1)S(1)} collective-permute-done((bf16[64,2048]{1,0:T(8,128)(2,1)S(1)}, bf16[64,2048]{1,0:T(8,128)(2,1)S(1)}, u32[]{:S(2)}, u32[]{:S(2)}) %collective-permute-start.21) | collective-permute-done | bytes 262176 | tf_op jit(solution)/shard_map/ppermute | solution.py:25
  92.9 2.6 %collective-permute-start.27 = (bf16[64,1024]{1,0:T(8,128)(2,1)S(1)}, bf16[64,1024]{1,0:T(8,128)(2,1)S(1)}, u32[]{:S(2)}, u32[]{:S(2)}) collective-permute-start(bf16[64,1024]{1,0:T(8,128)(2,1)S(1)} %get-tuple-element.63), channel_id=1, source_target_pairs={{0,12},{1,13},{2,14},{3,15},{4,8},{5,9},{6,10},{7,11},{8,4},{9,5},... | collective-permute-start | bytes 393224 | tf_op jit(solution)/shard_map/ppermute | solution.py:25
  95.9 1.9 collective-permute-start.31
  98.6 2.6 %collective-permute-done.27 = bf16[64,1024]{1,0:T(8,128)(2,1)S(1)} collective-permute-done((bf16[64,1024]{1,0:T(8,128)(2,1)S(1)}, bf16[64,1024]{1,0:T(8,128)(2,1)S(1)}, u32[]{:S(2)}, u32[]{:S(2)}) %collective-permute-start.27) | collective-permute-done | bytes 131104 | tf_op jit(solution)/shard_map/ppermute | solution.py:25
  102.0 2.7 %collective-permute-start.28 = (bf16[64,2048]{1,0:T(8,128)(2,1)S(1)}, bf16[64,2048]{1,0:T(8,128)(2,1)S(1)}, u32[]{:S(2)}, u32[]{:S(2)}) collective-permute-start(bf16[64,2048]{1,0:T(8,128)(2,1)S(1)} %convolution_convert_fusion.6), channel_id=1, source_target_pairs={{0,12},{1,13},{2,14},{3,15},{4,8},{5,9},{6,10},{7,11},{8,4},{9,5},... | collective-permute-start | bytes 786440 | tf_op jit(solution)/shard_map/ppermute | solution.py:25
  104.7 6.2 %collective-permute-done.29 = bf16[64,1024]{1,0:T(8,128)(2,1)S(1)} collective-permute-done((bf16[64,1024]{1,0:T(8,128)(2,1)S(1)}, bf16[64,1024]{1,0:T(8,128)(2,1)S(1)}, u32[]{:S(2)}, u32[]{:S(2)}) %collective-permute-start.29) | collective-permute-done | bytes 131104 | tf_op jit(solution)/shard_map/ppermute | solution.py:25
  112.7 3.3 %collective-permute-start.32 = (bf16[64,2048]{1,0:T(8,128)(2,1)S(1)}, bf16[64,2048]{1,0:T(8,128)(2,1)S(1)}, u32[]{:S(2)}, u32[]{:S(2)}) collective-permute-start(bf16[64,2048]{1,0:T(8,128)(2,1)S(1)} %convolution_convert_fusion.4), channel_id=1, source_target_pairs={{0,4},{1,5},{2,6},{3,7},{4,0},{5,1},{6,2},{7,3},{8,12},{9,13},{10,... | collective-permute-start | bytes 786440 | tf_op jit(solution)/shard_map/ppermute | solution.py:25
  116.8 10.9 %collective-permute-done.30 = bf16[64,2048]{1,0:T(8,128)(2,1)S(1)} collective-permute-done((bf16[64,2048]{1,0:T(8,128)(2,1)S(1)}, bf16[64,2048]{1,0:T(8,128)(2,1)S(1)}, u32[]{:S(2)}, u32[]{:S(2)}) %collective-permute-start.30) | collective-permute-done | bytes 262176 | tf_op jit(solution)/shard_map/ppermute | solution.py:25
  128.0 2.0 copy-done.4
  133.6 2.7 %collective-permute-start.38 = (bf16[64,2048]{1,0:T(8,128)(2,1)S(1)}, bf16[64,2048]{1,0:T(8,128)(2,1)S(1)}, u32[]{:S(2)}, u32[]{:S(2)}) collective-permute-start(bf16[64,2048]{1,0:T(8,128)(2,1)S(1)} %fusion.25), channel_id=1, source_target_pairs={{0,12},{1,13},{2,14},{3,15},{4,8},{5,9},{6,10},{7,11},{8,4},{9,5},... | collective-permute-start | bytes 786440 | tf_op jit(solution)/shard_map/ppermute | solution.py:25
  136.3 2.1 %collective-permute-done.36 = bf16[64,2048]{1,0:T(8,128)(2,1)} collective-permute-done((bf16[64,2048]{1,0:T(8,128)(2,1)S(1)}, bf16[64,2048]{1,0:T(8,128)(2,1)}, u32[]{:S(2)}, u32[]{:S(2)}) %collective-permute-start.36) | collective-permute-done | bytes 262176 | tf_op jit(solution)/shard_map/ppermute | solution.py:25
  140.6 5.9 %collective-permute-start.40 = (bf16[64,2048]{1,0:T(8,128)(2,1)S(1)}, bf16[64,2048]{1,0:T(8,128)(2,1)S(1)}, u32[]{:S(2)}, u32[]{:S(2)}) collective-permute-start(bf16[64,2048]{1,0:T(8,128)(2,1)S(1)} %fusion.25), channel_id=1, source_target_pairs={{0,8},{1,9},{2,10},{3,11},{4,12},{5,13},{6,14},{7,15},{8,0},{9,1},... | collective-permute-start | bytes 786440 | tf_op jit(solution)/shard_map/ppermute | solution.py:25
  149.8 9.3 %collective-permute-done.40 = bf16[64,2048]{1,0:T(8,128)(2,1)S(1)} collective-permute-done((bf16[64,2048]{1,0:T(8,128)(2,1)S(1)}, bf16[64,2048]{1,0:T(8,128)(2,1)S(1)}, u32[]{:S(2)}, u32[]{:S(2)}) %collective-permute-start.40) | collective-permute-done | bytes 262176 | tf_op jit(solution)/shard_map/ppermute | solution.py:25
  162.4 1.4 copy-done.5
  173.6 4.0 %collective-permute-done.44 = bf16[64,2048]{1,0:T(8,128)(2,1)S(1)} collective-permute-done((bf16[64,2048]{1,0:T(8,128)(2,1)S(1)}, bf16[64,2048]{1,0:T(8,128)(2,1)S(1)}, u32[]{:S(2)}, u32[]{:S(2)}) %collective-permute-start.44) | collective-permute-done | bytes 262176 | tf_op jit(solution)/shard_map/ppermute | solution.py:31
  177.7 2.7 %collective-permute-start.45 = (bf16[64,2048]{1,0:T(8,128)(2,1)S(1)}, bf16[64,2048]{1,0:T(8,128)(2,1)S(1)}, u32[]{:S(2)}, u32[]{:S(2)}) collective-permute-start(bf16[64,2048]{1,0:T(8,128)(2,1)S(1)} %add_convert_fusion.7), channel_id=1, source_target_pairs={{0,12},{1,13},{2,14},{3,15},{4,8},{5,9},{6,10},{7,11},{8,4},{9,5},... | collective-permute-start | bytes 786440 | tf_op jit(solution)/shard_map/ppermute | solution.py:25
  181.3 1.9 collective-permute-done.42
  183.3 3.1 %collective-permute-start.46 = (bf16[64,2048]{1,0:T(8,128)(2,1)S(1)}, bf16[64,2048]{1,0:T(8,128)(2,1)S(1)}, u32[]{:S(2)}, u32[]{:S(2)}) collective-permute-start(bf16[64,2048]{1,0:T(8,128)(2,1)S(1)} %add_convert_fusion.6), channel_id=1, source_target_pairs={{0,8},{1,9},{2,10},{3,11},{4,12},{5,13},{6,14},{7,15},{8,0},{9,1},... | collective-permute-start | bytes 786440 | tf_op jit(solution)/shard_map/ppermute | solution.py:25
  186.8 6.0 %collective-permute-start.48 = (bf16[64,2048]{1,0:T(8,128)(2,1)S(1)}, bf16[64,2048]{1,0:T(8,128)(2,1)S(1)}, u32[]{:S(2)}, u32[]{:S(2)}) collective-permute-start(bf16[64,2048]{1,0:T(8,128)(2,1)S(1)} %add_convert_fusion.5), channel_id=1, source_target_pairs={{0,4},{1,5},{2,6},{3,7},{4,0},{5,1},{6,2},{7,3},{8,12},{9,13},{10,... | collective-permute-start | bytes 786440 | tf_op jit(solution)/shard_map/ppermute | solution.py:25
  193.8 5.7 %collective-permute-done.46 = bf16[64,2048]{1,0:T(8,128)(2,1)S(1)} collective-permute-done((bf16[64,2048]{1,0:T(8,128)(2,1)S(1)}, bf16[64,2048]{1,0:T(8,128)(2,1)S(1)}, u32[]{:S(2)}, u32[]{:S(2)}) %collective-permute-start.46) | collective-permute-done | bytes 262176 | tf_op jit(solution)/shard_map/ppermute | solution.py:25
  199.5 1.5 collective-permute-done.48
  (177 shorter events, 48.4 us)
Async XLA Ops:
  3.4 10.8 %collective-permute-start.3 = (bf16[64,2176]{1,0:T(8,128)(2,1)S(1)}, bf16[64,2176]{1,0:T(8,128)(2,1)S(1)}, u32[]{:S(2)}, u32[]{:S(2)}) collective-permute-start(bf16[64,2176]{1,0:T(8,128)(2,1)S(1)} %pad_maximum_fusion.14), channel_id=1, source_target_pairs={{0,4},{1,5},{2,6},{3,7},{4,0},{5,1},{6,2},{7,3},{8,12},{9,13},{10,... | collective-permute-start | bytes 835592 | tf_op jit(solution)/shard_map/ppermute | solution.py:25
  6.5 16.1 %collective-permute-start.2 = (bf16[64,2176]{1,0:T(8,128)(2,1)S(1)}, bf16[64,2176]{1,0:T(8,128)(2,1)S(1)}, u32[]{:S(2)}, u32[]{:S(2)}) collective-permute-start(bf16[64,2176]{1,0:T(8,128)(2,1)S(1)} %pad_maximum_fusion.14), channel_id=1, source_target_pairs={{0,12},{1,13},{2,14},{3,15},{4,8},{5,9},{6,10},{7,11},{8,4},{9,5},... | collective-permute-start | bytes 835592 | tf_op jit(solution)/shard_map/ppermute | solution.py:25
  9.0 26.5 %collective-permute-start.7 = (bf16[64,2176]{1,0:T(8,128)(2,1)S(1)}, bf16[64,2176]{1,0:T(8,128)(2,1)}, u32[]{:S(2)}, u32[]{:S(2)}) collective-permute-start(bf16[64,2176]{1,0:T(8,128)(2,1)S(1)} %pad_maximum_fusion.14), channel_id=1, source_target_pairs={{0,8},{1,9},{2,10},{3,11},{4,12},{5,13},{6,14},{7,15},{8,0},{9,1},... | collective-permute-start | bytes 835592 | tf_op jit(solution)/shard_map/ppermute | solution.py:25
  9.1 9.6 %collective-permute-start = (bf16[64,2176]{1,0:T(8,128)(2,1)S(1)}, bf16[64,2176]{1,0:T(8,128)(2,1)S(1)}, u32[]{:S(2)}, u32[]{:S(2)}) collective-permute-start(bf16[64,2176]{1,0:T(8,128)(2,1)S(1)} %pad_maximum_fusion.14), channel_id=1, source_target_pairs={{0,2},{1,3},{2,0},{3,1},{4,6},{5,7},{6,4},{7,5},{8,10},{9,11},{10,... | collective-permute-start | bytes 835592 | tf_op jit(solution)/shard_map/ppermute | solution.py:31
  12.5 17.6 %collective-permute-start.22 = (bf16[64,2048]{1,0:T(8,128)(2,1)}, bf16[64,2048]{1,0:T(8,128)(2,1)}, u32[]{:S(2)}, u32[]{:S(2)}) collective-permute-start(bf16[64,2048]{1,0:T(8,128)(2,1)} %get-tuple-element.61), channel_id=1, source_target_pairs={{0,2},{1,3},{2,0},{3,1},{4,6},{5,7},{6,4},{7,5},{8,10},{9,11},{10,... | collective-permute-start | bytes 786440 | tf_op jit(solution)/shard_map/ppermute | solution.py:31
  14.2 14.3 %collective-permute-start.4 = (bf16[64,2176]{1,0:T(8,128)(2,1)S(1)}, bf16[64,2176]{1,0:T(8,128)(2,1)S(1)}, u32[]{:S(2)}, u32[]{:S(2)}) collective-permute-start(bf16[64,2176]{1,0:T(8,128)(2,1)S(1)} %collective-permute-done.3), channel_id=1, source_target_pairs={{0,2},{1,3},{2,0},{3,1},{4,6},{5,7},{6,4},{7,5},{8,10},{9,11},{10,... | collective-permute-start | bytes 835592 | tf_op jit(solution)/shard_map/ppermute | solution.py:31
  18.7 18.3 %collective-permute-start.1 = (bf16[128,2176]{1,0:T(8,128)(2,1)S(1)}, bf16[128,2176]{1,0:T(8,128)(2,1)S(1)}, u32[]{:S(2)}, u32[]{:S(2)}) collective-permute-start(bf16[128,2176]{1,0:T(8,128)(2,1)S(1)} %pad_maximum_fusion.6), channel_id=1, source_target_pairs={{0,1},{1,0},{2,3},{3,2},{4,5},{5,4},{6,7},{7,6},{8,9},{9,8},{10,11... | collective-permute-start | bytes 1671176 | tf_op jit(solution)/shard_map/ppermute | solution.py:31
  28.5 6.9 %collective-permute-start.5 = (bf16[64,2176]{1,0:T(8,128)(2,1)S(1)}, bf16[64,2176]{1,0:T(8,128)(2,1)S(1)}, u32[]{:S(2)}, u32[]{:S(2)}) collective-permute-start(bf16[64,2176]{1,0:T(8,128)(2,1)S(1)} %collective-permute-done.2), channel_id=1, source_target_pairs={{0,2},{1,3},{2,0},{3,1},{4,6},{5,7},{6,4},{7,5},{8,10},{9,11},{10,... | collective-permute-start | bytes 835592 | tf_op jit(solution)/shard_map/ppermute | solution.py:31
  30.1 16.3 %collective-permute-start.23 = (bf16[64,2048]{1,0:T(8,128)(2,1)}, bf16[64,2048]{1,0:T(8,128)(2,1)S(1)}, u32[]{:S(2)}, u32[]{:S(2)}) collective-permute-start(bf16[64,2048]{1,0:T(8,128)(2,1)} %collective-permute-done.22), channel_id=1, source_target_pairs={{0,16},{16,0},{1,17},{17,1},{2,18},{18,2},{3,19},{19,3},{4,20},{20... | collective-permute-start | bytes 786440 | tf_op jit(solution)/shard_map/ppermute | solution.py:147
  31.6 7.9 %collective-permute-start.10 = (bf16[128,2176]{1,0:T(8,128)(2,1)S(1)}, bf16[128,2176]{1,0:T(8,128)(2,1)S(1)}, u32[]{:S(2)}, u32[]{:S(2)}) collective-permute-start(bf16[128,2176]{1,0:T(8,128)(2,1)S(1)} %pad_maximum_fusion.9), channel_id=1, source_target_pairs={{0,1},{1,0},{2,3},{3,2},{4,5},{5,4},{6,7},{7,6},{8,9},{9,8},{10,11... | collective-permute-start | bytes 1671176 | tf_op jit(solution)/shard_map/ppermute | solution.py:31
  35.5 9.5 %collective-permute-start.8 = (bf16[64,2176]{1,0:T(8,128)(2,1)}, bf16[64,2176]{1,0:T(8,128)(2,1)S(1)}, u32[]{:S(2)}, u32[]{:S(2)}) collective-permute-start(bf16[64,2176]{1,0:T(8,128)(2,1)} %collective-permute-done.7), channel_id=1, source_target_pairs={{0,2},{1,3},{2,0},{3,1},{4,6},{5,7},{6,4},{7,5},{8,10},{9,11},{10,... | collective-permute-start | bytes 835592 | tf_op jit(solution)/shard_map/ppermute | solution.py:31
  37.2 4.9 %collective-permute-start.9 = (bf16[128,2176]{1,0:T(8,128)(2,1)S(1)}, bf16[128,2176]{1,0:T(8,128)(2,1)S(1)}, u32[]{:S(2)}, u32[]{:S(2)}) collective-permute-start(bf16[128,2176]{1,0:T(8,128)(2,1)S(1)} %pad_maximum_fusion.8), channel_id=1, source_target_pairs={{0,1},{1,0},{2,3},{3,2},{4,5},{5,4},{6,7},{7,6},{8,9},{9,8},{10,11... | collective-permute-start | bytes 1671176 | tf_op jit(solution)/shard_map/ppermute | solution.py:31
  44.4 4.2 %collective-permute-start.12 = (bf16[128,2048]{1,0:T(8,128)(2,1)S(1)}, bf16[128,2048]{1,0:T(8,128)(2,1)S(1)}, u32[]{:S(2)}, u32[]{:S(2)}) collective-permute-start(bf16[128,2048]{1,0:T(8,128)(2,1)S(1)} %slice.381), channel_id=1, source_target_pairs={{0,1},{1,0},{2,3},{3,2},{4,5},{5,4},{6,7},{7,6},{8,9},{9,8},{10,11... | collective-permute-start | bytes 1572872 | tf_op jit(solution)/shard_map/ppermute | solution.py:31
  47.4 4.5 %collective-permute-start.6 = (bf16[128,2048]{1,0:T(8,128)(2,1)S(1)}, bf16[128,2048]{1,0:T(8,128)(2,1)S(1)}, u32[]{:S(2)}, u32[]{:S(2)}) collective-permute-start(bf16[128,2048]{1,0:T(8,128)(2,1)S(1)} %slice.373), channel_id=1, source_target_pairs={{0,1},{1,0},{2,3},{3,2},{4,5},{5,4},{6,7},{7,6},{8,9},{9,8},{10,11... | collective-permute-start | bytes 1572872 | tf_op jit(solution)/shard_map/ppermute | solution.py:31
  48.0 17.4 %collective-permute-start.24 = (bf16[64,2048]{1,0:T(8,128)(2,1)S(1)}, bf16[64,2048]{1,0:T(8,128)(2,1)S(1)}, u32[]{:S(2)}, u32[]{:S(2)}) collective-permute-start(bf16[64,2048]{1,0:T(8,128)(2,1)S(1)} %copy-done.15), channel_id=1, source_target_pairs={{0,2},{1,3},{2,0},{3,1},{4,6},{5,7},{6,4},{7,5},{8,10},{9,11},{10,... | collective-permute-start | bytes 786440 | tf_op jit(solution)/shard_map/ppermute | solution.py:31
  48.6 3.5 %collective-permute-start.19 = (bf16[128,2048]{1,0:T(8,128)(2,1)S(1)}, bf16[128,2048]{1,0:T(8,128)(2,1)S(1)}, u32[]{:S(2)}, u32[]{:S(2)}) collective-permute-start(bf16[128,2048]{1,0:T(8,128)(2,1)S(1)} %slice.391), channel_id=1, source_target_pairs={{0,1},{1,0},{2,3},{3,2},{4,5},{5,4},{6,7},{7,6},{8,9},{9,8},{10,11... | collective-permute-start | bytes 1572872 | tf_op jit(solution)/shard_map/ppermute | solution.py:31
  48.6 79.4 %collective-permute-start.33 = (bf16[2048,1024]{1,0:T(8,128)(2,1)S(1)}, bf16[2048,1024]{1,0:T(8,128)(2,1)S(1)}, u32[]{:S(2)}, u32[]{:S(2)}) collective-permute-start(bf16[2048,1024]{1,0:T(8,128)(2,1)S(1)} %bitcast.63), channel_id=1, source_target_pairs={{0,1},{1,0},{2,3},{3,2},{4,5},{5,4},{6,7},{7,6},{8,9},{9,8},{10,11... | collective-permute-start | bytes 12582920 | tf_op jit(solution)/shard_map/ppermute | solution.py:31
  51.8 5.5 %collective-permute-start.13 = (bf16[128,2048]{1,0:T(8,128)(2,1)S(1)}, bf16[128,2048]{1,0:T(8,128)(2,1)S(1)}, u32[]{:S(2)}, u32[]{:S(2)}) collective-permute-start(bf16[128,2048]{1,0:T(8,128)(2,1)S(1)} %slice.385), channel_id=1, source_target_pairs={{0,1},{1,0},{2,3},{3,2},{4,5},{5,4},{6,7},{7,6},{8,9},{9,8},{10,11... | collective-permute-start | bytes 1572872 | tf_op jit(solution)/shard_map/ppermute | solution.py:31
  52.3 10.6 %collective-permute-start.16 = (bf16[64,2048]{1,0:T(8,128)(2,1)S(1)}, bf16[64,2048]{1,0:T(8,128)(2,1)S(1)}, u32[]{:S(2)}, u32[]{:S(2)}) collective-permute-start(bf16[64,2048]{1,0:T(8,128)(2,1)S(1)} %slice.388), channel_id=1, source_target_pairs={{0,2},{1,3},{2,0},{3,1},{4,6},{5,7},{6,4},{7,5},{8,10},{9,11},{10,... | collective-permute-start | bytes 786440 | tf_op jit(solution)/shard_map/ppermute | solution.py:31
  57.4 11.1 %collective-permute-start.14 = (bf16[64,2048]{1,0:T(8,128)(2,1)S(1)}, bf16[64,2048]{1,0:T(8,128)(2,1)S(1)}, u32[]{:S(2)}, u32[]{:S(2)}) collective-permute-start(bf16[64,2048]{1,0:T(8,128)(2,1)S(1)} %slice.386), channel_id=1, source_target_pairs={{0,2},{1,3},{2,0},{3,1},{4,6},{5,7},{6,4},{7,5},{8,10},{9,11},{10,... | collective-permute-start | bytes 786440 | tf_op jit(solution)/shard_map/ppermute | solution.py:31
  63.0 13.9 %collective-permute-start.17 = (bf16[64,2048]{1,0:T(8,128)(2,1)S(1)}, bf16[64,2048]{1,0:T(8,128)(2,1)S(1)}, u32[]{:S(2)}, u32[]{:S(2)}) collective-permute-start(bf16[64,2048]{1,0:T(8,128)(2,1)S(1)} %add_convert_fusion.12), channel_id=1, source_target_pairs={{0,12},{1,13},{2,14},{3,15},{4,8},{5,9},{6,10},{7,11},{8,4},{9,5},... | collective-permute-start | bytes 786440 | tf_op jit(solution)/shard_map/ppermute | solution.py:25
  65.4 11.3 %collective-permute-start.20 = (bf16[64,2048]{1,0:T(8,128)(2,1)S(1)}, bf16[64,2048]{1,0:T(8,128)(2,1)S(1)}, u32[]{:S(2)}, u32[]{:S(2)}) collective-permute-start(bf16[64,2048]{1,0:T(8,128)(2,1)S(1)} %slice.393), channel_id=1, source_target_pairs={{0,2},{1,3},{2,0},{3,1},{4,6},{5,7},{6,4},{7,5},{8,10},{9,11},{10,... | collective-permute-start | bytes 786440 | tf_op jit(solution)/shard_map/ppermute | solution.py:31
  68.5 6.5 %collective-permute-start.25 = (bf16[64,2048]{1,0:T(8,128)(2,1)S(1)}, bf16[64,2048]{1,0:T(8,128)(2,1)S(1)}, u32[]{:S(2)}, u32[]{:S(2)}) collective-permute-start(bf16[64,2048]{1,0:T(8,128)(2,1)S(1)} %collective-permute-done.24), channel_id=1, source_target_pairs={{0,16},{16,0},{1,17},{17,1},{2,18},{18,2},{3,19},{19,3},{4,20},{20... | collective-permute-start | bytes 786440 | tf_op jit(solution)/shard_map/ppermute | solution.py:147
  70.1 17.1 %collective-permute-start.18 = (bf16[64,2048]{1,0:T(8,128)(2,1)S(1)}, bf16[64,2048]{1,0:T(8,128)(2,1)S(1)}, u32[]{:S(2)}, u32[]{:S(2)}) collective-permute-start(bf16[64,2048]{1,0:T(8,128)(2,1)S(1)} %add_convert_fusion.11), channel_id=1, source_target_pairs={{0,8},{1,9},{2,10},{3,11},{4,12},{5,13},{6,14},{7,15},{8,0},{9,1},... | collective-permute-start | bytes 786440 | tf_op jit(solution)/shard_map/ppermute | solution.py:25
  75.0 12.2 %collective-permute-start.15 = (bf16[64,2048]{1,0:T(8,128)(2,1)S(1)}, bf16[64,2048]{1,0:T(8,128)(2,1)S(1)}, u32[]{:S(2)}, u32[]{:S(2)}) collective-permute-start(bf16[64,2048]{1,0:T(8,128)(2,1)S(1)} %slice.375), channel_id=1, source_target_pairs={{0,2},{1,3},{2,0},{3,1},{4,6},{5,7},{6,4},{7,5},{8,10},{9,11},{10,... | collective-permute-start | bytes 786440 | tf_op jit(solution)/shard_map/ppermute | solution.py:31
  76.7 19.1 %collective-permute-start.26 = (bf16[2,256,2048]{2,1,0:T(8,128)(2,1)S(1)}, bf16[2,256,2048]{2,1,0:T(8,128)(2,1)S(1)}, u32[]{:S(2)}, u32[]{:S(2)}) collective-permute-start(bf16[2,256,2048]{2,1,0:T(8,128)(2,1)S(1)} %maximum_select_fusion.1), channel_id=1, source_target_pairs={{0,1},{1,0},{2,3},{3,2},{4,5},{5,4},{6,7},{7,6},{8,9},{9,8},{10,11... | collective-permute-start | bytes 6291464 | tf_op jit(solution)/shard_map/ppermute | solution.py:31
  76.9 15.2 %collective-permute-start.21 = (bf16[64,2048]{1,0:T(8,128)(2,1)S(1)}, bf16[64,2048]{1,0:T(8,128)(2,1)S(1)}, u32[]{:S(2)}, u32[]{:S(2)}) collective-permute-start(bf16[64,2048]{1,0:T(8,128)(2,1)S(1)} %add_convert_fusion.10), channel_id=1, source_target_pairs={{0,4},{1,5},{2,6},{3,7},{4,0},{5,1},{6,2},{7,3},{8,12},{9,13},{10,... | collective-permute-start | bytes 786440 | tf_op jit(solution)/shard_map/ppermute | solution.py:25
  87.1 40.9 %collective-permute-start.34 = (bf16[512,2048]{1,0:T(8,128)(2,1)S(1)}, bf16[512,2048]{1,0:T(8,128)(2,1)S(1)}, u32[]{:S(2)}, u32[]{:S(2)}) collective-permute-start(bf16[512,2048]{1,0:T(8,128)(2,1)S(1)} %bitcast.64), channel_id=1, source_target_pairs={{0,1},{1,0},{2,3},{3,2},{4,5},{5,4},{6,7},{7,6},{8,9},{9,8},{10,11... | collective-permute-start | bytes 6291464 | tf_op jit(solution)/shard_map/ppermute | solution.py:31
  92.9 8.3 %collective-permute-start.27 = (bf16[64,1024]{1,0:T(8,128)(2,1)S(1)}, bf16[64,1024]{1,0:T(8,128)(2,1)S(1)}, u32[]{:S(2)}, u32[]{:S(2)}) collective-permute-start(bf16[64,1024]{1,0:T(8,128)(2,1)S(1)} %get-tuple-element.63), channel_id=1, source_target_pairs={{0,12},{1,13},{2,14},{3,15},{4,8},{5,9},{6,10},{7,11},{8,4},{9,5},... | collective-permute-start | bytes 393224 | tf_op jit(solution)/shard_map/ppermute | solution.py:25
  95.5 15.4 %collective-permute-start.29 = (bf16[64,1024]{1,0:T(8,128)(2,1)S(1)}, bf16[64,1024]{1,0:T(8,128)(2,1)S(1)}, u32[]{:S(2)}, u32[]{:S(2)}) collective-permute-start(bf16[64,1024]{1,0:T(8,128)(2,1)S(1)} %get-tuple-element.64), channel_id=1, source_target_pairs={{0,8},{1,9},{2,10},{3,11},{4,12},{5,13},{6,14},{7,15},{8,0},{9,1},... | collective-permute-start | bytes 393224 | tf_op jit(solution)/shard_map/ppermute | solution.py:25
  95.9 15.9 %collective-permute-start.31 = (bf16[64,1024]{1,0:T(8,128)(2,1)S(1)}, bf16[64,1024]{1,0:T(8,128)(2,1)S(1)}, u32[]{:S(2)}, u32[]{:S(2)}) collective-permute-start(bf16[64,1024]{1,0:T(8,128)(2,1)S(1)} %get-tuple-element.65), channel_id=1, source_target_pairs={{0,4},{1,5},{2,6},{3,7},{4,0},{5,1},{6,2},{7,3},{8,12},{9,13},{10,... | collective-permute-start | bytes 393224 | tf_op jit(solution)/shard_map/ppermute | solution.py:25
  102.0 14.8 %collective-permute-start.28 = (bf16[64,2048]{1,0:T(8,128)(2,1)S(1)}, bf16[64,2048]{1,0:T(8,128)(2,1)S(1)}, u32[]{:S(2)}, u32[]{:S(2)}) collective-permute-start(bf16[64,2048]{1,0:T(8,128)(2,1)S(1)} %convolution_convert_fusion.6), channel_id=1, source_target_pairs={{0,12},{1,13},{2,14},{3,15},{4,8},{5,9},{6,10},{7,11},{8,4},{9,5},... | collective-permute-start | bytes 786440 | tf_op jit(solution)/shard_map/ppermute | solution.py:25
  111.7 16.0 %collective-permute-start.30 = (bf16[64,2048]{1,0:T(8,128)(2,1)S(1)}, bf16[64,2048]{1,0:T(8,128)(2,1)S(1)}, u32[]{:S(2)}, u32[]{:S(2)}) collective-permute-start(bf16[64,2048]{1,0:T(8,128)(2,1)S(1)} %convolution_convert_fusion.5), channel_id=1, source_target_pairs={{0,8},{1,9},{2,10},{3,11},{4,12},{5,13},{6,14},{7,15},{8,0},{9,1},... | collective-permute-start | bytes 786440 | tf_op jit(solution)/shard_map/ppermute | solution.py:25
  112.7 15.1 %collective-permute-start.32 = (bf16[64,2048]{1,0:T(8,128)(2,1)S(1)}, bf16[64,2048]{1,0:T(8,128)(2,1)S(1)}, u32[]{:S(2)}, u32[]{:S(2)}) collective-permute-start(bf16[64,2048]{1,0:T(8,128)(2,1)S(1)} %convolution_convert_fusion.4), channel_id=1, source_target_pairs={{0,4},{1,5},{2,6},{3,7},{4,0},{5,1},{6,2},{7,3},{8,12},{9,13},{10,... | collective-permute-start | bytes 786440 | tf_op jit(solution)/shard_map/ppermute | solution.py:25
  130.0 8.4 %collective-permute-start.36 = (bf16[64,2048]{1,0:T(8,128)(2,1)S(1)}, bf16[64,2048]{1,0:T(8,128)(2,1)}, u32[]{:S(2)}, u32[]{:S(2)}) collective-permute-start(bf16[64,2048]{1,0:T(8,128)(2,1)S(1)} %fusion.25), channel_id=1, source_target_pairs={{0,4},{1,5},{2,6},{3,7},{4,0},{5,1},{6,2},{7,3},{8,12},{9,13},{10,... | collective-permute-start | bytes 786440 | tf_op jit(solution)/shard_map/ppermute | solution.py:25
  130.6 15.9 %collective-permute-start.35 = (bf16[64,2048]{1,0:T(8,128)(2,1)S(1)}, bf16[64,2048]{1,0:T(8,128)(2,1)}, u32[]{:S(2)}, u32[]{:S(2)}) collective-permute-start(bf16[64,2048]{1,0:T(8,128)(2,1)S(1)} %fusion.25), channel_id=1, source_target_pairs={{0,2},{1,3},{2,0},{3,1},{4,6},{5,7},{6,4},{7,5},{8,10},{9,11},{10,... | collective-permute-start | bytes 786440 | tf_op jit(solution)/shard_map/ppermute | solution.py:31
  133.6 14.0 %collective-permute-start.38 = (bf16[64,2048]{1,0:T(8,128)(2,1)S(1)}, bf16[64,2048]{1,0:T(8,128)(2,1)S(1)}, u32[]{:S(2)}, u32[]{:S(2)}) collective-permute-start(bf16[64,2048]{1,0:T(8,128)(2,1)S(1)} %fusion.25), channel_id=1, source_target_pairs={{0,12},{1,13},{2,14},{3,15},{4,8},{5,9},{6,10},{7,11},{8,4},{9,5},... | collective-permute-start | bytes 786440 | tf_op jit(solution)/shard_map/ppermute | solution.py:25
  138.5 9.2 %collective-permute-start.37 = (bf16[64,2048]{1,0:T(8,128)(2,1)}, bf16[64,2048]{1,0:T(8,128)(2,1)S(1)}, u32[]{:S(2)}, u32[]{:S(2)}) collective-permute-start(bf16[64,2048]{1,0:T(8,128)(2,1)} %collective-permute-done.36), channel_id=1, source_target_pairs={{0,2},{1,3},{2,0},{3,1},{4,6},{5,7},{6,4},{7,5},{8,10},{9,11},{10,... | collective-permute-start | bytes 786440 | tf_op jit(solution)/shard_map/ppermute | solution.py:31
  140.6 18.6 %collective-permute-start.40 = (bf16[64,2048]{1,0:T(8,128)(2,1)S(1)}, bf16[64,2048]{1,0:T(8,128)(2,1)S(1)}, u32[]{:S(2)}, u32[]{:S(2)}) collective-permute-start(bf16[64,2048]{1,0:T(8,128)(2,1)S(1)} %fusion.25), channel_id=1, source_target_pairs={{0,8},{1,9},{2,10},{3,11},{4,12},{5,13},{6,14},{7,15},{8,0},{9,1},... | collective-permute-start | bytes 786440 | tf_op jit(solution)/shard_map/ppermute | solution.py:25
  147.7 11.5 %collective-permute-start.39 = (bf16[64,2048]{1,0:T(8,128)(2,1)S(1)}, bf16[64,2048]{1,0:T(8,128)(2,1)S(1)}, u32[]{:S(2)}, u32[]{:S(2)}) collective-permute-start(bf16[64,2048]{1,0:T(8,128)(2,1)S(1)} %collective-permute-done.38), channel_id=1, source_target_pairs={{0,2},{1,3},{2,0},{3,1},{4,6},{5,7},{6,4},{7,5},{8,10},{9,11},{10,... | collective-permute-start | bytes 786440 | tf_op jit(solution)/shard_map/ppermute | solution.py:31
  159.2 10.7 %collective-permute-start.41 = (bf16[64,2048]{1,0:T(8,128)(2,1)S(1)}, bf16[64,2048]{1,0:T(8,128)(2,1)S(1)}, u32[]{:S(2)}, u32[]{:S(2)}) collective-permute-start(bf16[64,2048]{1,0:T(8,128)(2,1)S(1)} %collective-permute-done.40), channel_id=1, source_target_pairs={{0,2},{1,3},{2,0},{3,1},{4,6},{5,7},{6,4},{7,5},{8,10},{9,11},{10,... | collective-permute-start | bytes 786440 | tf_op jit(solution)/shard_map/ppermute | solution.py:31
  168.8 8.8 %collective-permute-start.44 = (bf16[64,2048]{1,0:T(8,128)(2,1)S(1)}, bf16[64,2048]{1,0:T(8,128)(2,1)S(1)}, u32[]{:S(2)}, u32[]{:S(2)}) collective-permute-start(bf16[64,2048]{1,0:T(8,128)(2,1)S(1)} %slice.414), channel_id=1, source_target_pairs={{0,2},{1,3},{2,0},{3,1},{4,6},{5,7},{6,4},{7,5},{8,10},{9,11},{10,... | collective-permute-start | bytes 786440 | tf_op jit(solution)/shard_map/ppermute | solution.py:31
  172.5 10.7 %collective-permute-start.42 = (bf16[64,2048]{1,0:T(8,128)(2,1)S(1)}, bf16[64,2048]{1,0:T(8,128)(2,1)S(1)}, u32[]{:S(2)}, u32[]{:S(2)}) collective-permute-start(bf16[64,2048]{1,0:T(8,128)(2,1)S(1)} %slice.412), channel_id=1, source_target_pairs={{0,2},{1,3},{2,0},{3,1},{4,6},{5,7},{6,4},{7,5},{8,10},{9,11},{10,... | collective-permute-start | bytes 786440 | tf_op jit(solution)/shard_map/ppermute | solution.py:31
  177.7 16.2 %collective-permute-start.45 = (bf16[64,2048]{1,0:T(8,128)(2,1)S(1)}, bf16[64,2048]{1,0:T(8,128)(2,1)S(1)}, u32[]{:S(2)}, u32[]{:S(2)}) collective-permute-start(bf16[64,2048]{1,0:T(8,128)(2,1)S(1)} %add_convert_fusion.7), channel_id=1, source_target_pairs={{0,12},{1,13},{2,14},{3,15},{4,8},{5,9},{6,10},{7,11},{8,4},{9,5},... | collective-permute-start | bytes 786440 | tf_op jit(solution)/shard_map/ppermute | solution.py:25
  180.3 6.4 %collective-permute-start.47 = (bf16[64,2048]{1,0:T(8,128)(2,1)S(1)}, bf16[64,2048]{1,0:T(8,128)(2,1)S(1)}, u32[]{:S(2)}, u32[]{:S(2)}) collective-permute-start(bf16[64,2048]{1,0:T(8,128)(2,1)S(1)} %get-tuple-element.48), channel_id=1, source_target_pairs={{0,2},{1,3},{2,0},{3,1},{4,6},{5,7},{6,4},{7,5},{8,10},{9,11},{10,... | collective-permute-start | bytes 786440 | tf_op jit(solution)/shard_map/ppermute | solution.py:31
  183.3 16.2 %collective-permute-start.46 = (bf16[64,2048]{1,0:T(8,128)(2,1)S(1)}, bf16[64,2048]{1,0:T(8,128)(2,1)S(1)}, u32[]{:S(2)}, u32[]{:S(2)}) collective-permute-start(bf16[64,2048]{1,0:T(8,128)(2,1)S(1)} %add_convert_fusion.6), channel_id=1, source_target_pairs={{0,8},{1,9},{2,10},{3,11},{4,12},{5,13},{6,14},{7,15},{8,0},{9,1},... | collective-permute-start | bytes 786440 | tf_op jit(solution)/shard_map/ppermute | solution.py:25
  186.8 14.2 %collective-permute-start.48 = (bf16[64,2048]{1,0:T(8,128)(2,1)S(1)}, bf16[64,2048]{1,0:T(8,128)(2,1)S(1)}, u32[]{:S(2)}, u32[]{:S(2)}) collective-permute-start(bf16[64,2048]{1,0:T(8,128)(2,1)S(1)} %add_convert_fusion.5), channel_id=1, source_target_pairs={{0,4},{1,5},{2,6},{3,7},{4,0},{5,1},{6,2},{7,3},{8,12},{9,13},{10,... | collective-permute-start | bytes 786440 | tf_op jit(solution)/shard_map/ppermute | solution.py:25
  192.7 8.3 %collective-permute-start.43 = (bf16[64,2048]{1,0:T(8,128)(2,1)S(1)}, bf16[64,2048]{1,0:T(8,128)(2,1)S(1)}, u32[]{:S(2)}, u32[]{:S(2)}) collective-permute-start(bf16[64,2048]{1,0:T(8,128)(2,1)S(1)} %get-tuple-element.47), channel_id=1, source_target_pairs={{0,2},{1,3},{2,0},{3,1},{4,6},{5,7},{6,4},{7,5},{8,10},{9,11},{10,... | collective-permute-start | bytes 786440 | tf_op jit(solution)/shard_map/ppermute | solution.py:31
  (20 other events, 189.1 us)

commit v13 on v12

--- a/solution.py
+++ b/solution.py
@@ -106,10 +106,10 @@
 
     halves = {}
     if paired:
-        both = work((0, 1), after(jnp.concatenate([chunk(0), chunk(1)], axis=0), crossed[3]))
-        third = work((3,), after(chunk(3), both))
+        third = work((3,), after(chunk(3), crossed[3]))
         halves[3] = halve(third)
-        last = work((2,), after(chunk(2), halves[3]))
+        both = work((0, 1), after(jnp.concatenate([chunk(0), chunk(1)], axis=0), third))
+        last = work((2,), after(chunk(2), both, halves[3]))
         count = both.shape[0] // 2
         done = {0: both[:count], 1: both[count:]}
     else:
@@ -177,7 +177,7 @@
     first_gate_up,
     first_down,
     second_routes,
-    second_gates,
+    second_weights,
     second_gate_up,
     second_down,
     hidden_gain,
@@ -186,21 +186,22 @@
 ):
     ring = Ring()
     width = hidden_rows.shape[1]
-    lanes = gate_lanes([(first_routes, first_gates), (second_routes, second_gates)])
+    lanes = gate_lanes([(first_routes, first_gates), (second_routes, second_weights)])
     top = first_routes.shape[1]
     people = (ring.me, ring.me ^ 1)
-    second_lanes = {}
+    second_gates = {}
 
     def first_work(slots, chunk):
         lanes = chunk[:, width:]
-        second_lanes[slots[0]] = lanes[: chunk.shape[0] // 2]
+        paired = lanes[: chunk.shape[0] // 2]
+        second_gates[slots[0]] = [gate_column(paired, who, 1, top) for who in people]
         return experts(
             chunk[:, :width], [gate_column(lanes, ring.me, 0, top)], [(first_gate_up[0], first_down[0])]
         )
 
     def second_work(slots, chunk):
-        lanes = jnp.concatenate([second_lanes[slot] for slot in slots], axis=0)
-        return experts(chunk, [gate_column(lanes, who, 1, top) for who in people], second_pair)
+        gates = [jnp.concatenate([second_gates[slot][i] for slot in slots], axis=0) for i in range(2)]
+        return experts(chunk, gates, second_pair)
 
     first, steps = routed(ring, jnp.concatenate([hidden_rows, lanes], axis=1), first_work, False)
     mine = (second_gate_up[0], second_down[0])
@@ -209,9 +210,9 @@
     weight = plane_weight(ring, merge_weight, other_half(ring, merge_weight, lax.axis_size("groups"), ties))
     after_first = (hidden_rows.astype(jnp.float32) + first).astype(jnp.bfloat16)
     merged_in = jnp.concatenate([normed(after_first, hidden_gain), normed(token_embed, embed_gain)], axis=1)
-    merged = merge(ring, merged_in, weight)
+    merged = merge(ring, merged_in, after(weight, *second_pair[1], *[g for slot in range(PLANES) for g in second_gates[slot]]))
     after_merge = (after_first.astype(jnp.float32) + jax.nn.silu(merged)).astype(jnp.bfloat16)
-    second, _ = routed(ring, after(after_merge, *second_pair[1]), second_work, True)
+    second, _ = routed(ring, after_merge, second_work, True)
     return (after_merge.astype(jnp.float32) + second).astype(jnp.bfloat16)
 
 

time: 202 us -> 223 us (1.10)
  matrix products: 20.9 us -> 45.9 us
  starting transfers between devices: 72.7 us -> 60.1 us
  waiting for transfers between devices: 82.6 us -> 88.5 us
  other arithmetic: 16.5 us -> 22.1 us
  local copies, waits for them, and re-layouts: 8.16 us -> 4.42 us
    dot_general x10, matrix products: 10.6 us -> 23.5 us  [experts(): projected = jnp.dot(rows, gate_up, preferred_element_type=jnp.float32)]
    ppermute x18, starting transfers between devices: 47.7 us -> 35.2 us  [send(): return lax.ppermute(values, 'inner', perm)]
    dot_general x10, matrix products: 6.98 us -> 16.6 us  [experts(): jnp.dot(hidden.astype(jnp.bfloat16), down, preferred_element_type=jnp.flo...]
    ppermute x18, waiting for transfers between devices: 50.8 us -> 55.7 us  [send(): return lax.ppermute(values, 'inner', perm)]
    unnamed x38 -> x34, local copies, waits for them, and re-layouts: 4.37 us -> 1.46 us
    ppermute x2, waiting for transfers between devices: 2.58 us -> 5.43 us  [other_half(): there = lax.ppermute(here, 'groups', [(g, g ^ 1) for g in range(groups)])]
    reduce_sum x7 -> x8, other arithmetic: 2.29 us -> 5.03 us  [gate_column(): jnp.sum(jnp.where(named == who.astype(jnp.float32), high + low, 0.0), axi...]
    dot_general x4, matrix products: 3.37 us -> 5.76 us  [merge(): jnp.dot(ring.between(piece, slot), weight, preferred_element_type=jnp.flo...]
  transfers between devices with their start and end apart: 49 -> 49, of which waited for: 20 -> 20; matrix products, arithmetic and copies ran while one was open for 18% -> 29% of each run, Pallas kernels for 0% -> 0%
where the time goes in v13:
time: 223 us; the launch traced here: 222 us
  waiting for transfers between devices  88.5 us (40%)
  starting transfers between devices  60.1 us (27%)
  matrix products  45.9 us (21%)
  other arithmetic  22.1 us (10%)
  local copies, waits for them, and re-layouts  4.42 us (2%)
    ppermute x18, waiting for transfers between devices, send(): return lax.ppermute(values, 'inner', perm)  55.7 us
    ppermute x18, starting transfers between devices, send(): return lax.ppermute(values, 'inner', perm)  35.2 us
    ppermute x29, waiting for transfers between devices, across(): lax.ppermute(values, 'inner', [(d, d ^ bit) for d in range(self.size)])  27.4 us
    dot_general x10, matrix products, experts(): projected = jnp.dot(rows, gate_up, preferred_element_type=jnp.float32)  23.5 us
    ppermute x29, starting transfers between devices, across(): lax.ppermute(values, 'inner', [(d, d ^ bit) for d in range(self.size)])  21.8 us
    dot_general x10, matrix products, experts(): jnp.dot(hidden.astype(jnp.bfloat16), down, preferred_element_type=jnp.flo...  16.6 us
    dot_general x4, matrix products, merge(): jnp.dot(ring.between(piece, slot), weight, preferred_element_type=jnp.flo...  5.76 us
    ppermute x2, waiting for transfers between devices, other_half(): there = lax.ppermute(here, 'groups', [(g, g ^ 1) for g in range(groups)])  5.43 us
  transfers between devices with their start and end apart: 49, of which 20 were waited for; matrix products, arithmetic and copies ran while one was open for 29% of the time, Pallas kernels for 0%

profile of v13, /device:TPU:0, one launch (start us, length us, event | category | flops | bytes accessed | tf_op | source)
XLA Modules:
  0.0 221.9 jit_solution(3968808037274550452)
XLA Ops:
  3.4 3.1 %collective-permute-start.3 = (bf16[64,2176]{1,0:T(8,128)(2,1)S(1)}, bf16[64,2176]{1,0:T(8,128)(2,1)S(1)}, u32[]{:S(2)}, u32[]{:S(2)}) collective-permute-start(bf16[64,2176]{1,0:T(8,128)(2,1)S(1)} %pad_maximum_fusion.14), channel_id=1, source_target_pairs={{0,4},{1,5},{2,6},{3,7},{4,0},{5,1},{6,2},{7,3},{8,12},{9,13},{10,... | collective-permute-start | bytes 835592 | tf_op jit(solution)/shard_map/ppermute | solution.py:25
  6.5 2.5 %collective-permute-start.2 = (bf16[64,2176]{1,0:T(8,128)(2,1)S(1)}, bf16[64,2176]{1,0:T(8,128)(2,1)S(1)}, u32[]{:S(2)}, u32[]{:S(2)}) collective-permute-start(bf16[64,2176]{1,0:T(8,128)(2,1)S(1)} %pad_maximum_fusion.14), channel_id=1, source_target_pairs={{0,12},{1,13},{2,14},{3,15},{4,8},{5,9},{6,10},{7,11},{8,4},{9,5},... | collective-permute-start | bytes 835592 | tf_op jit(solution)/shard_map/ppermute | solution.py:25
  10.6 1.9 constant_dynamic-slice_fusion.1
  14.1 1.6 collective-permute-start.4
  15.7 3.1 %collective-permute-done = bf16[64,2176]{1,0:T(8,128)(2,1)} collective-permute-done((bf16[64,2176]{1,0:T(8,128)(2,1)S(1)}, bf16[64,2176]{1,0:T(8,128)(2,1)}, u32[]{:S(2)}, u32[]{:S(2)}) %collective-permute-start) | collective-permute-done | bytes 278560 | tf_op jit(solution)/shard_map/ppermute | solution.py:31
  19.9 2.7 %collective-permute-done.2 = bf16[64,2176]{1,0:T(8,128)(2,1)S(1)} collective-permute-done((bf16[64,2176]{1,0:T(8,128)(2,1)S(1)}, bf16[64,2176]{1,0:T(8,128)(2,1)S(1)}, u32[]{:S(2)}, u32[]{:S(2)}) %collective-permute-start.2) | collective-permute-done | bytes 278560 | tf_op jit(solution)/shard_map/ppermute | solution.py:25
  22.5 6.0 %collective-permute-done.4 = bf16[64,2176]{1,0:T(8,128)(2,1)S(1)} collective-permute-done((bf16[64,2176]{1,0:T(8,128)(2,1)S(1)}, bf16[64,2176]{1,0:T(8,128)(2,1)S(1)}, u32[]{:S(2)}, u32[]{:S(2)}) %collective-permute-start.4) | collective-permute-done | bytes 278560 | tf_op jit(solution)/shard_map/ppermute | solution.py:31
  31.6 3.8 %collective-permute-done.5 = bf16[64,2176]{1,0:T(8,128)(2,1)S(1)} collective-permute-done((bf16[64,2176]{1,0:T(8,128)(2,1)S(1)}, bf16[64,2176]{1,0:T(8,128)(2,1)S(1)}, u32[]{:S(2)}, u32[]{:S(2)}) %collective-permute-start.5) | collective-permute-done | bytes 278560 | tf_op jit(solution)/shard_map/ppermute | solution.py:31
  35.5 1.6 collective-permute-start.8
  52.1 1.6 collective-permute-start.16
  55.4 5.8 %collective-permute-done.16 = bf16[64,2048]{1,0:T(8,128)(2,1)S(1)} collective-permute-done((bf16[64,2048]{1,0:T(8,128)(2,1)S(1)}, bf16[64,2048]{1,0:T(8,128)(2,1)S(1)}, u32[]{:S(2)}, u32[]{:S(2)}) %collective-permute-start.16) | collective-permute-done | bytes 262176 | tf_op jit(solution)/shard_map/ppermute | solution.py:31
  61.4 2.5 %collective-permute-start.17 = (bf16[64,2048]{1,0:T(8,128)(2,1)S(1)}, bf16[64,2048]{1,0:T(8,128)(2,1)S(1)}, u32[]{:S(2)}, u32[]{:S(2)}) collective-permute-start(bf16[64,2048]{1,0:T(8,128)(2,1)S(1)} %add_convert_fusion.12), channel_id=1, source_target_pairs={{0,12},{1,13},{2,14},{3,15},{4,8},{5,9},{6,10},{7,11},{8,4},{9,5},... | collective-permute-start | bytes 786440 | tf_op jit(solution)/shard_map/ppermute | solution.py:25
  68.5 5.4 %collective-permute-done.25 = bf16[64,2048]{1,0:T(8,128)(2,1)S(1)} collective-permute-done((bf16[64,2048]{1,0:T(8,128)(2,1)S(1)}, bf16[64,2048]{1,0:T(8,128)(2,1)S(1)}, u32[]{:S(2)}, u32[]{:S(2)}) %collective-permute-start.25) | collective-permute-done | bytes 262176 | tf_op jit(solution)/shard_map/ppermute | solution.py:147
  73.9 2.3 %collective-permute-start.18 = (bf16[64,2048]{1,0:T(8,128)(2,1)S(1)}, bf16[64,2048]{1,0:T(8,128)(2,1)S(1)}, u32[]{:S(2)}, u32[]{:S(2)}) collective-permute-start(bf16[64,2048]{1,0:T(8,128)(2,1)S(1)} %add_convert_fusion.11), channel_id=1, source_target_pairs={{0,8},{1,9},{2,10},{3,11},{4,12},{5,13},{6,14},{7,15},{8,0},{9,1},... | collective-permute-start | bytes 786440 | tf_op jit(solution)/shard_map/ppermute | solution.py:25
  76.6 1.7 maximum_select_fusion.1
  80.0 6.4 %collective-permute-done.18 = bf16[64,2048]{1,0:T(8,128)(2,1)S(1)} collective-permute-done((bf16[64,2048]{1,0:T(8,128)(2,1)S(1)}, bf16[64,2048]{1,0:T(8,128)(2,1)S(1)}, u32[]{:S(2)}, u32[]{:S(2)}) %collective-permute-start.18) | collective-permute-done | bytes 262176 | tf_op jit(solution)/shard_map/ppermute | solution.py:25
  90.3 3.9 %collective-permute-done.21 = bf16[64,2048]{1,0:T(8,128)(2,1)} collective-permute-done((bf16[64,2048]{1,0:T(8,128)(2,1)}, bf16[64,2048]{1,0:T(8,128)(2,1)}, u32[]{:S(2)}, u32[]{:S(2)}) %collective-permute-start.21) | collective-permute-done | bytes 262176 | tf_op jit(solution)/shard_map/ppermute | solution.py:25
  96.1 2.5 %collective-permute-start.29 = (bf16[64,1024]{1,0:T(8,128)(2,1)S(1)}, bf16[64,1024]{1,0:T(8,128)(2,1)S(1)}, u32[]{:S(2)}, u32[]{:S(2)}) collective-permute-start(bf16[64,1024]{1,0:T(8,128)(2,1)S(1)} %get-tuple-element.65), channel_id=1, source_target_pairs={{0,12},{1,13},{2,14},{3,15},{4,8},{5,9},{6,10},{7,11},{8,4},{9,5},... | collective-permute-start | bytes 393224 | tf_op jit(solution)/shard_map/ppermute | solution.py:25
  99.0 2.0 collective-permute-start.33
  101.0 3.0 %maximum_select_fusion = bf16[2,2,256,2048]{3,2,1,0:T(8,128)(2,1)S(1)} fusion(bf16[2,1,256,2048]{3,2,1,0:T(8,128)(2,1)S(1)} %maximum_select_fusion.2, bf16[2,1,256,2048]{3,2,1,0:T(8,128)(2,1)} %bitcast.4, pred[]{:T(512)S(6)} %eq.75), kind=kLoop, calls=%fused_computation | loop fusion | flops 6291456 | bytes 8388609 | tf_op jit(solution)/shard_map/jit(_where)/select_n | solution.py:157
  105.3 2.5 %collective-permute-start.30 = (bf16[64,2048]{1,0:T(8,128)(2,1)S(1)}, bf16[64,2048]{1,0:T(8,128)(2,1)S(1)}, u32[]{:S(2)}, u32[]{:S(2)}) collective-permute-start(bf16[64,2048]{1,0:T(8,128)(2,1)S(1)} %convolution_convert_fusion.6), channel_id=1, source_target_pairs={{0,12},{1,13},{2,14},{3,15},{4,8},{5,9},{6,10},{7,11},{8,4},{9,5},... | collective-permute-start | bytes 786440 | tf_op jit(solution)/shard_map/ppermute | solution.py:25
  107.8 10.7 %collective-permute-done.31 = bf16[64,1024]{1,0:T(8,128)(2,1)S(1)} collective-permute-done((bf16[64,1024]{1,0:T(8,128)(2,1)S(1)}, bf16[64,1024]{1,0:T(8,128)(2,1)S(1)}, u32[]{:S(2)}, u32[]{:S(2)}) %collective-permute-start.31) | collective-permute-done | bytes 131104 | tf_op jit(solution)/shard_map/ppermute | solution.py:25
  120.3 3.1 %collective-permute-start.34 = (bf16[64,2048]{1,0:T(8,128)(2,1)S(1)}, bf16[64,2048]{1,0:T(8,128)(2,1)S(1)}, u32[]{:S(2)}, u32[]{:S(2)}) collective-permute-start(bf16[64,2048]{1,0:T(8,128)(2,1)S(1)} %convolution_convert_fusion.4), channel_id=1, source_target_pairs={{0,4},{1,5},{2,6},{3,7},{4,0},{5,1},{6,2},{7,3},{8,12},{9,13},{10,... | collective-permute-start | bytes 786440 | tf_op jit(solution)/shard_map/ppermute | solution.py:25
  123.4 7.9 %collective-permute-done.32 = bf16[64,2048]{1,0:T(8,128)(2,1)S(1)} collective-permute-done((bf16[64,2048]{1,0:T(8,128)(2,1)S(1)}, bf16[64,2048]{1,0:T(8,128)(2,1)S(1)}, u32[]{:S(2)}, u32[]{:S(2)}) %collective-permute-start.32) | collective-permute-done | bytes 262176 | tf_op jit(solution)/shard_map/ppermute | solution.py:25
  132.3 3.2 %fusion.27 = bf16[64,2048]{1,0:T(8,128)(2,1)S(1)} fusion(bf16[64,2048]{1,0:T(8,128)(2,1)S(1)} %get-tuple-element.58, bf16[1024,2048]{1,0:T(8,128)(2,1)} %bitcast.68, bf16[64,2048]{1,0:T(8,128)(2,1)S(1)} %collective-permute-done.34, bf16[64,2048]{1,0:T(8,128)(2,1)S(1)} %collective-permute-done.32, bf16[64,2048]{1,0:T(8,128)(2,1)S(1)} %collective-permute-done.30, ...), kind=kOutput, calls=%fused_computation.68 | convolution fusion | flops 270401536 | bytes 6029316 | tf_op jit(solution)/shard_map/dot_general | solution.py:166
  137.4 2.1 collective-permute-start.38
  139.5 5.3 %collective-permute-done.36 = bf16[64,2048]{1,0:T(8,128)(2,1)S(1)} collective-permute-done((bf16[64,2048]{1,0:T(8,128)(2,1)S(1)}, bf16[64,2048]{1,0:T(8,128)(2,1)S(1)}, u32[]{:S(2)}, u32[]{:S(2)}) %collective-permute-start.36) | collective-permute-done | bytes 262176 | tf_op jit(solution)/shard_map/ppermute | solution.py:25
  146.7 3.8 %collective-permute-done.38 = bf16[64,2048]{1,0:T(8,128)(2,1)S(1)} collective-permute-done((bf16[64,2048]{1,0:T(8,128)(2,1)S(1)}, bf16[64,2048]{1,0:T(8,128)(2,1)S(1)}, u32[]{:S(2)}, u32[]{:S(2)}) %collective-permute-start.38) | collective-permute-done | bytes 262176 | tf_op jit(solution)/shard_map/ppermute | solution.py:25
  150.6 2.8 %collective-permute-done.37 = bf16[64,2048]{1,0:T(8,128)(2,1)S(1)} collective-permute-done((bf16[64,2048]{1,0:T(8,128)(2,1)S(1)}, bf16[64,2048]{1,0:T(8,128)(2,1)S(1)}, u32[]{:S(2)}, u32[]{:S(2)}) %collective-permute-start.37) | collective-permute-done | bytes 262176 | tf_op jit(solution)/shard_map/ppermute | solution.py:31
  153.8 7.3 %collective-permute-done.40 = bf16[64,2048]{1,0:T(8,128)(2,1)S(1)} collective-permute-done((bf16[64,2048]{1,0:T(8,128)(2,1)S(1)}, bf16[64,2048]{1,0:T(8,128)(2,1)S(1)}, u32[]{:S(2)}, u32[]{:S(2)}) %collective-permute-start.40) | collective-permute-done | bytes 262176 | tf_op jit(solution)/shard_map/ppermute | solution.py:25
  162.5 2.9 %fusion.99 = f32[128,1024]{1,0:T(8,128)S(1)} fusion(bf16[128,2048]{1,0:T(8,128)(2,1)S(1)} %pad_maximum_fusion.12, bf16[1,2048,1024]{2,1,0:T(8,128)(2,1)} %param.21), kind=kOutput, calls=%fused_computation.195 | convolution fusion | flops 536870912 | bytes 5242880 | tf_op jit(solution)/shard_map/dot_general | solution.py:82
  165.4 2.1 fusion.69
  167.5 2.9 %fusion.112 = f32[128,1024]{1,0:T(8,128)S(1)} fusion(bf16[128,2048]{1,0:T(8,128)(2,1)S(1)} %pad_maximum_fusion.12, bf16[2048,1024]{1,0:T(8,128)(2,1)} %collective-permute-done.27), kind=kOutput, calls=%fused_computation.208 | convolution fusion | flops 536870912 | bytes 5242880 | tf_op jit(solution)/shard_map/dot_general | solution.py:82
  170.5 2.1 fusion.9
  173.4 3.4 %fusion.97 = f32[256,1024]{1,0:T(8,128)S(1)} fusion(bf16[256,2048]{1,0:T(8,128)(2,1)S(1)} %pad_maximum_fusion.5, bf16[1,2048,1024]{2,1,0:T(8,128)(2,1)} %param.21), kind=kOutput, calls=%fused_computation.193 | convolution fusion | flops 1073741824 | bytes 6291456 | tf_op jit(solution)/shard_map/dot_general | solution.py:82
  176.8 2.4 %fusion.44 = f32[256,2048]{1,0:T(8,128)S(1)} fusion(f32[256,1024]{1,0:T(8,128)S(1)} %fusion.97, f32[256]{0:T(256)S(1)} %bitcast.75, bf16[1,512,2048]{2,1,0:T(8,128)(2,1)} %param.22), kind=kOutput, calls=%fused_computation.102 | convolution fusion | flops 537788416 | bytes 5243904 | tf_op jit(solution)/shard_map/dot_general | solution.py:84
  179.2 3.4 %fusion.113 = f32[256,1024]{1,0:T(8,128)S(1)} fusion(bf16[256,2048]{1,0:T(8,128)(2,1)S(1)} %pad_maximum_fusion.5, bf16[2048,1024]{1,0:T(8,128)(2,1)} %collective-permute-done.27), kind=kOutput, calls=%fused_computation.209 | convolution fusion | flops 1073741824 | bytes 6291456 | tf_op jit(solution)/shard_map/dot_general | solution.py:82
  182.6 2.4 %fusion.8 = bf16[256,2048]{1,0:T(8,128)(2,1)S(1)} fusion(f32[256,2048]{1,0:T(8,128)S(1)} %fusion.44, bf16[512,2048]{1,0:T(8,128)(2,1)} %collective-permute-done.28, f32[256,1024]{1,0:T(8,128)S(1)} %fusion.113, f32[256]{0:T(256)S(1)} %bitcast.76), kind=kOutput, calls=%fused_computation.10 | convolution fusion | flops 538836992 | bytes 6292480 | tf_op jit(solution)/shard_map/dot_general | solution.py:84
  185.2 2.9 %fusion.95 = f32[128,1024]{1,0:T(8,128)S(1)} fusion(bf16[128,2048]{1,0:T(8,128)(2,1)S(1)} %pad_maximum_fusion.13, bf16[1,2048,1024]{2,1,0:T(8,128)(2,1)} %param.21), kind=kOutput, calls=%fused_computation.191 | convolution fusion | flops 536870912 | bytes 5242880 | tf_op jit(solution)/shard_map/dot_general | solution.py:82
  188.1 2.1 fusion.72
  190.2 2.9 %fusion.114 = f32[128,1024]{1,0:T(8,128)S(1)} fusion(bf16[128,2048]{1,0:T(8,128)(2,1)S(1)} %pad_maximum_fusion.13, bf16[2048,1024]{1,0:T(8,128)(2,1)} %collective-permute-done.27), kind=kOutput, calls=%fused_computation.210 | convolution fusion | flops 536870912 | bytes 5242880 | tf_op jit(solution)/shard_map/dot_general | solution.py:82
  193.2 2.1 fusion.10
  196.9 2.4 %collective-permute-start.45 = (bf16[64,2048]{1,0:T(8,128)(2,1)S(1)}, bf16[64,2048]{1,0:T(8,128)(2,1)S(1)}, u32[]{:S(2)}, u32[]{:S(2)}) collective-permute-start(bf16[64,2048]{1,0:T(8,128)(2,1)S(1)} %add_convert_fusion.7), channel_id=1, source_target_pairs={{0,12},{1,13},{2,14},{3,15},{4,8},{5,9},{6,10},{7,11},{8,4},{9,5},... | collective-permute-start | bytes 786440 | tf_op jit(solution)/shard_map/ppermute | solution.py:25
  200.0 4.3 %collective-permute-done.42 = bf16[64,2048]{1,0:T(8,128)(2,1)S(1)} collective-permute-done((bf16[64,2048]{1,0:T(8,128)(2,1)S(1)}, bf16[64,2048]{1,0:T(8,128)(2,1)S(1)}, u32[]{:S(2)}, u32[]{:S(2)}) %collective-permute-start.42) | collective-permute-done | bytes 262176 | tf_op jit(solution)/shard_map/ppermute | solution.py:31
  204.4 4.8 %collective-permute-start.46 = (bf16[64,2048]{1,0:T(8,128)(2,1)S(1)}, bf16[64,2048]{1,0:T(8,128)(2,1)S(1)}, u32[]{:S(2)}, u32[]{:S(2)}) collective-permute-start(bf16[64,2048]{1,0:T(8,128)(2,1)S(1)} %add_convert_fusion.6), channel_id=1, source_target_pairs={{0,8},{1,9},{2,10},{3,11},{4,12},{5,13},{6,14},{7,15},{8,0},{9,1},... | collective-permute-start | bytes 786440 | tf_op jit(solution)/shard_map/ppermute | solution.py:25
  209.3 4.3 %collective-permute-start.48 = (bf16[64,2048]{1,0:T(8,128)(2,1)S(1)}, bf16[64,2048]{1,0:T(8,128)(2,1)S(1)}, u32[]{:S(2)}, u32[]{:S(2)}) collective-permute-start(bf16[64,2048]{1,0:T(8,128)(2,1)S(1)} %add_convert_fusion.5), channel_id=1, source_target_pairs={{0,4},{1,5},{2,6},{3,7},{4,0},{5,1},{6,2},{7,3},{8,12},{9,13},{10,... | collective-permute-start | bytes 786440 | tf_op jit(solution)/shard_map/ppermute | solution.py:25
  214.7 3.8 %collective-permute-done.46 = bf16[64,2048]{1,0:T(8,128)(2,1)S(1)} collective-permute-done((bf16[64,2048]{1,0:T(8,128)(2,1)S(1)}, bf16[64,2048]{1,0:T(8,128)(2,1)S(1)}, u32[]{:S(2)}, u32[]{:S(2)}) %collective-permute-start.46) | collective-permute-done | bytes 262176 | tf_op jit(solution)/shard_map/ppermute | solution.py:25
  218.5 2.5 %collective-permute-done.48 = bf16[64,2048]{1,0:T(8,128)(2,1)S(1)} collective-permute-done((bf16[64,2048]{1,0:T(8,128)(2,1)S(1)}, bf16[64,2048]{1,0:T(8,128)(2,1)S(1)}, u32[]{:S(2)}, u32[]{:S(2)}) %collective-permute-start.48) | collective-permute-done | bytes 262176 | tf_op jit(solution)/shard_map/ppermute | solution.py:25
  (173 shorter events, 54.9 us)
Async XLA Ops:
  3.4 10.7 %collective-permute-start.3 = (bf16[64,2176]{1,0:T(8,128)(2,1)S(1)}, bf16[64,2176]{1,0:T(8,128)(2,1)S(1)}, u32[]{:S(2)}, u32[]{:S(2)}) collective-permute-start(bf16[64,2176]{1,0:T(8,128)(2,1)S(1)} %pad_maximum_fusion.14), channel_id=1, source_target_pairs={{0,4},{1,5},{2,6},{3,7},{4,0},{5,1},{6,2},{7,3},{8,12},{9,13},{10,... | collective-permute-start | bytes 835592 | tf_op jit(solution)/shard_map/ppermute | solution.py:25
  6.5 16.1 %collective-permute-start.2 = (bf16[64,2176]{1,0:T(8,128)(2,1)S(1)}, bf16[64,2176]{1,0:T(8,128)(2,1)S(1)}, u32[]{:S(2)}, u32[]{:S(2)}) collective-permute-start(bf16[64,2176]{1,0:T(8,128)(2,1)S(1)} %pad_maximum_fusion.14), channel_id=1, source_target_pairs={{0,12},{1,13},{2,14},{3,15},{4,8},{5,9},{6,10},{7,11},{8,4},{9,5},... | collective-permute-start | bytes 835592 | tf_op jit(solution)/shard_map/ppermute | solution.py:25
  9.0 26.5 %collective-permute-start.7 = (bf16[64,2176]{1,0:T(8,128)(2,1)S(1)}, bf16[64,2176]{1,0:T(8,128)(2,1)S(1)}, u32[]{:S(2)}, u32[]{:S(2)}) collective-permute-start(bf16[64,2176]{1,0:T(8,128)(2,1)S(1)} %pad_maximum_fusion.14), channel_id=1, source_target_pairs={{0,8},{1,9},{2,10},{3,11},{4,12},{5,13},{6,14},{7,15},{8,0},{9,1},... | collective-permute-start | bytes 835592 | tf_op jit(solution)/shard_map/ppermute | solution.py:25
  9.1 9.7 %collective-permute-start = (bf16[64,2176]{1,0:T(8,128)(2,1)S(1)}, bf16[64,2176]{1,0:T(8,128)(2,1)}, u32[]{:S(2)}, u32[]{:S(2)}) collective-permute-start(bf16[64,2176]{1,0:T(8,128)(2,1)S(1)} %pad_maximum_fusion.14), channel_id=1, source_target_pairs={{0,2},{1,3},{2,0},{3,1},{4,6},{5,7},{6,4},{7,5},{8,10},{9,11},{10,... | collective-permute-start | bytes 835592 | tf_op jit(solution)/shard_map/ppermute | solution.py:31
  12.5 17.6 %collective-permute-start.22 = (bf16[64,2048]{1,0:T(8,128)(2,1)}, bf16[64,2048]{1,0:T(8,128)(2,1)}, u32[]{:S(2)}, u32[]{:S(2)}) collective-permute-start(bf16[64,2048]{1,0:T(8,128)(2,1)} %get-tuple-element.63), channel_id=1, source_target_pairs={{0,2},{1,3},{2,0},{3,1},{4,6},{5,7},{6,4},{7,5},{8,10},{9,11},{10,... | collective-permute-start | bytes 786440 | tf_op jit(solution)/shard_map/ppermute | solution.py:31
  14.1 14.4 %collective-permute-start.4 = (bf16[64,2176]{1,0:T(8,128)(2,1)S(1)}, bf16[64,2176]{1,0:T(8,128)(2,1)S(1)}, u32[]{:S(2)}, u32[]{:S(2)}) collective-permute-start(bf16[64,2176]{1,0:T(8,128)(2,1)S(1)} %collective-permute-done.3), channel_id=1, source_target_pairs={{0,2},{1,3},{2,0},{3,1},{4,6},{5,7},{6,4},{7,5},{8,10},{9,11},{10,... | collective-permute-start | bytes 835592 | tf_op jit(solution)/shard_map/ppermute | solution.py:31
  19.8 17.3 %collective-permute-start.1 = (bf16[128,2176]{1,0:T(8,128)(2,1)S(1)}, bf16[128,2176]{1,0:T(8,128)(2,1)S(1)}, u32[]{:S(2)}, u32[]{:S(2)}) collective-permute-start(bf16[128,2176]{1,0:T(8,128)(2,1)S(1)} %pad_maximum_fusion.6), channel_id=1, source_target_pairs={{0,1},{1,0},{2,3},{3,2},{4,5},{5,4},{6,7},{7,6},{8,9},{9,8},{10,11... | collective-permute-start | bytes 1671176 | tf_op jit(solution)/shard_map/ppermute | solution.py:31
  28.5 6.9 %collective-permute-start.5 = (bf16[64,2176]{1,0:T(8,128)(2,1)S(1)}, bf16[64,2176]{1,0:T(8,128)(2,1)S(1)}, u32[]{:S(2)}, u32[]{:S(2)}) collective-permute-start(bf16[64,2176]{1,0:T(8,128)(2,1)S(1)} %collective-permute-done.2), channel_id=1, source_target_pairs={{0,2},{1,3},{2,0},{3,1},{4,6},{5,7},{6,4},{7,5},{8,10},{9,11},{10,... | collective-permute-start | bytes 835592 | tf_op jit(solution)/shard_map/ppermute | solution.py:31
  30.1 15.0 %collective-permute-start.23 = (bf16[64,2048]{1,0:T(8,128)(2,1)}, bf16[64,2048]{1,0:T(8,128)(2,1)S(1)}, u32[]{:S(2)}, u32[]{:S(2)}) collective-permute-start(bf16[64,2048]{1,0:T(8,128)(2,1)} %collective-permute-done.22), channel_id=1, source_target_pairs={{0,16},{16,0},{1,17},{17,1},{2,18},{18,2},{3,19},{19,3},{4,20},{20... | collective-permute-start | bytes 786440 | tf_op jit(solution)/shard_map/ppermute | solution.py:147
  31.6 7.9 %collective-permute-start.10 = (bf16[128,2176]{1,0:T(8,128)(2,1)S(1)}, bf16[128,2176]{1,0:T(8,128)(2,1)S(1)}, u32[]{:S(2)}, u32[]{:S(2)}) collective-permute-start(bf16[128,2176]{1,0:T(8,128)(2,1)S(1)} %pad_maximum_fusion.9), channel_id=1, source_target_pairs={{0,1},{1,0},{2,3},{3,2},{4,5},{5,4},{6,7},{7,6},{8,9},{9,8},{10,11... | collective-permute-start | bytes 1671176 | tf_op jit(solution)/shard_map/ppermute | solution.py:31
  35.5 9.4 %collective-permute-start.8 = (bf16[64,2176]{1,0:T(8,128)(2,1)S(1)}, bf16[64,2176]{1,0:T(8,128)(2,1)S(1)}, u32[]{:S(2)}, u32[]{:S(2)}) collective-permute-start(bf16[64,2176]{1,0:T(8,128)(2,1)S(1)} %collective-permute-done.7), channel_id=1, source_target_pairs={{0,2},{1,3},{2,0},{3,1},{4,6},{5,7},{6,4},{7,5},{8,10},{9,11},{10,... | collective-permute-start | bytes 835592 | tf_op jit(solution)/shard_map/ppermute | solution.py:31
  37.2 4.8 %collective-permute-start.9 = (bf16[128,2176]{1,0:T(8,128)(2,1)S(1)}, bf16[128,2176]{1,0:T(8,128)(2,1)S(1)}, u32[]{:S(2)}, u32[]{:S(2)}) collective-permute-start(bf16[128,2176]{1,0:T(8,128)(2,1)S(1)} %pad_maximum_fusion.8), channel_id=1, source_target_pairs={{0,1},{1,0},{2,3},{3,2},{4,5},{5,4},{6,7},{7,6},{8,9},{9,8},{10,11... | collective-permute-start | bytes 1671176 | tf_op jit(solution)/shard_map/ppermute | solution.py:31
  45.0 3.0 %collective-permute-start.11 = (bf16[128,2176]{1,0:T(8,128)(2,1)S(1)}, bf16[128,2176]{1,0:T(8,128)(2,1)S(1)}, u32[]{:S(2)}, u32[]{:S(2)}) collective-permute-start(bf16[128,2176]{1,0:T(8,128)(2,1)S(1)} %pad_maximum_fusion.7), channel_id=1, source_target_pairs={{0,1},{1,0},{2,3},{3,2},{4,5},{5,4},{6,7},{7,6},{8,9},{9,8},{10,11... | collective-permute-start | bytes 1671176 | tf_op jit(solution)/shard_map/ppermute | solution.py:31
  46.1 4.4 %collective-permute-start.6 = (bf16[128,2048]{1,0:T(8,128)(2,1)S(1)}, bf16[128,2048]{1,0:T(8,128)(2,1)S(1)}, u32[]{:S(2)}, u32[]{:S(2)}) collective-permute-start(bf16[128,2048]{1,0:T(8,128)(2,1)S(1)} %slice.397), channel_id=1, source_target_pairs={{0,1},{1,0},{2,3},{3,2},{4,5},{5,4},{6,7},{7,6},{8,9},{9,8},{10,11... | collective-permute-start | bytes 1572872 | tf_op jit(solution)/shard_map/ppermute | solution.py:31
  46.7 17.1 %collective-permute-start.24 = (bf16[64,2048]{1,0:T(8,128)(2,1)S(1)}, bf16[64,2048]{1,0:T(8,128)(2,1)S(1)}, u32[]{:S(2)}, u32[]{:S(2)}) collective-permute-start(bf16[64,2048]{1,0:T(8,128)(2,1)S(1)} %copy-done.10), channel_id=1, source_target_pairs={{0,2},{1,3},{2,0},{3,1},{4,6},{5,7},{6,4},{7,5},{8,10},{9,11},{10,... | collective-permute-start | bytes 786440 | tf_op jit(solution)/shard_map/ppermute | solution.py:31
  47.3 4.6 %collective-permute-start.19 = (bf16[128,2048]{1,0:T(8,128)(2,1)S(1)}, bf16[128,2048]{1,0:T(8,128)(2,1)S(1)}, u32[]{:S(2)}, u32[]{:S(2)}) collective-permute-start(bf16[128,2048]{1,0:T(8,128)(2,1)S(1)} %slice.415), channel_id=1, source_target_pairs={{0,1},{1,0},{2,3},{3,2},{4,5},{5,4},{6,7},{7,6},{8,9},{9,8},{10,11... | collective-permute-start | bytes 1572872 | tf_op jit(solution)/shard_map/ppermute | solution.py:31
  47.3 56.8 %collective-permute-start.28 = (bf16[512,2048]{1,0:T(8,128)(2,1)}, bf16[512,2048]{1,0:T(8,128)(2,1)}, u32[]{:S(2)}, u32[]{:S(2)}) collective-permute-start(bf16[512,2048]{1,0:T(8,128)(2,1)} %bitcast.9), channel_id=1, source_target_pairs={{0,1},{1,0},{2,3},{3,2},{4,5},{5,4},{6,7},{7,6},{8,9},{9,8},{10,11... | collective-permute-start | bytes 6291464 | tf_op jit(solution)/shard_map/ppermute | solution.py:31
  47.9 56.1 %collective-permute-start.27 = (bf16[2048,1024]{1,0:T(8,128)(2,1)}, bf16[2048,1024]{1,0:T(8,128)(2,1)}, u32[]{:S(2)}, u32[]{:S(2)}) collective-permute-start(bf16[2048,1024]{1,0:T(8,128)(2,1)} %bitcast.8), channel_id=1, source_target_pairs={{0,1},{1,0},{2,3},{3,2},{4,5},{5,4},{6,7},{7,6},{8,9},{9,8},{10,11... | collective-permute-start | bytes 12582920 | tf_op jit(solution)/shard_map/ppermute | solution.py:31
  50.5 3.2 %collective-permute-start.13 = (bf16[128,2048]{1,0:T(8,128)(2,1)S(1)}, bf16[128,2048]{1,0:T(8,128)(2,1)S(1)}, u32[]{:S(2)}, u32[]{:S(2)}) collective-permute-start(bf16[128,2048]{1,0:T(8,128)(2,1)S(1)} %slice.409), channel_id=1, source_target_pairs={{0,1},{1,0},{2,3},{3,2},{4,5},{5,4},{6,7},{7,6},{8,9},{9,8},{10,11... | collective-permute-start | bytes 1572872 | tf_op jit(solution)/shard_map/ppermute | solution.py:31
  52.1 9.2 %collective-permute-start.16 = (bf16[64,2048]{1,0:T(8,128)(2,1)S(1)}, bf16[64,2048]{1,0:T(8,128)(2,1)S(1)}, u32[]{:S(2)}, u32[]{:S(2)}) collective-permute-start(bf16[64,2048]{1,0:T(8,128)(2,1)S(1)} %slice.412), channel_id=1, source_target_pairs={{0,2},{1,3},{2,0},{3,1},{4,6},{5,7},{6,4},{7,5},{8,10},{9,11},{10,... | collective-permute-start | bytes 786440 | tf_op jit(solution)/shard_map/ppermute | solution.py:31
  53.9 13.1 %collective-permute-start.14 = (bf16[64,2048]{1,0:T(8,128)(2,1)S(1)}, bf16[64,2048]{1,0:T(8,128)(2,1)S(1)}, u32[]{:S(2)}, u32[]{:S(2)}) collective-permute-start(bf16[64,2048]{1,0:T(8,128)(2,1)S(1)} %slice.410), channel_id=1, source_target_pairs={{0,2},{1,3},{2,0},{3,1},{4,6},{5,7},{6,4},{7,5},{8,10},{9,11},{10,... | collective-permute-start | bytes 786440 | tf_op jit(solution)/shard_map/ppermute | solution.py:31
  61.4 17.7 %collective-permute-start.17 = (bf16[64,2048]{1,0:T(8,128)(2,1)S(1)}, bf16[64,2048]{1,0:T(8,128)(2,1)S(1)}, u32[]{:S(2)}, u32[]{:S(2)}) collective-permute-start(bf16[64,2048]{1,0:T(8,128)(2,1)S(1)} %add_convert_fusion.12), channel_id=1, source_target_pairs={{0,12},{1,13},{2,14},{3,15},{4,8},{5,9},{6,10},{7,11},{8,4},{9,5},... | collective-permute-start | bytes 786440 | tf_op jit(solution)/shard_map/ppermute | solution.py:25
  63.9 14.4 %collective-permute-start.20 = (bf16[64,2048]{1,0:T(8,128)(2,1)S(1)}, bf16[64,2048]{1,0:T(8,128)(2,1)S(1)}, u32[]{:S(2)}, u32[]{:S(2)}) collective-permute-start(bf16[64,2048]{1,0:T(8,128)(2,1)S(1)} %slice.417), channel_id=1, source_target_pairs={{0,2},{1,3},{2,0},{3,1},{4,6},{5,7},{6,4},{7,5},{8,10},{9,11},{10,... | collective-permute-start | bytes 786440 | tf_op jit(solution)/shard_map/ppermute | solution.py:31
  66.9 7.0 %collective-permute-start.25 = (bf16[64,2048]{1,0:T(8,128)(2,1)S(1)}, bf16[64,2048]{1,0:T(8,128)(2,1)S(1)}, u32[]{:S(2)}, u32[]{:S(2)}) collective-permute-start(bf16[64,2048]{1,0:T(8,128)(2,1)S(1)} %collective-permute-done.24), channel_id=1, source_target_pairs={{0,16},{16,0},{1,17},{17,1},{2,18},{18,2},{3,19},{19,3},{4,20},{20... | collective-permute-start | bytes 786440 | tf_op jit(solution)/shard_map/ppermute | solution.py:147
  73.9 12.6 %collective-permute-start.18 = (bf16[64,2048]{1,0:T(8,128)(2,1)S(1)}, bf16[64,2048]{1,0:T(8,128)(2,1)S(1)}, u32[]{:S(2)}, u32[]{:S(2)}) collective-permute-start(bf16[64,2048]{1,0:T(8,128)(2,1)S(1)} %add_convert_fusion.11), channel_id=1, source_target_pairs={{0,8},{1,9},{2,10},{3,11},{4,12},{5,13},{6,14},{7,15},{8,0},{9,1},... | collective-permute-start | bytes 786440 | tf_op jit(solution)/shard_map/ppermute | solution.py:25
  78.3 20.7 %collective-permute-start.26 = (bf16[2,256,2048]{2,1,0:T(8,128)(2,1)}, bf16[2,256,2048]{2,1,0:T(8,128)(2,1)}, u32[]{:S(2)}, u32[]{:S(2)}) collective-permute-start(bf16[2,256,2048]{2,1,0:T(8,128)(2,1)} %maximum_select_fusion.1), channel_id=1, source_target_pairs={{0,1},{1,0},{2,3},{3,2},{4,5},{5,4},{6,7},{7,6},{8,9},{9,8},{10,11... | collective-permute-start | bytes 6291464 | tf_op jit(solution)/shard_map/ppermute | solution.py:31
  79.1 10.5 %collective-permute-start.15 = (bf16[64,2048]{1,0:T(8,128)(2,1)}, bf16[64,2048]{1,0:T(8,128)(2,1)S(1)}, u32[]{:S(2)}, u32[]{:S(2)}) collective-permute-start(bf16[64,2048]{1,0:T(8,128)(2,1)} %slice.399), channel_id=1, source_target_pairs={{0,2},{1,3},{2,0},{3,1},{4,6},{5,7},{6,4},{7,5},{8,10},{9,11},{10,... | collective-permute-start | bytes 786440 | tf_op jit(solution)/shard_map/ppermute | solution.py:31
  86.5 7.7 %collective-permute-start.21 = (bf16[64,2048]{1,0:T(8,128)(2,1)}, bf16[64,2048]{1,0:T(8,128)(2,1)}, u32[]{:S(2)}, u32[]{:S(2)}) collective-permute-start(bf16[64,2048]{1,0:T(8,128)(2,1)} %add_convert_fusion.10), channel_id=1, source_target_pairs={{0,4},{1,5},{2,6},{3,7},{4,0},{5,1},{6,2},{7,3},{8,12},{9,13},{10,... | collective-permute-start | bytes 786440 | tf_op jit(solution)/shard_map/ppermute | solution.py:25
  96.1 8.3 %collective-permute-start.29 = (bf16[64,1024]{1,0:T(8,128)(2,1)S(1)}, bf16[64,1024]{1,0:T(8,128)(2,1)S(1)}, u32[]{:S(2)}, u32[]{:S(2)}) collective-permute-start(bf16[64,1024]{1,0:T(8,128)(2,1)S(1)} %get-tuple-element.65), channel_id=1, source_target_pairs={{0,12},{1,13},{2,14},{3,15},{4,8},{5,9},{6,10},{7,11},{8,4},{9,5},... | collective-permute-start | bytes 393224 | tf_op jit(solution)/shard_map/ppermute | solution.py:25
  98.6 19.8 %collective-permute-start.31 = (bf16[64,1024]{1,0:T(8,128)(2,1)S(1)}, bf16[64,1024]{1,0:T(8,128)(2,1)S(1)}, u32[]{:S(2)}, u32[]{:S(2)}) collective-permute-start(bf16[64,1024]{1,0:T(8,128)(2,1)S(1)} %get-tuple-element.66), channel_id=1, source_target_pairs={{0,8},{1,9},{2,10},{3,11},{4,12},{5,13},{6,14},{7,15},{8,0},{9,1},... | collective-permute-start | bytes 393224 | tf_op jit(solution)/shard_map/ppermute | solution.py:25
  99.0 20.4 %collective-permute-start.33 = (bf16[64,1024]{1,0:T(8,128)(2,1)S(1)}, bf16[64,1024]{1,0:T(8,128)(2,1)S(1)}, u32[]{:S(2)}, u32[]{:S(2)}) collective-permute-start(bf16[64,1024]{1,0:T(8,128)(2,1)S(1)} %get-tuple-element.67), channel_id=1, source_target_pairs={{0,4},{1,5},{2,6},{3,7},{4,0},{5,1},{6,2},{7,3},{8,12},{9,13},{10,... | collective-permute-start | bytes 393224 | tf_op jit(solution)/shard_map/ppermute | solution.py:25
  105.3 18.1 %collective-permute-start.30 = (bf16[64,2048]{1,0:T(8,128)(2,1)S(1)}, bf16[64,2048]{1,0:T(8,128)(2,1)S(1)}, u32[]{:S(2)}, u32[]{:S(2)}) collective-permute-start(bf16[64,2048]{1,0:T(8,128)(2,1)S(1)} %convolution_convert_fusion.6), channel_id=1, source_target_pairs={{0,12},{1,13},{2,14},{3,15},{4,8},{5,9},{6,10},{7,11},{8,4},{9,5},... | collective-permute-start | bytes 786440 | tf_op jit(solution)/shard_map/ppermute | solution.py:25
  119.3 12.0 %collective-permute-start.32 = (bf16[64,2048]{1,0:T(8,128)(2,1)S(1)}, bf16[64,2048]{1,0:T(8,128)(2,1)S(1)}, u32[]{:S(2)}, u32[]{:S(2)}) collective-permute-start(bf16[64,2048]{1,0:T(8,128)(2,1)S(1)} %convolution_convert_fusion.5), channel_id=1, source_target_pairs={{0,8},{1,9},{2,10},{3,11},{4,12},{5,13},{6,14},{7,15},{8,0},{9,1},... | collective-permute-start | bytes 786440 | tf_op jit(solution)/shard_map/ppermute | solution.py:25
  120.3 12.0 %collective-permute-start.34 = (bf16[64,2048]{1,0:T(8,128)(2,1)S(1)}, bf16[64,2048]{1,0:T(8,128)(2,1)S(1)}, u32[]{:S(2)}, u32[]{:S(2)}) collective-permute-start(bf16[64,2048]{1,0:T(8,128)(2,1)S(1)} %convolution_convert_fusion.4), channel_id=1, source_target_pairs={{0,4},{1,5},{2,6},{3,7},{4,0},{5,1},{6,2},{7,3},{8,12},{9,13},{10,... | collective-permute-start | bytes 786440 | tf_op jit(solution)/shard_map/ppermute | solution.py:25
  135.5 9.3 %collective-permute-start.36 = (bf16[64,2048]{1,0:T(8,128)(2,1)S(1)}, bf16[64,2048]{1,0:T(8,128)(2,1)S(1)}, u32[]{:S(2)}, u32[]{:S(2)}) collective-permute-start(bf16[64,2048]{1,0:T(8,128)(2,1)S(1)} %fusion.27), channel_id=1, source_target_pairs={{0,4},{1,5},{2,6},{3,7},{4,0},{5,1},{6,2},{7,3},{8,12},{9,13},{10,... | collective-permute-start | bytes 786440 | tf_op jit(solution)/shard_map/ppermute | solution.py:25
  135.6 11.1 %collective-permute-start.35 = (bf16[64,2048]{1,0:T(8,128)(2,1)S(1)}, bf16[64,2048]{1,0:T(8,128)(2,1)S(1)}, u32[]{:S(2)}, u32[]{:S(2)}) collective-permute-start(bf16[64,2048]{1,0:T(8,128)(2,1)S(1)} %fusion.27), channel_id=1, source_target_pairs={{0,2},{1,3},{2,0},{3,1},{4,6},{5,7},{6,4},{7,5},{8,10},{9,11},{10,... | collective-permute-start | bytes 786440 | tf_op jit(solution)/shard_map/ppermute | solution.py:31
  137.4 13.1 %collective-permute-start.38 = (bf16[64,2048]{1,0:T(8,128)(2,1)S(1)}, bf16[64,2048]{1,0:T(8,128)(2,1)S(1)}, u32[]{:S(2)}, u32[]{:S(2)}) collective-permute-start(bf16[64,2048]{1,0:T(8,128)(2,1)S(1)} %fusion.27), channel_id=1, source_target_pairs={{0,12},{1,13},{2,14},{3,15},{4,8},{5,9},{6,10},{7,11},{8,4},{9,5},... | collective-permute-start | bytes 786440 | tf_op jit(solution)/shard_map/ppermute | solution.py:25
  144.9 8.5 %collective-permute-start.37 = (bf16[64,2048]{1,0:T(8,128)(2,1)S(1)}, bf16[64,2048]{1,0:T(8,128)(2,1)S(1)}, u32[]{:S(2)}, u32[]{:S(2)}) collective-permute-start(bf16[64,2048]{1,0:T(8,128)(2,1)S(1)} %collective-permute-done.36), channel_id=1, source_target_pairs={{0,2},{1,3},{2,0},{3,1},{4,6},{5,7},{6,4},{7,5},{8,10},{9,11},{10,... | collective-permute-start | bytes 786440 | tf_op jit(solution)/shard_map/ppermute | solution.py:31
  145.9 15.1 %collective-permute-start.40 = (bf16[64,2048]{1,0:T(8,128)(2,1)S(1)}, bf16[64,2048]{1,0:T(8,128)(2,1)S(1)}, u32[]{:S(2)}, u32[]{:S(2)}) collective-permute-start(bf16[64,2048]{1,0:T(8,128)(2,1)S(1)} %fusion.27), channel_id=1, source_target_pairs={{0,8},{1,9},{2,10},{3,11},{4,12},{5,13},{6,14},{7,15},{8,0},{9,1},... | collective-permute-start | bytes 786440 | tf_op jit(solution)/shard_map/ppermute | solution.py:25
  153.3 7.7 %collective-permute-start.39 = (bf16[64,2048]{1,0:T(8,128)(2,1)S(1)}, bf16[64,2048]{1,0:T(8,128)(2,1)S(1)}, u32[]{:S(2)}, u32[]{:S(2)}) collective-permute-start(bf16[64,2048]{1,0:T(8,128)(2,1)S(1)} %collective-permute-done.38), channel_id=1, source_target_pairs={{0,2},{1,3},{2,0},{3,1},{4,6},{5,7},{6,4},{7,5},{8,10},{9,11},{10,... | collective-permute-start | bytes 786440 | tf_op jit(solution)/shard_map/ppermute | solution.py:31
  161.1 24.0 %collective-permute-start.41 = (bf16[64,2048]{1,0:T(8,128)(2,1)S(1)}, bf16[64,2048]{1,0:T(8,128)(2,1)S(1)}, u32[]{:S(2)}, u32[]{:S(2)}) collective-permute-start(bf16[64,2048]{1,0:T(8,128)(2,1)S(1)} %collective-permute-done.40), channel_id=1, source_target_pairs={{0,2},{1,3},{2,0},{3,1},{4,6},{5,7},{6,4},{7,5},{8,10},{9,11},{10,... | collective-permute-start | bytes 786440 | tf_op jit(solution)/shard_map/ppermute | solution.py:31
  172.6 24.2 %collective-permute-start.44 = (bf16[64,2048]{1,0:T(8,128)(2,1)S(1)}, bf16[64,2048]{1,0:T(8,128)(2,1)S(1)}, u32[]{:S(2)}, u32[]{:S(2)}) collective-permute-start(bf16[64,2048]{1,0:T(8,128)(2,1)S(1)} %slice.434), channel_id=1, source_target_pairs={{0,2},{1,3},{2,0},{3,1},{4,6},{5,7},{6,4},{7,5},{8,10},{9,11},{10,... | collective-permute-start | bytes 786440 | tf_op jit(solution)/shard_map/ppermute | solution.py:31
  195.4 8.9 %collective-permute-start.42 = (bf16[64,2048]{1,0:T(8,128)(2,1)S(1)}, bf16[64,2048]{1,0:T(8,128)(2,1)S(1)}, u32[]{:S(2)}, u32[]{:S(2)}) collective-permute-start(bf16[64,2048]{1,0:T(8,128)(2,1)S(1)} %slice.432), channel_id=1, source_target_pairs={{0,2},{1,3},{2,0},{3,1},{4,6},{5,7},{6,4},{7,5},{8,10},{9,11},{10,... | collective-permute-start | bytes 786440 | tf_op jit(solution)/shard_map/ppermute | solution.py:31
  196.9 17.8 %collective-permute-start.45 = (bf16[64,2048]{1,0:T(8,128)(2,1)S(1)}, bf16[64,2048]{1,0:T(8,128)(2,1)S(1)}, u32[]{:S(2)}, u32[]{:S(2)}) collective-permute-start(bf16[64,2048]{1,0:T(8,128)(2,1)S(1)} %add_convert_fusion.7), channel_id=1, source_target_pairs={{0,12},{1,13},{2,14},{3,15},{4,8},{5,9},{6,10},{7,11},{8,4},{9,5},... | collective-permute-start | bytes 786440 | tf_op jit(solution)/shard_map/ppermute | solution.py:25
  199.3 9.9 %collective-permute-start.47 = (bf16[64,2048]{1,0:T(8,128)(2,1)S(1)}, bf16[64,2048]{1,0:T(8,128)(2,1)S(1)}, u32[]{:S(2)}, u32[]{:S(2)}) collective-permute-start(bf16[64,2048]{1,0:T(8,128)(2,1)S(1)} %get-tuple-element.48), channel_id=1, source_target_pairs={{0,2},{1,3},{2,0},{3,1},{4,6},{5,7},{6,4},{7,5},{8,10},{9,11},{10,... | collective-permute-start | bytes 786440 | tf_op jit(solution)/shard_map/ppermute | solution.py:31
  204.4 14.1 %collective-permute-start.46 = (bf16[64,2048]{1,0:T(8,128)(2,1)S(1)}, bf16[64,2048]{1,0:T(8,128)(2,1)S(1)}, u32[]{:S(2)}, u32[]{:S(2)}) collective-permute-start(bf16[64,2048]{1,0:T(8,128)(2,1)S(1)} %add_convert_fusion.6), channel_id=1, source_target_pairs={{0,8},{1,9},{2,10},{3,11},{4,12},{5,13},{6,14},{7,15},{8,0},{9,1},... | collective-permute-start | bytes 786440 | tf_op jit(solution)/shard_map/ppermute | solution.py:25
  209.3 11.7 %collective-permute-start.48 = (bf16[64,2048]{1,0:T(8,128)(2,1)S(1)}, bf16[64,2048]{1,0:T(8,128)(2,1)S(1)}, u32[]{:S(2)}, u32[]{:S(2)}) collective-permute-start(bf16[64,2048]{1,0:T(8,128)(2,1)S(1)} %add_convert_fusion.5), channel_id=1, source_target_pairs={{0,4},{1,5},{2,6},{3,7},{4,0},{5,1},{6,2},{7,3},{8,12},{9,13},{10,... | collective-permute-start | bytes 786440 | tf_op jit(solution)/shard_map/ppermute | solution.py:25
  213.6 7.4 %collective-permute-start.43 = (bf16[64,2048]{1,0:T(8,128)(2,1)S(1)}, bf16[64,2048]{1,0:T(8,128)(2,1)S(1)}, u32[]{:S(2)}, u32[]{:S(2)}) collective-permute-start(bf16[64,2048]{1,0:T(8,128)(2,1)S(1)} %get-tuple-element.47), channel_id=1, source_target_pairs={{0,2},{1,3},{2,0},{3,1},{4,6},{5,7},{6,4},{7,5},{8,10},{9,11},{10,... | collective-permute-start | bytes 786440 | tf_op jit(solution)/shard_map/ppermute | solution.py:31
  (18 other events, 183.1 us)

commit v14 on v13

--- a/solution.py
+++ b/solution.py
@@ -210,9 +210,9 @@
     weight = plane_weight(ring, merge_weight, other_half(ring, merge_weight, lax.axis_size("groups"), ties))
     after_first = (hidden_rows.astype(jnp.float32) + first).astype(jnp.bfloat16)
     merged_in = jnp.concatenate([normed(after_first, hidden_gain), normed(token_embed, embed_gain)], axis=1)
-    merged = merge(ring, merged_in, after(weight, *second_pair[1], *[g for slot in range(PLANES) for g in second_gates[slot]]))
+    merged = merge(ring, merged_in, after(weight, *[g for slot in range(PLANES) for g in second_gates[slot]]))
     after_merge = (after_first.astype(jnp.float32) + jax.nn.silu(merged)).astype(jnp.bfloat16)
-    second, _ = routed(ring, after_merge, second_work, True)
+    second, _ = routed(ring, after(after_merge, *second_pair[1]), second_work, True)
     return (after_merge.astype(jnp.float32) + second).astype(jnp.bfloat16)
 
 

time: 223 us -> 208 us (0.933)
  waiting for transfers between devices: 88.5 us -> 76.6 us
  matrix products: 45.9 us -> 34.2 us
  starting transfers between devices: 60.1 us -> 67.4 us
  other arithmetic: 22.1 us -> 24.8 us
    dot_general x10, matrix products: 16.6 us -> 7.07 us  [experts(): jnp.dot(hidden.astype(jnp.bfloat16), down, preferred_element_type=jnp.flo...]
    ppermute x18, waiting for transfers between devices: 55.7 us -> 48.4 us  [send(): return lax.ppermute(values, 'inner', perm)]
    ppermute x18, starting transfers between devices: 35.2 us -> 40.8 us  [send(): return lax.ppermute(values, 'inner', perm)]
    ppermute x29, waiting for transfers between devices: 27.4 us -> 24.9 us  [across(): lax.ppermute(values, 'inner', [(d, d ^ bit) for d in range(self.size)])]
    dot_general x4, matrix products: 5.76 us -> 3.37 us  [merge(): jnp.dot(ring.between(piece, slot), weight, preferred_element_type=jnp.flo...]
  transfers between devices with their start and end apart: 49 -> 49, of which waited for: 20 -> 19; matrix products, arithmetic and copies ran while one was open for 29% -> 28% of each run, Pallas kernels for 0% -> 0%
where the time goes in v14:
time: 208 us
  waiting for transfers between devices  76.6 us (37%)
  starting transfers between devices  67.4 us (32%)
  matrix products  34.2 us (16%)
  other arithmetic  24.8 us (12%)
  local copies, waits for them, and re-layouts  3.77 us (2%)
    ppermute x18, waiting for transfers between devices, send(): return lax.ppermute(values, 'inner', perm)  48.4 us
    ppermute x18, starting transfers between devices, send(): return lax.ppermute(values, 'inner', perm)  40.8 us
    ppermute x29, waiting for transfers between devices, across(): lax.ppermute(values, 'inner', [(d, d ^ bit) for d in range(self.size)])  24.9 us
    dot_general x10, matrix products, experts(): projected = jnp.dot(rows, gate_up, preferred_element_type=jnp.float32)  23.8 us
    ppermute x29, starting transfers between devices, across(): lax.ppermute(values, 'inner', [(d, d ^ bit) for d in range(self.size)])  23.5 us
    dot_general x10, matrix products, experts(): jnp.dot(hidden.astype(jnp.bfloat16), down, preferred_element_type=jnp.flo...  7.07 us
    reduce_sum x8, other arithmetic, gate_column(): jnp.sum(jnp.where(named == who.astype(jnp.float32), high + low, 0.0), axi...  5.05 us
  transfers between devices with their start and end apart: 49, of which 19 were waited for; matrix products, arithmetic and copies ran while one was open for 28% of the time, Pallas kernels for 0%

profile of v14, /device:TPU:0, one launch (start us, length us, event | category | flops | bytes accessed | tf_op | source)
XLA Modules:
  0.0 207.6 jit_solution(11234943873927993992)
XLA Ops:
  3.4 3.1 %collective-permute-start.3 = (bf16[64,2176]{1,0:T(8,128)(2,1)S(1)}, bf16[64,2176]{1,0:T(8,128)(2,1)S(1)}, u32[]{:S(2)}, u32[]{:S(2)}) collective-permute-start(bf16[64,2176]{1,0:T(8,128)(2,1)S(1)} %pad_maximum_fusion.14), channel_id=1, source_target_pairs={{0,4},{1,5},{2,6},{3,7},{4,0},{5,1},{6,2},{7,3},{8,12},{9,13},{10,... | collective-permute-start | bytes 835592 | tf_op jit(solution)/shard_map/ppermute | solution.py:25
  6.5 2.5 %collective-permute-start.2 = (bf16[64,2176]{1,0:T(8,128)(2,1)S(1)}, bf16[64,2176]{1,0:T(8,128)(2,1)S(1)}, u32[]{:S(2)}, u32[]{:S(2)}) collective-permute-start(bf16[64,2176]{1,0:T(8,128)(2,1)S(1)} %pad_maximum_fusion.14), channel_id=1, source_target_pairs={{0,12},{1,13},{2,14},{3,15},{4,8},{5,9},{6,10},{7,11},{8,4},{9,5},... | collective-permute-start | bytes 835592 | tf_op jit(solution)/shard_map/ppermute | solution.py:25
  9.1 1.5 collective-permute-start
  10.6 1.9 constant_dynamic-slice_fusion.1
  14.1 1.6 collective-permute-start.4
  15.7 3.1 %collective-permute-done = bf16[64,2176]{1,0:T(8,128)(2,1)} collective-permute-done((bf16[64,2176]{1,0:T(8,128)(2,1)S(1)}, bf16[64,2176]{1,0:T(8,128)(2,1)}, u32[]{:S(2)}, u32[]{:S(2)}) %collective-permute-start) | collective-permute-done | bytes 278560 | tf_op jit(solution)/shard_map/ppermute | solution.py:31
  19.9 2.7 %collective-permute-done.2 = bf16[64,2176]{1,0:T(8,128)(2,1)S(1)} collective-permute-done((bf16[64,2176]{1,0:T(8,128)(2,1)S(1)}, bf16[64,2176]{1,0:T(8,128)(2,1)S(1)}, u32[]{:S(2)}, u32[]{:S(2)}) %collective-permute-start.2) | collective-permute-done | bytes 278560 | tf_op jit(solution)/shard_map/ppermute | solution.py:25
  22.5 6.0 %collective-permute-done.4 = bf16[64,2176]{1,0:T(8,128)(2,1)S(1)} collective-permute-done((bf16[64,2176]{1,0:T(8,128)(2,1)S(1)}, bf16[64,2176]{1,0:T(8,128)(2,1)S(1)}, u32[]{:S(2)}, u32[]{:S(2)}) %collective-permute-start.4) | collective-permute-done | bytes 278560 | tf_op jit(solution)/shard_map/ppermute | solution.py:31
  28.5 1.5 collective-permute-start.5
  30.1 1.6 collective-permute-start.23
  31.6 3.8 %collective-permute-done.5 = bf16[64,2176]{1,0:T(8,128)(2,1)S(1)} collective-permute-done((bf16[64,2176]{1,0:T(8,128)(2,1)S(1)}, bf16[64,2176]{1,0:T(8,128)(2,1)S(1)}, u32[]{:S(2)}, u32[]{:S(2)}) %collective-permute-start.5) | collective-permute-done | bytes 278560 | tf_op jit(solution)/shard_map/ppermute | solution.py:31
  35.5 1.6 collective-permute-start.8
  51.6 1.6 collective-permute-start.16
  53.2 2.7 %collective-permute-done.13 = bf16[128,2048]{1,0:T(8,128)(2,1)S(1)} collective-permute-done((bf16[128,2048]{1,0:T(8,128)(2,1)S(1)}, bf16[128,2048]{1,0:T(8,128)(2,1)S(1)}, u32[]{:S(2)}, u32[]{:S(2)}) %collective-permute-start.13) | collective-permute-done | bytes 524320 | tf_op jit(solution)/shard_map/ppermute | solution.py:31
  56.1 1.6 collective-permute-start.14
  57.7 3.2 %collective-permute-done.16 = bf16[64,2048]{1,0:T(8,128)(2,1)S(1)} collective-permute-done((bf16[64,2048]{1,0:T(8,128)(2,1)S(1)}, bf16[64,2048]{1,0:T(8,128)(2,1)S(1)}, u32[]{:S(2)}, u32[]{:S(2)}) %collective-permute-start.16) | collective-permute-done | bytes 262176 | tf_op jit(solution)/shard_map/ppermute | solution.py:31
  60.9 2.5 %collective-permute-start.17 = (bf16[64,2048]{1,0:T(8,128)(2,1)S(1)}, bf16[64,2048]{1,0:T(8,128)(2,1)S(1)}, u32[]{:S(2)}, u32[]{:S(2)}) collective-permute-start(bf16[64,2048]{1,0:T(8,128)(2,1)S(1)} %add_convert_fusion.12), channel_id=1, source_target_pairs={{0,12},{1,13},{2,14},{3,15},{4,8},{5,9},{6,10},{7,11},{8,4},{9,5},... | collective-permute-start | bytes 786440 | tf_op jit(solution)/shard_map/ppermute | solution.py:25
  63.4 1.4 collective-permute-start.20
  64.9 1.6 collective-permute-done.14
  66.5 1.5 collective-permute-start.25
  68.7 2.3 %collective-permute-start.18 = (bf16[64,2048]{1,0:T(8,128)(2,1)}, bf16[64,2048]{1,0:T(8,128)(2,1)}, u32[]{:S(2)}, u32[]{:S(2)}) collective-permute-start(bf16[64,2048]{1,0:T(8,128)(2,1)} %add_convert_fusion.11), channel_id=1, source_target_pairs={{0,8},{1,9},{2,10},{3,11},{4,12},{5,13},{6,14},{7,15},{8,0},{9,1},... | collective-permute-start | bytes 786440 | tf_op jit(solution)/shard_map/ppermute | solution.py:25
  71.1 3.3 %collective-permute-done.25 = bf16[64,2048]{1,0:T(8,128)(2,1)S(1)} collective-permute-done((bf16[64,2048]{1,0:T(8,128)(2,1)S(1)}, bf16[64,2048]{1,0:T(8,128)(2,1)S(1)}, u32[]{:S(2)}, u32[]{:S(2)}) %collective-permute-start.25) | collective-permute-done | bytes 262176 | tf_op jit(solution)/shard_map/ppermute | solution.py:147
  76.7 1.7 maximum_select_fusion.1
  79.9 3.4 %collective-permute-start.21 = (bf16[64,2048]{1,0:T(8,128)(2,1)}, bf16[64,2048]{1,0:T(8,128)(2,1)}, u32[]{:S(2)}, u32[]{:S(2)}) collective-permute-start(bf16[64,2048]{1,0:T(8,128)(2,1)} %add_convert_fusion.10), channel_id=1, source_target_pairs={{0,4},{1,5},{2,6},{3,7},{4,0},{5,1},{6,2},{7,3},{8,12},{9,13},{10,... | collective-permute-start | bytes 786440 | tf_op jit(solution)/shard_map/ppermute | solution.py:25
  86.7 5.5 %collective-permute-done.21 = bf16[64,2048]{1,0:T(8,128)(2,1)} collective-permute-done((bf16[64,2048]{1,0:T(8,128)(2,1)}, bf16[64,2048]{1,0:T(8,128)(2,1)}, u32[]{:S(2)}, u32[]{:S(2)}) %collective-permute-start.21) | collective-permute-done | bytes 262176 | tf_op jit(solution)/shard_map/ppermute | solution.py:25
  92.2 1.6 fusion.22
  94.2 2.5 %collective-permute-start.27 = (bf16[64,1024]{1,0:T(8,128)(2,1)S(1)}, bf16[64,1024]{1,0:T(8,128)(2,1)S(1)}, u32[]{:S(2)}, u32[]{:S(2)}) collective-permute-start(bf16[64,1024]{1,0:T(8,128)(2,1)S(1)} %get-tuple-element.67), channel_id=1, source_target_pairs={{0,12},{1,13},{2,14},{3,15},{4,8},{5,9},{6,10},{7,11},{8,4},{9,5},... | collective-permute-start | bytes 393224 | tf_op jit(solution)/shard_map/ppermute | solution.py:25
  97.1 2.0 collective-permute-start.31
  99.1 3.0 %maximum_select_fusion = bf16[2,2,256,2048]{3,2,1,0:T(8,128)(2,1)S(1)} fusion(bf16[2,1,256,2048]{3,2,1,0:T(8,128)(2,1)S(1)} %maximum_select_fusion.2, bf16[2,1,256,2048]{3,2,1,0:T(8,128)(2,1)} %bitcast.4, pred[]{:T(512)S(6)} %eq.75), kind=kLoop, calls=%fused_computation | loop fusion | flops 6291456 | bytes 8388609 | tf_op jit(solution)/shard_map/jit(_where)/select_n | solution.py:157
  103.4 2.5 %collective-permute-start.28 = (bf16[64,2048]{1,0:T(8,128)(2,1)S(1)}, bf16[64,2048]{1,0:T(8,128)(2,1)S(1)}, u32[]{:S(2)}, u32[]{:S(2)}) collective-permute-start(bf16[64,2048]{1,0:T(8,128)(2,1)S(1)} %convolution_convert_fusion.6), channel_id=1, source_target_pairs={{0,12},{1,13},{2,14},{3,15},{4,8},{5,9},{6,10},{7,11},{8,4},{9,5},... | collective-permute-start | bytes 786440 | tf_op jit(solution)/shard_map/ppermute | solution.py:25
  105.9 1.8 collective-permute-done.29
  109.4 3.1 %collective-permute-start.32 = (bf16[64,2048]{1,0:T(8,128)(2,1)S(1)}, bf16[64,2048]{1,0:T(8,128)(2,1)S(1)}, u32[]{:S(2)}, u32[]{:S(2)}) collective-permute-start(bf16[64,2048]{1,0:T(8,128)(2,1)S(1)} %convolution_convert_fusion.4), channel_id=1, source_target_pairs={{0,4},{1,5},{2,6},{3,7},{4,0},{5,1},{6,2},{7,3},{8,12},{9,13},{10,... | collective-permute-start | bytes 786440 | tf_op jit(solution)/shard_map/ppermute | solution.py:25
  113.9 15.7 %collective-permute-done.30 = bf16[64,2048]{1,0:T(8,128)(2,1)S(1)} collective-permute-done((bf16[64,2048]{1,0:T(8,128)(2,1)S(1)}, bf16[64,2048]{1,0:T(8,128)(2,1)S(1)}, u32[]{:S(2)}, u32[]{:S(2)}) %collective-permute-start.30) | collective-permute-done | bytes 262176 | tf_op jit(solution)/shard_map/ppermute | solution.py:25
  132.3 2.5 %collective-permute-start.38 = (bf16[64,2048]{1,0:T(8,128)(2,1)S(1)}, bf16[64,2048]{1,0:T(8,128)(2,1)S(1)}, u32[]{:S(2)}, u32[]{:S(2)}) collective-permute-start(bf16[64,2048]{1,0:T(8,128)(2,1)S(1)} %fusion.25), channel_id=1, source_target_pairs={{0,12},{1,13},{2,14},{3,15},{4,8},{5,9},{6,10},{7,11},{8,4},{9,5},... | collective-permute-start | bytes 786440 | tf_op jit(solution)/shard_map/ppermute | solution.py:25
  134.8 3.3 %collective-permute-done.36 = bf16[64,2048]{1,0:T(8,128)(2,1)S(1)} collective-permute-done((bf16[64,2048]{1,0:T(8,128)(2,1)S(1)}, bf16[64,2048]{1,0:T(8,128)(2,1)S(1)}, u32[]{:S(2)}, u32[]{:S(2)}) %collective-permute-start.36) | collective-permute-done | bytes 262176 | tf_op jit(solution)/shard_map/ppermute | solution.py:25
  140.3 5.8 %collective-permute-start.40 = (bf16[64,2048]{1,0:T(8,128)(2,1)S(1)}, bf16[64,2048]{1,0:T(8,128)(2,1)S(1)}, u32[]{:S(2)}, u32[]{:S(2)}) collective-permute-start(bf16[64,2048]{1,0:T(8,128)(2,1)S(1)} %fusion.25), channel_id=1, source_target_pairs={{0,8},{1,9},{2,10},{3,11},{4,12},{5,13},{6,14},{7,15},{8,0},{9,1},... | collective-permute-start | bytes 786440 | tf_op jit(solution)/shard_map/ppermute | solution.py:25
  147.3 10.9 %collective-permute-done.40 = bf16[64,2048]{1,0:T(8,128)(2,1)S(1)} collective-permute-done((bf16[64,2048]{1,0:T(8,128)(2,1)S(1)}, bf16[64,2048]{1,0:T(8,128)(2,1)S(1)}, u32[]{:S(2)}, u32[]{:S(2)}) %collective-permute-start.40) | collective-permute-done | bytes 262176 | tf_op jit(solution)/shard_map/ppermute | solution.py:25
  159.2 2.9 %fusion.98 = f32[128,1024]{1,0:T(8,128)S(1)} fusion(bf16[128,2048]{1,0:T(8,128)(2,1)S(1)} %pad_maximum_fusion.12, bf16[1,2048,1024]{2,1,0:T(8,128)(2,1)} %param.21), kind=kOutput, calls=%fused_computation.193 | convolution fusion | flops 536870912 | bytes 5242880 | tf_op jit(solution)/shard_map/dot_general | solution.py:82
  162.7 2.9 %fusion.111 = f32[128,1024]{1,0:T(8,128)S(1)} fusion(bf16[128,2048]{1,0:T(8,128)(2,1)S(1)} %pad_maximum_fusion.12, bf16[2048,1024]{1,0:T(8,128)(2,1)} %collective-permute-done.33), kind=kOutput, calls=%fused_computation.206 | convolution fusion | flops 536870912 | bytes 5242880 | tf_op jit(solution)/shard_map/dot_general | solution.py:82
  167.4 3.5 %fusion.96 = f32[256,1024]{1,0:T(8,128)S(1)} fusion(bf16[256,2048]{1,0:T(8,128)(2,1)S(1)} %pad_maximum_fusion.5, bf16[1,2048,1024]{2,1,0:T(8,128)(2,1)} %param.21), kind=kOutput, calls=%fused_computation.191 | convolution fusion | flops 1073741824 | bytes 6291456 | tf_op jit(solution)/shard_map/dot_general | solution.py:82
  171.7 3.5 %fusion.112 = f32[256,1024]{1,0:T(8,128)S(1)} fusion(bf16[256,2048]{1,0:T(8,128)(2,1)S(1)} %pad_maximum_fusion.5, bf16[2048,1024]{1,0:T(8,128)(2,1)} %collective-permute-done.33), kind=kOutput, calls=%fused_computation.207 | convolution fusion | flops 1073741824 | bytes 6291456 | tf_op jit(solution)/shard_map/dot_general | solution.py:82
  176.2 2.9 %fusion.94 = f32[128,1024]{1,0:T(8,128)S(1)} fusion(bf16[128,2048]{1,0:T(8,128)(2,1)S(1)} %pad_maximum_fusion.13, bf16[1,2048,1024]{2,1,0:T(8,128)(2,1)} %param.21), kind=kOutput, calls=%fused_computation.189 | convolution fusion | flops 536870912 | bytes 5242880 | tf_op jit(solution)/shard_map/dot_general | solution.py:82
  179.7 2.9 %fusion.113 = f32[128,1024]{1,0:T(8,128)S(1)} fusion(bf16[128,2048]{1,0:T(8,128)(2,1)S(1)} %pad_maximum_fusion.13, bf16[2048,1024]{1,0:T(8,128)(2,1)} %collective-permute-done.33), kind=kOutput, calls=%fused_computation.208 | convolution fusion | flops 536870912 | bytes 5242880 | tf_op jit(solution)/shard_map/dot_general | solution.py:82
  184.2 2.5 %collective-permute-start.45 = (bf16[64,2048]{1,0:T(8,128)(2,1)S(1)}, bf16[64,2048]{1,0:T(8,128)(2,1)S(1)}, u32[]{:S(2)}, u32[]{:S(2)}) collective-permute-start(bf16[64,2048]{1,0:T(8,128)(2,1)S(1)} %add_convert_fusion.7), channel_id=1, source_target_pairs={{0,12},{1,13},{2,14},{3,15},{4,8},{5,9},{6,10},{7,11},{8,4},{9,5},... | collective-permute-start | bytes 786440 | tf_op jit(solution)/shard_map/ppermute | solution.py:25
  187.9 4.5 %collective-permute-done.42 = bf16[64,2048]{1,0:T(8,128)(2,1)S(1)} collective-permute-done((bf16[64,2048]{1,0:T(8,128)(2,1)S(1)}, bf16[64,2048]{1,0:T(8,128)(2,1)S(1)}, u32[]{:S(2)}, u32[]{:S(2)}) %collective-permute-start.42) | collective-permute-done | bytes 262176 | tf_op jit(solution)/shard_map/ppermute | solution.py:31
  192.5 3.7 %collective-permute-start.46 = (bf16[64,2048]{1,0:T(8,128)(2,1)S(1)}, bf16[64,2048]{1,0:T(8,128)(2,1)S(1)}, u32[]{:S(2)}, u32[]{:S(2)}) collective-permute-start(bf16[64,2048]{1,0:T(8,128)(2,1)S(1)} %add_convert_fusion.6), channel_id=1, source_target_pairs={{0,8},{1,9},{2,10},{3,11},{4,12},{5,13},{6,14},{7,15},{8,0},{9,1},... | collective-permute-start | bytes 786440 | tf_op jit(solution)/shard_map/ppermute | solution.py:25
  196.2 2.1 %collective-permute-start.48 = (bf16[64,2048]{1,0:T(8,128)(2,1)S(1)}, bf16[64,2048]{1,0:T(8,128)(2,1)S(1)}, u32[]{:S(2)}, u32[]{:S(2)}) collective-permute-start(bf16[64,2048]{1,0:T(8,128)(2,1)S(1)} %add_convert_fusion.5), channel_id=1, source_target_pairs={{0,4},{1,5},{2,6},{3,7},{4,0},{5,1},{6,2},{7,3},{8,12},{9,13},{10,... | collective-permute-start | bytes 786440 | tf_op jit(solution)/shard_map/ppermute | solution.py:25
  199.4 7.2 %collective-permute-done.46 = bf16[64,2048]{1,0:T(8,128)(2,1)S(1)} collective-permute-done((bf16[64,2048]{1,0:T(8,128)(2,1)S(1)}, bf16[64,2048]{1,0:T(8,128)(2,1)S(1)}, u32[]{:S(2)}, u32[]{:S(2)}) %collective-permute-start.46) | collective-permute-done | bytes 262176 | tf_op jit(solution)/shard_map/ppermute | solution.py:25
  (176 shorter events, 50.3 us)
Async XLA Ops:
  3.4 10.7 %collective-permute-start.3 = (bf16[64,2176]{1,0:T(8,128)(2,1)S(1)}, bf16[64,2176]{1,0:T(8,128)(2,1)S(1)}, u32[]{:S(2)}, u32[]{:S(2)}) collective-permute-start(bf16[64,2176]{1,0:T(8,128)(2,1)S(1)} %pad_maximum_fusion.14), channel_id=1, source_target_pairs={{0,4},{1,5},{2,6},{3,7},{4,0},{5,1},{6,2},{7,3},{8,12},{9,13},{10,... | collective-permute-start | bytes 835592 | tf_op jit(solution)/shard_map/ppermute | solution.py:25
  6.5 16.1 %collective-permute-start.2 = (bf16[64,2176]{1,0:T(8,128)(2,1)S(1)}, bf16[64,2176]{1,0:T(8,128)(2,1)S(1)}, u32[]{:S(2)}, u32[]{:S(2)}) collective-permute-start(bf16[64,2176]{1,0:T(8,128)(2,1)S(1)} %pad_maximum_fusion.14), channel_id=1, source_target_pairs={{0,12},{1,13},{2,14},{3,15},{4,8},{5,9},{6,10},{7,11},{8,4},{9,5},... | collective-permute-start | bytes 835592 | tf_op jit(solution)/shard_map/ppermute | solution.py:25
  9.0 26.5 %collective-permute-start.7 = (bf16[64,2176]{1,0:T(8,128)(2,1)S(1)}, bf16[64,2176]{1,0:T(8,128)(2,1)S(1)}, u32[]{:S(2)}, u32[]{:S(2)}) collective-permute-start(bf16[64,2176]{1,0:T(8,128)(2,1)S(1)} %pad_maximum_fusion.14), channel_id=1, source_target_pairs={{0,8},{1,9},{2,10},{3,11},{4,12},{5,13},{6,14},{7,15},{8,0},{9,1},... | collective-permute-start | bytes 835592 | tf_op jit(solution)/shard_map/ppermute | solution.py:25
  9.1 9.7 %collective-permute-start = (bf16[64,2176]{1,0:T(8,128)(2,1)S(1)}, bf16[64,2176]{1,0:T(8,128)(2,1)}, u32[]{:S(2)}, u32[]{:S(2)}) collective-permute-start(bf16[64,2176]{1,0:T(8,128)(2,1)S(1)} %pad_maximum_fusion.14), channel_id=1, source_target_pairs={{0,2},{1,3},{2,0},{3,1},{4,6},{5,7},{6,4},{7,5},{8,10},{9,11},{10,... | collective-permute-start | bytes 835592 | tf_op jit(solution)/shard_map/ppermute | solution.py:31
  12.5 17.6 %collective-permute-start.22 = (bf16[64,2048]{1,0:T(8,128)(2,1)}, bf16[64,2048]{1,0:T(8,128)(2,1)}, u32[]{:S(2)}, u32[]{:S(2)}) collective-permute-start(bf16[64,2048]{1,0:T(8,128)(2,1)} %get-tuple-element.65), channel_id=1, source_target_pairs={{0,2},{1,3},{2,0},{3,1},{4,6},{5,7},{6,4},{7,5},{8,10},{9,11},{10,... | collective-permute-start | bytes 786440 | tf_op jit(solution)/shard_map/ppermute | solution.py:31
  14.1 14.4 %collective-permute-start.4 = (bf16[64,2176]{1,0:T(8,128)(2,1)S(1)}, bf16[64,2176]{1,0:T(8,128)(2,1)S(1)}, u32[]{:S(2)}, u32[]{:S(2)}) collective-permute-start(bf16[64,2176]{1,0:T(8,128)(2,1)S(1)} %collective-permute-done.3), channel_id=1, source_target_pairs={{0,2},{1,3},{2,0},{3,1},{4,6},{5,7},{6,4},{7,5},{8,10},{9,11},{10,... | collective-permute-start | bytes 835592 | tf_op jit(solution)/shard_map/ppermute | solution.py:31
  19.8 17.3 %collective-permute-start.1 = (bf16[128,2176]{1,0:T(8,128)(2,1)S(1)}, bf16[128,2176]{1,0:T(8,128)(2,1)S(1)}, u32[]{:S(2)}, u32[]{:S(2)}) collective-permute-start(bf16[128,2176]{1,0:T(8,128)(2,1)S(1)} %pad_maximum_fusion.6), channel_id=1, source_target_pairs={{0,1},{1,0},{2,3},{3,2},{4,5},{5,4},{6,7},{7,6},{8,9},{9,8},{10,11... | collective-permute-start | bytes 1671176 | tf_op jit(solution)/shard_map/ppermute | solution.py:31
  28.5 6.9 %collective-permute-start.5 = (bf16[64,2176]{1,0:T(8,128)(2,1)S(1)}, bf16[64,2176]{1,0:T(8,128)(2,1)S(1)}, u32[]{:S(2)}, u32[]{:S(2)}) collective-permute-start(bf16[64,2176]{1,0:T(8,128)(2,1)S(1)} %collective-permute-done.2), channel_id=1, source_target_pairs={{0,2},{1,3},{2,0},{3,1},{4,6},{5,7},{6,4},{7,5},{8,10},{9,11},{10,... | collective-permute-start | bytes 835592 | tf_op jit(solution)/shard_map/ppermute | solution.py:31
  30.1 15.0 %collective-permute-start.23 = (bf16[64,2048]{1,0:T(8,128)(2,1)}, bf16[64,2048]{1,0:T(8,128)(2,1)S(1)}, u32[]{:S(2)}, u32[]{:S(2)}) collective-permute-start(bf16[64,2048]{1,0:T(8,128)(2,1)} %collective-permute-done.22), channel_id=1, source_target_pairs={{0,16},{16,0},{1,17},{17,1},{2,18},{18,2},{3,19},{19,3},{4,20},{20... | collective-permute-start | bytes 786440 | tf_op jit(solution)/shard_map/ppermute | solution.py:147
  31.6 7.9 %collective-permute-start.10 = (bf16[128,2176]{1,0:T(8,128)(2,1)S(1)}, bf16[128,2176]{1,0:T(8,128)(2,1)S(1)}, u32[]{:S(2)}, u32[]{:S(2)}) collective-permute-start(bf16[128,2176]{1,0:T(8,128)(2,1)S(1)} %pad_maximum_fusion.9), channel_id=1, source_target_pairs={{0,1},{1,0},{2,3},{3,2},{4,5},{5,4},{6,7},{7,6},{8,9},{9,8},{10,11... | collective-permute-start | bytes 1671176 | tf_op jit(solution)/shard_map/ppermute | solution.py:31
  35.5 9.4 %collective-permute-start.8 = (bf16[64,2176]{1,0:T(8,128)(2,1)S(1)}, bf16[64,2176]{1,0:T(8,128)(2,1)S(1)}, u32[]{:S(2)}, u32[]{:S(2)}) collective-permute-start(bf16[64,2176]{1,0:T(8,128)(2,1)S(1)} %collective-permute-done.7), channel_id=1, source_target_pairs={{0,2},{1,3},{2,0},{3,1},{4,6},{5,7},{6,4},{7,5},{8,10},{9,11},{10,... | collective-permute-start | bytes 835592 | tf_op jit(solution)/shard_map/ppermute | solution.py:31
  37.2 4.8 %collective-permute-start.9 = (bf16[128,2176]{1,0:T(8,128)(2,1)S(1)}, bf16[128,2176]{1,0:T(8,128)(2,1)S(1)}, u32[]{:S(2)}, u32[]{:S(2)}) collective-permute-start(bf16[128,2176]{1,0:T(8,128)(2,1)S(1)} %pad_maximum_fusion.8), channel_id=1, source_target_pairs={{0,1},{1,0},{2,3},{3,2},{4,5},{5,4},{6,7},{7,6},{8,9},{9,8},{10,11... | collective-permute-start | bytes 1671176 | tf_op jit(solution)/shard_map/ppermute | solution.py:31
  45.0 3.0 %collective-permute-start.11 = (bf16[128,2176]{1,0:T(8,128)(2,1)S(1)}, bf16[128,2176]{1,0:T(8,128)(2,1)S(1)}, u32[]{:S(2)}, u32[]{:S(2)}) collective-permute-start(bf16[128,2176]{1,0:T(8,128)(2,1)S(1)} %pad_maximum_fusion.7), channel_id=1, source_target_pairs={{0,1},{1,0},{2,3},{3,2},{4,5},{5,4},{6,7},{7,6},{8,9},{9,8},{10,11... | collective-permute-start | bytes 1671176 | tf_op jit(solution)/shard_map/ppermute | solution.py:31
  46.1 4.4 %collective-permute-start.6 = (bf16[128,2048]{1,0:T(8,128)(2,1)S(1)}, bf16[128,2048]{1,0:T(8,128)(2,1)S(1)}, u32[]{:S(2)}, u32[]{:S(2)}) collective-permute-start(bf16[128,2048]{1,0:T(8,128)(2,1)S(1)} %slice.397), channel_id=1, source_target_pairs={{0,1},{1,0},{2,3},{3,2},{4,5},{5,4},{6,7},{7,6},{8,9},{9,8},{10,11... | collective-permute-start | bytes 1572872 | tf_op jit(solution)/shard_map/ppermute | solution.py:31
  46.7 18.2 %collective-permute-start.24 = (bf16[64,2048]{1,0:T(8,128)(2,1)S(1)}, bf16[64,2048]{1,0:T(8,128)(2,1)S(1)}, u32[]{:S(2)}, u32[]{:S(2)}) collective-permute-start(bf16[64,2048]{1,0:T(8,128)(2,1)S(1)} %copy-done.13), channel_id=1, source_target_pairs={{0,2},{1,3},{2,0},{3,1},{4,6},{5,7},{6,4},{7,5},{8,10},{9,11},{10,... | collective-permute-start | bytes 786440 | tf_op jit(solution)/shard_map/ppermute | solution.py:31
  47.3 4.1 %collective-permute-start.19 = (bf16[128,2048]{1,0:T(8,128)(2,1)S(1)}, bf16[128,2048]{1,0:T(8,128)(2,1)S(1)}, u32[]{:S(2)}, u32[]{:S(2)}) collective-permute-start(bf16[128,2048]{1,0:T(8,128)(2,1)S(1)} %slice.415), channel_id=1, source_target_pairs={{0,1},{1,0},{2,3},{3,2},{4,5},{5,4},{6,7},{7,6},{8,9},{9,8},{10,11... | collective-permute-start | bytes 1572872 | tf_op jit(solution)/shard_map/ppermute | solution.py:31
  47.3 82.5 %collective-permute-start.33 = (bf16[2048,1024]{1,0:T(8,128)(2,1)}, bf16[2048,1024]{1,0:T(8,128)(2,1)}, u32[]{:S(2)}, u32[]{:S(2)}) collective-permute-start(bf16[2048,1024]{1,0:T(8,128)(2,1)} %bitcast.12), channel_id=1, source_target_pairs={{0,1},{1,0},{2,3},{3,2},{4,5},{5,4},{6,7},{7,6},{8,9},{9,8},{10,11... | collective-permute-start | bytes 12582920 | tf_op jit(solution)/shard_map/ppermute | solution.py:31
  50.4 5.5 %collective-permute-start.13 = (bf16[128,2048]{1,0:T(8,128)(2,1)S(1)}, bf16[128,2048]{1,0:T(8,128)(2,1)S(1)}, u32[]{:S(2)}, u32[]{:S(2)}) collective-permute-start(bf16[128,2048]{1,0:T(8,128)(2,1)S(1)} %slice.409), channel_id=1, source_target_pairs={{0,1},{1,0},{2,3},{3,2},{4,5},{5,4},{6,7},{7,6},{8,9},{9,8},{10,11... | collective-permute-start | bytes 1572872 | tf_op jit(solution)/shard_map/ppermute | solution.py:31
  51.6 9.2 %collective-permute-start.16 = (bf16[64,2048]{1,0:T(8,128)(2,1)S(1)}, bf16[64,2048]{1,0:T(8,128)(2,1)S(1)}, u32[]{:S(2)}, u32[]{:S(2)}) collective-permute-start(bf16[64,2048]{1,0:T(8,128)(2,1)S(1)} %slice.412), channel_id=1, source_target_pairs={{0,2},{1,3},{2,0},{3,1},{4,6},{5,7},{6,4},{7,5},{8,10},{9,11},{10,... | collective-permute-start | bytes 786440 | tf_op jit(solution)/shard_map/ppermute | solution.py:31
  56.1 10.4 %collective-permute-start.14 = (bf16[64,2048]{1,0:T(8,128)(2,1)S(1)}, bf16[64,2048]{1,0:T(8,128)(2,1)S(1)}, u32[]{:S(2)}, u32[]{:S(2)}) collective-permute-start(bf16[64,2048]{1,0:T(8,128)(2,1)S(1)} %slice.410), channel_id=1, source_target_pairs={{0,2},{1,3},{2,0},{3,1},{4,6},{5,7},{6,4},{7,5},{8,10},{9,11},{10,... | collective-permute-start | bytes 786440 | tf_op jit(solution)/shard_map/ppermute | solution.py:31
  60.9 18.3 %collective-permute-start.17 = (bf16[64,2048]{1,0:T(8,128)(2,1)S(1)}, bf16[64,2048]{1,0:T(8,128)(2,1)S(1)}, u32[]{:S(2)}, u32[]{:S(2)}) collective-permute-start(bf16[64,2048]{1,0:T(8,128)(2,1)S(1)} %add_convert_fusion.12), channel_id=1, source_target_pairs={{0,12},{1,13},{2,14},{3,15},{4,8},{5,9},{6,10},{7,11},{8,4},{9,5},... | collective-permute-start | bytes 786440 | tf_op jit(solution)/shard_map/ppermute | solution.py:25
  63.4 15.0 %collective-permute-start.20 = (bf16[64,2048]{1,0:T(8,128)(2,1)S(1)}, bf16[64,2048]{1,0:T(8,128)(2,1)S(1)}, u32[]{:S(2)}, u32[]{:S(2)}) collective-permute-start(bf16[64,2048]{1,0:T(8,128)(2,1)S(1)} %slice.417), channel_id=1, source_target_pairs={{0,2},{1,3},{2,0},{3,1},{4,6},{5,7},{6,4},{7,5},{8,10},{9,11},{10,... | collective-permute-start | bytes 786440 | tf_op jit(solution)/shard_map/ppermute | solution.py:31
  66.5 7.8 %collective-permute-start.25 = (bf16[64,2048]{1,0:T(8,128)(2,1)S(1)}, bf16[64,2048]{1,0:T(8,128)(2,1)S(1)}, u32[]{:S(2)}, u32[]{:S(2)}) collective-permute-start(bf16[64,2048]{1,0:T(8,128)(2,1)S(1)} %collective-permute-done.24), channel_id=1, source_target_pairs={{0,16},{16,0},{1,17},{17,1},{2,18},{18,2},{3,19},{19,3},{4,20},{20... | collective-permute-start | bytes 786440 | tf_op jit(solution)/shard_map/ppermute | solution.py:147
  68.7 17.9 %collective-permute-start.18 = (bf16[64,2048]{1,0:T(8,128)(2,1)}, bf16[64,2048]{1,0:T(8,128)(2,1)}, u32[]{:S(2)}, u32[]{:S(2)}) collective-permute-start(bf16[64,2048]{1,0:T(8,128)(2,1)} %add_convert_fusion.11), channel_id=1, source_target_pairs={{0,8},{1,9},{2,10},{3,11},{4,12},{5,13},{6,14},{7,15},{8,0},{9,1},... | collective-permute-start | bytes 786440 | tf_op jit(solution)/shard_map/ppermute | solution.py:25
  74.3 12.3 %collective-permute-start.15 = (bf16[64,2048]{1,0:T(8,128)(2,1)}, bf16[64,2048]{1,0:T(8,128)(2,1)}, u32[]{:S(2)}, u32[]{:S(2)}) collective-permute-start(bf16[64,2048]{1,0:T(8,128)(2,1)} %slice.399), channel_id=1, source_target_pairs={{0,2},{1,3},{2,0},{3,1},{4,6},{5,7},{6,4},{7,5},{8,10},{9,11},{10,... | collective-permute-start | bytes 786440 | tf_op jit(solution)/shard_map/ppermute | solution.py:31
  78.4 18.6 %collective-permute-start.26 = (bf16[2,256,2048]{2,1,0:T(8,128)(2,1)}, bf16[2,256,2048]{2,1,0:T(8,128)(2,1)}, u32[]{:S(2)}, u32[]{:S(2)}) collective-permute-start(bf16[2,256,2048]{2,1,0:T(8,128)(2,1)} %maximum_select_fusion.1), channel_id=1, source_target_pairs={{0,1},{1,0},{2,3},{3,2},{4,5},{5,4},{6,7},{7,6},{8,9},{9,8},{10,11... | collective-permute-start | bytes 6291464 | tf_op jit(solution)/shard_map/ppermute | solution.py:31
  79.9 12.3 %collective-permute-start.21 = (bf16[64,2048]{1,0:T(8,128)(2,1)}, bf16[64,2048]{1,0:T(8,128)(2,1)}, u32[]{:S(2)}, u32[]{:S(2)}) collective-permute-start(bf16[64,2048]{1,0:T(8,128)(2,1)} %add_convert_fusion.10), channel_id=1, source_target_pairs={{0,4},{1,5},{2,6},{3,7},{4,0},{5,1},{6,2},{7,3},{8,12},{9,13},{10,... | collective-permute-start | bytes 786440 | tf_op jit(solution)/shard_map/ppermute | solution.py:25
  86.7 43.2 %collective-permute-start.34 = (bf16[512,2048]{1,0:T(8,128)(2,1)S(1)}, bf16[512,2048]{1,0:T(8,128)(2,1)S(1)}, u32[]{:S(2)}, u32[]{:S(2)}) collective-permute-start(bf16[512,2048]{1,0:T(8,128)(2,1)S(1)} %bitcast.69), channel_id=1, source_target_pairs={{0,1},{1,0},{2,3},{3,2},{4,5},{5,4},{6,7},{7,6},{8,9},{9,8},{10,11... | collective-permute-start | bytes 6291464 | tf_op jit(solution)/shard_map/ppermute | solution.py:31
  94.2 8.3 %collective-permute-start.27 = (bf16[64,1024]{1,0:T(8,128)(2,1)S(1)}, bf16[64,1024]{1,0:T(8,128)(2,1)S(1)}, u32[]{:S(2)}, u32[]{:S(2)}) collective-permute-start(bf16[64,1024]{1,0:T(8,128)(2,1)S(1)} %get-tuple-element.67), channel_id=1, source_target_pairs={{0,12},{1,13},{2,14},{3,15},{4,8},{5,9},{6,10},{7,11},{8,4},{9,5},... | collective-permute-start | bytes 393224 | tf_op jit(solution)/shard_map/ppermute | solution.py:25
  96.7 10.9 %collective-permute-start.29 = (bf16[64,1024]{1,0:T(8,128)(2,1)S(1)}, bf16[64,1024]{1,0:T(8,128)(2,1)S(1)}, u32[]{:S(2)}, u32[]{:S(2)}) collective-permute-start(bf16[64,1024]{1,0:T(8,128)(2,1)S(1)} %get-tuple-element.68), channel_id=1, source_target_pairs={{0,8},{1,9},{2,10},{3,11},{4,12},{5,13},{6,14},{7,15},{8,0},{9,1},... | collective-permute-start | bytes 393224 | tf_op jit(solution)/shard_map/ppermute | solution.py:25
  97.1 11.5 %collective-permute-start.31 = (bf16[64,1024]{1,0:T(8,128)(2,1)S(1)}, bf16[64,1024]{1,0:T(8,128)(2,1)S(1)}, u32[]{:S(2)}, u32[]{:S(2)}) collective-permute-start(bf16[64,1024]{1,0:T(8,128)(2,1)S(1)} %get-tuple-element.69), channel_id=1, source_target_pairs={{0,4},{1,5},{2,6},{3,7},{4,0},{5,1},{6,2},{7,3},{8,12},{9,13},{10,... | collective-permute-start | bytes 393224 | tf_op jit(solution)/shard_map/ppermute | solution.py:25
  103.4 10.5 %collective-permute-start.28 = (bf16[64,2048]{1,0:T(8,128)(2,1)S(1)}, bf16[64,2048]{1,0:T(8,128)(2,1)S(1)}, u32[]{:S(2)}, u32[]{:S(2)}) collective-permute-start(bf16[64,2048]{1,0:T(8,128)(2,1)S(1)} %convolution_convert_fusion.6), channel_id=1, source_target_pairs={{0,12},{1,13},{2,14},{3,15},{4,8},{5,9},{6,10},{7,11},{8,4},{9,5},... | collective-permute-start | bytes 786440 | tf_op jit(solution)/shard_map/ppermute | solution.py:25
  108.5 21.0 %collective-permute-start.30 = (bf16[64,2048]{1,0:T(8,128)(2,1)S(1)}, bf16[64,2048]{1,0:T(8,128)(2,1)S(1)}, u32[]{:S(2)}, u32[]{:S(2)}) collective-permute-start(bf16[64,2048]{1,0:T(8,128)(2,1)S(1)} %convolution_convert_fusion.5), channel_id=1, source_target_pairs={{0,8},{1,9},{2,10},{3,11},{4,12},{5,13},{6,14},{7,15},{8,0},{9,1},... | collective-permute-start | bytes 786440 | tf_op jit(solution)/shard_map/ppermute | solution.py:25
  109.4 20.1 %collective-permute-start.32 = (bf16[64,2048]{1,0:T(8,128)(2,1)S(1)}, bf16[64,2048]{1,0:T(8,128)(2,1)S(1)}, u32[]{:S(2)}, u32[]{:S(2)}) collective-permute-start(bf16[64,2048]{1,0:T(8,128)(2,1)S(1)} %convolution_convert_fusion.4), channel_id=1, source_target_pairs={{0,4},{1,5},{2,6},{3,7},{4,0},{5,1},{6,2},{7,3},{8,12},{9,13},{10,... | collective-permute-start | bytes 786440 | tf_op jit(solution)/shard_map/ppermute | solution.py:25
  129.8 8.3 %collective-permute-start.36 = (bf16[64,2048]{1,0:T(8,128)(2,1)S(1)}, bf16[64,2048]{1,0:T(8,128)(2,1)S(1)}, u32[]{:S(2)}, u32[]{:S(2)}) collective-permute-start(bf16[64,2048]{1,0:T(8,128)(2,1)S(1)} %fusion.25), channel_id=1, source_target_pairs={{0,4},{1,5},{2,6},{3,7},{4,0},{5,1},{6,2},{7,3},{8,12},{9,13},{10,... | collective-permute-start | bytes 786440 | tf_op jit(solution)/shard_map/ppermute | solution.py:25
  129.9 16.1 %collective-permute-start.35 = (bf16[64,2048]{1,0:T(8,128)(2,1)S(1)}, bf16[64,2048]{1,0:T(8,128)(2,1)S(1)}, u32[]{:S(2)}, u32[]{:S(2)}) collective-permute-start(bf16[64,2048]{1,0:T(8,128)(2,1)S(1)} %fusion.25), channel_id=1, source_target_pairs={{0,2},{1,3},{2,0},{3,1},{4,6},{5,7},{6,4},{7,5},{8,10},{9,11},{10,... | collective-permute-start | bytes 786440 | tf_op jit(solution)/shard_map/ppermute | solution.py:31
  132.3 13.8 %collective-permute-start.38 = (bf16[64,2048]{1,0:T(8,128)(2,1)S(1)}, bf16[64,2048]{1,0:T(8,128)(2,1)S(1)}, u32[]{:S(2)}, u32[]{:S(2)}) collective-permute-start(bf16[64,2048]{1,0:T(8,128)(2,1)S(1)} %fusion.25), channel_id=1, source_target_pairs={{0,12},{1,13},{2,14},{3,15},{4,8},{5,9},{6,10},{7,11},{8,4},{9,5},... | collective-permute-start | bytes 786440 | tf_op jit(solution)/shard_map/ppermute | solution.py:25
  138.1 8.0 %collective-permute-start.37 = (bf16[64,2048]{1,0:T(8,128)(2,1)S(1)}, bf16[64,2048]{1,0:T(8,128)(2,1)S(1)}, u32[]{:S(2)}, u32[]{:S(2)}) collective-permute-start(bf16[64,2048]{1,0:T(8,128)(2,1)S(1)} %collective-permute-done.36), channel_id=1, source_target_pairs={{0,2},{1,3},{2,0},{3,1},{4,6},{5,7},{6,4},{7,5},{8,10},{9,11},{10,... | collective-permute-start | bytes 786440 | tf_op jit(solution)/shard_map/ppermute | solution.py:31
  140.3 17.9 %collective-permute-start.40 = (bf16[64,2048]{1,0:T(8,128)(2,1)S(1)}, bf16[64,2048]{1,0:T(8,128)(2,1)S(1)}, u32[]{:S(2)}, u32[]{:S(2)}) collective-permute-start(bf16[64,2048]{1,0:T(8,128)(2,1)S(1)} %fusion.25), channel_id=1, source_target_pairs={{0,8},{1,9},{2,10},{3,11},{4,12},{5,13},{6,14},{7,15},{8,0},{9,1},... | collective-permute-start | bytes 786440 | tf_op jit(solution)/shard_map/ppermute | solution.py:25
  146.1 12.1 %collective-permute-start.39 = (bf16[64,2048]{1,0:T(8,128)(2,1)S(1)}, bf16[64,2048]{1,0:T(8,128)(2,1)S(1)}, u32[]{:S(2)}, u32[]{:S(2)}) collective-permute-start(bf16[64,2048]{1,0:T(8,128)(2,1)S(1)} %collective-permute-done.38), channel_id=1, source_target_pairs={{0,2},{1,3},{2,0},{3,1},{4,6},{5,7},{6,4},{7,5},{8,10},{9,11},{10,... | collective-permute-start | bytes 786440 | tf_op jit(solution)/shard_map/ppermute | solution.py:31
  158.3 17.9 %collective-permute-start.41 = (bf16[64,2048]{1,0:T(8,128)(2,1)S(1)}, bf16[64,2048]{1,0:T(8,128)(2,1)S(1)}, u32[]{:S(2)}, u32[]{:S(2)}) collective-permute-start(bf16[64,2048]{1,0:T(8,128)(2,1)S(1)} %collective-permute-done.40), channel_id=1, source_target_pairs={{0,2},{1,3},{2,0},{3,1},{4,6},{5,7},{6,4},{7,5},{8,10},{9,11},{10,... | collective-permute-start | bytes 786440 | tf_op jit(solution)/shard_map/ppermute | solution.py:31
  166.3 17.9 %collective-permute-start.44 = (bf16[64,2048]{1,0:T(8,128)(2,1)S(1)}, bf16[64,2048]{1,0:T(8,128)(2,1)S(1)}, u32[]{:S(2)}, u32[]{:S(2)}) collective-permute-start(bf16[64,2048]{1,0:T(8,128)(2,1)S(1)} %slice.434), channel_id=1, source_target_pairs={{0,2},{1,3},{2,0},{3,1},{4,6},{5,7},{6,4},{7,5},{8,10},{9,11},{10,... | collective-permute-start | bytes 786440 | tf_op jit(solution)/shard_map/ppermute | solution.py:31
  183.2 9.2 %collective-permute-start.42 = (bf16[64,2048]{1,0:T(8,128)(2,1)S(1)}, bf16[64,2048]{1,0:T(8,128)(2,1)S(1)}, u32[]{:S(2)}, u32[]{:S(2)}) collective-permute-start(bf16[64,2048]{1,0:T(8,128)(2,1)S(1)} %slice.432), channel_id=1, source_target_pairs={{0,2},{1,3},{2,0},{3,1},{4,6},{5,7},{6,4},{7,5},{8,10},{9,11},{10,... | collective-permute-start | bytes 786440 | tf_op jit(solution)/shard_map/ppermute | solution.py:31
  184.2 15.2 %collective-permute-start.45 = (bf16[64,2048]{1,0:T(8,128)(2,1)S(1)}, bf16[64,2048]{1,0:T(8,128)(2,1)S(1)}, u32[]{:S(2)}, u32[]{:S(2)}) collective-permute-start(bf16[64,2048]{1,0:T(8,128)(2,1)S(1)} %add_convert_fusion.7), channel_id=1, source_target_pairs={{0,12},{1,13},{2,14},{3,15},{4,8},{5,9},{6,10},{7,11},{8,4},{9,5},... | collective-permute-start | bytes 786440 | tf_op jit(solution)/shard_map/ppermute | solution.py:25
  186.8 9.4 %collective-permute-start.47 = (bf16[64,2048]{1,0:T(8,128)(2,1)S(1)}, bf16[64,2048]{1,0:T(8,128)(2,1)S(1)}, u32[]{:S(2)}, u32[]{:S(2)}) collective-permute-start(bf16[64,2048]{1,0:T(8,128)(2,1)S(1)} %get-tuple-element.50), channel_id=1, source_target_pairs={{0,2},{1,3},{2,0},{3,1},{4,6},{5,7},{6,4},{7,5},{8,10},{9,11},{10,... | collective-permute-start | bytes 786440 | tf_op jit(solution)/shard_map/ppermute | solution.py:31
  192.5 14.2 %collective-permute-start.46 = (bf16[64,2048]{1,0:T(8,128)(2,1)S(1)}, bf16[64,2048]{1,0:T(8,128)(2,1)S(1)}, u32[]{:S(2)}, u32[]{:S(2)}) collective-permute-start(bf16[64,2048]{1,0:T(8,128)(2,1)S(1)} %add_convert_fusion.6), channel_id=1, source_target_pairs={{0,8},{1,9},{2,10},{3,11},{4,12},{5,13},{6,14},{7,15},{8,0},{9,1},... | collective-permute-start | bytes 786440 | tf_op jit(solution)/shard_map/ppermute | solution.py:25
  196.2 10.4 %collective-permute-start.48 = (bf16[64,2048]{1,0:T(8,128)(2,1)S(1)}, bf16[64,2048]{1,0:T(8,128)(2,1)S(1)}, u32[]{:S(2)}, u32[]{:S(2)}) collective-permute-start(bf16[64,2048]{1,0:T(8,128)(2,1)S(1)} %add_convert_fusion.5), channel_id=1, source_target_pairs={{0,4},{1,5},{2,6},{3,7},{4,0},{5,1},{6,2},{7,3},{8,12},{9,13},{10,... | collective-permute-start | bytes 786440 | tf_op jit(solution)/shard_map/ppermute | solution.py:25
  198.4 8.3 %collective-permute-start.43 = (bf16[64,2048]{1,0:T(8,128)(2,1)S(1)}, bf16[64,2048]{1,0:T(8,128)(2,1)S(1)}, u32[]{:S(2)}, u32[]{:S(2)}) collective-permute-start(bf16[64,2048]{1,0:T(8,128)(2,1)S(1)} %get-tuple-element.49), channel_id=1, source_target_pairs={{0,2},{1,3},{2,0},{3,1},{4,6},{5,7},{6,4},{7,5},{8,10},{9,11},{10,... | collective-permute-start | bytes 786440 | tf_op jit(solution)/shard_map/ppermute | solution.py:31
  (19 other events, 182.1 us)

commit v15 on v12

--- a/solution.py
+++ b/solution.py
@@ -91,7 +91,8 @@
     columns = {0: rows}
     for slot in (1, 3, 2):
         columns[slot] = ring.between(rows, slot)
-    crossed = {slot: ring.across(columns[slot], top) for slot in (0, 1)}
+    crossed = {0: ring.across(rows, top)}
+    crossed[1] = ring.across(after(columns[1], crossed[0]) if paired else columns[1], top)
     crossed[3] = ring.across(after(columns[3], crossed[1]), top)
     crossed[2] = ring.across(after(columns[2], crossed[3]), top)
 
@@ -106,12 +107,11 @@
 
     halves = {}
     if paired:
-        both = work((0, 1), after(jnp.concatenate([chunk(0), chunk(1)], axis=0), crossed[3]))
-        third = work((3,), after(chunk(3), both))
-        halves[3] = halve(third)
-        last = work((2,), after(chunk(2), halves[3]))
+        both = work((3, 0), after(jnp.concatenate([chunk(3), chunk(0)], axis=0), crossed[3]))
         count = both.shape[0] // 2
-        done = {0: both[:count], 1: both[count:]}
+        halves[3] = halve(both[:count])
+        done = {0: both[count:], 1: work((1,), after(chunk(1), both))}
+        last = work((2,), after(chunk(2), done[1], halves[3]))
     else:
         done = {}
         ties = [crossed[3]]

time: 202 us -> 200 us (0.990)
  waiting for transfers between devices: 82.6 us -> 80.1 us
    ppermute x18, waiting for transfers between devices: 50.8 us -> 45.9 us  [send(): return lax.ppermute(values, 'inner', perm)]
    ppermute x29, waiting for transfers between devices: 29.2 us -> 31.6 us  [across(): lax.ppermute(values, 'inner', [(d, d ^ bit) for d in range(self.size)])]
    unnamed x38 -> x40, local copies, waits for them, and re-layouts: 4.37 us -> 3.76 us
  transfers between devices with their start and end apart: 49 -> 49, of which waited for: 20 -> 20; matrix products, arithmetic and copies ran while one was open for 18% -> 19% of each run, Pallas kernels for 0% -> 0%
where the time goes in v15:
time: 200 us; the launch traced here: 199 us
  waiting for transfers between devices  80.1 us (40%)
  starting transfers between devices  72.2 us (36%)
  matrix products  20.9 us (10%)
  other arithmetic  17.7 us (9%)
  local copies, waits for them, and re-layouts  7.55 us (4%)
    ppermute x18, starting transfers between devices, send(): return lax.ppermute(values, 'inner', perm)  47.2 us
    ppermute x18, waiting for transfers between devices, send(): return lax.ppermute(values, 'inner', perm)  45.9 us
    ppermute x29, waiting for transfers between devices, across(): lax.ppermute(values, 'inner', [(d, d ^ bit) for d in range(self.size)])  31.6 us
    ppermute x29, starting transfers between devices, across(): lax.ppermute(values, 'inner', [(d, d ^ bit) for d in range(self.size)])  22 us
    dot_general x10, matrix products, experts(): projected = jnp.dot(rows, gate_up, preferred_element_type=jnp.float32)  10.6 us
    dot_general x10, matrix products, experts(): jnp.dot(hidden.astype(jnp.bfloat16), down, preferred_element_type=jnp.flo...  6.95 us
    concatenate x8, other arithmetic, chunk(): part = after(jnp.concatenate([columns[slot], crossed[slot]], axis=0), *ties)  4.85 us
  transfers between devices with their start and end apart: 49, of which 20 were waited for; matrix products, arithmetic and copies ran while one was open for 19% of the time, Pallas kernels for 0%

profile of v15, /device:TPU:0, one launch (start us, length us, event | category | flops | bytes accessed | tf_op | source)
XLA Modules:
  0.0 199.4 jit_solution(4780472086901791729)
XLA Ops:
  3.4 3.1 %collective-permute-start.3 = (bf16[64,2176]{1,0:T(8,128)(2,1)S(1)}, bf16[64,2176]{1,0:T(8,128)(2,1)S(1)}, u32[]{:S(2)}, u32[]{:S(2)}) collective-permute-start(bf16[64,2176]{1,0:T(8,128)(2,1)S(1)} %pad_maximum_fusion.14), channel_id=1, source_target_pairs={{0,4},{1,5},{2,6},{3,7},{4,0},{5,1},{6,2},{7,3},{8,12},{9,13},{10,... | collective-permute-start | bytes 835592 | tf_op jit(solution)/shard_map/ppermute | solution.py:25
  6.5 2.5 %collective-permute-start.2 = (bf16[64,2176]{1,0:T(8,128)(2,1)S(1)}, bf16[64,2176]{1,0:T(8,128)(2,1)S(1)}, u32[]{:S(2)}, u32[]{:S(2)}) collective-permute-start(bf16[64,2176]{1,0:T(8,128)(2,1)S(1)} %pad_maximum_fusion.14), channel_id=1, source_target_pairs={{0,12},{1,13},{2,14},{3,15},{4,8},{5,9},{6,10},{7,11},{8,4},{9,5},... | collective-permute-start | bytes 835592 | tf_op jit(solution)/shard_map/ppermute | solution.py:25
  9.1 1.5 collective-permute-start
  10.6 1.9 constant_dynamic-slice_fusion.1
  14.2 1.6 collective-permute-start.4
  15.8 2.9 %collective-permute-done = bf16[64,2176]{1,0:T(8,128)(2,1)S(1)} collective-permute-done((bf16[64,2176]{1,0:T(8,128)(2,1)S(1)}, bf16[64,2176]{1,0:T(8,128)(2,1)S(1)}, u32[]{:S(2)}, u32[]{:S(2)}) %collective-permute-start) | collective-permute-done | bytes 278560 | tf_op jit(solution)/shard_map/ppermute | solution.py:31
  18.8 3.7 %collective-permute-done.2 = bf16[64,2176]{1,0:T(8,128)(2,1)S(1)} collective-permute-done((bf16[64,2176]{1,0:T(8,128)(2,1)S(1)}, bf16[64,2176]{1,0:T(8,128)(2,1)S(1)}, u32[]{:S(2)}, u32[]{:S(2)}) %collective-permute-start.2) | collective-permute-done | bytes 278560 | tf_op jit(solution)/shard_map/ppermute | solution.py:25
  22.5 6.0 %collective-permute-done.4 = bf16[64,2176]{1,0:T(8,128)(2,1)S(1)} collective-permute-done((bf16[64,2176]{1,0:T(8,128)(2,1)S(1)}, bf16[64,2176]{1,0:T(8,128)(2,1)S(1)}, u32[]{:S(2)}, u32[]{:S(2)}) %collective-permute-start.4) | collective-permute-done | bytes 278560 | tf_op jit(solution)/shard_map/ppermute | solution.py:31
  28.5 1.5 collective-permute-start.5
  30.1 1.6 collective-permute-start.23
  31.6 3.8 %collective-permute-done.5 = bf16[64,2176]{1,0:T(8,128)(2,1)S(1)} collective-permute-done((bf16[64,2176]{1,0:T(8,128)(2,1)S(1)}, bf16[64,2176]{1,0:T(8,128)(2,1)S(1)}, u32[]{:S(2)}, u32[]{:S(2)}) %collective-permute-start.5) | collective-permute-done | bytes 278560 | tf_op jit(solution)/shard_map/ppermute | solution.py:31
  35.5 1.6 collective-permute-start.8
  37.2 1.3 fusion.6
  42.2 1.3 fusion.2
  45.0 1.3 pad_maximum_fusion.7
  49.4 1.3 fusion
  52.3 1.6 collective-permute-start.16
  53.9 3.4 %collective-permute-done.13 = bf16[128,2048]{1,0:T(8,128)(2,1)S(1)} collective-permute-done((bf16[128,2048]{1,0:T(8,128)(2,1)S(1)}, bf16[128,2048]{1,0:T(8,128)(2,1)S(1)}, u32[]{:S(2)}, u32[]{:S(2)}) %collective-permute-start.13) | collective-permute-done | bytes 524320 | tf_op jit(solution)/shard_map/ppermute | solution.py:31
  57.4 1.6 collective-permute-start.14
  59.0 3.9 %collective-permute-done.16 = bf16[64,2048]{1,0:T(8,128)(2,1)S(1)} collective-permute-done((bf16[64,2048]{1,0:T(8,128)(2,1)S(1)}, bf16[64,2048]{1,0:T(8,128)(2,1)S(1)}, u32[]{:S(2)}, u32[]{:S(2)}) %collective-permute-start.16) | collective-permute-done | bytes 262176 | tf_op jit(solution)/shard_map/ppermute | solution.py:31
  63.0 2.4 %collective-permute-start.17 = (bf16[64,2048]{1,0:T(8,128)(2,1)S(1)}, bf16[64,2048]{1,0:T(8,128)(2,1)S(1)}, u32[]{:S(2)}, u32[]{:S(2)}) collective-permute-start(bf16[64,2048]{1,0:T(8,128)(2,1)S(1)} %add_convert_fusion.12), channel_id=1, source_target_pairs={{0,12},{1,13},{2,14},{3,15},{4,8},{5,9},{6,10},{7,11},{8,4},{9,5},... | collective-permute-start | bytes 786440 | tf_op jit(solution)/shard_map/ppermute | solution.py:25
  65.5 3.0 %collective-permute-done.14 = bf16[64,2048]{1,0:T(8,128)(2,1)S(1)} collective-permute-done((bf16[64,2048]{1,0:T(8,128)(2,1)S(1)}, bf16[64,2048]{1,0:T(8,128)(2,1)S(1)}, u32[]{:S(2)}, u32[]{:S(2)}) %collective-permute-start.14) | collective-permute-done | bytes 262176 | tf_op jit(solution)/shard_map/ppermute | solution.py:31
  68.5 1.5 collective-permute-start.25
  70.1 2.3 %collective-permute-start.18 = (bf16[64,2048]{1,0:T(8,128)(2,1)S(1)}, bf16[64,2048]{1,0:T(8,128)(2,1)S(1)}, u32[]{:S(2)}, u32[]{:S(2)}) collective-permute-start(bf16[64,2048]{1,0:T(8,128)(2,1)S(1)} %add_convert_fusion.11), channel_id=1, source_target_pairs={{0,8},{1,9},{2,10},{3,11},{4,12},{5,13},{6,14},{7,15},{8,0},{9,1},... | collective-permute-start | bytes 786440 | tf_op jit(solution)/shard_map/ppermute | solution.py:25
  72.4 2.6 %collective-permute-done.25 = bf16[64,2048]{1,0:T(8,128)(2,1)S(1)} collective-permute-done((bf16[64,2048]{1,0:T(8,128)(2,1)S(1)}, bf16[64,2048]{1,0:T(8,128)(2,1)S(1)}, u32[]{:S(2)}, u32[]{:S(2)}) %collective-permute-start.25) | collective-permute-done | bytes 262176 | tf_op jit(solution)/shard_map/ppermute | solution.py:147
  76.9 6.3 %collective-permute-start.21 = (bf16[64,2048]{1,0:T(8,128)(2,1)S(1)}, bf16[64,2048]{1,0:T(8,128)(2,1)S(1)}, u32[]{:S(2)}, u32[]{:S(2)}) collective-permute-start(bf16[64,2048]{1,0:T(8,128)(2,1)S(1)} %add_convert_fusion.10), channel_id=1, source_target_pairs={{0,4},{1,5},{2,6},{3,7},{4,0},{5,1},{6,2},{7,3},{8,12},{9,13},{10,... | collective-permute-start | bytes 786440 | tf_op jit(solution)/shard_map/ppermute | solution.py:25
  83.4 3.7 %collective-permute-done.18 = bf16[64,2048]{1,0:T(8,128)(2,1)S(1)} collective-permute-done((bf16[64,2048]{1,0:T(8,128)(2,1)S(1)}, bf16[64,2048]{1,0:T(8,128)(2,1)S(1)}, u32[]{:S(2)}, u32[]{:S(2)}) %collective-permute-start.18) | collective-permute-done | bytes 262176 | tf_op jit(solution)/shard_map/ppermute | solution.py:25
  87.1 5.0 %collective-permute-done.21 = bf16[64,2048]{1,0:T(8,128)(2,1)S(1)} collective-permute-done((bf16[64,2048]{1,0:T(8,128)(2,1)S(1)}, bf16[64,2048]{1,0:T(8,128)(2,1)S(1)}, u32[]{:S(2)}, u32[]{:S(2)}) %collective-permute-start.21) | collective-permute-done | bytes 262176 | tf_op jit(solution)/shard_map/ppermute | solution.py:25
  92.9 2.6 %collective-permute-start.27 = (bf16[64,1024]{1,0:T(8,128)(2,1)S(1)}, bf16[64,1024]{1,0:T(8,128)(2,1)S(1)}, u32[]{:S(2)}, u32[]{:S(2)}) collective-permute-start(bf16[64,1024]{1,0:T(8,128)(2,1)S(1)} %get-tuple-element.65), channel_id=1, source_target_pairs={{0,12},{1,13},{2,14},{3,15},{4,8},{5,9},{6,10},{7,11},{8,4},{9,5},... | collective-permute-start | bytes 393224 | tf_op jit(solution)/shard_map/ppermute | solution.py:25
  95.9 1.9 collective-permute-start.31
  98.6 2.6 %collective-permute-done.27 = bf16[64,1024]{1,0:T(8,128)(2,1)S(1)} collective-permute-done((bf16[64,1024]{1,0:T(8,128)(2,1)S(1)}, bf16[64,1024]{1,0:T(8,128)(2,1)S(1)}, u32[]{:S(2)}, u32[]{:S(2)}) %collective-permute-start.27) | collective-permute-done | bytes 131104 | tf_op jit(solution)/shard_map/ppermute | solution.py:25
  102.0 2.6 %collective-permute-start.28 = (bf16[64,2048]{1,0:T(8,128)(2,1)S(1)}, bf16[64,2048]{1,0:T(8,128)(2,1)S(1)}, u32[]{:S(2)}, u32[]{:S(2)}) collective-permute-start(bf16[64,2048]{1,0:T(8,128)(2,1)S(1)} %convolution_convert_fusion.6), channel_id=1, source_target_pairs={{0,12},{1,13},{2,14},{3,15},{4,8},{5,9},{6,10},{7,11},{8,4},{9,5},... | collective-permute-start | bytes 786440 | tf_op jit(solution)/shard_map/ppermute | solution.py:25
  104.7 6.2 %collective-permute-done.29 = bf16[64,1024]{1,0:T(8,128)(2,1)S(1)} collective-permute-done((bf16[64,1024]{1,0:T(8,128)(2,1)S(1)}, bf16[64,1024]{1,0:T(8,128)(2,1)S(1)}, u32[]{:S(2)}, u32[]{:S(2)}) %collective-permute-start.29) | collective-permute-done | bytes 131104 | tf_op jit(solution)/shard_map/ppermute | solution.py:25
  112.7 3.3 %collective-permute-start.32 = (bf16[64,2048]{1,0:T(8,128)(2,1)S(1)}, bf16[64,2048]{1,0:T(8,128)(2,1)S(1)}, u32[]{:S(2)}, u32[]{:S(2)}) collective-permute-start(bf16[64,2048]{1,0:T(8,128)(2,1)S(1)} %convolution_convert_fusion.4), channel_id=1, source_target_pairs={{0,4},{1,5},{2,6},{3,7},{4,0},{5,1},{6,2},{7,3},{8,12},{9,13},{10,... | collective-permute-start | bytes 786440 | tf_op jit(solution)/shard_map/ppermute | solution.py:25
  116.9 10.9 %collective-permute-done.30 = bf16[64,2048]{1,0:T(8,128)(2,1)S(1)} collective-permute-done((bf16[64,2048]{1,0:T(8,128)(2,1)S(1)}, bf16[64,2048]{1,0:T(8,128)(2,1)S(1)}, u32[]{:S(2)}, u32[]{:S(2)}) %collective-permute-start.30) | collective-permute-done | bytes 262176 | tf_op jit(solution)/shard_map/ppermute | solution.py:25
  128.0 2.0 copy-done.4
  131.1 2.6 %collective-permute-start.35 = (bf16[64,2048]{1,0:T(8,128)(2,1)S(1)}, bf16[64,2048]{1,0:T(8,128)(2,1)}, u32[]{:S(2)}, u32[]{:S(2)}) collective-permute-start(bf16[64,2048]{1,0:T(8,128)(2,1)S(1)} %fusion.25), channel_id=1, source_target_pairs={{0,12},{1,13},{2,14},{3,15},{4,8},{5,9},{6,10},{7,11},{8,4},{9,5},... | collective-permute-start | bytes 786440 | tf_op jit(solution)/shard_map/ppermute | solution.py:25
  133.7 4.7 %collective-permute-done.37 = bf16[64,2048]{1,0:T(8,128)(2,1)S(1)} collective-permute-done((bf16[64,2048]{1,0:T(8,128)(2,1)S(1)}, bf16[64,2048]{1,0:T(8,128)(2,1)S(1)}, u32[]{:S(2)}, u32[]{:S(2)}) %collective-permute-start.37) | collective-permute-done | bytes 262176 | tf_op jit(solution)/shard_map/ppermute | solution.py:31
  143.4 6.1 %collective-permute-start.40 = (bf16[64,2048]{1,0:T(8,128)(2,1)S(1)}, bf16[64,2048]{1,0:T(8,128)(2,1)S(1)}, u32[]{:S(2)}, u32[]{:S(2)}) collective-permute-start(bf16[64,2048]{1,0:T(8,128)(2,1)S(1)} %fusion.25), channel_id=1, source_target_pairs={{0,8},{1,9},{2,10},{3,11},{4,12},{5,13},{6,14},{7,15},{8,0},{9,1},... | collective-permute-start | bytes 786440 | tf_op jit(solution)/shard_map/ppermute | solution.py:25
  152.9 4.2 %collective-permute-done.40 = bf16[64,2048]{1,0:T(8,128)(2,1)S(1)} collective-permute-done((bf16[64,2048]{1,0:T(8,128)(2,1)S(1)}, bf16[64,2048]{1,0:T(8,128)(2,1)S(1)}, u32[]{:S(2)}, u32[]{:S(2)}) %collective-permute-start.40) | collective-permute-done | bytes 262176 | tf_op jit(solution)/shard_map/ppermute | solution.py:25
  159.3 1.3 fusion.100
  161.4 1.4 copy-done.5
  172.5 1.7 collective-permute-done.44
  174.3 9.0 %collective-permute-start.45 = (bf16[64,2048]{1,0:T(8,128)(2,1)S(1)}, bf16[64,2048]{1,0:T(8,128)(2,1)S(1)}, u32[]{:S(2)}, u32[]{:S(2)}) collective-permute-start(bf16[64,2048]{1,0:T(8,128)(2,1)S(1)} %add_convert_fusion.7), channel_id=1, source_target_pairs={{0,12},{1,13},{2,14},{3,15},{4,8},{5,9},{6,10},{7,11},{8,4},{9,5},... | collective-permute-start | bytes 786440 | tf_op jit(solution)/shard_map/ppermute | solution.py:25
  184.3 2.0 collective-permute-start.46
  187.4 2.3 %collective-permute-done.47 = bf16[64,2048]{1,0:T(8,128)(2,1)S(1)} collective-permute-done((bf16[64,2048]{1,0:T(8,128)(2,1)S(1)}, bf16[64,2048]{1,0:T(8,128)(2,1)S(1)}, u32[]{:S(2)}, u32[]{:S(2)}) %collective-permute-start.47) | collective-permute-done | bytes 262176 | tf_op jit(solution)/shard_map/ppermute | solution.py:31
  189.9 5.8 %collective-permute-done.46 = bf16[64,2048]{1,0:T(8,128)(2,1)S(1)} collective-permute-done((bf16[64,2048]{1,0:T(8,128)(2,1)S(1)}, bf16[64,2048]{1,0:T(8,128)(2,1)S(1)}, u32[]{:S(2)}, u32[]{:S(2)}) %collective-permute-start.46) | collective-permute-done | bytes 262176 | tf_op jit(solution)/shard_map/ppermute | solution.py:25
  195.7 2.7 %collective-permute-done.48 = bf16[64,2048]{1,0:T(8,128)(2,1)S(1)} collective-permute-done((bf16[64,2048]{1,0:T(8,128)(2,1)S(1)}, bf16[64,2048]{1,0:T(8,128)(2,1)S(1)}, u32[]{:S(2)}, u32[]{:S(2)}) %collective-permute-start.48) | collective-permute-done | bytes 262176 | tf_op jit(solution)/shard_map/ppermute | solution.py:25
  (179 shorter events, 48.5 us)
Async XLA Ops:
  3.4 10.8 %collective-permute-start.3 = (bf16[64,2176]{1,0:T(8,128)(2,1)S(1)}, bf16[64,2176]{1,0:T(8,128)(2,1)S(1)}, u32[]{:S(2)}, u32[]{:S(2)}) collective-permute-start(bf16[64,2176]{1,0:T(8,128)(2,1)S(1)} %pad_maximum_fusion.14), channel_id=1, source_target_pairs={{0,4},{1,5},{2,6},{3,7},{4,0},{5,1},{6,2},{7,3},{8,12},{9,13},{10,... | collective-permute-start | bytes 835592 | tf_op jit(solution)/shard_map/ppermute | solution.py:25
  6.5 16.1 %collective-permute-start.2 = (bf16[64,2176]{1,0:T(8,128)(2,1)S(1)}, bf16[64,2176]{1,0:T(8,128)(2,1)S(1)}, u32[]{:S(2)}, u32[]{:S(2)}) collective-permute-start(bf16[64,2176]{1,0:T(8,128)(2,1)S(1)} %pad_maximum_fusion.14), channel_id=1, source_target_pairs={{0,12},{1,13},{2,14},{3,15},{4,8},{5,9},{6,10},{7,11},{8,4},{9,5},... | collective-permute-start | bytes 835592 | tf_op jit(solution)/shard_map/ppermute | solution.py:25
  9.0 26.5 %collective-permute-start.7 = (bf16[64,2176]{1,0:T(8,128)(2,1)S(1)}, bf16[64,2176]{1,0:T(8,128)(2,1)}, u32[]{:S(2)}, u32[]{:S(2)}) collective-permute-start(bf16[64,2176]{1,0:T(8,128)(2,1)S(1)} %pad_maximum_fusion.14), channel_id=1, source_target_pairs={{0,8},{1,9},{2,10},{3,11},{4,12},{5,13},{6,14},{7,15},{8,0},{9,1},... | collective-permute-start | bytes 835592 | tf_op jit(solution)/shard_map/ppermute | solution.py:25
  9.1 9.6 %collective-permute-start = (bf16[64,2176]{1,0:T(8,128)(2,1)S(1)}, bf16[64,2176]{1,0:T(8,128)(2,1)S(1)}, u32[]{:S(2)}, u32[]{:S(2)}) collective-permute-start(bf16[64,2176]{1,0:T(8,128)(2,1)S(1)} %pad_maximum_fusion.14), channel_id=1, source_target_pairs={{0,2},{1,3},{2,0},{3,1},{4,6},{5,7},{6,4},{7,5},{8,10},{9,11},{10,... | collective-permute-start | bytes 835592 | tf_op jit(solution)/shard_map/ppermute | solution.py:31
  12.5 17.6 %collective-permute-start.22 = (bf16[64,2048]{1,0:T(8,128)(2,1)}, bf16[64,2048]{1,0:T(8,128)(2,1)}, u32[]{:S(2)}, u32[]{:S(2)}) collective-permute-start(bf16[64,2048]{1,0:T(8,128)(2,1)} %get-tuple-element.63), channel_id=1, source_target_pairs={{0,2},{1,3},{2,0},{3,1},{4,6},{5,7},{6,4},{7,5},{8,10},{9,11},{10,... | collective-permute-start | bytes 786440 | tf_op jit(solution)/shard_map/ppermute | solution.py:31
  14.2 14.3 %collective-permute-start.4 = (bf16[64,2176]{1,0:T(8,128)(2,1)S(1)}, bf16[64,2176]{1,0:T(8,128)(2,1)S(1)}, u32[]{:S(2)}, u32[]{:S(2)}) collective-permute-start(bf16[64,2176]{1,0:T(8,128)(2,1)S(1)} %collective-permute-done.3), channel_id=1, source_target_pairs={{0,2},{1,3},{2,0},{3,1},{4,6},{5,7},{6,4},{7,5},{8,10},{9,11},{10,... | collective-permute-start | bytes 835592 | tf_op jit(solution)/shard_map/ppermute | solution.py:31
  18.7 18.3 %collective-permute-start.1 = (bf16[128,2176]{1,0:T(8,128)(2,1)S(1)}, bf16[128,2176]{1,0:T(8,128)(2,1)S(1)}, u32[]{:S(2)}, u32[]{:S(2)}) collective-permute-start(bf16[128,2176]{1,0:T(8,128)(2,1)S(1)} %pad_maximum_fusion.6), channel_id=1, source_target_pairs={{0,1},{1,0},{2,3},{3,2},{4,5},{5,4},{6,7},{7,6},{8,9},{9,8},{10,11... | collective-permute-start | bytes 1671176 | tf_op jit(solution)/shard_map/ppermute | solution.py:31
  28.5 6.9 %collective-permute-start.5 = (bf16[64,2176]{1,0:T(8,128)(2,1)S(1)}, bf16[64,2176]{1,0:T(8,128)(2,1)S(1)}, u32[]{:S(2)}, u32[]{:S(2)}) collective-permute-start(bf16[64,2176]{1,0:T(8,128)(2,1)S(1)} %collective-permute-done.2), channel_id=1, source_target_pairs={{0,2},{1,3},{2,0},{3,1},{4,6},{5,7},{6,4},{7,5},{8,10},{9,11},{10,... | collective-permute-start | bytes 835592 | tf_op jit(solution)/shard_map/ppermute | solution.py:31
  30.1 16.3 %collective-permute-start.23 = (bf16[64,2048]{1,0:T(8,128)(2,1)}, bf16[64,2048]{1,0:T(8,128)(2,1)S(1)}, u32[]{:S(2)}, u32[]{:S(2)}) collective-permute-start(bf16[64,2048]{1,0:T(8,128)(2,1)} %collective-permute-done.22), channel_id=1, source_target_pairs={{0,16},{16,0},{1,17},{17,1},{2,18},{18,2},{3,19},{19,3},{4,20},{20... | collective-permute-start | bytes 786440 | tf_op jit(solution)/shard_map/ppermute | solution.py:147
  31.6 7.9 %collective-permute-start.10 = (bf16[128,2176]{1,0:T(8,128)(2,1)S(1)}, bf16[128,2176]{1,0:T(8,128)(2,1)S(1)}, u32[]{:S(2)}, u32[]{:S(2)}) collective-permute-start(bf16[128,2176]{1,0:T(8,128)(2,1)S(1)} %pad_maximum_fusion.9), channel_id=1, source_target_pairs={{0,1},{1,0},{2,3},{3,2},{4,5},{5,4},{6,7},{7,6},{8,9},{9,8},{10,11... | collective-permute-start | bytes 1671176 | tf_op jit(solution)/shard_map/ppermute | solution.py:31
  35.5 9.5 %collective-permute-start.8 = (bf16[64,2176]{1,0:T(8,128)(2,1)}, bf16[64,2176]{1,0:T(8,128)(2,1)S(1)}, u32[]{:S(2)}, u32[]{:S(2)}) collective-permute-start(bf16[64,2176]{1,0:T(8,128)(2,1)} %collective-permute-done.7), channel_id=1, source_target_pairs={{0,2},{1,3},{2,0},{3,1},{4,6},{5,7},{6,4},{7,5},{8,10},{9,11},{10,... | collective-permute-start | bytes 835592 | tf_op jit(solution)/shard_map/ppermute | solution.py:31
  37.2 4.8 %collective-permute-start.9 = (bf16[128,2176]{1,0:T(8,128)(2,1)S(1)}, bf16[128,2176]{1,0:T(8,128)(2,1)S(1)}, u32[]{:S(2)}, u32[]{:S(2)}) collective-permute-start(bf16[128,2176]{1,0:T(8,128)(2,1)S(1)} %pad_maximum_fusion.8), channel_id=1, source_target_pairs={{0,1},{1,0},{2,3},{3,2},{4,5},{5,4},{6,7},{7,6},{8,9},{9,8},{10,11... | collective-permute-start | bytes 1671176 | tf_op jit(solution)/shard_map/ppermute | solution.py:31
  44.4 4.2 %collective-permute-start.12 = (bf16[128,2048]{1,0:T(8,128)(2,1)S(1)}, bf16[128,2048]{1,0:T(8,128)(2,1)S(1)}, u32[]{:S(2)}, u32[]{:S(2)}) collective-permute-start(bf16[128,2048]{1,0:T(8,128)(2,1)S(1)} %slice.381), channel_id=1, source_target_pairs={{0,1},{1,0},{2,3},{3,2},{4,5},{5,4},{6,7},{7,6},{8,9},{9,8},{10,11... | collective-permute-start | bytes 1572872 | tf_op jit(solution)/shard_map/ppermute | solution.py:31
  47.4 4.5 %collective-permute-start.6 = (bf16[128,2048]{1,0:T(8,128)(2,1)S(1)}, bf16[128,2048]{1,0:T(8,128)(2,1)S(1)}, u32[]{:S(2)}, u32[]{:S(2)}) collective-permute-start(bf16[128,2048]{1,0:T(8,128)(2,1)S(1)} %slice.373), channel_id=1, source_target_pairs={{0,1},{1,0},{2,3},{3,2},{4,5},{5,4},{6,7},{7,6},{8,9},{9,8},{10,11... | collective-permute-start | bytes 1572872 | tf_op jit(solution)/shard_map/ppermute | solution.py:31
  48.0 17.4 %collective-permute-start.24 = (bf16[64,2048]{1,0:T(8,128)(2,1)S(1)}, bf16[64,2048]{1,0:T(8,128)(2,1)S(1)}, u32[]{:S(2)}, u32[]{:S(2)}) collective-permute-start(bf16[64,2048]{1,0:T(8,128)(2,1)S(1)} %copy-done.15), channel_id=1, source_target_pairs={{0,2},{1,3},{2,0},{3,1},{4,6},{5,7},{6,4},{7,5},{8,10},{9,11},{10,... | collective-permute-start | bytes 786440 | tf_op jit(solution)/shard_map/ppermute | solution.py:31
  48.6 3.5 %collective-permute-start.19 = (bf16[128,2048]{1,0:T(8,128)(2,1)S(1)}, bf16[128,2048]{1,0:T(8,128)(2,1)S(1)}, u32[]{:S(2)}, u32[]{:S(2)}) collective-permute-start(bf16[128,2048]{1,0:T(8,128)(2,1)S(1)} %slice.391), channel_id=1, source_target_pairs={{0,1},{1,0},{2,3},{3,2},{4,5},{5,4},{6,7},{7,6},{8,9},{9,8},{10,11... | collective-permute-start | bytes 1572872 | tf_op jit(solution)/shard_map/ppermute | solution.py:31
  48.6 79.4 %collective-permute-start.33 = (bf16[2048,1024]{1,0:T(8,128)(2,1)S(1)}, bf16[2048,1024]{1,0:T(8,128)(2,1)S(1)}, u32[]{:S(2)}, u32[]{:S(2)}) collective-permute-start(bf16[2048,1024]{1,0:T(8,128)(2,1)S(1)} %bitcast.63), channel_id=1, source_target_pairs={{0,1},{1,0},{2,3},{3,2},{4,5},{5,4},{6,7},{7,6},{8,9},{9,8},{10,11... | collective-permute-start | bytes 12582920 | tf_op jit(solution)/shard_map/ppermute | solution.py:31
  51.8 5.5 %collective-permute-start.13 = (bf16[128,2048]{1,0:T(8,128)(2,1)S(1)}, bf16[128,2048]{1,0:T(8,128)(2,1)S(1)}, u32[]{:S(2)}, u32[]{:S(2)}) collective-permute-start(bf16[128,2048]{1,0:T(8,128)(2,1)S(1)} %slice.385), channel_id=1, source_target_pairs={{0,1},{1,0},{2,3},{3,2},{4,5},{5,4},{6,7},{7,6},{8,9},{9,8},{10,11... | collective-permute-start | bytes 1572872 | tf_op jit(solution)/shard_map/ppermute | solution.py:31
  52.3 10.6 %collective-permute-start.16 = (bf16[64,2048]{1,0:T(8,128)(2,1)S(1)}, bf16[64,2048]{1,0:T(8,128)(2,1)S(1)}, u32[]{:S(2)}, u32[]{:S(2)}) collective-permute-start(bf16[64,2048]{1,0:T(8,128)(2,1)S(1)} %slice.388), channel_id=1, source_target_pairs={{0,2},{1,3},{2,0},{3,1},{4,6},{5,7},{6,4},{7,5},{8,10},{9,11},{10,... | collective-permute-start | bytes 786440 | tf_op jit(solution)/shard_map/ppermute | solution.py:31
  57.4 11.1 %collective-permute-start.14 = (bf16[64,2048]{1,0:T(8,128)(2,1)S(1)}, bf16[64,2048]{1,0:T(8,128)(2,1)S(1)}, u32[]{:S(2)}, u32[]{:S(2)}) collective-permute-start(bf16[64,2048]{1,0:T(8,128)(2,1)S(1)} %slice.386), channel_id=1, source_target_pairs={{0,2},{1,3},{2,0},{3,1},{4,6},{5,7},{6,4},{7,5},{8,10},{9,11},{10,... | collective-permute-start | bytes 786440 | tf_op jit(solution)/shard_map/ppermute | solution.py:31
  63.0 13.9 %collective-permute-start.17 = (bf16[64,2048]{1,0:T(8,128)(2,1)S(1)}, bf16[64,2048]{1,0:T(8,128)(2,1)S(1)}, u32[]{:S(2)}, u32[]{:S(2)}) collective-permute-start(bf16[64,2048]{1,0:T(8,128)(2,1)S(1)} %add_convert_fusion.12), channel_id=1, source_target_pairs={{0,12},{1,13},{2,14},{3,15},{4,8},{5,9},{6,10},{7,11},{8,4},{9,5},... | collective-permute-start | bytes 786440 | tf_op jit(solution)/shard_map/ppermute | solution.py:25
  65.4 11.4 %collective-permute-start.20 = (bf16[64,2048]{1,0:T(8,128)(2,1)S(1)}, bf16[64,2048]{1,0:T(8,128)(2,1)S(1)}, u32[]{:S(2)}, u32[]{:S(2)}) collective-permute-start(bf16[64,2048]{1,0:T(8,128)(2,1)S(1)} %slice.393), channel_id=1, source_target_pairs={{0,2},{1,3},{2,0},{3,1},{4,6},{5,7},{6,4},{7,5},{8,10},{9,11},{10,... | collective-permute-start | bytes 786440 | tf_op jit(solution)/shard_map/ppermute | solution.py:31
  68.5 6.5 %collective-permute-start.25 = (bf16[64,2048]{1,0:T(8,128)(2,1)S(1)}, bf16[64,2048]{1,0:T(8,128)(2,1)S(1)}, u32[]{:S(2)}, u32[]{:S(2)}) collective-permute-start(bf16[64,2048]{1,0:T(8,128)(2,1)S(1)} %collective-permute-done.24), channel_id=1, source_target_pairs={{0,16},{16,0},{1,17},{17,1},{2,18},{18,2},{3,19},{19,3},{4,20},{20... | collective-permute-start | bytes 786440 | tf_op jit(solution)/shard_map/ppermute | solution.py:147
  70.1 17.1 %collective-permute-start.18 = (bf16[64,2048]{1,0:T(8,128)(2,1)S(1)}, bf16[64,2048]{1,0:T(8,128)(2,1)S(1)}, u32[]{:S(2)}, u32[]{:S(2)}) collective-permute-start(bf16[64,2048]{1,0:T(8,128)(2,1)S(1)} %add_convert_fusion.11), channel_id=1, source_target_pairs={{0,8},{1,9},{2,10},{3,11},{4,12},{5,13},{6,14},{7,15},{8,0},{9,1},... | collective-permute-start | bytes 786440 | tf_op jit(solution)/shard_map/ppermute | solution.py:25
  75.0 12.2 %collective-permute-start.15 = (bf16[64,2048]{1,0:T(8,128)(2,1)S(1)}, bf16[64,2048]{1,0:T(8,128)(2,1)S(1)}, u32[]{:S(2)}, u32[]{:S(2)}) collective-permute-start(bf16[64,2048]{1,0:T(8,128)(2,1)S(1)} %slice.375), channel_id=1, source_target_pairs={{0,2},{1,3},{2,0},{3,1},{4,6},{5,7},{6,4},{7,5},{8,10},{9,11},{10,... | collective-permute-start | bytes 786440 | tf_op jit(solution)/shard_map/ppermute | solution.py:31
  76.8 19.1 %collective-permute-start.26 = (bf16[2,256,2048]{2,1,0:T(8,128)(2,1)S(1)}, bf16[2,256,2048]{2,1,0:T(8,128)(2,1)S(1)}, u32[]{:S(2)}, u32[]{:S(2)}) collective-permute-start(bf16[2,256,2048]{2,1,0:T(8,128)(2,1)S(1)} %maximum_select_fusion.1), channel_id=1, source_target_pairs={{0,1},{1,0},{2,3},{3,2},{4,5},{5,4},{6,7},{7,6},{8,9},{9,8},{10,11... | collective-permute-start | bytes 6291464 | tf_op jit(solution)/shard_map/ppermute | solution.py:31
  76.9 15.2 %collective-permute-start.21 = (bf16[64,2048]{1,0:T(8,128)(2,1)S(1)}, bf16[64,2048]{1,0:T(8,128)(2,1)S(1)}, u32[]{:S(2)}, u32[]{:S(2)}) collective-permute-start(bf16[64,2048]{1,0:T(8,128)(2,1)S(1)} %add_convert_fusion.10), channel_id=1, source_target_pairs={{0,4},{1,5},{2,6},{3,7},{4,0},{5,1},{6,2},{7,3},{8,12},{9,13},{10,... | collective-permute-start | bytes 786440 | tf_op jit(solution)/shard_map/ppermute | solution.py:25
  87.1 40.9 %collective-permute-start.34 = (bf16[512,2048]{1,0:T(8,128)(2,1)S(1)}, bf16[512,2048]{1,0:T(8,128)(2,1)S(1)}, u32[]{:S(2)}, u32[]{:S(2)}) collective-permute-start(bf16[512,2048]{1,0:T(8,128)(2,1)S(1)} %bitcast.64), channel_id=1, source_target_pairs={{0,1},{1,0},{2,3},{3,2},{4,5},{5,4},{6,7},{7,6},{8,9},{9,8},{10,11... | collective-permute-start | bytes 6291464 | tf_op jit(solution)/shard_map/ppermute | solution.py:31
  92.9 8.3 %collective-permute-start.27 = (bf16[64,1024]{1,0:T(8,128)(2,1)S(1)}, bf16[64,1024]{1,0:T(8,128)(2,1)S(1)}, u32[]{:S(2)}, u32[]{:S(2)}) collective-permute-start(bf16[64,1024]{1,0:T(8,128)(2,1)S(1)} %get-tuple-element.65), channel_id=1, source_target_pairs={{0,12},{1,13},{2,14},{3,15},{4,8},{5,9},{6,10},{7,11},{8,4},{9,5},... | collective-permute-start | bytes 393224 | tf_op jit(solution)/shard_map/ppermute | solution.py:25
  95.5 15.4 %collective-permute-start.29 = (bf16[64,1024]{1,0:T(8,128)(2,1)S(1)}, bf16[64,1024]{1,0:T(8,128)(2,1)S(1)}, u32[]{:S(2)}, u32[]{:S(2)}) collective-permute-start(bf16[64,1024]{1,0:T(8,128)(2,1)S(1)} %get-tuple-element.66), channel_id=1, source_target_pairs={{0,8},{1,9},{2,10},{3,11},{4,12},{5,13},{6,14},{7,15},{8,0},{9,1},... | collective-permute-start | bytes 393224 | tf_op jit(solution)/shard_map/ppermute | solution.py:25
  95.9 15.9 %collective-permute-start.31 = (bf16[64,1024]{1,0:T(8,128)(2,1)S(1)}, bf16[64,1024]{1,0:T(8,128)(2,1)S(1)}, u32[]{:S(2)}, u32[]{:S(2)}) collective-permute-start(bf16[64,1024]{1,0:T(8,128)(2,1)S(1)} %get-tuple-element.67), channel_id=1, source_target_pairs={{0,4},{1,5},{2,6},{3,7},{4,0},{5,1},{6,2},{7,3},{8,12},{9,13},{10,... | collective-permute-start | bytes 393224 | tf_op jit(solution)/shard_map/ppermute | solution.py:25
  102.0 14.8 %collective-permute-start.28 = (bf16[64,2048]{1,0:T(8,128)(2,1)S(1)}, bf16[64,2048]{1,0:T(8,128)(2,1)S(1)}, u32[]{:S(2)}, u32[]{:S(2)}) collective-permute-start(bf16[64,2048]{1,0:T(8,128)(2,1)S(1)} %convolution_convert_fusion.6), channel_id=1, source_target_pairs={{0,12},{1,13},{2,14},{3,15},{4,8},{5,9},{6,10},{7,11},{8,4},{9,5},... | collective-permute-start | bytes 786440 | tf_op jit(solution)/shard_map/ppermute | solution.py:25
  111.7 16.0 %collective-permute-start.30 = (bf16[64,2048]{1,0:T(8,128)(2,1)S(1)}, bf16[64,2048]{1,0:T(8,128)(2,1)S(1)}, u32[]{:S(2)}, u32[]{:S(2)}) collective-permute-start(bf16[64,2048]{1,0:T(8,128)(2,1)S(1)} %convolution_convert_fusion.5), channel_id=1, source_target_pairs={{0,8},{1,9},{2,10},{3,11},{4,12},{5,13},{6,14},{7,15},{8,0},{9,1},... | collective-permute-start | bytes 786440 | tf_op jit(solution)/shard_map/ppermute | solution.py:25
  112.7 15.1 %collective-permute-start.32 = (bf16[64,2048]{1,0:T(8,128)(2,1)S(1)}, bf16[64,2048]{1,0:T(8,128)(2,1)S(1)}, u32[]{:S(2)}, u32[]{:S(2)}) collective-permute-start(bf16[64,2048]{1,0:T(8,128)(2,1)S(1)} %convolution_convert_fusion.4), channel_id=1, source_target_pairs={{0,4},{1,5},{2,6},{3,7},{4,0},{5,1},{6,2},{7,3},{8,12},{9,13},{10,... | collective-permute-start | bytes 786440 | tf_op jit(solution)/shard_map/ppermute | solution.py:25
  130.0 8.3 %collective-permute-start.37 = (bf16[64,2048]{1,0:T(8,128)(2,1)S(1)}, bf16[64,2048]{1,0:T(8,128)(2,1)S(1)}, u32[]{:S(2)}, u32[]{:S(2)}) collective-permute-start(bf16[64,2048]{1,0:T(8,128)(2,1)S(1)} %fusion.25), channel_id=1, source_target_pairs={{0,2},{1,3},{2,0},{3,1},{4,6},{5,7},{6,4},{7,5},{8,10},{9,11},{10,... | collective-permute-start | bytes 786440 | tf_op jit(solution)/shard_map/ppermute | solution.py:31
  131.1 8.3 %collective-permute-start.36 = (bf16[64,2048]{1,0:T(8,128)(2,1)S(1)}, bf16[64,2048]{1,0:T(8,128)(2,1)}, u32[]{:S(2)}, u32[]{:S(2)}) collective-permute-start(bf16[64,2048]{1,0:T(8,128)(2,1)S(1)} %fusion.25), channel_id=1, source_target_pairs={{0,4},{1,5},{2,6},{3,7},{4,0},{5,1},{6,2},{7,3},{8,12},{9,13},{10,... | collective-permute-start | bytes 786440 | tf_op jit(solution)/shard_map/ppermute | solution.py:25
  131.1 18.4 %collective-permute-start.35 = (bf16[64,2048]{1,0:T(8,128)(2,1)S(1)}, bf16[64,2048]{1,0:T(8,128)(2,1)}, u32[]{:S(2)}, u32[]{:S(2)}) collective-permute-start(bf16[64,2048]{1,0:T(8,128)(2,1)S(1)} %fusion.25), channel_id=1, source_target_pairs={{0,12},{1,13},{2,14},{3,15},{4,8},{5,9},{6,10},{7,11},{8,4},{9,5},... | collective-permute-start | bytes 786440 | tf_op jit(solution)/shard_map/ppermute | solution.py:25
  139.4 10.1 %collective-permute-start.38 = (bf16[64,2048]{1,0:T(8,128)(2,1)}, bf16[64,2048]{1,0:T(8,128)(2,1)}, u32[]{:S(2)}, u32[]{:S(2)}) collective-permute-start(bf16[64,2048]{1,0:T(8,128)(2,1)} %collective-permute-done.36), channel_id=1, source_target_pairs={{0,2},{1,3},{2,0},{3,1},{4,6},{5,7},{6,4},{7,5},{8,10},{9,11},{10,... | collective-permute-start | bytes 786440 | tf_op jit(solution)/shard_map/ppermute | solution.py:31
  143.4 13.8 %collective-permute-start.40 = (bf16[64,2048]{1,0:T(8,128)(2,1)S(1)}, bf16[64,2048]{1,0:T(8,128)(2,1)S(1)}, u32[]{:S(2)}, u32[]{:S(2)}) collective-permute-start(bf16[64,2048]{1,0:T(8,128)(2,1)S(1)} %fusion.25), channel_id=1, source_target_pairs={{0,8},{1,9},{2,10},{3,11},{4,12},{5,13},{6,14},{7,15},{8,0},{9,1},... | collective-permute-start | bytes 786440 | tf_op jit(solution)/shard_map/ppermute | solution.py:25
  149.5 7.7 %collective-permute-start.39 = (bf16[64,2048]{1,0:T(8,128)(2,1)}, bf16[64,2048]{1,0:T(8,128)(2,1)S(1)}, u32[]{:S(2)}, u32[]{:S(2)}) collective-permute-start(bf16[64,2048]{1,0:T(8,128)(2,1)} %collective-permute-done.35), channel_id=1, source_target_pairs={{0,2},{1,3},{2,0},{3,1},{4,6},{5,7},{6,4},{7,5},{8,10},{9,11},{10,... | collective-permute-start | bytes 786440 | tf_op jit(solution)/shard_map/ppermute | solution.py:31
  158.2 10.7 %collective-permute-start.41 = (bf16[64,2048]{1,0:T(8,128)(2,1)S(1)}, bf16[64,2048]{1,0:T(8,128)(2,1)S(1)}, u32[]{:S(2)}, u32[]{:S(2)}) collective-permute-start(bf16[64,2048]{1,0:T(8,128)(2,1)S(1)} %collective-permute-done.40), channel_id=1, source_target_pairs={{0,2},{1,3},{2,0},{3,1},{4,6},{5,7},{6,4},{7,5},{8,10},{9,11},{10,... | collective-permute-start | bytes 786440 | tf_op jit(solution)/shard_map/ppermute | solution.py:31
  167.8 6.4 %collective-permute-start.44 = (bf16[64,2048]{1,0:T(8,128)(2,1)S(1)}, bf16[64,2048]{1,0:T(8,128)(2,1)S(1)}, u32[]{:S(2)}, u32[]{:S(2)}) collective-permute-start(bf16[64,2048]{1,0:T(8,128)(2,1)S(1)} %get-tuple-element.60), channel_id=1, source_target_pairs={{0,2},{1,3},{2,0},{3,1},{4,6},{5,7},{6,4},{7,5},{8,10},{9,11},{10,... | collective-permute-start | bytes 786440 | tf_op jit(solution)/shard_map/ppermute | solution.py:31
  171.5 12.8 %collective-permute-start.42 = (bf16[64,2048]{1,0:T(8,128)(2,1)S(1)}, bf16[64,2048]{1,0:T(8,128)(2,1)S(1)}, u32[]{:S(2)}, u32[]{:S(2)}) collective-permute-start(bf16[64,2048]{1,0:T(8,128)(2,1)S(1)} %slice.412), channel_id=1, source_target_pairs={{0,2},{1,3},{2,0},{3,1},{4,6},{5,7},{6,4},{7,5},{8,10},{9,11},{10,... | collective-permute-start | bytes 786440 | tf_op jit(solution)/shard_map/ppermute | solution.py:31
  174.3 15.6 %collective-permute-start.45 = (bf16[64,2048]{1,0:T(8,128)(2,1)S(1)}, bf16[64,2048]{1,0:T(8,128)(2,1)S(1)}, u32[]{:S(2)}, u32[]{:S(2)}) collective-permute-start(bf16[64,2048]{1,0:T(8,128)(2,1)S(1)} %add_convert_fusion.7), channel_id=1, source_target_pairs={{0,12},{1,13},{2,14},{3,15},{4,8},{5,9},{6,10},{7,11},{8,4},{9,5},... | collective-permute-start | bytes 786440 | tf_op jit(solution)/shard_map/ppermute | solution.py:25
  183.2 6.4 %collective-permute-start.47 = (bf16[64,2048]{1,0:T(8,128)(2,1)S(1)}, bf16[64,2048]{1,0:T(8,128)(2,1)S(1)}, u32[]{:S(2)}, u32[]{:S(2)}) collective-permute-start(bf16[64,2048]{1,0:T(8,128)(2,1)S(1)} %slice.417), channel_id=1, source_target_pairs={{0,2},{1,3},{2,0},{3,1},{4,6},{5,7},{6,4},{7,5},{8,10},{9,11},{10,... | collective-permute-start | bytes 786440 | tf_op jit(solution)/shard_map/ppermute | solution.py:31
  184.3 11.4 %collective-permute-start.46 = (bf16[64,2048]{1,0:T(8,128)(2,1)S(1)}, bf16[64,2048]{1,0:T(8,128)(2,1)S(1)}, u32[]{:S(2)}, u32[]{:S(2)}) collective-permute-start(bf16[64,2048]{1,0:T(8,128)(2,1)S(1)} %add_convert_fusion.6), channel_id=1, source_target_pairs={{0,8},{1,9},{2,10},{3,11},{4,12},{5,13},{6,14},{7,15},{8,0},{9,1},... | collective-permute-start | bytes 786440 | tf_op jit(solution)/shard_map/ppermute | solution.py:25
  186.3 9.4 %collective-permute-start.43 = (bf16[64,2048]{1,0:T(8,128)(2,1)S(1)}, bf16[64,2048]{1,0:T(8,128)(2,1)S(1)}, u32[]{:S(2)}, u32[]{:S(2)}) collective-permute-start(bf16[64,2048]{1,0:T(8,128)(2,1)S(1)} %get-tuple-element.49), channel_id=1, source_target_pairs={{0,2},{1,3},{2,0},{3,1},{4,6},{5,7},{6,4},{7,5},{8,10},{9,11},{10,... | collective-permute-start | bytes 786440 | tf_op jit(solution)/shard_map/ppermute | solution.py:31
  189.7 8.8 %collective-permute-start.48 = (bf16[64,2048]{1,0:T(8,128)(2,1)S(1)}, bf16[64,2048]{1,0:T(8,128)(2,1)S(1)}, u32[]{:S(2)}, u32[]{:S(2)}) collective-permute-start(bf16[64,2048]{1,0:T(8,128)(2,1)S(1)} %add_convert_fusion.5), channel_id=1, source_target_pairs={{0,4},{1,5},{2,6},{3,7},{4,0},{5,1},{6,2},{7,3},{8,12},{9,13},{10,... | collective-permute-start | bytes 786440 | tf_op jit(solution)/shard_map/ppermute | solution.py:25
  (21 other events, 184.1 us)

commit v16 on v14

--- a/solution.py
+++ b/solution.py
@@ -91,7 +91,8 @@
     columns = {0: rows}
     for slot in (1, 3, 2):
         columns[slot] = ring.between(rows, slot)
-    crossed = {slot: ring.across(columns[slot], top) for slot in (0, 1)}
+    crossed = {0: ring.across(rows, top)}
+    crossed[1] = ring.across(after(columns[1], crossed[0]) if paired else columns[1], top)
     crossed[3] = ring.across(after(columns[3], crossed[1]), top)
     crossed[2] = ring.across(after(columns[2], crossed[3]), top)
 
@@ -106,12 +107,11 @@
 
     halves = {}
     if paired:
-        third = work((3,), after(chunk(3), crossed[3]))
-        halves[3] = halve(third)
-        both = work((0, 1), after(jnp.concatenate([chunk(0), chunk(1)], axis=0), third))
-        last = work((2,), after(chunk(2), both, halves[3]))
+        both = work((3, 0), after(jnp.concatenate([chunk(3), chunk(0)], axis=0), crossed[3]))
         count = both.shape[0] // 2
-        done = {0: both[:count], 1: both[count:]}
+        halves[3] = halve(both[:count])
+        done = {0: both[count:], 1: work((1,), after(chunk(1), both))}
+        last = work((2,), after(chunk(2), done[1], halves[3]))
     else:
         done = {}
         ties = [crossed[3]]

time: 208 us -> 209 us (level)
    ppermute x29, waiting for transfers between devices: 24.9 us -> 28.3 us  [across(): lax.ppermute(values, 'inner', [(d, d ^ bit) for d in range(self.size)])]
    ppermute x18, waiting for transfers between devices: 48.4 us -> 45.7 us  [send(): return lax.ppermute(values, 'inner', perm)]
  transfers between devices with their start and end apart: 49 -> 49, of which waited for: 19 -> 20; matrix products, arithmetic and copies ran while one was open for 28% -> 28% of each run, Pallas kernels for 0% -> 0%
where the time goes in v16:
time: 209 us; the launch traced here: 208 us
  waiting for transfers between devices  77.3 us (37%)
  starting transfers between devices  67.6 us (32%)
  matrix products  34.2 us (16%)
  other arithmetic  24.8 us (12%)
  local copies, waits for them, and re-layouts  3.77 us (2%)
    ppermute x18, waiting for transfers between devices, send(): return lax.ppermute(values, 'inner', perm)  45.7 us
    ppermute x18, starting transfers between devices, send(): return lax.ppermute(values, 'inner', perm)  41.3 us
    ppermute x29, waiting for transfers between devices, across(): lax.ppermute(values, 'inner', [(d, d ^ bit) for d in range(self.size)])  28.3 us
    dot_general x10, matrix products, experts(): projected = jnp.dot(rows, gate_up, preferred_element_type=jnp.float32)  23.8 us
    ppermute x29, starting transfers between devices, across(): lax.ppermute(values, 'inner', [(d, d ^ bit) for d in range(self.size)])  23.2 us
    dot_general x10, matrix products, experts(): jnp.dot(hidden.astype(jnp.bfloat16), down, preferred_element_type=jnp.flo...  7.07 us
    reduce_sum x8, other arithmetic, gate_column(): jnp.sum(jnp.where(named == who.astype(jnp.float32), high + low, 0.0), axi...  5.05 us
  transfers between devices with their start and end apart: 49, of which 20 were waited for; matrix products, arithmetic and copies ran while one was open for 28% of the time, Pallas kernels for 0%

profile of v16, /device:TPU:0, one launch (start us, length us, event | category | flops | bytes accessed | tf_op | source)
XLA Modules:
  0.0 208.5 jit_solution(9298110386094289362)
XLA Ops:
  3.4 3.1 %collective-permute-start.3 = (bf16[64,2176]{1,0:T(8,128)(2,1)S(1)}, bf16[64,2176]{1,0:T(8,128)(2,1)S(1)}, u32[]{:S(2)}, u32[]{:S(2)}) collective-permute-start(bf16[64,2176]{1,0:T(8,128)(2,1)S(1)} %pad_maximum_fusion.14), channel_id=1, source_target_pairs={{0,4},{1,5},{2,6},{3,7},{4,0},{5,1},{6,2},{7,3},{8,12},{9,13},{10,... | collective-permute-start | bytes 835592 | tf_op jit(solution)/shard_map/ppermute | solution.py:25
  6.5 2.5 %collective-permute-start.2 = (bf16[64,2176]{1,0:T(8,128)(2,1)S(1)}, bf16[64,2176]{1,0:T(8,128)(2,1)S(1)}, u32[]{:S(2)}, u32[]{:S(2)}) collective-permute-start(bf16[64,2176]{1,0:T(8,128)(2,1)S(1)} %pad_maximum_fusion.14), channel_id=1, source_target_pairs={{0,12},{1,13},{2,14},{3,15},{4,8},{5,9},{6,10},{7,11},{8,4},{9,5},... | collective-permute-start | bytes 835592 | tf_op jit(solution)/shard_map/ppermute | solution.py:25
  9.1 1.5 collective-permute-start
  10.6 1.9 constant_dynamic-slice_fusion.1
  14.1 1.6 collective-permute-start.4
  15.7 3.1 %collective-permute-done = bf16[64,2176]{1,0:T(8,128)(2,1)} collective-permute-done((bf16[64,2176]{1,0:T(8,128)(2,1)S(1)}, bf16[64,2176]{1,0:T(8,128)(2,1)}, u32[]{:S(2)}, u32[]{:S(2)}) %collective-permute-start) | collective-permute-done | bytes 278560 | tf_op jit(solution)/shard_map/ppermute | solution.py:31
  19.9 2.7 %collective-permute-done.2 = bf16[64,2176]{1,0:T(8,128)(2,1)S(1)} collective-permute-done((bf16[64,2176]{1,0:T(8,128)(2,1)S(1)}, bf16[64,2176]{1,0:T(8,128)(2,1)S(1)}, u32[]{:S(2)}, u32[]{:S(2)}) %collective-permute-start.2) | collective-permute-done | bytes 278560 | tf_op jit(solution)/shard_map/ppermute | solution.py:25
  22.5 6.0 %collective-permute-done.4 = bf16[64,2176]{1,0:T(8,128)(2,1)S(1)} collective-permute-done((bf16[64,2176]{1,0:T(8,128)(2,1)S(1)}, bf16[64,2176]{1,0:T(8,128)(2,1)S(1)}, u32[]{:S(2)}, u32[]{:S(2)}) %collective-permute-start.4) | collective-permute-done | bytes 278560 | tf_op jit(solution)/shard_map/ppermute | solution.py:31
  28.5 1.5 collective-permute-start.5
  30.1 1.6 collective-permute-start.23
  31.6 3.8 %collective-permute-done.5 = bf16[64,2176]{1,0:T(8,128)(2,1)S(1)} collective-permute-done((bf16[64,2176]{1,0:T(8,128)(2,1)S(1)}, bf16[64,2176]{1,0:T(8,128)(2,1)S(1)}, u32[]{:S(2)}, u32[]{:S(2)}) %collective-permute-start.5) | collective-permute-done | bytes 278560 | tf_op jit(solution)/shard_map/ppermute | solution.py:31
  35.5 1.6 collective-permute-start.8
  51.6 1.6 collective-permute-start.16
  53.2 2.7 %collective-permute-done.13 = bf16[128,2048]{1,0:T(8,128)(2,1)S(1)} collective-permute-done((bf16[128,2048]{1,0:T(8,128)(2,1)S(1)}, bf16[128,2048]{1,0:T(8,128)(2,1)S(1)}, u32[]{:S(2)}, u32[]{:S(2)}) %collective-permute-start.13) | collective-permute-done | bytes 524320 | tf_op jit(solution)/shard_map/ppermute | solution.py:31
  56.1 1.6 collective-permute-start.14
  57.7 3.2 %collective-permute-done.16 = bf16[64,2048]{1,0:T(8,128)(2,1)S(1)} collective-permute-done((bf16[64,2048]{1,0:T(8,128)(2,1)S(1)}, bf16[64,2048]{1,0:T(8,128)(2,1)S(1)}, u32[]{:S(2)}, u32[]{:S(2)}) %collective-permute-start.16) | collective-permute-done | bytes 262176 | tf_op jit(solution)/shard_map/ppermute | solution.py:31
  60.9 2.5 %collective-permute-start.17 = (bf16[64,2048]{1,0:T(8,128)(2,1)S(1)}, bf16[64,2048]{1,0:T(8,128)(2,1)S(1)}, u32[]{:S(2)}, u32[]{:S(2)}) collective-permute-start(bf16[64,2048]{1,0:T(8,128)(2,1)S(1)} %add_convert_fusion.12), channel_id=1, source_target_pairs={{0,12},{1,13},{2,14},{3,15},{4,8},{5,9},{6,10},{7,11},{8,4},{9,5},... | collective-permute-start | bytes 786440 | tf_op jit(solution)/shard_map/ppermute | solution.py:25
  63.4 1.4 collective-permute-start.20
  64.9 1.6 collective-permute-done.14
  66.5 1.5 collective-permute-start.25
  68.7 2.3 %collective-permute-start.18 = (bf16[64,2048]{1,0:T(8,128)(2,1)}, bf16[64,2048]{1,0:T(8,128)(2,1)}, u32[]{:S(2)}, u32[]{:S(2)}) collective-permute-start(bf16[64,2048]{1,0:T(8,128)(2,1)} %add_convert_fusion.11), channel_id=1, source_target_pairs={{0,8},{1,9},{2,10},{3,11},{4,12},{5,13},{6,14},{7,15},{8,0},{9,1},... | collective-permute-start | bytes 786440 | tf_op jit(solution)/shard_map/ppermute | solution.py:25
  71.1 3.3 %collective-permute-done.25 = bf16[64,2048]{1,0:T(8,128)(2,1)S(1)} collective-permute-done((bf16[64,2048]{1,0:T(8,128)(2,1)S(1)}, bf16[64,2048]{1,0:T(8,128)(2,1)S(1)}, u32[]{:S(2)}, u32[]{:S(2)}) %collective-permute-start.25) | collective-permute-done | bytes 262176 | tf_op jit(solution)/shard_map/ppermute | solution.py:147
  76.7 1.7 maximum_select_fusion.1
  79.9 3.4 %collective-permute-start.21 = (bf16[64,2048]{1,0:T(8,128)(2,1)}, bf16[64,2048]{1,0:T(8,128)(2,1)}, u32[]{:S(2)}, u32[]{:S(2)}) collective-permute-start(bf16[64,2048]{1,0:T(8,128)(2,1)} %add_convert_fusion.10), channel_id=1, source_target_pairs={{0,4},{1,5},{2,6},{3,7},{4,0},{5,1},{6,2},{7,3},{8,12},{9,13},{10,... | collective-permute-start | bytes 786440 | tf_op jit(solution)/shard_map/ppermute | solution.py:25
  86.7 5.5 %collective-permute-done.21 = bf16[64,2048]{1,0:T(8,128)(2,1)} collective-permute-done((bf16[64,2048]{1,0:T(8,128)(2,1)}, bf16[64,2048]{1,0:T(8,128)(2,1)}, u32[]{:S(2)}, u32[]{:S(2)}) %collective-permute-start.21) | collective-permute-done | bytes 262176 | tf_op jit(solution)/shard_map/ppermute | solution.py:25
  92.2 1.6 fusion.22
  94.2 2.5 %collective-permute-start.27 = (bf16[64,1024]{1,0:T(8,128)(2,1)S(1)}, bf16[64,1024]{1,0:T(8,128)(2,1)S(1)}, u32[]{:S(2)}, u32[]{:S(2)}) collective-permute-start(bf16[64,1024]{1,0:T(8,128)(2,1)S(1)} %get-tuple-element.69), channel_id=1, source_target_pairs={{0,12},{1,13},{2,14},{3,15},{4,8},{5,9},{6,10},{7,11},{8,4},{9,5},... | collective-permute-start | bytes 393224 | tf_op jit(solution)/shard_map/ppermute | solution.py:25
  97.1 2.0 collective-permute-start.31
  99.1 3.0 %maximum_select_fusion = bf16[2,2,256,2048]{3,2,1,0:T(8,128)(2,1)S(1)} fusion(bf16[2,1,256,2048]{3,2,1,0:T(8,128)(2,1)S(1)} %maximum_select_fusion.2, bf16[2,1,256,2048]{3,2,1,0:T(8,128)(2,1)} %bitcast.4, pred[]{:T(512)S(6)} %eq.75), kind=kLoop, calls=%fused_computation | loop fusion | flops 6291456 | bytes 8388609 | tf_op jit(solution)/shard_map/jit(_where)/select_n | solution.py:157
  103.4 2.5 %collective-permute-start.28 = (bf16[64,2048]{1,0:T(8,128)(2,1)S(1)}, bf16[64,2048]{1,0:T(8,128)(2,1)S(1)}, u32[]{:S(2)}, u32[]{:S(2)}) collective-permute-start(bf16[64,2048]{1,0:T(8,128)(2,1)S(1)} %convolution_convert_fusion.6), channel_id=1, source_target_pairs={{0,12},{1,13},{2,14},{3,15},{4,8},{5,9},{6,10},{7,11},{8,4},{9,5},... | collective-permute-start | bytes 786440 | tf_op jit(solution)/shard_map/ppermute | solution.py:25
  105.9 1.8 collective-permute-done.29
  109.4 3.1 %collective-permute-start.32 = (bf16[64,2048]{1,0:T(8,128)(2,1)S(1)}, bf16[64,2048]{1,0:T(8,128)(2,1)S(1)}, u32[]{:S(2)}, u32[]{:S(2)}) collective-permute-start(bf16[64,2048]{1,0:T(8,128)(2,1)S(1)} %convolution_convert_fusion.4), channel_id=1, source_target_pairs={{0,4},{1,5},{2,6},{3,7},{4,0},{5,1},{6,2},{7,3},{8,12},{9,13},{10,... | collective-permute-start | bytes 786440 | tf_op jit(solution)/shard_map/ppermute | solution.py:25
  113.9 15.7 %collective-permute-done.30 = bf16[64,2048]{1,0:T(8,128)(2,1)S(1)} collective-permute-done((bf16[64,2048]{1,0:T(8,128)(2,1)S(1)}, bf16[64,2048]{1,0:T(8,128)(2,1)S(1)}, u32[]{:S(2)}, u32[]{:S(2)}) %collective-permute-start.30) | collective-permute-done | bytes 262176 | tf_op jit(solution)/shard_map/ppermute | solution.py:25
  132.2 2.5 %collective-permute-start.35 = (bf16[64,2048]{1,0:T(8,128)(2,1)S(1)}, bf16[64,2048]{1,0:T(8,128)(2,1)S(1)}, u32[]{:S(2)}, u32[]{:S(2)}) collective-permute-start(bf16[64,2048]{1,0:T(8,128)(2,1)S(1)} %fusion.25), channel_id=1, source_target_pairs={{0,12},{1,13},{2,14},{3,15},{4,8},{5,9},{6,10},{7,11},{8,4},{9,5},... | collective-permute-start | bytes 786440 | tf_op jit(solution)/shard_map/ppermute | solution.py:25
  134.7 3.4 %collective-permute-done.37 = bf16[64,2048]{1,0:T(8,128)(2,1)S(1)} collective-permute-done((bf16[64,2048]{1,0:T(8,128)(2,1)S(1)}, bf16[64,2048]{1,0:T(8,128)(2,1)S(1)}, u32[]{:S(2)}, u32[]{:S(2)}) %collective-permute-start.37) | collective-permute-done | bytes 262176 | tf_op jit(solution)/shard_map/ppermute | solution.py:31
  141.1 5.3 %collective-permute-start.40 = (bf16[64,2048]{1,0:T(8,128)(2,1)S(1)}, bf16[64,2048]{1,0:T(8,128)(2,1)S(1)}, u32[]{:S(2)}, u32[]{:S(2)}) collective-permute-start(bf16[64,2048]{1,0:T(8,128)(2,1)S(1)} %fusion.25), channel_id=1, source_target_pairs={{0,8},{1,9},{2,10},{3,11},{4,12},{5,13},{6,14},{7,15},{8,0},{9,1},... | collective-permute-start | bytes 786440 | tf_op jit(solution)/shard_map/ppermute | solution.py:25
  147.6 10.6 %collective-permute-done.40 = bf16[64,2048]{1,0:T(8,128)(2,1)S(1)} collective-permute-done((bf16[64,2048]{1,0:T(8,128)(2,1)S(1)}, bf16[64,2048]{1,0:T(8,128)(2,1)S(1)}, u32[]{:S(2)}, u32[]{:S(2)}) %collective-permute-start.40) | collective-permute-done | bytes 262176 | tf_op jit(solution)/shard_map/ppermute | solution.py:25
  159.3 3.5 %fusion.98 = f32[256,1024]{1,0:T(8,128)S(1)} fusion(bf16[256,2048]{1,0:T(8,128)(2,1)S(1)} %pad_maximum_fusion.5, bf16[1,2048,1024]{2,1,0:T(8,128)(2,1)} %param.21), kind=kOutput, calls=%fused_computation.193 | convolution fusion | flops 1073741824 | bytes 6291456 | tf_op jit(solution)/shard_map/dot_general | solution.py:82
  163.6 3.5 %fusion.111 = f32[256,1024]{1,0:T(8,128)S(1)} fusion(bf16[256,2048]{1,0:T(8,128)(2,1)S(1)} %pad_maximum_fusion.5, bf16[2048,1024]{1,0:T(8,128)(2,1)} %collective-permute-done.33), kind=kOutput, calls=%fused_computation.206 | convolution fusion | flops 1073741824 | bytes 6291456 | tf_op jit(solution)/shard_map/dot_general | solution.py:82
  168.0 2.9 %fusion.96 = f32[128,1024]{1,0:T(8,128)S(1)} fusion(bf16[128,2048]{1,0:T(8,128)(2,1)S(1)} %pad_maximum_fusion.13, bf16[1,2048,1024]{2,1,0:T(8,128)(2,1)} %param.21), kind=kOutput, calls=%fused_computation.191 | convolution fusion | flops 536870912 | bytes 5242880 | tf_op jit(solution)/shard_map/dot_general | solution.py:82
  171.5 2.9 %fusion.112 = f32[128,1024]{1,0:T(8,128)S(1)} fusion(bf16[128,2048]{1,0:T(8,128)(2,1)S(1)} %pad_maximum_fusion.13, bf16[2048,1024]{1,0:T(8,128)(2,1)} %collective-permute-done.33), kind=kOutput, calls=%fused_computation.207 | convolution fusion | flops 536870912 | bytes 5242880 | tf_op jit(solution)/shard_map/dot_general | solution.py:82
  176.3 2.9 %fusion.94 = f32[128,1024]{1,0:T(8,128)S(1)} fusion(bf16[128,2048]{1,0:T(8,128)(2,1)S(1)} %pad_maximum_fusion.12, bf16[1,2048,1024]{2,1,0:T(8,128)(2,1)} %param.21), kind=kOutput, calls=%fused_computation.189 | convolution fusion | flops 536870912 | bytes 5242880 | tf_op jit(solution)/shard_map/dot_general | solution.py:82
  179.7 2.9 %fusion.113 = f32[128,1024]{1,0:T(8,128)S(1)} fusion(bf16[128,2048]{1,0:T(8,128)(2,1)S(1)} %pad_maximum_fusion.12, bf16[2048,1024]{1,0:T(8,128)(2,1)} %collective-permute-done.33), kind=kOutput, calls=%fused_computation.208 | convolution fusion | flops 536870912 | bytes 5242880 | tf_op jit(solution)/shard_map/dot_general | solution.py:82
  184.3 2.5 %collective-permute-start.45 = (bf16[64,2048]{1,0:T(8,128)(2,1)S(1)}, bf16[64,2048]{1,0:T(8,128)(2,1)S(1)}, u32[]{:S(2)}, u32[]{:S(2)}) collective-permute-start(bf16[64,2048]{1,0:T(8,128)(2,1)S(1)} %add_convert_fusion.7), channel_id=1, source_target_pairs={{0,12},{1,13},{2,14},{3,15},{4,8},{5,9},{6,10},{7,11},{8,4},{9,5},... | collective-permute-start | bytes 786440 | tf_op jit(solution)/shard_map/ppermute | solution.py:25
  188.0 4.5 %collective-permute-done.42 = bf16[64,2048]{1,0:T(8,128)(2,1)S(1)} collective-permute-done((bf16[64,2048]{1,0:T(8,128)(2,1)S(1)}, bf16[64,2048]{1,0:T(8,128)(2,1)S(1)}, u32[]{:S(2)}, u32[]{:S(2)}) %collective-permute-start.42) | collective-permute-done | bytes 262176 | tf_op jit(solution)/shard_map/ppermute | solution.py:31
  192.6 5.2 %collective-permute-start.46 = (bf16[64,2048]{1,0:T(8,128)(2,1)S(1)}, bf16[64,2048]{1,0:T(8,128)(2,1)S(1)}, u32[]{:S(2)}, u32[]{:S(2)}) collective-permute-start(bf16[64,2048]{1,0:T(8,128)(2,1)S(1)} %add_convert_fusion.6), channel_id=1, source_target_pairs={{0,8},{1,9},{2,10},{3,11},{4,12},{5,13},{6,14},{7,15},{8,0},{9,1},... | collective-permute-start | bytes 786440 | tf_op jit(solution)/shard_map/ppermute | solution.py:25
  198.7 1.7 collective-permute-start.48
  200.4 6.3 %collective-permute-done.46 = bf16[64,2048]{1,0:T(8,128)(2,1)S(1)} collective-permute-done((bf16[64,2048]{1,0:T(8,128)(2,1)S(1)}, bf16[64,2048]{1,0:T(8,128)(2,1)S(1)}, u32[]{:S(2)}, u32[]{:S(2)}) %collective-permute-start.46) | collective-permute-done | bytes 262176 | tf_op jit(solution)/shard_map/ppermute | solution.py:25
  (176 shorter events, 51.7 us)
Async XLA Ops:
  3.4 10.7 %collective-permute-start.3 = (bf16[64,2176]{1,0:T(8,128)(2,1)S(1)}, bf16[64,2176]{1,0:T(8,128)(2,1)S(1)}, u32[]{:S(2)}, u32[]{:S(2)}) collective-permute-start(bf16[64,2176]{1,0:T(8,128)(2,1)S(1)} %pad_maximum_fusion.14), channel_id=1, source_target_pairs={{0,4},{1,5},{2,6},{3,7},{4,0},{5,1},{6,2},{7,3},{8,12},{9,13},{10,... | collective-permute-start | bytes 835592 | tf_op jit(solution)/shard_map/ppermute | solution.py:25
  6.5 16.1 %collective-permute-start.2 = (bf16[64,2176]{1,0:T(8,128)(2,1)S(1)}, bf16[64,2176]{1,0:T(8,128)(2,1)S(1)}, u32[]{:S(2)}, u32[]{:S(2)}) collective-permute-start(bf16[64,2176]{1,0:T(8,128)(2,1)S(1)} %pad_maximum_fusion.14), channel_id=1, source_target_pairs={{0,12},{1,13},{2,14},{3,15},{4,8},{5,9},{6,10},{7,11},{8,4},{9,5},... | collective-permute-start | bytes 835592 | tf_op jit(solution)/shard_map/ppermute | solution.py:25
  9.0 26.5 %collective-permute-start.7 = (bf16[64,2176]{1,0:T(8,128)(2,1)S(1)}, bf16[64,2176]{1,0:T(8,128)(2,1)S(1)}, u32[]{:S(2)}, u32[]{:S(2)}) collective-permute-start(bf16[64,2176]{1,0:T(8,128)(2,1)S(1)} %pad_maximum_fusion.14), channel_id=1, source_target_pairs={{0,8},{1,9},{2,10},{3,11},{4,12},{5,13},{6,14},{7,15},{8,0},{9,1},... | collective-permute-start | bytes 835592 | tf_op jit(solution)/shard_map/ppermute | solution.py:25
  9.1 9.7 %collective-permute-start = (bf16[64,2176]{1,0:T(8,128)(2,1)S(1)}, bf16[64,2176]{1,0:T(8,128)(2,1)}, u32[]{:S(2)}, u32[]{:S(2)}) collective-permute-start(bf16[64,2176]{1,0:T(8,128)(2,1)S(1)} %pad_maximum_fusion.14), channel_id=1, source_target_pairs={{0,2},{1,3},{2,0},{3,1},{4,6},{5,7},{6,4},{7,5},{8,10},{9,11},{10,... | collective-permute-start | bytes 835592 | tf_op jit(solution)/shard_map/ppermute | solution.py:31
  12.5 17.6 %collective-permute-start.22 = (bf16[64,2048]{1,0:T(8,128)(2,1)}, bf16[64,2048]{1,0:T(8,128)(2,1)}, u32[]{:S(2)}, u32[]{:S(2)}) collective-permute-start(bf16[64,2048]{1,0:T(8,128)(2,1)} %get-tuple-element.67), channel_id=1, source_target_pairs={{0,2},{1,3},{2,0},{3,1},{4,6},{5,7},{6,4},{7,5},{8,10},{9,11},{10,... | collective-permute-start | bytes 786440 | tf_op jit(solution)/shard_map/ppermute | solution.py:31
  14.1 14.4 %collective-permute-start.4 = (bf16[64,2176]{1,0:T(8,128)(2,1)S(1)}, bf16[64,2176]{1,0:T(8,128)(2,1)S(1)}, u32[]{:S(2)}, u32[]{:S(2)}) collective-permute-start(bf16[64,2176]{1,0:T(8,128)(2,1)S(1)} %collective-permute-done.3), channel_id=1, source_target_pairs={{0,2},{1,3},{2,0},{3,1},{4,6},{5,7},{6,4},{7,5},{8,10},{9,11},{10,... | collective-permute-start | bytes 835592 | tf_op jit(solution)/shard_map/ppermute | solution.py:31
  19.8 17.3 %collective-permute-start.1 = (bf16[128,2176]{1,0:T(8,128)(2,1)S(1)}, bf16[128,2176]{1,0:T(8,128)(2,1)S(1)}, u32[]{:S(2)}, u32[]{:S(2)}) collective-permute-start(bf16[128,2176]{1,0:T(8,128)(2,1)S(1)} %pad_maximum_fusion.6), channel_id=1, source_target_pairs={{0,1},{1,0},{2,3},{3,2},{4,5},{5,4},{6,7},{7,6},{8,9},{9,8},{10,11... | collective-permute-start | bytes 1671176 | tf_op jit(solution)/shard_map/ppermute | solution.py:31
  28.5 6.9 %collective-permute-start.5 = (bf16[64,2176]{1,0:T(8,128)(2,1)S(1)}, bf16[64,2176]{1,0:T(8,128)(2,1)S(1)}, u32[]{:S(2)}, u32[]{:S(2)}) collective-permute-start(bf16[64,2176]{1,0:T(8,128)(2,1)S(1)} %collective-permute-done.2), channel_id=1, source_target_pairs={{0,2},{1,3},{2,0},{3,1},{4,6},{5,7},{6,4},{7,5},{8,10},{9,11},{10,... | collective-permute-start | bytes 835592 | tf_op jit(solution)/shard_map/ppermute | solution.py:31
  30.1 15.0 %collective-permute-start.23 = (bf16[64,2048]{1,0:T(8,128)(2,1)}, bf16[64,2048]{1,0:T(8,128)(2,1)S(1)}, u32[]{:S(2)}, u32[]{:S(2)}) collective-permute-start(bf16[64,2048]{1,0:T(8,128)(2,1)} %collective-permute-done.22), channel_id=1, source_target_pairs={{0,16},{16,0},{1,17},{17,1},{2,18},{18,2},{3,19},{19,3},{4,20},{20... | collective-permute-start | bytes 786440 | tf_op jit(solution)/shard_map/ppermute | solution.py:147
  31.6 7.9 %collective-permute-start.10 = (bf16[128,2176]{1,0:T(8,128)(2,1)S(1)}, bf16[128,2176]{1,0:T(8,128)(2,1)S(1)}, u32[]{:S(2)}, u32[]{:S(2)}) collective-permute-start(bf16[128,2176]{1,0:T(8,128)(2,1)S(1)} %pad_maximum_fusion.9), channel_id=1, source_target_pairs={{0,1},{1,0},{2,3},{3,2},{4,5},{5,4},{6,7},{7,6},{8,9},{9,8},{10,11... | collective-permute-start | bytes 1671176 | tf_op jit(solution)/shard_map/ppermute | solution.py:31
  35.5 9.4 %collective-permute-start.8 = (bf16[64,2176]{1,0:T(8,128)(2,1)S(1)}, bf16[64,2176]{1,0:T(8,128)(2,1)S(1)}, u32[]{:S(2)}, u32[]{:S(2)}) collective-permute-start(bf16[64,2176]{1,0:T(8,128)(2,1)S(1)} %collective-permute-done.7), channel_id=1, source_target_pairs={{0,2},{1,3},{2,0},{3,1},{4,6},{5,7},{6,4},{7,5},{8,10},{9,11},{10,... | collective-permute-start | bytes 835592 | tf_op jit(solution)/shard_map/ppermute | solution.py:31
  37.2 4.8 %collective-permute-start.9 = (bf16[128,2176]{1,0:T(8,128)(2,1)S(1)}, bf16[128,2176]{1,0:T(8,128)(2,1)S(1)}, u32[]{:S(2)}, u32[]{:S(2)}) collective-permute-start(bf16[128,2176]{1,0:T(8,128)(2,1)S(1)} %pad_maximum_fusion.8), channel_id=1, source_target_pairs={{0,1},{1,0},{2,3},{3,2},{4,5},{5,4},{6,7},{7,6},{8,9},{9,8},{10,11... | collective-permute-start | bytes 1671176 | tf_op jit(solution)/shard_map/ppermute | solution.py:31
  45.0 3.0 %collective-permute-start.11 = (bf16[128,2176]{1,0:T(8,128)(2,1)S(1)}, bf16[128,2176]{1,0:T(8,128)(2,1)S(1)}, u32[]{:S(2)}, u32[]{:S(2)}) collective-permute-start(bf16[128,2176]{1,0:T(8,128)(2,1)S(1)} %pad_maximum_fusion.7), channel_id=1, source_target_pairs={{0,1},{1,0},{2,3},{3,2},{4,5},{5,4},{6,7},{7,6},{8,9},{9,8},{10,11... | collective-permute-start | bytes 1671176 | tf_op jit(solution)/shard_map/ppermute | solution.py:31
  46.1 4.4 %collective-permute-start.6 = (bf16[128,2048]{1,0:T(8,128)(2,1)S(1)}, bf16[128,2048]{1,0:T(8,128)(2,1)S(1)}, u32[]{:S(2)}, u32[]{:S(2)}) collective-permute-start(bf16[128,2048]{1,0:T(8,128)(2,1)S(1)} %slice.397), channel_id=1, source_target_pairs={{0,1},{1,0},{2,3},{3,2},{4,5},{5,4},{6,7},{7,6},{8,9},{9,8},{10,11... | collective-permute-start | bytes 1572872 | tf_op jit(solution)/shard_map/ppermute | solution.py:31
  46.7 18.2 %collective-permute-start.24 = (bf16[64,2048]{1,0:T(8,128)(2,1)S(1)}, bf16[64,2048]{1,0:T(8,128)(2,1)S(1)}, u32[]{:S(2)}, u32[]{:S(2)}) collective-permute-start(bf16[64,2048]{1,0:T(8,128)(2,1)S(1)} %copy-done.13), channel_id=1, source_target_pairs={{0,2},{1,3},{2,0},{3,1},{4,6},{5,7},{6,4},{7,5},{8,10},{9,11},{10,... | collective-permute-start | bytes 786440 | tf_op jit(solution)/shard_map/ppermute | solution.py:31
  47.3 4.1 %collective-permute-start.19 = (bf16[128,2048]{1,0:T(8,128)(2,1)S(1)}, bf16[128,2048]{1,0:T(8,128)(2,1)S(1)}, u32[]{:S(2)}, u32[]{:S(2)}) collective-permute-start(bf16[128,2048]{1,0:T(8,128)(2,1)S(1)} %slice.415), channel_id=1, source_target_pairs={{0,1},{1,0},{2,3},{3,2},{4,5},{5,4},{6,7},{7,6},{8,9},{9,8},{10,11... | collective-permute-start | bytes 1572872 | tf_op jit(solution)/shard_map/ppermute | solution.py:31
  47.3 82.5 %collective-permute-start.33 = (bf16[2048,1024]{1,0:T(8,128)(2,1)}, bf16[2048,1024]{1,0:T(8,128)(2,1)}, u32[]{:S(2)}, u32[]{:S(2)}) collective-permute-start(bf16[2048,1024]{1,0:T(8,128)(2,1)} %bitcast.12), channel_id=1, source_target_pairs={{0,1},{1,0},{2,3},{3,2},{4,5},{5,4},{6,7},{7,6},{8,9},{9,8},{10,11... | collective-permute-start | bytes 12582920 | tf_op jit(solution)/shard_map/ppermute | solution.py:31
  50.4 5.5 %collective-permute-start.13 = (bf16[128,2048]{1,0:T(8,128)(2,1)S(1)}, bf16[128,2048]{1,0:T(8,128)(2,1)S(1)}, u32[]{:S(2)}, u32[]{:S(2)}) collective-permute-start(bf16[128,2048]{1,0:T(8,128)(2,1)S(1)} %slice.409), channel_id=1, source_target_pairs={{0,1},{1,0},{2,3},{3,2},{4,5},{5,4},{6,7},{7,6},{8,9},{9,8},{10,11... | collective-permute-start | bytes 1572872 | tf_op jit(solution)/shard_map/ppermute | solution.py:31
  51.6 9.2 %collective-permute-start.16 = (bf16[64,2048]{1,0:T(8,128)(2,1)S(1)}, bf16[64,2048]{1,0:T(8,128)(2,1)S(1)}, u32[]{:S(2)}, u32[]{:S(2)}) collective-permute-start(bf16[64,2048]{1,0:T(8,128)(2,1)S(1)} %slice.412), channel_id=1, source_target_pairs={{0,2},{1,3},{2,0},{3,1},{4,6},{5,7},{6,4},{7,5},{8,10},{9,11},{10,... | collective-permute-start | bytes 786440 | tf_op jit(solution)/shard_map/ppermute | solution.py:31
  56.1 10.4 %collective-permute-start.14 = (bf16[64,2048]{1,0:T(8,128)(2,1)S(1)}, bf16[64,2048]{1,0:T(8,128)(2,1)S(1)}, u32[]{:S(2)}, u32[]{:S(2)}) collective-permute-start(bf16[64,2048]{1,0:T(8,128)(2,1)S(1)} %slice.410), channel_id=1, source_target_pairs={{0,2},{1,3},{2,0},{3,1},{4,6},{5,7},{6,4},{7,5},{8,10},{9,11},{10,... | collective-permute-start | bytes 786440 | tf_op jit(solution)/shard_map/ppermute | solution.py:31
  60.9 18.3 %collective-permute-start.17 = (bf16[64,2048]{1,0:T(8,128)(2,1)S(1)}, bf16[64,2048]{1,0:T(8,128)(2,1)S(1)}, u32[]{:S(2)}, u32[]{:S(2)}) collective-permute-start(bf16[64,2048]{1,0:T(8,128)(2,1)S(1)} %add_convert_fusion.12), channel_id=1, source_target_pairs={{0,12},{1,13},{2,14},{3,15},{4,8},{5,9},{6,10},{7,11},{8,4},{9,5},... | collective-permute-start | bytes 786440 | tf_op jit(solution)/shard_map/ppermute | solution.py:25
  63.4 15.0 %collective-permute-start.20 = (bf16[64,2048]{1,0:T(8,128)(2,1)S(1)}, bf16[64,2048]{1,0:T(8,128)(2,1)S(1)}, u32[]{:S(2)}, u32[]{:S(2)}) collective-permute-start(bf16[64,2048]{1,0:T(8,128)(2,1)S(1)} %slice.417), channel_id=1, source_target_pairs={{0,2},{1,3},{2,0},{3,1},{4,6},{5,7},{6,4},{7,5},{8,10},{9,11},{10,... | collective-permute-start | bytes 786440 | tf_op jit(solution)/shard_map/ppermute | solution.py:31
  66.5 7.8 %collective-permute-start.25 = (bf16[64,2048]{1,0:T(8,128)(2,1)S(1)}, bf16[64,2048]{1,0:T(8,128)(2,1)S(1)}, u32[]{:S(2)}, u32[]{:S(2)}) collective-permute-start(bf16[64,2048]{1,0:T(8,128)(2,1)S(1)} %collective-permute-done.24), channel_id=1, source_target_pairs={{0,16},{16,0},{1,17},{17,1},{2,18},{18,2},{3,19},{19,3},{4,20},{20... | collective-permute-start | bytes 786440 | tf_op jit(solution)/shard_map/ppermute | solution.py:147
  68.7 17.9 %collective-permute-start.18 = (bf16[64,2048]{1,0:T(8,128)(2,1)}, bf16[64,2048]{1,0:T(8,128)(2,1)}, u32[]{:S(2)}, u32[]{:S(2)}) collective-permute-start(bf16[64,2048]{1,0:T(8,128)(2,1)} %add_convert_fusion.11), channel_id=1, source_target_pairs={{0,8},{1,9},{2,10},{3,11},{4,12},{5,13},{6,14},{7,15},{8,0},{9,1},... | collective-permute-start | bytes 786440 | tf_op jit(solution)/shard_map/ppermute | solution.py:25
  74.3 12.3 %collective-permute-start.15 = (bf16[64,2048]{1,0:T(8,128)(2,1)}, bf16[64,2048]{1,0:T(8,128)(2,1)}, u32[]{:S(2)}, u32[]{:S(2)}) collective-permute-start(bf16[64,2048]{1,0:T(8,128)(2,1)} %slice.399), channel_id=1, source_target_pairs={{0,2},{1,3},{2,0},{3,1},{4,6},{5,7},{6,4},{7,5},{8,10},{9,11},{10,... | collective-permute-start | bytes 786440 | tf_op jit(solution)/shard_map/ppermute | solution.py:31
  78.4 18.6 %collective-permute-start.26 = (bf16[2,256,2048]{2,1,0:T(8,128)(2,1)}, bf16[2,256,2048]{2,1,0:T(8,128)(2,1)}, u32[]{:S(2)}, u32[]{:S(2)}) collective-permute-start(bf16[2,256,2048]{2,1,0:T(8,128)(2,1)} %maximum_select_fusion.1), channel_id=1, source_target_pairs={{0,1},{1,0},{2,3},{3,2},{4,5},{5,4},{6,7},{7,6},{8,9},{9,8},{10,11... | collective-permute-start | bytes 6291464 | tf_op jit(solution)/shard_map/ppermute | solution.py:31
  79.9 12.3 %collective-permute-start.21 = (bf16[64,2048]{1,0:T(8,128)(2,1)}, bf16[64,2048]{1,0:T(8,128)(2,1)}, u32[]{:S(2)}, u32[]{:S(2)}) collective-permute-start(bf16[64,2048]{1,0:T(8,128)(2,1)} %add_convert_fusion.10), channel_id=1, source_target_pairs={{0,4},{1,5},{2,6},{3,7},{4,0},{5,1},{6,2},{7,3},{8,12},{9,13},{10,... | collective-permute-start | bytes 786440 | tf_op jit(solution)/shard_map/ppermute | solution.py:25
  86.7 43.2 %collective-permute-start.34 = (bf16[512,2048]{1,0:T(8,128)(2,1)S(1)}, bf16[512,2048]{1,0:T(8,128)(2,1)S(1)}, u32[]{:S(2)}, u32[]{:S(2)}) collective-permute-start(bf16[512,2048]{1,0:T(8,128)(2,1)S(1)} %bitcast.69), channel_id=1, source_target_pairs={{0,1},{1,0},{2,3},{3,2},{4,5},{5,4},{6,7},{7,6},{8,9},{9,8},{10,11... | collective-permute-start | bytes 6291464 | tf_op jit(solution)/shard_map/ppermute | solution.py:31
  94.2 8.3 %collective-permute-start.27 = (bf16[64,1024]{1,0:T(8,128)(2,1)S(1)}, bf16[64,1024]{1,0:T(8,128)(2,1)S(1)}, u32[]{:S(2)}, u32[]{:S(2)}) collective-permute-start(bf16[64,1024]{1,0:T(8,128)(2,1)S(1)} %get-tuple-element.69), channel_id=1, source_target_pairs={{0,12},{1,13},{2,14},{3,15},{4,8},{5,9},{6,10},{7,11},{8,4},{9,5},... | collective-permute-start | bytes 393224 | tf_op jit(solution)/shard_map/ppermute | solution.py:25
  96.7 10.9 %collective-permute-start.29 = (bf16[64,1024]{1,0:T(8,128)(2,1)S(1)}, bf16[64,1024]{1,0:T(8,128)(2,1)S(1)}, u32[]{:S(2)}, u32[]{:S(2)}) collective-permute-start(bf16[64,1024]{1,0:T(8,128)(2,1)S(1)} %get-tuple-element.70), channel_id=1, source_target_pairs={{0,8},{1,9},{2,10},{3,11},{4,12},{5,13},{6,14},{7,15},{8,0},{9,1},... | collective-permute-start | bytes 393224 | tf_op jit(solution)/shard_map/ppermute | solution.py:25
  97.1 11.5 %collective-permute-start.31 = (bf16[64,1024]{1,0:T(8,128)(2,1)S(1)}, bf16[64,1024]{1,0:T(8,128)(2,1)S(1)}, u32[]{:S(2)}, u32[]{:S(2)}) collective-permute-start(bf16[64,1024]{1,0:T(8,128)(2,1)S(1)} %get-tuple-element.71), channel_id=1, source_target_pairs={{0,4},{1,5},{2,6},{3,7},{4,0},{5,1},{6,2},{7,3},{8,12},{9,13},{10,... | collective-permute-start | bytes 393224 | tf_op jit(solution)/shard_map/ppermute | solution.py:25
  103.4 10.5 %collective-permute-start.28 = (bf16[64,2048]{1,0:T(8,128)(2,1)S(1)}, bf16[64,2048]{1,0:T(8,128)(2,1)S(1)}, u32[]{:S(2)}, u32[]{:S(2)}) collective-permute-start(bf16[64,2048]{1,0:T(8,128)(2,1)S(1)} %convolution_convert_fusion.6), channel_id=1, source_target_pairs={{0,12},{1,13},{2,14},{3,15},{4,8},{5,9},{6,10},{7,11},{8,4},{9,5},... | collective-permute-start | bytes 786440 | tf_op jit(solution)/shard_map/ppermute | solution.py:25
  108.5 21.0 %collective-permute-start.30 = (bf16[64,2048]{1,0:T(8,128)(2,1)S(1)}, bf16[64,2048]{1,0:T(8,128)(2,1)S(1)}, u32[]{:S(2)}, u32[]{:S(2)}) collective-permute-start(bf16[64,2048]{1,0:T(8,128)(2,1)S(1)} %convolution_convert_fusion.5), channel_id=1, source_target_pairs={{0,8},{1,9},{2,10},{3,11},{4,12},{5,13},{6,14},{7,15},{8,0},{9,1},... | collective-permute-start | bytes 786440 | tf_op jit(solution)/shard_map/ppermute | solution.py:25
  109.4 20.1 %collective-permute-start.32 = (bf16[64,2048]{1,0:T(8,128)(2,1)S(1)}, bf16[64,2048]{1,0:T(8,128)(2,1)S(1)}, u32[]{:S(2)}, u32[]{:S(2)}) collective-permute-start(bf16[64,2048]{1,0:T(8,128)(2,1)S(1)} %convolution_convert_fusion.4), channel_id=1, source_target_pairs={{0,4},{1,5},{2,6},{3,7},{4,0},{5,1},{6,2},{7,3},{8,12},{9,13},{10,... | collective-permute-start | bytes 786440 | tf_op jit(solution)/shard_map/ppermute | solution.py:25
  129.8 8.3 %collective-permute-start.37 = (bf16[64,2048]{1,0:T(8,128)(2,1)S(1)}, bf16[64,2048]{1,0:T(8,128)(2,1)S(1)}, u32[]{:S(2)}, u32[]{:S(2)}) collective-permute-start(bf16[64,2048]{1,0:T(8,128)(2,1)S(1)} %fusion.25), channel_id=1, source_target_pairs={{0,2},{1,3},{2,0},{3,1},{4,6},{5,7},{6,4},{7,5},{8,10},{9,11},{10,... | collective-permute-start | bytes 786440 | tf_op jit(solution)/shard_map/ppermute | solution.py:31
  131.0 8.2 %collective-permute-start.36 = (bf16[64,2048]{1,0:T(8,128)(2,1)S(1)}, bf16[64,2048]{1,0:T(8,128)(2,1)S(1)}, u32[]{:S(2)}, u32[]{:S(2)}) collective-permute-start(bf16[64,2048]{1,0:T(8,128)(2,1)S(1)} %fusion.25), channel_id=1, source_target_pairs={{0,4},{1,5},{2,6},{3,7},{4,0},{5,1},{6,2},{7,3},{8,12},{9,13},{10,... | collective-permute-start | bytes 786440 | tf_op jit(solution)/shard_map/ppermute | solution.py:25
  132.2 14.3 %collective-permute-start.35 = (bf16[64,2048]{1,0:T(8,128)(2,1)S(1)}, bf16[64,2048]{1,0:T(8,128)(2,1)S(1)}, u32[]{:S(2)}, u32[]{:S(2)}) collective-permute-start(bf16[64,2048]{1,0:T(8,128)(2,1)S(1)} %fusion.25), channel_id=1, source_target_pairs={{0,12},{1,13},{2,14},{3,15},{4,8},{5,9},{6,10},{7,11},{8,4},{9,5},... | collective-permute-start | bytes 786440 | tf_op jit(solution)/shard_map/ppermute | solution.py:25
  139.2 7.3 %collective-permute-start.38 = (bf16[64,2048]{1,0:T(8,128)(2,1)S(1)}, bf16[64,2048]{1,0:T(8,128)(2,1)S(1)}, u32[]{:S(2)}, u32[]{:S(2)}) collective-permute-start(bf16[64,2048]{1,0:T(8,128)(2,1)S(1)} %collective-permute-done.36), channel_id=1, source_target_pairs={{0,2},{1,3},{2,0},{3,1},{4,6},{5,7},{6,4},{7,5},{8,10},{9,11},{10,... | collective-permute-start | bytes 786440 | tf_op jit(solution)/shard_map/ppermute | solution.py:31
  141.1 17.1 %collective-permute-start.40 = (bf16[64,2048]{1,0:T(8,128)(2,1)S(1)}, bf16[64,2048]{1,0:T(8,128)(2,1)S(1)}, u32[]{:S(2)}, u32[]{:S(2)}) collective-permute-start(bf16[64,2048]{1,0:T(8,128)(2,1)S(1)} %fusion.25), channel_id=1, source_target_pairs={{0,8},{1,9},{2,10},{3,11},{4,12},{5,13},{6,14},{7,15},{8,0},{9,1},... | collective-permute-start | bytes 786440 | tf_op jit(solution)/shard_map/ppermute | solution.py:25
  146.5 11.7 %collective-permute-start.39 = (bf16[64,2048]{1,0:T(8,128)(2,1)S(1)}, bf16[64,2048]{1,0:T(8,128)(2,1)S(1)}, u32[]{:S(2)}, u32[]{:S(2)}) collective-permute-start(bf16[64,2048]{1,0:T(8,128)(2,1)S(1)} %collective-permute-done.35), channel_id=1, source_target_pairs={{0,2},{1,3},{2,0},{3,1},{4,6},{5,7},{6,4},{7,5},{8,10},{9,11},{10,... | collective-permute-start | bytes 786440 | tf_op jit(solution)/shard_map/ppermute | solution.py:31
  158.3 18.0 %collective-permute-start.41 = (bf16[64,2048]{1,0:T(8,128)(2,1)S(1)}, bf16[64,2048]{1,0:T(8,128)(2,1)S(1)}, u32[]{:S(2)}, u32[]{:S(2)}) collective-permute-start(bf16[64,2048]{1,0:T(8,128)(2,1)S(1)} %collective-permute-done.40), channel_id=1, source_target_pairs={{0,2},{1,3},{2,0},{3,1},{4,6},{5,7},{6,4},{7,5},{8,10},{9,11},{10,... | collective-permute-start | bytes 786440 | tf_op jit(solution)/shard_map/ppermute | solution.py:31
  175.0 9.2 %collective-permute-start.44 = (bf16[64,2048]{1,0:T(8,128)(2,1)S(1)}, bf16[64,2048]{1,0:T(8,128)(2,1)S(1)}, u32[]{:S(2)}, u32[]{:S(2)}) collective-permute-start(bf16[64,2048]{1,0:T(8,128)(2,1)S(1)} %get-tuple-element.64), channel_id=1, source_target_pairs={{0,2},{1,3},{2,0},{3,1},{4,6},{5,7},{6,4},{7,5},{8,10},{9,11},{10,... | collective-permute-start | bytes 786440 | tf_op jit(solution)/shard_map/ppermute | solution.py:31
  183.3 9.2 %collective-permute-start.42 = (bf16[64,2048]{1,0:T(8,128)(2,1)S(1)}, bf16[64,2048]{1,0:T(8,128)(2,1)S(1)}, u32[]{:S(2)}, u32[]{:S(2)}) collective-permute-start(bf16[64,2048]{1,0:T(8,128)(2,1)S(1)} %slice.432), channel_id=1, source_target_pairs={{0,2},{1,3},{2,0},{3,1},{4,6},{5,7},{6,4},{7,5},{8,10},{9,11},{10,... | collective-permute-start | bytes 786440 | tf_op jit(solution)/shard_map/ppermute | solution.py:31
  184.3 16.1 %collective-permute-start.45 = (bf16[64,2048]{1,0:T(8,128)(2,1)S(1)}, bf16[64,2048]{1,0:T(8,128)(2,1)S(1)}, u32[]{:S(2)}, u32[]{:S(2)}) collective-permute-start(bf16[64,2048]{1,0:T(8,128)(2,1)S(1)} %add_convert_fusion.7), channel_id=1, source_target_pairs={{0,12},{1,13},{2,14},{3,15},{4,8},{5,9},{6,10},{7,11},{8,4},{9,5},... | collective-permute-start | bytes 786440 | tf_op jit(solution)/shard_map/ppermute | solution.py:25
  186.9 11.8 %collective-permute-start.47 = (bf16[64,2048]{1,0:T(8,128)(2,1)S(1)}, bf16[64,2048]{1,0:T(8,128)(2,1)S(1)}, u32[]{:S(2)}, u32[]{:S(2)}) collective-permute-start(bf16[64,2048]{1,0:T(8,128)(2,1)S(1)} %slice.437), channel_id=1, source_target_pairs={{0,2},{1,3},{2,0},{3,1},{4,6},{5,7},{6,4},{7,5},{8,10},{9,11},{10,... | collective-permute-start | bytes 786440 | tf_op jit(solution)/shard_map/ppermute | solution.py:31
  192.6 14.1 %collective-permute-start.46 = (bf16[64,2048]{1,0:T(8,128)(2,1)S(1)}, bf16[64,2048]{1,0:T(8,128)(2,1)S(1)}, u32[]{:S(2)}, u32[]{:S(2)}) collective-permute-start(bf16[64,2048]{1,0:T(8,128)(2,1)S(1)} %add_convert_fusion.6), channel_id=1, source_target_pairs={{0,8},{1,9},{2,10},{3,11},{4,12},{5,13},{6,14},{7,15},{8,0},{9,1},... | collective-permute-start | bytes 786440 | tf_op jit(solution)/shard_map/ppermute | solution.py:25
  197.7 9.0 %collective-permute-start.43 = (bf16[64,2048]{1,0:T(8,128)(2,1)S(1)}, bf16[64,2048]{1,0:T(8,128)(2,1)S(1)}, u32[]{:S(2)}, u32[]{:S(2)}) collective-permute-start(bf16[64,2048]{1,0:T(8,128)(2,1)S(1)} %get-tuple-element.51), channel_id=1, source_target_pairs={{0,2},{1,3},{2,0},{3,1},{4,6},{5,7},{6,4},{7,5},{8,10},{9,11},{10,... | collective-permute-start | bytes 786440 | tf_op jit(solution)/shard_map/ppermute | solution.py:31
  198.7 8.8 %collective-permute-start.48 = (bf16[64,2048]{1,0:T(8,128)(2,1)S(1)}, bf16[64,2048]{1,0:T(8,128)(2,1)S(1)}, u32[]{:S(2)}, u32[]{:S(2)}) collective-permute-start(bf16[64,2048]{1,0:T(8,128)(2,1)S(1)} %add_convert_fusion.5), channel_id=1, source_target_pairs={{0,4},{1,5},{2,6},{3,7},{4,0},{5,1},{6,2},{7,3},{8,12},{9,13},{10,... | collective-permute-start | bytes 786440 | tf_op jit(solution)/shard_map/ppermute | solution.py:25
  (19 other events, 182.8 us)

commit v17 on v15

--- a/solution.py
+++ b/solution.py
@@ -119,7 +119,8 @@
             done[slot] = work((slot,), after(chunk(slot), *ties))
             ties = [done[slot]]
         halves[3] = halve(done[3])
-        last = work((2,), after(chunk(2, *ties), halves[3]))
+        early = ring.across(halves[3][rows.shape[0] :], top)
+        last = work((2,), after(chunk(2, *ties), early))
     halves[2] = halve(last)
     for slot in (1, 0):
         halves[slot] = halve(done[slot])
@@ -127,10 +128,13 @@
     own = rows.shape[0]
     back = {}
     for slot, ties in ((3, []), (2, []), (1, [3]), (0, [2])):
+        if slot == 3 and not paired:
+            back[slot] = early
+            continue
         away = after(halves[slot][own:], *[back[t] for t in ties], *([halves[2]] if ties else []))
         back[slot] = ring.across(away, top)
     sums = plane_sums(ring, lambda slot: add(halves[slot][:own], back[slot]))
-    return sums, [crossed[1], crossed[2], back[2]]
+    return sums, [crossed[1], crossed[2], back[3], back[2]]
 
 
 def other_half(ring, weight, groups, ties):
@@ -205,7 +209,7 @@
     first, steps = routed(ring, jnp.concatenate([hidden_rows, lanes], axis=1), first_work, False)
     mine = (second_gate_up[0], second_down[0])
     second_pair = (mine, tuple(ring.across(after(w, steps[1]), ring.bits[-1]) for w in mine))
-    ties = [([], [steps[0]]), ([steps[1]], [steps[2]])]
+    ties = [([], [steps[0]]), ([steps[2]], [steps[3]])]
     weight = plane_weight(ring, merge_weight, other_half(ring, merge_weight, lax.axis_size("groups"), ties))
     after_first = (hidden_rows.astype(jnp.float32) + first).astype(jnp.bfloat16)
     merged_in = jnp.concatenate([normed(after_first, hidden_gain), normed(token_embed, embed_gain)], axis=1)

time: 200 us -> 205 us (1.025)
  waiting for transfers between devices: 80.1 us -> 103 us
  starting transfers between devices: 72.2 us -> 53.9 us
    ppermute x18, starting transfers between devices: 47.2 us -> 29.8 us  [send(): return lax.ppermute(values, 'inner', perm)]
    ppermute x29, waiting for transfers between devices: 31.6 us -> 46.3 us  [across(): lax.ppermute(values, 'inner', [(d, d ^ bit) for d in range(self.size)])]
    ppermute x18, waiting for transfers between devices: 45.9 us -> 53.7 us  [send(): return lax.ppermute(values, 'inner', perm)]
  transfers between devices with their start and end apart: 49 -> 49, of which waited for: 20 -> 23; matrix products, arithmetic and copies ran while one was open for 19% -> 18% of each run, Pallas kernels for 0% -> 0%
where the time goes in v17:
time: 205 us; the launch traced here: 204 us
  waiting for transfers between devices  103 us (50%)
  starting transfers between devices  53.9 us (26%)
  matrix products  20.8 us (10%)
  other arithmetic  17.7 us (9%)
  local copies, waits for them, and re-layouts  8.15 us (4%)
    ppermute x18, waiting for transfers between devices, send(): return lax.ppermute(values, 'inner', perm)  53.7 us
    ppermute x29, waiting for transfers between devices, across(): lax.ppermute(values, 'inner', [(d, d ^ bit) for d in range(self.size)])  46.3 us
    ppermute x18, starting transfers between devices, send(): return lax.ppermute(values, 'inner', perm)  29.8 us
    ppermute x29, starting transfers between devices, across(): lax.ppermute(values, 'inner', [(d, d ^ bit) for d in range(self.size)])  21.1 us
    dot_general x10, matrix products, experts(): projected = jnp.dot(rows, gate_up, preferred_element_type=jnp.float32)  10.5 us
    dot_general x10, matrix products, experts(): jnp.dot(hidden.astype(jnp.bfloat16), down, preferred_element_type=jnp.flo...  6.92 us
    concatenate x8, other arithmetic, chunk(): part = after(jnp.concatenate([columns[slot], crossed[slot]], axis=0), *ties)  4.83 us
    unnamed x40, local copies, waits for them, and re-layouts  4.36 us
  transfers between devices with their start and end apart: 49, of which 23 were waited for; matrix products, arithmetic and copies ran while one was open for 18% of the time, Pallas kernels for 0%

profile of v17, /device:TPU:0, one launch (start us, length us, event | category | flops | bytes accessed | tf_op | source)
XLA Modules:
  0.0 204.2 jit_solution(16206781381930719363)
XLA Ops:
  3.4 3.1 %collective-permute-start.3 = (bf16[64,2176]{1,0:T(8,128)(2,1)S(1)}, bf16[64,2176]{1,0:T(8,128)(2,1)S(1)}, u32[]{:S(2)}, u32[]{:S(2)}) collective-permute-start(bf16[64,2176]{1,0:T(8,128)(2,1)S(1)} %pad_maximum_fusion.14), channel_id=1, source_target_pairs={{0,4},{1,5},{2,6},{3,7},{4,0},{5,1},{6,2},{7,3},{8,12},{9,13},{10,... | collective-permute-start | bytes 835592 | tf_op jit(solution)/shard_map/ppermute | solution.py:25
  6.5 2.5 %collective-permute-start.2 = (bf16[64,2176]{1,0:T(8,128)(2,1)S(1)}, bf16[64,2176]{1,0:T(8,128)(2,1)S(1)}, u32[]{:S(2)}, u32[]{:S(2)}) collective-permute-start(bf16[64,2176]{1,0:T(8,128)(2,1)S(1)} %pad_maximum_fusion.14), channel_id=1, source_target_pairs={{0,12},{1,13},{2,14},{3,15},{4,8},{5,9},{6,10},{7,11},{8,4},{9,5},... | collective-permute-start | bytes 835592 | tf_op jit(solution)/shard_map/ppermute | solution.py:25
  9.1 1.5 collective-permute-start
  10.6 1.9 constant_dynamic-slice_fusion.1
  14.2 1.6 collective-permute-start.4
  15.8 2.9 %collective-permute-done = bf16[64,2176]{1,0:T(8,128)(2,1)S(1)} collective-permute-done((bf16[64,2176]{1,0:T(8,128)(2,1)S(1)}, bf16[64,2176]{1,0:T(8,128)(2,1)S(1)}, u32[]{:S(2)}, u32[]{:S(2)}) %collective-permute-start) | collective-permute-done | bytes 278560 | tf_op jit(solution)/shard_map/ppermute | solution.py:31
  18.8 3.7 %collective-permute-done.2 = bf16[64,2176]{1,0:T(8,128)(2,1)S(1)} collective-permute-done((bf16[64,2176]{1,0:T(8,128)(2,1)S(1)}, bf16[64,2176]{1,0:T(8,128)(2,1)S(1)}, u32[]{:S(2)}, u32[]{:S(2)}) %collective-permute-start.2) | collective-permute-done | bytes 278560 | tf_op jit(solution)/shard_map/ppermute | solution.py:25
  22.5 6.0 %collective-permute-done.4 = bf16[64,2176]{1,0:T(8,128)(2,1)S(1)} collective-permute-done((bf16[64,2176]{1,0:T(8,128)(2,1)S(1)}, bf16[64,2176]{1,0:T(8,128)(2,1)S(1)}, u32[]{:S(2)}, u32[]{:S(2)}) %collective-permute-start.4) | collective-permute-done | bytes 278560 | tf_op jit(solution)/shard_map/ppermute | solution.py:31
  28.5 1.5 collective-permute-start.5
  30.1 1.6 collective-permute-start.23
  31.6 3.8 %collective-permute-done.5 = bf16[64,2176]{1,0:T(8,128)(2,1)S(1)} collective-permute-done((bf16[64,2176]{1,0:T(8,128)(2,1)S(1)}, bf16[64,2176]{1,0:T(8,128)(2,1)S(1)}, u32[]{:S(2)}, u32[]{:S(2)}) %collective-permute-start.5) | collective-permute-done | bytes 278560 | tf_op jit(solution)/shard_map/ppermute | solution.py:31
  35.5 1.6 collective-permute-start.8
  37.2 1.3 fusion.6
  44.9 1.3 pad_maximum_fusion.7
  49.4 7.7 %collective-permute-done.13 = bf16[64,2048]{1,0:T(8,128)(2,1)S(1)} collective-permute-done((bf16[64,2048]{1,0:T(8,128)(2,1)S(1)}, bf16[64,2048]{1,0:T(8,128)(2,1)S(1)}, u32[]{:S(2)}, u32[]{:S(2)}) %collective-permute-start.13) | collective-permute-done | bytes 262176 | tf_op jit(solution)/shard_map/ppermute | solution.py:31
  57.0 1.3 fusion
  62.7 2.4 %collective-permute-start.17 = (bf16[64,2048]{1,0:T(8,128)(2,1)S(1)}, bf16[64,2048]{1,0:T(8,128)(2,1)S(1)}, u32[]{:S(2)}, u32[]{:S(2)}) collective-permute-start(bf16[64,2048]{1,0:T(8,128)(2,1)S(1)} %add_convert_fusion.12), channel_id=1, source_target_pairs={{0,12},{1,13},{2,14},{3,15},{4,8},{5,9},{6,10},{7,11},{8,4},{9,5},... | collective-permute-start | bytes 786440 | tf_op jit(solution)/shard_map/ppermute | solution.py:25
  66.2 3.4 %collective-permute-done.24 = bf16[64,2048]{1,0:T(8,128)(2,1)S(1)} collective-permute-done((bf16[64,2048]{1,0:T(8,128)(2,1)S(1)}, bf16[64,2048]{1,0:T(8,128)(2,1)S(1)}, u32[]{:S(2)}, u32[]{:S(2)}) %collective-permute-start.24) | collective-permute-done | bytes 262176 | tf_op jit(solution)/shard_map/ppermute | solution.py:31
  69.5 5.6 %collective-permute-done.15 = bf16[64,2048]{1,0:T(8,128)(2,1)S(1)} collective-permute-done((bf16[64,2048]{1,0:T(8,128)(2,1)S(1)}, bf16[64,2048]{1,0:T(8,128)(2,1)S(1)}, u32[]{:S(2)}, u32[]{:S(2)}) %collective-permute-start.15) | collective-permute-done | bytes 262176 | tf_op jit(solution)/shard_map/ppermute | solution.py:31
  75.2 1.5 collective-permute-start.25
  76.7 2.3 %collective-permute-start.18 = (bf16[64,2048]{1,0:T(8,128)(2,1)S(1)}, bf16[64,2048]{1,0:T(8,128)(2,1)S(1)}, u32[]{:S(2)}, u32[]{:S(2)}) collective-permute-start(bf16[64,2048]{1,0:T(8,128)(2,1)S(1)} %add_convert_fusion.11), channel_id=1, source_target_pairs={{0,8},{1,9},{2,10},{3,11},{4,12},{5,13},{6,14},{7,15},{8,0},{9,1},... | collective-permute-start | bytes 786440 | tf_op jit(solution)/shard_map/ppermute | solution.py:25
  79.0 2.7 %collective-permute-done.25 = bf16[64,2048]{1,0:T(8,128)(2,1)S(1)} collective-permute-done((bf16[64,2048]{1,0:T(8,128)(2,1)S(1)}, bf16[64,2048]{1,0:T(8,128)(2,1)S(1)}, u32[]{:S(2)}, u32[]{:S(2)}) %collective-permute-start.25) | collective-permute-done | bytes 262176 | tf_op jit(solution)/shard_map/ppermute | solution.py:151
  83.2 1.3 collective-permute-start.21
  84.6 5.1 %collective-permute-done.18 = bf16[64,2048]{1,0:T(8,128)(2,1)S(1)} collective-permute-done((bf16[64,2048]{1,0:T(8,128)(2,1)S(1)}, bf16[64,2048]{1,0:T(8,128)(2,1)S(1)}, u32[]{:S(2)}, u32[]{:S(2)}) %collective-permute-start.18) | collective-permute-done | bytes 262176 | tf_op jit(solution)/shard_map/ppermute | solution.py:25
  89.7 5.5 %collective-permute-done.21 = bf16[64,2048]{1,0:T(8,128)(2,1)S(1)} collective-permute-done((bf16[64,2048]{1,0:T(8,128)(2,1)S(1)}, bf16[64,2048]{1,0:T(8,128)(2,1)S(1)}, u32[]{:S(2)}, u32[]{:S(2)}) %collective-permute-start.21) | collective-permute-done | bytes 262176 | tf_op jit(solution)/shard_map/ppermute | solution.py:25
  96.0 2.4 %collective-permute-start.27 = (bf16[64,1024]{1,0:T(8,128)(2,1)S(1)}, bf16[64,1024]{1,0:T(8,128)(2,1)S(1)}, u32[]{:S(2)}, u32[]{:S(2)}) collective-permute-start(bf16[64,1024]{1,0:T(8,128)(2,1)S(1)} %get-tuple-element.65), channel_id=1, source_target_pairs={{0,12},{1,13},{2,14},{3,15},{4,8},{5,9},{6,10},{7,11},{8,4},{9,5},... | collective-permute-start | bytes 393224 | tf_op jit(solution)/shard_map/ppermute | solution.py:25
  98.7 2.1 %collective-permute-start.31 = (bf16[64,1024]{1,0:T(8,128)(2,1)S(1)}, bf16[64,1024]{1,0:T(8,128)(2,1)S(1)}, u32[]{:S(2)}, u32[]{:S(2)}) collective-permute-start(bf16[64,1024]{1,0:T(8,128)(2,1)S(1)} %get-tuple-element.67), channel_id=1, source_target_pairs={{0,4},{1,5},{2,6},{3,7},{4,0},{5,1},{6,2},{7,3},{8,12},{9,13},{10,... | collective-permute-start | bytes 393224 | tf_op jit(solution)/shard_map/ppermute | solution.py:25
  101.7 2.6 %collective-permute-done.27 = bf16[64,1024]{1,0:T(8,128)(2,1)S(1)} collective-permute-done((bf16[64,1024]{1,0:T(8,128)(2,1)S(1)}, bf16[64,1024]{1,0:T(8,128)(2,1)S(1)}, u32[]{:S(2)}, u32[]{:S(2)}) %collective-permute-start.27) | collective-permute-done | bytes 131104 | tf_op jit(solution)/shard_map/ppermute | solution.py:25
  105.1 2.4 %collective-permute-start.28 = (bf16[64,2048]{1,0:T(8,128)(2,1)S(1)}, bf16[64,2048]{1,0:T(8,128)(2,1)S(1)}, u32[]{:S(2)}, u32[]{:S(2)}) collective-permute-start(bf16[64,2048]{1,0:T(8,128)(2,1)S(1)} %convolution_convert_fusion.6), channel_id=1, source_target_pairs={{0,12},{1,13},{2,14},{3,15},{4,8},{5,9},{6,10},{7,11},{8,4},{9,5},... | collective-permute-start | bytes 786440 | tf_op jit(solution)/shard_map/ppermute | solution.py:25
  107.5 2.4 %collective-permute-done.29 = bf16[64,1024]{1,0:T(8,128)(2,1)S(1)} collective-permute-done((bf16[64,1024]{1,0:T(8,128)(2,1)S(1)}, bf16[64,1024]{1,0:T(8,128)(2,1)S(1)}, u32[]{:S(2)}, u32[]{:S(2)}) %collective-permute-start.29) | collective-permute-done | bytes 131104 | tf_op jit(solution)/shard_map/ppermute | solution.py:25
  111.7 3.0 %collective-permute-start.32 = (bf16[64,2048]{1,0:T(8,128)(2,1)S(1)}, bf16[64,2048]{1,0:T(8,128)(2,1)S(1)}, u32[]{:S(2)}, u32[]{:S(2)}) collective-permute-start(bf16[64,2048]{1,0:T(8,128)(2,1)S(1)} %convolution_convert_fusion.4), channel_id=1, source_target_pairs={{0,4},{1,5},{2,6},{3,7},{4,0},{5,1},{6,2},{7,3},{8,12},{9,13},{10,... | collective-permute-start | bytes 786440 | tf_op jit(solution)/shard_map/ppermute | solution.py:25
  115.5 15.9 %collective-permute-done.30 = bf16[64,2048]{1,0:T(8,128)(2,1)S(1)} collective-permute-done((bf16[64,2048]{1,0:T(8,128)(2,1)S(1)}, bf16[64,2048]{1,0:T(8,128)(2,1)S(1)}, u32[]{:S(2)}, u32[]{:S(2)}) %collective-permute-start.30) | collective-permute-done | bytes 262176 | tf_op jit(solution)/shard_map/ppermute | solution.py:25
  131.7 2.0 copy-done.4
  134.3 2.4 %collective-permute-start.35 = (bf16[64,2048]{1,0:T(8,128)(2,1)S(1)}, bf16[64,2048]{1,0:T(8,128)(2,1)}, u32[]{:S(2)}, u32[]{:S(2)}) collective-permute-start(bf16[64,2048]{1,0:T(8,128)(2,1)S(1)} %fusion.25), channel_id=1, source_target_pairs={{0,12},{1,13},{2,14},{3,15},{4,8},{5,9},{6,10},{7,11},{8,4},{9,5},... | collective-permute-start | bytes 786440 | tf_op jit(solution)/shard_map/ppermute | solution.py:25
  136.7 5.2 %collective-permute-done.37 = bf16[64,2048]{1,0:T(8,128)(2,1)S(1)} collective-permute-done((bf16[64,2048]{1,0:T(8,128)(2,1)S(1)}, bf16[64,2048]{1,0:T(8,128)(2,1)S(1)}, u32[]{:S(2)}, u32[]{:S(2)}) %collective-permute-start.37) | collective-permute-done | bytes 262176 | tf_op jit(solution)/shard_map/ppermute | solution.py:31
  142.6 1.4 collective-permute-start.38
  147.1 1.9 collective-permute-start.40
  149.0 1.4 collective-permute-done.38
  153.5 7.0 %collective-permute-done.40 = bf16[64,2048]{1,0:T(8,128)(2,1)S(1)} collective-permute-done((bf16[64,2048]{1,0:T(8,128)(2,1)S(1)}, bf16[64,2048]{1,0:T(8,128)(2,1)S(1)}, u32[]{:S(2)}, u32[]{:S(2)}) %collective-permute-start.40) | collective-permute-done | bytes 262176 | tf_op jit(solution)/shard_map/ppermute | solution.py:25
  165.0 1.4 copy-done.5
  176.1 4.5 %collective-permute-done.44 = bf16[64,2048]{1,0:T(8,128)(2,1)S(1)} collective-permute-done((bf16[64,2048]{1,0:T(8,128)(2,1)S(1)}, bf16[64,2048]{1,0:T(8,128)(2,1)S(1)}, u32[]{:S(2)}, u32[]{:S(2)}) %collective-permute-start.44) | collective-permute-done | bytes 262176 | tf_op jit(solution)/shard_map/ppermute | solution.py:31
  180.7 2.5 %collective-permute-start.45 = (bf16[64,2048]{1,0:T(8,128)(2,1)S(1)}, bf16[64,2048]{1,0:T(8,128)(2,1)S(1)}, u32[]{:S(2)}, u32[]{:S(2)}) collective-permute-start(bf16[64,2048]{1,0:T(8,128)(2,1)S(1)} %add_convert_fusion.7), channel_id=1, source_target_pairs={{0,12},{1,13},{2,14},{3,15},{4,8},{5,9},{6,10},{7,11},{8,4},{9,5},... | collective-permute-start | bytes 786440 | tf_op jit(solution)/shard_map/ppermute | solution.py:25
  183.2 1.3 collective-permute-start.47
  184.5 1.7 collective-permute-done.42
  186.3 1.4 collective-permute-start.46
  187.7 1.3 collective-permute-start.43
  188.9 3.5 %collective-permute-done.47 = bf16[64,2048]{1,0:T(8,128)(2,1)S(1)} collective-permute-done((bf16[64,2048]{1,0:T(8,128)(2,1)S(1)}, bf16[64,2048]{1,0:T(8,128)(2,1)S(1)}, u32[]{:S(2)}, u32[]{:S(2)}) %collective-permute-start.47) | collective-permute-done | bytes 262176 | tf_op jit(solution)/shard_map/ppermute | solution.py:31
  192.6 9.7 %collective-permute-done.46 = bf16[64,2048]{1,0:T(8,128)(2,1)S(1)} collective-permute-done((bf16[64,2048]{1,0:T(8,128)(2,1)S(1)}, bf16[64,2048]{1,0:T(8,128)(2,1)S(1)}, u32[]{:S(2)}, u32[]{:S(2)}) %collective-permute-start.46) | collective-permute-done | bytes 262176 | tf_op jit(solution)/shard_map/ppermute | solution.py:25
  (179 shorter events, 51.0 us)
Async XLA Ops:
  3.4 10.8 %collective-permute-start.3 = (bf16[64,2176]{1,0:T(8,128)(2,1)S(1)}, bf16[64,2176]{1,0:T(8,128)(2,1)S(1)}, u32[]{:S(2)}, u32[]{:S(2)}) collective-permute-start(bf16[64,2176]{1,0:T(8,128)(2,1)S(1)} %pad_maximum_fusion.14), channel_id=1, source_target_pairs={{0,4},{1,5},{2,6},{3,7},{4,0},{5,1},{6,2},{7,3},{8,12},{9,13},{10,... | collective-permute-start | bytes 835592 | tf_op jit(solution)/shard_map/ppermute | solution.py:25
  6.5 16.1 %collective-permute-start.2 = (bf16[64,2176]{1,0:T(8,128)(2,1)S(1)}, bf16[64,2176]{1,0:T(8,128)(2,1)S(1)}, u32[]{:S(2)}, u32[]{:S(2)}) collective-permute-start(bf16[64,2176]{1,0:T(8,128)(2,1)S(1)} %pad_maximum_fusion.14), channel_id=1, source_target_pairs={{0,12},{1,13},{2,14},{3,15},{4,8},{5,9},{6,10},{7,11},{8,4},{9,5},... | collective-permute-start | bytes 835592 | tf_op jit(solution)/shard_map/ppermute | solution.py:25
  9.0 26.5 %collective-permute-start.7 = (bf16[64,2176]{1,0:T(8,128)(2,1)S(1)}, bf16[64,2176]{1,0:T(8,128)(2,1)}, u32[]{:S(2)}, u32[]{:S(2)}) collective-permute-start(bf16[64,2176]{1,0:T(8,128)(2,1)S(1)} %pad_maximum_fusion.14), channel_id=1, source_target_pairs={{0,8},{1,9},{2,10},{3,11},{4,12},{5,13},{6,14},{7,15},{8,0},{9,1},... | collective-permute-start | bytes 835592 | tf_op jit(solution)/shard_map/ppermute | solution.py:25
  9.1 9.6 %collective-permute-start = (bf16[64,2176]{1,0:T(8,128)(2,1)S(1)}, bf16[64,2176]{1,0:T(8,128)(2,1)S(1)}, u32[]{:S(2)}, u32[]{:S(2)}) collective-permute-start(bf16[64,2176]{1,0:T(8,128)(2,1)S(1)} %pad_maximum_fusion.14), channel_id=1, source_target_pairs={{0,2},{1,3},{2,0},{3,1},{4,6},{5,7},{6,4},{7,5},{8,10},{9,11},{10,... | collective-permute-start | bytes 835592 | tf_op jit(solution)/shard_map/ppermute | solution.py:31
  12.5 17.6 %collective-permute-start.22 = (bf16[64,2048]{1,0:T(8,128)(2,1)}, bf16[64,2048]{1,0:T(8,128)(2,1)}, u32[]{:S(2)}, u32[]{:S(2)}) collective-permute-start(bf16[64,2048]{1,0:T(8,128)(2,1)} %get-tuple-element.63), channel_id=1, source_target_pairs={{0,2},{1,3},{2,0},{3,1},{4,6},{5,7},{6,4},{7,5},{8,10},{9,11},{10,... | collective-permute-start | bytes 786440 | tf_op jit(solution)/shard_map/ppermute | solution.py:31
  14.2 14.3 %collective-permute-start.4 = (bf16[64,2176]{1,0:T(8,128)(2,1)S(1)}, bf16[64,2176]{1,0:T(8,128)(2,1)S(1)}, u32[]{:S(2)}, u32[]{:S(2)}) collective-permute-start(bf16[64,2176]{1,0:T(8,128)(2,1)S(1)} %collective-permute-done.3), channel_id=1, source_target_pairs={{0,2},{1,3},{2,0},{3,1},{4,6},{5,7},{6,4},{7,5},{8,10},{9,11},{10,... | collective-permute-start | bytes 835592 | tf_op jit(solution)/shard_map/ppermute | solution.py:31
  18.7 18.3 %collective-permute-start.1 = (bf16[128,2176]{1,0:T(8,128)(2,1)S(1)}, bf16[128,2176]{1,0:T(8,128)(2,1)S(1)}, u32[]{:S(2)}, u32[]{:S(2)}) collective-permute-start(bf16[128,2176]{1,0:T(8,128)(2,1)S(1)} %pad_maximum_fusion.6), channel_id=1, source_target_pairs={{0,1},{1,0},{2,3},{3,2},{4,5},{5,4},{6,7},{7,6},{8,9},{9,8},{10,11... | collective-permute-start | bytes 1671176 | tf_op jit(solution)/shard_map/ppermute | solution.py:31
  28.5 6.9 %collective-permute-start.5 = (bf16[64,2176]{1,0:T(8,128)(2,1)S(1)}, bf16[64,2176]{1,0:T(8,128)(2,1)S(1)}, u32[]{:S(2)}, u32[]{:S(2)}) collective-permute-start(bf16[64,2176]{1,0:T(8,128)(2,1)S(1)} %collective-permute-done.2), channel_id=1, source_target_pairs={{0,2},{1,3},{2,0},{3,1},{4,6},{5,7},{6,4},{7,5},{8,10},{9,11},{10,... | collective-permute-start | bytes 835592 | tf_op jit(solution)/shard_map/ppermute | solution.py:31
  30.1 16.2 %collective-permute-start.23 = (bf16[64,2048]{1,0:T(8,128)(2,1)}, bf16[64,2048]{1,0:T(8,128)(2,1)S(1)}, u32[]{:S(2)}, u32[]{:S(2)}) collective-permute-start(bf16[64,2048]{1,0:T(8,128)(2,1)} %collective-permute-done.22), channel_id=1, source_target_pairs={{0,16},{16,0},{1,17},{17,1},{2,18},{18,2},{3,19},{19,3},{4,20},{20... | collective-permute-start | bytes 786440 | tf_op jit(solution)/shard_map/ppermute | solution.py:151
  31.6 7.9 %collective-permute-start.10 = (bf16[128,2176]{1,0:T(8,128)(2,1)S(1)}, bf16[128,2176]{1,0:T(8,128)(2,1)S(1)}, u32[]{:S(2)}, u32[]{:S(2)}) collective-permute-start(bf16[128,2176]{1,0:T(8,128)(2,1)S(1)} %pad_maximum_fusion.9), channel_id=1, source_target_pairs={{0,1},{1,0},{2,3},{3,2},{4,5},{5,4},{6,7},{7,6},{8,9},{9,8},{10,11... | collective-permute-start | bytes 1671176 | tf_op jit(solution)/shard_map/ppermute | solution.py:31
  35.5 9.4 %collective-permute-start.8 = (bf16[64,2176]{1,0:T(8,128)(2,1)}, bf16[64,2176]{1,0:T(8,128)(2,1)S(1)}, u32[]{:S(2)}, u32[]{:S(2)}) collective-permute-start(bf16[64,2176]{1,0:T(8,128)(2,1)} %collective-permute-done.7), channel_id=1, source_target_pairs={{0,2},{1,3},{2,0},{3,1},{4,6},{5,7},{6,4},{7,5},{8,10},{9,11},{10,... | collective-permute-start | bytes 835592 | tf_op jit(solution)/shard_map/ppermute | solution.py:31
  37.2 4.8 %collective-permute-start.9 = (bf16[128,2176]{1,0:T(8,128)(2,1)S(1)}, bf16[128,2176]{1,0:T(8,128)(2,1)S(1)}, u32[]{:S(2)}, u32[]{:S(2)}) collective-permute-start(bf16[128,2176]{1,0:T(8,128)(2,1)S(1)} %pad_maximum_fusion.8), channel_id=1, source_target_pairs={{0,1},{1,0},{2,3},{3,2},{4,5},{5,4},{6,7},{7,6},{8,9},{9,8},{10,11... | collective-permute-start | bytes 1671176 | tf_op jit(solution)/shard_map/ppermute | solution.py:31
  44.4 4.2 %collective-permute-start.12 = (bf16[128,2048]{1,0:T(8,128)(2,1)S(1)}, bf16[128,2048]{1,0:T(8,128)(2,1)S(1)}, u32[]{:S(2)}, u32[]{:S(2)}) collective-permute-start(bf16[128,2048]{1,0:T(8,128)(2,1)S(1)} %slice.381), channel_id=1, source_target_pairs={{0,1},{1,0},{2,3},{3,2},{4,5},{5,4},{6,7},{7,6},{8,9},{9,8},{10,11... | collective-permute-start | bytes 1572872 | tf_op jit(solution)/shard_map/ppermute | solution.py:31
  46.2 3.1 %collective-permute-start.11 = (bf16[128,2176]{1,0:T(8,128)(2,1)S(1)}, bf16[128,2176]{1,0:T(8,128)(2,1)S(1)}, u32[]{:S(2)}, u32[]{:S(2)}) collective-permute-start(bf16[128,2176]{1,0:T(8,128)(2,1)S(1)} %pad_maximum_fusion.7), channel_id=1, source_target_pairs={{0,1},{1,0},{2,3},{3,2},{4,5},{5,4},{6,7},{7,6},{8,9},{9,8},{10,11... | collective-permute-start | bytes 1671176 | tf_op jit(solution)/shard_map/ppermute | solution.py:31
  47.3 12.2 %collective-permute-start.6 = (bf16[128,2048]{1,0:T(8,128)(2,1)S(1)}, bf16[128,2048]{1,0:T(8,128)(2,1)S(1)}, u32[]{:S(2)}, u32[]{:S(2)}) collective-permute-start(bf16[128,2048]{1,0:T(8,128)(2,1)S(1)} %slice.373), channel_id=1, source_target_pairs={{0,1},{1,0},{2,3},{3,2},{4,5},{5,4},{6,7},{7,6},{8,9},{9,8},{10,11... | collective-permute-start | bytes 1572872 | tf_op jit(solution)/shard_map/ppermute | solution.py:31
  47.9 11.8 %collective-permute-start.19 = (bf16[128,2048]{1,0:T(8,128)(2,1)S(1)}, bf16[128,2048]{1,0:T(8,128)(2,1)S(1)}, u32[]{:S(2)}, u32[]{:S(2)}) collective-permute-start(bf16[128,2048]{1,0:T(8,128)(2,1)S(1)} %slice.391), channel_id=1, source_target_pairs={{0,1},{1,0},{2,3},{3,2},{4,5},{5,4},{6,7},{7,6},{8,9},{9,8},{10,11... | collective-permute-start | bytes 1572872 | tf_op jit(solution)/shard_map/ppermute | solution.py:31
  48.0 83.6 %collective-permute-start.33 = (bf16[2048,1024]{1,0:T(8,128)(2,1)S(1)}, bf16[2048,1024]{1,0:T(8,128)(2,1)S(1)}, u32[]{:S(2)}, u32[]{:S(2)}) collective-permute-start(bf16[2048,1024]{1,0:T(8,128)(2,1)S(1)} %bitcast.63), channel_id=1, source_target_pairs={{0,1},{1,0},{2,3},{3,2},{4,5},{5,4},{6,7},{7,6},{8,9},{9,8},{10,11... | collective-permute-start | bytes 12582920 | tf_op jit(solution)/shard_map/ppermute | solution.py:31
  48.7 8.4 %collective-permute-start.13 = (bf16[64,2048]{1,0:T(8,128)(2,1)S(1)}, bf16[64,2048]{1,0:T(8,128)(2,1)S(1)}, u32[]{:S(2)}, u32[]{:S(2)}) collective-permute-start(bf16[64,2048]{1,0:T(8,128)(2,1)S(1)} %slice.382), channel_id=1, source_target_pairs={{0,2},{1,3},{2,0},{3,1},{4,6},{5,7},{6,4},{7,5},{8,10},{9,11},{10,... | collective-permute-start | bytes 786440 | tf_op jit(solution)/shard_map/ppermute | solution.py:31
  60.4 9.2 %collective-permute-start.24 = (bf16[64,2048]{1,0:T(8,128)(2,1)S(1)}, bf16[64,2048]{1,0:T(8,128)(2,1)S(1)}, u32[]{:S(2)}, u32[]{:S(2)}) collective-permute-start(bf16[64,2048]{1,0:T(8,128)(2,1)S(1)} %copy-done.15), channel_id=1, source_target_pairs={{0,2},{1,3},{2,0},{3,1},{4,6},{5,7},{6,4},{7,5},{8,10},{9,11},{10,... | collective-permute-start | bytes 786440 | tf_op jit(solution)/shard_map/ppermute | solution.py:31
  61.6 13.6 %collective-permute-start.15 = (bf16[64,2048]{1,0:T(8,128)(2,1)S(1)}, bf16[64,2048]{1,0:T(8,128)(2,1)S(1)}, u32[]{:S(2)}, u32[]{:S(2)}) collective-permute-start(bf16[64,2048]{1,0:T(8,128)(2,1)S(1)} %slice.387), channel_id=1, source_target_pairs={{0,2},{1,3},{2,0},{3,1},{4,6},{5,7},{6,4},{7,5},{8,10},{9,11},{10,... | collective-permute-start | bytes 786440 | tf_op jit(solution)/shard_map/ppermute | solution.py:31
  62.7 20.4 %collective-permute-start.17 = (bf16[64,2048]{1,0:T(8,128)(2,1)S(1)}, bf16[64,2048]{1,0:T(8,128)(2,1)S(1)}, u32[]{:S(2)}, u32[]{:S(2)}) collective-permute-start(bf16[64,2048]{1,0:T(8,128)(2,1)S(1)} %add_convert_fusion.12), channel_id=1, source_target_pairs={{0,12},{1,13},{2,14},{3,15},{4,8},{5,9},{6,10},{7,11},{8,4},{9,5},... | collective-permute-start | bytes 786440 | tf_op jit(solution)/shard_map/ppermute | solution.py:25
  65.1 17.9 %collective-permute-start.20 = (bf16[64,2048]{1,0:T(8,128)(2,1)S(1)}, bf16[64,2048]{1,0:T(8,128)(2,1)S(1)}, u32[]{:S(2)}, u32[]{:S(2)}) collective-permute-start(bf16[64,2048]{1,0:T(8,128)(2,1)S(1)} %slice.393), channel_id=1, source_target_pairs={{0,2},{1,3},{2,0},{3,1},{4,6},{5,7},{6,4},{7,5},{8,10},{9,11},{10,... | collective-permute-start | bytes 786440 | tf_op jit(solution)/shard_map/ppermute | solution.py:31
  75.2 6.6 %collective-permute-start.25 = (bf16[64,2048]{1,0:T(8,128)(2,1)S(1)}, bf16[64,2048]{1,0:T(8,128)(2,1)S(1)}, u32[]{:S(2)}, u32[]{:S(2)}) collective-permute-start(bf16[64,2048]{1,0:T(8,128)(2,1)S(1)} %collective-permute-done.24), channel_id=1, source_target_pairs={{0,16},{16,0},{1,17},{17,1},{2,18},{18,2},{3,19},{19,3},{4,20},{20... | collective-permute-start | bytes 786440 | tf_op jit(solution)/shard_map/ppermute | solution.py:151
  76.7 13.0 %collective-permute-start.18 = (bf16[64,2048]{1,0:T(8,128)(2,1)S(1)}, bf16[64,2048]{1,0:T(8,128)(2,1)S(1)}, u32[]{:S(2)}, u32[]{:S(2)}) collective-permute-start(bf16[64,2048]{1,0:T(8,128)(2,1)S(1)} %add_convert_fusion.11), channel_id=1, source_target_pairs={{0,8},{1,9},{2,10},{3,11},{4,12},{5,13},{6,14},{7,15},{8,0},{9,1},... | collective-permute-start | bytes 786440 | tf_op jit(solution)/shard_map/ppermute | solution.py:25
  81.7 8.0 %collective-permute-start.16 = (bf16[64,2048]{1,0:T(8,128)(2,1)S(1)}, bf16[64,2048]{1,0:T(8,128)(2,1)S(1)}, u32[]{:S(2)}, u32[]{:S(2)}) collective-permute-start(bf16[64,2048]{1,0:T(8,128)(2,1)S(1)} %slice.375), channel_id=1, source_target_pairs={{0,2},{1,3},{2,0},{3,1},{4,6},{5,7},{6,4},{7,5},{8,10},{9,11},{10,... | collective-permute-start | bytes 786440 | tf_op jit(solution)/shard_map/ppermute | solution.py:31
  83.0 15.7 %collective-permute-start.26 = (bf16[2,256,2048]{2,1,0:T(8,128)(2,1)S(1)}, bf16[2,256,2048]{2,1,0:T(8,128)(2,1)S(1)}, u32[]{:S(2)}, u32[]{:S(2)}) collective-permute-start(bf16[2,256,2048]{2,1,0:T(8,128)(2,1)S(1)} %maximum_select_fusion.1), channel_id=1, source_target_pairs={{0,1},{1,0},{2,3},{3,2},{4,5},{5,4},{6,7},{7,6},{8,9},{9,8},{10,11... | collective-permute-start | bytes 6291464 | tf_op jit(solution)/shard_map/ppermute | solution.py:31
  83.2 12.1 %collective-permute-start.21 = (bf16[64,2048]{1,0:T(8,128)(2,1)S(1)}, bf16[64,2048]{1,0:T(8,128)(2,1)S(1)}, u32[]{:S(2)}, u32[]{:S(2)}) collective-permute-start(bf16[64,2048]{1,0:T(8,128)(2,1)S(1)} %add_convert_fusion.10), channel_id=1, source_target_pairs={{0,4},{1,5},{2,6},{3,7},{4,0},{5,1},{6,2},{7,3},{8,12},{9,13},{10,... | collective-permute-start | bytes 786440 | tf_op jit(solution)/shard_map/ppermute | solution.py:25
  89.7 41.9 %collective-permute-start.34 = (bf16[512,2048]{1,0:T(8,128)(2,1)S(1)}, bf16[512,2048]{1,0:T(8,128)(2,1)S(1)}, u32[]{:S(2)}, u32[]{:S(2)}) collective-permute-start(bf16[512,2048]{1,0:T(8,128)(2,1)S(1)} %bitcast.64), channel_id=1, source_target_pairs={{0,1},{1,0},{2,3},{3,2},{4,5},{5,4},{6,7},{7,6},{8,9},{9,8},{10,11... | collective-permute-start | bytes 6291464 | tf_op jit(solution)/shard_map/ppermute | solution.py:31
  96.0 8.3 %collective-permute-start.27 = (bf16[64,1024]{1,0:T(8,128)(2,1)S(1)}, bf16[64,1024]{1,0:T(8,128)(2,1)S(1)}, u32[]{:S(2)}, u32[]{:S(2)}) collective-permute-start(bf16[64,1024]{1,0:T(8,128)(2,1)S(1)} %get-tuple-element.65), channel_id=1, source_target_pairs={{0,12},{1,13},{2,14},{3,15},{4,8},{5,9},{6,10},{7,11},{8,4},{9,5},... | collective-permute-start | bytes 393224 | tf_op jit(solution)/shard_map/ppermute | solution.py:25
  98.4 11.5 %collective-permute-start.29 = (bf16[64,1024]{1,0:T(8,128)(2,1)S(1)}, bf16[64,1024]{1,0:T(8,128)(2,1)S(1)}, u32[]{:S(2)}, u32[]{:S(2)}) collective-permute-start(bf16[64,1024]{1,0:T(8,128)(2,1)S(1)} %get-tuple-element.66), channel_id=1, source_target_pairs={{0,8},{1,9},{2,10},{3,11},{4,12},{5,13},{6,14},{7,15},{8,0},{9,1},... | collective-permute-start | bytes 393224 | tf_op jit(solution)/shard_map/ppermute | solution.py:25
  98.7 12.1 %collective-permute-start.31 = (bf16[64,1024]{1,0:T(8,128)(2,1)S(1)}, bf16[64,1024]{1,0:T(8,128)(2,1)S(1)}, u32[]{:S(2)}, u32[]{:S(2)}) collective-permute-start(bf16[64,1024]{1,0:T(8,128)(2,1)S(1)} %get-tuple-element.67), channel_id=1, source_target_pairs={{0,4},{1,5},{2,6},{3,7},{4,0},{5,1},{6,2},{7,3},{8,12},{9,13},{10,... | collective-permute-start | bytes 393224 | tf_op jit(solution)/shard_map/ppermute | solution.py:25
  105.1 10.4 %collective-permute-start.28 = (bf16[64,2048]{1,0:T(8,128)(2,1)S(1)}, bf16[64,2048]{1,0:T(8,128)(2,1)S(1)}, u32[]{:S(2)}, u32[]{:S(2)}) collective-permute-start(bf16[64,2048]{1,0:T(8,128)(2,1)S(1)} %convolution_convert_fusion.6), channel_id=1, source_target_pairs={{0,12},{1,13},{2,14},{3,15},{4,8},{5,9},{6,10},{7,11},{8,4},{9,5},... | collective-permute-start | bytes 786440 | tf_op jit(solution)/shard_map/ppermute | solution.py:25
  110.7 20.6 %collective-permute-start.30 = (bf16[64,2048]{1,0:T(8,128)(2,1)S(1)}, bf16[64,2048]{1,0:T(8,128)(2,1)S(1)}, u32[]{:S(2)}, u32[]{:S(2)}) collective-permute-start(bf16[64,2048]{1,0:T(8,128)(2,1)S(1)} %convolution_convert_fusion.5), channel_id=1, source_target_pairs={{0,8},{1,9},{2,10},{3,11},{4,12},{5,13},{6,14},{7,15},{8,0},{9,1},... | collective-permute-start | bytes 786440 | tf_op jit(solution)/shard_map/ppermute | solution.py:25
  111.7 19.7 %collective-permute-start.32 = (bf16[64,2048]{1,0:T(8,128)(2,1)S(1)}, bf16[64,2048]{1,0:T(8,128)(2,1)S(1)}, u32[]{:S(2)}, u32[]{:S(2)}) collective-permute-start(bf16[64,2048]{1,0:T(8,128)(2,1)S(1)} %convolution_convert_fusion.4), channel_id=1, source_target_pairs={{0,4},{1,5},{2,6},{3,7},{4,0},{5,1},{6,2},{7,3},{8,12},{9,13},{10,... | collective-permute-start | bytes 786440 | tf_op jit(solution)/shard_map/ppermute | solution.py:25
  133.7 8.2 %collective-permute-start.37 = (bf16[64,2048]{1,0:T(8,128)(2,1)S(1)}, bf16[64,2048]{1,0:T(8,128)(2,1)S(1)}, u32[]{:S(2)}, u32[]{:S(2)}) collective-permute-start(bf16[64,2048]{1,0:T(8,128)(2,1)S(1)} %fusion.25), channel_id=1, source_target_pairs={{0,2},{1,3},{2,0},{3,1},{4,6},{5,7},{6,4},{7,5},{8,10},{9,11},{10,... | collective-permute-start | bytes 786440 | tf_op jit(solution)/shard_map/ppermute | solution.py:31
  134.3 8.3 %collective-permute-start.36 = (bf16[64,2048]{1,0:T(8,128)(2,1)S(1)}, bf16[64,2048]{1,0:T(8,128)(2,1)}, u32[]{:S(2)}, u32[]{:S(2)}) collective-permute-start(bf16[64,2048]{1,0:T(8,128)(2,1)S(1)} %fusion.25), channel_id=1, source_target_pairs={{0,4},{1,5},{2,6},{3,7},{4,0},{5,1},{6,2},{7,3},{8,12},{9,13},{10,... | collective-permute-start | bytes 786440 | tf_op jit(solution)/shard_map/ppermute | solution.py:25
  134.3 14.7 %collective-permute-start.35 = (bf16[64,2048]{1,0:T(8,128)(2,1)S(1)}, bf16[64,2048]{1,0:T(8,128)(2,1)}, u32[]{:S(2)}, u32[]{:S(2)}) collective-permute-start(bf16[64,2048]{1,0:T(8,128)(2,1)S(1)} %fusion.25), channel_id=1, source_target_pairs={{0,12},{1,13},{2,14},{3,15},{4,8},{5,9},{6,10},{7,11},{8,4},{9,5},... | collective-permute-start | bytes 786440 | tf_op jit(solution)/shard_map/ppermute | solution.py:25
  142.6 7.8 %collective-permute-start.38 = (bf16[64,2048]{1,0:T(8,128)(2,1)}, bf16[64,2048]{1,0:T(8,128)(2,1)}, u32[]{:S(2)}, u32[]{:S(2)}) collective-permute-start(bf16[64,2048]{1,0:T(8,128)(2,1)} %collective-permute-done.36), channel_id=1, source_target_pairs={{0,2},{1,3},{2,0},{3,1},{4,6},{5,7},{6,4},{7,5},{8,10},{9,11},{10,... | collective-permute-start | bytes 786440 | tf_op jit(solution)/shard_map/ppermute | solution.py:31
  147.1 13.5 %collective-permute-start.40 = (bf16[64,2048]{1,0:T(8,128)(2,1)S(1)}, bf16[64,2048]{1,0:T(8,128)(2,1)S(1)}, u32[]{:S(2)}, u32[]{:S(2)}) collective-permute-start(bf16[64,2048]{1,0:T(8,128)(2,1)S(1)} %fusion.25), channel_id=1, source_target_pairs={{0,8},{1,9},{2,10},{3,11},{4,12},{5,13},{6,14},{7,15},{8,0},{9,1},... | collective-permute-start | bytes 786440 | tf_op jit(solution)/shard_map/ppermute | solution.py:25
  150.4 10.2 %collective-permute-start.39 = (bf16[64,2048]{1,0:T(8,128)(2,1)}, bf16[64,2048]{1,0:T(8,128)(2,1)S(1)}, u32[]{:S(2)}, u32[]{:S(2)}) collective-permute-start(bf16[64,2048]{1,0:T(8,128)(2,1)} %collective-permute-done.35), channel_id=1, source_target_pairs={{0,2},{1,3},{2,0},{3,1},{4,6},{5,7},{6,4},{7,5},{8,10},{9,11},{10,... | collective-permute-start | bytes 786440 | tf_op jit(solution)/shard_map/ppermute | solution.py:31
  161.6 10.7 %collective-permute-start.41 = (bf16[64,2048]{1,0:T(8,128)(2,1)S(1)}, bf16[64,2048]{1,0:T(8,128)(2,1)S(1)}, u32[]{:S(2)}, u32[]{:S(2)}) collective-permute-start(bf16[64,2048]{1,0:T(8,128)(2,1)S(1)} %collective-permute-done.40), channel_id=1, source_target_pairs={{0,2},{1,3},{2,0},{3,1},{4,6},{5,7},{6,4},{7,5},{8,10},{9,11},{10,... | collective-permute-start | bytes 786440 | tf_op jit(solution)/shard_map/ppermute | solution.py:31
  171.3 9.3 %collective-permute-start.44 = (bf16[64,2048]{1,0:T(8,128)(2,1)S(1)}, bf16[64,2048]{1,0:T(8,128)(2,1)S(1)}, u32[]{:S(2)}, u32[]{:S(2)}) collective-permute-start(bf16[64,2048]{1,0:T(8,128)(2,1)S(1)} %get-tuple-element.60), channel_id=1, source_target_pairs={{0,2},{1,3},{2,0},{3,1},{4,6},{5,7},{6,4},{7,5},{8,10},{9,11},{10,... | collective-permute-start | bytes 786440 | tf_op jit(solution)/shard_map/ppermute | solution.py:31
  174.9 11.3 %collective-permute-start.42 = (bf16[64,2048]{1,0:T(8,128)(2,1)S(1)}, bf16[64,2048]{1,0:T(8,128)(2,1)S(1)}, u32[]{:S(2)}, u32[]{:S(2)}) collective-permute-start(bf16[64,2048]{1,0:T(8,128)(2,1)S(1)} %slice.412), channel_id=1, source_target_pairs={{0,2},{1,3},{2,0},{3,1},{4,6},{5,7},{6,4},{7,5},{8,10},{9,11},{10,... | collective-permute-start | bytes 786440 | tf_op jit(solution)/shard_map/ppermute | solution.py:31
  180.7 11.9 %collective-permute-start.45 = (bf16[64,2048]{1,0:T(8,128)(2,1)S(1)}, bf16[64,2048]{1,0:T(8,128)(2,1)S(1)}, u32[]{:S(2)}, u32[]{:S(2)}) collective-permute-start(bf16[64,2048]{1,0:T(8,128)(2,1)S(1)} %add_convert_fusion.7), channel_id=1, source_target_pairs={{0,12},{1,13},{2,14},{3,15},{4,8},{5,9},{6,10},{7,11},{8,4},{9,5},... | collective-permute-start | bytes 786440 | tf_op jit(solution)/shard_map/ppermute | solution.py:25
  183.2 9.2 %collective-permute-start.47 = (bf16[64,2048]{1,0:T(8,128)(2,1)S(1)}, bf16[64,2048]{1,0:T(8,128)(2,1)S(1)}, u32[]{:S(2)}, u32[]{:S(2)}) collective-permute-start(bf16[64,2048]{1,0:T(8,128)(2,1)S(1)} %slice.417), channel_id=1, source_target_pairs={{0,2},{1,3},{2,0},{3,1},{4,6},{5,7},{6,4},{7,5},{8,10},{9,11},{10,... | collective-permute-start | bytes 786440 | tf_op jit(solution)/shard_map/ppermute | solution.py:31
  186.3 16.0 %collective-permute-start.46 = (bf16[64,2048]{1,0:T(8,128)(2,1)S(1)}, bf16[64,2048]{1,0:T(8,128)(2,1)S(1)}, u32[]{:S(2)}, u32[]{:S(2)}) collective-permute-start(bf16[64,2048]{1,0:T(8,128)(2,1)S(1)} %add_convert_fusion.6), channel_id=1, source_target_pairs={{0,8},{1,9},{2,10},{3,11},{4,12},{5,13},{6,14},{7,15},{8,0},{9,1},... | collective-permute-start | bytes 786440 | tf_op jit(solution)/shard_map/ppermute | solution.py:25
  187.7 14.6 %collective-permute-start.43 = (bf16[64,2048]{1,0:T(8,128)(2,1)S(1)}, bf16[64,2048]{1,0:T(8,128)(2,1)S(1)}, u32[]{:S(2)}, u32[]{:S(2)}) collective-permute-start(bf16[64,2048]{1,0:T(8,128)(2,1)S(1)} %get-tuple-element.49), channel_id=1, source_target_pairs={{0,2},{1,3},{2,0},{3,1},{4,6},{5,7},{6,4},{7,5},{8,10},{9,11},{10,... | collective-permute-start | bytes 786440 | tf_op jit(solution)/shard_map/ppermute | solution.py:31
  192.5 10.8 %collective-permute-start.48 = (bf16[64,2048]{1,0:T(8,128)(2,1)S(1)}, bf16[64,2048]{1,0:T(8,128)(2,1)S(1)}, u32[]{:S(2)}, u32[]{:S(2)}) collective-permute-start(bf16[64,2048]{1,0:T(8,128)(2,1)S(1)} %add_convert_fusion.5), channel_id=1, source_target_pairs={{0,4},{1,5},{2,6},{3,7},{4,0},{5,1},{6,2},{7,3},{8,12},{9,13},{10,... | collective-permute-start | bytes 786440 | tf_op jit(solution)/shard_map/ppermute | solution.py:25
  (21 other events, 173.9 us)
